TPU v7x, 32 devices: a whole 2x2x4 slice. The times are simulated.
32 devices in a mesh: dp: 8 (over z, x), tensor: 4 (over y, core).
Axes of the slice: x: 2, y: 2, z: 4, core: 2. Of those that a mesh axis runs over, the one named last changes fastest.
Arguments:
- text_states: bfloat16 [2, 1024, 4096], P(None, 'dp'), may hold values from -16 to 16, as said below
- image_states: bfloat16 [2, 32, 4096], P(None, 'dp'), may hold values from -81 to 81
- out_grad: bfloat16 [2, 1024, 4096], P(None, 'dp'), may hold values from -6 to 6
- text_lengths: int32 [2], replicated, may hold values from 256 to 1024
- query_weight: bfloat16 [4096, 4096], P('dp', 'tensor'), as said below
- key_weight: bfloat16 [4096, 4096], P('dp', 'tensor'), as said below
- value_weight: bfloat16 [4096, 4096], P('dp', 'tensor'), may hold values from -0.09375 to 0.09375
- out_weight: bfloat16 [4096, 4096], P('tensor', 'dp'), may hold values from -0.09375 to 0.09375
Outputs:
- text_grad: bfloat16 [2, 1024, 4096], P(None, 'dp', 'tensor')
- image_grad: bfloat16 [2, 32, 4096], P(None, 'dp', 'tensor')
- out_weight_grad: bfloat16 [4096, 4096], P('tensor', 'dp')
Inputs may be any that keep to these rules, and one draw needn't show every extreme that they name: `text_states`: text states are normal rows with row scales; rows at multiples of 256 have entries within 3. `query_weight`: entries within 8 / sqrt(4096) in magnitude. `key_weight`: entries within 8 / sqrt(4096) in magnitude.
All inputs are finite; a program needn't handle non-finite values.
Results may differ from a plain program's by a relative error of at most 0.019.
The roundings to bfloat16 on the way count: a program that leaves them out, or rounds other values in their place, can miss the bound.
Values may be sent and summed in bfloat16 or wider, within the bound.
No kernel may reach another device: no remote copies, remote signals or barrier semaphores. Data moves between devices by JAX's collectives and lax.ppermute only.
A program may use at most 128 MiB of HBM per device.

v0:
```python
import jax
import jax.numpy as jnp
from jax import lax
from jax.sharding import PartitionSpec as P

HEAD_DIM = 128


def softmax_rows(scores):
    peak = jnp.max(scores, axis=-1, keepdims=True)
    expo = jnp.exp(scores - peak)
    return expo / jnp.sum(expo, axis=-1, keepdims=True)


def shards(
    text_states,
    image_states,
    out_grad,
    text_lengths,
    query_weight,
    key_weight,
    value_weight,
    out_weight,
):
    score_scale = HEAD_DIM ** (-0.5)
    samples, tok_rows, width = text_states.shape
    image_own = image_states.shape[1]
    first_row = lax.axis_index("dp") * tok_rows
    positions = first_row + lax.iota(jnp.int32, tok_rows)
    live_rows = positions[None, :] < text_lengths[:, None]
    grad_live = jnp.where(live_rows[..., None], out_grad, jnp.zeros_like(out_grad))
    text_flat = text_states.reshape(samples * tok_rows, width)
    live_flat = grad_live.reshape(samples * tok_rows, width)
    back_dims = (((1,), (1,)), ((), ()))
    wq_full, wk_full, wv_full, wo_full = (
        lax.all_gather(query_weight, "dp", axis=0, tiled=True),
        lax.all_gather(key_weight, "dp", axis=0, tiled=True),
        lax.all_gather(value_weight, "dp", axis=0, tiled=True),
        lax.all_gather(out_weight, "dp", axis=1, tiled=True),
    )
    local_cols = wq_full.shape[1]
    image_flat = image_states.reshape(samples * image_own, width)
    keys_own = jnp.dot(image_flat, wk_full, preferred_element_type=jnp.float32).astype(jnp.bfloat16)
    values_own = jnp.dot(image_flat, wv_full, preferred_element_type=jnp.float32).astype(
        jnp.bfloat16
    )
    keys_own = keys_own.reshape(samples, image_own, local_cols)
    values_own = values_own.reshape(samples, image_own, local_cols)
    keys_all, values_all = (
        lax.all_gather(keys_own, "dp", axis=1, tiled=True),
        lax.all_gather(values_own, "dp", axis=1, tiled=True),
    )
    image_count = keys_all.shape[1]
    head_count = local_cols // HEAD_DIM
    queries = jnp.dot(text_flat, wq_full, preferred_element_type=jnp.float32).astype(jnp.bfloat16)
    query_heads = queries.reshape(samples, tok_rows, head_count, HEAD_DIM)
    key_heads = keys_all.reshape(samples, image_count, head_count, HEAD_DIM)
    value_heads = values_all.reshape(samples, image_count, head_count, HEAD_DIM)
    scores = (
        jnp.einsum("sthd,sjhd->shtj", query_heads, key_heads, preferred_element_type=jnp.float32)
        * score_scale
    )
    soft_prob = softmax_rows(scores)
    prob_low = soft_prob.astype(jnp.bfloat16)
    attended = jnp.einsum(
        "shtj,sjhd->sthd", prob_low, value_heads, preferred_element_type=jnp.float32
    )
    attended = attended.astype(jnp.bfloat16).reshape(samples * tok_rows, local_cols)
    summed = lax.psum_scatter(
        lax.dot_general(
            live_flat, attended, (((0,), (0,)), ((), ())), preferred_element_type=jnp.float32
        ).astype(jnp.bfloat16),
        "dp",
        scatter_dimension=0,
        tiled=True,
    ).astype(jnp.float32)
    weight_grad = summed.T.astype(jnp.bfloat16)
    attended_grad = lax.dot_general(
        live_flat, wo_full, back_dims, preferred_element_type=jnp.float32
    )
    grad_heads = attended_grad.astype(jnp.bfloat16).reshape(samples, tok_rows, head_count, HEAD_DIM)
    value_part_grad = jnp.einsum(
        "shtj,sthd->sjhd", prob_low, grad_heads, preferred_element_type=jnp.float32
    )
    value_part_grad = value_part_grad.reshape(samples, image_count, local_cols)
    prob_grad = jnp.einsum(
        "sthd,sjhd->shtj", grad_heads, value_heads, preferred_element_type=jnp.float32
    )
    row_delta = jnp.sum(soft_prob * prob_grad, axis=-1, keepdims=True)
    score_grad = (soft_prob * (prob_grad - row_delta) * score_scale).astype(jnp.bfloat16)
    query_grad = jnp.einsum(
        "shtj,sjhd->sthd", score_grad, key_heads, preferred_element_type=jnp.float32
    ).astype(jnp.bfloat16)
    key_part_grad = jnp.einsum(
        "shtj,sthd->sjhd", score_grad, query_heads, preferred_element_type=jnp.float32
    )
    key_part_grad = key_part_grad.reshape(samples, image_count, local_cols)
    query_grad = query_grad.reshape(samples * tok_rows, local_cols)
    text_term = lax.dot_general(query_grad, wq_full, back_dims, preferred_element_type=jnp.float32)
    text_term = text_term.reshape(samples, tok_rows, width)
    key_grad, value_grad = (
        lax.psum_scatter(
            key_part_grad.astype(jnp.bfloat16), "dp", scatter_dimension=1, tiled=True
        ).astype(jnp.float32),
        lax.psum_scatter(
            value_part_grad.astype(jnp.bfloat16), "dp", scatter_dimension=1, tiled=True
        ).astype(jnp.float32),
    )
    key_low = key_grad.astype(jnp.bfloat16).reshape(samples * image_own, local_cols)
    value_low = value_grad.astype(jnp.bfloat16).reshape(samples * image_own, local_cols)
    image_term = lax.dot_general(key_low, wk_full, back_dims, preferred_element_type=jnp.float32)
    image_term = image_term + lax.dot_general(
        value_low, wv_full, back_dims, preferred_element_type=jnp.float32
    )
    image_term = image_term.reshape(samples, image_own, width)
    text_part, image_part = (
        lax.psum_scatter(
            text_term.astype(jnp.bfloat16), "tensor", scatter_dimension=2, tiled=True
        ).astype(jnp.float32),
        lax.psum_scatter(
            image_term.astype(jnp.bfloat16), "tensor", scatter_dimension=2, tiled=True
        ).astype(jnp.float32),
    )
    return (text_part.astype(jnp.bfloat16), image_part.astype(jnp.bfloat16), weight_grad)


def solution(mesh):
    return jax.shard_map(
        shards,
        mesh=mesh,
        in_specs=(
            P(None, "dp", None),
            P(None, "dp", None),
            P(None, "dp", None),
            P(),
            P("dp", "tensor"),
            P("dp", "tensor"),
            P("dp", "tensor"),
            P("tensor", "dp"),
        ),
        out_specs=(P(None, "dp", "tensor"), P(None, "dp", "tensor"), P("tensor", "dp")),
        check_vma=False,
    )
```

profile of v0, /device:TPU:4, one launch (start us, length us, event | category | flops | bytes accessed | tf_op | source)
XLA Modules:
  0.0 830.1 jit_solution(9635399581053093787)
XLA Ops:
  7.2 0.7 all-gather.9.cloned.1.call-update
  8.0 0.7 all-gather.11.cloned.1.call-update
  8.7 0.7 all-gather.5.cloned.1.call-update
  9.4 0.5 all-gather.7.cloned.1.call-update
  10.0 0.9 reshape.87
  10.9 0.7 broadcast_compare_fusion
  11.6 3.1 broadcast_select_fusion
  14.7 122.0 %all-gather.9.cloned.1.call-done = bf16[1024,4096]{1,0:T(8,128)(2,1)} async-done(((bf16[1024,512]{1,0:T(8,128)(2,1)}), bf16[1024,4096]{1,0:T(8,128)(2,1)}) %all-gather.9.cloned.1.call-update) | async-done | bytes 8388624 | tf_op jit(solution)/shard_map/all_gather | solution.py:39
  136.7 6.4 fusion.9
  143.1 0.1 copy.63
  143.2 118.8 %all-gather.11.cloned.1.call-done = bf16[4096,1024]{1,0:T(8,128)(2,1)} async-done(((bf16[512,1024]{1,0:T(8,128)(2,1)}), bf16[4096,1024]{1,0:T(8,128)(2,1)}) %all-gather.11.cloned.1.call-update) | async-done | bytes 8388624 | tf_op jit(solution)/shard_map/all_gather | solution.py:38
  262.0 4.6 convolution_convert_fusion.7
  266.6 31.6 %all_gather.23 = bf16[2,32,1024]{2,0,1:T(2,128)(2,1)S(1)} all-gather(bf16[2,4,1024]{2,0,1:T(2,128)(2,1)S(1)} %copy.34), channel_id=1, replica_groups=mesh['dp'=8,'tensor'=4] {'dp'}, dimensions={1}, use_global_device_ids=true | all-gather | bytes 147456 | tf_op jit(solution)/shard_map/all_gather | solution.py:51
  298.1 0.1 reshape.101
  298.2 90.0 %all-gather.5.cloned.1.call-done = bf16[4096,1024]{1,0:T(8,128)(2,1)} async-done(((bf16[512,1024]{1,0:T(8,128)(2,1)}), bf16[4096,1024]{1,0:T(8,128)(2,1)}) %all-gather.5.cloned.1.call-update) | async-done | bytes 8388624 | tf_op jit(solution)/shard_map/all_gather | solution.py:37
  388.2 4.6 convolution_convert_fusion.8
  392.8 31.5 %all_gather.19 = bf16[2,32,1024]{2,0,1:T(2,128)(2,1)S(1)} all-gather(bf16[2,4,1024]{2,0,1:T(2,128)(2,1)S(1)} %copy.30), channel_id=1, replica_groups=mesh['dp'=8,'tensor'=4] {'dp'}, dimensions={1}, use_global_device_ids=true | all-gather | bytes 147456 | tf_op jit(solution)/shard_map/all_gather | solution.py:50
  424.3 0.1 reshape.100
  424.4 89.8 %all-gather.7.cloned.1.call-done = bf16[4096,1024]{1,0:T(8,128)(2,1)} async-done(((bf16[512,1024]{1,0:T(8,128)(2,1)}), bf16[4096,1024]{1,0:T(8,128)(2,1)}) %all-gather.7.cloned.1.call-update) | async-done | bytes 8388624 | tf_op jit(solution)/shard_map/all_gather | solution.py:36
  514.2 5.7 fusion.8
  519.9 0.1 copy.62
  520.1 0.4 convolution_multiply_fusion
  520.4 0.7 fusion.42
  521.1 0.4 fusion.26
  521.5 0.3 fusion.18
  521.7 0.3 fusion.17
  522.0 0.7 copy.88
  522.7 0.7 copy.87
  523.4 0.2 reduce-scatter.12.cloned.1.call-start
  523.6 0.6 dynamic-slice
  524.9 0.3 fusion.10
  525.2 0.3 copy.45
  525.5 67.1 %all-reduce.5.cloned.1.call-done = (bf16[2,32,1024]{2,1,0:T(8,128)(2,1)}, bf16[2,32,1024]{2,1,0:T(8,128)(2,1)}) async-done(((bf16[2,32,1024]{2,1,0:T(8,128)(2,1)}, bf16[2,32,1024]{2,1,0:T(8,128)(2,1)}), (bf16[2,32,1024]{2,1,0:T(8,128)(2,1)}, bf16[2,32,1024]{2,1,0:T(8,128)(2,1)})) %all-reduce.5.cloned.1.call-update) | async-done | bytes 262160
  592.6 0.8 constant_dynamic-slice_fusion
  593.4 5.6 fusion.43
  599.1 5.8 fusion.7
  604.9 4.0 copy.58
  608.9 4.7 reshape.106
  613.7 5.6 convolution_convert_fusion
  619.4 0.3 reduce-scatter.8.cloned.1.call-start
  619.7 0.4 convolution_convert_fusion.4
  620.0 7.5 fusion.4
  627.5 9.4 %reduce-scatter.12.cloned.1.call-done = bf16[1024,8]{1,0:T(8,128)(2,1)} async-done(((bf16[4096,8]{1,0:T(8,128)(2,1)}), bf16[1024,8]{1,0:T(8,128)(2,1)}) %reduce-scatter.12.cloned.1.call-update) | async-done | bytes 16400
  636.9 1.2 reshape.107
  638.1 1.0 copy.59
  639.1 151.7 %reduce-scatter.10.cloned.1.call-done = bf16[512,1024]{1,0:T(8,128)(2,1)} async-done(((bf16[4096,1024]{1,0:T(8,128)(2,1)}), bf16[512,1024]{1,0:T(8,128)(2,1)}) %reduce-scatter.10.cloned.1.call-update) | async-done | bytes 1048592 | tf_op jit(solution)/shard_map/reduce_scatter | solution.py:69
  790.7 2.3 copy.46
  793.0 30.3 %reduce-scatter.8.cloned.1.call-done = bf16[2,128,1024]{2,1,0:T(8,128)(2,1)} async-done(((bf16[2,128,4096]{2,1,0:T(8,128)(2,1)}), bf16[2,128,1024]{2,1,0:T(8,128)(2,1)}) %reduce-scatter.8.cloned.1.call-update) | async-done | bytes 524304 | tf_op jit(solution)/shard_map/reduce_scatter | solution.py:117
  (26 shorter events, 0.5 us)
Async XLA Ops:
  7.2 507.1 %copy-start = (bf16[2,128,4096]{2,1,0:T(8,128)(2,1)S(1)}, bf16[2,128,4096]{2,1,0:T(8,128)(2,1)}, u32[]{:S(2)}) copy-start(bf16[2,128,4096]{2,1,0:T(8,128)(2,1)} %param.8) | copy-start | bytes 6291460
  7.2 129.5 %all-gather.9.cloned.1.call-start = ((), (), s32[]{:S(2)}) async-start(), calls=%async_computation.5 | async-start | bytes 9437184 | tf_op jit(solution)/shard_map/all_gather | solution.py:39
  7.9 254.0 %all-gather.11.cloned.1.call-start = ((), (), s32[]{:S(2)}) async-start(), calls=%async_computation.6 | async-start | bytes 9437184 | tf_op jit(solution)/shard_map/all_gather | solution.py:38
  8.7 379.5 %all-gather.5.cloned.1.call-start = ((), (), s32[]{:S(2)}) async-start(), calls=%async_computation.3 | async-start | bytes 9437184 | tf_op jit(solution)/shard_map/all_gather | solution.py:37
  9.4 504.8 %all-gather.7.cloned.1.call-start = ((), (), s32[]{:S(2)}) async-start(), calls=%async_computation.4 | async-start | bytes 9437184 | tf_op jit(solution)/shard_map/all_gather | solution.py:36
  10.0 582.6 %all-reduce.5.cloned.1.call-start = ((), (), s32[]{:S(2)}) async-start(), calls=%async_computation.10 | async-start | bytes 524288
  514.2 9.4 %copy-start.3 = (u32[32]{0:T(128)S(1)}, u32[32]{0:T(128)}, u32[]{:S(2)}) copy-start(u32[32]{0:T(128)} %constant.19) | copy-start | bytes 388
  523.4 113.5 %reduce-scatter.12.cloned.1.call-start = ((), (), s32[]{:S(2)}) async-start(), calls=%async_computation.9 | async-start | bytes 1310720
  599.1 14.7 %copy-start.2 = (bf16[2,128,4096]{2,1,0:T(8,128)(2,1)S(1)}, bf16[2,128,4096]{2,1,0:T(8,128)(2,1)}, u32[]{:S(2)}) copy-start(bf16[2,128,4096]{2,1,0:T(8,128)(2,1)} %broadcast_select_fusion) | copy-start | bytes 6291460
  613.7 177.0 %reduce-scatter.10.cloned.1.call-start = ((), (), s32[]{:S(2)}) async-start(), calls=%async_computation.8 | async-start | bytes 9437184 | tf_op jit(solution)/shard_map/reduce_scatter | solution.py:69
  619.4 203.9 %reduce-scatter.8.cloned.1.call-start = ((), (), s32[]{:S(2)}) async-start(), calls=%async_computation.7 | async-start | bytes 2621440 | tf_op jit(solution)/shard_map/reduce_scatter | solution.py:117
  620.0 203.3 %copy-start.1 = (bf16[2,128,4096]{2,1,0:T(8,128)(2,1)S(1)}, bf16[2,128,4096]{2,1,0:T(8,128)(2,1)}, u32[]{:S(2)}) copy-start(bf16[2,128,4096]{2,1,0:T(8,128)(2,1)} %param.8) | copy-start | bytes 6291460
Sparse Core Ops, SparseCore 0:
  10.1 126.5 all-gather.8
  138.8 123.0 all-gather.10
  264.1 124.0 all-gather.4
  390.2 124.0 all-gather.6
  523.5 69.0 all-reduce.4
  613.8 23.0 reduce-scatter.11
  640.5 150.1 reduce-scatter.9
  794.0 29.2 reduce-scatter.7
where the time goes:
time: 833 us; the launch traced here: 830 us
  waiting for transfers between devices  682 us (82%)
  blocking collectives  63 us (8%)
  matrix products  47.8 us (6%)
  local copies, waits for them, and re-layouts  17.6 us (2%)
  between operations  15 us (2%)
    reduce_scatter x1, waiting for transfers between devices, shards(): lax.psum_scatter(lax.dot_general(live_flat, attended, (((0,), (0,)), ((),...  152 us
    all_gather x1, waiting for transfers between devices, shards(): lax.all_gather(out_weight, 'dp', axis=1, tiled=True)  122 us
    all_gather x1, waiting for transfers between devices, shards(): lax.all_gather(value_weight, 'dp', axis=0, tiled=True)  119 us
    all_gather x1, waiting for transfers between devices, shards(): lax.all_gather(key_weight, 'dp', axis=0, tiled=True)  90 us
    all_gather x1, waiting for transfers between devices, shards(): lax.all_gather(query_weight, 'dp', axis=0, tiled=True)  89.8 us
    unnamed x10, waiting for transfers between devices  79.1 us
    all_gather x1, blocking collectives, shards(): lax.all_gather(values_own, 'dp', axis=1, tiled=True)  31.6 us
    all_gather x1, blocking collectives, shards(): lax.all_gather(keys_own, 'dp', axis=1, tiled=True)  31.5 us
  transfers between devices with their start and end apart: 8, of which 8 were waited for; matrix products, arithmetic and copies ran while one was open for 5% of the time, Pallas kernels for 0%

commit v1 on v0

v1 whole, which is shorter than its diff:
```python
import jax
import jax.numpy as jnp
from jax import lax
from jax.sharding import PartitionSpec as P

HEAD_DIM = 128
F32 = jnp.float32
BF16 = jnp.bfloat16
BACK = (((1,), (1,)), ((), ()))


def softmax_rows(scores):
    peak = jnp.max(scores, axis=-1, keepdims=True)
    expo = jnp.exp(scores - peak)
    return expo / jnp.sum(expo, axis=-1, keepdims=True)


def low(values):
    return lax.reduce_precision(values, 8, 7)


def shards(
    text_states,
    image_states,
    out_grad,
    text_lengths,
    query_weight,
    key_weight,
    value_weight,
    out_weight,
):
    score_scale = HEAD_DIM ** (-0.5)
    samples, tok_rows, width = text_states.shape
    image_own = image_states.shape[1]
    n_dp = lax.axis_size("dp")
    n_tensor = lax.axis_size("tensor")
    rows = samples * tok_rows
    image_rows = samples * image_own
    local_cols = query_weight.shape[1]
    own_width = query_weight.shape[0]
    head_count = local_cols // HEAD_DIM
    image_count = n_dp * image_own

    wq_full = lax.all_gather(query_weight, "dp", axis=0, tiled=True)
    wo_full = lax.all_gather(out_weight, "dp", axis=1, tiled=True)

    first_row = lax.axis_index("dp") * tok_rows
    positions = first_row + lax.iota(jnp.int32, tok_rows)
    live_rows = positions[None, :] < text_lengths[:, None]
    grad_live = jnp.where(live_rows[..., None], out_grad, jnp.zeros_like(out_grad))
    text_flat = text_states.reshape(rows, width)
    live_flat = grad_live.reshape(rows, width)

    image_flat = image_states.reshape(image_rows, width)
    image_cols = lax.all_to_all(image_flat, "dp", split_axis=1, concat_axis=0, tiled=True)
    part_kv = jnp.concatenate(
        [
            jnp.dot(image_cols, key_weight, preferred_element_type=F32),
            jnp.dot(image_cols, value_weight, preferred_element_type=F32),
        ],
        axis=1,
    )
    part_kv = part_kv.reshape(n_dp, image_rows, 2 * local_cols)
    kv_own = jnp.sum(lax.all_to_all(part_kv, "dp", split_axis=0, concat_axis=0), axis=0)
    kv_all = lax.all_gather(kv_own.astype(BF16), "dp", axis=0)
    kv_all = kv_all.reshape(n_dp, samples, image_own, 2, head_count, HEAD_DIM)
    kv_all = kv_all.transpose(3, 1, 0, 2, 4, 5).reshape(
        2, samples, image_count, head_count, HEAD_DIM
    )
    key_heads, value_heads = kv_all[0], kv_all[1]

    queries = jnp.dot(text_flat, wq_full, preferred_element_type=F32).astype(BF16)
    query_heads = queries.reshape(samples, tok_rows, head_count, HEAD_DIM)
    scores = (
        jnp.einsum("sthd,sjhd->shtj", query_heads, key_heads, preferred_element_type=F32)
        * score_scale
    )
    soft_prob = softmax_rows(scores)
    prob_low = soft_prob.astype(BF16)
    attended = jnp.einsum("shtj,sjhd->sthd", prob_low, value_heads, preferred_element_type=F32)
    attended = attended.astype(BF16).reshape(rows, local_cols)

    live_cols = lax.all_to_all(live_flat, "dp", split_axis=1, concat_axis=0, tiled=True)
    live_cols = live_cols.reshape(n_dp, rows, own_width)
    attended_all = lax.all_gather(attended, "dp", axis=0)
    partial = lax.dot_general(
        attended_all, live_cols, (((1,), (1,)), ((0,), (0,))), preferred_element_type=F32
    )
    weight_grad = jnp.sum(low(partial), axis=0).astype(BF16)

    attended_grad = lax.dot_general(live_flat, wo_full, BACK, preferred_element_type=F32)
    grad_heads = attended_grad.astype(BF16).reshape(samples, tok_rows, head_count, HEAD_DIM)
    value_part = jnp.einsum("shtj,sthd->sjhd", prob_low, grad_heads, preferred_element_type=F32)
    prob_grad = jnp.einsum(
        "sthd,sjhd->shtj", grad_heads, value_heads, preferred_element_type=F32
    )
    row_delta = jnp.sum(soft_prob * prob_grad, axis=-1, keepdims=True)
    score_grad = (soft_prob * (prob_grad - row_delta) * score_scale).astype(BF16)
    query_grad = jnp.einsum(
        "shtj,sjhd->sthd", score_grad, key_heads, preferred_element_type=F32
    ).astype(BF16)
    key_part = jnp.einsum("shtj,sthd->sjhd", score_grad, query_heads, preferred_element_type=F32)

    query_grad = query_grad.reshape(rows, local_cols)
    text_term = lax.dot_general(query_grad, wq_full, BACK, preferred_element_type=F32)
    text_term = text_term.astype(BF16)
    text_parts = lax.all_to_all(
        text_term.reshape(rows, n_tensor, width // n_tensor), "tensor", split_axis=1, concat_axis=0
    )
    text_grad = jnp.sum(text_parts.astype(F32), axis=0).astype(BF16)
    text_grad = text_grad.reshape(samples, tok_rows, width // n_tensor)

    kv_part = jnp.stack([key_part, value_part], axis=2)
    kv_part = kv_part.reshape(samples, n_dp, image_own, 2 * local_cols).transpose(1, 0, 2, 3)
    kv_part = kv_part.reshape(n_dp, image_rows, 2 * local_cols)
    kv_grad = jnp.sum(lax.all_to_all(kv_part, "dp", split_axis=0, concat_axis=0), axis=0)
    kv_grad_all = lax.all_gather(kv_grad.astype(BF16), "dp", axis=0, tiled=True)
    key_low, value_low = kv_grad_all[:, :local_cols], kv_grad_all[:, local_cols:]
    image_term = lax.dot_general(key_low, key_weight, BACK, preferred_element_type=F32)
    image_term = image_term + lax.dot_general(
        value_low, value_weight, BACK, preferred_element_type=F32
    )
    image_term = lax.all_to_all(
        image_term.astype(BF16), "dp", split_axis=0, concat_axis=1, tiled=True
    )
    image_parts = lax.all_to_all(
        image_term.reshape(image_rows, n_tensor, width // n_tensor),
        "tensor",
        split_axis=1,
        concat_axis=0,
    )
    image_grad = jnp.sum(image_parts.astype(F32), axis=0).astype(BF16)
    image_grad = image_grad.reshape(samples, image_own, width // n_tensor)
    return text_grad, image_grad, weight_grad


def solution(mesh):
    return jax.shard_map(
        shards,
        mesh=mesh,
        in_specs=(
            P(None, "dp", None),
            P(None, "dp", None),
            P(None, "dp", None),
            P(),
            P("dp", "tensor"),
            P("dp", "tensor"),
            P("dp", "tensor"),
            P("tensor", "dp"),
        ),
        out_specs=(P(None, "dp", "tensor"), P(None, "dp", "tensor"), P("tensor", "dp")),
        check_vma=False,
    )
```

time: 833 us -> 478 us (0.57)
  waiting for transfers between devices: 682 us -> 287 us
  starting transfers between devices: 0.72 us -> 31.1 us
    all_gather x4 -> x3, waiting for transfers between devices: 421 us -> 177 us  [the longest x1 118 us: shards(): wq_full = lax.all_gather(query_weight, 'dp', axis=0, tiled=True)]
    reduce_scatter x2 -> x0, waiting for transfers between devices: 182 us -> none  [the longest x1 152 us: shards(): lax.psum_scatter(lax.dot_general(live_flat, attended, (((0,), (0,)), ((),...]
    all_to_all x0 -> x7, waiting for transfers between devices: none -> 108 us  [the longest x1 45 us: shards(): lax.all_to_all(live_flat, 'dp', split_axis=1, concat_axis=0, tiled=True)]
    unnamed x10 -> x3, waiting for transfers between devices: 79.1 us -> 1.39 us
    all_to_all x0 -> x7, starting transfers between devices: none -> 31 us  [the longest x1 5.81 us: shards(): lax.all_to_all(image_flat, 'dp', split_axis=1, concat_axis=0, tiled=True)]
    dot_general x8, matrix products: 45.8 us -> 30.3 us  [the longest x1 7.12 us: shards(): lax.dot_general(query_grad, wq_full, BACK, preferred_element_type=F32)]
    another operation x0 -> x4, local copies, waits for them, and re-layouts: none -> 11.3 us  [the longest x2 8.09 us: shards(): lax.all_to_all(text_term.reshape(rows, n_tensor, width // n_tensor), 'ten...]
    unnamed x17 -> x18, local copies, waits for them, and re-layouts: 14.7 us -> 3.55 us
  transfers between devices with their start and end apart: 8 -> 10, of which waited for: 8 -> 8; matrix products, arithmetic and copies ran while one was open for 5% -> 11% of each run, Pallas kernels for 0% -> 0%
where the time goes in v1:
time: 478 us; the launch traced here: 475 us
  waiting for transfers between devices  287 us (60%)
  blocking collectives  65.7 us (14%)
  matrix products  39.8 us (8%)
  starting transfers between devices  31.1 us (7%)
  local copies, waits for them, and re-layouts  25.9 us (5%)
  between operations  14 us (3%)
  other arithmetic  11 us (2%)
    all_gather x1, waiting for transfers between devices, shards(): wq_full = lax.all_gather(query_weight, 'dp', axis=0, tiled=True)  118 us
    all_gather x1, waiting for transfers between devices, shards(): wo_full = lax.all_gather(out_weight, 'dp', axis=1, tiled=True)  59.1 us
    all_to_all x1, waiting for transfers between devices, shards(): lax.all_to_all(live_flat, 'dp', split_axis=1, concat_axis=0, tiled=True)  45 us
    all_gather x1, blocking collectives, shards(): kv_all = lax.all_gather(kv_own.astype(BF16), 'dp', axis=0)  34.2 us
    all_gather x1, blocking collectives, shards(): kv_grad_all = lax.all_gather(kv_grad.astype(BF16), 'dp', axis=0, tiled=True)  31.5 us
    all_to_all x1, waiting for transfers between devices, shards(): lax.all_to_all(part_kv, 'dp', split_axis=0, concat_axis=0)  23.1 us
    all_to_all x1, waiting for transfers between devices, shards(): lax.all_to_all(text_term.reshape(rows, n_tensor, width // n_tensor), 'ten...  19.6 us
  transfers between devices with their start and end apart: 10, of which 8 were waited for; matrix products, arithmetic and copies ran while one was open for 11% of the time, Pallas kernels for 0%

profile of v1, /device:TPU:4, one launch (start us, length us, event | category | flops | bytes accessed | tf_op | source)
XLA Modules:
  0.0 474.7 jit_solution(2607134326900987189)
XLA Ops:
  8.0 0.7 all-gather.5.cloned.1.call-update
  9.4 5.8 %all-to-all-start = ((bf16[8,8,512]{2,0,1:T(8,128)(2,1)}), bf16[8,8,512]{2,0,1:T(8,128)(2,1)S(1)}, u32[]{:S(2)}, u32[]{:S(2)}) async-start(bf16[8,8,512]{2,0,1:T(8,128)(2,1)} %copy.42), calls=%async_computation | async-start | bytes 131072 | tf_op jit(solution)/shard_map/all_to_all | solution.py:55
  15.3 6.8 %all-to-all-done = bf16[8,8,512]{2,0,1:T(8,128)(2,1)S(1)} async-done(((bf16[8,8,512]{2,0,1:T(8,128)(2,1)}), bf16[8,8,512]{2,0,1:T(8,128)(2,1)S(1)}, u32[]{:S(2)}, u32[]{:S(2)}) %all-to-all-start) | async-done | bytes 65568 | tf_op jit(solution)/shard_map/all_to_all | solution.py:55
  22.1 1.6 fusion.31
  24.0 0.8 maximum_bitcast_fusion
  24.8 4.1 all-to-all-start.1
  29.0 3.2 broadcast_select_fusion
  32.1 23.1 %all-to-all-done.1 = f32[8,8,2048]{2,1,0:T(8,128)} async-done(((f32[8,8,2048]{2,1,0:T(8,128)}), f32[8,8,2048]{2,1,0:T(8,128)}, u32[]{:S(2)}, u32[]{:S(2)}) %all-to-all-start.1) | async-done | bytes 524320 | tf_op jit(solution)/shard_map/all_to_all | solution.py:64
  55.3 1.1 reduce_sum.69
  56.3 34.2 %all-gather = bf16[64,2048]{1,0:T(8,128)(2,1)S(1)} all-gather(bf16[8,2048]{1,0:T(8,128)(2,1)S(1)} %reduce_sum.69), channel_id=2, replica_groups=mesh['dp'=8,'tensor'=4] {'dp'}, dimensions={0}, use_global_device_ids=true | all-gather | bytes 294912 | tf_op jit(solution)/shard_map/all_gather | solution.py:65
  90.7 0.7 copy.45
  91.4 59.1 %all-gather.7.cloned.1.call-done = bf16[1024,4096]{1,0:T(8,128)(2,1)} async-done(((bf16[1024,512]{1,0:T(8,128)(2,1)}), bf16[1024,4096]{1,0:T(8,128)(2,1)}) %all-gather.7.cloned.1.call-update) | async-done | bytes 8388624 | tf_op jit(solution)/shard_map/all_gather | solution.py:45
  150.5 6.4 %fusion.4 = bf16[32,8,8,128]{3,1,2,0:T(8,128)(2,1)S(1)} fusion(bf16[256,4096]{1,0:T(8,128)(2,1)} %bitcast.79, bf16[1024,4096]{1,0:T(8,128)(2,1)} %all-gather.7.cloned.1.call-done), kind=kOutput, calls=%fused_computation.11 | convolution fusion | flops 2147745792 | bytes 11010048 | tf_op jit(solution)/shard_map/dot_general | solution.py:91
  156.9 0.9 copy.62
  157.8 118.2 %all-gather.5.cloned.1.call-done = bf16[4096,1024]{1,0:T(8,128)(2,1)} async-done(((bf16[512,1024]{1,0:T(8,128)(2,1)}), bf16[4096,1024]{1,0:T(8,128)(2,1)}) %all-gather.5.cloned.1.call-update) | async-done | bytes 8388624 | tf_op jit(solution)/shard_map/all_gather | solution.py:44
  276.0 5.7 %fusion.3 = bf16[32,8,8,128]{3,1,2,0:T(8,128)(2,1)S(1)} fusion(bf16[256,4096]{1,0:T(8,128)(2,1)S(1)} %bitcast.78, bf16[4096,1024]{1,0:T(8,128)(2,1)} %all-gather.5.cloned.1.call-done), kind=kOutput, calls=%fused_computation.10 | convolution fusion | flops 2147745792 | bytes 11010048 | tf_op jit(solution)/shard_map/dot_general | solution.py:72
  282.2 0.8 fusion.42
  283.0 1.1 fusion.22
  284.1 2.0 convolution_bitcast_fusion
  286.1 2.3 convolution_bitcast_fusion.1
  288.4 1.1 pad_maximum_fusion
  289.5 1.1 copy.51
  290.6 2.0 reshape.112
  292.6 1.3 copy.52
  294.0 1.1 copy.53
  295.1 4.1 all-to-all-start.3
  299.3 2.1 fusion.6
  301.3 2.2 copy.56
  303.5 2.1 all_gather_reshape.3
  305.5 8.0 %all-to-all-done.3 = f32[8,8,2048]{2,1,0:T(8,128)} async-done(((f32[8,8,2048]{2,1,0:T(8,128)}), f32[8,8,2048]{2,1,0:T(8,128)}, u32[]{:S(2)}, u32[]{:S(2)}) %all-to-all-start.3) | async-done | bytes 524320 | tf_op jit(solution)/shard_map/all_to_all | solution.py:116
  313.6 1.1 reduce_sum.73
  314.7 31.5 %all_gather.19 = bf16[64,2048]{1,0:T(8,128)(2,1)S(1)} all-gather(bf16[8,2048]{1,0:T(8,128)(2,1)S(1)} %reduce_sum.73), channel_id=1, replica_groups=mesh['dp'=8,'tensor'=4] {'dp'}, dimensions={0}, use_global_device_ids=true | all-gather | bytes 294912 | tf_op jit(solution)/shard_map/all_gather | solution.py:117
  346.6 2.3 fusion.14
  349.0 4.0 all-to-all-start.4
  352.9 1.6 fusion.5
  354.8 5.9 %all-to-all-done.4 = bf16[8,8,512]{2,1,0:T(8,128)(2,1)} async-done(((bf16[8,8,512]{2,1,0:T(8,128)(2,1)}), bf16[8,8,512]{2,1,0:T(8,128)(2,1)}, u32[]{:S(2)}, u32[]{:S(2)}) %all-to-all-start.4) | async-done | bytes 65568 | tf_op jit(solution)/shard_map/all_to_all | solution.py:123
  360.7 3.9 all-to-all-start.5
  364.6 7.1 %convolution_convert_fusion = bf16[256,4096]{1,0:T(8,128)(2,1)} fusion(bf16[4096,1024]{1,0:T(8,128)(2,1)} %all-gather.5.cloned.1.call-done, bf16[32,8,8,128]{3,2,1,0:T(8,128)(2,1)S(1)} %bitcast.94), kind=kOutput, calls=%fused_computation.3 | convolution fusion | flops 2148532224 | bytes 11010048 | tf_op jit(solution)/shard_map/dot_general | solution.py:105
  371.8 4.5 broadcast_in_dim_reshape.6
  376.3 3.6 copy.48
  379.9 4.6 all-to-all-start.2
  384.5 2.5 copy.64
  387.0 2.0 copy.57
  389.0 19.6 %all-to-all-done.2 = bf16[1,256,4,1024]{3,1,0,2:T(8,128)(2,1)} async-done(((bf16[1,256,4,1024]{3,1,0,2:T(8,128)(2,1)}), bf16[1,256,4,1024]{3,1,0,2:T(8,128)(2,1)}, u32[]{:S(2)}, u32[]{:S(2)}) %all-to-all-start.2) | async-done | bytes 2097184 | tf_op jit(solution)/shard_map/all_to_all | solution.py:107
  408.6 4.4 all-to-all-start.6
  413.6 2.9 reduce_sum.72
  416.6 45.0 %all-to-all-done.6 = bf16[256,8,512]{2,0,1:T(8,128)(2,1)} async-done(((bf16[256,8,512]{2,0,1:T(8,128)(2,1)}), bf16[256,8,512]{2,0,1:T(8,128)(2,1)}, u32[]{:S(2)}, u32[]{:S(2)}) %all-to-all-start.6) | async-done | bytes 2097184 | tf_op jit(solution)/shard_map/all_to_all | solution.py:83
  461.6 6.5 %reduce-precision_reduce_fusion = bf16[1024,512]{1,0:T(8,128)(2,1)} fusion(bf16[8,256,1024]{2,1,0:T(8,128)(2,1)} %all-gather.9.cloned.1.call-done, bf16[256,8,512]{2,0,1:T(8,128)(2,1)} %all-to-all-done.6), kind=kOutput, calls=%fused_computation.2 | convolution fusion | flops 2155347968 | bytes 7340032 | tf_op jit(solution)/shard_map/dot_general | solution.py:86
  (35 shorter events, 3.9 us)
Async XLA Ops:
  7.2 268.9 %copy-start = (bf16[2,128,4096]{2,1,0:T(8,128)(2,1)S(1)}, bf16[2,128,4096]{2,1,0:T(8,128)(2,1)}, u32[]{:S(2)}) copy-start(bf16[2,128,4096]{2,1,0:T(8,128)(2,1)} %param.8) | copy-start | bytes 6291460
  7.2 1.5 copy-start.5
  7.2 8.0 %copy-start.6 = (s32[2]{0:T(128)S(1)}, s32[2]{0:T(128)}, u32[]{:S(2)}) copy-start(s32[2]{0:T(128)} %param.11) | copy-start | bytes 28
  7.2 16.5 %copy-start.1 = (bf16[512,1024]{1,0:T(8,128)(2,1)S(1)}, bf16[512,1024]{1,0:T(8,128)(2,1)}, u32[]{:S(2)}) copy-start(bf16[512,1024]{1,0:T(8,128)(2,1)} %param.13) | copy-start | bytes 3145732
  7.2 143.3 %all-gather.7.cloned.1.call-start = ((), (), s32[]{:S(2)}) async-start(), calls=%async_computation.8 | async-start | bytes 9437184 | tf_op jit(solution)/shard_map/all_gather | solution.py:45
  7.9 268.1 %all-gather.5.cloned.1.call-start = ((), (), s32[]{:S(2)}) async-start(), calls=%async_computation.7 | async-start | bytes 9437184 | tf_op jit(solution)/shard_map/all_gather | solution.py:44
  9.4 12.7 %all-to-all-start = ((bf16[8,8,512]{2,0,1:T(8,128)(2,1)}), bf16[8,8,512]{2,0,1:T(8,128)(2,1)S(1)}, u32[]{:S(2)}, u32[]{:S(2)}) async-start(bf16[8,8,512]{2,0,1:T(8,128)(2,1)} %copy.42), calls=%async_computation | async-start | bytes 131072 | tf_op jit(solution)/shard_map/all_to_all | solution.py:55
  24.8 30.4 %all-to-all-start.1 = ((f32[8,8,2048]{2,1,0:T(8,128)}), f32[8,8,2048]{2,1,0:T(8,128)}, u32[]{:S(2)}, u32[]{:S(2)}) async-start(f32[8,8,2048]{2,1,0:T(8,128)} %maximum_bitcast_fusion), calls=%async_computation.1 | async-start | bytes 1048576 | tf_op jit(solution)/shard_map/all_to_all | solution.py:64
  281.7 1.3 copy-start.2
  281.7 1.3 copy-start.4
  281.9 2.2 copy-start.3
  295.1 18.5 %all-to-all-start.3 = ((f32[8,8,2048]{2,1,0:T(8,128)}), f32[8,8,2048]{2,1,0:T(8,128)}, u32[]{:S(2)}, u32[]{:S(2)}) async-start(f32[8,8,2048]{2,1,0:T(8,128)} %copy.53), calls=%async_computation.3 | async-start | bytes 1048576 | tf_op jit(solution)/shard_map/all_to_all | solution.py:116
  299.2 162.4 %all-gather.9.cloned.1.call-start = ((), (), s32[]{:S(2)}) async-start(), calls=%async_computation.9 | async-start | bytes 4718592 | tf_op jit(solution)/shard_map/all_gather | solution.py:85
  349.0 11.8 %all-to-all-start.4 = ((bf16[8,8,512]{2,1,0:T(8,128)(2,1)}), bf16[8,8,512]{2,1,0:T(8,128)(2,1)}, u32[]{:S(2)}, u32[]{:S(2)}) async-start(bf16[8,8,512]{2,1,0:T(8,128)(2,1)} %fusion.14), calls=%async_computation.4 | async-start | bytes 131072 | tf_op jit(solution)/shard_map/all_to_all | solution.py:123
  360.7 19.2 %all-to-all-start.5 = ((bf16[1,8,4,1024]{3,1,0,2:T(8,128)(2,1)}), bf16[1,8,4,1024]{3,1,0,2:T(8,128)(2,1)S(1)}, u32[]{:S(2)}, u32[]{:S(2)}) async-start(bf16[1,8,4,1024]{3,1,0,2:T(8,128)(2,1)} %bitcast.19), calls=%async_computation.5 | async-start | bytes 131072 | tf_op jit(solution)/shard_map/all_to_all | solution.py:126
  379.9 28.8 %all-to-all-start.2 = ((bf16[1,256,4,1024]{3,1,0,2:T(8,128)(2,1)}), bf16[1,256,4,1024]{3,1,0,2:T(8,128)(2,1)}, u32[]{:S(2)}, u32[]{:S(2)}) async-start(bf16[1,256,4,1024]{3,1,0,2:T(8,128)(2,1)} %copy.48), calls=%async_computation.2 | async-start | bytes 4194304 | tf_op jit(solution)/shard_map/all_to_all | solution.py:107
  408.6 52.9 %all-to-all-start.6 = ((bf16[256,8,512]{2,0,1:T(8,128)(2,1)}), bf16[256,8,512]{2,0,1:T(8,128)(2,1)}, u32[]{:S(2)}, u32[]{:S(2)}) async-start(bf16[256,8,512]{2,0,1:T(8,128)(2,1)} %copy.57), calls=%async_computation.6 | async-start | bytes 4194304 | tf_op jit(solution)/shard_map/all_to_all | solution.py:83
Sparse Core Ops, SparseCore 0:
  10.1 140.3 all-gather.6
  152.6 123.3 all-gather.4
  305.7 77.3 all-gather.8

commit v2 on v1

--- a/solution.py
+++ b/solution.py
@@ -17,6 +17,68 @@
 
 def low(values):
     return lax.reduce_precision(values, 8, 7)
+
+
+def after(values, *others):
+    return lax.optimization_barrier((values, *others))[0]
+
+
+class Line:
+    def __init__(self):
+        self.n_dp = lax.axis_size("dp")
+        self.n_z = self.n_dp // 2
+        self.place = lax.axis_index("dp")
+        self.z = self.place // 2
+        self.x = self.place % 2
+
+    def move(self, block, moves):
+        pairs = [(2 * a + e, 2 * b + e) for a, b in moves for e in range(2)]
+        return lax.ppermute(block, "dp", pairs)
+
+    def swap(self, block, planes=None):
+        planes = range(self.n_z) if planes is None else planes
+        pairs = [(2 * a + e, 2 * a + 1 - e) for a in planes for e in range(2)]
+        return lax.ppermute(block, "dp", pairs)
+
+    def along(self, block):
+        n = self.n_z
+        if n != 4:
+            shifted = [self.move(block, [((a + m) % n, a) for a in range(n)]) for m in range(1, n)]
+            return [(block, None)] + [(values, None) for values in shifted]
+        above = self.move(block, [(1, 0), (2, 1), (3, 2)])
+        below = self.move(block, [(0, 1), (1, 2), (2, 3)])
+        across = self.move(block, [(0, 2), (1, 3), (2, 0), (3, 1)])
+        edge = self.move(across, [(1, 0), (2, 3)])
+        return [
+            (block, None),
+            (above, (0, 1, 2)),
+            (across, None),
+            (below, (1, 2, 3)),
+            (edge, (0, 3)),
+        ]
+
+    def pick(self, raw):
+        if self.n_z != 4:
+            return raw
+        own, above, across, below, edge = raw
+        return [
+            own,
+            jnp.where(self.z == 3, edge, above),
+            across,
+            jnp.where(self.z == 0, edge, below),
+        ]
+
+    def rolled(self, values, axis):
+        doubled = jnp.concatenate([values, values], axis=axis)
+        return lax.dynamic_slice_in_dim(doubled, self.z, self.n_z, axis)
+
+    def unrolled(self, values, axis):
+        doubled = jnp.concatenate([values, values], axis=axis)
+        start = lax.rem(self.n_z - self.z, self.n_z)
+        return lax.dynamic_slice_in_dim(doubled, start, self.n_z, axis)
+
+    def own_first(self, values, axis):
+        return jnp.where(self.x == 0, values, jnp.flip(values, axis))
 
 
 def shards(
@@ -32,17 +94,20 @@
     score_scale = HEAD_DIM ** (-0.5)
     samples, tok_rows, width = text_states.shape
     image_own = image_states.shape[1]
-    n_dp = lax.axis_size("dp")
+    line = Line()
+    n_dp, n_z = line.n_dp, line.n_z
     n_tensor = lax.axis_size("tensor")
+    core = lax.axis_index("tensor") % 2
     rows = samples * tok_rows
     image_rows = samples * image_own
     local_cols = query_weight.shape[1]
     own_width = query_weight.shape[0]
     head_count = local_cols // HEAD_DIM
     image_count = n_dp * image_own
-
-    wq_full = lax.all_gather(query_weight, "dp", axis=0, tiled=True)
-    wo_full = lax.all_gather(out_weight, "dp", axis=1, tiled=True)
+    half_cols = local_cols // 2
+
+    def core_swap(block):
+        return lax.ppermute(block, "tensor", [(t, t ^ 1) for t in range(n_tensor)])
 
     first_row = lax.axis_index("dp") * tok_rows
     positions = first_row + lax.iota(jnp.int32, tok_rows)
@@ -50,6 +115,26 @@
     grad_live = jnp.where(live_rows[..., None], out_grad, jnp.zeros_like(out_grad))
     text_flat = text_states.reshape(rows, width)
     live_flat = grad_live.reshape(rows, width)
+
+    wq_raw = line.along(query_weight)
+    wq_other = [line.swap(values, planes) for values, planes in wq_raw]
+    wq_slots = list(zip(line.pick([values for values, _ in wq_raw]), line.pick(wq_other)))
+
+    wo_keep = lax.dynamic_slice_in_dim(out_weight, line.x * half_cols, half_cols, 0)
+    wo_send = lax.dynamic_slice_in_dim(out_weight, (1 - line.x) * half_cols, half_cols, 0)
+    wo_pair = jnp.concatenate([wo_keep, line.swap(wo_send)], axis=1)
+    wo_pair = after(wo_pair, wq_raw[2][0])
+    wo_raw = line.along(wo_pair)
+    wo_slots = line.pick([values for values, _ in wo_raw])
+
+    live_half = lax.dynamic_slice_in_dim(live_flat, core * (width // 2), width // 2, 1)
+    half_here = line.swap(live_half)
+    half_there = core_swap(half_here)
+    live_other = jnp.where(
+        core == 0,
+        jnp.concatenate([half_here, half_there], axis=1),
+        jnp.concatenate([half_there, half_here], axis=1),
+    )
 
     image_flat = image_states.reshape(image_rows, width)
     image_cols = lax.all_to_all(image_flat, "dp", split_axis=1, concat_axis=0, tiled=True)
@@ -62,14 +147,28 @@
     )
     part_kv = part_kv.reshape(n_dp, image_rows, 2 * local_cols)
     kv_own = jnp.sum(lax.all_to_all(part_kv, "dp", split_axis=0, concat_axis=0), axis=0)
-    kv_all = lax.all_gather(kv_own.astype(BF16), "dp", axis=0)
+
+    def everywhere(values):
+        copies = jnp.broadcast_to(values[None], (n_dp, *values.shape))
+        return lax.all_to_all(copies, "dp", split_axis=0, concat_axis=0)
+
+    kv_all = everywhere(kv_own.astype(BF16))
     kv_all = kv_all.reshape(n_dp, samples, image_own, 2, head_count, HEAD_DIM)
     kv_all = kv_all.transpose(3, 1, 0, 2, 4, 5).reshape(
         2, samples, image_count, head_count, HEAD_DIM
     )
     key_heads, value_heads = kv_all[0], kv_all[1]
 
-    queries = jnp.dot(text_flat, wq_full, preferred_element_type=F32).astype(BF16)
+    def relative(values):
+        cut = values.reshape(values.shape[0], n_z, 2, own_width)
+        return line.own_first(line.rolled(cut, 1), 2)
+
+    text_rel = relative(text_flat)
+    queries = 0.0
+    for m in range(n_z):
+        for e in range(2):
+            queries += jnp.dot(text_rel[:, m, e], wq_slots[m][e], preferred_element_type=F32)
+    queries = queries.astype(BF16)
     query_heads = queries.reshape(samples, tok_rows, head_count, HEAD_DIM)
     scores = (
         jnp.einsum("sthd,sjhd->shtj", query_heads, key_heads, preferred_element_type=F32)
@@ -80,16 +179,45 @@
     attended = jnp.einsum("shtj,sjhd->sthd", prob_low, value_heads, preferred_element_type=F32)
     attended = attended.astype(BF16).reshape(rows, local_cols)
 
-    live_cols = lax.all_to_all(live_flat, "dp", split_axis=1, concat_axis=0, tiled=True)
-    live_cols = live_cols.reshape(n_dp, rows, own_width)
-    attended_all = lax.all_gather(attended, "dp", axis=0)
+    half_rows = rows // 2
+    own_half = lax.dynamic_slice_in_dim(live_flat, core * half_rows, half_rows, 0)
+    own_half = after(own_half, wo_raw[2][0])
+    cols_here = lax.all_to_all(
+        own_half.reshape(half_rows, n_dp, own_width), "dp", split_axis=1, concat_axis=0
+    )
+    cols_here = cols_here.reshape(n_dp, half_rows, own_width)
+    live_cols = jnp.concatenate([cols_here, core_swap(cols_here)], axis=1)
+    live_cols = live_cols.reshape(n_z, 2, rows, own_width)
+    live_cols = line.own_first(line.rolled(live_cols, 0), 1).reshape(n_dp, rows, own_width)
+    attended_rel = attended.reshape(2, half_rows, local_cols)
+    attended_rel = jnp.where(core == 0, attended_rel, jnp.flip(attended_rel, 0))
+    att_raw = line.along(attended_rel.reshape(rows, local_cols))
+    att_other = [line.swap(values, planes) for values, planes in att_raw]
+    att_slots = zip(line.pick([values for values, _ in att_raw]), line.pick(att_other))
+    attended_all = jnp.stack([values for pair in att_slots for values in pair])
     partial = lax.dot_general(
         attended_all, live_cols, (((1,), (1,)), ((0,), (0,))), preferred_element_type=F32
     )
     weight_grad = jnp.sum(low(partial), axis=0).astype(BF16)
 
-    attended_grad = lax.dot_general(live_flat, wo_full, BACK, preferred_element_type=F32)
-    grad_heads = attended_grad.astype(BF16).reshape(samples, tok_rows, head_count, HEAD_DIM)
+    live_rel = relative(jnp.concatenate([live_flat, live_other], axis=0))
+    half_grad = 0.0
+    for m in range(n_z):
+        half_grad += lax.dot_general(
+            live_rel[:, m].reshape(2 * rows, 2 * own_width),
+            wo_slots[m],
+            BACK,
+            preferred_element_type=F32,
+        )
+    half_grad = half_grad.astype(BF16)
+    grad_keep, grad_send = half_grad[:rows], half_grad[rows:]
+    grad_come = line.swap(grad_send)
+    attended_grad = jnp.where(
+        line.x == 0,
+        jnp.concatenate([grad_keep, grad_come], axis=1),
+        jnp.concatenate([grad_come, grad_keep], axis=1),
+    )
+    grad_heads = attended_grad.reshape(samples, tok_rows, head_count, HEAD_DIM)
     value_part = jnp.einsum("shtj,sthd->sjhd", prob_low, grad_heads, preferred_element_type=F32)
     prob_grad = jnp.einsum(
         "sthd,sjhd->shtj", grad_heads, value_heads, preferred_element_type=F32
@@ -102,8 +230,19 @@
     key_part = jnp.einsum("shtj,sthd->sjhd", score_grad, query_heads, preferred_element_type=F32)
 
     query_grad = query_grad.reshape(rows, local_cols)
-    text_term = lax.dot_general(query_grad, wq_full, BACK, preferred_element_type=F32)
-    text_term = text_term.astype(BF16)
+    terms = [
+        jnp.stack(
+            [
+                lax.dot_general(
+                    query_grad, wq_slots[m][e], BACK, preferred_element_type=F32
+                ).astype(BF16)
+                for e in range(2)
+            ],
+            axis=1,
+        )
+        for m in range(n_z)
+    ]
+    text_term = line.unrolled(line.own_first(jnp.stack(terms, axis=1), 2), 1)
     text_parts = lax.all_to_all(
         text_term.reshape(rows, n_tensor, width // n_tensor), "tensor", split_axis=1, concat_axis=0
     )
@@ -114,7 +253,7 @@
     kv_part = kv_part.reshape(samples, n_dp, image_own, 2 * local_cols).transpose(1, 0, 2, 3)
     kv_part = kv_part.reshape(n_dp, image_rows, 2 * local_cols)
     kv_grad = jnp.sum(lax.all_to_all(kv_part, "dp", split_axis=0, concat_axis=0), axis=0)
-    kv_grad_all = lax.all_gather(kv_grad.astype(BF16), "dp", axis=0, tiled=True)
+    kv_grad_all = everywhere(kv_grad.astype(BF16)).reshape(n_dp * image_rows, 2 * local_cols)
     key_low, value_low = kv_grad_all[:, :local_cols], kv_grad_all[:, local_cols:]
     image_term = lax.dot_general(key_low, key_weight, BACK, preferred_element_type=F32)
     image_term = image_term + lax.dot_general(

time: 478 us -> 439 us (0.918)
  waiting for transfers between devices: 287 us -> 147 us
  starting transfers between devices: 31.1 us -> 131 us
  blocking collectives: 65.7 us -> 0 us
  local copies, waits for them, and re-layouts: 25.9 us -> 57.3 us
  other arithmetic: 11 us -> 42.2 us
  matrix products: 39.8 us -> 54.3 us
  between operations: 14 us -> 1.37 us
    all_gather x3 -> x0, waiting for transfers between devices: 177 us -> none  [the longest x1 118 us: shards(): wq_full = lax.all_gather(query_weight, 'dp', axis=0, tiled=True)]
    all_gather x2 -> x0, blocking collectives: 65.7 us -> none  [the longest x1 34.2 us: shards(): kv_all = lax.all_gather(kv_own.astype(BF16), 'dp', axis=0)]
    ppermute x0 -> x27, starting transfers between devices: none -> 57.1 us  [the longest x12 32.2 us: move(): return lax.ppermute(block, 'dp', pairs)]
    ppermute x0 -> x27, waiting for transfers between devices: none -> 54.5 us  [the longest x13 30 us: swap(): return lax.ppermute(block, 'dp', pairs)]
    all_to_all x1, starting transfers between devices: 4.14 us -> 27.4 us  [shards(): lax.all_to_all(part_kv, 'dp', split_axis=0, concat_axis=0)]
    all_to_all x1, waiting for transfers between devices: 23.1 us -> 0.01 us  [shards(): lax.all_to_all(part_kv, 'dp', split_axis=0, concat_axis=0)]
    dot_general x3 -> x20, matrix products: 19.2 us -> 41.5 us  [the longest x8 16.4 us: shards(): jnp.dot(text_rel[:, m, e], wq_slots[m][e], preferred_element_type=F32)]
    all_to_all x1 -> x3, waiting for transfers between devices: 45 us -> 65.8 us  [the longest x2 52 us: everywhere(): return lax.all_to_all(copies, 'dp', split_axis=0, concat_axis=0)]
  transfers between devices with their start and end apart: 10 -> 36, of which waited for: 8 -> 13; matrix products, arithmetic and copies ran while one was open for 11% -> 31% of each run, Pallas kernels for 0% -> 0%
where the time goes in v2:
time: 439 us; the launch traced here: 434 us
  waiting for transfers between devices  147 us (33%)
  starting transfers between devices  131 us (30%)
  local copies, waits for them, and re-layouts  57.3 us (13%)
  matrix products  54.3 us (12%)
  other arithmetic  42.2 us (10%)
    all_to_all x2, waiting for transfers between devices, everywhere(): return lax.all_to_all(copies, 'dp', split_axis=0, concat_axis=0)  52 us
    ppermute x12, starting transfers between devices, move(): return lax.ppermute(block, 'dp', pairs)  32.2 us
    ppermute x13, waiting for transfers between devices, swap(): return lax.ppermute(block, 'dp', pairs)  30 us
    all_to_all x1, starting transfers between devices, shards(): lax.all_to_all(part_kv, 'dp', split_axis=0, concat_axis=0)  27.4 us
    ppermute x13, starting transfers between devices, swap(): return lax.ppermute(block, 'dp', pairs)  24.7 us
    ppermute x12, waiting for transfers between devices, move(): return lax.ppermute(block, 'dp', pairs)  24.5 us
    all_to_all x1, waiting for transfers between devices, shards(): lax.all_to_all(image_flat, 'dp', split_axis=1, concat_axis=0, tiled=True)  18.5 us
    dot_general x8, matrix products, shards(): jnp.dot(text_rel[:, m, e], wq_slots[m][e], preferred_element_type=F32)  16.4 us
  transfers between devices with their start and end apart: 36, of which 13 were waited for; matrix products, arithmetic and copies ran while one was open for 31% of the time, Pallas kernels for 0%

profile of v2, /device:TPU:4, one launch (start us, length us, event | category | flops | bytes accessed | tf_op | source)
XLA Modules:
  0.0 433.6 jit_solution(6744757341409701945)
XLA Ops:
  0.7 2.7 collective-permute-start.1
  3.3 4.5 %collective-permute-start.7 = (bf16[512,1024]{1,0:T(8,128)(2,1)}, bf16[512,1024]{1,0:T(8,128)(2,1)}, u32[]{:S(2)}, u32[]{:S(2)}) collective-permute-start(bf16[512,1024]{1,0:T(8,128)(2,1)} %param.12), channel_id=1, source_target_pairs={{0,8},{4,12},{8,16},{12,20},{16,24},{20,28},{1,9},{5,13},{9,17},{1... | collective-permute-start | bytes 3145736 | tf_op jit(solution)/shard_map/ppermute | solution.py:36
  10.8 3.4 all-to-all-start
  24.8 4.5 %reshape_reshape.6 = bf16[256,4,2,512]{3,2,1,0:T(2,128)(2,1)} reshape(bf16[2,128,4096]{2,1,0:T(8,128)(2,1)} %param.8) | data formatting | bytes 4194304 | tf_op jit(solution)/shard_map/reshape;reshape | solution.py:163
  29.3 3.6 copy.77
  32.9 18.5 %all-to-all-done = bf16[8,8,512]{2,0,1:T(8,128)(2,1)S(1)} async-done(((bf16[8,8,512]{2,0,1:T(8,128)(2,1)}), bf16[8,8,512]{2,0,1:T(8,128)(2,1)S(1)}, u32[]{:S(2)}, u32[]{:S(2)}) %all-to-all-start) | async-done | bytes 65568 | tf_op jit(solution)/shard_map/all_to_all | solution.py:140
  54.0 27.4 %all-to-all-start.1 = ((f32[8,8,2048]{2,1,0:T(8,128)}), f32[8,8,2048]{2,1,0:T(8,128)}, u32[]{:S(2)}, u32[]{:S(2)}) async-start(f32[8,8,2048]{2,1,0:T(8,128)} %maximum_bitcast_fusion), calls=%async_computation.1 | async-start | bytes 1048576 | tf_op jit(solution)/shard_map/all_to_all | solution.py:149
  81.5 3.7 fusion.9
  85.2 2.9 reverse_select_fusion.3
  90.9 2.8 concatenate.52
  93.7 6.2 %copy.81 = bf16[256,4,2,512]{0,3,2,1:T(8,128)(2,1)} copy(bf16[256,4,2,512]{3,2,1,0:T(2,128)(2,1)} %concatenate.52) | data formatting | bytes 4194304 | tf_op jit(solution)/shard_map/concatenate | solution.py:203
  106.7 8.1 %all-to-all-start.2 = ((bf16[8,8,2048]{2,1,0:T(8,128)(2,1)}), bf16[8,8,2048]{2,1,0:T(8,128)(2,1)S(1)}, u32[]{:S(2)}, u32[]{:S(2)}) async-start(bf16[8,8,2048]{2,1,0:T(8,128)(2,1)} %broadcast_in_dim.14), calls=%async_computation.2 | async-start | bytes 524288 | tf_op jit(solution)/shard_map/all_to_all | solution.py:153
  114.9 3.0 collective-permute-start.12
  117.9 2.6 fusion.52
  121.8 2.6 convolution_add_fusion.6
  124.4 34.7 %all-to-all-done.2 = bf16[8,8,2048]{2,1,0:T(8,128)(2,1)S(1)} async-done(((bf16[8,8,2048]{2,1,0:T(8,128)(2,1)}), bf16[8,8,2048]{2,1,0:T(8,128)(2,1)S(1)}, u32[]{:S(2)}, u32[]{:S(2)}) %all-to-all-start.2) | async-done | bytes 262176 | tf_op jit(solution)/shard_map/all_to_all | solution.py:153
  161.3 2.6 maximum_select_fusion
  169.1 6.5 %collective-permute-start.15 = (bf16[512,1024]{1,0:T(8,128)(2,1)}, bf16[512,1024]{1,0:T(8,128)(2,1)}, u32[]{:S(2)}, u32[]{:S(2)}) collective-permute-start(bf16[512,1024]{1,0:T(8,128)(2,1)} %pad_maximum_fusion.1), channel_id=1, source_target_pairs={{0,8},{4,12},{8,16},{12,20},{16,24},{20,28},{1,9},{5,13},{9,17},{1... | collective-permute-start | bytes 3145736 | tf_op jit(solution)/shard_map/ppermute | solution.py:36
  175.6 3.4 collective-permute-start.5
  179.0 2.7 collective-permute-done.12
  182.9 19.7 %collective-permute-done.2 = bf16[512,1024]{1,0:T(8,128)(2,1)} collective-permute-done((bf16[512,1024]{1,0:T(8,128)(2,1)}, bf16[512,1024]{1,0:T(8,128)(2,1)}, u32[]{:S(2)}, u32[]{:S(2)}) %collective-permute-start.2) | collective-permute-done | bytes 1048608 | tf_op jit(solution)/shard_map/ppermute | solution.py:36
  202.6 2.7 fusion.51
  205.3 3.0 fusion.82
  208.3 3.5 collective-permute-start.4
  211.9 2.7 convolution_add_fusion.5
  214.6 2.9 fusion.83
  223.2 3.0 fusion.10
  230.9 5.7 %collective-permute-done.4 = bf16[512,1024]{1,0:T(8,128)(2,1)} collective-permute-done((bf16[512,1024]{1,0:T(8,128)(2,1)}, bf16[512,1024]{1,0:T(8,128)(2,1)}, u32[]{:S(2)}, u32[]{:S(2)}) %collective-permute-start.4) | collective-permute-done | bytes 1048608 | tf_op jit(solution)/shard_map/ppermute | solution.py:41
  238.3 17.5 %collective-permute-done.6 = bf16[512,1024]{1,0:T(8,128)(2,1)S(1)} collective-permute-done((bf16[512,1024]{1,0:T(8,128)(2,1)}, bf16[512,1024]{1,0:T(8,128)(2,1)S(1)}, u32[]{:S(2)}, u32[]{:S(2)}) %collective-permute-start.6) | collective-permute-done | bytes 1048608 | tf_op jit(solution)/shard_map/ppermute | solution.py:41
  268.0 16.4 %all-to-all-start.4 = ((f32[8,8,2048]{2,1,0:T(8,128)}), f32[8,8,2048]{2,1,0:T(8,128)S(1)}, u32[]{:S(2)}, u32[]{:S(2)}) async-start(f32[8,8,2048]{2,1,0:T(8,128)} %copy.92), calls=%async_computation.4 | async-start | bytes 1048576 | tf_op jit(solution)/shard_map/all_to_all | solution.py:255
  291.0 5.4 %collective-permute-start.24 = (bf16[256,1024]{0,1:T(8,128)(2,1)}, bf16[256,1024]{0,1:T(8,128)(2,1)}, u32[]{:S(2)}, u32[]{:S(2)}) collective-permute-start(bf16[256,1024]{0,1:T(8,128)(2,1)} %copy_bitcast_fusion), channel_id=1, source_target_pairs={{0,8},{4,12},{8,16},{12,20},{16,24},{20,28},{1,9},{5,13},{9,17},{1... | collective-permute-start | bytes 1572872 | tf_op jit(solution)/shard_map/ppermute | solution.py:36
  303.1 2.4 fusion.29
  305.5 5.7 %all-to-all-done.4 = f32[8,8,2048]{2,1,0:T(8,128)S(1)} async-done(((f32[8,8,2048]{2,1,0:T(8,128)}), f32[8,8,2048]{2,1,0:T(8,128)S(1)}, u32[]{:S(2)}, u32[]{:S(2)}) %all-to-all-start.4) | async-done | bytes 524320 | tf_op jit(solution)/shard_map/all_to_all | solution.py:255
  311.9 3.4 all-to-all-start.5
  317.8 2.4 fusion.28
  320.2 17.3 %all-to-all-done.5 = bf16[8,8,2048]{2,1,0:T(8,128)(2,1)S(1)} async-done(((bf16[8,8,2048]{2,1,0:T(8,128)(2,1)}), bf16[8,8,2048]{2,1,0:T(8,128)(2,1)S(1)}, u32[]{:S(2)}, u32[]{:S(2)}) %all-to-all-start.5) | async-done | bytes 262176 | tf_op jit(solution)/shard_map/all_to_all | solution.py:153
  337.5 3.8 all-to-all-start.8
  352.9 13.8 %all-to-all-done.8 = bf16[1,128,8,512]{3,1,0,2:T(8,128)(2,1)S(1)} async-done(((bf16[1,128,8,512]{3,1,0,2:T(8,128)(2,1)}), bf16[1,128,8,512]{3,1,0,2:T(8,128)(2,1)S(1)}, u32[]{:S(2)}, u32[]{:S(2)}) %all-to-all-start.8) | async-done | bytes 1048608 | tf_op jit(solution)/shard_map/all_to_all | solution.py:185
  367.7 4.0 all-to-all-start.6
  371.7 2.9 reverse_select_fusion.2
  374.6 3.8 collective-permute-start.22
  380.4 3.9 all-to-all-start.7
  386.4 4.1 copy.85
  393.9 3.6 all-to-all-start.3
  406.7 5.5 %collective-permute-done.23 = bf16[256,1024]{0,1:T(8,128)(2,1)} collective-permute-done((bf16[256,1024]{0,1:T(8,128)(2,1)}, bf16[256,1024]{0,1:T(8,128)(2,1)}, u32[]{:S(2)}, u32[]{:S(2)}) %collective-permute-start.23) | collective-permute-done | bytes 524320 | tf_op jit(solution)/shard_map/ppermute | solution.py:41
  418.7 2.9 all-to-all-done.3
  424.8 3.1 fusion.6
  430.1 3.4 reduce-precision_reduce_fusion
  (176 shorter events, 117.2 us)
Async XLA Ops:
  0.6 52.3 %copy-start = (bf16[512,1024]{1,0:T(8,128)(2,1)S(1)}, bf16[512,1024]{1,0:T(8,128)(2,1)}, u32[]{:S(2)}) copy-start(bf16[512,1024]{1,0:T(8,128)(2,1)} %param.13) | copy-start | bytes 3145732
  0.6 17.7 %copy-start.26 = (s32[2]{0:T(128)S(1)}, s32[2]{0:T(128)}, u32[]{:S(2)}) copy-start(s32[2]{0:T(128)} %param.11) | copy-start | bytes 28
  0.7 114.2 %collective-permute-start.1 = (bf16[512,1024]{1,0:T(8,128)(2,1)}, bf16[512,1024]{1,0:T(8,128)(2,1)}, u32[]{:S(2)}, u32[]{:S(2)}) collective-permute-start(bf16[512,1024]{1,0:T(8,128)(2,1)} %param.12), channel_id=1, source_target_pairs={{0,16},{4,20},{8,24},{12,28},{16,0},{20,4},{24,8},{28,12},{1,17},{... | collective-permute-start | bytes 3145736 | tf_op jit(solution)/shard_map/ppermute | solution.py:36
  3.3 165.8 %collective-permute-start.7 = (bf16[512,1024]{1,0:T(8,128)(2,1)}, bf16[512,1024]{1,0:T(8,128)(2,1)}, u32[]{:S(2)}, u32[]{:S(2)}) collective-permute-start(bf16[512,1024]{1,0:T(8,128)(2,1)} %param.12), channel_id=1, source_target_pairs={{0,8},{4,12},{8,16},{12,20},{16,24},{20,28},{1,9},{5,13},{9,17},{1... | collective-permute-start | bytes 3145736 | tf_op jit(solution)/shard_map/ppermute | solution.py:36
  7.8 112.7 %collective-permute-start = (bf16[512,1024]{1,0:T(8,128)(2,1)}, bf16[512,1024]{1,0:T(8,128)(2,1)}, u32[]{:S(2)}, u32[]{:S(2)}) collective-permute-start(bf16[512,1024]{1,0:T(8,128)(2,1)} %param.12), channel_id=1, source_target_pairs={{0,4},{4,0},{8,12},{12,8},{16,20},{20,16},{24,28},{28,24},{1,5},{5... | collective-permute-start | bytes 3145736 | tf_op jit(solution)/shard_map/ppermute | solution.py:41
  10.8 40.5 %all-to-all-start = ((bf16[8,8,512]{2,0,1:T(8,128)(2,1)}), bf16[8,8,512]{2,0,1:T(8,128)(2,1)S(1)}, u32[]{:S(2)}, u32[]{:S(2)}) async-start(bf16[8,8,512]{2,0,1:T(8,128)(2,1)} %copy.75), calls=%async_computation | async-start | bytes 131072 | tf_op jit(solution)/shard_map/all_to_all | solution.py:140
  16.5 84.7 %collective-permute-start.11 = (bf16[512,512]{1,0:T(8,128)(2,1)}, bf16[512,512]{1,0:T(8,128)(2,1)}, u32[]{:S(2)}, u32[]{:S(2)}) collective-permute-start(bf16[512,512]{1,0:T(8,128)(2,1)} %get-tuple-element.18), channel_id=1, source_target_pairs={{0,4},{4,0},{8,12},{12,8},{16,20},{20,16},{24,28},{28,24},{1,5},{5... | collective-permute-start | bytes 1572872 | tf_op jit(solution)/shard_map/ppermute | solution.py:41
  23.6 64.5 %collective-permute-start.9 = (bf16[256,2048]{0,1:T(8,128)(2,1)}, bf16[256,2048]{0,1:T(8,128)(2,1)}, u32[]{:S(2)}, u32[]{:S(2)}) collective-permute-start(bf16[256,2048]{0,1:T(8,128)(2,1)} %copy.101), channel_id=1, source_target_pairs={{0,4},{4,0},{8,12},{12,8},{16,20},{20,16},{24,28},{28,24},{1,5},{5... | collective-permute-start | bytes 3145736 | tf_op jit(solution)/shard_map/ppermute | solution.py:41
  54.0 50.9 %all-to-all-start.1 = ((f32[8,8,2048]{2,1,0:T(8,128)}), f32[8,8,2048]{2,1,0:T(8,128)}, u32[]{:S(2)}, u32[]{:S(2)}) async-start(f32[8,8,2048]{2,1,0:T(8,128)} %maximum_bitcast_fusion), calls=%async_computation.1 | async-start | bytes 1048576 | tf_op jit(solution)/shard_map/all_to_all | solution.py:149
  88.1 71.9 %collective-permute-start.10 = (bf16[256,2048]{0,1:T(8,128)(2,1)}, bf16[256,2048]{0,1:T(8,128)(2,1)}, u32[]{:S(2)}, u32[]{:S(2)}) collective-permute-start(bf16[256,2048]{0,1:T(8,128)(2,1)} %collective-permute-done.9), channel_id=1, source_target_pairs={{0,1},{1,0},{2,3},{3,2},{4,5},{5,4},{6,7},{7,6},{8,9},{9,8},{10,11... | collective-permute-start | bytes 3145736 | tf_op jit(solution)/shard_map/ppermute | solution.py:110
  93.7 6.2 %copy-start.7 = (bf16[128,4096]{1,0:T(8,128)(2,1)S(1)}, bf16[128,4096]{1,0:T(8,128)(2,1)}, u32[]{:S(2)}) copy-start(bf16[128,4096]{1,0:T(8,128)(2,1)} %constant_dynamic-slice_fusion) | copy-start | bytes 3145732
  101.2 16.6 %copy-start.2 = (bf16[256,4,2,512]{3,0,2,1:T(8,128)(2,1)S(1)}, bf16[256,4,2,512]{3,0,2,1:T(8,128)(2,1)}, u32[]{:S(2)}) copy-start(bf16[256,4,2,512]{3,0,2,1:T(8,128)(2,1)} %copy-done.1) | copy-start | bytes 6291460
  101.2 74.4 %collective-permute-start.3 = (bf16[512,1024]{1,0:T(8,128)(2,1)}, bf16[512,1024]{1,0:T(8,128)(2,1)}, u32[]{:S(2)}, u32[]{:S(2)}) collective-permute-start(bf16[512,1024]{1,0:T(8,128)(2,1)} %param.12), channel_id=1, source_target_pairs={{8,0},{12,4},{16,8},{20,12},{24,16},{28,20},{9,1},{13,5},{17,9},{2... | collective-permute-start | bytes 3145736 | tf_op jit(solution)/shard_map/ppermute | solution.py:36
  106.7 52.4 %all-to-all-start.2 = ((bf16[8,8,2048]{2,1,0:T(8,128)(2,1)}), bf16[8,8,2048]{2,1,0:T(8,128)(2,1)S(1)}, u32[]{:S(2)}, u32[]{:S(2)}) async-start(bf16[8,8,2048]{2,1,0:T(8,128)(2,1)} %broadcast_in_dim.14), calls=%async_computation.2 | async-start | bytes 524288 | tf_op jit(solution)/shard_map/all_to_all | solution.py:153
  114.9 6.9 %copy-start.9 = (f32[256,1024]{1,0:T(8,128)S(1)}, f32[256,1024]{1,0:T(8,128)}, u32[]{:S(2)}) copy-start(f32[256,1024]{1,0:T(8,128)} %fusion.53) | copy-start | bytes 3145732
  114.9 66.8 %collective-permute-start.12 = (bf16[512,1024]{1,0:T(8,128)(2,1)}, bf16[512,1024]{1,0:T(8,128)(2,1)}, u32[]{:S(2)}, u32[]{:S(2)}) collective-permute-start(bf16[512,1024]{1,0:T(8,128)(2,1)} %pad_maximum_fusion.1), channel_id=1, source_target_pairs={{0,16},{4,20},{8,24},{12,28},{16,0},{20,4},{24,8},{28,12},{1,17},{... | collective-permute-start | bytes 3145736 | tf_op jit(solution)/shard_map/ppermute | solution.py:36
  120.5 99.3 %collective-permute-start.14 = (bf16[512,1024]{1,0:T(8,128)(2,1)}, bf16[512,1024]{1,0:T(8,128)(2,1)}, u32[]{:S(2)}, u32[]{:S(2)}) collective-permute-start(bf16[512,1024]{1,0:T(8,128)(2,1)} %pad_maximum_fusion.1), channel_id=1, source_target_pairs={{8,0},{12,4},{16,8},{20,12},{24,16},{28,20},{9,1},{13,5},{17,9},{2... | collective-permute-start | bytes 3145736 | tf_op jit(solution)/shard_map/ppermute | solution.py:36
  160.0 42.6 %collective-permute-start.2 = (bf16[512,1024]{1,0:T(8,128)(2,1)}, bf16[512,1024]{1,0:T(8,128)(2,1)}, u32[]{:S(2)}, u32[]{:S(2)}) collective-permute-start(bf16[512,1024]{1,0:T(8,128)(2,1)} %collective-permute-done.1), channel_id=1, source_target_pairs={{8,0},{12,4},{16,24},{20,28},{9,1},{13,5},{17,25},{21,29},{10,2},{... | collective-permute-start | bytes 3145736 | tf_op jit(solution)/shard_map/ppermute | solution.py:36
  169.1 57.1 %collective-permute-start.15 = (bf16[512,1024]{1,0:T(8,128)(2,1)}, bf16[512,1024]{1,0:T(8,128)(2,1)}, u32[]{:S(2)}, u32[]{:S(2)}) collective-permute-start(bf16[512,1024]{1,0:T(8,128)(2,1)} %pad_maximum_fusion.1), channel_id=1, source_target_pairs={{0,8},{4,12},{8,16},{12,20},{16,24},{20,28},{1,9},{5,13},{9,17},{1... | collective-permute-start | bytes 3145736 | tf_op jit(solution)/shard_map/ppermute | solution.py:36
  175.6 55.3 %collective-permute-start.5 = (bf16[512,1024]{1,0:T(8,128)(2,1)}, bf16[512,1024]{1,0:T(8,128)(2,1)}, u32[]{:S(2)}, u32[]{:S(2)}) collective-permute-start(bf16[512,1024]{1,0:T(8,128)(2,1)} %collective-permute-done.3), channel_id=1, source_target_pairs={{0,4},{4,0},{8,12},{12,8},{16,20},{20,16},{1,5},{5,1},{9,13},{13,9... | collective-permute-start | bytes 3145736 | tf_op jit(solution)/shard_map/ppermute | solution.py:41
  181.6 40.8 %collective-permute-start.13 = (bf16[512,1024]{1,0:T(8,128)(2,1)}, bf16[512,1024]{1,0:T(8,128)(2,1)}, u32[]{:S(2)}, u32[]{:S(2)}) collective-permute-start(bf16[512,1024]{1,0:T(8,128)(2,1)} %collective-permute-done.12), channel_id=1, source_target_pairs={{8,0},{12,4},{16,24},{20,28},{9,1},{13,5},{17,25},{21,29},{10,2},{... | collective-permute-start | bytes 3145736 | tf_op jit(solution)/shard_map/ppermute | solution.py:36
  205.3 6.5 %copy-start.5 = (f32[256,1024]{1,0:T(8,128)S(1)}, f32[256,1024]{1,0:T(8,128)}, u32[]{:S(2)}) copy-start(f32[256,1024]{1,0:T(8,128)} %convolution_add_fusion.6) | copy-start | bytes 3145732
  208.3 28.3 %collective-permute-start.4 = (bf16[512,1024]{1,0:T(8,128)(2,1)}, bf16[512,1024]{1,0:T(8,128)(2,1)}, u32[]{:S(2)}, u32[]{:S(2)}) collective-permute-start(bf16[512,1024]{1,0:T(8,128)(2,1)} %collective-permute-done.2), channel_id=1, source_target_pairs={{0,4},{4,0},{24,28},{28,24},{1,5},{5,1},{25,29},{29,25},{2,6},{6,2... | collective-permute-start | bytes 3145736 | tf_op jit(solution)/shard_map/ppermute | solution.py:41
  219.8 36.1 %collective-permute-start.6 = (bf16[512,1024]{1,0:T(8,128)(2,1)}, bf16[512,1024]{1,0:T(8,128)(2,1)S(1)}, u32[]{:S(2)}, u32[]{:S(2)}) collective-permute-start(bf16[512,1024]{1,0:T(8,128)(2,1)} %collective-permute-done.1), channel_id=1, source_target_pairs={{0,4},{4,0},{8,12},{12,8},{16,20},{20,16},{24,28},{28,24},{1,5},{5... | collective-permute-start | bytes 3145736 | tf_op jit(solution)/shard_map/ppermute | solution.py:41
  222.4 34.4 %collective-permute-start.8 = (bf16[512,1024]{1,0:T(8,128)(2,1)}, bf16[512,1024]{1,0:T(8,128)(2,1)S(1)}, u32[]{:S(2)}, u32[]{:S(2)}) collective-permute-start(bf16[512,1024]{1,0:T(8,128)(2,1)} %collective-permute-done.7), channel_id=1, source_target_pairs={{8,12},{12,8},{16,20},{20,16},{24,28},{28,24},{9,13},{13,9},{17,21... | collective-permute-start | bytes 3145736 | tf_op jit(solution)/shard_map/ppermute | solution.py:41
  226.2 10.4 %copy-start.10 = (f32[256,1024]{1,0:T(8,128)S(1)}, f32[256,1024]{1,0:T(8,128)}, u32[]{:S(2)}) copy-start(f32[256,1024]{1,0:T(8,128)} %convolution_add_fusion.5) | copy-start | bytes 3145732
  226.2 10.4 %copy-start.11 = (f32[256,1024]{1,0:T(8,128)S(1)}, f32[256,1024]{1,0:T(8,128)}, u32[]{:S(2)}) copy-start(f32[256,1024]{1,0:T(8,128)} %fusion.52) | copy-start | bytes 3145732
  229.2 26.7 %copy-start.6 = (f32[256,1024]{1,0:T(8,128)S(1)}, f32[256,1024]{1,0:T(8,128)}, u32[]{:S(2)}) copy-start(f32[256,1024]{1,0:T(8,128)} %fusion.51) | copy-start | bytes 3145732
  229.2 31.5 %collective-permute-start.16 = (bf16[256,512]{0,1:T(8,128)(2,1)}, bf16[256,512]{0,1:T(8,128)(2,1)}, u32[]{:S(2)}, u32[]{:S(2)}) collective-permute-start(bf16[256,512]{0,1:T(8,128)(2,1)} %get-tuple-element.20), channel_id=1, source_target_pairs={{0,4},{4,0},{8,12},{12,8},{16,20},{20,16},{24,28},{28,24},{1,5},{5... | collective-permute-start | bytes 786440 | tf_op jit(solution)/shard_map/ppermute | solution.py:41
  266.4 18.0 %copy-start.13 = (bf16[2,8,128,128]{3,2,1,0:T(8,128)(2,1)S(1)}, bf16[2,8,128,128]{3,2,1,0:T(8,128)(2,1)}, u32[]{:S(2)}) copy-start(bf16[2,8,128,128]{3,2,1,0:T(8,128)(2,1)} %copy-done.12) | copy-start | bytes 1572868
  268.0 43.1 %all-to-all-start.4 = ((f32[8,8,2048]{2,1,0:T(8,128)}), f32[8,8,2048]{2,1,0:T(8,128)S(1)}, u32[]{:S(2)}, u32[]{:S(2)}) async-start(f32[8,8,2048]{2,1,0:T(8,128)} %copy.92), calls=%async_computation.4 | async-start | bytes 1048576 | tf_op jit(solution)/shard_map/all_to_all | solution.py:255
  285.4 112.2 %collective-permute-start.17 = (bf16[256,1024]{0,1:T(8,128)(2,1)}, bf16[256,1024]{0,1:T(8,128)(2,1)}, u32[]{:S(2)}, u32[]{:S(2)}) collective-permute-start(bf16[256,1024]{0,1:T(8,128)(2,1)} %copy_bitcast_fusion), channel_id=1, source_target_pairs={{0,4},{4,0},{8,12},{12,8},{16,20},{20,16},{24,28},{28,24},{1,5},{5... | collective-permute-start | bytes 1572872 | tf_op jit(solution)/shard_map/ppermute | solution.py:41
  287.4 62.7 %collective-permute-start.18 = (bf16[256,1024]{0,1:T(8,128)(2,1)}, bf16[256,1024]{0,1:T(8,128)(2,1)}, u32[]{:S(2)}, u32[]{:S(2)}) collective-permute-start(bf16[256,1024]{0,1:T(8,128)(2,1)} %copy_bitcast_fusion), channel_id=1, source_target_pairs={{0,16},{4,20},{8,24},{12,28},{16,0},{20,4},{24,8},{28,12},{1,17},{... | collective-permute-start | bytes 1572872 | tf_op jit(solution)/shard_map/ppermute | solution.py:36
  289.7 84.8 %collective-permute-start.20 = (bf16[256,1024]{0,1:T(8,128)(2,1)}, bf16[256,1024]{0,1:T(8,128)(2,1)}, u32[]{:S(2)}, u32[]{:S(2)}) collective-permute-start(bf16[256,1024]{0,1:T(8,128)(2,1)} %copy_bitcast_fusion), channel_id=1, source_target_pairs={{8,0},{12,4},{16,8},{20,12},{24,16},{28,20},{9,1},{13,5},{17,9},{2... | collective-permute-start | bytes 1572872 | tf_op jit(solution)/shard_map/ppermute | solution.py:36
  291.0 101.4 %collective-permute-start.24 = (bf16[256,1024]{0,1:T(8,128)(2,1)}, bf16[256,1024]{0,1:T(8,128)(2,1)}, u32[]{:S(2)}, u32[]{:S(2)}) collective-permute-start(bf16[256,1024]{0,1:T(8,128)(2,1)} %copy_bitcast_fusion), channel_id=1, source_target_pairs={{0,8},{4,12},{8,16},{12,20},{16,24},{20,28},{1,9},{5,13},{9,17},{1... | collective-permute-start | bytes 1572872 | tf_op jit(solution)/shard_map/ppermute | solution.py:36
  301.9 15.9 %copy-start.22 = (bf16[2,128,8,128]{3,2,1,0:T(8,128)(2,1)}, bf16[2,128,8,128]{3,2,1,0:T(8,128)(2,1)S(1)}, u32[]{:S(2)}) copy-start(bf16[2,128,8,128]{3,2,1,0:T(8,128)(2,1)S(1)} %copy.84) | copy-start | bytes 1572868
  311.9 25.6 %all-to-all-start.5 = ((bf16[8,8,2048]{2,1,0:T(8,128)(2,1)}), bf16[8,8,2048]{2,1,0:T(8,128)(2,1)S(1)}, u32[]{:S(2)}, u32[]{:S(2)}) async-start(bf16[8,8,2048]{2,1,0:T(8,128)(2,1)} %broadcast_in_dim.17), calls=%async_computation.5 | async-start | bytes 524288 | tf_op jit(solution)/shard_map/all_to_all | solution.py:153
  320.2 22.5 %copy-start.17 = (bf16[512,1024]{1,0:T(8,128)(2,1)S(1)}, bf16[512,1024]{1,0:T(8,128)(2,1)}, u32[]{:S(2)}) copy-start(bf16[512,1024]{1,0:T(8,128)(2,1)} %param.12) | copy-start | bytes 3145732
  337.5 29.2 %all-to-all-start.8 = ((bf16[1,128,8,512]{3,1,0,2:T(8,128)(2,1)}), bf16[1,128,8,512]{3,1,0,2:T(8,128)(2,1)S(1)}, u32[]{:S(2)}, u32[]{:S(2)}) async-start(bf16[1,128,8,512]{3,1,0,2:T(8,128)(2,1)} %copy.97), calls=%async_computation.8 | async-start | bytes 2097152 | tf_op jit(solution)/shard_map/all_to_all | solution.py:185
  350.1 28.3 %collective-permute-start.19 = (bf16[256,1024]{0,1:T(8,128)(2,1)}, bf16[256,1024]{0,1:T(8,128)(2,1)}, u32[]{:S(2)}, u32[]{:S(2)}) collective-permute-start(bf16[256,1024]{0,1:T(8,128)(2,1)} %collective-permute-done.18), channel_id=1, source_target_pairs={{8,0},{12,4},{16,24},{20,28},{9,1},{13,5},{17,25},{21,29},{10,2},{... | collective-permute-start | bytes 1572872 | tf_op jit(solution)/shard_map/ppermute | solution.py:36
  367.7 12.7 %all-to-all-start.6 = ((bf16[8,8,512]{2,1,0:T(8,128)(2,1)}), bf16[8,8,512]{2,1,0:T(8,128)(2,1)}, u32[]{:S(2)}, u32[]{:S(2)}) async-start(bf16[8,8,512]{2,1,0:T(8,128)(2,1)} %fusion.32), calls=%async_computation.6 | async-start | bytes 131072 | tf_op jit(solution)/shard_map/all_to_all | solution.py:262
  374.6 27.0 %collective-permute-start.22 = (bf16[256,1024]{0,1:T(8,128)(2,1)}, bf16[256,1024]{0,1:T(8,128)(2,1)}, u32[]{:S(2)}, u32[]{:S(2)}) collective-permute-start(bf16[256,1024]{0,1:T(8,128)(2,1)} %collective-permute-done.20), channel_id=1, source_target_pairs={{0,4},{4,0},{8,12},{12,8},{16,20},{20,16},{1,5},{5,1},{9,13},{13,9... | collective-permute-start | bytes 1572872 | tf_op jit(solution)/shard_map/ppermute | solution.py:41
  378.4 24.5 %collective-permute-start.21 = (bf16[256,1024]{0,1:T(8,128)(2,1)}, bf16[256,1024]{0,1:T(8,128)(2,1)}, u32[]{:S(2)}, u32[]{:S(2)}) collective-permute-start(bf16[256,1024]{0,1:T(8,128)(2,1)} %collective-permute-done.19), channel_id=1, source_target_pairs={{0,4},{4,0},{24,28},{28,24},{1,5},{5,1},{25,29},{29,25},{2,6},{6,2... | collective-permute-start | bytes 1572872 | tf_op jit(solution)/shard_map/ppermute | solution.py:41
  380.4 13.5 %all-to-all-start.7 = ((bf16[1,8,4,1024]{3,1,0,2:T(8,128)(2,1)}), bf16[1,8,4,1024]{3,1,0,2:T(8,128)(2,1)S(1)}, u32[]{:S(2)}, u32[]{:S(2)}) async-start(bf16[1,8,4,1024]{3,1,0,2:T(8,128)(2,1)} %bitcast.48), calls=%async_computation.7 | async-start | bytes 131072 | tf_op jit(solution)/shard_map/all_to_all | solution.py:265
  390.6 21.7 %collective-permute-start.23 = (bf16[256,1024]{0,1:T(8,128)(2,1)}, bf16[256,1024]{0,1:T(8,128)(2,1)}, u32[]{:S(2)}, u32[]{:S(2)}) collective-permute-start(bf16[256,1024]{0,1:T(8,128)(2,1)} %collective-permute-done.18), channel_id=1, source_target_pairs={{0,4},{4,0},{8,12},{12,8},{16,20},{20,16},{24,28},{28,24},{1,5},{5... | collective-permute-start | bytes 1572872 | tf_op jit(solution)/shard_map/ppermute | solution.py:41
  392.5 23.6 %collective-permute-start.25 = (bf16[256,1024]{0,1:T(8,128)(2,1)}, bf16[256,1024]{0,1:T(8,128)(2,1)}, u32[]{:S(2)}, u32[]{:S(2)}) collective-permute-start(bf16[256,1024]{0,1:T(8,128)(2,1)} %collective-permute-done.24), channel_id=1, source_target_pairs={{8,12},{12,8},{16,20},{20,16},{24,28},{28,24},{9,13},{13,9},{17,21... | collective-permute-start | bytes 1572872 | tf_op jit(solution)/shard_map/ppermute | solution.py:41
  393.9 27.7 %all-to-all-start.3 = ((bf16[1,256,4,1024]{1,3,0,2:T(8,128)(2,1)}), bf16[1,256,4,1024]{1,3,0,2:T(8,128)(2,1)S(1)}, u32[]{:S(2)}, u32[]{:S(2)}) async-start(bf16[1,256,4,1024]{1,3,0,2:T(8,128)(2,1)} %bitcast.188), calls=%async_computation.3 | async-start | bytes 4194304 | tf_op jit(solution)/shard_map/all_to_all | solution.py:246
  399.5 25.3 %collective-permute-start.26 = (bf16[8,128,512]{2,1,0:T(8,128)(2,1)}, bf16[8,128,512]{2,1,0:T(8,128)(2,1)}, u32[]{:S(2)}, u32[]{:S(2)}) collective-permute-start(bf16[8,128,512]{2,1,0:T(8,128)(2,1)} %bitcast.189), channel_id=1, source_target_pairs={{0,1},{1,0},{2,3},{3,2},{4,5},{5,4},{6,7},{7,6},{8,9},{9,8},{10,11... | collective-permute-start | bytes 3145736 | tf_op jit(solution)/shard_map/ppermute | solution.py:110
  (15 other events, 32.4 us)

commit v3 on v1

v3 whole, which is shorter than its diff:
```python
import functools

import jax
import jax.numpy as jnp
from jax import lax
from jax.experimental import pallas as pl
from jax.experimental.pallas import tpu as pltpu
from jax.sharding import PartitionSpec as P

HEAD_DIM = 128
F32 = jnp.float32
BF16 = jnp.bfloat16
BACK = (((1,), (1,)), ((), ()))
FIRST = (((0,), (0,)), ((), ()))
VMEM_LIMIT = 48 * 1024 * 1024


def after(values, *others):
    return lax.optimization_barrier((values, *others))[0]


def matmul(a, b, dims=None):
    if dims is None:
        return jnp.dot(a, b, preferred_element_type=F32)
    return lax.dot_general(a, b, dims, preferred_element_type=F32)


class Line:
    def __init__(self):
        self.n_dp = lax.axis_size("dp")
        self.n_z = self.n_dp // 2

    def move(self, block, moves):
        pairs = [(2 * a + e, 2 * b + e) for a, b in moves for e in range(2)]
        return lax.ppermute(block, "dp", pairs)

    def swap(self, block, planes=None):
        planes = range(self.n_z) if planes is None else planes
        pairs = [(2 * a + e, 2 * a + 1 - e) for a in planes for e in range(2)]
        return lax.ppermute(block, "dp", pairs)

    def along(self, block):
        n = self.n_z
        if n != 4:
            return [self.move(block, [((a + m) % n, a) for a in range(n)]) for m in range(1, n)]
        above = self.move(block, [(1, 0), (2, 1), (3, 2)])
        below = self.move(block, [(0, 1), (1, 2), (2, 3)])
        across = self.move(block, [(0, 2), (1, 3), (2, 0), (3, 1)])
        return [above, across, below]

    def relay(self, moved):
        return [self.move(moved[1], [(1, 0), (2, 3)])] if self.n_z == 4 else []

    def swap_moved(self, moved):
        if self.n_z != 4:
            return [self.swap(block) for block in moved]
        planes = ((0, 1, 2), None, (1, 2, 3))
        return [self.swap(block, at) for block, at in zip(moved, planes)]

    def swap_relayed(self, relayed):
        return [self.swap(block, (0, 3)) for block in relayed]

    def slots(self, z):
        if self.n_z != 4:
            return [(m, None) for m in range(self.n_z)]
        return [
            (0, None),
            (1, z < 3),
            (2, None),
            (3, z > 0),
            (jnp.where(z == 3, 1, 3), (z == 3) | (z == 0)),
        ]


def each_block(line, place, body):
    z, x = place[0], place[1]
    for i, (m, came) in enumerate(line.slots(z)):
        plane = lax.rem(z + m, line.n_z)
        for e in range(2):
            index = 2 * plane + (x if e == 0 else 1 - x)
            if came is None:
                body(i, e, index)
            else:
                pl.when(came)(functools.partial(body, i, e, index))


def columns(index, size):
    return pl.ds(pl.multiple_of(index * size, size), size)


def probabilities(query, key, image_own):
    scores = matmul(key, query, BACK) * HEAD_DIM ** (-0.5)
    image = lax.broadcasted_iota(jnp.int32, scores.shape, 0)
    token = lax.broadcasted_iota(jnp.int32, scores.shape, 1)
    image_sample = lax.rem(lax.div(image, image_own), 2)
    same = image_sample == lax.div(token, scores.shape[1] // 2)
    scores = jnp.where(same, scores, -1e30)
    peak = jnp.max(scores, axis=0, keepdims=True)
    expo = jnp.where(same, jnp.exp(scores - peak), 0.0)
    return expo / jnp.sum(expo, axis=0, keepdims=True)


def forward_kernel(line, image_own, place, text, kv, *refs):
    n = (len(refs) - 3) // 2
    weights, (query_out, attended_out, total) = (refs[:n], refs[n : 2 * n]), refs[2 * n :]
    own_width = weights[0][0].shape[0]
    rows, cols = total.shape
    total[...] = jnp.zeros_like(total)

    def add(i, e, index):
        total[...] += matmul(text[:, columns(index, own_width)], weights[e][i][...])

    each_block(line, place, add)
    query_out[...] = total[...].astype(BF16)
    part = rows // 4
    quarter = place[2]
    for h in range(cols // HEAD_DIM):
        at = slice(h * HEAD_DIM, (h + 1) * HEAD_DIM)
        value = kv[:, cols + h * HEAD_DIM : cols + (h + 1) * HEAD_DIM]
        prob = probabilities(query_out[:, at], kv[:, at], image_own)
        attended = matmul(prob.astype(BF16), value, FIRST).astype(BF16)
        for r in range(4):
            low_bit = (quarter + r) % 2
            high_bit = (quarter // 2 + r // 2) % 2
            start = pl.multiple_of((2 * low_bit + high_bit) * part, part)
            attended_out[pl.ds(start, part), at] = attended[r * part : (r + 1) * part]


def grad_kernel(line, place, live, here, there, *refs):
    weights, (keep_out, send_out, keep, send) = refs[:-4], refs[-4:]
    own_width = weights[0].shape[1] // 2
    half = line.n_dp // 2
    core = place[2] % 2
    keep[...] = jnp.zeros_like(keep)
    send[...] = jnp.zeros_like(send)

    def add(i, e, index):
        weight = weights[i][:, e * own_width : (e + 1) * own_width]
        keep[...] += matmul(live[:, columns(index, own_width)], weight, BACK)
        inner = columns(lax.rem(index, half), own_width)
        other = jnp.where(lax.div(index, half) == core, here[:, inner], there[:, inner])
        send[...] += matmul(other, weight, BACK)

    each_block(line, place, add)
    keep_out[...] = keep[...].astype(BF16)
    send_out[...] = send[...].astype(BF16)


def backward_kernel(image_own, place, query, kv, keep, come, query_grad, kv_grad):
    cols = query.shape[1]
    half = cols // 2
    x = place[1]
    for h in range(cols // HEAD_DIM):
        at = slice(h * HEAD_DIM, (h + 1) * HEAD_DIM)
        value_at = slice(cols + h * HEAD_DIM, cols + (h + 1) * HEAD_DIM)
        side = h * HEAD_DIM // half
        inner = slice(h * HEAD_DIM - side * half, (h + 1) * HEAD_DIM - side * half)
        grad = jnp.where(x == side, keep[:, inner], come[:, inner])
        prob = probabilities(query[:, at], kv[:, at], image_own)
        kv_grad[:, value_at] = matmul(prob.astype(BF16), grad)
        prob_grad = matmul(kv[:, value_at], grad, BACK)
        delta = jnp.sum(prob * prob_grad, axis=0, keepdims=True)
        score_grad = (prob * (prob_grad - delta) * HEAD_DIM ** (-0.5)).astype(BF16)
        kv_grad[:, at] = matmul(score_grad, query[:, at])
        query_grad[:, at] = matmul(score_grad, kv[:, at], FIRST).astype(BF16)


def term_kernel(line, place, query_grad, *refs):
    n = (len(refs) - 1) // 2
    weights, out = (refs[:n], refs[n : 2 * n]), refs[-1]

    def write(i, e, index):
        out[index] = matmul(query_grad[...], weights[e][i][...], BACK).astype(BF16)

    each_block(line, place, write)


def weight_grad_kernel(line, place, *refs):
    live, refs = refs[:4], refs[4:]
    n = (len(refs) - 2) // 2
    attended, (out, total) = (refs[:n], refs[n : 2 * n]), refs[2 * n :]
    total[...] = jnp.zeros_like(total)

    def add(i, e, index):
        block = jnp.concatenate([part[index] for part in live], axis=0)
        term = matmul(attended[e][i][...], block, FIRST)
        total[...] += term.astype(BF16).astype(F32)

    each_block(line, place, add)
    out[...] = total[...].astype(BF16)


def call(kernel, place, operands, outs, scratch=(), flops=0):
    moved = sum(a.size * a.dtype.itemsize for a in (*operands, *outs))
    single = len(outs) == 1
    return pl.pallas_call(
        kernel,
        out_shape=outs[0] if single else outs,
        in_specs=[pl.BlockSpec(memory_space=pltpu.SMEM)]
        + [pl.BlockSpec(memory_space=pltpu.VMEM)] * len(operands),
        out_specs=pl.BlockSpec(memory_space=pltpu.VMEM)
        if single
        else [pl.BlockSpec(memory_space=pltpu.VMEM)] * len(outs),
        scratch_shapes=list(scratch),
        compiler_params=pltpu.CompilerParams(vmem_limit_bytes=VMEM_LIMIT),
        cost_estimate=pl.CostEstimate(flops=flops, bytes_accessed=moved, transcendentals=0),
    )(place, *operands)


def shards(
    text_states,
    image_states,
    out_grad,
    text_lengths,
    query_weight,
    key_weight,
    value_weight,
    out_weight,
):
    samples, tok_rows, width = text_states.shape
    image_own = image_states.shape[1]
    line = Line()
    n_dp = line.n_dp
    n_tensor = lax.axis_size("tensor")
    dp_at, tensor_at = lax.axis_index("dp"), lax.axis_index("tensor")
    x, core = dp_at % 2, tensor_at % 2
    place = jnp.stack([dp_at // 2, x, tensor_at % 4]).astype(jnp.int32)
    rows = samples * tok_rows
    image_rows = samples * image_own
    images = n_dp * image_rows
    local_cols = query_weight.shape[1]
    own_width = query_weight.shape[0]
    half_cols = local_cols // 2
    shape = jax.ShapeDtypeStruct

    def tensor_swap(block, bit):
        return lax.ppermute(block, "tensor", [(t, t ^ bit) for t in range(n_tensor)])

    positions = dp_at * tok_rows + lax.iota(jnp.int32, tok_rows)
    live_rows = positions[None, :] < text_lengths[:, None]
    grad_live = jnp.where(live_rows[..., None], out_grad, jnp.zeros_like(out_grad))
    text_flat = text_states.reshape(rows, width)
    live_flat = grad_live.reshape(rows, width)
    image_flat = image_states.reshape(image_rows, width)

    wq_moved = line.along(query_weight)
    wq_swapped = line.swap(query_weight)
    wo_keep = lax.dynamic_slice_in_dim(out_weight, x * half_cols, half_cols, 0)
    wo_send = lax.dynamic_slice_in_dim(out_weight, (1 - x) * half_cols, half_cols, 0)
    wo_come = line.swap(wo_send)
    live_half = lax.dynamic_slice_in_dim(live_flat, core * (width // 2), width // 2, 1)
    live_here = line.swap(live_half)
    image_cols = lax.all_to_all(image_flat, "dp", split_axis=1, concat_axis=0, tiled=True)
    first = (*wq_moved, wq_swapped, wo_come, live_here, image_cols)

    wo_pair = after(jnp.concatenate([wo_keep, wo_come], axis=1), *first)
    wo_moved = line.along(wo_pair)
    wq_gated = lax.optimization_barrier((*wq_moved, *first))[: len(wq_moved)]
    wq_relayed = line.relay(wq_gated)
    wq_others = line.swap_moved(wq_gated)
    live_there = tensor_swap(after(live_here, *first), 1)

    image_cols = after(image_cols, *first)
    part_kv = jnp.concatenate(
        [matmul(image_cols, key_weight), matmul(image_cols, value_weight)], axis=1
    )
    part_kv = part_kv.reshape(n_dp, image_rows, 2 * local_cols)
    kv_own = jnp.sum(lax.all_to_all(part_kv, "dp", split_axis=0, concat_axis=0), axis=0)
    second = (*wo_moved, *wq_relayed, *wq_others, live_there, kv_own)

    def everywhere(values):
        copies = jnp.broadcast_to(values[None], (n_dp, *values.shape))
        return lax.all_to_all(copies, "dp", split_axis=0, concat_axis=0)

    gated = lax.optimization_barrier((*wo_moved, *wq_relayed, kv_own, *second))
    wo_gated, wq_last = gated[: len(wo_moved)], gated[len(wo_moved) :][: len(wq_relayed)]
    kv_gated = gated[len(wo_moved) + len(wq_relayed)]
    wo_relayed = line.relay(wo_gated)
    wq_last_other = line.swap_relayed(wq_last)
    kv_all = everywhere(kv_gated.astype(BF16)).reshape(images, 2 * local_cols)
    quarter_rows = rows // 4
    live_part = lax.dynamic_slice_in_dim(
        live_flat, (tensor_at % 4) * quarter_rows, quarter_rows, 0
    )
    live_part = after(live_part.reshape(quarter_rows, n_dp, own_width), *second)
    live_mine = lax.all_to_all(live_part, "dp", split_axis=1, concat_axis=0)
    live_mine = live_mine.reshape(n_dp, quarter_rows, own_width)
    live_y = tensor_swap(live_mine, 2)
    live_cols = [live_mine, live_y, tensor_swap(live_mine, 1), tensor_swap(live_y, 1)]

    wq_blocks = [query_weight, *wq_gated, *wq_last, wq_swapped, *wq_others, *wq_last_other]
    queries, attended = call(
        functools.partial(forward_kernel, line, image_own),
        place,
        (text_flat, kv_all, *wq_blocks),
        [shape((rows, local_cols), BF16)] * 2,
        [pltpu.VMEM((rows, local_cols), F32)],
        2 * rows * width * local_cols,
    )

    grad_keep, grad_send = call(
        functools.partial(grad_kernel, line),
        place,
        (live_flat, live_here, live_there, wo_pair, *wo_gated, *wo_relayed),
        [shape((rows, half_cols), BF16)] * 2,
        [pltpu.VMEM((rows, half_cols), F32)] * 2,
        2 * rows * width * local_cols,
    )
    grad_come = line.swap(grad_send)

    att_moved = line.along(attended)
    att_swapped = line.swap(attended)

    query_grad, kv_part = call(
        functools.partial(backward_kernel, image_own),
        place,
        (queries, kv_all, grad_keep, grad_come),
        [shape((rows, local_cols), BF16), shape((images, 2 * local_cols), F32)],
        (),
        10 * images * rows * local_cols,
    )

    att_ready = lax.optimization_barrier((*att_moved, att_swapped, query_grad))
    att_moved, att_swapped = att_ready[: len(att_moved)], att_ready[len(att_moved)]
    att_relayed = line.relay(att_moved)
    att_others = line.swap_moved(att_moved)
    att_last = line.swap_relayed(att_relayed)

    term = call(
        functools.partial(term_kernel, line),
        place,
        (att_ready[-1], *wq_blocks),
        [shape((n_dp, rows, own_width), BF16)],
        (),
        2 * rows * width * local_cols,
    )
    term = term.reshape(n_tensor, n_dp // n_tensor, rows, own_width)
    text_parts = lax.all_to_all(term, "tensor", split_axis=0, concat_axis=0)
    text_parts = text_parts.reshape(term.shape)
    text_grad = jnp.sum(text_parts.astype(F32), axis=0).astype(BF16)
    text_grad = text_grad.transpose(1, 0, 2).reshape(samples, tok_rows, width // n_tensor)

    kv_part = kv_part.reshape(n_dp, image_rows, 2 * local_cols)
    kv_grad = jnp.sum(lax.all_to_all(kv_part, "dp", split_axis=0, concat_axis=0), axis=0)
    kv_grad_all = everywhere(kv_grad.astype(BF16)).reshape(images, 2 * local_cols)
    image_term = matmul(kv_grad_all[:, :local_cols], key_weight, BACK)
    image_term = image_term + matmul(kv_grad_all[:, local_cols:], value_weight, BACK)
    image_term = lax.all_to_all(
        image_term.astype(BF16), "dp", split_axis=0, concat_axis=1, tiled=True
    )
    image_parts = lax.all_to_all(
        image_term.reshape(image_rows, n_tensor, width // n_tensor),
        "tensor",
        split_axis=1,
        concat_axis=0,
    )
    image_grad = jnp.sum(image_parts.astype(F32), axis=0).astype(BF16)
    image_grad = image_grad.reshape(samples, image_own, width // n_tensor)

    weight_grad = call(
        functools.partial(weight_grad_kernel, line),
        place,
        (*live_cols, attended, *att_moved, *att_relayed, att_swapped, *att_others, *att_last),
        [shape((local_cols, own_width), BF16)],
        [pltpu.VMEM((local_cols, own_width), F32)],
        2 * n_dp * rows * local_cols * own_width,
    )
    return text_grad, image_grad, weight_grad


def solution(mesh):
    return jax.shard_map(
        shards,
        mesh=mesh,
        in_specs=(
            P(None, "dp", None),
            P(None, "dp", None),
            P(None, "dp", None),
            P(),
            P("dp", "tensor"),
            P("dp", "tensor"),
            P("dp", "tensor"),
            P("tensor", "dp"),
        ),
        out_specs=(P(None, "dp", "tensor"), P(None, "dp", "tensor"), P("tensor", "dp")),
        check_vma=False,
    )
```

time: 478 us -> 427 us (0.89)
  starting transfers between devices: 31.1 us -> 110 us
  waiting for transfers between devices: 287 us -> 226 us
  blocking collectives: 65.7 us -> 18.5 us
  matrix products: 39.8 us -> 4.58 us
  Pallas kernels: 0 us -> 32.7 us
  between operations: 14 us -> 1.04 us
  local copies, waits for them, and re-layouts: 25.9 us -> 21.1 us
    all_gather x3 -> x0, waiting for transfers between devices: 177 us -> none  [the longest x1 118 us: shards(): wq_full = lax.all_gather(query_weight, 'dp', axis=0, tiled=True)]
    ppermute x0 -> x29, waiting for transfers between devices: none -> 153 us  [the longest x12 87.3 us: move(): return lax.ppermute(block, 'dp', pairs)]
    all_to_all x3 -> x4, waiting for transfers between devices: 87.8 us -> 6.02 us  [the longest x2 6.02 us: everywhere(): return lax.all_to_all(copies, 'dp', split_axis=0, concat_axis=0)]
    all_gather x2 -> x0, blocking collectives: 65.7 us -> none  [the longest x1 34.2 us: shards(): kv_all = lax.all_gather(kv_own.astype(BF16), 'dp', axis=0)]
    ppermute x0 -> x29, starting transfers between devices: none -> 56.3 us  [the longest x12 32.2 us: move(): return lax.ppermute(block, 'dp', pairs)]
    all_to_all x1, waiting for transfers between devices: 6.81 us -> 54.4 us  [shards(): lax.all_to_all(image_flat, 'dp', split_axis=1, concat_axis=0, tiled=True)]
    dot_general x14 -> x4, matrix products: 39.8 us -> 4.58 us  [the longest x2 2.76 us: matmul(): return lax.dot_general(a, b, dims, preferred_element_type=F32)]
    pallas_call x0 -> x5, Pallas kernels: none -> 32.7 us  [call(): pl.pallas_call(kernel, out_shape=outs[0] if single else outs, in_specs=[p...]
  transfers between devices with their start and end apart: 10 -> 37, of which waited for: 8 -> 12; matrix products, arithmetic and copies ran while one was open for 11% -> 4% of each run, Pallas kernels for 0% -> 7%
where the time goes in v3:
time: 427 us; the launch traced here: 423 us
  waiting for transfers between devices  226 us (53%)
  starting transfers between devices  110 us (26%)
  Pallas kernels  32.7 us (8%)
  local copies, waits for them, and re-layouts  21.1 us (5%)
  blocking collectives  18.5 us (4%)
  other arithmetic  8.34 us (2%)
  matrix products  4.58 us (1%)
    ppermute x12, waiting for transfers between devices, move(): return lax.ppermute(block, 'dp', pairs)  87.3 us
    all_to_all x1, waiting for transfers between devices, shards(): lax.all_to_all(image_flat, 'dp', split_axis=1, concat_axis=0, tiled=True)  54.4 us
    ppermute x4, waiting for transfers between devices, tensor_swap(): lax.ppermute(block, 'tensor', [(t, t ^ bit) for t in range(n_tensor)])  33.7 us
    pallas_call x5, Pallas kernels, call(): pl.pallas_call(kernel, out_shape=outs[0] if single else outs, in_specs=[p...  32.7 us
    ppermute x12, starting transfers between devices, move(): return lax.ppermute(block, 'dp', pairs)  32.2 us
    ppermute x13, waiting for transfers between devices, swap(): return lax.ppermute(block, 'dp', pairs)  32.2 us
    ppermute x13, starting transfers between devices, swap(): return lax.ppermute(block, 'dp', pairs)  23.7 us
    all_to_all x1, blocking collectives, shards(): lax.all_to_all(part_kv, 'dp', split_axis=0, concat_axis=0)  18.5 us
  transfers between devices with their start and end apart: 37, of which 12 were waited for; matrix products, arithmetic and copies ran while one was open for 4% of the time, Pallas kernels for 7%

profile of v3, /device:TPU:4, one launch (start us, length us, event | category | flops | bytes accessed | tf_op | source)
XLA Modules:
  0.0 422.6 jit_solution(7570794458200567997)
XLA Ops:
  0.7 2.4 constant_dynamic-slice_fusion.3
  3.1 1.5 collective-permute-start
  4.7 1.6 broadcast_select_fusion
  6.2 2.4 constant_dynamic-slice_fusion.1
  9.2 1.5 collective-permute-start.4
  12.0 3.7 collective-permute-start.2
  15.7 2.6 collective-permute-done
  18.2 4.5 %collective-permute-start.3 = (bf16[512,1024]{1,0:T(8,128)(2,1)S(1)}, bf16[512,1024]{1,0:T(8,128)(2,1)}, u32[]{:S(2)}, u32[]{:S(2)}) collective-permute-start(bf16[512,1024]{1,0:T(8,128)(2,1)S(1)} %copy-done.1), channel_id=1, source_target_pairs={{0,8},{4,12},{8,16},{12,20},{16,24},{20,28},{1,9},{5,13},{9,17},{1... | collective-permute-start | bytes 3145736 | tf_op jit(solution)/shard_map/ppermute | solution.py:35
  23.4 3.8 all-to-all-start
  27.2 2.4 pad_maximum_fusion.refs_0_
  29.6 54.4 %all-to-all-done = bf16[8,8,512]{2,0,1:T(8,128)(2,1)S(1)} async-done(((bf16[8,8,512]{2,0,1:T(8,128)(2,1)}), bf16[8,8,512]{2,0,1:T(8,128)(2,1)S(1)}, u32[]{:S(2)}, u32[]{:S(2)}) %all-to-all-start) | async-done | bytes 65568 | tf_op jit(solution)/shard_map/all_to_all | solution.py:253
  85.3 3.4 collective-permute-start.7
  88.7 4.0 collective-permute-start.8
  95.5 1.5 fusion.6
  97.0 15.9 %collective-permute-done.6.refs_1_ = bf16[512,1024]{1,0:T(8,128)(2,1)S(1)} collective-permute-done((bf16[512,1024]{1,0:T(8,128)(2,1)}, bf16[512,1024]{1,0:T(8,128)(2,1)S(1)}, u32[]{:S(2)}, u32[]{:S(2)}) %collective-permute-start.6) | collective-permute-done | bytes 1048608 | tf_op jit(solution)/shard_map/ppermute | solution.py:35
  113.9 3.5 collective-permute-start.10
  117.3 39.6 %collective-permute-done.7.refs_2_ = bf16[512,1024]{1,0:T(8,128)(2,1)} collective-permute-done((bf16[512,1024]{1,0:T(8,128)(2,1)}, bf16[512,1024]{1,0:T(8,128)(2,1)}, u32[]{:S(2)}, u32[]{:S(2)}) %collective-permute-start.7) | collective-permute-done | bytes 1048608 | tf_op jit(solution)/shard_map/ppermute | solution.py:35
  156.9 1.6 collective-permute-start.12
  159.6 18.5 %all_to_all.84 = f32[8,8,2048]{2,1,0:T(8,128)} all-to-all(f32[8,8,2048]{2,1,0:T(8,128)S(1)} %maximum_bitcast_fusion), channel_id=1, replica_groups=mesh['dp'=8,'tensor'=4] {'dp'}, dimensions={0} | all-to-all | bytes 1048576 | tf_op jit(solution)/shard_map/all_to_all | solution.py:268
  180.5 3.4 collective-permute-start.14
  184.6 11.2 %all-to-all-start.2 = ((bf16[8,8,2048]{2,1,0:T(8,128)(2,1)}), bf16[8,8,2048]{2,1,0:T(8,128)(2,1)S(1)}, u32[]{:S(2)}, u32[]{:S(2)}) async-start(bf16[8,8,2048]{2,1,0:T(8,128)(2,1)} %broadcast_in_dim.18), calls=%async_computation.2 | async-start | bytes 524288 | tf_op jit(solution)/shard_map/all_to_all | solution.py:273
  195.9 13.5 %collective-permute-done.19.refs_4_ = bf16[512,1024]{1,0:T(8,128)(2,1)} collective-permute-done((bf16[512,1024]{1,0:T(8,128)(2,1)}, bf16[512,1024]{1,0:T(8,128)(2,1)}, u32[]{:S(2)}, u32[]{:S(2)}) %collective-permute-start.19) | collective-permute-done | bytes 1048608 | tf_op jit(solution)/shard_map/ppermute | solution.py:35
  211.9 7.3 %shard_map.104 = (bf16[256,512]{1,0:T(8,128)(2,1)S(1)}, bf16[256,512]{1,0:T(8,128)(2,1)}) custom-call(s32[3]{0:T(128)S(1)} %pad_add_fusion.place, bf16[256,4096]{1,0:T(8,128)(2,1)} %bitcast.38, bf16[256,2048]{1,0:T(8,128)(2,1)} %collective-permute-done.5.here, bf16[256,2048]{1,0:T(8,128)(2,1)} %collective-permute-done.13.there, ...), custom_call_target="tpu_custom_call" | custom-call | flops 2147483648 | bytes 9961472 | tf_op jit(solution)/shard_map/pallas_call | solution.py:196
  219.9 1.8 collective-permute-start.20
  221.6 8.2 %shard_map.103 = (bf16[256,1024]{1,0:T(8,128)(2,1)S(1)}, bf16[256,1024]{1,0:T(8,128)(2,1)S(1)}) custom-call(s32[3]{0:T(128)S(1)} %pad_add_fusion.place, bf16[256,4096]{1,0:T(8,128)(2,1)} %bitcast.41, bf16[64,2048]{1,0:T(8,128)(2,1)S(1)} %bitcast.34, bf16[512,1024]{1,0:T(8,128)(2,1)S(1)} %copy-done.1, bf16[512,1024]{1,0:T(8,128)(2,1)S(1)} %collective-permute-done.1.refs_1_, ...), custom_call_target="tpu_custom_call" | custom-call | flops 2147483648 | bytes 13893632 | tf_op jit(solution)/shard_map/pallas_call | solution.py:196
  229.8 2.5 shard_map.105
  233.9 9.4 %all-to-all-start.4 = ((f32[8,8,2048]{2,1,0:T(8,128)}), f32[8,8,2048]{2,1,0:T(8,128)}, u32[]{:S(2)}, u32[]{:S(2)}) async-start(f32[8,8,2048]{2,1,0:T(8,128)} %bitcast.36), calls=%async_computation.4 | async-start | bytes 1048576 | tf_op jit(solution)/shard_map/all_to_all | solution.py:344
  243.4 11.4 %all-to-all-done.4 = f32[8,8,2048]{2,1,0:T(8,128)} async-done(((f32[8,8,2048]{2,1,0:T(8,128)}), f32[8,8,2048]{2,1,0:T(8,128)}, u32[]{:S(2)}, u32[]{:S(2)}) %all-to-all-start.4) | async-done | bytes 524320 | tf_op jit(solution)/shard_map/all_to_all | solution.py:344
  256.6 3.7 all-to-all-start.5
  262.5 6.0 %all-to-all-done.5 = bf16[8,8,2048]{2,1,0:T(8,128)(2,1)S(1)} async-done(((bf16[8,8,2048]{2,1,0:T(8,128)(2,1)}), bf16[8,8,2048]{2,1,0:T(8,128)(2,1)S(1)}, u32[]{:S(2)}, u32[]{:S(2)}) %all-to-all-start.5) | async-done | bytes 262176 | tf_op jit(solution)/shard_map/all_to_all | solution.py:273
  268.5 4.2 all-to-all-start.8
  272.7 1.3 collective-permute-start.15
  274.0 4.0 collective-permute-start.16
  278.0 4.9 %collective-permute-start.17 = (bf16[256,1024]{1,0:T(8,128)(2,1)}, bf16[256,1024]{1,0:T(8,128)(2,1)}, u32[]{:S(2)}, u32[]{:S(2)}) collective-permute-start(bf16[256,1024]{1,0:T(8,128)(2,1)} %copy-done.5), channel_id=1, source_target_pairs={{0,8},{4,12},{8,16},{12,20},{16,24},{20,28},{1,9},{5,13},{9,17},{1... | collective-permute-start | bytes 1572872 | tf_op jit(solution)/shard_map/ppermute | solution.py:35
  282.9 1.5 collective-permute-start.18
  284.8 2.3 fusion.1
  287.1 13.5 %all-to-all-start.6 = ((bf16[8,8,512]{2,1,0:T(8,128)(2,1)}), bf16[8,8,512]{2,1,0:T(8,128)(2,1)}, u32[]{:S(2)}, u32[]{:S(2)}) async-start(bf16[8,8,512]{2,1,0:T(8,128)(2,1)} %fusion.1), calls=%async_computation.6 | async-start | bytes 131072 | tf_op jit(solution)/shard_map/all_to_all | solution.py:348
  300.7 18.4 %collective-permute-done.16.refs_6_ = bf16[256,1024]{1,0:T(8,128)(2,1)} collective-permute-done((bf16[256,1024]{1,0:T(8,128)(2,1)}, bf16[256,1024]{1,0:T(8,128)(2,1)}, u32[]{:S(2)}, u32[]{:S(2)}) %collective-permute-start.16) | collective-permute-done | bytes 524320 | tf_op jit(solution)/shard_map/ppermute | solution.py:35
  320.0 3.8 all-to-all-start.7
  324.8 8.2 %shard_map.106 = bf16[8,256,512]{2,1,0:T(8,128)(2,1)} custom-call(s32[3]{0:T(128)S(1)} %pad_add_fusion.place, bf16[256,1024]{1,0:T(8,128)(2,1)S(1)} %copy-done.8, bf16[512,1024]{1,0:T(8,128)(2,1)S(1)} %copy-done.1, bf16[512,1024]{1,0:T(8,128)(2,1)S(1)} %collective-permute-done.1.refs_1_, bf16[512,1024]{1,0:T(8,128)(2,1)} %collective-permute-done.2.refs_2_, ...), custom_call_target="tpu_custom_call" | custom-call | flops 2147483648 | bytes 13107200 | tf_op jit(solution)/shard_map/pallas_call | solution.py:196
  332.9 4.5 %all-to-all-start.3 = ((bf16[4,2,256,512]{3,2,1,0:T(8,128)(2,1)}), bf16[4,2,256,512]{3,2,1,0:T(8,128)(2,1)}, u32[]{:S(2)}, u32[]{:S(2)}) async-start(bf16[4,2,256,512]{3,2,1,0:T(8,128)(2,1)} %bitcast.40), calls=%async_computation.3 | async-start | bytes 4194304 | tf_op jit(solution)/shard_map/all_to_all | solution.py:338
  339.0 33.7 %collective-permute-done.21.refs_1_ = bf16[8,64,512]{2,1,0:T(8,128)(2,1)S(1)} collective-permute-done((bf16[8,64,512]{2,1,0:T(8,128)(2,1)}, bf16[8,64,512]{2,1,0:T(8,128)(2,1)S(1)}, u32[]{:S(2)}, u32[]{:S(2)}) %collective-permute-start.21) | collective-permute-done | bytes 524320 | tf_op jit(solution)/shard_map/ppermute | solution.py:237
  373.5 3.1 collective-permute-start.25
  377.3 2.7 collective-permute-start.28
  380.1 18.8 %collective-permute-done.25.refs_10_ = bf16[256,1024]{1,0:T(8,128)(2,1)S(1)} collective-permute-done((bf16[256,1024]{1,0:T(8,128)(2,1)}, bf16[256,1024]{1,0:T(8,128)(2,1)S(1)}, u32[]{:S(2)}, u32[]{:S(2)}) %collective-permute-start.25) | collective-permute-done | bytes 524320 | tf_op jit(solution)/shard_map/ppermute | solution.py:40
  398.9 10.8 %collective-permute-done.28.refs_13_ = bf16[256,1024]{1,0:T(8,128)(2,1)S(1)} collective-permute-done((bf16[256,1024]{1,0:T(8,128)(2,1)S(1)}, bf16[256,1024]{1,0:T(8,128)(2,1)S(1)}, u32[]{:S(2)}, u32[]{:S(2)}) %collective-permute-start.28) | collective-permute-done | bytes 524320 | tf_op jit(solution)/shard_map/ppermute | solution.py:40
  411.5 6.6 %shard_map.107 = bf16[1024,512]{1,0:T(8,128)(2,1)} custom-call(s32[3]{0:T(128)S(1)} %pad_add_fusion.place, bf16[8,64,512]{2,1,0:T(8,128)(2,1)} %bitcast.20.refs_0_, bf16[8,64,512]{2,1,0:T(8,128)(2,1)S(1)} %collective-permute-done.21.refs_1_, bf16[8,64,512]{2,1,0:T(8,128)(2,1)S(1)} %collective-permute-done.22.refs_2_, ...), custom_call_target="tpu_custom_call" | custom-call | flops 2147483648 | bytes 8388608 | tf_op jit(solution)/shard_map/pallas_call | solution.py:196
  418.8 2.1 reduce_sum.43
  (96 shorter events, 30.3 us)
Async XLA Ops:
  0.6 94.6 %copy-start = (bf16[512,1024]{1,0:T(8,128)(2,1)S(1)}, bf16[512,1024]{1,0:T(8,128)(2,1)}, u32[]{:S(2)}) copy-start(bf16[512,1024]{1,0:T(8,128)(2,1)} %param.13) | copy-start | bytes 3145732
  0.6 4.0 copy-start.18
  0.7 4.0 copy-start.12
  3.1 15.1 %collective-permute-start = (bf16[512,512]{1,0:T(8,128)(2,1)}, bf16[512,512]{1,0:T(8,128)(2,1)}, u32[]{:S(2)}, u32[]{:S(2)}) collective-permute-start(bf16[512,512]{1,0:T(8,128)(2,1)} %get-tuple-element.50), channel_id=1, source_target_pairs={{0,4},{4,0},{8,12},{12,8},{16,20},{20,16},{24,28},{28,24},{1,5},{5... | collective-permute-start | bytes 1572872 | tf_op jit(solution)/shard_map/ppermute | solution.py:40
  6.2 2.9 copy-start.1
  6.2 16.5 %copy-start.17 = (bf16[2,4,4096]{2,1,0:T(4,128)(2,1)S(1)}, bf16[2,4,4096]{2,1,0:T(4,128)(2,1)}, u32[]{:S(2)}) copy-start(bf16[2,4,4096]{2,1,0:T(4,128)(2,1)} %param.9) | copy-start | bytes 196612
  8.6 75.3 %collective-permute-start.5 = (bf16[256,2048]{1,0:T(8,128)(2,1)}, bf16[256,2048]{1,0:T(8,128)(2,1)}, u32[]{:S(2)}, u32[]{:S(2)}) collective-permute-start(bf16[256,2048]{1,0:T(8,128)(2,1)} %constant_dynamic-slice_fusion.1), channel_id=1, source_target_pairs={{0,4},{4,0},{8,12},{12,8},{16,20},{20,16},{24,28},{28,24},{1,5},{5... | collective-permute-start | bytes 3145736 | tf_op jit(solution)/shard_map/ppermute | solution.py:40
  9.2 74.8 %collective-permute-start.4 = (bf16[512,1024]{1,0:T(8,128)(2,1)S(1)}, bf16[512,1024]{1,0:T(8,128)(2,1)}, u32[]{:S(2)}, u32[]{:S(2)}) collective-permute-start(bf16[512,1024]{1,0:T(8,128)(2,1)S(1)} %copy-done.1), channel_id=1, source_target_pairs={{0,4},{4,0},{8,12},{12,8},{16,20},{20,16},{24,28},{28,24},{1,5},{5... | collective-permute-start | bytes 3145736 | tf_op jit(solution)/shard_map/ppermute | solution.py:40
  10.7 73.3 %collective-permute-start.1 = (bf16[512,1024]{1,0:T(8,128)(2,1)S(1)}, bf16[512,1024]{1,0:T(8,128)(2,1)S(1)}, u32[]{:S(2)}, u32[]{:S(2)}) collective-permute-start(bf16[512,1024]{1,0:T(8,128)(2,1)S(1)} %copy-done.1), channel_id=1, source_target_pairs={{8,0},{12,4},{16,8},{20,12},{24,16},{28,20},{9,1},{13,5},{17,9},{2... | collective-permute-start | bytes 3145736 | tf_op jit(solution)/shard_map/ppermute | solution.py:35
  12.0 72.0 %collective-permute-start.2 = (bf16[512,1024]{1,0:T(8,128)(2,1)S(1)}, bf16[512,1024]{1,0:T(8,128)(2,1)}, u32[]{:S(2)}, u32[]{:S(2)}) collective-permute-start(bf16[512,1024]{1,0:T(8,128)(2,1)S(1)} %copy-done.1), channel_id=1, source_target_pairs={{0,16},{4,20},{8,24},{12,28},{16,0},{20,4},{24,8},{28,12},{1,17},{... | collective-permute-start | bytes 3145736 | tf_op jit(solution)/shard_map/ppermute | solution.py:35
  18.2 65.8 %collective-permute-start.3 = (bf16[512,1024]{1,0:T(8,128)(2,1)S(1)}, bf16[512,1024]{1,0:T(8,128)(2,1)}, u32[]{:S(2)}, u32[]{:S(2)}) collective-permute-start(bf16[512,1024]{1,0:T(8,128)(2,1)S(1)} %copy-done.1), channel_id=1, source_target_pairs={{0,8},{4,12},{8,16},{12,20},{16,24},{20,28},{1,9},{5,13},{9,17},{1... | collective-permute-start | bytes 3145736 | tf_op jit(solution)/shard_map/ppermute | solution.py:35
  23.4 60.6 %all-to-all-start = ((bf16[8,8,512]{2,0,1:T(8,128)(2,1)}), bf16[8,8,512]{2,0,1:T(8,128)(2,1)S(1)}, u32[]{:S(2)}, u32[]{:S(2)}) async-start(bf16[8,8,512]{2,0,1:T(8,128)(2,1)} %copy.20), calls=%async_computation | async-start | bytes 131072 | tf_op jit(solution)/shard_map/all_to_all | solution.py:253
  84.0 28.9 %collective-permute-start.6 = (bf16[512,1024]{1,0:T(8,128)(2,1)}, bf16[512,1024]{1,0:T(8,128)(2,1)S(1)}, u32[]{:S(2)}, u32[]{:S(2)}) collective-permute-start(bf16[512,1024]{1,0:T(8,128)(2,1)} %pad_maximum_fusion.refs_0_), channel_id=1, source_target_pairs={{8,0},{12,4},{16,8},{20,12},{24,16},{28,20},{9,1},{13,5},{17,9},{2... | collective-permute-start | bytes 3145736 | tf_op jit(solution)/shard_map/ppermute | solution.py:35
  85.3 71.6 %collective-permute-start.7 = (bf16[512,1024]{1,0:T(8,128)(2,1)}, bf16[512,1024]{1,0:T(8,128)(2,1)}, u32[]{:S(2)}, u32[]{:S(2)}) collective-permute-start(bf16[512,1024]{1,0:T(8,128)(2,1)} %pad_maximum_fusion.refs_0_), channel_id=1, source_target_pairs={{0,16},{4,20},{8,24},{12,28},{16,0},{20,4},{24,8},{28,12},{1,17},{... | collective-permute-start | bytes 3145736 | tf_op jit(solution)/shard_map/ppermute | solution.py:35
  88.7 69.9 %collective-permute-start.8 = (bf16[512,1024]{1,0:T(8,128)(2,1)}, bf16[512,1024]{1,0:T(8,128)(2,1)S(1)}, u32[]{:S(2)}, u32[]{:S(2)}) collective-permute-start(bf16[512,1024]{1,0:T(8,128)(2,1)} %pad_maximum_fusion.refs_0_), channel_id=1, source_target_pairs={{0,8},{4,12},{8,16},{12,20},{16,24},{20,28},{1,9},{5,13},{9,17},{1... | collective-permute-start | bytes 3145736 | tf_op jit(solution)/shard_map/ppermute | solution.py:35
  92.7 86.5 %collective-permute-start.11 = (bf16[512,1024]{1,0:T(8,128)(2,1)}, bf16[512,1024]{1,0:T(8,128)(2,1)}, u32[]{:S(2)}, u32[]{:S(2)}) collective-permute-start(bf16[512,1024]{1,0:T(8,128)(2,1)} %collective-permute-done.2.refs_2_), channel_id=1, source_target_pairs={{0,4},{4,0},{8,12},{12,8},{16,20},{20,16},{24,28},{28,24},{1,5},{5... | collective-permute-start | bytes 3145736 | tf_op jit(solution)/shard_map/ppermute | solution.py:40
  93.9 85.3 %collective-permute-start.9 = (bf16[512,1024]{1,0:T(8,128)(2,1)}, bf16[512,1024]{1,0:T(8,128)(2,1)}, u32[]{:S(2)}, u32[]{:S(2)}) collective-permute-start(bf16[512,1024]{1,0:T(8,128)(2,1)} %collective-permute-done.2.refs_2_), channel_id=1, source_target_pairs={{8,0},{12,4},{16,24},{20,28},{9,1},{13,5},{17,25},{21,29},{10,2},{... | collective-permute-start | bytes 3145736 | tf_op jit(solution)/shard_map/ppermute | solution.py:35
  113.9 65.3 %collective-permute-start.10 = (bf16[512,1024]{1,0:T(8,128)(2,1)S(1)}, bf16[512,1024]{1,0:T(8,128)(2,1)}, u32[]{:S(2)}, u32[]{:S(2)}) collective-permute-start(bf16[512,1024]{1,0:T(8,128)(2,1)S(1)} %collective-permute-done.1.refs_1_), channel_id=1, source_target_pairs={{0,4},{4,0},{8,12},{12,8},{16,20},{20,16},{1,5},{5,1},{9,13},{13,9... | collective-permute-start | bytes 3145736 | tf_op jit(solution)/shard_map/ppermute | solution.py:40
  156.9 22.3 %collective-permute-start.12 = (bf16[512,1024]{1,0:T(8,128)(2,1)}, bf16[512,1024]{1,0:T(8,128)(2,1)}, u32[]{:S(2)}, u32[]{:S(2)}) collective-permute-start(bf16[512,1024]{1,0:T(8,128)(2,1)} %collective-permute-done.3.refs_3_), channel_id=1, source_target_pairs={{8,12},{12,8},{16,20},{20,16},{24,28},{28,24},{9,13},{13,9},{17,21... | collective-permute-start | bytes 3145736 | tf_op jit(solution)/shard_map/ppermute | solution.py:40
  159.5 19.7 %collective-permute-start.13 = (bf16[256,2048]{1,0:T(8,128)(2,1)}, bf16[256,2048]{1,0:T(8,128)(2,1)}, u32[]{:S(2)}, u32[]{:S(2)}) collective-permute-start(bf16[256,2048]{1,0:T(8,128)(2,1)} %collective-permute-done.5.here), channel_id=1, source_target_pairs={{0,1},{1,0},{2,3},{3,2},{4,5},{5,4},{6,7},{7,6},{8,9},{9,8},{10,11... | collective-permute-start | bytes 3145736 | tf_op jit(solution)/shard_map/ppermute | solution.py:237
  179.2 30.2 %collective-permute-start.19 = (bf16[512,1024]{1,0:T(8,128)(2,1)}, bf16[512,1024]{1,0:T(8,128)(2,1)}, u32[]{:S(2)}, u32[]{:S(2)}) collective-permute-start(bf16[512,1024]{1,0:T(8,128)(2,1)} %collective-permute-done.7.refs_2_), channel_id=1, source_target_pairs={{8,0},{12,4},{16,24},{20,28},{9,1},{13,5},{17,25},{21,29},{10,2},{... | collective-permute-start | bytes 3145736 | tf_op jit(solution)/shard_map/ppermute | solution.py:35
  180.5 41.1 %collective-permute-start.14 = (bf16[512,1024]{1,0:T(8,128)(2,1)}, bf16[512,1024]{1,0:T(8,128)(2,1)}, u32[]{:S(2)}, u32[]{:S(2)}) collective-permute-start(bf16[512,1024]{1,0:T(8,128)(2,1)} %collective-permute-done.9.refs_4_), channel_id=1, source_target_pairs={{0,4},{4,0},{24,28},{28,24},{1,5},{5,1},{25,29},{29,25},{2,6},{6,2... | collective-permute-start | bytes 3145736 | tf_op jit(solution)/shard_map/ppermute | solution.py:40
  184.6 37.0 %all-to-all-start.2 = ((bf16[8,8,2048]{2,1,0:T(8,128)(2,1)}), bf16[8,8,2048]{2,1,0:T(8,128)(2,1)S(1)}, u32[]{:S(2)}, u32[]{:S(2)}) async-start(bf16[8,8,2048]{2,1,0:T(8,128)(2,1)} %broadcast_in_dim.18), calls=%async_computation.2 | async-start | bytes 524288 | tf_op jit(solution)/shard_map/all_to_all | solution.py:273
  209.4 1.2 copy-start.2
  210.7 1.2 copy-start.4
  219.9 10.0 %collective-permute-start.20 = (bf16[256,512]{1,0:T(8,128)(2,1)}, bf16[256,512]{1,0:T(8,128)(2,1)}, u32[]{:S(2)}, u32[]{:S(2)}) collective-permute-start(bf16[256,512]{1,0:T(8,128)(2,1)} %get-tuple-element.40), channel_id=1, source_target_pairs={{0,4},{4,0},{8,12},{12,8},{16,20},{20,16},{24,28},{28,24},{1,5},{5... | collective-permute-start | bytes 786440 | tf_op jit(solution)/shard_map/ppermute | solution.py:40
  221.6 8.2 %copy-start.11 = (bf16[256,512]{1,0:T(8,128)(2,1)S(1)}, bf16[256,512]{1,0:T(8,128)(2,1)}, u32[]{:S(2)}) copy-start(bf16[256,512]{1,0:T(8,128)(2,1)} %copy-done.10) | copy-start | bytes 786436
  229.8 2.5 copy-start.5
  233.9 20.9 %all-to-all-start.4 = ((f32[8,8,2048]{2,1,0:T(8,128)}), f32[8,8,2048]{2,1,0:T(8,128)}, u32[]{:S(2)}, u32[]{:S(2)}) async-start(f32[8,8,2048]{2,1,0:T(8,128)} %bitcast.36), calls=%async_computation.4 | async-start | bytes 1048576 | tf_op jit(solution)/shard_map/all_to_all | solution.py:344
  256.6 11.9 %all-to-all-start.5 = ((bf16[8,8,2048]{2,1,0:T(8,128)(2,1)}), bf16[8,8,2048]{2,1,0:T(8,128)(2,1)S(1)}, u32[]{:S(2)}, u32[]{:S(2)}) async-start(bf16[8,8,2048]{2,1,0:T(8,128)(2,1)} %broadcast_in_dim.32), calls=%async_computation.5 | async-start | bytes 524288 | tf_op jit(solution)/shard_map/all_to_all | solution.py:273
  268.5 18.6 %all-to-all-start.8 = ((bf16[1,64,8,512]{3,1,0,2:T(8,128)(2,1)}), bf16[1,64,8,512]{3,1,0,2:T(8,128)(2,1)}, u32[]{:S(2)}, u32[]{:S(2)}) async-start(bf16[1,64,8,512]{3,1,0,2:T(8,128)(2,1)} %copy.24), calls=%async_computation.8 | async-start | bytes 1048576 | tf_op jit(solution)/shard_map/all_to_all | solution.py:286
  272.7 28.0 %collective-permute-start.15 = (bf16[256,1024]{1,0:T(8,128)(2,1)}, bf16[256,1024]{1,0:T(8,128)(2,1)}, u32[]{:S(2)}, u32[]{:S(2)}) collective-permute-start(bf16[256,1024]{1,0:T(8,128)(2,1)} %copy-done.5), channel_id=1, source_target_pairs={{8,0},{12,4},{16,8},{20,12},{24,16},{28,20},{9,1},{13,5},{17,9},{2... | collective-permute-start | bytes 1572872 | tf_op jit(solution)/shard_map/ppermute | solution.py:35
  274.0 45.1 %collective-permute-start.16 = (bf16[256,1024]{1,0:T(8,128)(2,1)}, bf16[256,1024]{1,0:T(8,128)(2,1)}, u32[]{:S(2)}, u32[]{:S(2)}) collective-permute-start(bf16[256,1024]{1,0:T(8,128)(2,1)} %copy-done.5), channel_id=1, source_target_pairs={{0,16},{4,20},{8,24},{12,28},{16,0},{20,4},{24,8},{28,12},{1,17},{... | collective-permute-start | bytes 1572872 | tf_op jit(solution)/shard_map/ppermute | solution.py:35
  278.0 41.0 %collective-permute-start.17 = (bf16[256,1024]{1,0:T(8,128)(2,1)}, bf16[256,1024]{1,0:T(8,128)(2,1)}, u32[]{:S(2)}, u32[]{:S(2)}) collective-permute-start(bf16[256,1024]{1,0:T(8,128)(2,1)} %copy-done.5), channel_id=1, source_target_pairs={{0,8},{4,12},{8,16},{12,20},{16,24},{20,28},{1,9},{5,13},{9,17},{1... | collective-permute-start | bytes 1572872 | tf_op jit(solution)/shard_map/ppermute | solution.py:35
  282.9 36.1 %collective-permute-start.18 = (bf16[256,1024]{1,0:T(8,128)(2,1)}, bf16[256,1024]{1,0:T(8,128)(2,1)}, u32[]{:S(2)}, u32[]{:S(2)}) collective-permute-start(bf16[256,1024]{1,0:T(8,128)(2,1)} %copy-done.5), channel_id=1, source_target_pairs={{0,4},{4,0},{8,12},{12,8},{16,20},{20,16},{24,28},{28,24},{1,5},{5... | collective-permute-start | bytes 1572872 | tf_op jit(solution)/shard_map/ppermute | solution.py:40
  287.1 32.8 %all-to-all-start.6 = ((bf16[8,8,512]{2,1,0:T(8,128)(2,1)}), bf16[8,8,512]{2,1,0:T(8,128)(2,1)}, u32[]{:S(2)}, u32[]{:S(2)}) async-start(bf16[8,8,512]{2,1,0:T(8,128)(2,1)} %fusion.1), calls=%async_computation.6 | async-start | bytes 131072 | tf_op jit(solution)/shard_map/all_to_all | solution.py:348
  320.0 13.0 %all-to-all-start.7 = ((bf16[1,8,4,1024]{3,1,0,2:T(8,128)(2,1)}), bf16[1,8,4,1024]{3,1,0,2:T(8,128)(2,1)S(1)}, u32[]{:S(2)}, u32[]{:S(2)}) async-start(bf16[1,8,4,1024]{3,1,0,2:T(8,128)(2,1)} %bitcast.16), calls=%async_computation.7 | async-start | bytes 131072 | tf_op jit(solution)/shard_map/all_to_all | solution.py:351
  332.9 85.8 %all-to-all-start.3 = ((bf16[4,2,256,512]{3,2,1,0:T(8,128)(2,1)}), bf16[4,2,256,512]{3,2,1,0:T(8,128)(2,1)}, u32[]{:S(2)}, u32[]{:S(2)}) async-start(bf16[4,2,256,512]{3,2,1,0:T(8,128)(2,1)} %bitcast.40), calls=%async_computation.3 | async-start | bytes 4194304 | tf_op jit(solution)/shard_map/all_to_all | solution.py:338
  337.4 35.3 %collective-permute-start.21 = (bf16[8,64,512]{2,1,0:T(8,128)(2,1)}, bf16[8,64,512]{2,1,0:T(8,128)(2,1)S(1)}, u32[]{:S(2)}, u32[]{:S(2)}) collective-permute-start(bf16[8,64,512]{2,1,0:T(8,128)(2,1)} %bitcast.20.refs_0_), channel_id=1, source_target_pairs={{0,2},{1,3},{2,0},{3,1},{4,6},{5,7},{6,4},{7,5},{8,10},{9,11},{10,... | collective-permute-start | bytes 1572872 | tf_op jit(solution)/shard_map/ppermute | solution.py:237
  337.5 39.1 %collective-permute-start.22 = (bf16[8,64,512]{2,1,0:T(8,128)(2,1)}, bf16[8,64,512]{2,1,0:T(8,128)(2,1)S(1)}, u32[]{:S(2)}, u32[]{:S(2)}) collective-permute-start(bf16[8,64,512]{2,1,0:T(8,128)(2,1)} %bitcast.20.refs_0_), channel_id=1, source_target_pairs={{0,1},{1,0},{2,3},{3,2},{4,5},{5,4},{6,7},{7,6},{8,9},{9,8},{10,11... | collective-permute-start | bytes 1572872 | tf_op jit(solution)/shard_map/ppermute | solution.py:237
  337.7 39.6 %collective-permute-start.24 = (bf16[256,1024]{1,0:T(8,128)(2,1)}, bf16[256,1024]{1,0:T(8,128)(2,1)S(1)}, u32[]{:S(2)}, u32[]{:S(2)}) collective-permute-start(bf16[256,1024]{1,0:T(8,128)(2,1)} %collective-permute-done.16.refs_6_), channel_id=1, source_target_pairs={{8,0},{12,4},{16,24},{20,28},{9,1},{13,5},{17,25},{21,29},{10,2},{... | collective-permute-start | bytes 1572872 | tf_op jit(solution)/shard_map/ppermute | solution.py:35
  372.7 7.4 %collective-permute-start.23 = (bf16[8,64,512]{2,1,0:T(8,128)(2,1)S(1)}, bf16[8,64,512]{2,1,0:T(8,128)(2,1)S(1)}, u32[]{:S(2)}, u32[]{:S(2)}) collective-permute-start(bf16[8,64,512]{2,1,0:T(8,128)(2,1)S(1)} %collective-permute-done.21.refs_1_), channel_id=1, source_target_pairs={{0,1},{1,0},{2,3},{3,2},{4,5},{5,4},{6,7},{7,6},{8,9},{9,8},{10,11... | collective-permute-start | bytes 1572872 | tf_op jit(solution)/shard_map/ppermute | solution.py:237
  372.7 26.2 %collective-permute-start.26 = (bf16[256,1024]{1,0:T(8,128)(2,1)}, bf16[256,1024]{1,0:T(8,128)(2,1)S(1)}, u32[]{:S(2)}, u32[]{:S(2)}) collective-permute-start(bf16[256,1024]{1,0:T(8,128)(2,1)} %collective-permute-done.16.refs_6_), channel_id=1, source_target_pairs={{0,4},{4,0},{8,12},{12,8},{16,20},{20,16},{24,28},{28,24},{1,5},{5... | collective-permute-start | bytes 1572872 | tf_op jit(solution)/shard_map/ppermute | solution.py:40
  373.5 25.3 %collective-permute-start.25 = (bf16[256,1024]{1,0:T(8,128)(2,1)}, bf16[256,1024]{1,0:T(8,128)(2,1)S(1)}, u32[]{:S(2)}, u32[]{:S(2)}) collective-permute-start(bf16[256,1024]{1,0:T(8,128)(2,1)} %collective-permute-done.15.refs_5_), channel_id=1, source_target_pairs={{0,4},{4,0},{8,12},{12,8},{16,20},{20,16},{1,5},{5,1},{9,13},{13,9... | collective-permute-start | bytes 1572872 | tf_op jit(solution)/shard_map/ppermute | solution.py:40
  376.6 22.2 %collective-permute-start.27 = (bf16[256,1024]{1,0:T(8,128)(2,1)}, bf16[256,1024]{1,0:T(8,128)(2,1)S(1)}, u32[]{:S(2)}, u32[]{:S(2)}) collective-permute-start(bf16[256,1024]{1,0:T(8,128)(2,1)} %collective-permute-done.17.refs_7_), channel_id=1, source_target_pairs={{8,12},{12,8},{16,20},{20,16},{24,28},{28,24},{9,13},{13,9},{17,21... | collective-permute-start | bytes 1572872 | tf_op jit(solution)/shard_map/ppermute | solution.py:40
  377.3 32.4 %collective-permute-start.28 = (bf16[256,1024]{1,0:T(8,128)(2,1)S(1)}, bf16[256,1024]{1,0:T(8,128)(2,1)S(1)}, u32[]{:S(2)}, u32[]{:S(2)}) collective-permute-start(bf16[256,1024]{1,0:T(8,128)(2,1)S(1)} %collective-permute-done.24.refs_8_), channel_id=1, source_target_pairs={{0,4},{4,0},{24,28},{28,24},{1,5},{5,1},{25,29},{29,25},{2,6},{6,2... | collective-permute-start | bytes 1572872 | tf_op jit(solution)/shard_map/ppermute | solution.py:40
  398.8 10.8 %copy-start.14 = (bf16[256,1024]{1,0:T(8,128)(2,1)}, bf16[256,1024]{1,0:T(8,128)(2,1)S(1)}, u32[]{:S(2)}) copy-start(bf16[256,1024]{1,0:T(8,128)(2,1)S(1)} %collective-permute-done.26.refs_11_) | copy-start | bytes 1572868
  398.9 10.8 %copy-start.15 = (bf16[256,1024]{1,0:T(8,128)(2,1)}, bf16[256,1024]{1,0:T(8,128)(2,1)S(1)}, u32[]{:S(2)}) copy-start(bf16[256,1024]{1,0:T(8,128)(2,1)S(1)} %collective-permute-done.27.refs_12_) | copy-start | bytes 1572868
  (8 other events, 7.1 us)

commit v4 on v3

--- a/solution.py
+++ b/solution.py
@@ -39,29 +39,17 @@
         pairs = [(2 * a + e, 2 * a + 1 - e) for a in planes for e in range(2)]
         return lax.ppermute(block, "dp", pairs)
 
-    def along(self, block):
+    def shift(self, block, distance):
         n = self.n_z
-        if n != 4:
-            return [self.move(block, [((a + m) % n, a) for a in range(n)]) for m in range(1, n)]
+        return self.move(block, [((a + distance) % n, a) for a in range(n)])
+
+    def near(self, block):
         above = self.move(block, [(1, 0), (2, 1), (3, 2)])
         below = self.move(block, [(0, 1), (1, 2), (2, 3)])
-        across = self.move(block, [(0, 2), (1, 3), (2, 0), (3, 1)])
-        return [above, across, below]
-
-    def relay(self, moved):
-        return [self.move(moved[1], [(1, 0), (2, 3)])] if self.n_z == 4 else []
-
-    def swap_moved(self, moved):
-        if self.n_z != 4:
-            return [self.swap(block) for block in moved]
-        planes = ((0, 1, 2), None, (1, 2, 3))
-        return [self.swap(block, at) for block, at in zip(moved, planes)]
-
-    def swap_relayed(self, relayed):
-        return [self.swap(block, (0, 3)) for block in relayed]
-
-    def slots(self, z):
-        if self.n_z != 4:
+        return above, self.shift(block, 2), below
+
+    def slots(self, z, relayed):
+        if not relayed:
             return [(m, None) for m in range(self.n_z)]
         return [
             (0, None),
@@ -72,9 +60,9 @@
         ]
 
 
-def each_block(line, place, body):
+def each_block(line, place, relayed, body):
     z, x = place[0], place[1]
-    for i, (m, came) in enumerate(line.slots(z)):
+    for i, (m, came) in enumerate(line.slots(z, relayed)):
         plane = lax.rem(z + m, line.n_z)
         for e in range(2):
             index = 2 * plane + (x if e == 0 else 1 - x)
@@ -100,7 +88,7 @@
     return expo / jnp.sum(expo, axis=0, keepdims=True)
 
 
-def forward_kernel(line, image_own, place, text, kv, *refs):
+def forward_kernel(line, relayed, image_own, place, text, kv, *refs):
     n = (len(refs) - 3) // 2
     weights, (query_out, attended_out, total) = (refs[:n], refs[n : 2 * n]), refs[2 * n :]
     own_width = weights[0][0].shape[0]
@@ -110,7 +98,7 @@
     def add(i, e, index):
         total[...] += matmul(text[:, columns(index, own_width)], weights[e][i][...])
 
-    each_block(line, place, add)
+    each_block(line, place, relayed, add)
     query_out[...] = total[...].astype(BF16)
     part = rows // 4
     quarter = place[2]
@@ -141,7 +129,7 @@
         other = jnp.where(lax.div(index, half) == core, here[:, inner], there[:, inner])
         send[...] += matmul(other, weight, BACK)
 
-    each_block(line, place, add)
+    each_block(line, place, False, add)
     keep_out[...] = keep[...].astype(BF16)
     send_out[...] = send[...].astype(BF16)
 
@@ -165,28 +153,32 @@
         query_grad[:, at] = matmul(score_grad, kv[:, at], FIRST).astype(BF16)
 
 
-def term_kernel(line, place, query_grad, *refs):
+def term_kernel(line, relayed, place, query_grad, *refs):
+    out = refs[-1]
     n = (len(refs) - 1) // 2
-    weights, out = (refs[:n], refs[n : 2 * n]), refs[-1]
+    weights = (refs[:n], refs[n : 2 * n])
+    chunk = out.shape[1]
 
     def write(i, e, index):
-        out[index] = matmul(query_grad[...], weights[e][i][...], BACK).astype(BF16)
-
-    each_block(line, place, write)
+        term = matmul(query_grad[...], weights[e][i][...], BACK)
+        member = lax.bitwise_xor(lax.div(index, chunk), place[3])
+        out[member, lax.rem(index, chunk)] = term.astype(BF16)
+
+    each_block(line, place, relayed, write)
 
 
 def weight_grad_kernel(line, place, *refs):
-    live, refs = refs[:4], refs[4:]
+    live, refs = refs[:2], refs[2:]
     n = (len(refs) - 2) // 2
     attended, (out, total) = (refs[:n], refs[n : 2 * n]), refs[2 * n :]
     total[...] = jnp.zeros_like(total)
 
     def add(i, e, index):
-        block = jnp.concatenate([part[index] for part in live], axis=0)
+        block = jnp.concatenate([part[i, index] for part in live for i in range(2)], axis=0)
         term = matmul(attended[e][i][...], block, FIRST)
         total[...] += term.astype(BF16).astype(F32)
 
-    each_block(line, place, add)
+    each_block(line, place, False, add)
     out[...] = total[...].astype(BF16)
 
 
@@ -224,7 +216,7 @@
     n_tensor = lax.axis_size("tensor")
     dp_at, tensor_at = lax.axis_index("dp"), lax.axis_index("tensor")
     x, core = dp_at % 2, tensor_at % 2
-    place = jnp.stack([dp_at // 2, x, tensor_at % 4]).astype(jnp.int32)
+    place = jnp.stack([dp_at // 2, x, tensor_at % 4, tensor_at]).astype(jnp.int32)
     rows = samples * tok_rows
     image_rows = samples * image_own
     images = n_dp * image_rows
@@ -243,74 +235,85 @@
     live_flat = grad_live.reshape(rows, width)
     image_flat = image_states.reshape(image_rows, width)
 
-    wq_moved = line.along(query_weight)
+    gate = lax.optimization_barrier
+
+    relayed = line.n_z == 4
+    if relayed:
+        wq_moved = list(line.near(query_weight))
+    else:
+        wq_moved = [line.shift(query_weight, m) for m in range(1, line.n_z)]
     wq_swapped = line.swap(query_weight)
     wo_keep = lax.dynamic_slice_in_dim(out_weight, x * half_cols, half_cols, 0)
     wo_send = lax.dynamic_slice_in_dim(out_weight, (1 - x) * half_cols, half_cols, 0)
+    live_half = lax.dynamic_slice_in_dim(live_flat, core * (width // 2), width // 2, 1)
+    wo_send, live_half, _ = gate((wo_send, live_half, wq_swapped))
     wo_come = line.swap(wo_send)
-    live_half = lax.dynamic_slice_in_dim(live_flat, core * (width // 2), width // 2, 1)
     live_here = line.swap(live_half)
     image_cols = lax.all_to_all(image_flat, "dp", split_axis=1, concat_axis=0, tiled=True)
-    first = (*wq_moved, wq_swapped, wo_come, live_here, image_cols)
-
-    wo_pair = after(jnp.concatenate([wo_keep, wo_come], axis=1), *first)
-    wo_moved = line.along(wo_pair)
-    wq_gated = lax.optimization_barrier((*wq_moved, *first))[: len(wq_moved)]
-    wq_relayed = line.relay(wq_gated)
-    wq_others = line.swap_moved(wq_gated)
-    live_there = tensor_swap(after(live_here, *first), 1)
-
-    image_cols = after(image_cols, *first)
+    quarter_rows = rows // 4
+    live_part = lax.dynamic_slice_in_dim(
+        live_flat, (tensor_at % 4) * quarter_rows, quarter_rows, 0
+    ).reshape(quarter_rows, n_dp, own_width)
+    live_mine = lax.all_to_all(live_part, "dp", split_axis=1, concat_axis=0)
+    live_mine = live_mine.reshape(n_dp, quarter_rows, own_width)
+    wo_pair = jnp.concatenate([wo_keep, wo_come], axis=1)
+    wo_pair, live_here, live_mine, image_cols, wq_swapped, *wq_moved = gate(
+        (wo_pair, live_here, live_mine, image_cols, wq_swapped, *wq_moved)
+    )
+
+    if relayed:
+        wq_moved.append(line.move(wq_moved[1], [(1, 0), (2, 3)]))
+        planes = [(0, 1, 2), None, (1, 2, 3), (0, 3)]
+    else:
+        planes = [None] * len(wq_moved)
+    wo_far = [line.shift(wo_pair, m) for m in range(2, line.n_z - 1)]
+    wq_others = [line.swap(block, at) for block, at in zip(wq_moved[:2], planes)]
+    live_y = tensor_swap(live_mine, 2)
     part_kv = jnp.concatenate(
         [matmul(image_cols, key_weight), matmul(image_cols, value_weight)], axis=1
     )
     part_kv = part_kv.reshape(n_dp, image_rows, 2 * local_cols)
     kv_own = jnp.sum(lax.all_to_all(part_kv, "dp", split_axis=0, concat_axis=0), axis=0)
-    second = (*wo_moved, *wq_relayed, *wq_others, live_there, kv_own)
+    live_pair = jnp.stack([live_mine, live_y])
+    n_moved, n_far = len(wq_moved), len(wo_far)
+    second = gate((wo_pair, kv_own, live_here, live_pair, *wq_others, *wq_moved, *wo_far))
+    wo_pair, kv_own, live_here, live_pair, *second = second
+    wq_others, second = second[:2], second[2:]
+    wq_moved, wo_far = second[:n_moved], second[n_moved:]
 
     def everywhere(values):
         copies = jnp.broadcast_to(values[None], (n_dp, *values.shape))
         return lax.all_to_all(copies, "dp", split_axis=0, concat_axis=0)
 
-    gated = lax.optimization_barrier((*wo_moved, *wq_relayed, kv_own, *second))
-    wo_gated, wq_last = gated[: len(wo_moved)], gated[len(wo_moved) :][: len(wq_relayed)]
-    kv_gated = gated[len(wo_moved) + len(wq_relayed)]
-    wo_relayed = line.relay(wo_gated)
-    wq_last_other = line.swap_relayed(wq_last)
-    kv_all = everywhere(kv_gated.astype(BF16)).reshape(images, 2 * local_cols)
-    quarter_rows = rows // 4
-    live_part = lax.dynamic_slice_in_dim(
-        live_flat, (tensor_at % 4) * quarter_rows, quarter_rows, 0
-    )
-    live_part = after(live_part.reshape(quarter_rows, n_dp, own_width), *second)
-    live_mine = lax.all_to_all(live_part, "dp", split_axis=1, concat_axis=0)
-    live_mine = live_mine.reshape(n_dp, quarter_rows, own_width)
-    live_y = tensor_swap(live_mine, 2)
-    live_cols = [live_mine, live_y, tensor_swap(live_mine, 1), tensor_swap(live_y, 1)]
-
-    wq_blocks = [query_weight, *wq_gated, *wq_last, wq_swapped, *wq_others, *wq_last_other]
+    wo_next = [line.shift(wo_pair, m) for m in (1, line.n_z - 1)]
+    wq_others += [line.swap(block, at) for block, at in zip(wq_moved[2:], planes[2:])]
+    live_there = tensor_swap(live_here, 1)
+    kv_all = everywhere(kv_own.astype(BF16)).reshape(images, 2 * local_cols)
+    wq_blocks = [query_weight, *wq_moved, wq_swapped, *wq_others]
     queries, attended = call(
-        functools.partial(forward_kernel, line, image_own),
+        functools.partial(forward_kernel, line, relayed, image_own),
         place,
         (text_flat, kv_all, *wq_blocks),
         [shape((rows, local_cols), BF16)] * 2,
         [pltpu.VMEM((rows, local_cols), F32)],
         2 * rows * width * local_cols,
     )
-
+    attended, live_pair, live_there, wo_pair, *wo_rest = gate(
+        (attended, live_pair, live_there, wo_pair, *wo_next, *wo_far)
+    )
+
+    att_next = [line.shift(attended, m) for m in (1, line.n_z - 1)]
+    att_swapped = line.swap(attended)
     grad_keep, grad_send = call(
         functools.partial(grad_kernel, line),
         place,
-        (live_flat, live_here, live_there, wo_pair, *wo_gated, *wo_relayed),
+        (live_flat, live_here, live_there, wo_pair, wo_rest[0], *wo_rest[2:], wo_rest[1]),
         [shape((rows, half_cols), BF16)] * 2,
         [pltpu.VMEM((rows, half_cols), F32)] * 2,
         2 * rows * width * local_cols,
     )
     grad_come = line.swap(grad_send)
-
-    att_moved = line.along(attended)
-    att_swapped = line.swap(attended)
-
+    live_core = tensor_swap(live_pair, 1)
     query_grad, kv_part = call(
         functools.partial(backward_kernel, image_own),
         place,
@@ -319,30 +322,34 @@
         (),
         10 * images * rows * local_cols,
     )
-
-    att_ready = lax.optimization_barrier((*att_moved, att_swapped, query_grad))
-    att_moved, att_swapped = att_ready[: len(att_moved)], att_ready[len(att_moved)]
-    att_relayed = line.relay(att_moved)
-    att_others = line.swap_moved(att_moved)
-    att_last = line.swap_relayed(att_relayed)
-
+    chunk = n_dp // n_tensor
     term = call(
-        functools.partial(term_kernel, line),
-        place,
-        (att_ready[-1], *wq_blocks),
-        [shape((n_dp, rows, own_width), BF16)],
+        functools.partial(term_kernel, line, relayed),
+        place,
+        (query_grad, *wq_blocks),
+        [shape((n_tensor, chunk, rows, own_width), BF16)],
         (),
         2 * rows * width * local_cols,
     )
-    term = term.reshape(n_tensor, n_dp // n_tensor, rows, own_width)
-    text_parts = lax.all_to_all(term, "tensor", split_axis=0, concat_axis=0)
-    text_parts = text_parts.reshape(term.shape)
-    text_grad = jnp.sum(text_parts.astype(F32), axis=0).astype(BF16)
-    text_grad = text_grad.transpose(1, 0, 2).reshape(samples, tok_rows, width // n_tensor)
-
     kv_part = kv_part.reshape(n_dp, image_rows, 2 * local_cols)
+    kv_part, term, attended, live_core, att_swapped, *att_next = gate(
+        (kv_part, term, attended, live_core, att_swapped, *att_next)
+    )
+
+    text_parts = [term[0]]
+    for k in range(n_tensor - 1, 1, -1):
+        text_parts.append(tensor_swap(term[k], k))
+    att_far = [line.shift(attended, m) for m in range(2, line.n_z - 1)]
+    att_other_next = [line.swap(block) for block in att_next]
     kv_grad = jnp.sum(lax.all_to_all(kv_part, "dp", split_axis=0, concat_axis=0), axis=0)
-    kv_grad_all = everywhere(kv_grad.astype(BF16)).reshape(images, 2 * local_cols)
+    kv_grad, term_core, *third = gate(
+        (kv_grad.astype(BF16), term[1], *att_other_next, *att_far)
+    )
+    att_other_next, att_far = third[:2], third[2:]
+
+    text_parts.append(tensor_swap(term_core, 1))
+    att_other_far = [line.swap(block) for block in att_far]
+    kv_grad_all = everywhere(kv_grad).reshape(images, 2 * local_cols)
     image_term = matmul(kv_grad_all[:, :local_cols], key_weight, BACK)
     image_term = image_term + matmul(kv_grad_all[:, local_cols:], value_weight, BACK)
     image_term = lax.all_to_all(
@@ -356,11 +363,16 @@
     )
     image_grad = jnp.sum(image_parts.astype(F32), axis=0).astype(BF16)
     image_grad = image_grad.reshape(samples, image_own, width // n_tensor)
-
+    text_grad = functools.reduce(jnp.add, [part.astype(F32) for part in text_parts])
+    text_grad = text_grad.astype(BF16).transpose(1, 0, 2)
+    text_grad = text_grad.reshape(samples, tok_rows, width // n_tensor)
+
+    att_blocks = [attended, att_next[0], *att_far, att_next[1]]
+    att_others = [att_swapped, att_other_next[0], *att_other_far, att_other_next[1]]
     weight_grad = call(
         functools.partial(weight_grad_kernel, line),
         place,
-        (*live_cols, attended, *att_moved, *att_relayed, att_swapped, *att_others, *att_last),
+        (live_pair, live_core, *att_blocks, *att_others),
         [shape((local_cols, own_width), BF16)],
         [pltpu.VMEM((local_cols, own_width), F32)],
         2 * n_dp * rows * local_cols * own_width,

time: 427 us -> 362 us (0.85)
  starting transfers between devices: 110 us -> 79.9 us
  blocking collectives: 18.5 us -> 0 us
  waiting for transfers between devices: 226 us -> 214 us
    ppermute x12 -> x10, waiting for transfers between devices: 87.3 us -> 5.89 us  [move(): return lax.ppermute(block, 'dp', pairs)]
    all_to_all x2, waiting for transfers between devices: 6.02 us -> 51.2 us  [everywhere(): return lax.all_to_all(copies, 'dp', split_axis=0, concat_axis=0)]
    all_to_all x1, waiting for transfers between devices: 0.01 us -> 33.3 us  [shards(): lax.all_to_all(part_kv, 'dp', split_axis=0, concat_axis=0)]
    all_to_all x1 -> x0, blocking collectives: 18.5 us -> none  [shards(): lax.all_to_all(part_kv, 'dp', split_axis=0, concat_axis=0)]
    all_to_all x1, waiting for transfers between devices: 54.4 us -> 40.6 us  [shards(): lax.all_to_all(image_flat, 'dp', split_axis=1, concat_axis=0, tiled=True)]
    ppermute x4 -> x6, waiting for transfers between devices: 33.7 us -> 20 us  [tensor_swap(): lax.ppermute(block, 'tensor', [(t, t ^ bit) for t in range(n_tensor)])]
    ppermute x13 -> x12, waiting for transfers between devices: 32.2 us -> 43.1 us  [swap(): return lax.ppermute(block, 'dp', pairs)]
    all_to_all x1, starting transfers between devices: 13.5 us -> 3.97 us  [shards(): lax.all_to_all(image_term.astype(BF16), 'dp', split_axis=0, concat_axis=1...]
  transfers between devices with their start and end apart: 37 -> 36, of which waited for: 12 -> 12; matrix products, arithmetic and copies ran while one was open for 4% -> 7% of each run, Pallas kernels for 7% -> 8%
where the time goes in v4:
time: 362 us; the launch traced here: 359 us
  waiting for transfers between devices  214 us (59%)
  starting transfers between devices  79.9 us (22%)
  Pallas kernels  28.9 us (8%)
  local copies, waits for them, and re-layouts  21.1 us (6%)
  other arithmetic  9.97 us (3%)
  matrix products  4.72 us (1%)
    all_to_all x2, waiting for transfers between devices, everywhere(): return lax.all_to_all(copies, 'dp', split_axis=0, concat_axis=0)  51.2 us
    ppermute x12, waiting for transfers between devices, swap(): return lax.ppermute(block, 'dp', pairs)  43.1 us
    all_to_all x1, waiting for transfers between devices, shards(): lax.all_to_all(image_flat, 'dp', split_axis=1, concat_axis=0, tiled=True)  40.6 us
    all_to_all x1, waiting for transfers between devices, shards(): lax.all_to_all(part_kv, 'dp', split_axis=0, concat_axis=0)  33.3 us
    pallas_call x5, Pallas kernels, call(): pl.pallas_call(kernel, out_shape=outs[0] if single else outs, in_specs=[p...  28.9 us
    ppermute x10, starting transfers between devices, move(): return lax.ppermute(block, 'dp', pairs)  24.4 us
    ppermute x12, starting transfers between devices, swap(): return lax.ppermute(block, 'dp', pairs)  20.5 us
    ppermute x6, waiting for transfers between devices, tensor_swap(): lax.ppermute(block, 'tensor', [(t, t ^ bit) for t in range(n_tensor)])  20 us
  transfers between devices with their start and end apart: 36, of which 12 were waited for; matrix products, arithmetic and copies ran while one was open for 7% of the time, Pallas kernels for 8%

profile of v4, /device:TPU:4, one launch (start us, length us, event | category | flops | bytes accessed | tf_op | source)
XLA Modules:
  0.0 359.3 jit_solution(11726933924364337590)
XLA Ops:
  0.6 3.7 %collective-permute-start.5 = (bf16[512,1024]{1,0:T(8,128)(2,1)}, bf16[512,1024]{1,0:T(8,128)(2,1)S(1)}, u32[]{:S(2)}, u32[]{:S(2)}) collective-permute-start(bf16[512,1024]{1,0:T(8,128)(2,1)} %refs_0_.3), channel_id=1, source_target_pairs={{0,8},{4,12},{8,16},{12,20},{16,24},{20,28},{1,9},{5,13},{9,17},{1... | collective-permute-start | bytes 3145736 | tf_op jit(solution)/shard_map/ppermute | solution.py:35
  4.3 2.6 collective-permute-start.4
  6.9 1.3 collective-permute-start.3
  8.2 1.6 collective-permute-start
  11.3 4.7 %all-to-all-start.1 = ((bf16[8,8,512]{2,0,1:T(8,128)(2,1)}), bf16[8,8,512]{2,0,1:T(8,128)(2,1)S(1)}, u32[]{:S(2)}, u32[]{:S(2)}) async-start(bf16[8,8,512]{2,0,1:T(8,128)(2,1)} %copy.19), calls=%async_computation.1 | async-start | bytes 131072 | tf_op jit(solution)/shard_map/all_to_all | solution.py:252
  16.9 2.2 constant_dynamic-slice_fusion.3
  20.5 12.4 %collective-permute-done.refs_5_ = bf16[512,1024]{1,0:T(8,128)(2,1)S(1)} collective-permute-done((bf16[512,1024]{1,0:T(8,128)(2,1)}, bf16[512,1024]{1,0:T(8,128)(2,1)S(1)}, u32[]{:S(2)}, u32[]{:S(2)}) %collective-permute-start) | collective-permute-done | bytes 1048608 | tf_op jit(solution)/shard_map/ppermute | solution.py:40
  33.9 1.5 collective-permute-start.2
  36.5 40.6 %all-to-all-done.1 = bf16[8,8,512]{2,0,1:T(8,128)(2,1)S(1)} async-done(((bf16[8,8,512]{2,0,1:T(8,128)(2,1)}), bf16[8,8,512]{2,0,1:T(8,128)(2,1)S(1)}, u32[]{:S(2)}, u32[]{:S(2)}) %all-to-all-start.1) | async-done | bytes 65568 | tf_op jit(solution)/shard_map/all_to_all | solution.py:252
  77.2 4.1 %all-to-all-start = ((bf16[1,64,8,512]{3,1,0,2:T(8,128)(2,1)}), bf16[1,64,8,512]{3,1,0,2:T(8,128)(2,1)}, u32[]{:S(2)}, u32[]{:S(2)}) async-start(bf16[1,64,8,512]{3,1,0,2:T(8,128)(2,1)} %copy.18), calls=%async_computation | async-start | bytes 1048576 | tf_op jit(solution)/shard_map/all_to_all | solution.py:257
  81.3 1.9 collective-permute-start.1
  83.2 16.1 %collective-permute-done.1 = bf16[512,512]{1,0:T(8,128)(2,1)S(1)} collective-permute-done((bf16[512,512]{1,0:T(8,128)(2,1)}, bf16[512,512]{1,0:T(8,128)(2,1)S(1)}, u32[]{:S(2)}, u32[]{:S(2)}) %collective-permute-start.1) | collective-permute-done | bytes 524320 | tf_op jit(solution)/shard_map/ppermute | solution.py:40
  99.3 2.2 pad_maximum_fusion.refs_0_
  101.5 1.3 collective-permute-start.9
  103.6 1.5 fusion.10
  105.5 5.0 %collective-permute-start.10 = (bf16[512,1024]{1,0:T(8,128)(2,1)}, bf16[512,1024]{1,0:T(8,128)(2,1)}, u32[]{:S(2)}, u32[]{:S(2)}) collective-permute-start(bf16[512,1024]{1,0:T(8,128)(2,1)} %pad_maximum_fusion.refs_0_), channel_id=1, source_target_pairs={{16,0},{20,4},{24,8},{28,12},{0,16},{4,20},{8,24},{12,28},{17,1},{... | collective-permute-start | bytes 3145736 | tf_op jit(solution)/shard_map/ppermute | solution.py:35
  110.5 3.6 %collective-permute-start.7 = (bf16[512,1024]{1,0:T(8,128)(2,1)}, bf16[512,1024]{1,0:T(8,128)(2,1)}, u32[]{:S(2)}, u32[]{:S(2)}) collective-permute-start(bf16[512,1024]{1,0:T(8,128)(2,1)} %collective-permute-done.3.refs_1_), channel_id=1, source_target_pairs={{0,4},{4,0},{8,12},{12,8},{16,20},{20,16},{1,5},{5,1},{9,13},{13,9... | collective-permute-start | bytes 3145736 | tf_op jit(solution)/shard_map/ppermute | solution.py:40
  115.0 4.3 %all-to-all-start.2 = ((f32[8,8,2048]{2,1,0:T(8,128)}), f32[8,8,2048]{2,1,0:T(8,128)}, u32[]{:S(2)}, u32[]{:S(2)}) async-start(f32[8,8,2048]{2,1,0:T(8,128)} %maximum_bitcast_fusion), calls=%async_computation.2 | async-start | bytes 1048576 | tf_op jit(solution)/shard_map/all_to_all | solution.py:276
  119.8 11.0 %collective-permute-done.6 = bf16[8,64,512]{2,1,0:T(8,128)(2,1)S(1)} collective-permute-done((bf16[8,64,512]{2,1,0:T(8,128)(2,1)}, bf16[8,64,512]{2,1,0:T(8,128)(2,1)S(1)}, u32[]{:S(2)}, u32[]{:S(2)}) %collective-permute-start.6) | collective-permute-done | bytes 524320 | tf_op jit(solution)/shard_map/ppermute | solution.py:229
  130.8 2.1 pad_maximum_fusion.1.refs_0_
  132.9 33.3 %all-to-all-done.2 = f32[8,8,2048]{2,1,0:T(8,128)} async-done(((f32[8,8,2048]{2,1,0:T(8,128)}), f32[8,8,2048]{2,1,0:T(8,128)}, u32[]{:S(2)}, u32[]{:S(2)}) %all-to-all-start.2) | async-done | bytes 524320 | tf_op jit(solution)/shard_map/all_to_all | solution.py:276
  167.3 1.6 collective-permute-start.11
  168.9 3.3 collective-permute-start.12
  172.4 3.8 %collective-permute-start.14 = (bf16[512,1024]{1,0:T(8,128)(2,1)}, bf16[512,1024]{1,0:T(8,128)(2,1)}, u32[]{:S(2)}, u32[]{:S(2)}) collective-permute-start(bf16[512,1024]{1,0:T(8,128)(2,1)} %pad_maximum_fusion.refs_0_), channel_id=1, source_target_pairs={{8,0},{12,4},{16,8},{20,12},{24,16},{28,20},{0,24},{4,28},{9,1},{1... | collective-permute-start | bytes 3145736 | tf_op jit(solution)/shard_map/ppermute | solution.py:35
  176.9 3.4 all-to-all-start.3
  180.4 46.3 %all-to-all-done.3 = bf16[8,8,2048]{2,1,0:T(8,128)(2,1)S(1)} async-done(((bf16[8,8,2048]{2,1,0:T(8,128)(2,1)}), bf16[8,8,2048]{2,1,0:T(8,128)(2,1)S(1)}, u32[]{:S(2)}, u32[]{:S(2)}) %all-to-all-start.3) | async-done | bytes 262176 | tf_op jit(solution)/shard_map/all_to_all | solution.py:286
  226.8 8.2 %shard_map.103 = (bf16[256,1024]{1,0:T(8,128)(2,1)S(1)}, bf16[256,1024]{1,0:T(8,128)(2,1)S(1)}) custom-call(s32[4]{0:T(128)S(1)} %pad_add_fusion.place, bf16[256,4096]{1,0:T(8,128)(2,1)} %bitcast.52, bf16[64,2048]{1,0:T(8,128)(2,1)S(1)} %bitcast.46, bf16[512,1024]{1,0:T(8,128)(2,1)S(1)} %copy-done.1, bf16[512,1024]{1,0:T(8,128)(2,1)} %collective-permute-done.3.refs_1_, ...), custom_call_target="tpu_custom_call" | custom-call | flops 2147483648 | bytes 13893632 | tf_op jit(solution)/shard_map/pallas_call | solution.py:188
  236.0 3.0 collective-permute-start.19
  240.2 5.5 %shard_map.104 = (bf16[256,512]{1,0:T(8,128)(2,1)S(1)}, bf16[256,512]{1,0:T(8,128)(2,1)S(1)}) custom-call(s32[4]{0:T(128)S(1)} %pad_add_fusion.place, bf16[256,4096]{1,0:T(8,128)(2,1)} %bitcast.51, bf16[256,2048]{1,0:T(8,128)(2,1)S(1)} %copy-done.3, bf16[256,2048]{1,0:T(8,128)(2,1)} %collective-permute-done.13.there, ...), custom_call_target="tpu_custom_call" | custom-call | flops 2147483648 | bytes 8912896 | tf_op jit(solution)/shard_map/pallas_call | solution.py:188
  246.6 11.7 %collective-permute-done.16.come = bf16[256,512]{1,0:T(8,128)(2,1)S(1)} collective-permute-done((bf16[256,512]{1,0:T(8,128)(2,1)S(1)}, bf16[256,512]{1,0:T(8,128)(2,1)S(1)}, u32[]{:S(2)}, u32[]{:S(2)}) %collective-permute-start.16) | collective-permute-done | bytes 262176 | tf_op jit(solution)/shard_map/ppermute | solution.py:40
  258.4 1.9 shard_map.105
  261.1 8.3 %shard_map.106 = bf16[4,2,256,512]{3,2,1,0:T(8,128)(2,1)} custom-call(s32[4]{0:T(128)S(1)} %pad_add_fusion.place, bf16[256,1024]{1,0:T(8,128)(2,1)S(1)} %get-tuple-element.80.query_grad, bf16[512,1024]{1,0:T(8,128)(2,1)S(1)} %copy-done.1, bf16[512,1024]{1,0:T(8,128)(2,1)} %collective-permute-done.3.refs_1_, ...), custom_call_target="tpu_custom_call" | custom-call | flops 2147483648 | bytes 13107200 | tf_op jit(solution)/shard_map/pallas_call | solution.py:188
  271.3 3.5 all-to-all-start.4
  274.8 1.9 collective-permute-start.23
  276.9 2.8 collective-permute-start.25
  279.7 2.6 slice_bitcast_fusion.2
  282.3 19.5 %all-to-all-done.4 = f32[8,8,2048]{2,1,0:T(8,128)S(1)} async-done(((f32[8,8,2048]{2,1,0:T(8,128)}), f32[8,8,2048]{2,1,0:T(8,128)S(1)}, u32[]{:S(2)}, u32[]{:S(2)}) %all-to-all-start.4) | async-done | bytes 524320 | tf_op jit(solution)/shard_map/all_to_all | solution.py:344
  301.8 2.8 collective-permute-done.24.refs_9_
  305.4 5.9 %collective-permute-done.25.refs_4_ = bf16[256,1024]{1,0:T(8,128)(2,1)} collective-permute-done((bf16[256,1024]{1,0:T(8,128)(2,1)}, bf16[256,1024]{1,0:T(8,128)(2,1)}, u32[]{:S(2)}, u32[]{:S(2)}) %collective-permute-start.25) | collective-permute-done | bytes 524320 | tf_op jit(solution)/shard_map/ppermute | solution.py:35
  312.0 3.6 %all-to-all-start.5 = ((bf16[8,8,2048]{2,1,0:T(8,128)(2,1)}), bf16[8,8,2048]{2,1,0:T(8,128)(2,1)S(1)}, u32[]{:S(2)}, u32[]{:S(2)}) async-start(bf16[8,8,2048]{2,1,0:T(8,128)(2,1)} %broadcast_in_dim.17), calls=%async_computation.5 | async-start | bytes 524288 | tf_op jit(solution)/shard_map/all_to_all | solution.py:286
  317.5 2.0 collective-permute-start.27
  319.5 4.8 %all-to-all-done.5 = bf16[8,8,2048]{2,1,0:T(8,128)(2,1)S(1)} async-done(((bf16[8,8,2048]{2,1,0:T(8,128)(2,1)}), bf16[8,8,2048]{2,1,0:T(8,128)(2,1)S(1)}, u32[]{:S(2)}, u32[]{:S(2)}) %all-to-all-start.5) | async-done | bytes 262176 | tf_op jit(solution)/shard_map/all_to_all | solution.py:286
  324.9 2.5 fusion.1
  327.3 4.0 %all-to-all-start.6 = ((bf16[8,8,512]{2,1,0:T(8,128)(2,1)}), bf16[8,8,512]{2,1,0:T(8,128)(2,1)}, u32[]{:S(2)}, u32[]{:S(2)}) async-start(bf16[8,8,512]{2,1,0:T(8,128)(2,1)} %fusion.1), calls=%async_computation.6 | async-start | bytes 131072 | tf_op jit(solution)/shard_map/all_to_all | solution.py:355
  331.3 9.1 %collective-permute-done.22 = bf16[2,256,512]{2,1,0:T(8,128)(2,1)} collective-permute-done((bf16[2,256,512]{2,1,0:T(8,128)(2,1)}, bf16[2,256,512]{2,1,0:T(8,128)(2,1)}, u32[]{:S(2)}, u32[]{:S(2)}) %collective-permute-start.22) | collective-permute-done | bytes 524320 | tf_op jit(solution)/shard_map/ppermute | solution.py:229
  340.4 2.6 fusion.5
  342.9 4.8 %all-to-all-start.7 = ((bf16[1,8,4,1024]{3,1,0,2:T(8,128)(2,1)}), bf16[1,8,4,1024]{3,1,0,2:T(8,128)(2,1)S(1)}, u32[]{:S(2)}, u32[]{:S(2)}) async-start(bf16[1,8,4,1024]{3,1,0,2:T(8,128)(2,1)} %bitcast.24), calls=%async_computation.7 | async-start | bytes 131072 | tf_op jit(solution)/shard_map/all_to_all | solution.py:358
  352.0 5.0 %shard_map.107 = bf16[1024,512]{1,0:T(8,128)(2,1)} custom-call(s32[4]{0:T(128)S(1)} %pad_add_fusion.place, bf16[2,8,64,512]{3,2,1,0:T(8,128)(2,1)S(1)} %copy-done.5, bf16[2,8,64,512]{3,2,1,0:T(8,128)(2,1)} %copy-done.23, bf16[256,1024]{1,0:T(8,128)(2,1)S(1)} %copy-done.8, bf16[256,1024]{1,0:T(8,128)(2,1)S(1)} %copy-done.12, ...), custom_call_target="tpu_custom_call" | custom-call | flops 2147483648 | bytes 7340032 | tf_op jit(solution)/shard_map/pallas_call | solution.py:188
  (105 shorter events, 26.8 us)
Async XLA Ops:
  0.6 104.5 %copy-start = (bf16[512,1024]{1,0:T(8,128)(2,1)S(1)}, bf16[512,1024]{1,0:T(8,128)(2,1)}, u32[]{:S(2)}) copy-start(bf16[512,1024]{1,0:T(8,128)(2,1)} %param.13) | copy-start | bytes 3145732
  0.6 100.8 %collective-permute-start.5 = (bf16[512,1024]{1,0:T(8,128)(2,1)}, bf16[512,1024]{1,0:T(8,128)(2,1)S(1)}, u32[]{:S(2)}, u32[]{:S(2)}) collective-permute-start(bf16[512,1024]{1,0:T(8,128)(2,1)} %refs_0_.3), channel_id=1, source_target_pairs={{0,8},{4,12},{8,16},{12,20},{16,24},{20,28},{1,9},{5,13},{9,17},{1... | collective-permute-start | bytes 3145736 | tf_op jit(solution)/shard_map/ppermute | solution.py:35
  4.3 97.1 %collective-permute-start.4 = (bf16[512,1024]{1,0:T(8,128)(2,1)}, bf16[512,1024]{1,0:T(8,128)(2,1)}, u32[]{:S(2)}, u32[]{:S(2)}) collective-permute-start(bf16[512,1024]{1,0:T(8,128)(2,1)} %refs_0_.3), channel_id=1, source_target_pairs={{16,0},{20,4},{24,8},{28,12},{0,16},{4,20},{8,24},{12,28},{17,1},{... | collective-permute-start | bytes 3145736 | tf_op jit(solution)/shard_map/ppermute | solution.py:35
  6.9 94.6 %collective-permute-start.3 = (bf16[512,1024]{1,0:T(8,128)(2,1)}, bf16[512,1024]{1,0:T(8,128)(2,1)}, u32[]{:S(2)}, u32[]{:S(2)}) collective-permute-start(bf16[512,1024]{1,0:T(8,128)(2,1)} %refs_0_.3), channel_id=1, source_target_pairs={{8,0},{12,4},{16,8},{20,12},{24,16},{28,20},{9,1},{13,5},{17,9},{2... | collective-permute-start | bytes 3145736 | tf_op jit(solution)/shard_map/ppermute | solution.py:35
  8.2 24.7 %collective-permute-start = (bf16[512,1024]{1,0:T(8,128)(2,1)}, bf16[512,1024]{1,0:T(8,128)(2,1)S(1)}, u32[]{:S(2)}, u32[]{:S(2)}) collective-permute-start(bf16[512,1024]{1,0:T(8,128)(2,1)} %refs_0_.3), channel_id=1, source_target_pairs={{0,4},{4,0},{8,12},{12,8},{16,20},{20,16},{24,28},{28,24},{1,5},{5... | collective-permute-start | bytes 3145736 | tf_op jit(solution)/shard_map/ppermute | solution.py:40
  11.3 65.9 %all-to-all-start.1 = ((bf16[8,8,512]{2,0,1:T(8,128)(2,1)}), bf16[8,8,512]{2,0,1:T(8,128)(2,1)S(1)}, u32[]{:S(2)}, u32[]{:S(2)}) async-start(bf16[8,8,512]{2,0,1:T(8,128)(2,1)} %copy.19), calls=%async_computation.1 | async-start | bytes 131072 | tf_op jit(solution)/shard_map/all_to_all | solution.py:252
  19.3 16.3 %copy-start.19 = (bf16[2,128,4096]{2,1,0:T(8,128)(2,1)}, bf16[2,128,4096]{2,1,0:T(8,128)(2,1)S(1)}, u32[]{:S(2)}) copy-start(bf16[2,128,4096]{2,1,0:T(8,128)(2,1)S(1)} %broadcast_select_fusion) | copy-start | bytes 6291460
  33.9 67.6 %collective-permute-start.2 = (bf16[256,2048]{1,0:T(8,128)(2,1)}, bf16[256,2048]{1,0:T(8,128)(2,1)S(1)}, u32[]{:S(2)}, u32[]{:S(2)}) collective-permute-start(bf16[256,2048]{1,0:T(8,128)(2,1)} %constant_dynamic-slice_fusion.1), channel_id=1, source_target_pairs={{0,4},{4,0},{8,12},{12,8},{16,20},{20,16},{24,28},{28,24},{1,5},{5... | collective-permute-start | bytes 3145736 | tf_op jit(solution)/shard_map/ppermute | solution.py:40
  77.2 24.3 %all-to-all-start = ((bf16[1,64,8,512]{3,1,0,2:T(8,128)(2,1)}), bf16[1,64,8,512]{3,1,0,2:T(8,128)(2,1)}, u32[]{:S(2)}, u32[]{:S(2)}) async-start(bf16[1,64,8,512]{3,1,0,2:T(8,128)(2,1)} %copy.18), calls=%async_computation | async-start | bytes 1048576 | tf_op jit(solution)/shard_map/all_to_all | solution.py:257
  81.3 18.0 %collective-permute-start.1 = (bf16[512,512]{1,0:T(8,128)(2,1)}, bf16[512,512]{1,0:T(8,128)(2,1)S(1)}, u32[]{:S(2)}, u32[]{:S(2)}) collective-permute-start(bf16[512,512]{1,0:T(8,128)(2,1)} %get-tuple-element.49), channel_id=1, source_target_pairs={{0,4},{4,0},{8,12},{12,8},{16,20},{20,16},{24,28},{28,24},{1,5},{5... | collective-permute-start | bytes 1572872 | tf_op jit(solution)/shard_map/ppermute | solution.py:40
  101.5 12.6 %copy-start.2 = (bf16[256,2048]{1,0:T(8,128)(2,1)}, bf16[256,2048]{1,0:T(8,128)(2,1)S(1)}, u32[]{:S(2)}) copy-start(bf16[256,2048]{1,0:T(8,128)(2,1)S(1)} %collective-permute-done.2.here) | copy-start | bytes 3145732
  101.5 65.8 %collective-permute-start.9 = (bf16[512,1024]{1,0:T(8,128)(2,1)}, bf16[512,1024]{1,0:T(8,128)(2,1)}, u32[]{:S(2)}, u32[]{:S(2)}) collective-permute-start(bf16[512,1024]{1,0:T(8,128)(2,1)} %collective-permute-done.4.refs_2_), channel_id=1, source_target_pairs={{8,0},{12,4},{16,24},{20,28},{9,1},{13,5},{17,25},{21,29},{10,2},{... | collective-permute-start | bytes 3145736 | tf_op jit(solution)/shard_map/ppermute | solution.py:35
  102.8 64.5 %collective-permute-start.8 = (bf16[512,1024]{1,0:T(8,128)(2,1)}, bf16[512,1024]{1,0:T(8,128)(2,1)}, u32[]{:S(2)}, u32[]{:S(2)}) collective-permute-start(bf16[512,1024]{1,0:T(8,128)(2,1)} %collective-permute-done.4.refs_2_), channel_id=1, source_target_pairs={{0,4},{4,0},{8,12},{12,8},{16,20},{20,16},{24,28},{28,24},{1,5},{5... | collective-permute-start | bytes 3145736 | tf_op jit(solution)/shard_map/ppermute | solution.py:40
  105.5 61.8 %collective-permute-start.10 = (bf16[512,1024]{1,0:T(8,128)(2,1)}, bf16[512,1024]{1,0:T(8,128)(2,1)}, u32[]{:S(2)}, u32[]{:S(2)}) collective-permute-start(bf16[512,1024]{1,0:T(8,128)(2,1)} %pad_maximum_fusion.refs_0_), channel_id=1, source_target_pairs={{16,0},{20,4},{24,8},{28,12},{0,16},{4,20},{8,24},{12,28},{17,1},{... | collective-permute-start | bytes 3145736 | tf_op jit(solution)/shard_map/ppermute | solution.py:35
  110.5 56.8 %collective-permute-start.7 = (bf16[512,1024]{1,0:T(8,128)(2,1)}, bf16[512,1024]{1,0:T(8,128)(2,1)}, u32[]{:S(2)}, u32[]{:S(2)}) collective-permute-start(bf16[512,1024]{1,0:T(8,128)(2,1)} %collective-permute-done.3.refs_1_), channel_id=1, source_target_pairs={{0,4},{4,0},{8,12},{12,8},{16,20},{20,16},{1,5},{5,1},{9,13},{13,9... | collective-permute-start | bytes 3145736 | tf_op jit(solution)/shard_map/ppermute | solution.py:40
  115.0 111.8 %copy-start.1 = (bf16[512,1024]{1,0:T(8,128)(2,1)S(1)}, bf16[512,1024]{1,0:T(8,128)(2,1)}, u32[]{:S(2)}) copy-start(bf16[512,1024]{1,0:T(8,128)(2,1)} %refs_0_.3) | copy-start | bytes 3145732
  115.0 51.2 %all-to-all-start.2 = ((f32[8,8,2048]{2,1,0:T(8,128)}), f32[8,8,2048]{2,1,0:T(8,128)}, u32[]{:S(2)}, u32[]{:S(2)}) async-start(f32[8,8,2048]{2,1,0:T(8,128)} %maximum_bitcast_fusion), calls=%async_computation.2 | async-start | bytes 1048576 | tf_op jit(solution)/shard_map/all_to_all | solution.py:276
  119.2 11.5 %collective-permute-start.6 = (bf16[8,64,512]{2,1,0:T(8,128)(2,1)}, bf16[8,64,512]{2,1,0:T(8,128)(2,1)S(1)}, u32[]{:S(2)}, u32[]{:S(2)}) collective-permute-start(bf16[8,64,512]{2,1,0:T(8,128)(2,1)} %bitcast.8), channel_id=1, source_target_pairs={{0,2},{1,3},{2,0},{3,1},{4,6},{5,7},{6,4},{7,5},{8,10},{9,11},{10,... | collective-permute-start | bytes 1572872 | tf_op jit(solution)/shard_map/ppermute | solution.py:229
  167.3 59.5 %collective-permute-start.11 = (bf16[512,1024]{1,0:T(8,128)(2,1)S(1)}, bf16[512,1024]{1,0:T(8,128)(2,1)}, u32[]{:S(2)}, u32[]{:S(2)}) collective-permute-start(bf16[512,1024]{1,0:T(8,128)(2,1)S(1)} %collective-permute-done.5.refs_3_), channel_id=1, source_target_pairs={{8,12},{12,8},{16,20},{20,16},{24,28},{28,24},{9,13},{13,9},{17,21... | collective-permute-start | bytes 3145736 | tf_op jit(solution)/shard_map/ppermute | solution.py:40
  168.9 57.8 %collective-permute-start.12 = (bf16[512,1024]{1,0:T(8,128)(2,1)}, bf16[512,1024]{1,0:T(8,128)(2,1)}, u32[]{:S(2)}, u32[]{:S(2)}) collective-permute-start(bf16[512,1024]{1,0:T(8,128)(2,1)} %collective-permute-done.9.refs_4_), channel_id=1, source_target_pairs={{0,4},{4,0},{24,28},{28,24},{1,5},{5,1},{25,29},{29,25},{2,6},{6,2... | collective-permute-start | bytes 3145736 | tf_op jit(solution)/shard_map/ppermute | solution.py:40
  172.2 62.8 %collective-permute-start.13 = (bf16[256,2048]{1,0:T(8,128)(2,1)}, bf16[256,2048]{1,0:T(8,128)(2,1)}, u32[]{:S(2)}, u32[]{:S(2)}) collective-permute-start(bf16[256,2048]{1,0:T(8,128)(2,1)} %copy-done.2), channel_id=1, source_target_pairs={{0,1},{1,0},{2,3},{3,2},{4,5},{5,4},{6,7},{7,6},{8,9},{9,8},{10,11... | collective-permute-start | bytes 3145736 | tf_op jit(solution)/shard_map/ppermute | solution.py:229
  172.3 62.8 %collective-permute-start.15 = (bf16[512,1024]{1,0:T(8,128)(2,1)}, bf16[512,1024]{1,0:T(8,128)(2,1)}, u32[]{:S(2)}, u32[]{:S(2)}) collective-permute-start(bf16[512,1024]{1,0:T(8,128)(2,1)} %pad_maximum_fusion.refs_0_), channel_id=1, source_target_pairs={{24,0},{28,4},{0,8},{4,12},{8,16},{12,20},{16,24},{20,28},{25,1},{... | collective-permute-start | bytes 3145736 | tf_op jit(solution)/shard_map/ppermute | solution.py:35
  172.4 62.7 %collective-permute-start.14 = (bf16[512,1024]{1,0:T(8,128)(2,1)}, bf16[512,1024]{1,0:T(8,128)(2,1)}, u32[]{:S(2)}, u32[]{:S(2)}) collective-permute-start(bf16[512,1024]{1,0:T(8,128)(2,1)} %pad_maximum_fusion.refs_0_), channel_id=1, source_target_pairs={{8,0},{12,4},{16,8},{20,12},{24,16},{28,20},{0,24},{4,28},{9,1},{1... | collective-permute-start | bytes 3145736 | tf_op jit(solution)/shard_map/ppermute | solution.py:35
  176.9 49.9 %all-to-all-start.3 = ((bf16[8,8,2048]{2,1,0:T(8,128)(2,1)}), bf16[8,8,2048]{2,1,0:T(8,128)(2,1)S(1)}, u32[]{:S(2)}, u32[]{:S(2)}) async-start(bf16[8,8,2048]{2,1,0:T(8,128)(2,1)} %broadcast_in_dim.16), calls=%async_computation.3 | async-start | bytes 524288 | tf_op jit(solution)/shard_map/all_to_all | solution.py:286
  226.8 8.3 %copy-start.4 = (bf16[2,8,64,512]{3,2,1,0:T(8,128)(2,1)S(1)}, bf16[2,8,64,512]{3,2,1,0:T(8,128)(2,1)}, u32[]{:S(2)}) copy-start(bf16[2,8,64,512]{3,2,1,0:T(8,128)(2,1)} %pad_maximum_fusion.1.refs_0_) | copy-start | bytes 3145732
  226.8 13.4 %copy-start.3 = (bf16[256,2048]{1,0:T(8,128)(2,1)S(1)}, bf16[256,2048]{1,0:T(8,128)(2,1)}, u32[]{:S(2)}) copy-start(bf16[256,2048]{1,0:T(8,128)(2,1)} %copy-done.2) | copy-start | bytes 3145732
  235.0 10.6 %copy-start.7 = (bf16[256,1024]{1,0:T(8,128)(2,1)}, bf16[256,1024]{1,0:T(8,128)(2,1)S(1)}, u32[]{:S(2)}) copy-start(bf16[256,1024]{1,0:T(8,128)(2,1)S(1)} %get-tuple-element.87.refs_2_) | copy-start | bytes 1572868
  235.1 35.2 %collective-permute-start.17 = (bf16[2,8,64,512]{3,2,1,0:T(8,128)(2,1)S(1)}, bf16[2,8,64,512]{3,2,1,0:T(8,128)(2,1)S(1)}, u32[]{:S(2)}, u32[]{:S(2)}) collective-permute-start(bf16[2,8,64,512]{3,2,1,0:T(8,128)(2,1)S(1)} %copy-done.4), channel_id=1, source_target_pairs={{0,1},{1,0},{2,3},{3,2},{4,5},{5,4},{6,7},{7,6},{8,9},{9,8},{10,11... | collective-permute-start | bytes 3145736 | tf_op jit(solution)/shard_map/ppermute | solution.py:229
  235.2 34.2 %collective-permute-start.20 = (bf16[256,1024]{1,0:T(8,128)(2,1)S(1)}, bf16[256,1024]{1,0:T(8,128)(2,1)S(1)}, u32[]{:S(2)}, u32[]{:S(2)}) collective-permute-start(bf16[256,1024]{1,0:T(8,128)(2,1)S(1)} %get-tuple-element.87.refs_2_), channel_id=1, source_target_pairs={{24,0},{28,4},{0,8},{4,12},{8,16},{12,20},{16,24},{20,28},{25,1},{... | collective-permute-start | bytes 1572872 | tf_op jit(solution)/shard_map/ppermute | solution.py:35
  236.0 33.3 %collective-permute-start.19 = (bf16[256,1024]{1,0:T(8,128)(2,1)S(1)}, bf16[256,1024]{1,0:T(8,128)(2,1)S(1)}, u32[]{:S(2)}, u32[]{:S(2)}) collective-permute-start(bf16[256,1024]{1,0:T(8,128)(2,1)S(1)} %get-tuple-element.87.refs_2_), channel_id=1, source_target_pairs={{8,0},{12,4},{16,8},{20,12},{24,16},{28,20},{0,24},{4,28},{9,1},{1... | collective-permute-start | bytes 1572872 | tf_op jit(solution)/shard_map/ppermute | solution.py:35
  239.1 30.3 %collective-permute-start.18 = (bf16[256,1024]{1,0:T(8,128)(2,1)S(1)}, bf16[256,1024]{1,0:T(8,128)(2,1)S(1)}, u32[]{:S(2)}, u32[]{:S(2)}) collective-permute-start(bf16[256,1024]{1,0:T(8,128)(2,1)S(1)} %get-tuple-element.87.refs_2_), channel_id=1, source_target_pairs={{0,4},{4,0},{8,12},{12,8},{16,20},{20,16},{24,28},{28,24},{1,5},{5... | collective-permute-start | bytes 1572872 | tf_op jit(solution)/shard_map/ppermute | solution.py:40
  245.7 12.7 %collective-permute-start.16 = (bf16[256,512]{1,0:T(8,128)(2,1)S(1)}, bf16[256,512]{1,0:T(8,128)(2,1)S(1)}, u32[]{:S(2)}, u32[]{:S(2)}) collective-permute-start(bf16[256,512]{1,0:T(8,128)(2,1)S(1)} %get-tuple-element.78), channel_id=1, source_target_pairs={{0,4},{4,0},{8,12},{12,8},{16,20},{20,16},{24,28},{28,24},{1,5},{5... | collective-permute-start | bytes 786440 | tf_op jit(solution)/shard_map/ppermute | solution.py:40
  271.3 30.4 %all-to-all-start.4 = ((f32[8,8,2048]{2,1,0:T(8,128)}), f32[8,8,2048]{2,1,0:T(8,128)S(1)}, u32[]{:S(2)}, u32[]{:S(2)}) async-start(f32[8,8,2048]{2,1,0:T(8,128)} %bitcast.48), calls=%async_computation.4 | async-start | bytes 1048576 | tf_op jit(solution)/shard_map/all_to_all | solution.py:344
  274.8 27.0 %collective-permute-start.23 = (bf16[256,1024]{1,0:T(8,128)(2,1)}, bf16[256,1024]{1,0:T(8,128)(2,1)S(1)}, u32[]{:S(2)}, u32[]{:S(2)}) collective-permute-start(bf16[256,1024]{1,0:T(8,128)(2,1)} %copy-done.11), channel_id=1, source_target_pairs={{0,4},{4,0},{8,12},{12,8},{16,20},{20,16},{24,28},{28,24},{1,5},{5... | collective-permute-start | bytes 1572872 | tf_op jit(solution)/shard_map/ppermute | solution.py:40
  276.7 27.9 %collective-permute-start.24 = (bf16[256,1024]{1,0:T(8,128)(2,1)}, bf16[256,1024]{1,0:T(8,128)(2,1)S(1)}, u32[]{:S(2)}, u32[]{:S(2)}) collective-permute-start(bf16[256,1024]{1,0:T(8,128)(2,1)} %copy-done.9), channel_id=1, source_target_pairs={{0,4},{4,0},{8,12},{12,8},{16,20},{20,16},{24,28},{28,24},{1,5},{5... | collective-permute-start | bytes 1572872 | tf_op jit(solution)/shard_map/ppermute | solution.py:40
  276.9 34.4 %collective-permute-start.25 = (bf16[256,1024]{1,0:T(8,128)(2,1)}, bf16[256,1024]{1,0:T(8,128)(2,1)}, u32[]{:S(2)}, u32[]{:S(2)}) collective-permute-start(bf16[256,1024]{1,0:T(8,128)(2,1)} %copy-done.7), channel_id=1, source_target_pairs={{16,0},{20,4},{24,8},{28,12},{0,16},{4,20},{8,24},{12,28},{17,1},{... | collective-permute-start | bytes 1572872 | tf_op jit(solution)/shard_map/ppermute | solution.py:35
  301.8 22.6 %copy-start.15 = (bf16[256,1024]{1,0:T(8,128)(2,1)}, bf16[256,1024]{1,0:T(8,128)(2,1)S(1)}, u32[]{:S(2)}) copy-start(bf16[256,1024]{1,0:T(8,128)(2,1)S(1)} %collective-permute-done.23.refs_7_) | copy-start | bytes 1572868
  312.0 12.3 %all-to-all-start.5 = ((bf16[8,8,2048]{2,1,0:T(8,128)(2,1)}), bf16[8,8,2048]{2,1,0:T(8,128)(2,1)S(1)}, u32[]{:S(2)}, u32[]{:S(2)}) async-start(bf16[8,8,2048]{2,1,0:T(8,128)(2,1)} %broadcast_in_dim.17), calls=%async_computation.5 | async-start | bytes 524288 | tf_op jit(solution)/shard_map/all_to_all | solution.py:286
  315.7 15.6 %collective-permute-start.21 = (bf16[2,256,512]{2,1,0:T(8,128)(2,1)}, bf16[2,256,512]{2,1,0:T(8,128)(2,1)}, u32[]{:S(2)}, u32[]{:S(2)}) collective-permute-start(bf16[2,256,512]{2,1,0:T(8,128)(2,1)} %get-tuple-element.95), channel_id=1, source_target_pairs={{0,3},{1,2},{2,1},{3,0},{4,7},{5,6},{6,5},{7,4},{8,11},{9,10},{10,... | collective-permute-start | bytes 1572872 | tf_op jit(solution)/shard_map/ppermute | solution.py:229
  315.7 24.7 %collective-permute-start.22 = (bf16[2,256,512]{2,1,0:T(8,128)(2,1)}, bf16[2,256,512]{2,1,0:T(8,128)(2,1)}, u32[]{:S(2)}, u32[]{:S(2)}) collective-permute-start(bf16[2,256,512]{2,1,0:T(8,128)(2,1)} %get-tuple-element.97), channel_id=1, source_target_pairs={{0,2},{1,3},{2,0},{3,1},{4,6},{5,7},{6,4},{7,5},{8,10},{9,11},{10,... | collective-permute-start | bytes 1572872 | tf_op jit(solution)/shard_map/ppermute | solution.py:229
  316.5 23.8 %collective-permute-start.26 = (bf16[2,256,512]{2,1,0:T(8,128)(2,1)}, bf16[2,256,512]{2,1,0:T(8,128)(2,1)}, u32[]{:S(2)}, u32[]{:S(2)}) collective-permute-start(bf16[2,256,512]{2,1,0:T(8,128)(2,1)} %get-tuple-element.88), channel_id=1, source_target_pairs={{0,1},{1,0},{2,3},{3,2},{4,5},{5,4},{6,7},{7,6},{8,9},{9,8},{10,11... | collective-permute-start | bytes 1572872 | tf_op jit(solution)/shard_map/ppermute | solution.py:229
  317.5 30.3 %collective-permute-start.27 = (bf16[256,1024]{1,0:T(8,128)(2,1)}, bf16[256,1024]{1,0:T(8,128)(2,1)}, u32[]{:S(2)}, u32[]{:S(2)}) collective-permute-start(bf16[256,1024]{1,0:T(8,128)(2,1)} %collective-permute-done.25.refs_4_), channel_id=1, source_target_pairs={{0,4},{4,0},{8,12},{12,8},{16,20},{20,16},{24,28},{28,24},{1,5},{5... | collective-permute-start | bytes 1572872 | tf_op jit(solution)/shard_map/ppermute | solution.py:40
  324.8 23.0 %copy-start.5 = (bf16[2,8,64,512]{3,2,1,0:T(8,128)(2,1)S(1)}, bf16[2,8,64,512]{3,2,1,0:T(8,128)(2,1)}, u32[]{:S(2)}) copy-start(bf16[2,8,64,512]{3,2,1,0:T(8,128)(2,1)} %pad_maximum_fusion.1.refs_0_) | copy-start | bytes 3145732
  324.8 22.9 %copy-start.8 = (bf16[256,1024]{1,0:T(8,128)(2,1)S(1)}, bf16[256,1024]{1,0:T(8,128)(2,1)}, u32[]{:S(2)}) copy-start(bf16[256,1024]{1,0:T(8,128)(2,1)} %copy-done.7) | copy-start | bytes 1572868
  324.8 22.9 %copy-start.10 = (bf16[256,1024]{1,0:T(8,128)(2,1)S(1)}, bf16[256,1024]{1,0:T(8,128)(2,1)}, u32[]{:S(2)}) copy-start(bf16[256,1024]{1,0:T(8,128)(2,1)} %copy-done.9) | copy-start | bytes 1572868
  327.3 15.6 %all-to-all-start.6 = ((bf16[8,8,512]{2,1,0:T(8,128)(2,1)}), bf16[8,8,512]{2,1,0:T(8,128)(2,1)}, u32[]{:S(2)}, u32[]{:S(2)}) async-start(bf16[8,8,512]{2,1,0:T(8,128)(2,1)} %fusion.1), calls=%async_computation.6 | async-start | bytes 131072 | tf_op jit(solution)/shard_map/all_to_all | solution.py:355
  342.9 15.7 %all-to-all-start.7 = ((bf16[1,8,4,1024]{3,1,0,2:T(8,128)(2,1)}), bf16[1,8,4,1024]{3,1,0,2:T(8,128)(2,1)S(1)}, u32[]{:S(2)}, u32[]{:S(2)}) async-start(bf16[1,8,4,1024]{3,1,0,2:T(8,128)(2,1)} %bitcast.24), calls=%async_computation.7 | async-start | bytes 131072 | tf_op jit(solution)/shard_map/all_to_all | solution.py:358
  352.0 5.0 %copy-start.21 = (bf16[256,2,512]{2,0,1:T(8,128)(2,1)S(1)}, bf16[256,2,512]{2,0,1:T(8,128)(2,1)}, u32[]{:S(2)}) copy-start(bf16[256,2,512]{2,0,1:T(8,128)(2,1)} %fusion.5) | copy-start | bytes 1572868
  (12 other events, 13.9 us)

commit v5 on v4

--- a/solution.py
+++ b/solution.py
@@ -43,10 +43,23 @@
         n = self.n_z
         return self.move(block, [((a + distance) % n, a) for a in range(n)])
 
-    def near(self, block):
+    def first(self, block):
+        if self.n_z != 4:
+            return [self.shift(block, m) for m in range(1, self.n_z)]
         above = self.move(block, [(1, 0), (2, 1), (3, 2)])
         below = self.move(block, [(0, 1), (1, 2), (2, 3)])
-        return above, self.shift(block, 2), below
+        return [above, below]
+
+    def second(self, moved):
+        if self.n_z != 4:
+            return []
+        return [self.move(moved[0], [(1, 0), (2, 1)]), self.move(moved[1], [(1, 2), (2, 3)])]
+
+    def third(self, forwarded):
+        if self.n_z != 4:
+            return []
+        across = jnp.where(lax.axis_index("dp") < 4, forwarded[0], forwarded[1])
+        return [across, self.move(across, [(1, 0), (2, 3)])]
 
     def slots(self, z, relayed):
         if not relayed:
@@ -54,8 +67,8 @@
         return [
             (0, None),
             (1, z < 3),
+            (3, z > 0),
             (2, None),
-            (3, z > 0),
             (jnp.where(z == 3, 1, 3), (z == 3) | (z == 0)),
         ]
 
@@ -129,7 +142,7 @@
         other = jnp.where(lax.div(index, half) == core, here[:, inner], there[:, inner])
         send[...] += matmul(other, weight, BACK)
 
-    each_block(line, place, False, add)
+    each_block(line, place, line.n_z == 4, add)
     keep_out[...] = keep[...].astype(BF16)
     send_out[...] = send[...].astype(BF16)
 
@@ -197,6 +210,35 @@
         compiler_params=pltpu.CompilerParams(vmem_limit_bytes=VMEM_LIMIT),
         cost_estimate=pl.CostEstimate(flops=flops, bytes_accessed=moved, transcendentals=0),
     )(place, *operands)
+
+
+def to_owner(line, terms):
+    n_dp, n_tensor = line.n_dp, lax.axis_size("tensor")
+    images, cols = terms.shape
+    if line.n_z != n_tensor:
+        terms = lax.all_to_all(terms, "dp", split_axis=0, concat_axis=1, tiled=True)
+        terms = terms.reshape(images // n_dp, n_tensor, n_dp * cols // n_tensor)
+        parts = lax.all_to_all(terms, "tensor", split_axis=1, concat_axis=0)
+        return jnp.sum(parts.astype(F32), axis=0).astype(BF16)
+    parts = lax.all_to_all(
+        terms.reshape(n_tensor, images // n_tensor, cols), "tensor", split_axis=0, concat_axis=0
+    )
+    total = jnp.sum(parts.astype(F32), axis=0).astype(BF16)
+    total = total.reshape(2, images // n_dp, cols)
+    x = lax.axis_index("dp") % 2
+    come = []
+    for other in range(2):
+        block = jnp.where(x == other, total[0], total[1])
+        pairs = [
+            ((2 * z + e) * n_tensor + t, (2 * t + (e ^ other)) * n_tensor + z)
+            for z in range(line.n_z)
+            for e in range(2)
+            for t in range(n_tensor)
+        ]
+        come.append(lax.ppermute(block, ("dp", "tensor"), pairs))
+    return jnp.where(
+        x == 0, jnp.concatenate(come, axis=1), jnp.concatenate(come[::-1], axis=1)
+    )
 
 
 def shards(
@@ -238,58 +280,71 @@
     gate = lax.optimization_barrier
 
     relayed = line.n_z == 4
-    if relayed:
-        wq_moved = list(line.near(query_weight))
-    else:
-        wq_moved = [line.shift(query_weight, m) for m in range(1, line.n_z)]
-    wq_swapped = line.swap(query_weight)
+    wq_moved = line.first(query_weight)
     wo_keep = lax.dynamic_slice_in_dim(out_weight, x * half_cols, half_cols, 0)
     wo_send = lax.dynamic_slice_in_dim(out_weight, (1 - x) * half_cols, half_cols, 0)
+    wo_come = line.swap(wo_send)
+    wq_swapped = line.swap(query_weight)
     live_half = lax.dynamic_slice_in_dim(live_flat, core * (width // 2), width // 2, 1)
-    wo_send, live_half, _ = gate((wo_send, live_half, wq_swapped))
-    wo_come = line.swap(wo_send)
+    live_half, wo_come = gate((live_half, wo_come))
     live_here = line.swap(live_half)
     image_cols = lax.all_to_all(image_flat, "dp", split_axis=1, concat_axis=0, tiled=True)
+    wo_pair = jnp.concatenate([wo_keep, wo_come], axis=1)
+    wo_pair, image_cols, *wq_moved = gate((wo_pair, image_cols, *wq_moved))
+
+    planes = [(0, 1, 2), (1, 2, 3)] if relayed else [None] * len(wq_moved)
+    wq_two = line.second(wq_moved)
+    wo_moved = line.first(wo_pair)
+    above, live_here = gate((wq_moved[0], live_here))
+    wq_others = [line.swap(above, planes[0])]
+    part_kv = jnp.concatenate(
+        [matmul(image_cols, key_weight), matmul(image_cols, value_weight)], axis=1
+    )
+    part_kv = part_kv.reshape(n_dp, image_rows, 2 * local_cols)
+    kv_own = jnp.sum(lax.all_to_all(part_kv, "dp", split_axis=0, concat_axis=0), axis=0)
+    kv_own, live_here, wq_swapped, wq_others[0], *moved = gate(
+        (kv_own, live_here, wq_swapped, wq_others[0], *wq_moved, *wq_two, *wo_moved)
+    )
+    n_moved = len(wq_moved)
+    wq_moved, wq_two, wo_moved = moved[:n_moved], moved[n_moved:-n_moved], moved[-n_moved:]
+
+    def everywhere(values):
+        copies = jnp.broadcast_to(values[None], (n_dp, *values.shape))
+        return lax.all_to_all(copies, "dp", split_axis=0, concat_axis=0)
+
+    wq_last = line.third(wq_two)
+    wo_two = line.second(wo_moved)
+    wq_others += [line.swap(block, at) for block, at in zip(wq_moved[1:], planes[1:])]
+    wq_others += [line.swap(block) for block in wq_last[:1]]
+    kv_all = everywhere(kv_own.astype(BF16)).reshape(images, 2 * local_cols)
+    kv_all, live_here, wo_pair, live_flat, *moved = gate(
+        (kv_all, live_here, wo_pair, live_flat, *wo_moved, *wo_two, *wq_others, *wq_last)
+    )
+    wo_moved, moved = moved[:n_moved], moved[n_moved:]
+    wo_two, moved = moved[: len(wo_two)], moved[len(wo_two) :]
+    wq_others, wq_last = moved[: len(wq_others)], moved[len(wq_others) :]
+
+    wo_last = line.third(wo_two)
+    wq_others += [line.swap(block, (0, 3)) for block in wq_last[1:]]
+    live_there = tensor_swap(live_here, 1)
     quarter_rows = rows // 4
     live_part = lax.dynamic_slice_in_dim(
         live_flat, (tensor_at % 4) * quarter_rows, quarter_rows, 0
     ).reshape(quarter_rows, n_dp, own_width)
     live_mine = lax.all_to_all(live_part, "dp", split_axis=1, concat_axis=0)
     live_mine = live_mine.reshape(n_dp, quarter_rows, own_width)
-    wo_pair = jnp.concatenate([wo_keep, wo_come], axis=1)
-    wo_pair, live_here, live_mine, image_cols, wq_swapped, *wq_moved = gate(
-        (wo_pair, live_here, live_mine, image_cols, wq_swapped, *wq_moved)
-    )
-
-    if relayed:
-        wq_moved.append(line.move(wq_moved[1], [(1, 0), (2, 3)]))
-        planes = [(0, 1, 2), None, (1, 2, 3), (0, 3)]
-    else:
-        planes = [None] * len(wq_moved)
-    wo_far = [line.shift(wo_pair, m) for m in range(2, line.n_z - 1)]
-    wq_others = [line.swap(block, at) for block, at in zip(wq_moved[:2], planes)]
-    live_y = tensor_swap(live_mine, 2)
-    part_kv = jnp.concatenate(
-        [matmul(image_cols, key_weight), matmul(image_cols, value_weight)], axis=1
-    )
-    part_kv = part_kv.reshape(n_dp, image_rows, 2 * local_cols)
-    kv_own = jnp.sum(lax.all_to_all(part_kv, "dp", split_axis=0, concat_axis=0), axis=0)
-    live_pair = jnp.stack([live_mine, live_y])
-    n_moved, n_far = len(wq_moved), len(wo_far)
-    second = gate((wo_pair, kv_own, live_here, live_pair, *wq_others, *wq_moved, *wo_far))
-    wo_pair, kv_own, live_here, live_pair, *second = second
-    wq_others, second = second[:2], second[2:]
-    wq_moved, wo_far = second[:n_moved], second[n_moved:]
-
-    def everywhere(values):
-        copies = jnp.broadcast_to(values[None], (n_dp, *values.shape))
-        return lax.all_to_all(copies, "dp", split_axis=0, concat_axis=0)
-
-    wo_next = [line.shift(wo_pair, m) for m in (1, line.n_z - 1)]
-    wq_others += [line.swap(block, at) for block, at in zip(wq_moved[2:], planes[2:])]
-    live_there = tensor_swap(live_here, 1)
-    kv_all = everywhere(kv_own.astype(BF16)).reshape(images, 2 * local_cols)
-    wq_blocks = [query_weight, *wq_moved, wq_swapped, *wq_others]
+    wq_blocks = [query_weight, *wq_moved, *wq_last, wq_swapped, *wq_others]
+
+    grad_keep, grad_send = call(
+        functools.partial(grad_kernel, line),
+        place,
+        (live_flat, live_here, live_there, wo_pair, *wo_moved, *wo_last),
+        [shape((rows, half_cols), BF16)] * 2,
+        [pltpu.VMEM((rows, half_cols), F32)] * 2,
+        2 * rows * width * local_cols,
+    )
+    grad_come = line.swap(grad_send)
+    text_flat, live_mine, _ = gate((text_flat, live_mine, grad_send))
     queries, attended = call(
         functools.partial(forward_kernel, line, relayed, image_own),
         place,
@@ -298,22 +353,10 @@
         [pltpu.VMEM((rows, local_cols), F32)],
         2 * rows * width * local_cols,
     )
-    attended, live_pair, live_there, wo_pair, *wo_rest = gate(
-        (attended, live_pair, live_there, wo_pair, *wo_next, *wo_far)
-    )
 
     att_next = [line.shift(attended, m) for m in (1, line.n_z - 1)]
     att_swapped = line.swap(attended)
-    grad_keep, grad_send = call(
-        functools.partial(grad_kernel, line),
-        place,
-        (live_flat, live_here, live_there, wo_pair, wo_rest[0], *wo_rest[2:], wo_rest[1]),
-        [shape((rows, half_cols), BF16)] * 2,
-        [pltpu.VMEM((rows, half_cols), F32)] * 2,
-        2 * rows * width * local_cols,
-    )
-    grad_come = line.swap(grad_send)
-    live_core = tensor_swap(live_pair, 1)
+    live_pair = jnp.stack([live_mine, tensor_swap(live_mine, 2)])
     query_grad, kv_part = call(
         functools.partial(backward_kernel, image_own),
         place,
@@ -332,8 +375,9 @@
         2 * rows * width * local_cols,
     )
     kv_part = kv_part.reshape(n_dp, image_rows, 2 * local_cols)
-    kv_part, term, attended, live_core, att_swapped, *att_next = gate(
-        (kv_part, term, attended, live_core, att_swapped, *att_next)
+    kv_grad = jnp.sum(lax.all_to_all(kv_part, "dp", split_axis=0, concat_axis=0), axis=0)
+    kv_grad, term, attended, live_pair, att_swapped, *att_next = gate(
+        (kv_grad.astype(BF16), term, attended, live_pair, att_swapped, *att_next)
     )
 
     text_parts = [term[0]]
@@ -341,27 +385,18 @@
         text_parts.append(tensor_swap(term[k], k))
     att_far = [line.shift(attended, m) for m in range(2, line.n_z - 1)]
     att_other_next = [line.swap(block) for block in att_next]
-    kv_grad = jnp.sum(lax.all_to_all(kv_part, "dp", split_axis=0, concat_axis=0), axis=0)
-    kv_grad, term_core, *third = gate(
-        (kv_grad.astype(BF16), term[1], *att_other_next, *att_far)
+    kv_grad_all = everywhere(kv_grad).reshape(images, 2 * local_cols)
+    kv_grad_all, term_core, live_pair, *third = gate(
+        (kv_grad_all, term[1], live_pair, *att_other_next, *att_far)
     )
     att_other_next, att_far = third[:2], third[2:]
 
     text_parts.append(tensor_swap(term_core, 1))
+    live_core = tensor_swap(live_pair, 1)
     att_other_far = [line.swap(block) for block in att_far]
-    kv_grad_all = everywhere(kv_grad).reshape(images, 2 * local_cols)
     image_term = matmul(kv_grad_all[:, :local_cols], key_weight, BACK)
     image_term = image_term + matmul(kv_grad_all[:, local_cols:], value_weight, BACK)
-    image_term = lax.all_to_all(
-        image_term.astype(BF16), "dp", split_axis=0, concat_axis=1, tiled=True
-    )
-    image_parts = lax.all_to_all(
-        image_term.reshape(image_rows, n_tensor, width // n_tensor),
-        "tensor",
-        split_axis=1,
-        concat_axis=0,
-    )
-    image_grad = jnp.sum(image_parts.astype(F32), axis=0).astype(BF16)
+    image_grad = to_owner(line, image_term.astype(BF16))
     image_grad = image_grad.reshape(samples, image_own, width // n_tensor)
     text_grad = functools.reduce(jnp.add, [part.astype(F32) for part in text_parts])
     text_grad = text_grad.astype(BF16).transpose(1, 0, 2)

time: 362 us -> 350 us (0.967)
  waiting for transfers between devices: 214 us -> 174 us
  starting transfers between devices: 79.9 us -> 98.5 us
  other arithmetic: 9.97 us -> 15.9 us
    ppermute x12, waiting for transfers between devices: 43.1 us -> 13 us  [swap(): return lax.ppermute(block, 'dp', pairs)]
    ppermute x10 -> x13, waiting for transfers between devices: 5.89 us -> 28 us  [move(): return lax.ppermute(block, 'dp', pairs)]
    ppermute x6, waiting for transfers between devices: 20 us -> 0.02 us  [tensor_swap(): lax.ppermute(block, 'tensor', [(t, t ^ bit) for t in range(n_tensor)])]
    all_to_all x1, waiting for transfers between devices: 19.5 us -> 0.01 us  [shards(): lax.all_to_all(kv_part, 'dp', split_axis=0, concat_axis=0)]
    all_to_all x2, starting transfers between devices: 7.03 us -> 17.2 us  [everywhere(): return lax.all_to_all(copies, 'dp', split_axis=0, concat_axis=0)]
    ppermute x0 -> x2, waiting for transfers between devices: none -> 7.56 us  [to_owner(): come.append(lax.ppermute(block, ('dp', 'tensor'), pairs))]
    ppermute x0 -> x2, starting transfers between devices: none -> 6.24 us  [to_owner(): come.append(lax.ppermute(block, ('dp', 'tensor'), pairs))]
    all_to_all x2 -> x1, starting transfers between devices: 8.81 us -> 3.39 us  [to_owner(): lax.all_to_all(terms.reshape(n_tensor, images // n_tensor, cols), 'tensor...]
  transfers between devices with their start and end apart: 36 -> 40, of which waited for: 12 -> 12; matrix products, arithmetic and copies ran while one was open for 7% -> 9% of each run, Pallas kernels for 8% -> 7%
where the time goes in v5:
time: 350 us; the launch traced here: 348 us
  waiting for transfers between devices  174 us (50%)
  starting transfers between devices  98.5 us (28%)
  Pallas kernels  31.4 us (9%)
  local copies, waits for them, and re-layouts  22.1 us (6%)
  other arithmetic  15.9 us (5%)
  matrix products  4.57 us (1%)
    all_to_all x2, waiting for transfers between devices, everywhere(): return lax.all_to_all(copies, 'dp', split_axis=0, concat_axis=0)  49.1 us
    all_to_all x1, waiting for transfers between devices, shards(): lax.all_to_all(image_flat, 'dp', split_axis=1, concat_axis=0, tiled=True)  37.9 us
    all_to_all x1, waiting for transfers between devices, shards(): lax.all_to_all(part_kv, 'dp', split_axis=0, concat_axis=0)  36.9 us
    pallas_call x5, Pallas kernels, call(): pl.pallas_call(kernel, out_shape=outs[0] if single else outs, in_specs=[p...  31.4 us
    ppermute x13, waiting for transfers between devices, move(): return lax.ppermute(block, 'dp', pairs)  28 us
    ppermute x13, starting transfers between devices, move(): return lax.ppermute(block, 'dp', pairs)  27.6 us
    ppermute x12, starting transfers between devices, swap(): return lax.ppermute(block, 'dp', pairs)  19 us
    all_to_all x2, starting transfers between devices, everywhere(): return lax.all_to_all(copies, 'dp', split_axis=0, concat_axis=0)  17.2 us
  transfers between devices with their start and end apart: 40, of which 12 were waited for; matrix products, arithmetic and copies ran while one was open for 9% of the time, Pallas kernels for 7%

profile of v5, /device:TPU:4, one launch (start us, length us, event | category | flops | bytes accessed | tf_op | source)
XLA Modules:
  0.0 347.7 jit_solution(3905078111943888954)
XLA Ops:
  2.1 5.5 %collective-permute-start.2 = (bf16[512,1024]{1,0:T(8,128)(2,1)}, bf16[512,1024]{1,0:T(8,128)(2,1)}, u32[]{:S(2)}, u32[]{:S(2)}) collective-permute-start(bf16[512,1024]{1,0:T(8,128)(2,1)} %refs_0_.3), channel_id=1, source_target_pairs={{0,8},{4,12},{8,16},{12,20},{16,24},{20,28},{1,9},{5,13},{9,17},{1... | collective-permute-start | bytes 3145736 | tf_op jit(solution)/shard_map/ppermute | solution.py:35
  7.6 2.2 constant_dynamic-slice_fusion.3
  11.4 3.2 broadcast_select_fusion
  14.6 2.4 constant_dynamic-slice_fusion.2
  17.0 6.3 %collective-permute-done = bf16[512,512]{1,0:T(8,128)(2,1)} collective-permute-done((bf16[512,512]{1,0:T(8,128)(2,1)}, bf16[512,512]{1,0:T(8,128)(2,1)}, u32[]{:S(2)}, u32[]{:S(2)}) %collective-permute-start) | collective-permute-done | bytes 524320 | tf_op jit(solution)/shard_map/ppermute | solution.py:40
  26.0 3.9 %all-to-all-start = ((bf16[8,8,512]{2,0,1:T(8,128)(2,1)}), bf16[8,8,512]{2,0,1:T(8,128)(2,1)S(1)}, u32[]{:S(2)}, u32[]{:S(2)}) async-start(bf16[8,8,512]{2,0,1:T(8,128)(2,1)} %copy.16), calls=%async_computation | async-start | bytes 131072 | tf_op jit(solution)/shard_map/all_to_all | solution.py:291
  29.9 2.3 pad_maximum_fusion.refs_0_
  32.2 37.9 %all-to-all-done = bf16[8,8,512]{2,0,1:T(8,128)(2,1)S(1)} async-done(((bf16[8,8,512]{2,0,1:T(8,128)(2,1)}), bf16[8,8,512]{2,0,1:T(8,128)(2,1)S(1)}, u32[]{:S(2)}, u32[]{:S(2)}) %all-to-all-start) | async-done | bytes 65568 | tf_op jit(solution)/shard_map/all_to_all | solution.py:291
  71.4 5.6 %collective-permute-start.9 = (bf16[512,1024]{1,0:T(8,128)(2,1)}, bf16[512,1024]{1,0:T(8,128)(2,1)}, u32[]{:S(2)}, u32[]{:S(2)}) collective-permute-start(bf16[512,1024]{1,0:T(8,128)(2,1)} %pad_maximum_fusion.refs_0_), channel_id=1, source_target_pairs={{0,8},{4,12},{8,16},{12,20},{16,24},{20,28},{1,9},{5,13},{9,17},{1... | collective-permute-start | bytes 3145736 | tf_op jit(solution)/shard_map/ppermute | solution.py:35
  78.3 1.5 fusion.8
  80.1 1.6 collective-permute-start.7
  81.8 3.4 collective-permute-start.5
  86.0 5.8 %all-to-all-start.1 = ((f32[8,8,2048]{2,1,0:T(8,128)}), f32[8,8,2048]{2,1,0:T(8,128)}, u32[]{:S(2)}, u32[]{:S(2)}) async-start(f32[8,8,2048]{2,1,0:T(8,128)} %maximum_bitcast_fusion), calls=%async_computation.1 | async-start | bytes 1048576 | tf_op jit(solution)/shard_map/all_to_all | solution.py:304
  91.8 36.9 %all-to-all-done.1 = f32[8,8,2048]{2,1,0:T(8,128)} async-done(((f32[8,8,2048]{2,1,0:T(8,128)}), f32[8,8,2048]{2,1,0:T(8,128)}, u32[]{:S(2)}, u32[]{:S(2)}) %all-to-all-start.1) | async-done | bytes 524320 | tf_op jit(solution)/shard_map/all_to_all | solution.py:304
  131.1 1.6 collective-permute-start.13
  135.3 1.7 collective-permute-start.11
  137.0 1.7 collective-permute-start.12
  139.4 12.4 %all-to-all-start.2 = ((bf16[8,8,2048]{2,1,0:T(8,128)(2,1)}), bf16[8,8,2048]{2,1,0:T(8,128)(2,1)S(1)}, u32[]{:S(2)}, u32[]{:S(2)}) async-start(bf16[8,8,2048]{2,1,0:T(8,128)(2,1)} %broadcast_in_dim.16), calls=%async_computation.2 | async-start | bytes 524288 | tf_op jit(solution)/shard_map/all_to_all | solution.py:313
  151.8 30.5 %all-to-all-done.2 = bf16[8,8,2048]{2,1,0:T(8,128)(2,1)S(1)} async-done(((bf16[8,8,2048]{2,1,0:T(8,128)(2,1)}), bf16[8,8,2048]{2,1,0:T(8,128)(2,1)S(1)}, u32[]{:S(2)}, u32[]{:S(2)}) %all-to-all-start.2) | async-done | bytes 262176 | tf_op jit(solution)/shard_map/all_to_all | solution.py:313
  182.4 2.3 broadcast_select_fusion.1.refs_3_
  186.1 3.0 collective-permute-start.17
  191.3 7.1 %all-to-all-start.3 = ((bf16[1,64,8,512]{3,1,0,2:T(8,128)(2,1)}), bf16[1,64,8,512]{3,1,0,2:T(8,128)(2,1)}, u32[]{:S(2)}, u32[]{:S(2)}) async-start(bf16[1,64,8,512]{3,1,0,2:T(8,128)(2,1)} %copy.17), calls=%async_computation.3 | async-start | bytes 1048576 | tf_op jit(solution)/shard_map/all_to_all | solution.py:334
  198.5 15.7 %collective-permute-done.16.refs_4_ = bf16[512,1024]{1,0:T(8,128)(2,1)} collective-permute-done((bf16[512,1024]{1,0:T(8,128)(2,1)}, bf16[512,1024]{1,0:T(8,128)(2,1)}, u32[]{:S(2)}, u32[]{:S(2)}) %collective-permute-start.16) | collective-permute-done | bytes 1048608 | tf_op jit(solution)/shard_map/ppermute | solution.py:35
  215.4 7.6 %shard_map.103 = (bf16[256,512]{1,0:T(8,128)(2,1)S(1)}, bf16[256,512]{1,0:T(8,128)(2,1)}) custom-call(s32[4]{0:T(128)S(1)} %pad_add_fusion.place, bf16[256,4096]{1,0:T(8,128)(2,1)} %bitcast.47, bf16[256,2048]{1,0:T(8,128)(2,1)} %collective-permute-done.3.here, bf16[256,2048]{1,0:T(8,128)(2,1)} %collective-permute-done.15.there, ...), custom_call_target="tpu_custom_call" | custom-call | flops 2147483648 | bytes 9961472 | tf_op jit(solution)/shard_map/pallas_call | solution.py:201
  224.9 8.0 %shard_map.104 = (bf16[256,1024]{1,0:T(8,128)(2,1)S(1)}, bf16[256,1024]{1,0:T(8,128)(2,1)S(1)}) custom-call(s32[4]{0:T(128)S(1)} %pad_add_fusion.place, bf16[256,4096]{1,0:T(8,128)(2,1)} %bitcast.48, bf16[64,2048]{1,0:T(8,128)(2,1)S(1)} %bitcast.42, bf16[512,1024]{1,0:T(8,128)(2,1)S(1)} %copy-done.1, bf16[512,1024]{1,0:T(8,128)(2,1)S(1)} %copy-done.3, ...), custom_call_target="tpu_custom_call" | custom-call | flops 2147483648 | bytes 13893632 | tf_op jit(solution)/shard_map/pallas_call | solution.py:201
  233.0 2.5 shard_map.105
  237.1 7.3 %all-to-all-start.4 = ((f32[8,8,2048]{2,1,0:T(8,128)}), f32[8,8,2048]{2,1,0:T(8,128)}, u32[]{:S(2)}, u32[]{:S(2)}) async-start(f32[8,8,2048]{2,1,0:T(8,128)} %bitcast.44), calls=%async_computation.4 | async-start | bytes 1048576 | tf_op jit(solution)/shard_map/all_to_all | solution.py:378
  244.6 2.0 collective-permute-start.20
  246.6 3.3 collective-permute-start.21
  252.1 7.8 %shard_map.106 = bf16[4,2,256,512]{3,2,1,0:T(8,128)(2,1)} custom-call(s32[4]{0:T(128)S(1)} %pad_add_fusion.place, bf16[256,1024]{1,0:T(8,128)(2,1)S(1)} %copy-done.7, bf16[512,1024]{1,0:T(8,128)(2,1)S(1)} %copy-done.1, bf16[512,1024]{1,0:T(8,128)(2,1)S(1)} %copy-done.4, bf16[512,1024]{1,0:T(8,128)(2,1)} %collective-permute-done.2.refs_2_, ...), custom_call_target="tpu_custom_call" | custom-call | flops 2147483648 | bytes 13107200 | tf_op jit(solution)/shard_map/pallas_call | solution.py:201
  262.2 4.1 %collective-permute-done.21.refs_3_ = bf16[256,1024]{1,0:T(8,128)(2,1)} collective-permute-done((bf16[256,1024]{1,0:T(8,128)(2,1)}, bf16[256,1024]{1,0:T(8,128)(2,1)}, u32[]{:S(2)}, u32[]{:S(2)}) %collective-permute-start.21) | collective-permute-done | bytes 524320 | tf_op jit(solution)/shard_map/ppermute | solution.py:35
  266.3 8.2 %collective-permute-done.22.refs_5_ = bf16[256,1024]{1,0:T(8,128)(2,1)} collective-permute-done((bf16[256,1024]{1,0:T(8,128)(2,1)}, bf16[256,1024]{1,0:T(8,128)(2,1)}, u32[]{:S(2)}, u32[]{:S(2)}) %collective-permute-start.22) | collective-permute-done | bytes 524320 | tf_op jit(solution)/shard_map/ppermute | solution.py:35
  276.5 2.0 collective-permute-start.27
  279.3 4.8 %all-to-all-start.5 = ((bf16[8,8,2048]{2,1,0:T(8,128)(2,1)}), bf16[8,8,2048]{2,1,0:T(8,128)(2,1)S(1)}, u32[]{:S(2)}, u32[]{:S(2)}) async-start(bf16[8,8,2048]{2,1,0:T(8,128)(2,1)} %broadcast_in_dim.17), calls=%async_computation.5 | async-start | bytes 524288 | tf_op jit(solution)/shard_map/all_to_all | solution.py:313
  284.1 2.5 slice_bitcast_fusion.2
  287.0 18.5 %all-to-all-done.5 = bf16[8,8,2048]{2,1,0:T(8,128)(2,1)S(1)} async-done(((bf16[8,8,2048]{2,1,0:T(8,128)(2,1)}), bf16[8,8,2048]{2,1,0:T(8,128)(2,1)S(1)}, u32[]{:S(2)}, u32[]{:S(2)}) %all-to-all-start.5) | async-done | bytes 262176 | tf_op jit(solution)/shard_map/all_to_all | solution.py:313
  306.0 2.3 fusion
  308.3 3.4 all-to-all-start.6
  312.2 1.8 all-to-all-done.6
  314.0 3.7 %collective-permute-start.29 = (bf16[8,512]{1,0:T(8,128)(2,1)S(1)}, bf16[8,512]{1,0:T(8,128)(2,1)S(1)}, u32[]{:S(2)}, u32[]{:S(2)}) collective-permute-start(bf16[8,512]{1,0:T(8,128)(2,1)S(1)} %get-tuple-element.112), channel_id=1, source_target_pairs={{0,0},{1,8},{2,16},{3,24},{4,4},{5,12},{6,20},{7,28},{8,1},{9,9},{... | collective-permute-start | bytes 24584 | tf_op jit(solution)/shard_map/ppermute | solution.py:238
  317.7 3.7 %collective-permute-done.29 = bf16[8,512]{1,0:T(8,128)(2,1)S(1)} collective-permute-done((bf16[8,512]{1,0:T(8,128)(2,1)S(1)}, bf16[8,512]{1,0:T(8,128)(2,1)S(1)}, u32[]{:S(2)}, u32[]{:S(2)}) %collective-permute-start.29) | collective-permute-done | bytes 8224 | tf_op jit(solution)/shard_map/ppermute | solution.py:238
  321.4 2.6 collective-permute-start.30
  323.9 3.9 %collective-permute-done.30 = bf16[8,512]{1,0:T(8,128)(2,1)S(1)} collective-permute-done((bf16[8,512]{1,0:T(8,128)(2,1)S(1)}, bf16[8,512]{1,0:T(8,128)(2,1)S(1)}, u32[]{:S(2)}, u32[]{:S(2)}) %collective-permute-start.30) | collective-permute-done | bytes 8224 | tf_op jit(solution)/shard_map/ppermute | solution.py:238
  327.8 1.7 collective-permute-start.32
  330.2 1.8 fusion.4
  333.3 2.2 reshape.88
  335.5 6.7 %collective-permute-done.32.refs_8_ = bf16[256,1024]{1,0:T(8,128)(2,1)} collective-permute-done((bf16[256,1024]{1,0:T(8,128)(2,1)}, bf16[256,1024]{1,0:T(8,128)(2,1)}, u32[]{:S(2)}, u32[]{:S(2)}) %collective-permute-start.32) | collective-permute-done | bytes 524320 | tf_op jit(solution)/shard_map/ppermute | solution.py:40
  342.2 5.6 %shard_map.107 = bf16[1024,512]{1,0:T(8,128)(2,1)} custom-call(s32[4]{0:T(128)S(1)} %pad_add_fusion.place, bf16[2,8,64,512]{3,2,1,0:T(8,128)(2,1)S(1)} %pad_maximum_fusion.1.refs_0_, bf16[2,8,64,512]{3,2,1,0:T(8,128)(2,1)} %collective-permute-done.31.refs_1_, bf16[256,1024]{1,0:T(8,128)(2,1)S(1)} %copy-done.12, ...), custom_call_target="tpu_custom_call" | custom-call | flops 2147483648 | bytes 7340032 | tf_op jit(solution)/shard_map/pallas_call | solution.py:201
  (100 shorter events, 34.4 us)
Async XLA Ops:
  0.6 79.2 %copy-start = (bf16[512,1024]{1,0:T(8,128)(2,1)S(1)}, bf16[512,1024]{1,0:T(8,128)(2,1)}, u32[]{:S(2)}) copy-start(bf16[512,1024]{1,0:T(8,128)(2,1)} %param.14) | copy-start | bytes 3145732
  0.6 10.7 %copy-start.14 = (s32[2]{0:T(128)S(1)}, s32[2]{0:T(128)}, u32[]{:S(2)}) copy-start(s32[2]{0:T(128)} %param.11) | copy-start | bytes 28
  0.7 69.4 %collective-permute-start.1 = (bf16[512,1024]{1,0:T(8,128)(2,1)}, bf16[512,1024]{1,0:T(8,128)(2,1)S(1)}, u32[]{:S(2)}, u32[]{:S(2)}) collective-permute-start(bf16[512,1024]{1,0:T(8,128)(2,1)} %refs_0_.3), channel_id=1, source_target_pairs={{8,0},{12,4},{16,8},{20,12},{24,16},{28,20},{9,1},{13,5},{17,9},{2... | collective-permute-start | bytes 3145736 | tf_op jit(solution)/shard_map/ppermute | solution.py:35
  2.1 68.0 %collective-permute-start.2 = (bf16[512,1024]{1,0:T(8,128)(2,1)}, bf16[512,1024]{1,0:T(8,128)(2,1)}, u32[]{:S(2)}, u32[]{:S(2)}) collective-permute-start(bf16[512,1024]{1,0:T(8,128)(2,1)} %refs_0_.3), channel_id=1, source_target_pairs={{0,8},{4,12},{8,16},{12,20},{16,24},{20,28},{1,9},{5,13},{9,17},{1... | collective-permute-start | bytes 3145736 | tf_op jit(solution)/shard_map/ppermute | solution.py:35
  9.9 13.4 %collective-permute-start = (bf16[512,512]{1,0:T(8,128)(2,1)}, bf16[512,512]{1,0:T(8,128)(2,1)}, u32[]{:S(2)}, u32[]{:S(2)}) collective-permute-start(bf16[512,512]{1,0:T(8,128)(2,1)} %get-tuple-element.111), channel_id=1, source_target_pairs={{0,4},{4,0},{8,12},{12,8},{16,20},{20,16},{24,28},{28,24},{1,5},{5... | collective-permute-start | bytes 1572872 | tf_op jit(solution)/shard_map/ppermute | solution.py:40
  14.6 10.2 %copy-start.1 = (bf16[512,1024]{1,0:T(8,128)(2,1)S(1)}, bf16[512,1024]{1,0:T(8,128)(2,1)}, u32[]{:S(2)}) copy-start(bf16[512,1024]{1,0:T(8,128)(2,1)} %refs_0_.3) | copy-start | bytes 3145732
  14.6 10.7 %copy-start.13 = (bf16[2,4,4096]{2,1,0:T(4,128)(2,1)S(1)}, bf16[2,4,4096]{2,1,0:T(4,128)(2,1)}, u32[]{:S(2)}) copy-start(bf16[2,4,4096]{2,1,0:T(4,128)(2,1)} %param.9) | copy-start | bytes 196612
  23.3 56.8 %collective-permute-start.3 = (bf16[256,2048]{1,0:T(8,128)(2,1)}, bf16[256,2048]{1,0:T(8,128)(2,1)}, u32[]{:S(2)}, u32[]{:S(2)}) collective-permute-start(bf16[256,2048]{1,0:T(8,128)(2,1)} %constant_dynamic-slice_fusion.2), channel_id=1, source_target_pairs={{0,4},{4,0},{8,12},{12,8},{16,20},{20,16},{24,28},{28,24},{1,5},{5... | collective-permute-start | bytes 3145736 | tf_op jit(solution)/shard_map/ppermute | solution.py:40
  24.8 57.0 %collective-permute-start.4 = (bf16[512,1024]{1,0:T(8,128)(2,1)S(1)}, bf16[512,1024]{1,0:T(8,128)(2,1)}, u32[]{:S(2)}, u32[]{:S(2)}) collective-permute-start(bf16[512,1024]{1,0:T(8,128)(2,1)S(1)} %copy-done.1), channel_id=1, source_target_pairs={{0,4},{4,0},{8,12},{12,8},{16,20},{20,16},{24,28},{28,24},{1,5},{5... | collective-permute-start | bytes 3145736 | tf_op jit(solution)/shard_map/ppermute | solution.py:40
  26.0 44.1 %all-to-all-start = ((bf16[8,8,512]{2,0,1:T(8,128)(2,1)}), bf16[8,8,512]{2,0,1:T(8,128)(2,1)S(1)}, u32[]{:S(2)}, u32[]{:S(2)}) async-start(bf16[8,8,512]{2,0,1:T(8,128)(2,1)} %copy.16), calls=%async_computation | async-start | bytes 131072 | tf_op jit(solution)/shard_map/all_to_all | solution.py:291
  70.1 15.9 %copy-start.2 = (bf16[512,1024]{1,0:T(8,128)(2,1)}, bf16[512,1024]{1,0:T(8,128)(2,1)S(1)}, u32[]{:S(2)}) copy-start(bf16[512,1024]{1,0:T(8,128)(2,1)S(1)} %collective-permute-done.1.refs_1_) | copy-start | bytes 3145732
  70.1 59.7 %collective-permute-start.8 = (bf16[512,1024]{1,0:T(8,128)(2,1)}, bf16[512,1024]{1,0:T(8,128)(2,1)}, u32[]{:S(2)}, u32[]{:S(2)}) collective-permute-start(bf16[512,1024]{1,0:T(8,128)(2,1)} %pad_maximum_fusion.refs_0_), channel_id=1, source_target_pairs={{8,0},{12,4},{16,8},{20,12},{24,16},{28,20},{9,1},{13,5},{17,9},{2... | collective-permute-start | bytes 3145736 | tf_op jit(solution)/shard_map/ppermute | solution.py:35
  71.4 58.4 %collective-permute-start.9 = (bf16[512,1024]{1,0:T(8,128)(2,1)}, bf16[512,1024]{1,0:T(8,128)(2,1)}, u32[]{:S(2)}, u32[]{:S(2)}) collective-permute-start(bf16[512,1024]{1,0:T(8,128)(2,1)} %pad_maximum_fusion.refs_0_), channel_id=1, source_target_pairs={{0,8},{4,12},{8,16},{12,20},{16,24},{20,28},{1,9},{5,13},{9,17},{1... | collective-permute-start | bytes 3145736 | tf_op jit(solution)/shard_map/ppermute | solution.py:35
  77.0 52.8 %collective-permute-start.6 = (bf16[512,1024]{1,0:T(8,128)(2,1)S(1)}, bf16[512,1024]{1,0:T(8,128)(2,1)}, u32[]{:S(2)}, u32[]{:S(2)}) collective-permute-start(bf16[512,1024]{1,0:T(8,128)(2,1)S(1)} %collective-permute-done.1.refs_1_), channel_id=1, source_target_pairs={{8,0},{12,4},{16,8},{20,12},{9,1},{13,5},{17,9},{21,13},{10,2},{14... | collective-permute-start | bytes 3145736 | tf_op jit(solution)/shard_map/ppermute | solution.py:35
  80.1 49.6 %collective-permute-start.7 = (bf16[512,1024]{1,0:T(8,128)(2,1)}, bf16[512,1024]{1,0:T(8,128)(2,1)}, u32[]{:S(2)}, u32[]{:S(2)}) collective-permute-start(bf16[512,1024]{1,0:T(8,128)(2,1)} %collective-permute-done.2.refs_2_), channel_id=1, source_target_pairs={{8,16},{12,20},{16,24},{20,28},{9,17},{13,21},{17,25},{21,29},{10,... | collective-permute-start | bytes 3145736 | tf_op jit(solution)/shard_map/ppermute | solution.py:35
  81.8 48.0 %collective-permute-start.5 = (bf16[512,1024]{1,0:T(8,128)(2,1)S(1)}, bf16[512,1024]{1,0:T(8,128)(2,1)}, u32[]{:S(2)}, u32[]{:S(2)}) collective-permute-start(bf16[512,1024]{1,0:T(8,128)(2,1)S(1)} %collective-permute-done.1.refs_1_), channel_id=1, source_target_pairs={{0,4},{4,0},{8,12},{12,8},{16,20},{20,16},{1,5},{5,1},{9,13},{13,9... | collective-permute-start | bytes 3145736 | tf_op jit(solution)/shard_map/ppermute | solution.py:40
  86.0 42.7 %all-to-all-start.1 = ((f32[8,8,2048]{2,1,0:T(8,128)}), f32[8,8,2048]{2,1,0:T(8,128)}, u32[]{:S(2)}, u32[]{:S(2)}) async-start(f32[8,8,2048]{2,1,0:T(8,128)} %maximum_bitcast_fusion), calls=%async_computation.1 | async-start | bytes 1048576 | tf_op jit(solution)/shard_map/all_to_all | solution.py:304
  131.1 51.2 %collective-permute-start.13 = (bf16[512,1024]{1,0:T(8,128)(2,1)S(1)}, bf16[512,1024]{1,0:T(8,128)(2,1)}, u32[]{:S(2)}, u32[]{:S(2)}) collective-permute-start(bf16[512,1024]{1,0:T(8,128)(2,1)S(1)} %broadcast_select_fusion.2.refs_3_), channel_id=1, source_target_pairs={{0,4},{4,0},{8,12},{12,8},{16,20},{20,16},{24,28},{28,24},{1,5},{5... | collective-permute-start | bytes 3145736 | tf_op jit(solution)/shard_map/ppermute | solution.py:40
  132.7 49.7 %collective-permute-start.14 = (bf16[512,1024]{1,0:T(8,128)(2,1)S(1)}, bf16[512,1024]{1,0:T(8,128)(2,1)}, u32[]{:S(2)}, u32[]{:S(2)}) collective-permute-start(bf16[512,1024]{1,0:T(8,128)(2,1)S(1)} %broadcast_select_fusion.2.refs_3_), channel_id=1, source_target_pairs={{8,0},{12,4},{16,24},{20,28},{9,1},{13,5},{17,25},{21,29},{10,2},{... | collective-permute-start | bytes 3145736 | tf_op jit(solution)/shard_map/ppermute | solution.py:35
  134.0 48.4 %collective-permute-start.10 = (bf16[512,1024]{1,0:T(8,128)(2,1)}, bf16[512,1024]{1,0:T(8,128)(2,1)}, u32[]{:S(2)}, u32[]{:S(2)}) collective-permute-start(bf16[512,1024]{1,0:T(8,128)(2,1)} %collective-permute-done.8.refs_1_), channel_id=1, source_target_pairs={{8,0},{12,4},{16,8},{20,12},{9,1},{13,5},{17,9},{21,13},{10,2},{14... | collective-permute-start | bytes 3145736 | tf_op jit(solution)/shard_map/ppermute | solution.py:35
  135.3 47.1 %collective-permute-start.11 = (bf16[512,1024]{1,0:T(8,128)(2,1)}, bf16[512,1024]{1,0:T(8,128)(2,1)}, u32[]{:S(2)}, u32[]{:S(2)}) collective-permute-start(bf16[512,1024]{1,0:T(8,128)(2,1)} %collective-permute-done.9.refs_2_), channel_id=1, source_target_pairs={{8,16},{12,20},{16,24},{20,28},{9,17},{13,21},{17,25},{21,29},{10,... | collective-permute-start | bytes 3145736 | tf_op jit(solution)/shard_map/ppermute | solution.py:35
  137.0 45.4 %collective-permute-start.12 = (bf16[512,1024]{1,0:T(8,128)(2,1)}, bf16[512,1024]{1,0:T(8,128)(2,1)}, u32[]{:S(2)}, u32[]{:S(2)}) collective-permute-start(bf16[512,1024]{1,0:T(8,128)(2,1)} %collective-permute-done.2.refs_2_), channel_id=1, source_target_pairs={{8,12},{12,8},{16,20},{20,16},{24,28},{28,24},{9,13},{13,9},{17,21... | collective-permute-start | bytes 3145736 | tf_op jit(solution)/shard_map/ppermute | solution.py:40
  139.4 43.0 %all-to-all-start.2 = ((bf16[8,8,2048]{2,1,0:T(8,128)(2,1)}), bf16[8,8,2048]{2,1,0:T(8,128)(2,1)S(1)}, u32[]{:S(2)}, u32[]{:S(2)}) async-start(bf16[8,8,2048]{2,1,0:T(8,128)(2,1)} %broadcast_in_dim.16), calls=%async_computation.2 | async-start | bytes 524288 | tf_op jit(solution)/shard_map/all_to_all | solution.py:313
  184.7 29.5 %collective-permute-start.16 = (bf16[512,1024]{1,0:T(8,128)(2,1)}, bf16[512,1024]{1,0:T(8,128)(2,1)}, u32[]{:S(2)}, u32[]{:S(2)}) collective-permute-start(bf16[512,1024]{1,0:T(8,128)(2,1)} %broadcast_select_fusion.1.refs_3_), channel_id=1, source_target_pairs={{8,0},{12,4},{16,24},{20,28},{9,1},{13,5},{17,25},{21,29},{10,2},{... | collective-permute-start | bytes 3145736 | tf_op jit(solution)/shard_map/ppermute | solution.py:35
  186.0 28.2 %collective-permute-start.15 = (bf16[256,2048]{1,0:T(8,128)(2,1)}, bf16[256,2048]{1,0:T(8,128)(2,1)}, u32[]{:S(2)}, u32[]{:S(2)}) collective-permute-start(bf16[256,2048]{1,0:T(8,128)(2,1)} %collective-permute-done.3.here), channel_id=1, source_target_pairs={{0,1},{1,0},{2,3},{3,2},{4,5},{5,4},{6,7},{7,6},{8,9},{9,8},{10,11... | collective-permute-start | bytes 3145736 | tf_op jit(solution)/shard_map/ppermute | solution.py:271
  186.1 37.6 %collective-permute-start.17 = (bf16[512,1024]{1,0:T(8,128)(2,1)}, bf16[512,1024]{1,0:T(8,128)(2,1)}, u32[]{:S(2)}, u32[]{:S(2)}) collective-permute-start(bf16[512,1024]{1,0:T(8,128)(2,1)} %collective-permute-done.14.refs_4_), channel_id=1, source_target_pairs={{0,4},{4,0},{24,28},{28,24},{1,5},{5,1},{25,29},{29,25},{2,6},{6,2... | collective-permute-start | bytes 3145736 | tf_op jit(solution)/shard_map/ppermute | solution.py:40
  191.3 32.4 %all-to-all-start.3 = ((bf16[1,64,8,512]{3,1,0,2:T(8,128)(2,1)}), bf16[1,64,8,512]{3,1,0,2:T(8,128)(2,1)}, u32[]{:S(2)}, u32[]{:S(2)}) async-start(bf16[1,64,8,512]{3,1,0,2:T(8,128)(2,1)} %copy.17), calls=%async_computation.3 | async-start | bytes 1048576 | tf_op jit(solution)/shard_map/all_to_all | solution.py:334
  223.7 9.3 %collective-permute-start.18 = (bf16[256,512]{1,0:T(8,128)(2,1)}, bf16[256,512]{1,0:T(8,128)(2,1)}, u32[]{:S(2)}, u32[]{:S(2)}) collective-permute-start(bf16[256,512]{1,0:T(8,128)(2,1)} %get-tuple-element.78), channel_id=1, source_target_pairs={{0,4},{4,0},{8,12},{12,8},{16,20},{20,16},{24,28},{28,24},{1,5},{5... | collective-permute-start | bytes 786440 | tf_op jit(solution)/shard_map/ppermute | solution.py:40
  224.9 8.0 %copy-start.10 = (bf16[256,512]{1,0:T(8,128)(2,1)S(1)}, bf16[256,512]{1,0:T(8,128)(2,1)}, u32[]{:S(2)}) copy-start(bf16[256,512]{1,0:T(8,128)(2,1)} %copy-done.9) | copy-start | bytes 786436
  232.9 2.5 copy-start.11
  237.1 24.0 %all-to-all-start.4 = ((f32[8,8,2048]{2,1,0:T(8,128)}), f32[8,8,2048]{2,1,0:T(8,128)}, u32[]{:S(2)}, u32[]{:S(2)}) async-start(f32[8,8,2048]{2,1,0:T(8,128)} %bitcast.44), calls=%async_computation.4 | async-start | bytes 1048576 | tf_op jit(solution)/shard_map/all_to_all | solution.py:378
  244.4 15.5 %collective-permute-start.19 = (bf16[8,64,512]{2,1,0:T(8,128)(2,1)}, bf16[8,64,512]{2,1,0:T(8,128)(2,1)S(1)}, u32[]{:S(2)}, u32[]{:S(2)}) collective-permute-start(bf16[8,64,512]{2,1,0:T(8,128)(2,1)} %bitcast.12), channel_id=1, source_target_pairs={{0,2},{1,3},{2,0},{3,1},{4,6},{5,7},{6,4},{7,5},{8,10},{9,11},{10,... | collective-permute-start | bytes 1572872 | tf_op jit(solution)/shard_map/ppermute | solution.py:271
  244.6 17.7 %collective-permute-start.20 = (bf16[256,1024]{1,0:T(8,128)(2,1)}, bf16[256,1024]{1,0:T(8,128)(2,1)}, u32[]{:S(2)}, u32[]{:S(2)}) collective-permute-start(bf16[256,1024]{1,0:T(8,128)(2,1)} %copy-done.11), channel_id=1, source_target_pairs={{0,4},{4,0},{8,12},{12,8},{16,20},{20,16},{24,28},{28,24},{1,5},{5... | collective-permute-start | bytes 1572872 | tf_op jit(solution)/shard_map/ppermute | solution.py:40
  246.6 19.7 %collective-permute-start.21 = (bf16[256,1024]{1,0:T(8,128)(2,1)}, bf16[256,1024]{1,0:T(8,128)(2,1)}, u32[]{:S(2)}, u32[]{:S(2)}) collective-permute-start(bf16[256,1024]{1,0:T(8,128)(2,1)} %copy-done.11), channel_id=1, source_target_pairs={{8,0},{12,4},{16,8},{20,12},{24,16},{28,20},{0,24},{4,28},{9,1},{1... | collective-permute-start | bytes 1572872 | tf_op jit(solution)/shard_map/ppermute | solution.py:35
  249.9 24.6 %collective-permute-start.22 = (bf16[256,1024]{1,0:T(8,128)(2,1)}, bf16[256,1024]{1,0:T(8,128)(2,1)}, u32[]{:S(2)}, u32[]{:S(2)}) collective-permute-start(bf16[256,1024]{1,0:T(8,128)(2,1)} %copy-done.11), channel_id=1, source_target_pairs={{24,0},{28,4},{0,8},{4,12},{8,16},{12,20},{16,24},{20,28},{25,1},{... | collective-permute-start | bytes 1572872 | tf_op jit(solution)/shard_map/ppermute | solution.py:35
  259.9 16.6 %copy-start.12 = (bf16[256,1024]{1,0:T(8,128)(2,1)S(1)}, bf16[256,1024]{1,0:T(8,128)(2,1)}, u32[]{:S(2)}) copy-start(bf16[256,1024]{1,0:T(8,128)(2,1)} %copy-done.11) | copy-start | bytes 1572868
  274.5 31.0 %collective-permute-start.25 = (bf16[256,1024]{1,0:T(8,128)(2,1)}, bf16[256,1024]{1,0:T(8,128)(2,1)S(1)}, u32[]{:S(2)}, u32[]{:S(2)}) collective-permute-start(bf16[256,1024]{1,0:T(8,128)(2,1)} %collective-permute-done.21.refs_3_), channel_id=1, source_target_pairs={{0,4},{4,0},{8,12},{12,8},{16,20},{20,16},{24,28},{28,24},{1,5},{5... | collective-permute-start | bytes 1572872 | tf_op jit(solution)/shard_map/ppermute | solution.py:40
  275.9 29.6 %collective-permute-start.26 = (bf16[256,1024]{1,0:T(8,128)(2,1)}, bf16[256,1024]{1,0:T(8,128)(2,1)}, u32[]{:S(2)}, u32[]{:S(2)}) collective-permute-start(bf16[256,1024]{1,0:T(8,128)(2,1)} %collective-permute-done.22.refs_5_), channel_id=1, source_target_pairs={{0,4},{4,0},{8,12},{12,8},{16,20},{20,16},{24,28},{28,24},{1,5},{5... | collective-permute-start | bytes 1572872 | tf_op jit(solution)/shard_map/ppermute | solution.py:40
  276.5 29.0 %collective-permute-start.27 = (bf16[256,1024]{1,0:T(8,128)(2,1)S(1)}, bf16[256,1024]{1,0:T(8,128)(2,1)}, u32[]{:S(2)}, u32[]{:S(2)}) collective-permute-start(bf16[256,1024]{1,0:T(8,128)(2,1)S(1)} %copy-done.12), channel_id=1, source_target_pairs={{16,0},{20,4},{24,8},{28,12},{0,16},{4,20},{8,24},{12,28},{17,1},{... | collective-permute-start | bytes 1572872 | tf_op jit(solution)/shard_map/ppermute | solution.py:35
  279.3 26.2 %all-to-all-start.5 = ((bf16[8,8,2048]{2,1,0:T(8,128)(2,1)}), bf16[8,8,2048]{2,1,0:T(8,128)(2,1)S(1)}, u32[]{:S(2)}, u32[]{:S(2)}) async-start(bf16[8,8,2048]{2,1,0:T(8,128)(2,1)} %broadcast_in_dim.17), calls=%async_computation.5 | async-start | bytes 524288 | tf_op jit(solution)/shard_map/all_to_all | solution.py:313
  286.6 43.6 %collective-permute-start.23 = (bf16[2,256,512]{2,1,0:T(8,128)(2,1)}, bf16[2,256,512]{2,1,0:T(8,128)(2,1)}, u32[]{:S(2)}, u32[]{:S(2)}) collective-permute-start(bf16[2,256,512]{2,1,0:T(8,128)(2,1)} %get-tuple-element.107), channel_id=1, source_target_pairs={{0,3},{1,2},{2,1},{3,0},{4,7},{5,6},{6,5},{7,4},{8,11},{9,10},{10,... | collective-permute-start | bytes 1572872 | tf_op jit(solution)/shard_map/ppermute | solution.py:271
  286.6 43.6 %collective-permute-start.24 = (bf16[2,256,512]{2,1,0:T(8,128)(2,1)}, bf16[2,256,512]{2,1,0:T(8,128)(2,1)}, u32[]{:S(2)}, u32[]{:S(2)}) collective-permute-start(bf16[2,256,512]{2,1,0:T(8,128)(2,1)} %get-tuple-element.109), channel_id=1, source_target_pairs={{0,2},{1,3},{2,0},{3,1},{4,6},{5,7},{6,4},{7,5},{8,10},{9,11},{10,... | collective-permute-start | bytes 1572872 | tf_op jit(solution)/shard_map/ppermute | solution.py:271
  305.5 36.7 %collective-permute-start.31 = (bf16[2,8,64,512]{3,2,1,0:T(8,128)(2,1)S(1)}, bf16[2,8,64,512]{3,2,1,0:T(8,128)(2,1)}, u32[]{:S(2)}, u32[]{:S(2)}) collective-permute-start(bf16[2,8,64,512]{3,2,1,0:T(8,128)(2,1)S(1)} %pad_maximum_fusion.1.refs_0_), channel_id=1, source_target_pairs={{0,1},{1,0},{2,3},{3,2},{4,5},{5,4},{6,7},{7,6},{8,9},{9,8},{10,11... | collective-permute-start | bytes 3145736 | tf_op jit(solution)/shard_map/ppermute | solution.py:271
  308.3 5.7 %all-to-all-start.6 = ((bf16[4,16,512]{2,1,0:T(8,128)(2,1)}), bf16[4,16,512]{2,1,0:T(8,128)(2,1)S(1)}, u32[]{:S(2)}, u32[]{:S(2)}) async-start(bf16[4,16,512]{2,1,0:T(8,128)(2,1)} %bitcast.22), calls=%async_computation.6 | async-start | bytes 131072 | tf_op jit(solution)/shard_map/all_to_all | solution.py:223
  311.7 18.5 %collective-permute-start.28 = (bf16[2,256,512]{2,1,0:T(8,128)(2,1)}, bf16[2,256,512]{2,1,0:T(8,128)(2,1)}, u32[]{:S(2)}, u32[]{:S(2)}) collective-permute-start(bf16[2,256,512]{2,1,0:T(8,128)(2,1)} %get-tuple-element.100), channel_id=1, source_target_pairs={{0,1},{1,0},{2,3},{3,2},{4,5},{5,4},{6,7},{7,6},{8,9},{9,8},{10,11... | collective-permute-start | bytes 1572872 | tf_op jit(solution)/shard_map/ppermute | solution.py:271
  314.0 7.3 %collective-permute-start.29 = (bf16[8,512]{1,0:T(8,128)(2,1)S(1)}, bf16[8,512]{1,0:T(8,128)(2,1)S(1)}, u32[]{:S(2)}, u32[]{:S(2)}) collective-permute-start(bf16[8,512]{1,0:T(8,128)(2,1)S(1)} %get-tuple-element.112), channel_id=1, source_target_pairs={{0,0},{1,8},{2,16},{3,24},{4,4},{5,12},{6,20},{7,28},{8,1},{9,9},{... | collective-permute-start | bytes 24584 | tf_op jit(solution)/shard_map/ppermute | solution.py:238
  321.4 6.5 %collective-permute-start.30 = (bf16[8,512]{1,0:T(8,128)(2,1)S(1)}, bf16[8,512]{1,0:T(8,128)(2,1)S(1)}, u32[]{:S(2)}, u32[]{:S(2)}) collective-permute-start(bf16[8,512]{1,0:T(8,128)(2,1)S(1)} %get-tuple-element.113), channel_id=1, source_target_pairs={{0,4},{1,12},{2,20},{3,28},{4,0},{5,8},{6,16},{7,24},{8,5},{9,13},... | collective-permute-start | bytes 24584 | tf_op jit(solution)/shard_map/ppermute | solution.py:238
  327.8 14.3 %collective-permute-start.32 = (bf16[256,1024]{1,0:T(8,128)(2,1)}, bf16[256,1024]{1,0:T(8,128)(2,1)}, u32[]{:S(2)}, u32[]{:S(2)}) collective-permute-start(bf16[256,1024]{1,0:T(8,128)(2,1)} %collective-permute-done.27.refs_4_), channel_id=1, source_target_pairs={{0,4},{4,0},{8,12},{12,8},{16,20},{20,16},{24,28},{28,24},{1,5},{5... | collective-permute-start | bytes 1572872 | tf_op jit(solution)/shard_map/ppermute | solution.py:40
  (7 other events, 7.1 us)

commit v6 on v5

--- a/solution.py
+++ b/solution.py
@@ -13,10 +13,6 @@
 BACK = (((1,), (1,)), ((), ()))
 FIRST = (((0,), (0,)), ((), ()))
 VMEM_LIMIT = 48 * 1024 * 1024
-
-
-def after(values, *others):
-    return lax.optimization_barrier((values, *others))[0]
 
 
 def matmul(a, b, dims=None):
@@ -212,18 +208,19 @@
     )(place, *operands)
 
 
-def to_owner(line, terms):
+def to_owner(line, terms, *others):
     n_dp, n_tensor = line.n_dp, lax.axis_size("tensor")
     images, cols = terms.shape
     if line.n_z != n_tensor:
         terms = lax.all_to_all(terms, "dp", split_axis=0, concat_axis=1, tiled=True)
         terms = terms.reshape(images // n_dp, n_tensor, n_dp * cols // n_tensor)
         parts = lax.all_to_all(terms, "tensor", split_axis=1, concat_axis=0)
-        return jnp.sum(parts.astype(F32), axis=0).astype(BF16)
+        return (jnp.sum(parts.astype(F32), axis=0).astype(BF16), *others)
     parts = lax.all_to_all(
         terms.reshape(n_tensor, images // n_tensor, cols), "tensor", split_axis=0, concat_axis=0
     )
     total = jnp.sum(parts.astype(F32), axis=0).astype(BF16)
+    total, *others = lax.optimization_barrier((total, *others))
     total = total.reshape(2, images // n_dp, cols)
     x = lax.axis_index("dp") % 2
     come = []
@@ -236,9 +233,10 @@
             for t in range(n_tensor)
         ]
         come.append(lax.ppermute(block, ("dp", "tensor"), pairs))
-    return jnp.where(
+    rows = jnp.where(
         x == 0, jnp.concatenate(come, axis=1), jnp.concatenate(come[::-1], axis=1)
     )
+    return (rows, *others)
 
 
 def shards(
@@ -280,33 +278,35 @@
     gate = lax.optimization_barrier
 
     relayed = line.n_z == 4
-    wq_moved = line.first(query_weight)
+    image_cols = lax.all_to_all(image_flat, "dp", split_axis=1, concat_axis=0, tiled=True)
     wo_keep = lax.dynamic_slice_in_dim(out_weight, x * half_cols, half_cols, 0)
     wo_send = lax.dynamic_slice_in_dim(out_weight, (1 - x) * half_cols, half_cols, 0)
+    live_half = lax.dynamic_slice_in_dim(live_flat, core * (width // 2), width // 2, 1)
+    query_weight, image_cols, wo_send = gate((query_weight, image_cols, wo_send))
+    wq_moved = line.first(query_weight)
     wo_come = line.swap(wo_send)
-    wq_swapped = line.swap(query_weight)
-    live_half = lax.dynamic_slice_in_dim(live_flat, core * (width // 2), width // 2, 1)
-    live_half, wo_come = gate((live_half, wo_come))
-    live_here = line.swap(live_half)
-    image_cols = lax.all_to_all(image_flat, "dp", split_axis=1, concat_axis=0, tiled=True)
+    wq_others = [line.swap(query_weight)]
     wo_pair = jnp.concatenate([wo_keep, wo_come], axis=1)
-    wo_pair, image_cols, *wq_moved = gate((wo_pair, image_cols, *wq_moved))
-
-    planes = [(0, 1, 2), (1, 2, 3)] if relayed else [None] * len(wq_moved)
+    part_kv = jnp.concatenate(
+        [matmul(image_cols, key_weight), matmul(image_cols, value_weight)], axis=1
+    )
+    part_kv = part_kv.reshape(n_dp, image_rows, 2 * local_cols)
+    kv_own = jnp.sum(lax.all_to_all(part_kv, "dp", split_axis=0, concat_axis=0), axis=0)
+    kv_own, live_half, wo_pair, wq_others[0], *wq_moved = gate(
+        (kv_own.astype(BF16), live_half, wo_pair, wq_others[0], *wq_moved)
+    )
+
+    n_moved = len(wq_moved)
+    planes = [(0, 1, 2), (1, 2, 3)] if relayed else [None] * n_moved
     wq_two = line.second(wq_moved)
     wo_moved = line.first(wo_pair)
-    above, live_here = gate((wq_moved[0], live_here))
-    wq_others = [line.swap(above, planes[0])]
-    part_kv = jnp.concatenate(
-        [matmul(image_cols, key_weight), matmul(image_cols, value_weight)], axis=1
-    )
-    part_kv = part_kv.reshape(n_dp, image_rows, 2 * local_cols)
-    kv_own = jnp.sum(lax.all_to_all(part_kv, "dp", split_axis=0, concat_axis=0), axis=0)
-    kv_own, live_here, wq_swapped, wq_others[0], *moved = gate(
-        (kv_own, live_here, wq_swapped, wq_others[0], *wq_moved, *wq_two, *wo_moved)
-    )
-    n_moved = len(wq_moved)
-    wq_moved, wq_two, wo_moved = moved[:n_moved], moved[n_moved:-n_moved], moved[-n_moved:]
+    above, live_here = gate((wq_moved[0], line.swap(live_half)))
+    wq_others.append(line.swap(above, planes[0]))
+    kv_own, live_here, *staged = gate(
+        (kv_own, live_here, *wq_others, *wq_moved, *wq_two, *wo_moved)
+    )
+    wq_others, staged = staged[:2], staged[2:]
+    wq_moved, wq_two, wo_moved = staged[:n_moved], staged[n_moved:-n_moved], staged[-n_moved:]
 
     def everywhere(values):
         copies = jnp.broadcast_to(values[None], (n_dp, *values.shape))
@@ -316,13 +316,12 @@
     wo_two = line.second(wo_moved)
     wq_others += [line.swap(block, at) for block, at in zip(wq_moved[1:], planes[1:])]
     wq_others += [line.swap(block) for block in wq_last[:1]]
-    kv_all = everywhere(kv_own.astype(BF16)).reshape(images, 2 * local_cols)
-    kv_all, live_here, wo_pair, live_flat, *moved = gate(
-        (kv_all, live_here, wo_pair, live_flat, *wo_moved, *wo_two, *wq_others, *wq_last)
-    )
-    wo_moved, moved = moved[:n_moved], moved[n_moved:]
-    wo_two, moved = moved[: len(wo_two)], moved[len(wo_two) :]
-    wq_others, wq_last = moved[: len(wq_others)], moved[len(wq_others) :]
+    kv_all = everywhere(kv_own).reshape(images, 2 * local_cols)
+    kv_all, live_here, wo_pair, live_flat, *staged = gate(
+        (kv_all, live_here, wo_pair, live_flat, *wo_two, *wq_last, *wq_others)
+    )
+    wo_two, staged = staged[: len(wo_two)], staged[len(wo_two) :]
+    wq_last, wq_others = staged[: len(wq_last)], staged[len(wq_last) :]
 
     wo_last = line.third(wo_two)
     wq_others += [line.swap(block, (0, 3)) for block in wq_last[1:]]
@@ -333,7 +332,8 @@
     ).reshape(quarter_rows, n_dp, own_width)
     live_mine = lax.all_to_all(live_part, "dp", split_axis=1, concat_axis=0)
     live_mine = live_mine.reshape(n_dp, quarter_rows, own_width)
-    wq_blocks = [query_weight, *wq_moved, *wq_last, wq_swapped, *wq_others]
+    live_mine, live_flat = gate((live_mine, live_flat))
+    wq_blocks = [query_weight, *wq_moved, *wq_last, *wq_others]
 
     grad_keep, grad_send = call(
         functools.partial(grad_kernel, line),
@@ -343,8 +343,8 @@
         [pltpu.VMEM((rows, half_cols), F32)] * 2,
         2 * rows * width * local_cols,
     )
+    text_flat, grad_keep, grad_send = gate((text_flat, grad_keep, grad_send))
     grad_come = line.swap(grad_send)
-    text_flat, live_mine, _ = gate((text_flat, live_mine, grad_send))
     queries, attended = call(
         functools.partial(forward_kernel, line, relayed, image_own),
         place,
@@ -356,7 +356,8 @@
 
     att_next = [line.shift(attended, m) for m in (1, line.n_z - 1)]
     att_swapped = line.swap(attended)
-    live_pair = jnp.stack([live_mine, tensor_swap(live_mine, 2)])
+    live_y = tensor_swap(live_mine, 2)
+
     query_grad, kv_part = call(
         functools.partial(backward_kernel, image_own),
         place,
@@ -365,6 +366,8 @@
         (),
         10 * images * rows * local_cols,
     )
+    kv_part = kv_part.reshape(n_dp, image_rows, 2 * local_cols)
+    kv_grad = jnp.sum(lax.all_to_all(kv_part, "dp", split_axis=0, concat_axis=0), axis=0)
     chunk = n_dp // n_tensor
     term = call(
         functools.partial(term_kernel, line, relayed),
@@ -374,29 +377,28 @@
         (),
         2 * rows * width * local_cols,
     )
-    kv_part = kv_part.reshape(n_dp, image_rows, 2 * local_cols)
-    kv_grad = jnp.sum(lax.all_to_all(kv_part, "dp", split_axis=0, concat_axis=0), axis=0)
-    kv_grad, term, attended, live_pair, att_swapped, *att_next = gate(
-        (kv_grad.astype(BF16), term, attended, live_pair, att_swapped, *att_next)
-    )
+    kv_grad, term, attended, live_y, att_swapped, *att_next = gate(
+        (kv_grad.astype(BF16), term, attended, live_y, att_swapped, *att_next)
+    )
+    att_far = [line.shift(attended, m) for m in range(2, line.n_z - 1)]
+    att_other_next = [line.swap(block) for block in att_next]
 
     text_parts = [term[0]]
     for k in range(n_tensor - 1, 1, -1):
         text_parts.append(tensor_swap(term[k], k))
-    att_far = [line.shift(attended, m) for m in range(2, line.n_z - 1)]
-    att_other_next = [line.swap(block) for block in att_next]
+    live_pair = jnp.stack([live_mine, live_y])
     kv_grad_all = everywhere(kv_grad).reshape(images, 2 * local_cols)
     kv_grad_all, term_core, live_pair, *third = gate(
         (kv_grad_all, term[1], live_pair, *att_other_next, *att_far)
     )
     att_other_next, att_far = third[:2], third[2:]
 
+    att_other_far = [line.swap(block) for block in att_far]
+    live_core = tensor_swap(live_pair, 1)
     text_parts.append(tensor_swap(term_core, 1))
-    live_core = tensor_swap(live_pair, 1)
-    att_other_far = [line.swap(block) for block in att_far]
     image_term = matmul(kv_grad_all[:, :local_cols], key_weight, BACK)
     image_term = image_term + matmul(kv_grad_all[:, local_cols:], value_weight, BACK)
-    image_grad = to_owner(line, image_term.astype(BF16))
+    image_grad, *att_other_far = to_owner(line, image_term.astype(BF16), *att_other_far)
     image_grad = image_grad.reshape(samples, image_own, width // n_tensor)
     text_grad = functools.reduce(jnp.add, [part.astype(F32) for part in text_parts])
     text_grad = text_grad.astype(BF16).transpose(1, 0, 2)

time: 350 us -> 319 us (0.911)
  waiting for transfers between devices: 174 us -> 144 us
    all_to_all x1, waiting for transfers between devices: 36.9 us -> 0.01 us  [shards(): lax.all_to_all(part_kv, 'dp', split_axis=0, concat_axis=0)]
    all_to_all x1, waiting for transfers between devices: 37.9 us -> 3.9 us  [shards(): lax.all_to_all(image_flat, 'dp', split_axis=1, concat_axis=0, tiled=True)]
    ppermute x12, waiting for transfers between devices: 13 us -> 37.9 us  [swap(): return lax.ppermute(block, 'dp', pairs)]
    all_to_all x1, waiting for transfers between devices: 0.01 us -> 14.6 us  [shards(): live_mine = lax.all_to_all(live_part, 'dp', split_axis=1, concat_axis=0)]
    ppermute x13, waiting for transfers between devices: 28 us -> 37.2 us  [move(): return lax.ppermute(block, 'dp', pairs)]
    ppermute x2, waiting for transfers between devices: 7.56 us -> 0.01 us  [to_owner(): come.append(lax.ppermute(block, ('dp', 'tensor'), pairs))]
    unnamed x31 -> x29, local copies, waits for them, and re-layouts: 7.25 us -> 7.36 us
  transfers between devices with their start and end apart: 40 -> 40, of which waited for: 12 -> 13; matrix products, arithmetic and copies ran while one was open for 9% -> 10% of each run, Pallas kernels for 7% -> 7%
where the time goes in v6:
time: 319 us; the launch traced here: 318 us
  waiting for transfers between devices  144 us (45%)
  starting transfers between devices  98.7 us (31%)
  Pallas kernels  30 us (9%)
  local copies, waits for them, and re-layouts  23.2 us (7%)
  other arithmetic  16.4 us (5%)
  matrix products  4.57 us (1%)
    all_to_all x2, waiting for transfers between devices, everywhere(): return lax.all_to_all(copies, 'dp', split_axis=0, concat_axis=0)  47.7 us
    ppermute x12, waiting for transfers between devices, swap(): return lax.ppermute(block, 'dp', pairs)  37.9 us
    ppermute x13, waiting for transfers between devices, move(): return lax.ppermute(block, 'dp', pairs)  37.2 us
    pallas_call x5, Pallas kernels, call(): pl.pallas_call(kernel, out_shape=outs[0] if single else outs, in_specs=[p...  30 us
    ppermute x13, starting transfers between devices, move(): return lax.ppermute(block, 'dp', pairs)  27.5 us
    ppermute x12, starting transfers between devices, swap(): return lax.ppermute(block, 'dp', pairs)  18.7 us
    all_to_all x2, starting transfers between devices, everywhere(): return lax.all_to_all(copies, 'dp', split_axis=0, concat_axis=0)  17.1 us
    all_to_all x1, waiting for transfers between devices, shards(): live_mine = lax.all_to_all(live_part, 'dp', split_axis=1, concat_axis=0)  14.6 us
  transfers between devices with their start and end apart: 40, of which 13 were waited for; matrix products, arithmetic and copies ran while one was open for 10% of the time, Pallas kernels for 7%

profile of v6, /device:TPU:4, one launch (start us, length us, event | category | flops | bytes accessed | tf_op | source)
XLA Modules:
  0.0 317.6 jit_solution(3454493518038426429)
XLA Ops:
  2.3 5.8 %all-to-all-start = ((bf16[8,8,512]{2,0,1:T(8,128)(2,1)}), bf16[8,8,512]{2,0,1:T(8,128)(2,1)S(1)}, u32[]{:S(2)}, u32[]{:S(2)}) async-start(bf16[8,8,512]{2,0,1:T(8,128)(2,1)} %copy.16), calls=%async_computation | async-start | bytes 131072 | tf_op jit(solution)/shard_map/all_to_all | solution.py:281
  8.9 2.3 constant_dynamic-slice_fusion.1
  11.1 3.9 %all-to-all-done = bf16[8,8,512]{2,0,1:T(8,128)(2,1)S(1)} async-done(((bf16[8,8,512]{2,0,1:T(8,128)(2,1)}), bf16[8,8,512]{2,0,1:T(8,128)(2,1)S(1)}, u32[]{:S(2)}, u32[]{:S(2)}) %all-to-all-start) | async-done | bytes 65568 | tf_op jit(solution)/shard_map/all_to_all | solution.py:281
  16.7 5.5 %collective-permute-start.3 = (bf16[512,1024]{1,0:T(8,128)(2,1)S(1)}, bf16[512,1024]{1,0:T(8,128)(2,1)}, u32[]{:S(2)}, u32[]{:S(2)}) collective-permute-start(bf16[512,1024]{1,0:T(8,128)(2,1)S(1)} %copy-done.1), channel_id=1, source_target_pairs={{0,8},{4,12},{8,16},{12,20},{16,24},{20,28},{1,9},{5,13},{9,17},{1... | collective-permute-start | bytes 3145736 | tf_op jit(solution)/shard_map/ppermute | solution.py:31
  22.3 1.6 collective-permute-start
  26.6 4.2 %all-to-all-start.1 = ((f32[8,8,2048]{2,1,0:T(8,128)}), f32[8,8,2048]{2,1,0:T(8,128)}, u32[]{:S(2)}, u32[]{:S(2)}) async-start(f32[8,8,2048]{2,1,0:T(8,128)} %maximum_bitcast_fusion), calls=%async_computation.1 | async-start | bytes 1048576 | tf_op jit(solution)/shard_map/all_to_all | solution.py:294
  30.7 3.1 broadcast_select_fusion
  33.9 2.4 constant_dynamic-slice_fusion.2
  36.2 18.5 %collective-permute-done = bf16[512,512]{1,0:T(8,128)(2,1)} collective-permute-done((bf16[512,512]{1,0:T(8,128)(2,1)}, bf16[512,512]{1,0:T(8,128)(2,1)}, u32[]{:S(2)}, u32[]{:S(2)}) %collective-permute-start) | collective-permute-done | bytes 524320 | tf_op jit(solution)/shard_map/ppermute | solution.py:36
  54.8 2.1 pad_maximum_fusion.refs_0_
  59.7 5.5 %collective-permute-start.9 = (bf16[512,1024]{1,0:T(8,128)(2,1)}, bf16[512,1024]{1,0:T(8,128)(2,1)}, u32[]{:S(2)}, u32[]{:S(2)}) collective-permute-start(bf16[512,1024]{1,0:T(8,128)(2,1)} %pad_maximum_fusion.refs_0_), channel_id=1, source_target_pairs={{0,8},{4,12},{8,16},{12,20},{16,24},{20,28},{1,9},{5,13},{9,17},{1... | collective-permute-start | bytes 3145736 | tf_op jit(solution)/shard_map/ppermute | solution.py:31
  66.6 1.7 collective-permute-start.7
  68.2 12.0 %collective-permute-done.4.here = bf16[256,2048]{1,0:T(8,128)(2,1)} collective-permute-done((bf16[256,2048]{1,0:T(8,128)(2,1)}, bf16[256,2048]{1,0:T(8,128)(2,1)}, u32[]{:S(2)}, u32[]{:S(2)}) %collective-permute-start.4) | collective-permute-done | bytes 1048608 | tf_op jit(solution)/shard_map/ppermute | solution.py:36
  80.2 2.2 collective-permute-start.5
  83.4 21.2 %collective-permute-done.6 = bf16[512,1024]{1,0:T(8,128)(2,1)} collective-permute-done((bf16[512,1024]{1,0:T(8,128)(2,1)S(1)}, bf16[512,1024]{1,0:T(8,128)(2,1)}, u32[]{:S(2)}, u32[]{:S(2)}) %collective-permute-start.6) | collective-permute-done | bytes 1048608 | tf_op jit(solution)/shard_map/ppermute | solution.py:31
  107.3 1.8 collective-permute-start.14
  110.3 1.7 collective-permute-start.11
  112.0 1.7 collective-permute-start.13
  114.5 12.3 %all-to-all-start.2 = ((bf16[8,8,2048]{2,1,0:T(8,128)(2,1)}), bf16[8,8,2048]{2,1,0:T(8,128)(2,1)S(1)}, u32[]{:S(2)}, u32[]{:S(2)}) async-start(bf16[8,8,2048]{2,1,0:T(8,128)(2,1)} %broadcast_in_dim.16), calls=%async_computation.2 | async-start | bytes 524288 | tf_op jit(solution)/shard_map/all_to_all | solution.py:313
  126.8 29.6 %all-to-all-done.2 = bf16[8,8,2048]{2,1,0:T(8,128)(2,1)S(1)} async-done(((bf16[8,8,2048]{2,1,0:T(8,128)(2,1)}), bf16[8,8,2048]{2,1,0:T(8,128)(2,1)S(1)}, u32[]{:S(2)}, u32[]{:S(2)}) %all-to-all-start.2) | async-done | bytes 262176 | tf_op jit(solution)/shard_map/all_to_all | solution.py:313
  156.4 2.3 broadcast_select_fusion.1.refs_3_
  162.3 7.8 %all-to-all-start.3 = ((bf16[1,64,8,512]{3,1,0,2:T(8,128)(2,1)}), bf16[1,64,8,512]{3,1,0,2:T(8,128)(2,1)}, u32[]{:S(2)}, u32[]{:S(2)}) async-start(bf16[1,64,8,512]{3,1,0,2:T(8,128)(2,1)} %copy.17), calls=%async_computation.3 | async-start | bytes 1048576 | tf_op jit(solution)/shard_map/all_to_all | solution.py:333
  170.1 3.9 %collective-permute-start.17 = (bf16[512,1024]{1,0:T(8,128)(2,1)}, bf16[512,1024]{1,0:T(8,128)(2,1)}, u32[]{:S(2)}, u32[]{:S(2)}) collective-permute-start(bf16[512,1024]{1,0:T(8,128)(2,1)} %collective-permute-done.12.refs_4_), channel_id=1, source_target_pairs={{0,4},{4,0},{24,28},{28,24},{1,5},{5,1},{25,29},{29,25},{2,6},{6,2... | collective-permute-start | bytes 3145736 | tf_op jit(solution)/shard_map/ppermute | solution.py:36
  174.1 14.6 %all-to-all-done.3 = bf16[1,64,8,512]{3,1,0,2:T(8,128)(2,1)} async-done(((bf16[1,64,8,512]{3,1,0,2:T(8,128)(2,1)}), bf16[1,64,8,512]{3,1,0,2:T(8,128)(2,1)}, u32[]{:S(2)}, u32[]{:S(2)}) %all-to-all-start.3) | async-done | bytes 524320 | tf_op jit(solution)/shard_map/all_to_all | solution.py:333
  190.1 6.9 %shard_map.103 = (bf16[256,512]{1,0:T(8,128)(2,1)S(1)}, bf16[256,512]{1,0:T(8,128)(2,1)S(1)}) custom-call(s32[4]{0:T(128)S(1)} %pad_add_fusion.place, bf16[256,4096]{1,0:T(8,128)(2,1)} %bitcast.47, bf16[256,2048]{1,0:T(8,128)(2,1)} %collective-permute-done.4.here, bf16[256,2048]{1,0:T(8,128)(2,1)} %collective-permute-done.15.there, ...), custom_call_target="tpu_custom_call" | custom-call | flops 2147483648 | bytes 9961472 | tf_op jit(solution)/shard_map/pallas_call | solution.py:197
  197.9 4.0 %collective-permute-done.17.refs_9_ = bf16[512,1024]{1,0:T(8,128)(2,1)} collective-permute-done((bf16[512,1024]{1,0:T(8,128)(2,1)}, bf16[512,1024]{1,0:T(8,128)(2,1)}, u32[]{:S(2)}, u32[]{:S(2)}) %collective-permute-start.17) | collective-permute-done | bytes 1048608 | tf_op jit(solution)/shard_map/ppermute | solution.py:36
  201.9 8.0 %shard_map.104 = (bf16[256,1024]{1,0:T(8,128)(2,1)S(1)}, bf16[256,1024]{1,0:T(8,128)(2,1)S(1)}) custom-call(s32[4]{0:T(128)S(1)} %pad_add_fusion.place, bf16[256,4096]{1,0:T(8,128)(2,1)} %bitcast.48, bf16[64,2048]{1,0:T(8,128)(2,1)S(1)} %bitcast.42, bf16[512,1024]{1,0:T(8,128)(2,1)S(1)} %copy-done.1, bf16[512,1024]{1,0:T(8,128)(2,1)S(1)} %copy-done.3, ...), custom_call_target="tpu_custom_call" | custom-call | flops 2147483648 | bytes 13893632 | tf_op jit(solution)/shard_map/pallas_call | solution.py:197
  210.0 1.9 shard_map.105
  213.5 5.2 %all-to-all-start.4 = ((f32[8,8,2048]{2,1,0:T(8,128)}), f32[8,8,2048]{2,1,0:T(8,128)}, u32[]{:S(2)}, u32[]{:S(2)}) async-start(f32[8,8,2048]{2,1,0:T(8,128)} %bitcast.44), calls=%async_computation.4 | async-start | bytes 1048576 | tf_op jit(solution)/shard_map/all_to_all | solution.py:370
  219.2 2.0 collective-permute-start.20
  221.2 3.3 %collective-permute-start.21 = (bf16[256,1024]{1,0:T(8,128)(2,1)}, bf16[256,1024]{1,0:T(8,128)(2,1)}, u32[]{:S(2)}, u32[]{:S(2)}) collective-permute-start(bf16[256,1024]{1,0:T(8,128)(2,1)} %copy-done.9), channel_id=1, source_target_pairs={{8,0},{12,4},{16,8},{20,12},{24,16},{28,20},{0,24},{4,28},{9,1},{1... | collective-permute-start | bytes 1572872 | tf_op jit(solution)/shard_map/ppermute | solution.py:31
  226.8 7.8 %shard_map.106 = bf16[4,2,256,512]{3,2,1,0:T(8,128)(2,1)} custom-call(s32[4]{0:T(128)S(1)} %pad_add_fusion.place, bf16[256,1024]{1,0:T(8,128)(2,1)S(1)} %copy-done.7, bf16[512,1024]{1,0:T(8,128)(2,1)S(1)} %copy-done.1, bf16[512,1024]{1,0:T(8,128)(2,1)S(1)} %copy-done.4, bf16[512,1024]{1,0:T(8,128)(2,1)} %collective-permute-done.3.refs_2_, ...), custom_call_target="tpu_custom_call" | custom-call | flops 2147483648 | bytes 13107200 | tf_op jit(solution)/shard_map/pallas_call | solution.py:197
  237.2 3.9 %collective-permute-done.21.refs_3_ = bf16[256,1024]{1,0:T(8,128)(2,1)} collective-permute-done((bf16[256,1024]{1,0:T(8,128)(2,1)}, bf16[256,1024]{1,0:T(8,128)(2,1)}, u32[]{:S(2)}, u32[]{:S(2)}) %collective-permute-start.21) | collective-permute-done | bytes 524320 | tf_op jit(solution)/shard_map/ppermute | solution.py:31
  241.1 12.0 %collective-permute-done.22.refs_5_ = bf16[256,1024]{1,0:T(8,128)(2,1)} collective-permute-done((bf16[256,1024]{1,0:T(8,128)(2,1)}, bf16[256,1024]{1,0:T(8,128)(2,1)}, u32[]{:S(2)}, u32[]{:S(2)}) %collective-permute-start.22) | collective-permute-done | bytes 524320 | tf_op jit(solution)/shard_map/ppermute | solution.py:31
  255.2 2.1 collective-permute-start.27
  258.0 4.8 %all-to-all-start.5 = ((bf16[8,8,2048]{2,1,0:T(8,128)(2,1)}), bf16[8,8,2048]{2,1,0:T(8,128)(2,1)S(1)}, u32[]{:S(2)}, u32[]{:S(2)}) async-start(bf16[8,8,2048]{2,1,0:T(8,128)(2,1)} %broadcast_in_dim.17), calls=%async_computation.5 | async-start | bytes 524288 | tf_op jit(solution)/shard_map/all_to_all | solution.py:313
  262.8 2.5 slice_bitcast_fusion.2
  267.2 18.1 %all-to-all-done.5 = bf16[8,8,2048]{2,1,0:T(8,128)(2,1)S(1)} async-done(((bf16[8,8,2048]{2,1,0:T(8,128)(2,1)}), bf16[8,8,2048]{2,1,0:T(8,128)(2,1)S(1)}, u32[]{:S(2)}, u32[]{:S(2)}) %all-to-all-start.5) | async-done | bytes 262176 | tf_op jit(solution)/shard_map/all_to_all | solution.py:313
  285.3 1.7 collective-permute-start.29
  288.0 2.3 fusion
  290.3 3.8 %all-to-all-start.6 = ((bf16[4,16,512]{2,1,0:T(8,128)(2,1)}), bf16[4,16,512]{2,1,0:T(8,128)(2,1)S(1)}, u32[]{:S(2)}, u32[]{:S(2)}) async-start(bf16[4,16,512]{2,1,0:T(8,128)(2,1)} %bitcast.22), calls=%async_computation.6 | async-start | bytes 131072 | tf_op jit(solution)/shard_map/all_to_all | solution.py:219
  294.1 2.3 all-to-all-done.6
  296.3 1.8 collective-permute-done.29.refs_8_
  298.2 1.9 collective-permute-start.30
  300.1 5.1 %collective-permute-start.31 = (bf16[8,512]{1,0:T(8,128)(2,1)S(1)}, bf16[8,512]{1,0:T(8,128)(2,1)S(1)}, u32[]{:S(2)}, u32[]{:S(2)}) collective-permute-start(bf16[8,512]{1,0:T(8,128)(2,1)S(1)} %get-tuple-element.127), channel_id=1, source_target_pairs={{0,4},{1,12},{2,20},{3,28},{4,0},{5,8},{6,16},{7,24},{8,5},{9,13},... | collective-permute-start | bytes 24584 | tf_op jit(solution)/shard_map/ppermute | solution.py:235
  305.2 1.8 fusion.4
  308.3 2.2 reshape.88
  312.2 5.4 %shard_map.107 = bf16[1024,512]{1,0:T(8,128)(2,1)} custom-call(s32[4]{0:T(128)S(1)} %pad_add_fusion.place, bf16[2,8,64,512]{3,2,1,0:T(8,128)(2,1)S(1)} %pad_maximum_fusion.1.refs_0_, bf16[2,8,64,512]{3,2,1,0:T(8,128)(2,1)} %collective-permute-done.32.refs_1_, bf16[256,1024]{1,0:T(8,128)(2,1)S(1)} %copy-done.10, ...), custom_call_target="tpu_custom_call" | custom-call | flops 2147483648 | bytes 7340032 | tf_op jit(solution)/shard_map/pallas_call | solution.py:197
  (98 shorter events, 37.9 us)
Async XLA Ops:
  0.6 24.8 %copy-start = (bf16[512,1024]{1,0:T(8,128)(2,1)S(1)}, bf16[512,1024]{1,0:T(8,128)(2,1)}, u32[]{:S(2)}) copy-start(bf16[512,1024]{1,0:T(8,128)(2,1)} %param.14) | copy-start | bytes 3145732
  0.6 14.4 %copy-start.1 = (bf16[512,1024]{1,0:T(8,128)(2,1)S(1)}, bf16[512,1024]{1,0:T(8,128)(2,1)}, u32[]{:S(2)}) copy-start(bf16[512,1024]{1,0:T(8,128)(2,1)} %refs_0_.1) | copy-start | bytes 3145732
  2.3 12.7 %all-to-all-start = ((bf16[8,8,512]{2,0,1:T(8,128)(2,1)}), bf16[8,8,512]{2,0,1:T(8,128)(2,1)S(1)}, u32[]{:S(2)}, u32[]{:S(2)}) async-start(bf16[8,8,512]{2,0,1:T(8,128)(2,1)} %copy.16), calls=%async_computation | async-start | bytes 131072 | tf_op jit(solution)/shard_map/all_to_all | solution.py:281
  15.0 42.9 %collective-permute-start.1 = (bf16[512,1024]{1,0:T(8,128)(2,1)S(1)}, bf16[512,1024]{1,0:T(8,128)(2,1)}, u32[]{:S(2)}, u32[]{:S(2)}) collective-permute-start(bf16[512,1024]{1,0:T(8,128)(2,1)S(1)} %copy-done.1), channel_id=1, source_target_pairs={{0,4},{4,0},{8,12},{12,8},{16,20},{20,16},{24,28},{28,24},{1,5},{5... | collective-permute-start | bytes 3145736 | tf_op jit(solution)/shard_map/ppermute | solution.py:36
  15.4 42.5 %collective-permute-start.2 = (bf16[512,1024]{1,0:T(8,128)(2,1)S(1)}, bf16[512,1024]{1,0:T(8,128)(2,1)S(1)}, u32[]{:S(2)}, u32[]{:S(2)}) collective-permute-start(bf16[512,1024]{1,0:T(8,128)(2,1)S(1)} %copy-done.1), channel_id=1, source_target_pairs={{8,0},{12,4},{16,8},{20,12},{24,16},{28,20},{9,1},{13,5},{17,9},{2... | collective-permute-start | bytes 3145736 | tf_op jit(solution)/shard_map/ppermute | solution.py:31
  16.7 41.3 %collective-permute-start.3 = (bf16[512,1024]{1,0:T(8,128)(2,1)S(1)}, bf16[512,1024]{1,0:T(8,128)(2,1)}, u32[]{:S(2)}, u32[]{:S(2)}) collective-permute-start(bf16[512,1024]{1,0:T(8,128)(2,1)S(1)} %copy-done.1), channel_id=1, source_target_pairs={{0,8},{4,12},{8,16},{12,20},{16,24},{20,28},{1,9},{5,13},{9,17},{1... | collective-permute-start | bytes 3145736 | tf_op jit(solution)/shard_map/ppermute | solution.py:31
  22.3 32.5 %collective-permute-start = (bf16[512,512]{1,0:T(8,128)(2,1)}, bf16[512,512]{1,0:T(8,128)(2,1)}, u32[]{:S(2)}, u32[]{:S(2)}) collective-permute-start(bf16[512,512]{1,0:T(8,128)(2,1)} %get-tuple-element.63), channel_id=1, source_target_pairs={{0,4},{4,0},{8,12},{12,8},{16,20},{20,16},{24,28},{28,24},{1,5},{5... | collective-permute-start | bytes 1572872 | tf_op jit(solution)/shard_map/ppermute | solution.py:36
  26.6 30.3 %all-to-all-start.1 = ((f32[8,8,2048]{2,1,0:T(8,128)}), f32[8,8,2048]{2,1,0:T(8,128)}, u32[]{:S(2)}, u32[]{:S(2)}) async-start(f32[8,8,2048]{2,1,0:T(8,128)} %maximum_bitcast_fusion), calls=%async_computation.1 | async-start | bytes 1048576 | tf_op jit(solution)/shard_map/all_to_all | solution.py:294
  33.9 20.9 %copy-start.13 = (bf16[512,512]{1,0:T(8,128)(2,1)S(1)}, bf16[512,512]{1,0:T(8,128)(2,1)}, u32[]{:S(2)}) copy-start(bf16[512,512]{1,0:T(8,128)(2,1)} %get-tuple-element.124) | copy-start | bytes 1572868
  58.0 22.2 %collective-permute-start.4 = (bf16[256,2048]{1,0:T(8,128)(2,1)}, bf16[256,2048]{1,0:T(8,128)(2,1)}, u32[]{:S(2)}, u32[]{:S(2)}) collective-permute-start(bf16[256,2048]{1,0:T(8,128)(2,1)} %constant_dynamic-slice_fusion.2), channel_id=1, source_target_pairs={{0,4},{4,0},{8,12},{12,8},{16,20},{20,16},{24,28},{28,24},{1,5},{5... | collective-permute-start | bytes 3145736 | tf_op jit(solution)/shard_map/ppermute | solution.py:36
  58.5 46.2 %collective-permute-start.8 = (bf16[512,1024]{1,0:T(8,128)(2,1)}, bf16[512,1024]{1,0:T(8,128)(2,1)}, u32[]{:S(2)}, u32[]{:S(2)}) collective-permute-start(bf16[512,1024]{1,0:T(8,128)(2,1)} %pad_maximum_fusion.refs_0_), channel_id=1, source_target_pairs={{8,0},{12,4},{16,8},{20,12},{24,16},{28,20},{9,1},{13,5},{17,9},{2... | collective-permute-start | bytes 3145736 | tf_op jit(solution)/shard_map/ppermute | solution.py:31
  59.7 44.9 %collective-permute-start.9 = (bf16[512,1024]{1,0:T(8,128)(2,1)}, bf16[512,1024]{1,0:T(8,128)(2,1)}, u32[]{:S(2)}, u32[]{:S(2)}) collective-permute-start(bf16[512,1024]{1,0:T(8,128)(2,1)} %pad_maximum_fusion.refs_0_), channel_id=1, source_target_pairs={{0,8},{4,12},{8,16},{12,20},{16,24},{20,28},{1,9},{5,13},{9,17},{1... | collective-permute-start | bytes 3145736 | tf_op jit(solution)/shard_map/ppermute | solution.py:31
  65.3 39.3 %collective-permute-start.6 = (bf16[512,1024]{1,0:T(8,128)(2,1)S(1)}, bf16[512,1024]{1,0:T(8,128)(2,1)}, u32[]{:S(2)}, u32[]{:S(2)}) collective-permute-start(bf16[512,1024]{1,0:T(8,128)(2,1)S(1)} %collective-permute-done.2.refs_1_), channel_id=1, source_target_pairs={{8,0},{12,4},{16,8},{20,12},{9,1},{13,5},{17,9},{21,13},{10,2},{14... | collective-permute-start | bytes 3145736 | tf_op jit(solution)/shard_map/ppermute | solution.py:31
  66.6 38.0 %collective-permute-start.7 = (bf16[512,1024]{1,0:T(8,128)(2,1)}, bf16[512,1024]{1,0:T(8,128)(2,1)}, u32[]{:S(2)}, u32[]{:S(2)}) collective-permute-start(bf16[512,1024]{1,0:T(8,128)(2,1)} %collective-permute-done.3.refs_2_), channel_id=1, source_target_pairs={{8,16},{12,20},{16,24},{20,28},{9,17},{13,21},{17,25},{21,29},{10,... | collective-permute-start | bytes 3145736 | tf_op jit(solution)/shard_map/ppermute | solution.py:31
  80.2 24.4 %collective-permute-start.5 = (bf16[512,1024]{1,0:T(8,128)(2,1)S(1)}, bf16[512,1024]{1,0:T(8,128)(2,1)}, u32[]{:S(2)}, u32[]{:S(2)}) collective-permute-start(bf16[512,1024]{1,0:T(8,128)(2,1)S(1)} %collective-permute-done.2.refs_1_), channel_id=1, source_target_pairs={{0,4},{4,0},{8,12},{12,8},{16,20},{20,16},{1,5},{5,1},{9,13},{13,9... | collective-permute-start | bytes 3145736 | tf_op jit(solution)/shard_map/ppermute | solution.py:36
  106.0 50.4 %collective-permute-start.12 = (bf16[512,1024]{1,0:T(8,128)(2,1)S(1)}, bf16[512,1024]{1,0:T(8,128)(2,1)}, u32[]{:S(2)}, u32[]{:S(2)}) collective-permute-start(bf16[512,1024]{1,0:T(8,128)(2,1)S(1)} %broadcast_select_fusion.2.refs_3_), channel_id=1, source_target_pairs={{8,0},{12,4},{16,24},{20,28},{9,1},{13,5},{17,25},{21,29},{10,2},{... | collective-permute-start | bytes 3145736 | tf_op jit(solution)/shard_map/ppermute | solution.py:31
  107.3 49.1 %collective-permute-start.14 = (bf16[512,1024]{1,0:T(8,128)(2,1)S(1)}, bf16[512,1024]{1,0:T(8,128)(2,1)}, u32[]{:S(2)}, u32[]{:S(2)}) collective-permute-start(bf16[512,1024]{1,0:T(8,128)(2,1)S(1)} %broadcast_select_fusion.2.refs_3_), channel_id=1, source_target_pairs={{0,4},{4,0},{8,12},{12,8},{16,20},{20,16},{24,28},{28,24},{1,5},{5... | collective-permute-start | bytes 3145736 | tf_op jit(solution)/shard_map/ppermute | solution.py:36
  109.1 47.3 %collective-permute-start.10 = (bf16[512,1024]{1,0:T(8,128)(2,1)}, bf16[512,1024]{1,0:T(8,128)(2,1)}, u32[]{:S(2)}, u32[]{:S(2)}) collective-permute-start(bf16[512,1024]{1,0:T(8,128)(2,1)} %collective-permute-done.8.refs_1_), channel_id=1, source_target_pairs={{8,0},{12,4},{16,8},{20,12},{9,1},{13,5},{17,9},{21,13},{10,2},{14... | collective-permute-start | bytes 3145736 | tf_op jit(solution)/shard_map/ppermute | solution.py:31
  110.3 46.0 %collective-permute-start.11 = (bf16[512,1024]{1,0:T(8,128)(2,1)}, bf16[512,1024]{1,0:T(8,128)(2,1)}, u32[]{:S(2)}, u32[]{:S(2)}) collective-permute-start(bf16[512,1024]{1,0:T(8,128)(2,1)} %collective-permute-done.9.refs_2_), channel_id=1, source_target_pairs={{8,16},{12,20},{16,24},{20,28},{9,17},{13,21},{17,25},{21,29},{10,... | collective-permute-start | bytes 3145736 | tf_op jit(solution)/shard_map/ppermute | solution.py:31
  112.0 44.3 %collective-permute-start.13 = (bf16[512,1024]{1,0:T(8,128)(2,1)}, bf16[512,1024]{1,0:T(8,128)(2,1)}, u32[]{:S(2)}, u32[]{:S(2)}) collective-permute-start(bf16[512,1024]{1,0:T(8,128)(2,1)} %collective-permute-done.3.refs_2_), channel_id=1, source_target_pairs={{8,12},{12,8},{16,20},{20,16},{24,28},{28,24},{9,13},{13,9},{17,21... | collective-permute-start | bytes 3145736 | tf_op jit(solution)/shard_map/ppermute | solution.py:36
  114.5 41.9 %all-to-all-start.2 = ((bf16[8,8,2048]{2,1,0:T(8,128)(2,1)}), bf16[8,8,2048]{2,1,0:T(8,128)(2,1)S(1)}, u32[]{:S(2)}, u32[]{:S(2)}) async-start(bf16[8,8,2048]{2,1,0:T(8,128)(2,1)} %broadcast_in_dim.16), calls=%async_computation.2 | async-start | bytes 524288 | tf_op jit(solution)/shard_map/all_to_all | solution.py:313
  158.7 30.1 %collective-permute-start.16 = (bf16[512,1024]{1,0:T(8,128)(2,1)}, bf16[512,1024]{1,0:T(8,128)(2,1)}, u32[]{:S(2)}, u32[]{:S(2)}) collective-permute-start(bf16[512,1024]{1,0:T(8,128)(2,1)} %broadcast_select_fusion.1.refs_3_), channel_id=1, source_target_pairs={{8,0},{12,4},{16,24},{20,28},{9,1},{13,5},{17,25},{21,29},{10,2},{... | collective-permute-start | bytes 3145736 | tf_op jit(solution)/shard_map/ppermute | solution.py:31
  160.0 28.8 %collective-permute-start.15 = (bf16[256,2048]{1,0:T(8,128)(2,1)}, bf16[256,2048]{1,0:T(8,128)(2,1)}, u32[]{:S(2)}, u32[]{:S(2)}) collective-permute-start(bf16[256,2048]{1,0:T(8,128)(2,1)} %collective-permute-done.4.here), channel_id=1, source_target_pairs={{0,1},{1,0},{2,3},{3,2},{4,5},{5,4},{6,7},{7,6},{8,9},{9,8},{10,11... | collective-permute-start | bytes 3145736 | tf_op jit(solution)/shard_map/ppermute | solution.py:269
  162.3 26.5 %all-to-all-start.3 = ((bf16[1,64,8,512]{3,1,0,2:T(8,128)(2,1)}), bf16[1,64,8,512]{3,1,0,2:T(8,128)(2,1)}, u32[]{:S(2)}, u32[]{:S(2)}) async-start(bf16[1,64,8,512]{3,1,0,2:T(8,128)(2,1)} %copy.17), calls=%async_computation.3 | async-start | bytes 1048576 | tf_op jit(solution)/shard_map/all_to_all | solution.py:333
  170.1 31.8 %collective-permute-start.17 = (bf16[512,1024]{1,0:T(8,128)(2,1)}, bf16[512,1024]{1,0:T(8,128)(2,1)}, u32[]{:S(2)}, u32[]{:S(2)}) collective-permute-start(bf16[512,1024]{1,0:T(8,128)(2,1)} %collective-permute-done.12.refs_4_), channel_id=1, source_target_pairs={{0,4},{4,0},{24,28},{28,24},{1,5},{5,1},{25,29},{29,25},{2,6},{6,2... | collective-permute-start | bytes 3145736 | tf_op jit(solution)/shard_map/ppermute | solution.py:36
  188.8 13.2 %copy-start.3 = (bf16[512,1024]{1,0:T(8,128)(2,1)S(1)}, bf16[512,1024]{1,0:T(8,128)(2,1)}, u32[]{:S(2)}) copy-start(bf16[512,1024]{1,0:T(8,128)(2,1)} %copy-done.2) | copy-start | bytes 3145732
  188.8 1.3 copy-start.5
  197.0 13.0 %collective-permute-start.18 = (bf16[256,512]{1,0:T(8,128)(2,1)S(1)}, bf16[256,512]{1,0:T(8,128)(2,1)S(1)}, u32[]{:S(2)}, u32[]{:S(2)}) collective-permute-start(bf16[256,512]{1,0:T(8,128)(2,1)S(1)} %get-tuple-element.101), channel_id=1, source_target_pairs={{0,4},{4,0},{8,12},{12,8},{16,20},{20,16},{24,28},{28,24},{1,5},{5... | collective-permute-start | bytes 786440 | tf_op jit(solution)/shard_map/ppermute | solution.py:36
  210.0 1.9 copy-start.9
  213.5 21.1 %all-to-all-start.4 = ((f32[8,8,2048]{2,1,0:T(8,128)}), f32[8,8,2048]{2,1,0:T(8,128)}, u32[]{:S(2)}, u32[]{:S(2)}) async-start(f32[8,8,2048]{2,1,0:T(8,128)} %bitcast.44), calls=%async_computation.4 | async-start | bytes 1048576 | tf_op jit(solution)/shard_map/all_to_all | solution.py:370
  218.7 17.0 %collective-permute-start.19 = (bf16[8,64,512]{2,1,0:T(8,128)(2,1)}, bf16[8,64,512]{2,1,0:T(8,128)(2,1)}, u32[]{:S(2)}, u32[]{:S(2)}) collective-permute-start(bf16[8,64,512]{2,1,0:T(8,128)(2,1)} %bitcast.12), channel_id=1, source_target_pairs={{0,2},{1,3},{2,0},{3,1},{4,6},{5,7},{6,4},{7,5},{8,10},{9,11},{10,... | collective-permute-start | bytes 1572872 | tf_op jit(solution)/shard_map/ppermute | solution.py:269
  219.2 17.9 %collective-permute-start.20 = (bf16[256,1024]{1,0:T(8,128)(2,1)}, bf16[256,1024]{1,0:T(8,128)(2,1)}, u32[]{:S(2)}, u32[]{:S(2)}) collective-permute-start(bf16[256,1024]{1,0:T(8,128)(2,1)} %copy-done.9), channel_id=1, source_target_pairs={{0,4},{4,0},{8,12},{12,8},{16,20},{20,16},{24,28},{28,24},{1,5},{5... | collective-permute-start | bytes 1572872 | tf_op jit(solution)/shard_map/ppermute | solution.py:36
  221.2 19.9 %collective-permute-start.21 = (bf16[256,1024]{1,0:T(8,128)(2,1)}, bf16[256,1024]{1,0:T(8,128)(2,1)}, u32[]{:S(2)}, u32[]{:S(2)}) collective-permute-start(bf16[256,1024]{1,0:T(8,128)(2,1)} %copy-done.9), channel_id=1, source_target_pairs={{8,0},{12,4},{16,8},{20,12},{24,16},{28,20},{0,24},{4,28},{9,1},{1... | collective-permute-start | bytes 1572872 | tf_op jit(solution)/shard_map/ppermute | solution.py:31
  224.5 28.6 %collective-permute-start.22 = (bf16[256,1024]{1,0:T(8,128)(2,1)}, bf16[256,1024]{1,0:T(8,128)(2,1)}, u32[]{:S(2)}, u32[]{:S(2)}) collective-permute-start(bf16[256,1024]{1,0:T(8,128)(2,1)} %copy-done.9), channel_id=1, source_target_pairs={{24,0},{28,4},{0,8},{4,12},{8,16},{12,20},{16,24},{20,28},{25,1},{... | collective-permute-start | bytes 1572872 | tf_op jit(solution)/shard_map/ppermute | solution.py:31
  253.1 32.1 %collective-permute-start.25 = (bf16[256,1024]{1,0:T(8,128)(2,1)}, bf16[256,1024]{1,0:T(8,128)(2,1)S(1)}, u32[]{:S(2)}, u32[]{:S(2)}) collective-permute-start(bf16[256,1024]{1,0:T(8,128)(2,1)} %collective-permute-done.21.refs_3_), channel_id=1, source_target_pairs={{0,4},{4,0},{8,12},{12,8},{16,20},{20,16},{24,28},{28,24},{1,5},{5... | collective-permute-start | bytes 1572872 | tf_op jit(solution)/shard_map/ppermute | solution.py:36
  254.6 30.7 %collective-permute-start.26 = (bf16[256,1024]{1,0:T(8,128)(2,1)}, bf16[256,1024]{1,0:T(8,128)(2,1)S(1)}, u32[]{:S(2)}, u32[]{:S(2)}) collective-permute-start(bf16[256,1024]{1,0:T(8,128)(2,1)} %collective-permute-done.22.refs_5_), channel_id=1, source_target_pairs={{0,4},{4,0},{8,12},{12,8},{16,20},{20,16},{24,28},{28,24},{1,5},{5... | collective-permute-start | bytes 1572872 | tf_op jit(solution)/shard_map/ppermute | solution.py:36
  255.2 30.1 %collective-permute-start.27 = (bf16[256,1024]{1,0:T(8,128)(2,1)}, bf16[256,1024]{1,0:T(8,128)(2,1)}, u32[]{:S(2)}, u32[]{:S(2)}) collective-permute-start(bf16[256,1024]{1,0:T(8,128)(2,1)} %copy-done.9), channel_id=1, source_target_pairs={{16,0},{20,4},{24,8},{28,12},{0,16},{4,20},{8,24},{12,28},{17,1},{... | collective-permute-start | bytes 1572872 | tf_op jit(solution)/shard_map/ppermute | solution.py:31
  258.0 27.3 %all-to-all-start.5 = ((bf16[8,8,2048]{2,1,0:T(8,128)(2,1)}), bf16[8,8,2048]{2,1,0:T(8,128)(2,1)S(1)}, u32[]{:S(2)}, u32[]{:S(2)}) async-start(bf16[8,8,2048]{2,1,0:T(8,128)(2,1)} %broadcast_in_dim.17), calls=%async_computation.5 | async-start | bytes 524288 | tf_op jit(solution)/shard_map/all_to_all | solution.py:313
  265.3 34.8 %collective-permute-start.23 = (bf16[2,256,512]{2,1,0:T(8,128)(2,1)}, bf16[2,256,512]{2,1,0:T(8,128)(2,1)}, u32[]{:S(2)}, u32[]{:S(2)}) collective-permute-start(bf16[2,256,512]{2,1,0:T(8,128)(2,1)} %get-tuple-element.121), channel_id=1, source_target_pairs={{0,3},{1,2},{2,1},{3,0},{4,7},{5,6},{6,5},{7,4},{8,11},{9,10},{10,... | collective-permute-start | bytes 1572872 | tf_op jit(solution)/shard_map/ppermute | solution.py:269
  265.3 39.8 %collective-permute-start.24 = (bf16[2,256,512]{2,1,0:T(8,128)(2,1)}, bf16[2,256,512]{2,1,0:T(8,128)(2,1)}, u32[]{:S(2)}, u32[]{:S(2)}) collective-permute-start(bf16[2,256,512]{2,1,0:T(8,128)(2,1)} %get-tuple-element.123), channel_id=1, source_target_pairs={{0,2},{1,3},{2,0},{3,1},{4,6},{5,7},{6,4},{7,5},{8,10},{9,11},{10,... | collective-permute-start | bytes 1572872 | tf_op jit(solution)/shard_map/ppermute | solution.py:269
  285.3 14.8 %copy-start.11 = (bf16[256,1024]{1,0:T(8,128)(2,1)}, bf16[256,1024]{1,0:T(8,128)(2,1)S(1)}, u32[]{:S(2)}) copy-start(bf16[256,1024]{1,0:T(8,128)(2,1)S(1)} %collective-permute-done.26.refs_9_) | copy-start | bytes 1572868
  285.3 12.9 %collective-permute-start.29 = (bf16[256,1024]{1,0:T(8,128)(2,1)}, bf16[256,1024]{1,0:T(8,128)(2,1)}, u32[]{:S(2)}, u32[]{:S(2)}) collective-permute-start(bf16[256,1024]{1,0:T(8,128)(2,1)} %collective-permute-done.27.refs_4_), channel_id=1, source_target_pairs={{0,4},{4,0},{8,12},{12,8},{16,20},{20,16},{24,28},{28,24},{1,5},{5... | collective-permute-start | bytes 1572872 | tf_op jit(solution)/shard_map/ppermute | solution.py:36
  287.0 24.2 %collective-permute-start.32 = (bf16[2,8,64,512]{3,2,1,0:T(8,128)(2,1)S(1)}, bf16[2,8,64,512]{3,2,1,0:T(8,128)(2,1)}, u32[]{:S(2)}, u32[]{:S(2)}) collective-permute-start(bf16[2,8,64,512]{3,2,1,0:T(8,128)(2,1)S(1)} %pad_maximum_fusion.1.refs_0_), channel_id=1, source_target_pairs={{0,1},{1,0},{2,3},{3,2},{4,5},{5,4},{6,7},{7,6},{8,9},{9,8},{10,11... | collective-permute-start | bytes 3145736 | tf_op jit(solution)/shard_map/ppermute | solution.py:269
  287.4 17.7 %collective-permute-start.28 = (bf16[2,256,512]{2,1,0:T(8,128)(2,1)}, bf16[2,256,512]{2,1,0:T(8,128)(2,1)}, u32[]{:S(2)}, u32[]{:S(2)}) collective-permute-start(bf16[2,256,512]{2,1,0:T(8,128)(2,1)} %get-tuple-element.112), channel_id=1, source_target_pairs={{0,1},{1,0},{2,3},{3,2},{4,5},{5,4},{6,7},{7,6},{8,9},{9,8},{10,11... | collective-permute-start | bytes 1572872 | tf_op jit(solution)/shard_map/ppermute | solution.py:269
  290.3 6.0 %all-to-all-start.6 = ((bf16[4,16,512]{2,1,0:T(8,128)(2,1)}), bf16[4,16,512]{2,1,0:T(8,128)(2,1)S(1)}, u32[]{:S(2)}, u32[]{:S(2)}) async-start(bf16[4,16,512]{2,1,0:T(8,128)(2,1)} %bitcast.22), calls=%async_computation.6 | async-start | bytes 131072 | tf_op jit(solution)/shard_map/all_to_all | solution.py:219
  298.2 12.3 %collective-permute-start.30 = (bf16[8,512]{1,0:T(8,128)(2,1)S(1)}, bf16[8,512]{1,0:T(8,128)(2,1)S(1)}, u32[]{:S(2)}, u32[]{:S(2)}) collective-permute-start(bf16[8,512]{1,0:T(8,128)(2,1)S(1)} %get-tuple-element.126), channel_id=1, source_target_pairs={{0,0},{1,8},{2,16},{3,24},{4,4},{5,12},{6,20},{7,28},{8,1},{9,9},{... | collective-permute-start | bytes 24584 | tf_op jit(solution)/shard_map/ppermute | solution.py:235
  300.1 11.0 %copy-start.10 = (bf16[256,1024]{1,0:T(8,128)(2,1)S(1)}, bf16[256,1024]{1,0:T(8,128)(2,1)}, u32[]{:S(2)}) copy-start(bf16[256,1024]{1,0:T(8,128)(2,1)} %copy-done.9) | copy-start | bytes 1572868
  300.1 10.4 %collective-permute-start.31 = (bf16[8,512]{1,0:T(8,128)(2,1)S(1)}, bf16[8,512]{1,0:T(8,128)(2,1)S(1)}, u32[]{:S(2)}, u32[]{:S(2)}) collective-permute-start(bf16[8,512]{1,0:T(8,128)(2,1)S(1)} %get-tuple-element.127), channel_id=1, source_target_pairs={{0,4},{1,12},{2,20},{3,28},{4,0},{5,8},{6,16},{7,24},{8,5},{9,13},... | collective-permute-start | bytes 24584 | tf_op jit(solution)/shard_map/ppermute | solution.py:235
  (6 other events, 5.9 us)

commit v7 on v6

--- a/solution.py
+++ b/solution.py
@@ -69,16 +69,18 @@
         ]
 
 
-def each_block(line, place, relayed, body):
+def each_block(line, place, relayed, which, body):
     z, x = place[0], place[1]
-    for i, (m, came) in enumerate(line.slots(z, relayed)):
+    slots = line.slots(z, relayed)
+    for j, at in enumerate(which):
+        m, came = slots[at]
         plane = lax.rem(z + m, line.n_z)
         for e in range(2):
             index = 2 * plane + (x if e == 0 else 1 - x)
             if came is None:
-                body(i, e, index)
+                body(j, e, index)
             else:
-                pl.when(came)(functools.partial(body, i, e, index))
+                pl.when(came)(functools.partial(body, j, e, index))
 
 
 def columns(index, size):
@@ -97,19 +99,31 @@
     return expo / jnp.sum(expo, axis=0, keepdims=True)
 
 
-def forward_kernel(line, relayed, image_own, place, text, kv, *refs):
-    n = (len(refs) - 3) // 2
+def query_kernel(line, relayed, which, place, text, *refs):
+    n = len(which)
+    weights, total = (refs[:n], refs[n : 2 * n]), refs[-1]
+    own_width = weights[0][0].shape[0]
+    total[...] = jnp.zeros_like(total)
+
+    def add(j, e, index):
+        total[...] += matmul(text[:, columns(index, own_width)], weights[e][j][...])
+
+    each_block(line, place, relayed, which, add)
+
+
+def forward_kernel(line, relayed, which, image_own, place, text, kv, part, *refs):
+    n = len(which)
     weights, (query_out, attended_out, total) = (refs[:n], refs[n : 2 * n]), refs[2 * n :]
-    own_width = weights[0][0].shape[0]
     rows, cols = total.shape
-    total[...] = jnp.zeros_like(total)
-
-    def add(i, e, index):
-        total[...] += matmul(text[:, columns(index, own_width)], weights[e][i][...])
-
-    each_block(line, place, relayed, add)
+    total[...] = part[...]
+
+    def add(j, e, index):
+        weight = weights[e][j]
+        total[...] += matmul(text[:, columns(index, weight.shape[0])], weight[...])
+
+    each_block(line, place, relayed, which, add)
     query_out[...] = total[...].astype(BF16)
-    part = rows // 4
+    part_rows = rows // 4
     quarter = place[2]
     for h in range(cols // HEAD_DIM):
         at = slice(h * HEAD_DIM, (h + 1) * HEAD_DIM)
@@ -119,28 +133,33 @@
         for r in range(4):
             low_bit = (quarter + r) % 2
             high_bit = (quarter // 2 + r // 2) % 2
-            start = pl.multiple_of((2 * low_bit + high_bit) * part, part)
-            attended_out[pl.ds(start, part), at] = attended[r * part : (r + 1) * part]
-
-
-def grad_kernel(line, place, live, here, there, *refs):
-    weights, (keep_out, send_out, keep, send) = refs[:-4], refs[-4:]
-    own_width = weights[0].shape[1] // 2
+            start = pl.multiple_of((2 * low_bit + high_bit) * part_rows, part_rows)
+            attended_out[pl.ds(start, part_rows), at] = attended[
+                r * part_rows : (r + 1) * part_rows
+            ]
+
+
+def grad_kernel(line, which, parts, place, live, here, there, *refs):
+    before, refs = refs[:parts], refs[parts:]
+    weights, outs = refs[: len(which)], refs[len(which) :]
     half = line.n_dp // 2
     core = place[2] % 2
-    keep[...] = jnp.zeros_like(keep)
-    send[...] = jnp.zeros_like(send)
-
-    def add(i, e, index):
-        weight = weights[i][:, e * own_width : (e + 1) * own_width]
+    keep, send = outs[-2:]
+    keep[...] = before[0][...] if parts else jnp.zeros_like(keep)
+    send[...] = before[1][...] if parts else jnp.zeros_like(send)
+
+    def add(j, e, index):
+        own_width = weights[j].shape[1] // 2
+        weight = weights[j][:, e * own_width : (e + 1) * own_width]
         keep[...] += matmul(live[:, columns(index, own_width)], weight, BACK)
         inner = columns(lax.rem(index, half), own_width)
         other = jnp.where(lax.div(index, half) == core, here[:, inner], there[:, inner])
         send[...] += matmul(other, weight, BACK)
 
-    each_block(line, place, line.n_z == 4, add)
-    keep_out[...] = keep[...].astype(BF16)
-    send_out[...] = send[...].astype(BF16)
+    each_block(line, place, line.n_z == 4, which, add)
+    if parts:
+        outs[0][...] = keep[...].astype(BF16)
+        outs[1][...] = send[...].astype(BF16)
 
 
 def backward_kernel(image_own, place, query, kv, keep, come, query_grad, kv_grad):
@@ -173,7 +192,7 @@
         member = lax.bitwise_xor(lax.div(index, chunk), place[3])
         out[member, lax.rem(index, chunk)] = term.astype(BF16)
 
-    each_block(line, place, relayed, write)
+    each_block(line, place, relayed, range(n), write)
 
 
 def weight_grad_kernel(line, place, *refs):
@@ -187,8 +206,18 @@
         term = matmul(attended[e][i][...], block, FIRST)
         total[...] += term.astype(BF16).astype(F32)
 
-    each_block(line, place, False, add)
+    each_block(line, place, False, range(n), add)
     out[...] = total[...].astype(BF16)
+
+
+def sum_kernel(place, term, *refs):
+    parts, out = refs[:-1], refs[-1]
+    width = term.shape[3]
+    for c in range(term.shape[1]):
+        total = term[0, c].astype(F32)
+        for part in parts:
+            total = total + part[c].astype(F32)
+        out[:, c * width : (c + 1) * width] = total.astype(BF16)
 
 
 def call(kernel, place, operands, outs, scratch=(), flops=0):
@@ -282,18 +311,10 @@
     wo_keep = lax.dynamic_slice_in_dim(out_weight, x * half_cols, half_cols, 0)
     wo_send = lax.dynamic_slice_in_dim(out_weight, (1 - x) * half_cols, half_cols, 0)
     live_half = lax.dynamic_slice_in_dim(live_flat, core * (width // 2), width // 2, 1)
-    query_weight, image_cols, wo_send = gate((query_weight, image_cols, wo_send))
     wq_moved = line.first(query_weight)
-    wo_come = line.swap(wo_send)
-    wq_others = [line.swap(query_weight)]
-    wo_pair = jnp.concatenate([wo_keep, wo_come], axis=1)
-    part_kv = jnp.concatenate(
-        [matmul(image_cols, key_weight), matmul(image_cols, value_weight)], axis=1
-    )
-    part_kv = part_kv.reshape(n_dp, image_rows, 2 * local_cols)
-    kv_own = jnp.sum(lax.all_to_all(part_kv, "dp", split_axis=0, concat_axis=0), axis=0)
-    kv_own, live_half, wo_pair, wq_others[0], *wq_moved = gate(
-        (kv_own.astype(BF16), live_half, wo_pair, wq_others[0], *wq_moved)
+    wo_pair = jnp.concatenate([wo_keep, line.swap(wo_send)], axis=1)
+    image_cols, wo_pair, live_half, wq_other, *wq_moved = gate(
+        (image_cols, wo_pair, live_half, line.swap(query_weight), *wq_moved)
     )
 
     n_moved = len(wq_moved)
@@ -301,9 +322,14 @@
     wq_two = line.second(wq_moved)
     wo_moved = line.first(wo_pair)
     above, live_here = gate((wq_moved[0], line.swap(live_half)))
-    wq_others.append(line.swap(above, planes[0]))
+    wq_others = [wq_other, line.swap(above, planes[0])]
+    part_kv = jnp.concatenate(
+        [matmul(image_cols, key_weight), matmul(image_cols, value_weight)], axis=1
+    )
+    part_kv = part_kv.reshape(n_dp, image_rows, 2 * local_cols)
+    kv_own = jnp.sum(lax.all_to_all(part_kv, "dp", split_axis=0, concat_axis=0), axis=0)
     kv_own, live_here, *staged = gate(
-        (kv_own, live_here, *wq_others, *wq_moved, *wq_two, *wo_moved)
+        (kv_own.astype(BF16), live_here, *wq_others, *wq_moved, *wq_two, *wo_moved)
     )
     wq_others, staged = staged[:2], staged[2:]
     wq_moved, wq_two, wo_moved = staged[:n_moved], staged[n_moved:-n_moved], staged[-n_moved:]
@@ -332,27 +358,52 @@
     ).reshape(quarter_rows, n_dp, own_width)
     live_mine = lax.all_to_all(live_part, "dp", split_axis=1, concat_axis=0)
     live_mine = live_mine.reshape(n_dp, quarter_rows, own_width)
-    live_mine, live_flat = gate((live_mine, live_flat))
-    wq_blocks = [query_weight, *wq_moved, *wq_last, *wq_others]
-
+    arrivals = [query_weight, *wq_moved, *wq_last]
+    early = range(4 if relayed else len(arrivals))
+    late = range(len(early), len(arrivals))
+    query_part = call(
+        functools.partial(query_kernel, line, relayed, early),
+        place,
+        (text_flat, *arrivals[: len(early)], *wq_others[: len(early)]),
+        [shape((rows, local_cols), F32)],
+        (),
+        2 * rows * width * local_cols,
+    )
+    half = shape((rows, half_cols), F32)
+    wo_early = [wo_pair, *wo_moved]
+    grad_parts = call(
+        functools.partial(grad_kernel, line, range(len(wo_early)), 0),
+        place,
+        (live_flat, live_here, live_there, *wo_early),
+        [half] * 2,
+        (),
+        rows * width * local_cols,
+    )
+
+    query_part, *grad_parts = gate((query_part, *grad_parts))
+
+    wo_late = range(len(wo_early), len(wo_early) + len(wo_last))
     grad_keep, grad_send = call(
-        functools.partial(grad_kernel, line),
-        place,
-        (live_flat, live_here, live_there, wo_pair, *wo_moved, *wo_last),
+        functools.partial(grad_kernel, line, wo_late, 2),
+        place,
+        (live_flat, live_here, live_there, *grad_parts, *wo_last),
         [shape((rows, half_cols), BF16)] * 2,
         [pltpu.VMEM((rows, half_cols), F32)] * 2,
-        2 * rows * width * local_cols,
-    )
-    text_flat, grad_keep, grad_send = gate((text_flat, grad_keep, grad_send))
+        rows * width * local_cols,
+    )
+    text_flat, live_mine, grad_keep, grad_send = gate(
+        (text_flat, live_mine, grad_keep, grad_send)
+    )
     grad_come = line.swap(grad_send)
     queries, attended = call(
-        functools.partial(forward_kernel, line, relayed, image_own),
-        place,
-        (text_flat, kv_all, *wq_blocks),
+        functools.partial(forward_kernel, line, relayed, late, image_own),
+        place,
+        (text_flat, kv_all, query_part, *arrivals[len(early) :], *wq_others[len(early) :]),
         [shape((rows, local_cols), BF16)] * 2,
         [pltpu.VMEM((rows, local_cols), F32)],
-        2 * rows * width * local_cols,
-    )
+        rows * width * local_cols,
+    )
+    wq_blocks = [*arrivals, *wq_others]
 
     att_next = [line.shift(attended, m) for m in (1, line.n_z - 1)]
     att_swapped = line.swap(attended)
@@ -377,31 +428,35 @@
         (),
         2 * rows * width * local_cols,
     )
-    kv_grad, term, attended, live_y, att_swapped, *att_next = gate(
-        (kv_grad.astype(BF16), term, attended, live_y, att_swapped, *att_next)
-    )
+    kv_grad, term, live_y = gate((kv_grad.astype(BF16), term, live_y))
+
+    text_parts = [tensor_swap(term[k], k) for k in range(2, n_tensor)]
+    live_pair = jnp.stack([live_mine, live_y])
+    kv_grad_all = everywhere(kv_grad).reshape(images, 2 * local_cols)
+    kv_grad_all, term, attended, att_swapped, *staged = gate(
+        (kv_grad_all, term, attended, att_swapped, *att_next, *text_parts)
+    )
+    att_next, text_parts = staged[:2], staged[2:]
+
     att_far = [line.shift(attended, m) for m in range(2, line.n_z - 1)]
     att_other_next = [line.swap(block) for block in att_next]
-
-    text_parts = [term[0]]
-    for k in range(n_tensor - 1, 1, -1):
-        text_parts.append(tensor_swap(term[k], k))
-    live_pair = jnp.stack([live_mine, live_y])
-    kv_grad_all = everywhere(kv_grad).reshape(images, 2 * local_cols)
-    kv_grad_all, term_core, live_pair, *third = gate(
-        (kv_grad_all, term[1], live_pair, *att_other_next, *att_far)
-    )
-    att_other_next, att_far = third[:2], third[2:]
-
-    att_other_far = [line.swap(block) for block in att_far]
     live_core = tensor_swap(live_pair, 1)
-    text_parts.append(tensor_swap(term_core, 1))
+    text_parts.append(tensor_swap(term[1], 1))
     image_term = matmul(kv_grad_all[:, :local_cols], key_weight, BACK)
     image_term = image_term + matmul(kv_grad_all[:, local_cols:], value_weight, BACK)
-    image_grad, *att_other_far = to_owner(line, image_term.astype(BF16), *att_other_far)
+    image_grad, live_core, *staged = to_owner(
+        line, image_term.astype(BF16), live_core, *text_parts, *att_other_next, *att_far
+    )
+    text_parts, staged = staged[: n_tensor - 1], staged[n_tensor - 1 :]
+    att_other_next, att_far = staged[:2], staged[2:]
+    att_other_far = [line.swap(block) for block in att_far]
     image_grad = image_grad.reshape(samples, image_own, width // n_tensor)
-    text_grad = functools.reduce(jnp.add, [part.astype(F32) for part in text_parts])
-    text_grad = text_grad.astype(BF16).transpose(1, 0, 2)
+    text_grad = call(
+        sum_kernel,
+        place,
+        (term, *text_parts),
+        [shape((rows, width // n_tensor), BF16)],
+    )
     text_grad = text_grad.reshape(samples, tok_rows, width // n_tensor)
 
     att_blocks = [attended, att_next[0], *att_far, att_next[1]]

time: 319 us -> 317 us (level)
  waiting for transfers between devices: 144 us -> 122 us
  starting transfers between devices: 98.7 us -> 106 us
  Pallas kernels: 30 us -> 36.3 us
  blocking collectives: 0 us -> 5.36 us
    all_to_all x1, waiting for transfers between devices: 0.01 us -> 29.4 us  [shards(): lax.all_to_all(part_kv, 'dp', split_axis=0, concat_axis=0)]
    ppermute x13, waiting for transfers between devices: 37.2 us -> 8.17 us  [move(): return lax.ppermute(block, 'dp', pairs)]
    all_to_all x1, waiting for transfers between devices: 14.6 us -> 0.01 us  [shards(): live_mine = lax.all_to_all(live_part, 'dp', split_axis=1, concat_axis=0)]
    all_to_all x2, waiting for transfers between devices: 47.7 us -> 37.8 us  [everywhere(): return lax.all_to_all(copies, 'dp', split_axis=0, concat_axis=0)]
    ppermute x12, waiting for transfers between devices: 37.9 us -> 46.5 us  [swap(): return lax.ppermute(block, 'dp', pairs)]
    all_to_all x2, starting transfers between devices: 17.1 us -> 24 us  [everywhere(): return lax.all_to_all(copies, 'dp', split_axis=0, concat_axis=0)]
    pallas_call x5 -> x8, Pallas kernels: 30 us -> 36.3 us  [call(): pl.pallas_call(kernel, out_shape=outs[0] if single else outs, in_specs=[p...]
    all_to_all x0 -> x1, blocking collectives: none -> 5.36 us  [to_owner(): lax.all_to_all(terms.reshape(n_tensor, images // n_tensor, cols), 'tensor...]
  transfers between devices with their start and end apart: 40 -> 39, of which waited for: 13 -> 11; matrix products, arithmetic and copies ran while one was open for 10% -> 8% of each run, Pallas kernels for 7% -> 9%
where the time goes in v7:
time: 317 us; the launch traced here: 313 us
  waiting for transfers between devices  122 us (38%)
  starting transfers between devices  106 us (33%)
  Pallas kernels  36.3 us (11%)
  local copies, waits for them, and re-layouts  24.4 us (8%)
  other arithmetic  15 us (5%)
  blocking collectives  5.36 us (2%)
    ppermute x12, waiting for transfers between devices, swap(): return lax.ppermute(block, 'dp', pairs)  46.5 us
    all_to_all x2, waiting for transfers between devices, everywhere(): return lax.all_to_all(copies, 'dp', split_axis=0, concat_axis=0)  37.8 us
    pallas_call x8, Pallas kernels, call(): pl.pallas_call(kernel, out_shape=outs[0] if single else outs, in_specs=[p...  36.3 us
    ppermute x13, starting transfers between devices, move(): return lax.ppermute(block, 'dp', pairs)  31.2 us
    all_to_all x1, waiting for transfers between devices, shards(): lax.all_to_all(part_kv, 'dp', split_axis=0, concat_axis=0)  29.4 us
    all_to_all x2, starting transfers between devices, everywhere(): return lax.all_to_all(copies, 'dp', split_axis=0, concat_axis=0)  24 us
    ppermute x12, starting transfers between devices, swap(): return lax.ppermute(block, 'dp', pairs)  18.2 us
    unnamed x49, local copies, waits for them, and re-layouts  12.4 us
  transfers between devices with their start and end apart: 39, of which 11 were waited for; matrix products, arithmetic and copies ran while one was open for 8% of the time, Pallas kernels for 9%

profile of v7, /device:TPU:4, one launch (start us, length us, event | category | flops | bytes accessed | tf_op | source)
XLA Modules:
  0.0 313.1 jit_solution(412089403723240600)
XLA Ops:
  0.7 1.6 collective-permute-start.1
  3.5 4.6 %collective-permute-start.3 = (bf16[512,1024]{1,0:T(8,128)(2,1)}, bf16[512,1024]{1,0:T(8,128)(2,1)S(1)}, u32[]{:S(2)}, u32[]{:S(2)}) collective-permute-start(bf16[512,1024]{1,0:T(8,128)(2,1)} %refs_0_.3), channel_id=1, source_target_pairs={{0,8},{4,12},{8,16},{12,20},{16,24},{20,28},{1,9},{5,13},{9,17},{1... | collective-permute-start | bytes 3145736 | tf_op jit(solution)/shard_map/ppermute | solution.py:31
  8.2 2.2 constant_dynamic-slice_fusion.3
  11.6 4.8 %all-to-all-start = ((bf16[8,8,512]{2,0,1:T(8,128)(2,1)}), bf16[8,8,512]{2,0,1:T(8,128)(2,1)S(1)}, u32[]{:S(2)}, u32[]{:S(2)}) async-start(bf16[8,8,512]{2,0,1:T(8,128)(2,1)} %copy.14), calls=%async_computation | async-start | bytes 131072 | tf_op jit(solution)/shard_map/all_to_all | solution.py:310
  16.5 3.1 %broadcast_select_fusion = bf16[2,128,4096]{2,1,0:T(8,128)(2,1)} fusion(bf16[2,128,4096]{2,1,0:T(8,128)(2,1)} %param.10, pred[2,128]{1,0:T(4,128)(4,1)S(1)} %broadcast_compare_fusion), kind=kLoop, calls=%fused_computation | loop fusion | flops 1048576 | bytes 4194560 | tf_op jit(solution)/shard_map/jit(_where)/select_n | solution.py:302
  19.6 2.4 constant_dynamic-slice_fusion.1
  22.0 15.8 %collective-permute-done = bf16[512,512]{1,0:T(8,128)(2,1)} collective-permute-done((bf16[512,512]{1,0:T(8,128)(2,1)}, bf16[512,512]{1,0:T(8,128)(2,1)}, u32[]{:S(2)}, u32[]{:S(2)}) %collective-permute-start) | collective-permute-done | bytes 524320 | tf_op jit(solution)/shard_map/ppermute | solution.py:36
  37.8 2.1 pad_maximum_fusion.refs_0_
  40.0 1.6 collective-permute-start.4
  42.8 5.5 %collective-permute-start.9 = (bf16[512,1024]{1,0:T(8,128)(2,1)}, bf16[512,1024]{1,0:T(8,128)(2,1)}, u32[]{:S(2)}, u32[]{:S(2)}) collective-permute-start(bf16[512,1024]{1,0:T(8,128)(2,1)} %pad_maximum_fusion.refs_0_), channel_id=1, source_target_pairs={{0,8},{4,12},{8,16},{12,20},{16,24},{20,28},{1,9},{5,13},{9,17},{1... | collective-permute-start | bytes 3145736 | tf_op jit(solution)/shard_map/ppermute | solution.py:31
  49.6 1.7 collective-permute-start.7
  51.3 1.5 fusion.4
  53.1 11.2 %collective-permute-done.4.here = bf16[256,2048]{1,0:T(8,128)(2,1)} collective-permute-done((bf16[256,2048]{1,0:T(8,128)(2,1)}, bf16[256,2048]{1,0:T(8,128)(2,1)}, u32[]{:S(2)}, u32[]{:S(2)}) %collective-permute-start.4) | collective-permute-done | bytes 1048608 | tf_op jit(solution)/shard_map/ppermute | solution.py:36
  64.3 3.4 %collective-permute-start.5 = (bf16[512,1024]{1,0:T(8,128)(2,1)S(1)}, bf16[512,1024]{1,0:T(8,128)(2,1)}, u32[]{:S(2)}, u32[]{:S(2)}) collective-permute-start(bf16[512,1024]{1,0:T(8,128)(2,1)S(1)} %collective-permute-done.2.refs_1_), channel_id=1, source_target_pairs={{0,4},{4,0},{8,12},{12,8},{16,20},{20,16},{1,5},{5,1},{9,13},{13,9... | collective-permute-start | bytes 3145736 | tf_op jit(solution)/shard_map/ppermute | solution.py:36
  68.5 4.1 %all-to-all-start.1 = ((f32[8,8,2048]{2,1,0:T(8,128)}), f32[8,8,2048]{2,1,0:T(8,128)}, u32[]{:S(2)}, u32[]{:S(2)}) async-start(f32[8,8,2048]{2,1,0:T(8,128)} %maximum_bitcast_fusion), calls=%async_computation.1 | async-start | bytes 1048576 | tf_op jit(solution)/shard_map/all_to_all | solution.py:330
  72.7 29.4 %all-to-all-done.1 = f32[8,8,2048]{2,1,0:T(8,128)} async-done(((f32[8,8,2048]{2,1,0:T(8,128)}), f32[8,8,2048]{2,1,0:T(8,128)}, u32[]{:S(2)}, u32[]{:S(2)}) %all-to-all-start.1) | async-done | bytes 524320 | tf_op jit(solution)/shard_map/all_to_all | solution.py:330
  108.0 1.6 collective-permute-start.11
  109.6 1.7 collective-permute-start.13
  112.1 12.4 %all-to-all-start.2 = ((bf16[8,8,2048]{2,1,0:T(8,128)(2,1)}), bf16[8,8,2048]{2,1,0:T(8,128)(2,1)S(1)}, u32[]{:S(2)}, u32[]{:S(2)}) async-start(bf16[8,8,2048]{2,1,0:T(8,128)(2,1)} %broadcast_in_dim.16), calls=%async_computation.2 | async-start | bytes 524288 | tf_op jit(solution)/shard_map/all_to_all | solution.py:339
  124.4 31.5 %all-to-all-done.2 = bf16[8,8,2048]{2,1,0:T(8,128)(2,1)S(1)} async-done(((bf16[8,8,2048]{2,1,0:T(8,128)(2,1)}), bf16[8,8,2048]{2,1,0:T(8,128)(2,1)S(1)}, u32[]{:S(2)}, u32[]{:S(2)}) %all-to-all-start.2) | async-done | bytes 262176 | tf_op jit(solution)/shard_map/all_to_all | solution.py:339
  155.9 2.3 broadcast_select_fusion.1.refs_2_
  162.0 8.2 %all-to-all-start.3 = ((bf16[1,64,8,512]{3,1,0,2:T(8,128)(2,1)}), bf16[1,64,8,512]{3,1,0,2:T(8,128)(2,1)}, u32[]{:S(2)}, u32[]{:S(2)}) async-start(bf16[1,64,8,512]{3,1,0,2:T(8,128)(2,1)} %copy.15), calls=%async_computation.3 | async-start | bytes 1048576 | tf_op jit(solution)/shard_map/all_to_all | solution.py:359
  170.2 3.9 %collective-permute-start.17 = (bf16[512,1024]{1,0:T(8,128)(2,1)}, bf16[512,1024]{1,0:T(8,128)(2,1)}, u32[]{:S(2)}, u32[]{:S(2)}) collective-permute-start(bf16[512,1024]{1,0:T(8,128)(2,1)} %collective-permute-done.12.refs_0_.refs_4_), channel_id=1, source_target_pairs={{0,4},{4,0},{24,28},{28,24},{1,5},{5,1},{25,29},{29,25},{2,6},{6,2... | collective-permute-start | bytes 3145736 | tf_op jit(solution)/shard_map/ppermute | solution.py:36
  176.6 5.2 %shard_map.103.part = f32[256,1024]{1,0:T(8,128)S(1)} custom-call(s32[4]{0:T(128)S(1)} %pad_add_fusion.place, bf16[256,4096]{1,0:T(8,128)(2,1)} %bitcast.45, bf16[512,1024]{1,0:T(8,128)(2,1)S(1)} %copy-done.2, bf16[512,1024]{1,0:T(8,128)(2,1)S(1)} %copy-done.4, bf16[512,1024]{1,0:T(8,128)(2,1)S(1)} %copy-done.7, ...), custom_call_target="tpu_custom_call" | custom-call | flops 2147483648 | bytes 11534336 | tf_op jit(solution)/shard_map/pallas_call | solution.py:226
  182.9 4.5 %shard_map.104 = (f32[256,512]{1,0:T(8,128)S(1)}, f32[256,512]{1,0:T(8,128)S(1)}) custom-call(s32[4]{0:T(128)S(1)} %pad_add_fusion.place, bf16[256,4096]{1,0:T(8,128)(2,1)} %bitcast.43, bf16[256,2048]{1,0:T(8,128)(2,1)} %collective-permute-done.4.here, bf16[256,2048]{1,0:T(8,128)(2,1)} %collective-permute-done.15.there, bf16[512,1024]{1,0:T(8,128)(2,1)S(1)} %copy-done.11, ...), custom_call_target="tpu_custom_call" | custom-call | flops 1073741824 | bytes 8388608 | tf_op jit(solution)/shard_map/pallas_call | solution.py:226
  187.4 2.1 collective-permute-done.16.refs_3_
  189.5 4.6 %shard_map.105 = (bf16[256,512]{1,0:T(8,128)(2,1)S(1)}, bf16[256,512]{1,0:T(8,128)(2,1)S(1)}) custom-call(s32[4]{0:T(128)S(1)} %pad_add_fusion.place, bf16[256,4096]{1,0:T(8,128)(2,1)} %bitcast.44, bf16[256,2048]{1,0:T(8,128)(2,1)} %collective-permute-done.4.here, bf16[256,2048]{1,0:T(8,128)(2,1)} %collective-permute-done.15.there, ...), custom_call_target="tpu_custom_call" | custom-call | flops 1073741824 | bytes 7864320 | tf_op jit(solution)/shard_map/pallas_call | solution.py:226
  195.9 6.1 %collective-permute-done.17.refs_1_.refs_9_ = bf16[512,1024]{1,0:T(8,128)(2,1)} collective-permute-done((bf16[512,1024]{1,0:T(8,128)(2,1)}, bf16[512,1024]{1,0:T(8,128)(2,1)}, u32[]{:S(2)}, u32[]{:S(2)}) %collective-permute-start.17) | collective-permute-done | bytes 1048608 | tf_op jit(solution)/shard_map/ppermute | solution.py:36
  203.2 4.2 %shard_map.106 = (bf16[256,1024]{1,0:T(8,128)(2,1)S(1)}, bf16[256,1024]{1,0:T(8,128)(2,1)S(1)}) custom-call(s32[4]{0:T(128)S(1)} %pad_add_fusion.place, bf16[256,4096]{1,0:T(8,128)(2,1)} %bitcast.46, bf16[64,2048]{1,0:T(8,128)(2,1)S(1)} %bitcast.38, f32[256,1024]{1,0:T(8,128)S(1)} %copy-done.10, bf16[512,1024]{1,0:T(8,128)(2,1)} %collective-permute-done.12.refs_0_.refs_4_, ...), custom_call_target="tpu_custom_call" | custom-call | flops 1073741824 | bytes 6553600 | tf_op jit(solution)/shard_map/pallas_call | solution.py:226
  207.5 1.9 shard_map.107
  211.0 5.2 %all-to-all-start.4 = ((f32[8,8,2048]{2,1,0:T(8,128)}), f32[8,8,2048]{2,1,0:T(8,128)}, u32[]{:S(2)}, u32[]{:S(2)}) async-start(f32[8,8,2048]{2,1,0:T(8,128)} %bitcast.40), calls=%async_computation.4 | async-start | bytes 1048576 | tf_op jit(solution)/shard_map/all_to_all | solution.py:421
  216.7 2.0 collective-permute-start.20
  218.7 3.3 %collective-permute-start.21 = (bf16[256,1024]{1,0:T(8,128)(2,1)}, bf16[256,1024]{1,0:T(8,128)(2,1)}, u32[]{:S(2)}, u32[]{:S(2)}) collective-permute-start(bf16[256,1024]{1,0:T(8,128)(2,1)} %copy-done.17), channel_id=1, source_target_pairs={{8,0},{12,4},{16,8},{20,12},{24,16},{28,20},{0,24},{4,28},{9,1},{1... | collective-permute-start | bytes 1572872 | tf_op jit(solution)/shard_map/ppermute | solution.py:31
  225.5 7.5 %shard_map.108.term = bf16[4,2,256,512]{3,2,1,0:T(8,128)(2,1)} custom-call(s32[4]{0:T(128)S(1)} %pad_add_fusion.place, bf16[256,1024]{1,0:T(8,128)(2,1)S(1)} %copy-done.13, bf16[512,1024]{1,0:T(8,128)(2,1)S(1)} %copy-done.2, bf16[512,1024]{1,0:T(8,128)(2,1)S(1)} %copy-done.5, bf16[512,1024]{1,0:T(8,128)(2,1)S(1)} %copy-done.8, ...), custom_call_target="tpu_custom_call" | custom-call | flops 2147483648 | bytes 13107200 | tf_op jit(solution)/shard_map/pallas_call | solution.py:226
  234.1 2.4 slice_bitcast_fusion.1
  236.4 1.5 collective-permute-start.23
  238.7 11.7 %all-to-all-start.5 = ((bf16[8,8,2048]{2,1,0:T(8,128)(2,1)}), bf16[8,8,2048]{2,1,0:T(8,128)(2,1)S(1)}, u32[]{:S(2)}, u32[]{:S(2)}) async-start(bf16[8,8,2048]{2,1,0:T(8,128)(2,1)} %broadcast_in_dim.17), calls=%async_computation.5 | async-start | bytes 524288 | tf_op jit(solution)/shard_map/all_to_all | solution.py:339
  250.3 2.3 pad_maximum_fusion.1.refs_0_
  254.0 6.3 %all-to-all-done.5 = bf16[8,8,2048]{2,1,0:T(8,128)(2,1)S(1)} async-done(((bf16[8,8,2048]{2,1,0:T(8,128)(2,1)}), bf16[8,8,2048]{2,1,0:T(8,128)(2,1)S(1)}, u32[]{:S(2)}, u32[]{:S(2)}) %all-to-all-start.5) | async-done | bytes 262176 | tf_op jit(solution)/shard_map/all_to_all | solution.py:339
  263.4 6.6 %collective-permute-start.29 = (bf16[256,1024]{1,0:T(8,128)(2,1)}, bf16[256,1024]{1,0:T(8,128)(2,1)}, u32[]{:S(2)}, u32[]{:S(2)}) collective-permute-start(bf16[256,1024]{1,0:T(8,128)(2,1)} %copy-done.17), channel_id=1, source_target_pairs={{16,0},{20,4},{24,8},{28,12},{0,16},{4,20},{8,24},{12,28},{17,1},{... | collective-permute-start | bytes 1572872 | tf_op jit(solution)/shard_map/ppermute | solution.py:31
  270.9 5.4 %all_to_all.59 = bf16[4,16,512]{2,1,0:T(8,128)(2,1)S(1)} all-to-all(bf16[4,16,512]{2,1,0:T(8,128)(2,1)S(1)} %bitcast.54), channel_id=1, replica_groups=mesh['dp'=8,'tensor'=4] {'tensor'}, dimensions={0} | all-to-all | bytes 131072 | tf_op jit(solution)/shard_map/all_to_all | solution.py:248
  276.4 10.7 %collective-permute-done.28.refs_9_ = bf16[256,1024]{1,0:T(8,128)(2,1)} collective-permute-done((bf16[256,1024]{1,0:T(8,128)(2,1)}, bf16[256,1024]{1,0:T(8,128)(2,1)}, u32[]{:S(2)}, u32[]{:S(2)}) %collective-permute-start.28) | collective-permute-done | bytes 524320 | tf_op jit(solution)/shard_map/ppermute | solution.py:36
  287.1 6.0 %collective-permute-done.29.refs_4_ = bf16[256,1024]{1,0:T(8,128)(2,1)} collective-permute-done((bf16[256,1024]{1,0:T(8,128)(2,1)}, bf16[256,1024]{1,0:T(8,128)(2,1)}, u32[]{:S(2)}, u32[]{:S(2)}) %collective-permute-start.29) | collective-permute-done | bytes 524320 | tf_op jit(solution)/shard_map/ppermute | solution.py:31
  293.4 2.1 collective-permute-start.30
  295.5 4.8 %collective-permute-start.31 = (bf16[8,512]{1,0:T(8,128)(2,1)S(1)}, bf16[8,512]{1,0:T(8,128)(2,1)S(1)}, u32[]{:S(2)}, u32[]{:S(2)}) collective-permute-start(bf16[8,512]{1,0:T(8,128)(2,1)S(1)} %get-tuple-element.136), channel_id=1, source_target_pairs={{0,4},{1,12},{2,20},{3,28},{4,0},{5,8},{6,16},{7,24},{8,5},{9,13},... | collective-permute-start | bytes 24584 | tf_op jit(solution)/shard_map/ppermute | solution.py:264
  300.3 2.4 shard_map.109
  303.4 2.6 collective-permute-done.32.refs_8_
  307.1 6.0 %shard_map.110 = bf16[1024,512]{1,0:T(8,128)(2,1)} custom-call(s32[4]{0:T(128)S(1)} %pad_add_fusion.place, bf16[2,8,64,512]{3,2,1,0:T(8,128)(2,1)} %pad_maximum_fusion.1.refs_0_, bf16[2,8,64,512]{3,2,1,0:T(8,128)(2,1)} %collective-permute-done.25.refs_1_, bf16[256,1024]{1,0:T(8,128)(2,1)S(1)} %copy-done.18, ...), custom_call_target="tpu_custom_call" | custom-call | flops 2147483648 | bytes 7340032 | tf_op jit(solution)/shard_map/pallas_call | solution.py:226
  (118 shorter events, 37.9 us)
Async XLA Ops:
  0.6 52.2 %copy-start = (bf16[512,1024]{1,0:T(8,128)(2,1)S(1)}, bf16[512,1024]{1,0:T(8,128)(2,1)}, u32[]{:S(2)}) copy-start(bf16[512,1024]{1,0:T(8,128)(2,1)} %param.14) | copy-start | bytes 3145732
  0.6 10.3 %copy-start.22 = (bf16[2,4,4096]{2,1,0:T(4,128)(2,1)S(1)}, bf16[2,4,4096]{2,1,0:T(4,128)(2,1)}, u32[]{:S(2)}) copy-start(bf16[2,4,4096]{2,1,0:T(4,128)(2,1)} %param.9) | copy-start | bytes 196612
  0.7 15.8 %copy-start.23 = (s32[2]{0:T(128)S(1)}, s32[2]{0:T(128)}, u32[]{:S(2)}) copy-start(s32[2]{0:T(128)} %param.11) | copy-start | bytes 28
  0.7 39.3 %collective-permute-start.1 = (bf16[512,1024]{1,0:T(8,128)(2,1)}, bf16[512,1024]{1,0:T(8,128)(2,1)}, u32[]{:S(2)}, u32[]{:S(2)}) collective-permute-start(bf16[512,1024]{1,0:T(8,128)(2,1)} %refs_0_.3), channel_id=1, source_target_pairs={{0,4},{4,0},{8,12},{12,8},{16,20},{20,16},{24,28},{28,24},{1,5},{5... | collective-permute-start | bytes 3145736 | tf_op jit(solution)/shard_map/ppermute | solution.py:36
  2.2 37.7 %collective-permute-start.2 = (bf16[512,1024]{1,0:T(8,128)(2,1)}, bf16[512,1024]{1,0:T(8,128)(2,1)S(1)}, u32[]{:S(2)}, u32[]{:S(2)}) collective-permute-start(bf16[512,1024]{1,0:T(8,128)(2,1)} %refs_0_.3), channel_id=1, source_target_pairs={{8,0},{12,4},{16,8},{20,12},{24,16},{28,20},{9,1},{13,5},{17,9},{2... | collective-permute-start | bytes 3145736 | tf_op jit(solution)/shard_map/ppermute | solution.py:31
  3.5 36.4 %collective-permute-start.3 = (bf16[512,1024]{1,0:T(8,128)(2,1)}, bf16[512,1024]{1,0:T(8,128)(2,1)S(1)}, u32[]{:S(2)}, u32[]{:S(2)}) collective-permute-start(bf16[512,1024]{1,0:T(8,128)(2,1)} %refs_0_.3), channel_id=1, source_target_pairs={{0,8},{4,12},{8,16},{12,20},{16,24},{20,28},{1,9},{5,13},{9,17},{1... | collective-permute-start | bytes 3145736 | tf_op jit(solution)/shard_map/ppermute | solution.py:31
  10.4 27.4 %collective-permute-start = (bf16[512,512]{1,0:T(8,128)(2,1)}, bf16[512,512]{1,0:T(8,128)(2,1)}, u32[]{:S(2)}, u32[]{:S(2)}) collective-permute-start(bf16[512,512]{1,0:T(8,128)(2,1)} %get-tuple-element.134), channel_id=1, source_target_pairs={{0,4},{4,0},{8,12},{12,8},{16,20},{20,16},{24,28},{28,24},{1,5},{5... | collective-permute-start | bytes 1572872 | tf_op jit(solution)/shard_map/ppermute | solution.py:36
  11.6 28.3 %all-to-all-start = ((bf16[8,8,512]{2,0,1:T(8,128)(2,1)}), bf16[8,8,512]{2,0,1:T(8,128)(2,1)S(1)}, u32[]{:S(2)}, u32[]{:S(2)}) async-start(bf16[8,8,512]{2,0,1:T(8,128)(2,1)} %copy.14), calls=%async_computation | async-start | bytes 131072 | tf_op jit(solution)/shard_map/all_to_all | solution.py:310
  19.6 18.2 %copy-start.21 = (bf16[512,512]{1,0:T(8,128)(2,1)S(1)}, bf16[512,512]{1,0:T(8,128)(2,1)}, u32[]{:S(2)}) copy-start(bf16[512,512]{1,0:T(8,128)(2,1)} %get-tuple-element.133) | copy-start | bytes 1572868
  39.9 28.6 %copy-start.3 = (bf16[512,1024]{1,0:T(8,128)(2,1)}, bf16[512,1024]{1,0:T(8,128)(2,1)S(1)}, u32[]{:S(2)}) copy-start(bf16[512,1024]{1,0:T(8,128)(2,1)S(1)} %collective-permute-done.2.refs_1_) | copy-start | bytes 3145732
  40.0 69.7 %copy-start.6 = (bf16[512,1024]{1,0:T(8,128)(2,1)}, bf16[512,1024]{1,0:T(8,128)(2,1)S(1)}, u32[]{:S(2)}) copy-start(bf16[512,1024]{1,0:T(8,128)(2,1)S(1)} %collective-permute-done.3.refs_2_) | copy-start | bytes 3145732
  40.0 24.3 %collective-permute-start.4 = (bf16[256,2048]{1,0:T(8,128)(2,1)}, bf16[256,2048]{1,0:T(8,128)(2,1)}, u32[]{:S(2)}, u32[]{:S(2)}) collective-permute-start(bf16[256,2048]{1,0:T(8,128)(2,1)} %constant_dynamic-slice_fusion.1), channel_id=1, source_target_pairs={{0,4},{4,0},{8,12},{12,8},{16,20},{20,16},{24,28},{28,24},{1,5},{5... | collective-permute-start | bytes 3145736 | tf_op jit(solution)/shard_map/ppermute | solution.py:36
  41.5 61.7 %collective-permute-start.8 = (bf16[512,1024]{1,0:T(8,128)(2,1)}, bf16[512,1024]{1,0:T(8,128)(2,1)}, u32[]{:S(2)}, u32[]{:S(2)}) collective-permute-start(bf16[512,1024]{1,0:T(8,128)(2,1)} %pad_maximum_fusion.refs_0_), channel_id=1, source_target_pairs={{8,0},{12,4},{16,8},{20,12},{24,16},{28,20},{9,1},{13,5},{17,9},{2... | collective-permute-start | bytes 3145736 | tf_op jit(solution)/shard_map/ppermute | solution.py:31
  42.8 60.4 %collective-permute-start.9 = (bf16[512,1024]{1,0:T(8,128)(2,1)}, bf16[512,1024]{1,0:T(8,128)(2,1)}, u32[]{:S(2)}, u32[]{:S(2)}) collective-permute-start(bf16[512,1024]{1,0:T(8,128)(2,1)} %pad_maximum_fusion.refs_0_), channel_id=1, source_target_pairs={{0,8},{4,12},{8,16},{12,20},{16,24},{20,28},{1,9},{5,13},{9,17},{1... | collective-permute-start | bytes 3145736 | tf_op jit(solution)/shard_map/ppermute | solution.py:31
  48.3 54.8 %collective-permute-start.6 = (bf16[512,1024]{1,0:T(8,128)(2,1)S(1)}, bf16[512,1024]{1,0:T(8,128)(2,1)}, u32[]{:S(2)}, u32[]{:S(2)}) collective-permute-start(bf16[512,1024]{1,0:T(8,128)(2,1)S(1)} %collective-permute-done.2.refs_1_), channel_id=1, source_target_pairs={{8,0},{12,4},{16,8},{20,12},{9,1},{13,5},{17,9},{21,13},{10,2},{14... | collective-permute-start | bytes 3145736 | tf_op jit(solution)/shard_map/ppermute | solution.py:31
  49.6 53.6 %collective-permute-start.7 = (bf16[512,1024]{1,0:T(8,128)(2,1)S(1)}, bf16[512,1024]{1,0:T(8,128)(2,1)}, u32[]{:S(2)}, u32[]{:S(2)}) collective-permute-start(bf16[512,1024]{1,0:T(8,128)(2,1)S(1)} %collective-permute-done.3.refs_2_), channel_id=1, source_target_pairs={{8,16},{12,20},{16,24},{20,28},{9,17},{13,21},{17,25},{21,29},{10,... | collective-permute-start | bytes 3145736 | tf_op jit(solution)/shard_map/ppermute | solution.py:31
  64.3 38.9 %collective-permute-start.5 = (bf16[512,1024]{1,0:T(8,128)(2,1)S(1)}, bf16[512,1024]{1,0:T(8,128)(2,1)}, u32[]{:S(2)}, u32[]{:S(2)}) collective-permute-start(bf16[512,1024]{1,0:T(8,128)(2,1)S(1)} %collective-permute-done.2.refs_1_), channel_id=1, source_target_pairs={{0,4},{4,0},{8,12},{12,8},{16,20},{20,16},{1,5},{5,1},{9,13},{13,9... | collective-permute-start | bytes 3145736 | tf_op jit(solution)/shard_map/ppermute | solution.py:36
  68.5 33.6 %all-to-all-start.1 = ((f32[8,8,2048]{2,1,0:T(8,128)}), f32[8,8,2048]{2,1,0:T(8,128)}, u32[]{:S(2)}, u32[]{:S(2)}) async-start(f32[8,8,2048]{2,1,0:T(8,128)} %maximum_bitcast_fusion), calls=%async_computation.1 | async-start | bytes 1048576 | tf_op jit(solution)/shard_map/all_to_all | solution.py:330
  104.6 51.3 %collective-permute-start.12 = (bf16[512,1024]{1,0:T(8,128)(2,1)S(1)}, bf16[512,1024]{1,0:T(8,128)(2,1)}, u32[]{:S(2)}, u32[]{:S(2)}) collective-permute-start(bf16[512,1024]{1,0:T(8,128)(2,1)S(1)} %broadcast_select_fusion.2.refs_3_), channel_id=1, source_target_pairs={{8,0},{12,4},{16,24},{20,28},{9,1},{13,5},{17,25},{21,29},{10,2},{... | collective-permute-start | bytes 3145736 | tf_op jit(solution)/shard_map/ppermute | solution.py:31
  105.9 50.0 %collective-permute-start.14 = (bf16[512,1024]{1,0:T(8,128)(2,1)S(1)}, bf16[512,1024]{1,0:T(8,128)(2,1)}, u32[]{:S(2)}, u32[]{:S(2)}) collective-permute-start(bf16[512,1024]{1,0:T(8,128)(2,1)S(1)} %broadcast_select_fusion.2.refs_3_), channel_id=1, source_target_pairs={{0,4},{4,0},{8,12},{12,8},{16,20},{20,16},{24,28},{28,24},{1,5},{5... | collective-permute-start | bytes 3145736 | tf_op jit(solution)/shard_map/ppermute | solution.py:36
  106.7 49.2 %collective-permute-start.10 = (bf16[512,1024]{1,0:T(8,128)(2,1)}, bf16[512,1024]{1,0:T(8,128)(2,1)}, u32[]{:S(2)}, u32[]{:S(2)}) collective-permute-start(bf16[512,1024]{1,0:T(8,128)(2,1)} %collective-permute-done.8.refs_1_), channel_id=1, source_target_pairs={{8,0},{12,4},{16,8},{20,12},{9,1},{13,5},{17,9},{21,13},{10,2},{14... | collective-permute-start | bytes 3145736 | tf_op jit(solution)/shard_map/ppermute | solution.py:31
  108.0 47.9 %collective-permute-start.11 = (bf16[512,1024]{1,0:T(8,128)(2,1)}, bf16[512,1024]{1,0:T(8,128)(2,1)}, u32[]{:S(2)}, u32[]{:S(2)}) collective-permute-start(bf16[512,1024]{1,0:T(8,128)(2,1)} %collective-permute-done.9.refs_2_), channel_id=1, source_target_pairs={{8,16},{12,20},{16,24},{20,28},{9,17},{13,21},{17,25},{21,29},{10,... | collective-permute-start | bytes 3145736 | tf_op jit(solution)/shard_map/ppermute | solution.py:31
  109.6 46.3 %collective-permute-start.13 = (bf16[512,1024]{1,0:T(8,128)(2,1)S(1)}, bf16[512,1024]{1,0:T(8,128)(2,1)}, u32[]{:S(2)}, u32[]{:S(2)}) collective-permute-start(bf16[512,1024]{1,0:T(8,128)(2,1)S(1)} %collective-permute-done.3.refs_2_), channel_id=1, source_target_pairs={{8,12},{12,8},{16,20},{20,16},{24,28},{28,24},{9,13},{13,9},{17,21... | collective-permute-start | bytes 3145736 | tf_op jit(solution)/shard_map/ppermute | solution.py:36
  112.1 43.8 %all-to-all-start.2 = ((bf16[8,8,2048]{2,1,0:T(8,128)(2,1)}), bf16[8,8,2048]{2,1,0:T(8,128)(2,1)S(1)}, u32[]{:S(2)}, u32[]{:S(2)}) async-start(bf16[8,8,2048]{2,1,0:T(8,128)(2,1)} %broadcast_in_dim.16), calls=%async_computation.2 | async-start | bytes 524288 | tf_op jit(solution)/shard_map/all_to_all | solution.py:339
  158.3 15.9 %copy-start.2 = (bf16[512,1024]{1,0:T(8,128)(2,1)S(1)}, bf16[512,1024]{1,0:T(8,128)(2,1)}, u32[]{:S(2)}) copy-start(bf16[512,1024]{1,0:T(8,128)(2,1)} %refs_0_.3) | copy-start | bytes 3145732
  158.3 31.3 %collective-permute-start.16 = (bf16[512,1024]{1,0:T(8,128)(2,1)}, bf16[512,1024]{1,0:T(8,128)(2,1)}, u32[]{:S(2)}, u32[]{:S(2)}) collective-permute-start(bf16[512,1024]{1,0:T(8,128)(2,1)} %broadcast_select_fusion.1.refs_2_), channel_id=1, source_target_pairs={{8,0},{12,4},{16,24},{20,28},{9,1},{13,5},{17,25},{21,29},{10,2},{... | collective-permute-start | bytes 3145736 | tf_op jit(solution)/shard_map/ppermute | solution.py:31
  159.7 23.2 %collective-permute-start.15 = (bf16[256,2048]{1,0:T(8,128)(2,1)}, bf16[256,2048]{1,0:T(8,128)(2,1)}, u32[]{:S(2)}, u32[]{:S(2)}) collective-permute-start(bf16[256,2048]{1,0:T(8,128)(2,1)} %collective-permute-done.4.here), channel_id=1, source_target_pairs={{0,1},{1,0},{2,3},{3,2},{4,5},{5,4},{6,7},{7,6},{8,9},{9,8},{10,11... | collective-permute-start | bytes 3145736 | tf_op jit(solution)/shard_map/ppermute | solution.py:298
  162.0 33.6 %all-to-all-start.3 = ((bf16[1,64,8,512]{3,1,0,2:T(8,128)(2,1)}), bf16[1,64,8,512]{3,1,0,2:T(8,128)(2,1)}, u32[]{:S(2)}, u32[]{:S(2)}) async-start(bf16[1,64,8,512]{3,1,0,2:T(8,128)(2,1)} %copy.15), calls=%async_computation.3 | async-start | bytes 1048576 | tf_op jit(solution)/shard_map/all_to_all | solution.py:359
  170.2 31.8 %collective-permute-start.17 = (bf16[512,1024]{1,0:T(8,128)(2,1)}, bf16[512,1024]{1,0:T(8,128)(2,1)}, u32[]{:S(2)}, u32[]{:S(2)}) collective-permute-start(bf16[512,1024]{1,0:T(8,128)(2,1)} %collective-permute-done.12.refs_0_.refs_4_), channel_id=1, source_target_pairs={{0,4},{4,0},{24,28},{28,24},{1,5},{5,1},{25,29},{29,25},{2,6},{6,2... | collective-permute-start | bytes 3145736 | tf_op jit(solution)/shard_map/ppermute | solution.py:36
  195.6 11.9 %collective-permute-start.18 = (bf16[256,512]{1,0:T(8,128)(2,1)}, bf16[256,512]{1,0:T(8,128)(2,1)S(1)}, u32[]{:S(2)}, u32[]{:S(2)}) collective-permute-start(bf16[256,512]{1,0:T(8,128)(2,1)} %copy-done.19), channel_id=1, source_target_pairs={{0,4},{4,0},{8,12},{12,8},{16,20},{20,16},{24,28},{28,24},{1,5},{5... | collective-permute-start | bytes 786440 | tf_op jit(solution)/shard_map/ppermute | solution.py:36
  211.0 22.0 %all-to-all-start.4 = ((f32[8,8,2048]{2,1,0:T(8,128)}), f32[8,8,2048]{2,1,0:T(8,128)}, u32[]{:S(2)}, u32[]{:S(2)}) async-start(f32[8,8,2048]{2,1,0:T(8,128)} %bitcast.40), calls=%async_computation.4 | async-start | bytes 1048576 | tf_op jit(solution)/shard_map/all_to_all | solution.py:421
  216.2 17.9 %collective-permute-start.19 = (bf16[8,64,512]{2,1,0:T(8,128)(2,1)}, bf16[8,64,512]{2,1,0:T(8,128)(2,1)}, u32[]{:S(2)}, u32[]{:S(2)}) collective-permute-start(bf16[8,64,512]{2,1,0:T(8,128)(2,1)} %bitcast.12), channel_id=1, source_target_pairs={{0,2},{1,3},{2,0},{3,1},{4,6},{5,7},{6,4},{7,5},{8,10},{9,11},{10,... | collective-permute-start | bytes 1572872 | tf_op jit(solution)/shard_map/ppermute | solution.py:298
  216.7 35.9 %collective-permute-start.20 = (bf16[256,1024]{1,0:T(8,128)(2,1)}, bf16[256,1024]{1,0:T(8,128)(2,1)}, u32[]{:S(2)}, u32[]{:S(2)}) collective-permute-start(bf16[256,1024]{1,0:T(8,128)(2,1)} %copy-done.17), channel_id=1, source_target_pairs={{0,4},{4,0},{8,12},{12,8},{16,20},{20,16},{24,28},{28,24},{1,5},{5... | collective-permute-start | bytes 1572872 | tf_op jit(solution)/shard_map/ppermute | solution.py:36
  218.7 35.3 %collective-permute-start.21 = (bf16[256,1024]{1,0:T(8,128)(2,1)}, bf16[256,1024]{1,0:T(8,128)(2,1)}, u32[]{:S(2)}, u32[]{:S(2)}) collective-permute-start(bf16[256,1024]{1,0:T(8,128)(2,1)} %copy-done.17), channel_id=1, source_target_pairs={{8,0},{12,4},{16,8},{20,12},{24,16},{28,20},{0,24},{4,28},{9,1},{1... | collective-permute-start | bytes 1572872 | tf_op jit(solution)/shard_map/ppermute | solution.py:31
  222.0 32.0 %collective-permute-start.22 = (bf16[256,1024]{1,0:T(8,128)(2,1)}, bf16[256,1024]{1,0:T(8,128)(2,1)}, u32[]{:S(2)}, u32[]{:S(2)}) collective-permute-start(bf16[256,1024]{1,0:T(8,128)(2,1)} %copy-done.17), channel_id=1, source_target_pairs={{24,0},{28,4},{0,8},{4,12},{8,16},{12,20},{16,24},{20,28},{25,1},{... | collective-permute-start | bytes 1572872 | tf_op jit(solution)/shard_map/ppermute | solution.py:31
  234.0 26.3 %copy-start.1 = (bf16[4,2,256,512]{3,2,1,0:T(8,128)(2,1)S(1)}, bf16[4,2,256,512]{3,2,1,0:T(8,128)(2,1)}, u32[]{:S(2)}) copy-start(bf16[4,2,256,512]{3,2,1,0:T(8,128)(2,1)} %shard_map.108.term) | copy-start | bytes 6291460
  236.4 23.9 %collective-permute-start.23 = (bf16[2,256,512]{2,1,0:T(8,128)(2,1)}, bf16[2,256,512]{2,1,0:T(8,128)(2,1)}, u32[]{:S(2)}, u32[]{:S(2)}) collective-permute-start(bf16[2,256,512]{2,1,0:T(8,128)(2,1)} %get-tuple-element.132), channel_id=1, source_target_pairs={{0,2},{1,3},{2,0},{3,1},{4,6},{5,7},{6,4},{7,5},{8,10},{9,11},{10,... | collective-permute-start | bytes 1572872 | tf_op jit(solution)/shard_map/ppermute | solution.py:298
  238.0 22.4 %collective-permute-start.24 = (bf16[2,256,512]{2,1,0:T(8,128)(2,1)}, bf16[2,256,512]{2,1,0:T(8,128)(2,1)}, u32[]{:S(2)}, u32[]{:S(2)}) collective-permute-start(bf16[2,256,512]{2,1,0:T(8,128)(2,1)} %get-tuple-element.131), channel_id=1, source_target_pairs={{0,3},{1,2},{2,1},{3,0},{4,7},{5,6},{6,5},{7,4},{8,11},{9,10},{10,... | collective-permute-start | bytes 1572872 | tf_op jit(solution)/shard_map/ppermute | solution.py:298
  238.7 21.7 %all-to-all-start.5 = ((bf16[8,8,2048]{2,1,0:T(8,128)(2,1)}), bf16[8,8,2048]{2,1,0:T(8,128)(2,1)S(1)}, u32[]{:S(2)}, u32[]{:S(2)}) async-start(bf16[8,8,2048]{2,1,0:T(8,128)(2,1)} %broadcast_in_dim.17), calls=%async_computation.5 | async-start | bytes 524288 | tf_op jit(solution)/shard_map/all_to_all | solution.py:339
  252.6 23.6 %collective-permute-start.25 = (bf16[2,8,64,512]{3,2,1,0:T(8,128)(2,1)}, bf16[2,8,64,512]{3,2,1,0:T(8,128)(2,1)}, u32[]{:S(2)}, u32[]{:S(2)}) collective-permute-start(bf16[2,8,64,512]{3,2,1,0:T(8,128)(2,1)} %pad_maximum_fusion.1.refs_0_), channel_id=1, source_target_pairs={{0,1},{1,0},{2,3},{3,2},{4,5},{5,4},{6,7},{7,6},{8,9},{9,8},{10,11... | collective-permute-start | bytes 3145736 | tf_op jit(solution)/shard_map/ppermute | solution.py:298
  260.3 10.1 %copy-start.20 = (bf16[512,1024]{1,0:T(8,128)(2,1)S(1)}, bf16[512,1024]{1,0:T(8,128)(2,1)}, u32[]{:S(2)}) copy-start(bf16[512,1024]{1,0:T(8,128)(2,1)} %param.13) | copy-start | bytes 3145732
  261.2 15.1 %collective-permute-start.26 = (bf16[2,256,512]{2,1,0:T(8,128)(2,1)}, bf16[2,256,512]{2,1,0:T(8,128)(2,1)}, u32[]{:S(2)}, u32[]{:S(2)}) collective-permute-start(bf16[2,256,512]{2,1,0:T(8,128)(2,1)} %slice_bitcast_fusion), channel_id=1, source_target_pairs={{0,1},{1,0},{2,3},{3,2},{4,5},{5,4},{6,7},{7,6},{8,9},{9,8},{10,11... | collective-permute-start | bytes 1572872 | tf_op jit(solution)/shard_map/ppermute | solution.py:298
  261.3 15.1 %collective-permute-start.27 = (bf16[256,1024]{1,0:T(8,128)(2,1)}, bf16[256,1024]{1,0:T(8,128)(2,1)}, u32[]{:S(2)}, u32[]{:S(2)}) collective-permute-start(bf16[256,1024]{1,0:T(8,128)(2,1)} %collective-permute-done.21.refs_3_), channel_id=1, source_target_pairs={{0,4},{4,0},{8,12},{12,8},{16,20},{20,16},{24,28},{28,24},{1,5},{5... | collective-permute-start | bytes 1572872 | tf_op jit(solution)/shard_map/ppermute | solution.py:36
  262.8 24.3 %collective-permute-start.28 = (bf16[256,1024]{1,0:T(8,128)(2,1)}, bf16[256,1024]{1,0:T(8,128)(2,1)}, u32[]{:S(2)}, u32[]{:S(2)}) collective-permute-start(bf16[256,1024]{1,0:T(8,128)(2,1)} %collective-permute-done.22.refs_5_), channel_id=1, source_target_pairs={{0,4},{4,0},{8,12},{12,8},{16,20},{20,16},{24,28},{28,24},{1,5},{5... | collective-permute-start | bytes 1572872 | tf_op jit(solution)/shard_map/ppermute | solution.py:36
  263.4 29.7 %collective-permute-start.29 = (bf16[256,1024]{1,0:T(8,128)(2,1)}, bf16[256,1024]{1,0:T(8,128)(2,1)}, u32[]{:S(2)}, u32[]{:S(2)}) collective-permute-start(bf16[256,1024]{1,0:T(8,128)(2,1)} %copy-done.17), channel_id=1, source_target_pairs={{16,0},{20,4},{24,8},{28,12},{0,16},{4,20},{8,24},{12,28},{17,1},{... | collective-permute-start | bytes 1572872 | tf_op jit(solution)/shard_map/ppermute | solution.py:31
  293.1 13.0 %collective-permute-start.32 = (bf16[256,1024]{1,0:T(8,128)(2,1)}, bf16[256,1024]{1,0:T(8,128)(2,1)}, u32[]{:S(2)}, u32[]{:S(2)}) collective-permute-start(bf16[256,1024]{1,0:T(8,128)(2,1)} %collective-permute-done.29.refs_4_), channel_id=1, source_target_pairs={{0,4},{4,0},{8,12},{12,8},{16,20},{20,16},{24,28},{28,24},{1,5},{5... | collective-permute-start | bytes 1572872 | tf_op jit(solution)/shard_map/ppermute | solution.py:36
  293.4 9.4 %collective-permute-start.30 = (bf16[8,512]{1,0:T(8,128)(2,1)S(1)}, bf16[8,512]{1,0:T(8,128)(2,1)S(1)}, u32[]{:S(2)}, u32[]{:S(2)}) collective-permute-start(bf16[8,512]{1,0:T(8,128)(2,1)S(1)} %get-tuple-element.135), channel_id=1, source_target_pairs={{0,0},{1,8},{2,16},{3,24},{4,4},{5,12},{6,20},{7,28},{8,1},{9,9},{... | collective-permute-start | bytes 24584 | tf_op jit(solution)/shard_map/ppermute | solution.py:264
  295.5 7.3 %collective-permute-start.31 = (bf16[8,512]{1,0:T(8,128)(2,1)S(1)}, bf16[8,512]{1,0:T(8,128)(2,1)S(1)}, u32[]{:S(2)}, u32[]{:S(2)}) collective-permute-start(bf16[8,512]{1,0:T(8,128)(2,1)S(1)} %get-tuple-element.136), channel_id=1, source_target_pairs={{0,4},{1,12},{2,20},{3,28},{4,0},{5,8},{6,16},{7,24},{8,5},{9,13},... | collective-permute-start | bytes 24584 | tf_op jit(solution)/shard_map/ppermute | solution.py:264
  (15 other events, 24.7 us)

commit v8 on v7

--- a/solution.py
+++ b/solution.py
@@ -139,11 +139,10 @@
             ]
 
 
-def grad_kernel(line, which, parts, place, live, here, there, *refs):
+def grad_kernel(line, which, parts, place, live, mine, by_core, by_y, by_both, *refs):
     before, refs = refs[:parts], refs[parts:]
     weights, outs = refs[: len(which)], refs[len(which) :]
-    half = line.n_dp // 2
-    core = place[2] % 2
+    cut = line.n_dp // 4
     keep, send = outs[-2:]
     keep[...] = before[0][...] if parts else jnp.zeros_like(keep)
     send[...] = before[1][...] if parts else jnp.zeros_like(send)
@@ -152,8 +151,11 @@
         own_width = weights[j].shape[1] // 2
         weight = weights[j][:, e * own_width : (e + 1) * own_width]
         keep[...] += matmul(live[:, columns(index, own_width)], weight, BACK)
-        inner = columns(lax.rem(index, half), own_width)
-        other = jnp.where(lax.div(index, half) == core, here[:, inner], there[:, inner])
+        inner = columns(lax.rem(index, cut), own_width)
+        member = lax.bitwise_xor(lax.div(index, cut), place[2])
+        other = mine[:, inner]
+        for at, piece in ((1, by_core), (2, by_y), (3, by_both)):
+            other = jnp.where(member == at, piece[:, inner], other)
         send[...] += matmul(other, weight, BACK)
 
     each_block(line, place, line.n_z == 4, which, add)
@@ -284,8 +286,8 @@
     n_dp = line.n_dp
     n_tensor = lax.axis_size("tensor")
     dp_at, tensor_at = lax.axis_index("dp"), lax.axis_index("tensor")
-    x, core = dp_at % 2, tensor_at % 2
-    place = jnp.stack([dp_at // 2, x, tensor_at % 4, tensor_at]).astype(jnp.int32)
+    x, quarter = dp_at % 2, tensor_at % 4
+    place = jnp.stack([dp_at // 2, x, quarter, tensor_at]).astype(jnp.int32)
     rows = samples * tok_rows
     image_rows = samples * image_own
     images = n_dp * image_rows
@@ -307,21 +309,29 @@
     gate = lax.optimization_barrier
 
     relayed = line.n_z == 4
+    wq_moved = line.first(query_weight)
     image_cols = lax.all_to_all(image_flat, "dp", split_axis=1, concat_axis=0, tiled=True)
     wo_keep = lax.dynamic_slice_in_dim(out_weight, x * half_cols, half_cols, 0)
     wo_send = lax.dynamic_slice_in_dim(out_weight, (1 - x) * half_cols, half_cols, 0)
-    live_half = lax.dynamic_slice_in_dim(live_flat, core * (width // 2), width // 2, 1)
-    wq_moved = line.first(query_weight)
     wo_pair = jnp.concatenate([wo_keep, line.swap(wo_send)], axis=1)
-    image_cols, wo_pair, live_half, wq_other, *wq_moved = gate(
-        (image_cols, wo_pair, live_half, line.swap(query_weight), *wq_moved)
+    quarter_cols = width // 4
+    live_part = lax.dynamic_slice_in_dim(live_flat, quarter * quarter_cols, quarter_cols, 1)
+    live_here = line.swap(live_part)
+    quarter_rows = rows // 4
+    live_rows = lax.dynamic_slice_in_dim(live_flat, quarter * quarter_rows, quarter_rows, 0)
+    live_mine = lax.all_to_all(
+        live_rows.reshape(quarter_rows, n_dp, own_width), "dp", split_axis=1, concat_axis=0
+    )
+    live_mine = live_mine.reshape(n_dp, quarter_rows, own_width)
+    image_cols, wo_pair, live_here, live_mine, query_weight, *wq_moved = gate(
+        (image_cols, wo_pair, live_here, live_mine, query_weight, *wq_moved)
     )
 
     n_moved = len(wq_moved)
     planes = [(0, 1, 2), (1, 2, 3)] if relayed else [None] * n_moved
     wq_two = line.second(wq_moved)
     wo_moved = line.first(wo_pair)
-    above, live_here = gate((wq_moved[0], line.swap(live_half)))
+    above, wq_other = gate((wq_moved[0], line.swap(query_weight)))
     wq_others = [wq_other, line.swap(above, planes[0])]
     part_kv = jnp.concatenate(
         [matmul(image_cols, key_weight), matmul(image_cols, value_weight)], axis=1
@@ -342,22 +352,19 @@
     wo_two = line.second(wo_moved)
     wq_others += [line.swap(block, at) for block, at in zip(wq_moved[1:], planes[1:])]
     wq_others += [line.swap(block) for block in wq_last[:1]]
+    kv_own, *wq_edge = gate((kv_own, *wq_last[1:]))
     kv_all = everywhere(kv_own).reshape(images, 2 * local_cols)
+    edge_other = [line.swap(block, (0, 3)) for block in wq_edge]
     kv_all, live_here, wo_pair, live_flat, *staged = gate(
-        (kv_all, live_here, wo_pair, live_flat, *wo_two, *wq_last, *wq_others)
+        (kv_all, live_here, wo_pair, live_flat, *wo_two, *wq_edge, *wq_others)
     )
     wo_two, staged = staged[: len(wo_two)], staged[len(wo_two) :]
-    wq_last, wq_others = staged[: len(wq_last)], staged[len(wq_last) :]
+    wq_last[1:], wq_others = staged[: len(wq_edge)], staged[len(wq_edge) :]
 
     wo_last = line.third(wo_two)
-    wq_others += [line.swap(block, (0, 3)) for block in wq_last[1:]]
-    live_there = tensor_swap(live_here, 1)
-    quarter_rows = rows // 4
-    live_part = lax.dynamic_slice_in_dim(
-        live_flat, (tensor_at % 4) * quarter_rows, quarter_rows, 0
-    ).reshape(quarter_rows, n_dp, own_width)
-    live_mine = lax.all_to_all(live_part, "dp", split_axis=1, concat_axis=0)
-    live_mine = live_mine.reshape(n_dp, quarter_rows, own_width)
+    by_y = tensor_swap(live_here, 2)
+    live_pieces = [live_here, tensor_swap(live_here, 1), by_y, tensor_swap(by_y, 1)]
+    wq_others += edge_other
     arrivals = [query_weight, *wq_moved, *wq_last]
     early = range(4 if relayed else len(arrivals))
     late = range(len(early), len(arrivals))
@@ -374,7 +381,7 @@
     grad_parts = call(
         functools.partial(grad_kernel, line, range(len(wo_early)), 0),
         place,
-        (live_flat, live_here, live_there, *wo_early),
+        (live_flat, *live_pieces, *wo_early),
         [half] * 2,
         (),
         rows * width * local_cols,
@@ -386,7 +393,7 @@
     grad_keep, grad_send = call(
         functools.partial(grad_kernel, line, wo_late, 2),
         place,
-        (live_flat, live_here, live_there, *grad_parts, *wo_last),
+        (live_flat, *live_pieces, *grad_parts, *wo_last),
         [shape((rows, half_cols), BF16)] * 2,
         [pltpu.VMEM((rows, half_cols), F32)] * 2,
         rows * width * local_cols,
@@ -428,18 +435,17 @@
         (),
         2 * rows * width * local_cols,
     )
-    kv_grad, term, live_y = gate((kv_grad.astype(BF16), term, live_y))
+    kv_grad, term, live_mine, live_y = gate((kv_grad.astype(BF16), term, live_mine, live_y))
+    kv_grad_all = everywhere(kv_grad).reshape(images, 2 * local_cols)
+    live_pair = jnp.stack([live_mine, live_y])
 
     text_parts = [tensor_swap(term[k], k) for k in range(2, n_tensor)]
-    live_pair = jnp.stack([live_mine, live_y])
-    kv_grad_all = everywhere(kv_grad).reshape(images, 2 * local_cols)
-    kv_grad_all, term, attended, att_swapped, *staged = gate(
-        (kv_grad_all, term, attended, att_swapped, *att_next, *text_parts)
-    )
-    att_next, text_parts = staged[:2], staged[2:]
-
+    attended, att_swapped, *att_next = gate((attended, att_swapped, *att_next))
     att_far = [line.shift(attended, m) for m in range(2, line.n_z - 1)]
     att_other_next = [line.swap(block) for block in att_next]
+    kv_grad_all, live_pair, *staged = gate((kv_grad_all, live_pair, *text_parts, *att_far))
+    text_parts, att_far = staged[: n_tensor - 2], staged[n_tensor - 2 :]
+
     live_core = tensor_swap(live_pair, 1)
     text_parts.append(tensor_swap(term[1], 1))
     image_term = matmul(kv_grad_all[:, :local_cols], key_weight, BACK)

time: 317 us -> 342 us (1.079)
  waiting for transfers between devices: 122 us -> 172 us
  starting transfers between devices: 106 us -> 84.7 us
  local copies, waits for them, and re-layouts: 24.4 us -> 19.1 us
    ppermute x13, waiting for transfers between devices: 8.17 us -> 68.1 us  [move(): return lax.ppermute(block, 'dp', pairs)]
    all_to_all x2, waiting for transfers between devices: 37.8 us -> 3.96 us  [everywhere(): return lax.all_to_all(copies, 'dp', split_axis=0, concat_axis=0)]
    all_to_all x2, starting transfers between devices: 24 us -> 11.5 us  [everywhere(): return lax.all_to_all(copies, 'dp', split_axis=0, concat_axis=0)]
    all_to_all x1, waiting for transfers between devices: 0.01 us -> 12.5 us  [shards(): lax.all_to_all(image_flat, 'dp', split_axis=1, concat_axis=0, tiled=True)]
    ppermute x12, waiting for transfers between devices: 46.5 us -> 55.4 us  [swap(): return lax.ppermute(block, 'dp', pairs)]
    ppermute x6 -> x8, waiting for transfers between devices: 0.02 us -> 3.68 us  [tensor_swap(): lax.ppermute(block, 'tensor', [(t, t ^ bit) for t in range(n_tensor)])]
    unnamed x49 -> x31, local copies, waits for them, and re-layouts: 12.4 us -> 9.34 us
  transfers between devices with their start and end apart: 39 -> 41, of which waited for: 11 -> 20; matrix products, arithmetic and copies ran while one was open for 8% -> 8% of each run, Pallas kernels for 9% -> 9%
where the time goes in v8:
time: 342 us; the launch traced here: 339 us
  waiting for transfers between devices  172 us (50%)
  starting transfers between devices  84.7 us (25%)
  Pallas kernels  37.5 us (11%)
  local copies, waits for them, and re-layouts  19.1 us (6%)
  other arithmetic  15.9 us (5%)
  blocking collectives  5.4 us (2%)
  matrix products  3.93 us (1%)
    ppermute x13, waiting for transfers between devices, move(): return lax.ppermute(block, 'dp', pairs)  68.1 us
    ppermute x12, waiting for transfers between devices, swap(): return lax.ppermute(block, 'dp', pairs)  55.4 us
    pallas_call x8, Pallas kernels, call(): pl.pallas_call(kernel, out_shape=outs[0] if single else outs, in_specs=[p...  37.5 us
    ppermute x13, starting transfers between devices, move(): return lax.ppermute(block, 'dp', pairs)  28 us
    all_to_all x1, waiting for transfers between devices, shards(): lax.all_to_all(part_kv, 'dp', split_axis=0, concat_axis=0)  27.7 us
    ppermute x12, starting transfers between devices, swap(): return lax.ppermute(block, 'dp', pairs)  18.8 us
    all_to_all x1, waiting for transfers between devices, shards(): lax.all_to_all(image_flat, 'dp', split_axis=1, concat_axis=0, tiled=True)  12.5 us
    all_to_all x2, starting transfers between devices, everywhere(): return lax.all_to_all(copies, 'dp', split_axis=0, concat_axis=0)  11.5 us
  transfers between devices with their start and end apart: 41, of which 20 were waited for; matrix products, arithmetic and copies ran while one was open for 8% of the time, Pallas kernels for 9%

profile of v8, /device:TPU:4, one launch (start us, length us, event | category | flops | bytes accessed | tf_op | source)
XLA Modules:
  0.0 339.3 jit_solution(7754849385386250983)
XLA Ops:
  2.1 5.5 %collective-permute-start.3 = (bf16[512,1024]{1,0:T(8,128)(2,1)}, bf16[512,1024]{1,0:T(8,128)(2,1)}, u32[]{:S(2)}, u32[]{:S(2)}) collective-permute-start(bf16[512,1024]{1,0:T(8,128)(2,1)} %refs_0_.1), channel_id=1, source_target_pairs={{0,8},{4,12},{8,16},{12,20},{16,24},{20,28},{1,9},{5,13},{9,17},{1... | collective-permute-start | bytes 3145736 | tf_op jit(solution)/shard_map/ppermute | solution.py:31
  9.1 3.9 %all-to-all-start = ((bf16[8,8,512]{2,0,1:T(8,128)(2,1)}), bf16[8,8,512]{2,0,1:T(8,128)(2,1)S(1)}, u32[]{:S(2)}, u32[]{:S(2)}) async-start(bf16[8,8,512]{2,0,1:T(8,128)(2,1)} %copy.14), calls=%async_computation | async-start | bytes 131072 | tf_op jit(solution)/shard_map/all_to_all | solution.py:313
  13.8 3.1 broadcast_select_fusion
  19.2 12.5 %all-to-all-done = bf16[8,8,512]{2,0,1:T(8,128)(2,1)S(1)} async-done(((bf16[8,8,512]{2,0,1:T(8,128)(2,1)}), bf16[8,8,512]{2,0,1:T(8,128)(2,1)S(1)}, u32[]{:S(2)}, u32[]{:S(2)}) %all-to-all-start) | async-done | bytes 65568 | tf_op jit(solution)/shard_map/all_to_all | solution.py:313
  31.7 5.3 %all-to-all-start.1 = ((bf16[1,64,8,512]{3,1,0,2:T(8,128)(2,1)}), bf16[1,64,8,512]{3,1,0,2:T(8,128)(2,1)}, u32[]{:S(2)}, u32[]{:S(2)}) async-start(bf16[1,64,8,512]{3,1,0,2:T(8,128)(2,1)} %copy.15), calls=%async_computation.1 | async-start | bytes 1048576 | tf_op jit(solution)/shard_map/all_to_all | solution.py:322
  38.0 2.0 collective-permute-start
  41.3 15.2 %collective-permute-done = bf16[512,512]{1,0:T(8,128)(2,1)} collective-permute-done((bf16[512,512]{1,0:T(8,128)(2,1)}, bf16[512,512]{1,0:T(8,128)(2,1)}, u32[]{:S(2)}, u32[]{:S(2)}) %collective-permute-start) | collective-permute-done | bytes 524320 | tf_op jit(solution)/shard_map/ppermute | solution.py:36
  56.5 2.3 pad_maximum_fusion.refs_0_
  58.8 7.5 %collective-permute-done.1.mine = bf16[256,1024]{1,0:T(8,128)(2,1)} collective-permute-done((bf16[256,1024]{1,0:T(8,128)(2,1)S(1)}, bf16[256,1024]{1,0:T(8,128)(2,1)}, u32[]{:S(2)}, u32[]{:S(2)}) %collective-permute-start.1) | collective-permute-done | bytes 524320 | tf_op jit(solution)/shard_map/ppermute | solution.py:36
  68.7 5.6 %collective-permute-start.9 = (bf16[512,1024]{1,0:T(8,128)(2,1)}, bf16[512,1024]{1,0:T(8,128)(2,1)}, u32[]{:S(2)}, u32[]{:S(2)}) collective-permute-start(bf16[512,1024]{1,0:T(8,128)(2,1)} %pad_maximum_fusion.refs_0_), channel_id=1, source_target_pairs={{0,8},{4,12},{8,16},{12,20},{16,24},{20,28},{1,9},{5,13},{9,17},{1... | collective-permute-start | bytes 3145736 | tf_op jit(solution)/shard_map/ppermute | solution.py:31
  79.1 11.1 %collective-permute-done.4.refs_4_.refs_5_ = bf16[512,1024]{1,0:T(8,128)(2,1)S(1)} collective-permute-done((bf16[512,1024]{1,0:T(8,128)(2,1)S(1)}, bf16[512,1024]{1,0:T(8,128)(2,1)S(1)}, u32[]{:S(2)}, u32[]{:S(2)}) %collective-permute-start.4) | collective-permute-done | bytes 1048608 | tf_op jit(solution)/shard_map/ppermute | solution.py:36
  91.2 3.2 collective-permute-start.5
  95.3 4.2 %all-to-all-start.2 = ((f32[8,8,2048]{2,1,0:T(8,128)}), f32[8,8,2048]{2,1,0:T(8,128)}, u32[]{:S(2)}, u32[]{:S(2)}) async-start(f32[8,8,2048]{2,1,0:T(8,128)} %maximum_bitcast_fusion), calls=%async_computation.2 | async-start | bytes 1048576 | tf_op jit(solution)/shard_map/all_to_all | solution.py:340
  99.4 27.7 %all-to-all-done.2 = f32[8,8,2048]{2,1,0:T(8,128)} async-done(((f32[8,8,2048]{2,1,0:T(8,128)}), f32[8,8,2048]{2,1,0:T(8,128)}, u32[]{:S(2)}, u32[]{:S(2)}) %all-to-all-start.2) | async-done | bytes 524320 | tf_op jit(solution)/shard_map/all_to_all | solution.py:340
  130.9 1.8 collective-permute-start.14
  137.4 20.4 %collective-permute-done.10.refs_0_.refs_4_ = bf16[512,1024]{1,0:T(8,128)(2,1)} collective-permute-done((bf16[512,1024]{1,0:T(8,128)(2,1)S(1)}, bf16[512,1024]{1,0:T(8,128)(2,1)}, u32[]{:S(2)}, u32[]{:S(2)}) %collective-permute-start.10) | collective-permute-done | bytes 1048608 | tf_op jit(solution)/shard_map/ppermute | solution.py:31
  158.4 7.0 %all-to-all-start.3 = ((bf16[8,8,2048]{2,1,0:T(8,128)(2,1)}), bf16[8,8,2048]{2,1,0:T(8,128)(2,1)S(1)}, u32[]{:S(2)}, u32[]{:S(2)}) async-start(bf16[8,8,2048]{2,1,0:T(8,128)(2,1)} %broadcast_in_dim.16), calls=%async_computation.3 | async-start | bytes 524288 | tf_op jit(solution)/shard_map/all_to_all | solution.py:349
  165.5 14.5 %collective-permute-done.11 = bf16[512,1024]{1,0:T(8,128)(2,1)} collective-permute-done((bf16[512,1024]{1,0:T(8,128)(2,1)}, bf16[512,1024]{1,0:T(8,128)(2,1)}, u32[]{:S(2)}, u32[]{:S(2)}) %collective-permute-start.11) | collective-permute-done | bytes 1048608 | tf_op jit(solution)/shard_map/ppermute | solution.py:31
  182.0 2.3 broadcast_select_fusion.1.refs_2_
  185.6 2.1 collective-permute-start.19
  187.8 3.7 %collective-permute-done.16.by_y = bf16[256,1024]{1,0:T(8,128)(2,1)} collective-permute-done((bf16[256,1024]{1,0:T(8,128)(2,1)}, bf16[256,1024]{1,0:T(8,128)(2,1)}, u32[]{:S(2)}, u32[]{:S(2)}) %collective-permute-start.16) | collective-permute-done | bytes 524320 | tf_op jit(solution)/shard_map/ppermute | solution.py:300
  192.8 5.5 %shard_map.103.part = f32[256,1024]{1,0:T(8,128)S(1)} custom-call(s32[4]{0:T(128)S(1)} %pad_add_fusion.place, bf16[256,4096]{1,0:T(8,128)(2,1)} %bitcast.41, bf16[512,1024]{1,0:T(8,128)(2,1)S(1)} %copy-done.2, bf16[512,1024]{1,0:T(8,128)(2,1)S(1)} %copy-done.4, bf16[512,1024]{1,0:T(8,128)(2,1)} %collective-permute-done.3.refs_2_, ...), custom_call_target="tpu_custom_call" | custom-call | flops 2147483648 | bytes 11534336 | tf_op jit(solution)/shard_map/pallas_call | solution.py:228
  198.3 4.6 %shard_map.104 = (f32[256,512]{1,0:T(8,128)S(1)}, f32[256,512]{1,0:T(8,128)S(1)}) custom-call(s32[4]{0:T(128)S(1)} %pad_add_fusion.place, bf16[256,4096]{1,0:T(8,128)(2,1)} %bitcast.7.live, bf16[256,1024]{1,0:T(8,128)(2,1)} %collective-permute-done.1.mine, bf16[256,1024]{1,0:T(8,128)(2,1)} %collective-permute-done.15.by_core, ...), custom_call_target="tpu_custom_call" | custom-call | flops 1073741824 | bytes 8388608 | tf_op jit(solution)/shard_map/pallas_call | solution.py:228
  202.9 4.2 %collective-permute-done.18.refs_3_ = bf16[512,1024]{1,0:T(8,128)(2,1)} collective-permute-done((bf16[512,1024]{1,0:T(8,128)(2,1)}, bf16[512,1024]{1,0:T(8,128)(2,1)}, u32[]{:S(2)}, u32[]{:S(2)}) %collective-permute-start.18) | collective-permute-done | bytes 1048608 | tf_op jit(solution)/shard_map/ppermute | solution.py:31
  207.1 4.6 %shard_map.105 = (bf16[256,512]{1,0:T(8,128)(2,1)S(1)}, bf16[256,512]{1,0:T(8,128)(2,1)S(1)}) custom-call(s32[4]{0:T(128)S(1)} %pad_add_fusion.place, bf16[256,4096]{1,0:T(8,128)(2,1)} %bitcast.7.live, bf16[256,1024]{1,0:T(8,128)(2,1)} %collective-permute-done.1.mine, bf16[256,1024]{1,0:T(8,128)(2,1)} %collective-permute-done.15.by_core, ...), custom_call_target="tpu_custom_call" | custom-call | flops 1073741824 | bytes 7864320 | tf_op jit(solution)/shard_map/pallas_call | solution.py:228
  212.0 5.0 %shard_map.106 = (bf16[256,1024]{1,0:T(8,128)(2,1)S(1)}, bf16[256,1024]{1,0:T(8,128)(2,1)}) custom-call(s32[4]{0:T(128)S(1)} %pad_add_fusion.place, bf16[256,4096]{1,0:T(8,128)(2,1)} %bitcast.42, bf16[64,2048]{1,0:T(8,128)(2,1)S(1)} %bitcast.38, f32[256,1024]{1,0:T(8,128)S(1)} %shard_map.103.part, bf16[512,1024]{1,0:T(8,128)(2,1)} %collective-permute-done.10.refs_0_.refs_4_, ...), custom_call_target="tpu_custom_call" | custom-call | flops 1073741824 | bytes 6553600 | tf_op jit(solution)/shard_map/pallas_call | solution.py:228
  218.2 1.9 shard_map.107
  221.6 5.4 %all-to-all-start.4 = ((f32[8,8,2048]{2,1,0:T(8,128)}), f32[8,8,2048]{2,1,0:T(8,128)}, u32[]{:S(2)}, u32[]{:S(2)}) async-start(f32[8,8,2048]{2,1,0:T(8,128)} %bitcast.40), calls=%async_computation.4 | async-start | bytes 1048576 | tf_op jit(solution)/shard_map/all_to_all | solution.py:428
  227.0 2.0 collective-permute-start.24
  229.1 3.3 collective-permute-start.25
  236.1 7.8 %shard_map.108.term = bf16[4,2,256,512]{3,2,1,0:T(8,128)(2,1)} custom-call(s32[4]{0:T(128)S(1)} %pad_add_fusion.place, bf16[256,1024]{1,0:T(8,128)(2,1)S(1)} %copy-done.9, bf16[512,1024]{1,0:T(8,128)(2,1)S(1)} %copy-done.2, bf16[512,1024]{1,0:T(8,128)(2,1)S(1)} %copy-done.5, bf16[512,1024]{1,0:T(8,128)(2,1)} %collective-permute-done.3.refs_2_, ...), custom_call_target="tpu_custom_call" | custom-call | flops 2147483648 | bytes 13107200 | tf_op jit(solution)/shard_map/pallas_call | solution.py:228
  245.6 3.3 collective-permute-done.25.refs_3_
  249.0 11.9 %collective-permute-done.26.refs_5_ = bf16[256,1024]{1,0:T(8,128)(2,1)} collective-permute-done((bf16[256,1024]{1,0:T(8,128)(2,1)}, bf16[256,1024]{1,0:T(8,128)(2,1)}, u32[]{:S(2)}, u32[]{:S(2)}) %collective-permute-start.26) | collective-permute-done | bytes 524320 | tf_op jit(solution)/shard_map/ppermute | solution.py:31
  260.9 2.5 collective-permute-start.27
  264.4 2.5 slice_bitcast_fusion
  267.7 4.4 %all-to-all-start.5 = ((bf16[8,8,2048]{2,1,0:T(8,128)(2,1)}), bf16[8,8,2048]{2,1,0:T(8,128)(2,1)S(1)}, u32[]{:S(2)}, u32[]{:S(2)}) async-start(bf16[8,8,2048]{2,1,0:T(8,128)(2,1)} %broadcast_in_dim.17), calls=%async_computation.5 | async-start | bytes 524288 | tf_op jit(solution)/shard_map/all_to_all | solution.py:349
  272.2 2.4 pad_maximum_fusion.1.refs_0_
  274.6 13.8 %collective-permute-done.27.refs_4_ = bf16[256,1024]{1,0:T(8,128)(2,1)} collective-permute-done((bf16[256,1024]{1,0:T(8,128)(2,1)}, bf16[256,1024]{1,0:T(8,128)(2,1)}, u32[]{:S(2)}, u32[]{:S(2)}) %collective-permute-start.27) | collective-permute-done | bytes 524320 | tf_op jit(solution)/shard_map/ppermute | solution.py:31
  288.3 2.5 all-to-all-done.5
  290.8 2.5 collective-permute-start.30
  295.6 5.4 %all_to_all.59 = bf16[4,16,512]{2,1,0:T(8,128)(2,1)S(1)} all-to-all(bf16[4,16,512]{2,1,0:T(8,128)(2,1)S(1)} %bitcast.50), channel_id=1, replica_groups=mesh['dp'=8,'tensor'=4] {'tensor'}, dimensions={0} | all-to-all | bytes 131072 | tf_op jit(solution)/shard_map/all_to_all | solution.py:250
  301.0 5.4 %collective-permute-done.30.refs_7_ = bf16[256,1024]{1,0:T(8,128)(2,1)} collective-permute-done((bf16[256,1024]{1,0:T(8,128)(2,1)}, bf16[256,1024]{1,0:T(8,128)(2,1)}, u32[]{:S(2)}, u32[]{:S(2)}) %collective-permute-start.30) | collective-permute-done | bytes 524320 | tf_op jit(solution)/shard_map/ppermute | solution.py:36
  306.4 11.0 %collective-permute-done.31.refs_9_ = bf16[256,1024]{1,0:T(8,128)(2,1)} collective-permute-done((bf16[256,1024]{1,0:T(8,128)(2,1)}, bf16[256,1024]{1,0:T(8,128)(2,1)}, u32[]{:S(2)}, u32[]{:S(2)}) %collective-permute-start.31) | collective-permute-done | bytes 524320 | tf_op jit(solution)/shard_map/ppermute | solution.py:36
  319.1 1.9 collective-permute-start.32
  321.0 3.6 %collective-permute-start.33 = (bf16[8,512]{1,0:T(8,128)(2,1)S(1)}, bf16[8,512]{1,0:T(8,128)(2,1)S(1)}, u32[]{:S(2)}, u32[]{:S(2)}) collective-permute-start(bf16[8,512]{1,0:T(8,128)(2,1)S(1)} %get-tuple-element.145), channel_id=1, source_target_pairs={{0,4},{1,12},{2,20},{3,28},{4,0},{5,8},{6,16},{7,24},{8,5},{9,13},... | collective-permute-start | bytes 24584 | tf_op jit(solution)/shard_map/ppermute | solution.py:266
  324.6 2.4 shard_map.109
  328.1 3.2 collective-permute-done.34.refs_8_
  333.6 5.7 %shard_map.110 = bf16[1024,512]{1,0:T(8,128)(2,1)} custom-call(s32[4]{0:T(128)S(1)} %pad_add_fusion.place, bf16[2,8,64,512]{3,2,1,0:T(8,128)(2,1)S(1)} %copy-done.7, bf16[2,8,64,512]{3,2,1,0:T(8,128)(2,1)} %collective-permute-done.28.refs_1_, bf16[256,1024]{1,0:T(8,128)(2,1)} %get-tuple-element.122.refs_2_, ...), custom_call_target="tpu_custom_call" | custom-call | flops 2147483648 | bytes 7340032 | tf_op jit(solution)/shard_map/pallas_call | solution.py:228
  (103 shorter events, 48.7 us)
Async XLA Ops:
  0.6 78.2 %copy-start = (bf16[512,1024]{1,0:T(8,128)(2,1)S(1)}, bf16[512,1024]{1,0:T(8,128)(2,1)}, u32[]{:S(2)}) copy-start(bf16[512,1024]{1,0:T(8,128)(2,1)} %param.14) | copy-start | bytes 3145732
  0.6 65.7 %collective-permute-start.2 = (bf16[512,1024]{1,0:T(8,128)(2,1)}, bf16[512,1024]{1,0:T(8,128)(2,1)S(1)}, u32[]{:S(2)}, u32[]{:S(2)}) collective-permute-start(bf16[512,1024]{1,0:T(8,128)(2,1)} %refs_0_.1), channel_id=1, source_target_pairs={{8,0},{12,4},{16,8},{20,12},{24,16},{28,20},{9,1},{13,5},{17,9},{2... | collective-permute-start | bytes 3145736 | tf_op jit(solution)/shard_map/ppermute | solution.py:31
  2.1 64.3 %collective-permute-start.3 = (bf16[512,1024]{1,0:T(8,128)(2,1)}, bf16[512,1024]{1,0:T(8,128)(2,1)}, u32[]{:S(2)}, u32[]{:S(2)}) collective-permute-start(bf16[512,1024]{1,0:T(8,128)(2,1)} %refs_0_.1), channel_id=1, source_target_pairs={{0,8},{4,12},{8,16},{12,20},{16,24},{20,28},{1,9},{5,13},{9,17},{1... | collective-permute-start | bytes 3145736 | tf_op jit(solution)/shard_map/ppermute | solution.py:31
  9.1 22.6 %all-to-all-start = ((bf16[8,8,512]{2,0,1:T(8,128)(2,1)}), bf16[8,8,512]{2,0,1:T(8,128)(2,1)S(1)}, u32[]{:S(2)}, u32[]{:S(2)}) async-start(bf16[8,8,512]{2,0,1:T(8,128)(2,1)} %copy.14), calls=%async_computation | async-start | bytes 131072 | tf_op jit(solution)/shard_map/all_to_all | solution.py:313
  16.9 20.1 %copy-start.14 = (bf16[1024,512]{1,0:T(8,128)(2,1)S(1)}, bf16[1024,512]{1,0:T(8,128)(2,1)}, u32[]{:S(2)}) copy-start(bf16[1024,512]{1,0:T(8,128)(2,1)} %param.15) | copy-start | bytes 3145732
  31.7 34.6 %all-to-all-start.1 = ((bf16[1,64,8,512]{3,1,0,2:T(8,128)(2,1)}), bf16[1,64,8,512]{3,1,0,2:T(8,128)(2,1)}, u32[]{:S(2)}, u32[]{:S(2)}) async-start(bf16[1,64,8,512]{3,1,0,2:T(8,128)(2,1)} %copy.15), calls=%async_computation.1 | async-start | bytes 1048576 | tf_op jit(solution)/shard_map/all_to_all | solution.py:322
  38.0 28.3 %copy-start.2 = (bf16[512,1024]{1,0:T(8,128)(2,1)S(1)}, bf16[512,1024]{1,0:T(8,128)(2,1)}, u32[]{:S(2)}) copy-start(bf16[512,1024]{1,0:T(8,128)(2,1)} %refs_0_.1) | copy-start | bytes 3145732
  38.0 18.5 %collective-permute-start = (bf16[512,512]{1,0:T(8,128)(2,1)}, bf16[512,512]{1,0:T(8,128)(2,1)}, u32[]{:S(2)}, u32[]{:S(2)}) collective-permute-start(bf16[512,512]{1,0:T(8,128)(2,1)} %get-tuple-element.143), channel_id=1, source_target_pairs={{0,4},{4,0},{8,12},{12,8},{16,20},{20,16},{24,28},{28,24},{1,5},{5... | collective-permute-start | bytes 1572872 | tf_op jit(solution)/shard_map/ppermute | solution.py:36
  41.1 25.2 %collective-permute-start.1 = (bf16[256,1024]{1,0:T(8,128)(2,1)S(1)}, bf16[256,1024]{1,0:T(8,128)(2,1)}, u32[]{:S(2)}, u32[]{:S(2)}) collective-permute-start(bf16[256,1024]{1,0:T(8,128)(2,1)S(1)} %constant_dynamic-slice_fusion.1), channel_id=1, source_target_pairs={{0,4},{4,0},{8,12},{12,8},{16,20},{20,16},{24,28},{28,24},{1,5},{5... | collective-permute-start | bytes 1572872 | tf_op jit(solution)/shard_map/ppermute | solution.py:36
  66.3 28.9 %copy-start.3 = (bf16[512,1024]{1,0:T(8,128)(2,1)}, bf16[512,1024]{1,0:T(8,128)(2,1)S(1)}, u32[]{:S(2)}) copy-start(bf16[512,1024]{1,0:T(8,128)(2,1)S(1)} %collective-permute-done.2.refs_1_) | copy-start | bytes 3145732
  66.4 23.8 %collective-permute-start.4 = (bf16[512,1024]{1,0:T(8,128)(2,1)S(1)}, bf16[512,1024]{1,0:T(8,128)(2,1)S(1)}, u32[]{:S(2)}, u32[]{:S(2)}) collective-permute-start(bf16[512,1024]{1,0:T(8,128)(2,1)S(1)} %copy-done.2), channel_id=1, source_target_pairs={{0,4},{4,0},{8,12},{12,8},{16,20},{20,16},{24,28},{28,24},{1,5},{5... | collective-permute-start | bytes 3145736 | tf_op jit(solution)/shard_map/ppermute | solution.py:36
  67.5 60.8 %collective-permute-start.8 = (bf16[512,1024]{1,0:T(8,128)(2,1)}, bf16[512,1024]{1,0:T(8,128)(2,1)}, u32[]{:S(2)}, u32[]{:S(2)}) collective-permute-start(bf16[512,1024]{1,0:T(8,128)(2,1)} %pad_maximum_fusion.refs_0_), channel_id=1, source_target_pairs={{8,0},{12,4},{16,8},{20,12},{24,16},{28,20},{9,1},{13,5},{17,9},{2... | collective-permute-start | bytes 3145736 | tf_op jit(solution)/shard_map/ppermute | solution.py:31
  68.7 59.5 %collective-permute-start.9 = (bf16[512,1024]{1,0:T(8,128)(2,1)}, bf16[512,1024]{1,0:T(8,128)(2,1)}, u32[]{:S(2)}, u32[]{:S(2)}) collective-permute-start(bf16[512,1024]{1,0:T(8,128)(2,1)} %pad_maximum_fusion.refs_0_), channel_id=1, source_target_pairs={{0,8},{4,12},{8,16},{12,20},{16,24},{20,28},{1,9},{5,13},{9,17},{1... | collective-permute-start | bytes 3145736 | tf_op jit(solution)/shard_map/ppermute | solution.py:31
  74.3 53.9 %collective-permute-start.6 = (bf16[512,1024]{1,0:T(8,128)(2,1)S(1)}, bf16[512,1024]{1,0:T(8,128)(2,1)}, u32[]{:S(2)}, u32[]{:S(2)}) collective-permute-start(bf16[512,1024]{1,0:T(8,128)(2,1)S(1)} %collective-permute-done.2.refs_1_), channel_id=1, source_target_pairs={{8,0},{12,4},{16,8},{20,12},{9,1},{13,5},{17,9},{21,13},{10,2},{14... | collective-permute-start | bytes 3145736 | tf_op jit(solution)/shard_map/ppermute | solution.py:31
  75.6 52.6 %collective-permute-start.7 = (bf16[512,1024]{1,0:T(8,128)(2,1)}, bf16[512,1024]{1,0:T(8,128)(2,1)}, u32[]{:S(2)}, u32[]{:S(2)}) collective-permute-start(bf16[512,1024]{1,0:T(8,128)(2,1)} %collective-permute-done.3.refs_2_), channel_id=1, source_target_pairs={{8,16},{12,20},{16,24},{20,28},{9,17},{13,21},{17,25},{21,29},{10,... | collective-permute-start | bytes 3145736 | tf_op jit(solution)/shard_map/ppermute | solution.py:31
  91.2 37.1 %collective-permute-start.5 = (bf16[512,1024]{1,0:T(8,128)(2,1)S(1)}, bf16[512,1024]{1,0:T(8,128)(2,1)}, u32[]{:S(2)}, u32[]{:S(2)}) collective-permute-start(bf16[512,1024]{1,0:T(8,128)(2,1)S(1)} %collective-permute-done.2.refs_1_), channel_id=1, source_target_pairs={{0,4},{4,0},{8,12},{12,8},{16,20},{20,16},{1,5},{5,1},{9,13},{13,9... | collective-permute-start | bytes 3145736 | tf_op jit(solution)/shard_map/ppermute | solution.py:36
  95.3 31.9 %all-to-all-start.2 = ((f32[8,8,2048]{2,1,0:T(8,128)}), f32[8,8,2048]{2,1,0:T(8,128)}, u32[]{:S(2)}, u32[]{:S(2)}) async-start(f32[8,8,2048]{2,1,0:T(8,128)} %maximum_bitcast_fusion), calls=%async_computation.2 | async-start | bytes 1048576 | tf_op jit(solution)/shard_map/all_to_all | solution.py:340
  129.6 28.1 %collective-permute-start.10 = (bf16[512,1024]{1,0:T(8,128)(2,1)S(1)}, bf16[512,1024]{1,0:T(8,128)(2,1)}, u32[]{:S(2)}, u32[]{:S(2)}) collective-permute-start(bf16[512,1024]{1,0:T(8,128)(2,1)S(1)} %broadcast_select_fusion.2.refs_3_), channel_id=1, source_target_pairs={{8,0},{12,4},{16,24},{20,28},{9,1},{13,5},{17,25},{21,29},{10,2},{... | collective-permute-start | bytes 3145736 | tf_op jit(solution)/shard_map/ppermute | solution.py:31
  130.9 34.5 %collective-permute-start.14 = (bf16[512,1024]{1,0:T(8,128)(2,1)S(1)}, bf16[512,1024]{1,0:T(8,128)(2,1)}, u32[]{:S(2)}, u32[]{:S(2)}) collective-permute-start(bf16[512,1024]{1,0:T(8,128)(2,1)S(1)} %broadcast_select_fusion.2.refs_3_), channel_id=1, source_target_pairs={{0,4},{4,0},{8,12},{12,8},{16,20},{20,16},{24,28},{28,24},{1,5},{5... | collective-permute-start | bytes 3145736 | tf_op jit(solution)/shard_map/ppermute | solution.py:36
  132.7 47.3 %collective-permute-start.11 = (bf16[512,1024]{1,0:T(8,128)(2,1)}, bf16[512,1024]{1,0:T(8,128)(2,1)}, u32[]{:S(2)}, u32[]{:S(2)}) collective-permute-start(bf16[512,1024]{1,0:T(8,128)(2,1)} %collective-permute-done.8.refs_1_), channel_id=1, source_target_pairs={{8,0},{12,4},{16,8},{20,12},{9,1},{13,5},{17,9},{21,13},{10,2},{14... | collective-permute-start | bytes 3145736 | tf_op jit(solution)/shard_map/ppermute | solution.py:31
  134.0 46.0 %collective-permute-start.12 = (bf16[512,1024]{1,0:T(8,128)(2,1)}, bf16[512,1024]{1,0:T(8,128)(2,1)}, u32[]{:S(2)}, u32[]{:S(2)}) collective-permute-start(bf16[512,1024]{1,0:T(8,128)(2,1)} %collective-permute-done.9.refs_2_), channel_id=1, source_target_pairs={{8,16},{12,20},{16,24},{20,28},{9,17},{13,21},{17,25},{21,29},{10,... | collective-permute-start | bytes 3145736 | tf_op jit(solution)/shard_map/ppermute | solution.py:31
  135.6 44.3 %collective-permute-start.13 = (bf16[512,1024]{1,0:T(8,128)(2,1)}, bf16[512,1024]{1,0:T(8,128)(2,1)}, u32[]{:S(2)}, u32[]{:S(2)}) collective-permute-start(bf16[512,1024]{1,0:T(8,128)(2,1)} %collective-permute-done.3.refs_2_), channel_id=1, source_target_pairs={{8,12},{12,8},{16,20},{20,16},{24,28},{28,24},{9,13},{13,9},{17,21... | collective-permute-start | bytes 3145736 | tf_op jit(solution)/shard_map/ppermute | solution.py:36
  158.4 23.0 %all-to-all-start.3 = ((bf16[8,8,2048]{2,1,0:T(8,128)(2,1)}), bf16[8,8,2048]{2,1,0:T(8,128)(2,1)S(1)}, u32[]{:S(2)}, u32[]{:S(2)}) async-start(bf16[8,8,2048]{2,1,0:T(8,128)(2,1)} %broadcast_in_dim.16), calls=%async_computation.3 | async-start | bytes 524288 | tf_op jit(solution)/shard_map/all_to_all | solution.py:349
  181.5 10.0 %collective-permute-start.16 = (bf16[256,1024]{1,0:T(8,128)(2,1)}, bf16[256,1024]{1,0:T(8,128)(2,1)}, u32[]{:S(2)}, u32[]{:S(2)}) collective-permute-start(bf16[256,1024]{1,0:T(8,128)(2,1)} %collective-permute-done.1.mine), channel_id=1, source_target_pairs={{0,2},{1,3},{2,0},{3,1},{4,6},{5,7},{6,4},{7,5},{8,10},{9,11},{10,... | collective-permute-start | bytes 1572872 | tf_op jit(solution)/shard_map/ppermute | solution.py:300
  184.3 22.8 %collective-permute-start.18 = (bf16[512,1024]{1,0:T(8,128)(2,1)}, bf16[512,1024]{1,0:T(8,128)(2,1)}, u32[]{:S(2)}, u32[]{:S(2)}) collective-permute-start(bf16[512,1024]{1,0:T(8,128)(2,1)} %broadcast_select_fusion.1.refs_2_), channel_id=1, source_target_pairs={{8,0},{12,4},{16,24},{20,28},{9,1},{13,5},{17,25},{21,29},{10,2},{... | collective-permute-start | bytes 3145736 | tf_op jit(solution)/shard_map/ppermute | solution.py:31
  185.6 26.5 %collective-permute-start.19 = (bf16[512,1024]{1,0:T(8,128)(2,1)}, bf16[512,1024]{1,0:T(8,128)(2,1)}, u32[]{:S(2)}, u32[]{:S(2)}) collective-permute-start(bf16[512,1024]{1,0:T(8,128)(2,1)} %collective-permute-done.10.refs_0_.refs_4_), channel_id=1, source_target_pairs={{0,4},{4,0},{24,28},{28,24},{1,5},{5,1},{25,29},{29,25},{2,6},{6,2... | collective-permute-start | bytes 3145736 | tf_op jit(solution)/shard_map/ppermute | solution.py:36
  187.7 10.6 %collective-permute-start.15 = (bf16[256,1024]{1,0:T(8,128)(2,1)}, bf16[256,1024]{1,0:T(8,128)(2,1)}, u32[]{:S(2)}, u32[]{:S(2)}) collective-permute-start(bf16[256,1024]{1,0:T(8,128)(2,1)} %collective-permute-done.1.mine), channel_id=1, source_target_pairs={{0,1},{1,0},{2,3},{3,2},{4,5},{5,4},{6,7},{7,6},{8,9},{9,8},{10,11... | collective-permute-start | bytes 1572872 | tf_op jit(solution)/shard_map/ppermute | solution.py:300
  191.5 6.8 %collective-permute-start.17 = (bf16[256,1024]{1,0:T(8,128)(2,1)}, bf16[256,1024]{1,0:T(8,128)(2,1)}, u32[]{:S(2)}, u32[]{:S(2)}) collective-permute-start(bf16[256,1024]{1,0:T(8,128)(2,1)} %collective-permute-done.16.by_y), channel_id=1, source_target_pairs={{0,1},{1,0},{2,3},{3,2},{4,5},{5,4},{6,7},{7,6},{8,9},{9,8},{10,11... | collective-permute-start | bytes 1572872 | tf_op jit(solution)/shard_map/ppermute | solution.py:300
  191.5 1.2 copy-start.4
  192.8 5.5 %copy-start.6 = (bf16[512,1024]{1,0:T(8,128)(2,1)S(1)}, bf16[512,1024]{1,0:T(8,128)(2,1)}, u32[]{:S(2)}) copy-start(bf16[512,1024]{1,0:T(8,128)(2,1)} %pad_maximum_fusion.refs_0_) | copy-start | bytes 3145732
  211.7 6.4 %collective-permute-start.20 = (bf16[256,512]{1,0:T(8,128)(2,1)S(1)}, bf16[256,512]{1,0:T(8,128)(2,1)S(1)}, u32[]{:S(2)}, u32[]{:S(2)}) collective-permute-start(bf16[256,512]{1,0:T(8,128)(2,1)S(1)} %get-tuple-element.113), channel_id=1, source_target_pairs={{0,4},{4,0},{8,12},{12,8},{16,20},{20,16},{24,28},{28,24},{1,5},{5... | collective-permute-start | bytes 786440 | tf_op jit(solution)/shard_map/ppermute | solution.py:36
  221.6 41.7 %all-to-all-start.4 = ((f32[8,8,2048]{2,1,0:T(8,128)}), f32[8,8,2048]{2,1,0:T(8,128)}, u32[]{:S(2)}, u32[]{:S(2)}) async-start(f32[8,8,2048]{2,1,0:T(8,128)} %bitcast.40), calls=%async_computation.4 | async-start | bytes 1048576 | tf_op jit(solution)/shard_map/all_to_all | solution.py:428
  227.0 17.8 %collective-permute-start.24 = (bf16[256,1024]{1,0:T(8,128)(2,1)}, bf16[256,1024]{1,0:T(8,128)(2,1)S(1)}, u32[]{:S(2)}, u32[]{:S(2)}) collective-permute-start(bf16[256,1024]{1,0:T(8,128)(2,1)} %get-tuple-element.122.refs_2_), channel_id=1, source_target_pairs={{0,4},{4,0},{8,12},{12,8},{16,20},{20,16},{24,28},{28,24},{1,5},{5... | collective-permute-start | bytes 1572872 | tf_op jit(solution)/shard_map/ppermute | solution.py:36
  229.1 19.9 %collective-permute-start.25 = (bf16[256,1024]{1,0:T(8,128)(2,1)}, bf16[256,1024]{1,0:T(8,128)(2,1)}, u32[]{:S(2)}, u32[]{:S(2)}) collective-permute-start(bf16[256,1024]{1,0:T(8,128)(2,1)} %get-tuple-element.122.refs_2_), channel_id=1, source_target_pairs={{8,0},{12,4},{16,8},{20,12},{24,16},{28,20},{0,24},{4,28},{9,1},{1... | collective-permute-start | bytes 1572872 | tf_op jit(solution)/shard_map/ppermute | solution.py:31
  232.3 28.5 %collective-permute-start.26 = (bf16[256,1024]{1,0:T(8,128)(2,1)}, bf16[256,1024]{1,0:T(8,128)(2,1)}, u32[]{:S(2)}, u32[]{:S(2)}) collective-permute-start(bf16[256,1024]{1,0:T(8,128)(2,1)} %get-tuple-element.122.refs_2_), channel_id=1, source_target_pairs={{24,0},{28,4},{0,8},{4,12},{8,16},{12,20},{16,24},{20,28},{25,1},{... | collective-permute-start | bytes 1572872 | tf_op jit(solution)/shard_map/ppermute | solution.py:31
  232.3 32.1 %collective-permute-start.21 = (bf16[8,64,512]{2,1,0:T(8,128)(2,1)}, bf16[8,64,512]{2,1,0:T(8,128)(2,1)}, u32[]{:S(2)}, u32[]{:S(2)}) collective-permute-start(bf16[8,64,512]{2,1,0:T(8,128)(2,1)} %bitcast.10), channel_id=1, source_target_pairs={{0,2},{1,3},{2,0},{3,1},{4,6},{5,7},{6,4},{7,5},{8,10},{9,11},{10,... | collective-permute-start | bytes 1572872 | tf_op jit(solution)/shard_map/ppermute | solution.py:300
  260.9 27.5 %collective-permute-start.27 = (bf16[256,1024]{1,0:T(8,128)(2,1)}, bf16[256,1024]{1,0:T(8,128)(2,1)}, u32[]{:S(2)}, u32[]{:S(2)}) collective-permute-start(bf16[256,1024]{1,0:T(8,128)(2,1)} %get-tuple-element.122.refs_2_), channel_id=1, source_target_pairs={{16,0},{20,4},{24,8},{28,12},{0,16},{4,20},{8,24},{12,28},{17,1},{... | collective-permute-start | bytes 1572872 | tf_op jit(solution)/shard_map/ppermute | solution.py:31
  267.0 23.8 %collective-permute-start.22 = (bf16[2,256,512]{2,1,0:T(8,128)(2,1)}, bf16[2,256,512]{2,1,0:T(8,128)(2,1)}, u32[]{:S(2)}, u32[]{:S(2)}) collective-permute-start(bf16[2,256,512]{2,1,0:T(8,128)(2,1)} %get-tuple-element.141), channel_id=1, source_target_pairs={{0,2},{1,3},{2,0},{3,1},{4,6},{5,7},{6,4},{7,5},{8,10},{9,11},{10,... | collective-permute-start | bytes 1572872 | tf_op jit(solution)/shard_map/ppermute | solution.py:300
  267.0 23.8 %collective-permute-start.23 = (bf16[2,256,512]{2,1,0:T(8,128)(2,1)}, bf16[2,256,512]{2,1,0:T(8,128)(2,1)}, u32[]{:S(2)}, u32[]{:S(2)}) collective-permute-start(bf16[2,256,512]{2,1,0:T(8,128)(2,1)} %get-tuple-element.140), channel_id=1, source_target_pairs={{0,3},{1,2},{2,1},{3,0},{4,7},{5,6},{6,5},{7,4},{8,11},{9,10},{10,... | collective-permute-start | bytes 1572872 | tf_op jit(solution)/shard_map/ppermute | solution.py:300
  267.7 23.1 %all-to-all-start.5 = ((bf16[8,8,2048]{2,1,0:T(8,128)(2,1)}), bf16[8,8,2048]{2,1,0:T(8,128)(2,1)S(1)}, u32[]{:S(2)}, u32[]{:S(2)}) async-start(bf16[8,8,2048]{2,1,0:T(8,128)(2,1)} %broadcast_in_dim.17), calls=%async_computation.5 | async-start | bytes 524288 | tf_op jit(solution)/shard_map/all_to_all | solution.py:349
  272.2 52.5 %copy-start.1 = (bf16[4,2,256,512]{3,2,1,0:T(8,128)(2,1)S(1)}, bf16[4,2,256,512]{3,2,1,0:T(8,128)(2,1)}, u32[]{:S(2)}) copy-start(bf16[4,2,256,512]{3,2,1,0:T(8,128)(2,1)} %shard_map.108.term) | copy-start | bytes 6291460
  290.8 26.6 %collective-permute-start.28 = (bf16[2,8,64,512]{3,2,1,0:T(8,128)(2,1)}, bf16[2,8,64,512]{3,2,1,0:T(8,128)(2,1)}, u32[]{:S(2)}, u32[]{:S(2)}) collective-permute-start(bf16[2,8,64,512]{3,2,1,0:T(8,128)(2,1)} %pad_maximum_fusion.1.refs_0_), channel_id=1, source_target_pairs={{0,1},{1,0},{2,3},{3,2},{4,5},{5,4},{6,7},{7,6},{8,9},{9,8},{10,11... | collective-permute-start | bytes 3145736 | tf_op jit(solution)/shard_map/ppermute | solution.py:300
  290.8 15.6 %collective-permute-start.30 = (bf16[256,1024]{1,0:T(8,128)(2,1)}, bf16[256,1024]{1,0:T(8,128)(2,1)}, u32[]{:S(2)}, u32[]{:S(2)}) collective-permute-start(bf16[256,1024]{1,0:T(8,128)(2,1)} %collective-permute-done.25.refs_3_), channel_id=1, source_target_pairs={{0,4},{4,0},{8,12},{12,8},{16,20},{20,16},{24,28},{28,24},{1,5},{5... | collective-permute-start | bytes 1572872 | tf_op jit(solution)/shard_map/ppermute | solution.py:36
  293.3 24.1 %collective-permute-start.31 = (bf16[256,1024]{1,0:T(8,128)(2,1)}, bf16[256,1024]{1,0:T(8,128)(2,1)}, u32[]{:S(2)}, u32[]{:S(2)}) collective-permute-start(bf16[256,1024]{1,0:T(8,128)(2,1)} %collective-permute-done.26.refs_5_), channel_id=1, source_target_pairs={{0,4},{4,0},{8,12},{12,8},{16,20},{20,16},{24,28},{28,24},{1,5},{5... | collective-permute-start | bytes 1572872 | tf_op jit(solution)/shard_map/ppermute | solution.py:36
  293.4 24.0 %collective-permute-start.29 = (bf16[2,256,512]{2,1,0:T(8,128)(2,1)}, bf16[2,256,512]{2,1,0:T(8,128)(2,1)}, u32[]{:S(2)}, u32[]{:S(2)}) collective-permute-start(bf16[2,256,512]{2,1,0:T(8,128)(2,1)} %get-tuple-element.139), channel_id=1, source_target_pairs={{0,1},{1,0},{2,3},{3,2},{4,5},{5,4},{6,7},{7,6},{8,9},{9,8},{10,11... | collective-permute-start | bytes 1572872 | tf_op jit(solution)/shard_map/ppermute | solution.py:300
  317.4 14.0 %collective-permute-start.34 = (bf16[256,1024]{1,0:T(8,128)(2,1)}, bf16[256,1024]{1,0:T(8,128)(2,1)}, u32[]{:S(2)}, u32[]{:S(2)}) collective-permute-start(bf16[256,1024]{1,0:T(8,128)(2,1)} %collective-permute-done.27.refs_4_), channel_id=1, source_target_pairs={{0,4},{4,0},{8,12},{12,8},{16,20},{20,16},{24,28},{28,24},{1,5},{5... | collective-permute-start | bytes 1572872 | tf_op jit(solution)/shard_map/ppermute | solution.py:36
  319.1 7.9 %collective-permute-start.32 = (bf16[8,512]{1,0:T(8,128)(2,1)S(1)}, bf16[8,512]{1,0:T(8,128)(2,1)S(1)}, u32[]{:S(2)}, u32[]{:S(2)}) collective-permute-start(bf16[8,512]{1,0:T(8,128)(2,1)S(1)} %get-tuple-element.144), channel_id=1, source_target_pairs={{0,0},{1,8},{2,16},{3,24},{4,4},{5,12},{6,20},{7,28},{8,1},{9,9},{... | collective-permute-start | bytes 24584 | tf_op jit(solution)/shard_map/ppermute | solution.py:266
  321.0 6.5 %collective-permute-start.33 = (bf16[8,512]{1,0:T(8,128)(2,1)S(1)}, bf16[8,512]{1,0:T(8,128)(2,1)S(1)}, u32[]{:S(2)}, u32[]{:S(2)}) collective-permute-start(bf16[8,512]{1,0:T(8,128)(2,1)S(1)} %get-tuple-element.145), channel_id=1, source_target_pairs={{0,4},{1,12},{2,20},{3,28},{4,0},{5,8},{6,16},{7,24},{8,5},{9,13},... | collective-permute-start | bytes 24584 | tf_op jit(solution)/shard_map/ppermute | solution.py:266
  (8 other events, 7.9 us)

commit v9 on v8

--- a/solution.py
+++ b/solution.py
@@ -12,7 +12,7 @@
 BF16 = jnp.bfloat16
 BACK = (((1,), (1,)), ((), ()))
 FIRST = (((0,), (0,)), ((), ()))
-VMEM_LIMIT = 48 * 1024 * 1024
+VMEM_LIMIT = 60 * 1024 * 1024
 
 
 def matmul(a, b, dims=None):
@@ -191,8 +191,7 @@
 
     def write(i, e, index):
         term = matmul(query_grad[...], weights[e][i][...], BACK)
-        member = lax.bitwise_xor(lax.div(index, chunk), place[3])
-        out[member, lax.rem(index, chunk)] = term.astype(BF16)
+        out[lax.div(index, chunk), lax.rem(index, chunk)] = term.astype(BF16)
 
     each_block(line, place, relayed, range(n), write)
 
@@ -212,13 +211,12 @@
     out[...] = total[...].astype(BF16)
 
 
-def sum_kernel(place, term, *refs):
-    parts, out = refs[:-1], refs[-1]
-    width = term.shape[3]
-    for c in range(term.shape[1]):
-        total = term[0, c].astype(F32)
-        for part in parts:
-            total = total + part[c].astype(F32)
+def sum_kernel(place, parts, out):
+    width = parts.shape[3]
+    for c in range(parts.shape[1]):
+        total = parts[0, c].astype(F32)
+        for k in range(1, parts.shape[0]):
+            total = total + parts[k, c].astype(F32)
         out[:, c * width : (c + 1) * width] = total.astype(BF16)
 
 
@@ -317,14 +315,8 @@
     quarter_cols = width // 4
     live_part = lax.dynamic_slice_in_dim(live_flat, quarter * quarter_cols, quarter_cols, 1)
     live_here = line.swap(live_part)
-    quarter_rows = rows // 4
-    live_rows = lax.dynamic_slice_in_dim(live_flat, quarter * quarter_rows, quarter_rows, 0)
-    live_mine = lax.all_to_all(
-        live_rows.reshape(quarter_rows, n_dp, own_width), "dp", split_axis=1, concat_axis=0
-    )
-    live_mine = live_mine.reshape(n_dp, quarter_rows, own_width)
-    image_cols, wo_pair, live_here, live_mine, query_weight, *wq_moved = gate(
-        (image_cols, wo_pair, live_here, live_mine, query_weight, *wq_moved)
+    image_cols, wo_pair, live_here, live_flat, query_weight, *wq_moved = gate(
+        (image_cols, wo_pair, live_here, live_flat, query_weight, *wq_moved)
     )
 
     n_moved = len(wq_moved)
@@ -338,8 +330,8 @@
     )
     part_kv = part_kv.reshape(n_dp, image_rows, 2 * local_cols)
     kv_own = jnp.sum(lax.all_to_all(part_kv, "dp", split_axis=0, concat_axis=0), axis=0)
-    kv_own, live_here, *staged = gate(
-        (kv_own.astype(BF16), live_here, *wq_others, *wq_moved, *wq_two, *wo_moved)
+    kv_own, live_here, live_flat, *staged = gate(
+        (kv_own.astype(BF16), live_here, live_flat, *wq_others, *wq_moved, *wq_two, *wo_moved)
     )
     wq_others, staged = staged[:2], staged[2:]
     wq_moved, wq_two, wo_moved = staged[:n_moved], staged[n_moved:-n_moved], staged[-n_moved:]
@@ -352,19 +344,23 @@
     wo_two = line.second(wo_moved)
     wq_others += [line.swap(block, at) for block, at in zip(wq_moved[1:], planes[1:])]
     wq_others += [line.swap(block) for block in wq_last[:1]]
-    kv_own, *wq_edge = gate((kv_own, *wq_last[1:]))
     kv_all = everywhere(kv_own).reshape(images, 2 * local_cols)
-    edge_other = [line.swap(block, (0, 3)) for block in wq_edge]
-    kv_all, live_here, wo_pair, live_flat, *staged = gate(
-        (kv_all, live_here, wo_pair, live_flat, *wo_two, *wq_edge, *wq_others)
+    quarter_rows = rows // 4
+    live_rows = lax.dynamic_slice_in_dim(live_flat, quarter * quarter_rows, quarter_rows, 0)
+    live_mine = lax.all_to_all(
+        live_rows.reshape(quarter_rows, n_dp, own_width), "dp", split_axis=1, concat_axis=0
+    )
+    live_mine = live_mine.reshape(n_dp, quarter_rows, own_width)
+    kv_all, live_here, live_mine, wo_pair, live_flat, *staged = gate(
+        (kv_all, live_here, live_mine, wo_pair, live_flat, *wo_two, *wq_last, *wq_others)
     )
     wo_two, staged = staged[: len(wo_two)], staged[len(wo_two) :]
-    wq_last[1:], wq_others = staged[: len(wq_edge)], staged[len(wq_edge) :]
+    wq_last, wq_others = staged[: len(wq_last)], staged[len(wq_last) :]
 
     wo_last = line.third(wo_two)
     by_y = tensor_swap(live_here, 2)
     live_pieces = [live_here, tensor_swap(live_here, 1), by_y, tensor_swap(by_y, 1)]
-    wq_others += edge_other
+    wq_others += [line.swap(block, (0, 3)) for block in wq_last[1:]]
     arrivals = [query_weight, *wq_moved, *wq_last]
     early = range(4 if relayed else len(arrivals))
     late = range(len(early), len(arrivals))
@@ -439,29 +435,22 @@
     kv_grad_all = everywhere(kv_grad).reshape(images, 2 * local_cols)
     live_pair = jnp.stack([live_mine, live_y])
 
-    text_parts = [tensor_swap(term[k], k) for k in range(2, n_tensor)]
+    text_parts = lax.all_to_all(term, "tensor", split_axis=0, concat_axis=0).reshape(term.shape)
     attended, att_swapped, *att_next = gate((attended, att_swapped, *att_next))
     att_far = [line.shift(attended, m) for m in range(2, line.n_z - 1)]
     att_other_next = [line.swap(block) for block in att_next]
-    kv_grad_all, live_pair, *staged = gate((kv_grad_all, live_pair, *text_parts, *att_far))
-    text_parts, att_far = staged[: n_tensor - 2], staged[n_tensor - 2 :]
-
     live_core = tensor_swap(live_pair, 1)
-    text_parts.append(tensor_swap(term[1], 1))
+
     image_term = matmul(kv_grad_all[:, :local_cols], key_weight, BACK)
     image_term = image_term + matmul(kv_grad_all[:, local_cols:], value_weight, BACK)
-    image_grad, live_core, *staged = to_owner(
-        line, image_term.astype(BF16), live_core, *text_parts, *att_other_next, *att_far
-    )
-    text_parts, staged = staged[: n_tensor - 1], staged[n_tensor - 1 :]
+    image_grad, text_parts, live_core, *staged = to_owner(
+        line, image_term.astype(BF16), text_parts, live_core, *att_other_next, *att_far
+    )
     att_other_next, att_far = staged[:2], staged[2:]
     att_other_far = [line.swap(block) for block in att_far]
     image_grad = image_grad.reshape(samples, image_own, width // n_tensor)
     text_grad = call(
-        sum_kernel,
-        place,
-        (term, *text_parts),
-        [shape((rows, width // n_tensor), BF16)],
+        sum_kernel, place, (text_parts,), [shape((rows, width // n_tensor), BF16)]
     )
     text_grad = text_grad.reshape(samples, tok_rows, width // n_tensor)
 

time: 342 us -> 329 us (0.962)
  waiting for transfers between devices: 172 us -> 140 us
  blocking collectives: 5.4 us -> 34.1 us
  local copies, waits for them, and re-layouts: 19.1 us -> 6.72 us
  Pallas kernels: 37.5 us -> 45.6 us
    ppermute x13, waiting for transfers between devices: 68.1 us -> 14.9 us  [move(): return lax.ppermute(block, 'dp', pairs)]
    all_to_all x0 -> x2, blocking collectives: none -> 28.8 us  [the longest x1 16.1 us: shards(): lax.all_to_all(live_rows.reshape(quarter_rows, n_dp, own_width), 'dp', sp...]
    all_to_all x2 -> x1, waiting for transfers between devices: 3.96 us -> 31.1 us  [everywhere(): return lax.all_to_all(copies, 'dp', split_axis=0, concat_axis=0)]
    pallas_call x8, Pallas kernels: 37.5 us -> 45.6 us  [call(): pl.pallas_call(kernel, out_shape=outs[0] if single else outs, in_specs=[p...]
    unnamed x31 -> x25, local copies, waits for them, and re-layouts: 9.34 us -> 1.87 us
    ppermute x12, waiting for transfers between devices: 55.4 us -> 48.6 us  [swap(): return lax.ppermute(block, 'dp', pairs)]
    all_to_all x1, waiting for transfers between devices: 0.01 us -> 5.08 us  [shards(): lax.all_to_all(kv_part, 'dp', split_axis=0, concat_axis=0)]
    all_to_all x1, waiting for transfers between devices: 12.5 us -> 7.82 us  [shards(): lax.all_to_all(image_flat, 'dp', split_axis=1, concat_axis=0, tiled=True)]
  transfers between devices with their start and end apart: 41 -> 37, of which waited for: 20 -> 14; matrix products, arithmetic and copies ran while one was open for 8% -> 5% of each run, Pallas kernels for 9% -> 11%
where the time goes in v9:
time: 329 us; the launch traced here: 325 us
  waiting for transfers between devices  140 us (43%)
  starting transfers between devices  82.4 us (25%)
  Pallas kernels  45.6 us (14%)
  blocking collectives  34.1 us (10%)
  other arithmetic  13.2 us (4%)
  local copies, waits for them, and re-layouts  6.72 us (2%)
    ppermute x12, waiting for transfers between devices, swap(): return lax.ppermute(block, 'dp', pairs)  48.6 us
    pallas_call x8, Pallas kernels, call(): pl.pallas_call(kernel, out_shape=outs[0] if single else outs, in_specs=[p...  45.6 us
    all_to_all x1, waiting for transfers between devices, everywhere(): return lax.all_to_all(copies, 'dp', split_axis=0, concat_axis=0)  31.1 us
    all_to_all x1, waiting for transfers between devices, shards(): lax.all_to_all(part_kv, 'dp', split_axis=0, concat_axis=0)  29.3 us
    ppermute x13, starting transfers between devices, move(): return lax.ppermute(block, 'dp', pairs)  25.8 us
    ppermute x12, starting transfers between devices, swap(): return lax.ppermute(block, 'dp', pairs)  18.7 us
    all_to_all x1, blocking collectives, shards(): lax.all_to_all(live_rows.reshape(quarter_rows, n_dp, own_width), 'dp', sp...  16.1 us
    ppermute x13, waiting for transfers between devices, move(): return lax.ppermute(block, 'dp', pairs)  14.9 us
  transfers between devices with their start and end apart: 37, of which 14 were waited for; matrix products, arithmetic and copies ran while one was open for 5% of the time, Pallas kernels for 11%

profile of v9, /device:TPU:4, one launch (start us, length us, event | category | flops | bytes accessed | tf_op | source)
XLA Modules:
  0.0 325.4 jit_solution(4204619882343793056)
XLA Ops:
  0.7 1.4 collective-permute-start.2
  2.1 5.5 %collective-permute-start.3 = (bf16[512,1024]{1,0:T(8,128)(2,1)}, bf16[512,1024]{1,0:T(8,128)(2,1)}, u32[]{:S(2)}, u32[]{:S(2)}) collective-permute-start(bf16[512,1024]{1,0:T(8,128)(2,1)} %refs_0_.1), channel_id=1, source_target_pairs={{0,8},{4,12},{8,16},{12,20},{16,24},{20,28},{1,9},{5,13},{9,17},{1... | collective-permute-start | bytes 3145736 | tf_op jit(solution)/shard_map/ppermute | solution.py:31
  7.6 2.3 constant_dynamic-slice_fusion.3
  9.9 1.5 collective-permute-start
  11.5 1.8 broadcast_select_fusion
  15.5 4.8 %all-to-all-start = ((bf16[8,8,512]{2,0,1:T(8,128)(2,1)}), bf16[8,8,512]{2,0,1:T(8,128)(2,1)S(1)}, u32[]{:S(2)}, u32[]{:S(2)}) async-start(bf16[8,8,512]{2,0,1:T(8,128)(2,1)} %copy.14), calls=%async_computation | async-start | bytes 131072 | tf_op jit(solution)/shard_map/all_to_all | solution.py:311
  20.3 4.8 %collective-permute-done = bf16[512,512]{1,0:T(8,128)(2,1)} collective-permute-done((bf16[512,512]{1,0:T(8,128)(2,1)}, bf16[512,512]{1,0:T(8,128)(2,1)}, u32[]{:S(2)}, u32[]{:S(2)}) %collective-permute-start) | collective-permute-done | bytes 524320 | tf_op jit(solution)/shard_map/ppermute | solution.py:36
  25.1 2.3 pad_maximum_fusion.refs_0_
  27.4 7.8 %all-to-all-done = bf16[8,8,512]{2,0,1:T(8,128)(2,1)S(1)} async-done(((bf16[8,8,512]{2,0,1:T(8,128)(2,1)}), bf16[8,8,512]{2,0,1:T(8,128)(2,1)S(1)}, u32[]{:S(2)}, u32[]{:S(2)}) %all-to-all-start) | async-done | bytes 65568 | tf_op jit(solution)/shard_map/all_to_all | solution.py:311
  35.2 1.6 collective-permute-start.4
  38.0 5.6 %collective-permute-start.9 = (bf16[512,1024]{1,0:T(8,128)(2,1)}, bf16[512,1024]{1,0:T(8,128)(2,1)}, u32[]{:S(2)}, u32[]{:S(2)}) collective-permute-start(bf16[512,1024]{1,0:T(8,128)(2,1)} %pad_maximum_fusion.refs_0_), channel_id=1, source_target_pairs={{0,8},{4,12},{8,16},{12,20},{16,24},{20,28},{1,9},{5,13},{9,17},{1... | collective-permute-start | bytes 3145736 | tf_op jit(solution)/shard_map/ppermute | solution.py:31
  44.9 1.7 collective-permute-start.7
  46.9 1.5 fusion.5
  48.4 10.6 %collective-permute-done.4.refs_4_.refs_5_ = bf16[512,1024]{1,0:T(8,128)(2,1)} collective-permute-done((bf16[512,1024]{1,0:T(8,128)(2,1)}, bf16[512,1024]{1,0:T(8,128)(2,1)}, u32[]{:S(2)}, u32[]{:S(2)}) %collective-permute-start.4) | collective-permute-done | bytes 1048608 | tf_op jit(solution)/shard_map/ppermute | solution.py:36
  59.1 3.4 %collective-permute-start.5 = (bf16[512,1024]{1,0:T(8,128)(2,1)}, bf16[512,1024]{1,0:T(8,128)(2,1)}, u32[]{:S(2)}, u32[]{:S(2)}) collective-permute-start(bf16[512,1024]{1,0:T(8,128)(2,1)} %collective-permute-done.2.refs_1_), channel_id=1, source_target_pairs={{0,4},{4,0},{8,12},{12,8},{16,20},{20,16},{1,5},{5,1},{9,13},{13,9... | collective-permute-start | bytes 3145736 | tf_op jit(solution)/shard_map/ppermute | solution.py:36
  63.3 4.1 %all-to-all-start.1 = ((f32[8,8,2048]{2,1,0:T(8,128)}), f32[8,8,2048]{2,1,0:T(8,128)}, u32[]{:S(2)}, u32[]{:S(2)}) async-start(f32[8,8,2048]{2,1,0:T(8,128)} %maximum_bitcast_fusion), calls=%async_computation.1 | async-start | bytes 1048576 | tf_op jit(solution)/shard_map/all_to_all | solution.py:332
  67.5 29.3 %all-to-all-done.1 = f32[8,8,2048]{2,1,0:T(8,128)} async-done(((f32[8,8,2048]{2,1,0:T(8,128)}), f32[8,8,2048]{2,1,0:T(8,128)}, u32[]{:S(2)}, u32[]{:S(2)}) %all-to-all-start.1) | async-done | bytes 524320 | tf_op jit(solution)/shard_map/all_to_all | solution.py:332
  97.8 2.3 broadcast_select_fusion.2.refs_3_
  103.6 1.6 collective-permute-start.11
  105.2 1.6 collective-permute-start.13
  107.5 12.5 %all-to-all-start.2 = ((bf16[8,8,2048]{2,1,0:T(8,128)(2,1)}), bf16[8,8,2048]{2,1,0:T(8,128)(2,1)S(1)}, u32[]{:S(2)}, u32[]{:S(2)}) async-start(bf16[8,8,2048]{2,1,0:T(8,128)(2,1)} %broadcast_in_dim.16), calls=%async_computation.2 | async-start | bytes 524288 | tf_op jit(solution)/shard_map/all_to_all | solution.py:341
  120.4 31.1 %all-to-all-done.2 = bf16[8,8,2048]{2,1,0:T(8,128)(2,1)S(1)} async-done(((bf16[8,8,2048]{2,1,0:T(8,128)(2,1)}), bf16[8,8,2048]{2,1,0:T(8,128)(2,1)S(1)}, u32[]{:S(2)}, u32[]{:S(2)}) %all-to-all-start.2) | async-done | bytes 262176 | tf_op jit(solution)/shard_map/all_to_all | solution.py:341
  151.5 16.1 %all_to_all.64 = bf16[1,64,8,512]{3,1,0,2:T(8,128)(2,1)} all-to-all(bf16[1,64,8,512]{3,1,0,2:T(8,128)(2,1)S(1)} %copy.15), channel_id=1, replica_groups=mesh['dp'=8,'tensor'=4] {'dp'}, dimensions={2} | all-to-all | bytes 1048576 | tf_op jit(solution)/shard_map/all_to_all | solution.py:350
  170.8 3.3 %collective-permute-start.19 = (bf16[512,1024]{1,0:T(8,128)(2,1)}, bf16[512,1024]{1,0:T(8,128)(2,1)S(1)}, u32[]{:S(2)}, u32[]{:S(2)}) collective-permute-start(bf16[512,1024]{1,0:T(8,128)(2,1)} %collective-permute-done.12.refs_0_.refs_4_), channel_id=1, source_target_pairs={{0,4},{4,0},{24,28},{28,24},{1,5},{5,1},{25,29},{29,25},{2,6},{6,2... | collective-permute-start | bytes 3145736 | tf_op jit(solution)/shard_map/ppermute | solution.py:36
  174.3 2.9 collective-permute-done.16.by_y
  177.7 7.3 %shard_map.103.part = f32[256,1024]{1,0:T(8,128)} custom-call(s32[4]{0:T(128)} %pad_add_fusion.place, bf16[256,4096]{1,0:T(8,128)(2,1)} %bitcast.36, bf16[512,1024]{1,0:T(8,128)(2,1)} %refs_0_.1, bf16[512,1024]{1,0:T(8,128)(2,1)} %collective-permute-done.2.refs_1_, bf16[512,1024]{1,0:T(8,128)(2,1)} %collective-permute-done.3.refs_2_, ...), custom_call_target="tpu_custom_call" | custom-call | flops 2147483648 | bytes 11534336 | tf_op jit(solution)/shard_map/pallas_call | solution.py:226
  185.1 5.9 %shard_map.104 = (f32[256,512]{1,0:T(8,128)}, f32[256,512]{1,0:T(8,128)}) custom-call(s32[4]{0:T(128)} %pad_add_fusion.place, bf16[256,4096]{1,0:T(8,128)(2,1)} %bitcast.34, bf16[256,1024]{1,0:T(8,128)(2,1)} %collective-permute-done.1.mine, bf16[256,1024]{1,0:T(8,128)(2,1)} %collective-permute-done.15.by_core, ...), custom_call_target="tpu_custom_call" | custom-call | flops 1073741824 | bytes 8388608 | tf_op jit(solution)/shard_map/pallas_call | solution.py:226
  191.0 5.7 %shard_map.105 = (bf16[256,512]{1,0:T(8,128)(2,1)}, bf16[256,512]{1,0:T(8,128)(2,1)}) custom-call(s32[4]{0:T(128)} %pad_add_fusion.place, bf16[256,4096]{1,0:T(8,128)(2,1)} %bitcast.35, bf16[256,1024]{1,0:T(8,128)(2,1)} %collective-permute-done.1.mine, bf16[256,1024]{1,0:T(8,128)(2,1)} %collective-permute-done.15.by_core, ...), custom_call_target="tpu_custom_call" | custom-call | flops 1073741824 | bytes 7864320 | tf_op jit(solution)/shard_map/pallas_call | solution.py:226
  199.1 5.4 %shard_map.106 = (bf16[256,1024]{1,0:T(8,128)(2,1)}, bf16[256,1024]{1,0:T(8,128)(2,1)}) custom-call(s32[4]{0:T(128)} %pad_add_fusion.place, bf16[256,4096]{1,0:T(8,128)(2,1)} %bitcast.37, bf16[64,2048]{1,0:T(8,128)(2,1)} %bitcast.38, f32[256,1024]{1,0:T(8,128)} %shard_map.103.part, bf16[512,1024]{1,0:T(8,128)(2,1)} %collective-permute-done.12.refs_0_.refs_4_, ...), custom_call_target="tpu_custom_call" | custom-call | flops 1073741824 | bytes 6553600 | tf_op jit(solution)/shard_map/pallas_call | solution.py:226
  206.3 3.6 %shard_map.107 = (bf16[256,1024]{1,0:T(8,128)(2,1)}, f32[64,2048]{1,0:T(8,128)}) custom-call(s32[4]{0:T(128)} %pad_add_fusion.place, bf16[256,1024]{1,0:T(8,128)(2,1)} %get-tuple-element.106.query, bf16[64,2048]{1,0:T(8,128)(2,1)} %bitcast.39, bf16[256,512]{1,0:T(8,128)(2,1)} %get-tuple-element.107.keep, bf16[256,512]{1,0:T(8,128)(2,1)} %copy-done.8), custom_call_target="tpu_custom_call" | custom-call | flops 167772160 | bytes 2359296 | tf_op jit(solution)/shard_map/pallas_call | solution.py:226
  209.9 3.6 %all-to-all-start.4 = ((f32[8,8,2048]{2,1,0:T(8,128)}), f32[8,8,2048]{2,1,0:T(8,128)S(1)}, u32[]{:S(2)}, u32[]{:S(2)}) async-start(f32[8,8,2048]{2,1,0:T(8,128)} %bitcast.48), calls=%async_computation.4 | async-start | bytes 1048576 | tf_op jit(solution)/shard_map/all_to_all | solution.py:424
  214.1 8.8 %shard_map.108 = bf16[4,2,256,512]{3,2,1,0:T(8,128)(2,1)} custom-call(s32[4]{0:T(128)} %pad_add_fusion.place, bf16[256,1024]{1,0:T(8,128)(2,1)} %get-tuple-element.110.query_grad, bf16[512,1024]{1,0:T(8,128)(2,1)} %refs_0_.1, bf16[512,1024]{1,0:T(8,128)(2,1)} %collective-permute-done.2.refs_1_, bf16[512,1024]{1,0:T(8,128)(2,1)} %collective-permute-done.3.refs_2_, ...), custom_call_target="tpu_custom_call" | custom-call | flops 2147483648 | bytes 13107200 | tf_op jit(solution)/shard_map/pallas_call | solution.py:226
  222.9 5.1 %all-to-all-done.4 = f32[8,8,2048]{2,1,0:T(8,128)S(1)} async-done(((f32[8,8,2048]{2,1,0:T(8,128)}), f32[8,8,2048]{2,1,0:T(8,128)S(1)}, u32[]{:S(2)}, u32[]{:S(2)}) %all-to-all-start.4) | async-done | bytes 524320 | tf_op jit(solution)/shard_map/all_to_all | solution.py:424
  228.1 12.7 %all_to_all.65 = bf16[8,8,2048]{2,1,0:T(8,128)(2,1)S(1)} all-to-all(bf16[8,8,2048]{2,1,0:T(8,128)(2,1)S(1)} %broadcast_in_dim.17), channel_id=1, replica_groups=mesh['dp'=8,'tensor'=4] {'dp'}, dimensions={0} | all-to-all | bytes 524288 | tf_op jit(solution)/shard_map/all_to_all | solution.py:341
  241.7 5.4 %all_to_all.66 = bf16[4,16,512]{2,1,0:T(8,128)(2,1)S(1)} all-to-all(bf16[4,16,512]{2,1,0:T(8,128)(2,1)S(1)} %bitcast.50), channel_id=1, replica_groups=mesh['dp'=8,'tensor'=4] {'tensor'}, dimensions={0} | all-to-all | bytes 131072 | tf_op jit(solution)/shard_map/all_to_all | solution.py:248
  247.0 5.4 %all-to-all-start.7 = ((bf16[4,2,256,512]{3,2,1,0:T(8,128)(2,1)}), bf16[4,2,256,512]{3,2,1,0:T(8,128)(2,1)S(1)}, u32[]{:S(2)}, u32[]{:S(2)}) async-start(bf16[4,2,256,512]{3,2,1,0:T(8,128)(2,1)} %shard_map.108), calls=%async_computation.7 | async-start | bytes 4194304 | tf_op jit(solution)/shard_map/all_to_all | solution.py:438
  255.9 2.3 pad_maximum_fusion.1.refs_0_
  258.2 8.5 %collective-permute-done.23.refs_6_ = bf16[256,1024]{1,0:T(8,128)(2,1)S(1)} collective-permute-done((bf16[256,1024]{1,0:T(8,128)(2,1)}, bf16[256,1024]{1,0:T(8,128)(2,1)S(1)}, u32[]{:S(2)}, u32[]{:S(2)}) %collective-permute-start.23) | collective-permute-done | bytes 524320 | tf_op jit(solution)/shard_map/ppermute | solution.py:36
  266.7 12.5 %collective-permute-done.24.refs_3_ = bf16[256,1024]{1,0:T(8,128)(2,1)} collective-permute-done((bf16[256,1024]{1,0:T(8,128)(2,1)}, bf16[256,1024]{1,0:T(8,128)(2,1)}, u32[]{:S(2)}, u32[]{:S(2)}) %collective-permute-start.24) | collective-permute-done | bytes 524320 | tf_op jit(solution)/shard_map/ppermute | solution.py:31
  281.2 1.5 collective-permute-start.28
  282.7 11.6 %collective-permute-done.26.refs_7_ = bf16[256,1024]{1,0:T(8,128)(2,1)} collective-permute-done((bf16[256,1024]{1,0:T(8,128)(2,1)}, bf16[256,1024]{1,0:T(8,128)(2,1)}, u32[]{:S(2)}, u32[]{:S(2)}) %collective-permute-start.26) | collective-permute-done | bytes 524320 | tf_op jit(solution)/shard_map/ppermute | solution.py:36
  294.3 9.1 %collective-permute-done.27.refs_9_ = bf16[256,1024]{1,0:T(8,128)(2,1)} collective-permute-done((bf16[256,1024]{1,0:T(8,128)(2,1)}, bf16[256,1024]{1,0:T(8,128)(2,1)}, u32[]{:S(2)}, u32[]{:S(2)}) %collective-permute-start.27) | collective-permute-done | bytes 524320 | tf_op jit(solution)/shard_map/ppermute | solution.py:36
  303.4 2.4 collective-permute-done.28.refs_4_
  306.9 1.9 collective-permute-start.29
  308.8 4.3 %collective-permute-start.30 = (bf16[8,512]{1,0:T(8,128)(2,1)S(1)}, bf16[8,512]{1,0:T(8,128)(2,1)S(1)}, u32[]{:S(2)}, u32[]{:S(2)}) collective-permute-start(bf16[8,512]{1,0:T(8,128)(2,1)S(1)} %get-tuple-element.130), channel_id=1, source_target_pairs={{0,4},{1,12},{2,20},{3,28},{4,0},{5,8},{6,16},{7,24},{8,5},{9,13},... | collective-permute-start | bytes 24584 | tf_op jit(solution)/shard_map/ppermute | solution.py:264
  313.1 2.6 shard_map.109
  316.4 2.8 collective-permute-done.31.refs_8_
  319.2 6.2 %shard_map.110 = bf16[1024,512]{1,0:T(8,128)(2,1)} custom-call(s32[4]{0:T(128)} %pad_add_fusion.place, bf16[2,8,64,512]{3,2,1,0:T(8,128)(2,1)} %pad_maximum_fusion.1.refs_0_, bf16[2,8,64,512]{3,2,1,0:T(8,128)(2,1)} %collective-permute-done.22.refs_1_, bf16[256,1024]{1,0:T(8,128)(2,1)} %get-tuple-element.119.refs_2_, ...), custom_call_target="tpu_custom_call" | custom-call | flops 2147483648 | bytes 7340032 | tf_op jit(solution)/shard_map/pallas_call | solution.py:226
  (90 shorter events, 28.4 us)
Async XLA Ops:
  0.6 46.0 %copy-start = (bf16[512,1024]{1,0:T(8,128)(2,1)S(1)}, bf16[512,1024]{1,0:T(8,128)(2,1)}, u32[]{:S(2)}) copy-start(bf16[512,1024]{1,0:T(8,128)(2,1)} %param.13) | copy-start | bytes 3145732
  0.6 10.8 %copy-start.11 = (s32[2]{0:T(128)S(1)}, s32[2]{0:T(128)}, u32[]{:S(2)}) copy-start(s32[2]{0:T(128)} %param.11) | copy-start | bytes 28
  0.7 34.5 %collective-permute-start.2 = (bf16[512,1024]{1,0:T(8,128)(2,1)}, bf16[512,1024]{1,0:T(8,128)(2,1)}, u32[]{:S(2)}, u32[]{:S(2)}) collective-permute-start(bf16[512,1024]{1,0:T(8,128)(2,1)} %refs_0_.1), channel_id=1, source_target_pairs={{8,0},{12,4},{16,8},{20,12},{24,16},{28,20},{9,1},{13,5},{17,9},{2... | collective-permute-start | bytes 3145736 | tf_op jit(solution)/shard_map/ppermute | solution.py:31
  2.1 33.1 %collective-permute-start.3 = (bf16[512,1024]{1,0:T(8,128)(2,1)}, bf16[512,1024]{1,0:T(8,128)(2,1)}, u32[]{:S(2)}, u32[]{:S(2)}) collective-permute-start(bf16[512,1024]{1,0:T(8,128)(2,1)} %refs_0_.1), channel_id=1, source_target_pairs={{0,8},{4,12},{8,16},{12,20},{16,24},{20,28},{1,9},{5,13},{9,17},{1... | collective-permute-start | bytes 3145736 | tf_op jit(solution)/shard_map/ppermute | solution.py:31
  9.9 15.2 %collective-permute-start = (bf16[512,512]{1,0:T(8,128)(2,1)}, bf16[512,512]{1,0:T(8,128)(2,1)}, u32[]{:S(2)}, u32[]{:S(2)}) collective-permute-start(bf16[512,512]{1,0:T(8,128)(2,1)} %get-tuple-element.128), channel_id=1, source_target_pairs={{0,4},{4,0},{8,12},{12,8},{16,20},{20,16},{24,28},{28,24},{1,5},{5... | collective-permute-start | bytes 1572872 | tf_op jit(solution)/shard_map/ppermute | solution.py:36
  11.5 3.3 %copy-start.9 = (bf16[2,4,4096]{2,1,0:T(4,128)(2,1)S(1)}, bf16[2,4,4096]{2,1,0:T(4,128)(2,1)}, u32[]{:S(2)}) copy-start(bf16[2,4,4096]{2,1,0:T(4,128)(2,1)} %param.9) | copy-start | bytes 196612
  13.3 106.7 %copy-start.1 = (bf16[2,128,4096]{2,1,0:T(8,128)(2,1)}, bf16[2,128,4096]{2,1,0:T(8,128)(2,1)S(1)}, u32[]{:S(2)}) copy-start(bf16[2,128,4096]{2,1,0:T(8,128)(2,1)S(1)} %broadcast_select_fusion) | copy-start | bytes 6291460
  14.3 20.9 %collective-permute-start.1 = (bf16[256,1024]{1,0:T(8,128)(2,1)}, bf16[256,1024]{1,0:T(8,128)(2,1)}, u32[]{:S(2)}, u32[]{:S(2)}) collective-permute-start(bf16[256,1024]{1,0:T(8,128)(2,1)} %constant_dynamic-slice_fusion.1), channel_id=1, source_target_pairs={{0,4},{4,0},{8,12},{12,8},{16,20},{20,16},{24,28},{28,24},{1,5},{5... | collective-permute-start | bytes 1572872 | tf_op jit(solution)/shard_map/ppermute | solution.py:36
  15.5 19.7 %all-to-all-start = ((bf16[8,8,512]{2,0,1:T(8,128)(2,1)}), bf16[8,8,512]{2,0,1:T(8,128)(2,1)S(1)}, u32[]{:S(2)}, u32[]{:S(2)}) async-start(bf16[8,8,512]{2,0,1:T(8,128)(2,1)} %copy.14), calls=%async_computation | async-start | bytes 131072 | tf_op jit(solution)/shard_map/all_to_all | solution.py:311
  35.2 23.9 %collective-permute-start.4 = (bf16[512,1024]{1,0:T(8,128)(2,1)}, bf16[512,1024]{1,0:T(8,128)(2,1)}, u32[]{:S(2)}, u32[]{:S(2)}) collective-permute-start(bf16[512,1024]{1,0:T(8,128)(2,1)} %refs_0_.1), channel_id=1, source_target_pairs={{0,4},{4,0},{8,12},{12,8},{16,20},{20,16},{24,28},{28,24},{1,5},{5... | collective-permute-start | bytes 3145736 | tf_op jit(solution)/shard_map/ppermute | solution.py:36
  36.7 61.1 %collective-permute-start.8 = (bf16[512,1024]{1,0:T(8,128)(2,1)}, bf16[512,1024]{1,0:T(8,128)(2,1)}, u32[]{:S(2)}, u32[]{:S(2)}) collective-permute-start(bf16[512,1024]{1,0:T(8,128)(2,1)} %pad_maximum_fusion.refs_0_), channel_id=1, source_target_pairs={{8,0},{12,4},{16,8},{20,12},{24,16},{28,20},{9,1},{13,5},{17,9},{2... | collective-permute-start | bytes 3145736 | tf_op jit(solution)/shard_map/ppermute | solution.py:31
  38.0 59.8 %collective-permute-start.9 = (bf16[512,1024]{1,0:T(8,128)(2,1)}, bf16[512,1024]{1,0:T(8,128)(2,1)}, u32[]{:S(2)}, u32[]{:S(2)}) collective-permute-start(bf16[512,1024]{1,0:T(8,128)(2,1)} %pad_maximum_fusion.refs_0_), channel_id=1, source_target_pairs={{0,8},{4,12},{8,16},{12,20},{16,24},{20,28},{1,9},{5,13},{9,17},{1... | collective-permute-start | bytes 3145736 | tf_op jit(solution)/shard_map/ppermute | solution.py:31
  43.6 54.2 %collective-permute-start.6 = (bf16[512,1024]{1,0:T(8,128)(2,1)}, bf16[512,1024]{1,0:T(8,128)(2,1)}, u32[]{:S(2)}, u32[]{:S(2)}) collective-permute-start(bf16[512,1024]{1,0:T(8,128)(2,1)} %collective-permute-done.2.refs_1_), channel_id=1, source_target_pairs={{8,0},{12,4},{16,8},{20,12},{9,1},{13,5},{17,9},{21,13},{10,2},{14... | collective-permute-start | bytes 3145736 | tf_op jit(solution)/shard_map/ppermute | solution.py:31
  44.9 52.9 %collective-permute-start.7 = (bf16[512,1024]{1,0:T(8,128)(2,1)}, bf16[512,1024]{1,0:T(8,128)(2,1)}, u32[]{:S(2)}, u32[]{:S(2)}) collective-permute-start(bf16[512,1024]{1,0:T(8,128)(2,1)} %collective-permute-done.3.refs_2_), channel_id=1, source_target_pairs={{8,16},{12,20},{16,24},{20,28},{9,17},{13,21},{17,25},{21,29},{10,... | collective-permute-start | bytes 3145736 | tf_op jit(solution)/shard_map/ppermute | solution.py:31
  59.1 38.8 %collective-permute-start.5 = (bf16[512,1024]{1,0:T(8,128)(2,1)}, bf16[512,1024]{1,0:T(8,128)(2,1)}, u32[]{:S(2)}, u32[]{:S(2)}) collective-permute-start(bf16[512,1024]{1,0:T(8,128)(2,1)} %collective-permute-done.2.refs_1_), channel_id=1, source_target_pairs={{0,4},{4,0},{8,12},{12,8},{16,20},{20,16},{1,5},{5,1},{9,13},{13,9... | collective-permute-start | bytes 3145736 | tf_op jit(solution)/shard_map/ppermute | solution.py:36
  63.3 33.4 %all-to-all-start.1 = ((f32[8,8,2048]{2,1,0:T(8,128)}), f32[8,8,2048]{2,1,0:T(8,128)}, u32[]{:S(2)}, u32[]{:S(2)}) async-start(f32[8,8,2048]{2,1,0:T(8,128)} %maximum_bitcast_fusion), calls=%async_computation.1 | async-start | bytes 1048576 | tf_op jit(solution)/shard_map/all_to_all | solution.py:332
  100.2 67.4 %collective-permute-start.12 = (bf16[512,1024]{1,0:T(8,128)(2,1)}, bf16[512,1024]{1,0:T(8,128)(2,1)}, u32[]{:S(2)}, u32[]{:S(2)}) collective-permute-start(bf16[512,1024]{1,0:T(8,128)(2,1)} %broadcast_select_fusion.2.refs_3_), channel_id=1, source_target_pairs={{8,0},{12,4},{16,24},{20,28},{9,1},{13,5},{17,25},{21,29},{10,2},{... | collective-permute-start | bytes 3145736 | tf_op jit(solution)/shard_map/ppermute | solution.py:31
  101.5 66.1 %collective-permute-start.14 = (bf16[512,1024]{1,0:T(8,128)(2,1)}, bf16[512,1024]{1,0:T(8,128)(2,1)}, u32[]{:S(2)}, u32[]{:S(2)}) collective-permute-start(bf16[512,1024]{1,0:T(8,128)(2,1)} %broadcast_select_fusion.2.refs_3_), channel_id=1, source_target_pairs={{0,4},{4,0},{8,12},{12,8},{16,20},{20,16},{24,28},{28,24},{1,5},{5... | collective-permute-start | bytes 3145736 | tf_op jit(solution)/shard_map/ppermute | solution.py:36
  102.3 65.3 %collective-permute-start.10 = (bf16[512,1024]{1,0:T(8,128)(2,1)}, bf16[512,1024]{1,0:T(8,128)(2,1)}, u32[]{:S(2)}, u32[]{:S(2)}) collective-permute-start(bf16[512,1024]{1,0:T(8,128)(2,1)} %collective-permute-done.8.refs_1_), channel_id=1, source_target_pairs={{8,0},{12,4},{16,8},{20,12},{9,1},{13,5},{17,9},{21,13},{10,2},{14... | collective-permute-start | bytes 3145736 | tf_op jit(solution)/shard_map/ppermute | solution.py:31
  103.6 64.0 %collective-permute-start.11 = (bf16[512,1024]{1,0:T(8,128)(2,1)}, bf16[512,1024]{1,0:T(8,128)(2,1)}, u32[]{:S(2)}, u32[]{:S(2)}) collective-permute-start(bf16[512,1024]{1,0:T(8,128)(2,1)} %collective-permute-done.9.refs_2_), channel_id=1, source_target_pairs={{8,16},{12,20},{16,24},{20,28},{9,17},{13,21},{17,25},{21,29},{10,... | collective-permute-start | bytes 3145736 | tf_op jit(solution)/shard_map/ppermute | solution.py:31
  105.2 62.4 %collective-permute-start.13 = (bf16[512,1024]{1,0:T(8,128)(2,1)}, bf16[512,1024]{1,0:T(8,128)(2,1)}, u32[]{:S(2)}, u32[]{:S(2)}) collective-permute-start(bf16[512,1024]{1,0:T(8,128)(2,1)} %collective-permute-done.3.refs_2_), channel_id=1, source_target_pairs={{8,12},{12,8},{16,20},{20,16},{24,28},{28,24},{9,13},{13,9},{17,21... | collective-permute-start | bytes 3145736 | tf_op jit(solution)/shard_map/ppermute | solution.py:36
  107.5 44.0 %all-to-all-start.2 = ((bf16[8,8,2048]{2,1,0:T(8,128)(2,1)}), bf16[8,8,2048]{2,1,0:T(8,128)(2,1)S(1)}, u32[]{:S(2)}, u32[]{:S(2)}) async-start(bf16[8,8,2048]{2,1,0:T(8,128)(2,1)} %broadcast_in_dim.16), calls=%async_computation.2 | async-start | bytes 524288 | tf_op jit(solution)/shard_map/all_to_all | solution.py:341
  151.5 18.0 %copy-start.6 = (bf16[8,8,2048]{2,1,0:T(8,128)(2,1)}, bf16[8,8,2048]{2,1,0:T(8,128)(2,1)S(1)}, u32[]{:S(2)}) copy-start(bf16[8,8,2048]{2,1,0:T(8,128)(2,1)S(1)} %all-to-all-done.2) | copy-start | bytes 786436
  167.6 9.6 %collective-permute-start.16 = (bf16[256,1024]{1,0:T(8,128)(2,1)}, bf16[256,1024]{1,0:T(8,128)(2,1)}, u32[]{:S(2)}, u32[]{:S(2)}) collective-permute-start(bf16[256,1024]{1,0:T(8,128)(2,1)} %collective-permute-done.1.mine), channel_id=1, source_target_pairs={{0,2},{1,3},{2,0},{3,1},{4,6},{5,7},{6,4},{7,5},{8,10},{9,11},{10,... | collective-permute-start | bytes 1572872 | tf_op jit(solution)/shard_map/ppermute | solution.py:298
  169.5 15.5 %copy-start.5 = (bf16[512,1024]{1,0:T(8,128)(2,1)}, bf16[512,1024]{1,0:T(8,128)(2,1)S(1)}, u32[]{:S(2)}) copy-start(bf16[512,1024]{1,0:T(8,128)(2,1)S(1)} %broadcast_select_fusion.1.refs_2_) | copy-start | bytes 3145732
  169.5 21.4 %collective-permute-start.18 = (bf16[512,1024]{1,0:T(8,128)(2,1)S(1)}, bf16[512,1024]{1,0:T(8,128)(2,1)}, u32[]{:S(2)}, u32[]{:S(2)}) collective-permute-start(bf16[512,1024]{1,0:T(8,128)(2,1)S(1)} %broadcast_select_fusion.1.refs_2_), channel_id=1, source_target_pairs={{8,0},{12,4},{16,24},{20,28},{9,1},{13,5},{17,25},{21,29},{10,2},{... | collective-permute-start | bytes 3145736 | tf_op jit(solution)/shard_map/ppermute | solution.py:31
  170.8 27.3 %collective-permute-start.19 = (bf16[512,1024]{1,0:T(8,128)(2,1)}, bf16[512,1024]{1,0:T(8,128)(2,1)S(1)}, u32[]{:S(2)}, u32[]{:S(2)}) collective-permute-start(bf16[512,1024]{1,0:T(8,128)(2,1)} %collective-permute-done.12.refs_0_.refs_4_), channel_id=1, source_target_pairs={{0,4},{4,0},{24,28},{28,24},{1,5},{5,1},{25,29},{29,25},{2,6},{6,2... | collective-permute-start | bytes 3145736 | tf_op jit(solution)/shard_map/ppermute | solution.py:36
  174.2 10.9 %collective-permute-start.15 = (bf16[256,1024]{1,0:T(8,128)(2,1)}, bf16[256,1024]{1,0:T(8,128)(2,1)}, u32[]{:S(2)}, u32[]{:S(2)}) collective-permute-start(bf16[256,1024]{1,0:T(8,128)(2,1)} %collective-permute-done.1.mine), channel_id=1, source_target_pairs={{0,1},{1,0},{2,3},{3,2},{4,5},{5,4},{6,7},{7,6},{8,9},{9,8},{10,11... | collective-permute-start | bytes 1572872 | tf_op jit(solution)/shard_map/ppermute | solution.py:298
  177.2 7.9 %collective-permute-start.17 = (bf16[256,1024]{1,0:T(8,128)(2,1)}, bf16[256,1024]{1,0:T(8,128)(2,1)}, u32[]{:S(2)}, u32[]{:S(2)}) collective-permute-start(bf16[256,1024]{1,0:T(8,128)(2,1)} %collective-permute-done.16.by_y), channel_id=1, source_target_pairs={{0,1},{1,0},{2,3},{3,2},{4,5},{5,4},{6,7},{7,6},{8,9},{9,8},{10,11... | collective-permute-start | bytes 1572872 | tf_op jit(solution)/shard_map/ppermute | solution.py:298
  196.7 8.9 %collective-permute-start.20 = (bf16[256,512]{1,0:T(8,128)(2,1)}, bf16[256,512]{1,0:T(8,128)(2,1)S(1)}, u32[]{:S(2)}, u32[]{:S(2)}) collective-permute-start(bf16[256,512]{1,0:T(8,128)(2,1)} %get-tuple-element.108), channel_id=1, source_target_pairs={{0,4},{4,0},{8,12},{12,8},{16,20},{20,16},{24,28},{28,24},{1,5},{5... | collective-permute-start | bytes 786440 | tf_op jit(solution)/shard_map/ppermute | solution.py:36
  198.1 1.0 copy-start.4
  204.5 9.0 %copy-start.7 = (bf16[1,64,8,512]{3,1,0,2:T(8,128)(2,1)S(1)}, bf16[1,64,8,512]{3,1,0,2:T(8,128)(2,1)}, u32[]{:S(2)}) copy-start(bf16[1,64,8,512]{3,1,0,2:T(8,128)(2,1)} %all_to_all.64) | copy-start | bytes 1572868
  209.9 18.1 %all-to-all-start.4 = ((f32[8,8,2048]{2,1,0:T(8,128)}), f32[8,8,2048]{2,1,0:T(8,128)S(1)}, u32[]{:S(2)}, u32[]{:S(2)}) async-start(f32[8,8,2048]{2,1,0:T(8,128)} %bitcast.48), calls=%async_computation.4 | async-start | bytes 1048576 | tf_op jit(solution)/shard_map/all_to_all | solution.py:424
  213.5 14.5 %collective-permute-start.21 = (bf16[8,64,512]{2,1,0:T(8,128)(2,1)S(1)}, bf16[8,64,512]{2,1,0:T(8,128)(2,1)}, u32[]{:S(2)}, u32[]{:S(2)}) collective-permute-start(bf16[8,64,512]{2,1,0:T(8,128)(2,1)S(1)} %bitcast.43), channel_id=1, source_target_pairs={{0,2},{1,3},{2,0},{3,1},{4,6},{5,7},{6,4},{7,5},{8,10},{9,11},{10,... | collective-permute-start | bytes 1572872 | tf_op jit(solution)/shard_map/ppermute | solution.py:298
  222.9 18.3 %copy-start.3 = (bf16[512,1024]{1,0:T(8,128)(2,1)S(1)}, bf16[512,1024]{1,0:T(8,128)(2,1)}, u32[]{:S(2)}) copy-start(bf16[512,1024]{1,0:T(8,128)(2,1)} %param.14) | copy-start | bytes 3145732
  247.0 58.7 %all-to-all-start.7 = ((bf16[4,2,256,512]{3,2,1,0:T(8,128)(2,1)}), bf16[4,2,256,512]{3,2,1,0:T(8,128)(2,1)S(1)}, u32[]{:S(2)}, u32[]{:S(2)}) async-start(bf16[4,2,256,512]{3,2,1,0:T(8,128)(2,1)} %shard_map.108), calls=%async_computation.7 | async-start | bytes 4194304 | tf_op jit(solution)/shard_map/all_to_all | solution.py:438
  252.5 14.2 %collective-permute-start.23 = (bf16[256,1024]{1,0:T(8,128)(2,1)}, bf16[256,1024]{1,0:T(8,128)(2,1)S(1)}, u32[]{:S(2)}, u32[]{:S(2)}) collective-permute-start(bf16[256,1024]{1,0:T(8,128)(2,1)} %get-tuple-element.119.refs_2_), channel_id=1, source_target_pairs={{0,4},{4,0},{8,12},{12,8},{16,20},{20,16},{24,28},{28,24},{1,5},{5... | collective-permute-start | bytes 1572872 | tf_op jit(solution)/shard_map/ppermute | solution.py:36
  253.9 25.2 %collective-permute-start.24 = (bf16[256,1024]{1,0:T(8,128)(2,1)}, bf16[256,1024]{1,0:T(8,128)(2,1)}, u32[]{:S(2)}, u32[]{:S(2)}) collective-permute-start(bf16[256,1024]{1,0:T(8,128)(2,1)} %get-tuple-element.119.refs_2_), channel_id=1, source_target_pairs={{8,0},{12,4},{16,8},{20,12},{24,16},{28,20},{0,24},{4,28},{9,1},{1... | collective-permute-start | bytes 1572872 | tf_op jit(solution)/shard_map/ppermute | solution.py:31
  255.1 24.0 %collective-permute-start.25 = (bf16[256,1024]{1,0:T(8,128)(2,1)}, bf16[256,1024]{1,0:T(8,128)(2,1)}, u32[]{:S(2)}, u32[]{:S(2)}) collective-permute-start(bf16[256,1024]{1,0:T(8,128)(2,1)} %get-tuple-element.119.refs_2_), channel_id=1, source_target_pairs={{24,0},{28,4},{0,8},{4,12},{8,16},{12,20},{16,24},{20,28},{25,1},{... | collective-permute-start | bytes 1572872 | tf_op jit(solution)/shard_map/ppermute | solution.py:31
  258.2 47.6 %collective-permute-start.22 = (bf16[2,8,64,512]{3,2,1,0:T(8,128)(2,1)}, bf16[2,8,64,512]{3,2,1,0:T(8,128)(2,1)}, u32[]{:S(2)}, u32[]{:S(2)}) collective-permute-start(bf16[2,8,64,512]{3,2,1,0:T(8,128)(2,1)} %pad_maximum_fusion.1.refs_0_), channel_id=1, source_target_pairs={{0,1},{1,0},{2,3},{3,2},{4,5},{5,4},{6,7},{7,6},{8,9},{9,8},{10,11... | collective-permute-start | bytes 3145736 | tf_op jit(solution)/shard_map/ppermute | solution.py:298
  266.7 14.5 %copy-start.10 = (bf16[256,1024]{1,0:T(8,128)(2,1)}, bf16[256,1024]{1,0:T(8,128)(2,1)S(1)}, u32[]{:S(2)}) copy-start(bf16[256,1024]{1,0:T(8,128)(2,1)S(1)} %collective-permute-done.23.refs_6_) | copy-start | bytes 1572868
  279.1 15.2 %collective-permute-start.26 = (bf16[256,1024]{1,0:T(8,128)(2,1)}, bf16[256,1024]{1,0:T(8,128)(2,1)}, u32[]{:S(2)}, u32[]{:S(2)}) collective-permute-start(bf16[256,1024]{1,0:T(8,128)(2,1)} %collective-permute-done.24.refs_3_), channel_id=1, source_target_pairs={{0,4},{4,0},{8,12},{12,8},{16,20},{20,16},{24,28},{28,24},{1,5},{5... | collective-permute-start | bytes 1572872 | tf_op jit(solution)/shard_map/ppermute | solution.py:36
  280.2 23.2 %collective-permute-start.27 = (bf16[256,1024]{1,0:T(8,128)(2,1)}, bf16[256,1024]{1,0:T(8,128)(2,1)}, u32[]{:S(2)}, u32[]{:S(2)}) collective-permute-start(bf16[256,1024]{1,0:T(8,128)(2,1)} %collective-permute-done.25.refs_5_), channel_id=1, source_target_pairs={{0,4},{4,0},{8,12},{12,8},{16,20},{20,16},{24,28},{28,24},{1,5},{5... | collective-permute-start | bytes 1572872 | tf_op jit(solution)/shard_map/ppermute | solution.py:36
  281.2 24.6 %collective-permute-start.28 = (bf16[256,1024]{1,0:T(8,128)(2,1)}, bf16[256,1024]{1,0:T(8,128)(2,1)}, u32[]{:S(2)}, u32[]{:S(2)}) collective-permute-start(bf16[256,1024]{1,0:T(8,128)(2,1)} %get-tuple-element.119.refs_2_), channel_id=1, source_target_pairs={{16,0},{20,4},{24,8},{28,12},{0,16},{4,20},{8,24},{12,28},{17,1},{... | collective-permute-start | bytes 1572872 | tf_op jit(solution)/shard_map/ppermute | solution.py:31
  305.8 7.3 %copy-start.2 = (bf16[4,2,256,512]{3,2,1,0:T(8,128)(2,1)}, bf16[4,2,256,512]{3,2,1,0:T(8,128)(2,1)S(1)}, u32[]{:S(2)}) copy-start(bf16[4,2,256,512]{3,2,1,0:T(8,128)(2,1)S(1)} %all-to-all-done.7.parts) | copy-start | bytes 6291460
  305.8 13.4 %collective-permute-start.31 = (bf16[256,1024]{1,0:T(8,128)(2,1)}, bf16[256,1024]{1,0:T(8,128)(2,1)}, u32[]{:S(2)}, u32[]{:S(2)}) collective-permute-start(bf16[256,1024]{1,0:T(8,128)(2,1)} %collective-permute-done.28.refs_4_), channel_id=1, source_target_pairs={{0,4},{4,0},{8,12},{12,8},{16,20},{20,16},{24,28},{28,24},{1,5},{5... | collective-permute-start | bytes 1572872 | tf_op jit(solution)/shard_map/ppermute | solution.py:36
  306.9 8.8 %collective-permute-start.29 = (bf16[8,512]{1,0:T(8,128)(2,1)S(1)}, bf16[8,512]{1,0:T(8,128)(2,1)S(1)}, u32[]{:S(2)}, u32[]{:S(2)}) collective-permute-start(bf16[8,512]{1,0:T(8,128)(2,1)S(1)} %get-tuple-element.129), channel_id=1, source_target_pairs={{0,0},{1,8},{2,16},{3,24},{4,4},{5,12},{6,20},{7,28},{8,1},{9,9},{... | collective-permute-start | bytes 24584 | tf_op jit(solution)/shard_map/ppermute | solution.py:264
  308.8 6.9 %collective-permute-start.30 = (bf16[8,512]{1,0:T(8,128)(2,1)S(1)}, bf16[8,512]{1,0:T(8,128)(2,1)S(1)}, u32[]{:S(2)}, u32[]{:S(2)}) collective-permute-start(bf16[8,512]{1,0:T(8,128)(2,1)S(1)} %get-tuple-element.130), channel_id=1, source_target_pairs={{0,4},{1,12},{2,20},{3,28},{4,0},{5,8},{6,16},{7,24},{8,5},{9,13},... | collective-permute-start | bytes 24584 | tf_op jit(solution)/shard_map/ppermute | solution.py:264
  (1 other events, 0.7 us)

commit v10 on v9

--- a/solution.py
+++ b/solution.py
@@ -308,16 +308,22 @@
 
     relayed = line.n_z == 4
     wq_moved = line.first(query_weight)
-    image_cols = lax.all_to_all(image_flat, "dp", split_axis=1, concat_axis=0, tiled=True)
+    quarter_rows = rows // 4
+    live_rows = lax.dynamic_slice_in_dim(live_flat, quarter * quarter_rows, quarter_rows, 0)
+    both = jnp.concatenate([live_rows, image_flat], axis=0).reshape(-1, n_dp, own_width)
+    both = lax.all_to_all(both, "dp", split_axis=1, concat_axis=0)
+    both = both.reshape(n_dp, quarter_rows + image_rows, own_width)
     wo_keep = lax.dynamic_slice_in_dim(out_weight, x * half_cols, half_cols, 0)
     wo_send = lax.dynamic_slice_in_dim(out_weight, (1 - x) * half_cols, half_cols, 0)
     wo_pair = jnp.concatenate([wo_keep, line.swap(wo_send)], axis=1)
     quarter_cols = width // 4
     live_part = lax.dynamic_slice_in_dim(live_flat, quarter * quarter_cols, quarter_cols, 1)
     live_here = line.swap(live_part)
-    image_cols, wo_pair, live_here, live_flat, query_weight, *wq_moved = gate(
-        (image_cols, wo_pair, live_here, live_flat, query_weight, *wq_moved)
-    )
+    both, wo_pair, live_here, query_weight, *wq_moved = gate(
+        (both, wo_pair, live_here, query_weight, *wq_moved)
+    )
+    live_mine = both[:, :quarter_rows]
+    image_cols = both[:, quarter_rows:].reshape(images, own_width)
 
     n_moved = len(wq_moved)
     planes = [(0, 1, 2), (1, 2, 3)] if relayed else [None] * n_moved
@@ -330,8 +336,8 @@
     )
     part_kv = part_kv.reshape(n_dp, image_rows, 2 * local_cols)
     kv_own = jnp.sum(lax.all_to_all(part_kv, "dp", split_axis=0, concat_axis=0), axis=0)
-    kv_own, live_here, live_flat, *staged = gate(
-        (kv_own.astype(BF16), live_here, live_flat, *wq_others, *wq_moved, *wq_two, *wo_moved)
+    kv_own, live_here, *staged = gate(
+        (kv_own.astype(BF16), live_here, *wq_others, *wq_moved, *wq_two, *wo_moved)
     )
     wq_others, staged = staged[:2], staged[2:]
     wq_moved, wq_two, wo_moved = staged[:n_moved], staged[n_moved:-n_moved], staged[-n_moved:]
@@ -345,14 +351,8 @@
     wq_others += [line.swap(block, at) for block, at in zip(wq_moved[1:], planes[1:])]
     wq_others += [line.swap(block) for block in wq_last[:1]]
     kv_all = everywhere(kv_own).reshape(images, 2 * local_cols)
-    quarter_rows = rows // 4
-    live_rows = lax.dynamic_slice_in_dim(live_flat, quarter * quarter_rows, quarter_rows, 0)
-    live_mine = lax.all_to_all(
-        live_rows.reshape(quarter_rows, n_dp, own_width), "dp", split_axis=1, concat_axis=0
-    )
-    live_mine = live_mine.reshape(n_dp, quarter_rows, own_width)
-    kv_all, live_here, live_mine, wo_pair, live_flat, *staged = gate(
-        (kv_all, live_here, live_mine, wo_pair, live_flat, *wo_two, *wq_last, *wq_others)
+    kv_all, live_here, wo_pair, live_flat, *staged = gate(
+        (kv_all, live_here, wo_pair, live_flat, *wo_two, *wq_last, *wq_others)
     )
     wo_two, staged = staged[: len(wo_two)], staged[len(wo_two) :]
     wq_last, wq_others = staged[: len(wq_last)], staged[len(wq_last) :]
@@ -394,9 +394,7 @@
         [pltpu.VMEM((rows, half_cols), F32)] * 2,
         rows * width * local_cols,
     )
-    text_flat, live_mine, grad_keep, grad_send = gate(
-        (text_flat, live_mine, grad_keep, grad_send)
-    )
+    text_flat, grad_keep, grad_send = gate((text_flat, grad_keep, grad_send))
     grad_come = line.swap(grad_send)
     queries, attended = call(
         functools.partial(forward_kernel, line, relayed, late, image_own),
@@ -409,9 +407,8 @@
     wq_blocks = [*arrivals, *wq_others]
 
     att_next = [line.shift(attended, m) for m in (1, line.n_z - 1)]
+    att_far = [line.shift(attended, m) for m in range(2, line.n_z - 1)]
     att_swapped = line.swap(attended)
-    live_y = tensor_swap(live_mine, 2)
-
     query_grad, kv_part = call(
         functools.partial(backward_kernel, image_own),
         place,
@@ -431,23 +428,26 @@
         (),
         2 * rows * width * local_cols,
     )
-    kv_grad, term, live_mine, live_y = gate((kv_grad.astype(BF16), term, live_mine, live_y))
+    kv_grad, term, live_mine, att_swapped, *att_next = gate(
+        (kv_grad.astype(BF16), term, live_mine, att_swapped, *att_next)
+    )
     kv_grad_all = everywhere(kv_grad).reshape(images, 2 * local_cols)
-    live_pair = jnp.stack([live_mine, live_y])
 
     text_parts = lax.all_to_all(term, "tensor", split_axis=0, concat_axis=0).reshape(term.shape)
-    attended, att_swapped, *att_next = gate((attended, att_swapped, *att_next))
-    att_far = [line.shift(attended, m) for m in range(2, line.n_z - 1)]
     att_other_next = [line.swap(block) for block in att_next]
+    live_pair = jnp.stack([live_mine, tensor_swap(live_mine, 2)])
+    kv_grad_all, text_parts, live_pair, *staged = gate(
+        (kv_grad_all, text_parts, live_pair, *att_other_next, *att_far)
+    )
+    att_other_next, att_far = staged[:2], staged[2:]
+    att_other_far = [line.swap(block) for block in att_far]
     live_core = tensor_swap(live_pair, 1)
 
     image_term = matmul(kv_grad_all[:, :local_cols], key_weight, BACK)
     image_term = image_term + matmul(kv_grad_all[:, local_cols:], value_weight, BACK)
-    image_grad, text_parts, live_core, *staged = to_owner(
-        line, image_term.astype(BF16), text_parts, live_core, *att_other_next, *att_far
-    )
-    att_other_next, att_far = staged[:2], staged[2:]
-    att_other_far = [line.swap(block) for block in att_far]
+    image_grad, live_core, *att_other_far = to_owner(
+        line, image_term.astype(BF16), live_core, *att_other_far
+    )
     image_grad = image_grad.reshape(samples, image_own, width // n_tensor)
     text_grad = call(
         sum_kernel, place, (text_parts,), [shape((rows, width // n_tensor), BF16)]

time: 329 us -> 334 us (1.015)
  blocking collectives: 34.1 us -> 60.3 us
  waiting for transfers between devices: 140 us -> 125 us
  starting transfers between devices: 82.4 us -> 71.2 us
  local copies, waits for them, and re-layouts: 6.72 us -> 12.5 us
    all_to_all x1 -> x2, blocking collectives: 12.7 us -> 60.3 us  [everywhere(): return lax.all_to_all(copies, 'dp', split_axis=0, concat_axis=0)]
    all_to_all x2, waiting for transfers between devices: 38.9 us -> 0.01 us  [the longest x1 0.01 us: to_owner(): lax.all_to_all(terms.reshape(n_tensor, images // n_tensor, cols), 'tensor...]
    ppermute x5, waiting for transfers between devices: 2.93 us -> 35.4 us  [tensor_swap(): lax.ppermute(block, 'tensor', [(t, t ^ bit) for t in range(n_tensor)])]
    all_to_all x2 -> x0, blocking collectives: 21.4 us -> none  [the longest x1 16.1 us: shards(): lax.all_to_all(live_rows.reshape(quarter_rows, n_dp, own_width), 'dp', sp...]
    ppermute x13, waiting for transfers between devices: 14.9 us -> 6.21 us  [move(): return lax.ppermute(block, 'dp', pairs)]
    all_to_all x2, starting transfers between devices: 17.3 us -> 9.72 us  [the longest x1 4.92 us: to_owner(): lax.all_to_all(terms.reshape(n_tensor, images // n_tensor, cols), 'tensor...]
    ppermute x12, waiting for transfers between devices: 48.6 us -> 41.1 us  [swap(): return lax.ppermute(block, 'dp', pairs)]
    all_to_all x1, waiting for transfers between devices: 5.08 us -> 10.6 us  [shards(): lax.all_to_all(kv_part, 'dp', split_axis=0, concat_axis=0)]
  transfers between devices with their start and end apart: 37 -> 37, of which waited for: 14 -> 10; matrix products, arithmetic and copies ran while one was open for 5% -> 6% of each run, Pallas kernels for 11% -> 13%
where the time goes in v10:
time: 334 us; the launch traced here: 333 us
  waiting for transfers between devices  125 us (37%)
  starting transfers between devices  71.2 us (21%)
  blocking collectives  60.3 us (18%)
  Pallas kernels  45.5 us (14%)
  local copies, waits for them, and re-layouts  12.5 us (4%)
  other arithmetic  11.9 us (4%)
  matrix products  5.02 us (2%)
    all_to_all x2, blocking collectives, everywhere(): return lax.all_to_all(copies, 'dp', split_axis=0, concat_axis=0)  60.3 us
    pallas_call x8, Pallas kernels, call(): pl.pallas_call(kernel, out_shape=outs[0] if single else outs, in_specs=[p...  45.5 us
    ppermute x12, waiting for transfers between devices, swap(): return lax.ppermute(block, 'dp', pairs)  41.1 us
    ppermute x5, waiting for transfers between devices, tensor_swap(): lax.ppermute(block, 'tensor', [(t, t ^ bit) for t in range(n_tensor)])  35.4 us
    all_to_all x1, waiting for transfers between devices, shards(): lax.all_to_all(part_kv, 'dp', split_axis=0, concat_axis=0)  31.7 us
    ppermute x13, starting transfers between devices, move(): return lax.ppermute(block, 'dp', pairs)  25.2 us
    ppermute x12, starting transfers between devices, swap(): return lax.ppermute(block, 'dp', pairs)  17.6 us
    all_to_all x1, waiting for transfers between devices, shards(): lax.all_to_all(kv_part, 'dp', split_axis=0, concat_axis=0)  10.6 us
  transfers between devices with their start and end apart: 37, of which 10 were waited for; matrix products, arithmetic and copies ran while one was open for 6% of the time, Pallas kernels for 13%

profile of v10, /device:TPU:4, one launch (start us, length us, event | category | flops | bytes accessed | tf_op | source)
XLA Modules:
  0.0 332.6 jit_solution(13519577118165991535)
XLA Ops:
  0.6 1.4 collective-permute-start.2
  2.1 5.5 %collective-permute-start.3 = (bf16[512,1024]{1,0:T(8,128)(2,1)}, bf16[512,1024]{1,0:T(8,128)(2,1)}, u32[]{:S(2)}, u32[]{:S(2)}) collective-permute-start(bf16[512,1024]{1,0:T(8,128)(2,1)} %refs_0_.1), channel_id=1, source_target_pairs={{0,8},{4,12},{8,16},{12,20},{16,24},{20,28},{1,9},{5,13},{9,17},{1... | collective-permute-start | bytes 3145736 | tf_op jit(solution)/shard_map/ppermute | solution.py:31
  9.2 1.8 broadcast_select_fusion
  12.5 4.8 %all-to-all-start = ((bf16[1,72,8,512]{3,1,0,2:T(8,128)(2,1)}), bf16[1,72,8,512]{3,1,0,2:T(8,128)(2,1)}, u32[]{:S(2)}, u32[]{:S(2)}) async-start(bf16[1,72,8,512]{3,1,0,2:T(8,128)(2,1)} %copy.13), calls=%async_computation | async-start | bytes 1179648 | tf_op jit(solution)/shard_map/all_to_all | solution.py:314
  17.3 2.2 constant_dynamic-slice_fusion.2
  19.6 2.0 collective-permute-start
  21.8 17.4 %collective-permute-done = bf16[512,512]{1,0:T(8,128)(2,1)} collective-permute-done((bf16[512,512]{1,0:T(8,128)(2,1)}, bf16[512,512]{1,0:T(8,128)(2,1)}, u32[]{:S(2)}, u32[]{:S(2)}) %collective-permute-start) | collective-permute-done | bytes 524320 | tf_op jit(solution)/shard_map/ppermute | solution.py:36
  39.1 2.3 pad_maximum_fusion.refs_0_
  41.4 7.8 %collective-permute-done.1.mine = bf16[256,1024]{1,0:T(8,128)(2,1)} collective-permute-done((bf16[256,1024]{1,0:T(8,128)(2,1)S(1)}, bf16[256,1024]{1,0:T(8,128)(2,1)}, u32[]{:S(2)}, u32[]{:S(2)}) %collective-permute-start.1) | collective-permute-done | bytes 524320 | tf_op jit(solution)/shard_map/ppermute | solution.py:36
  50.5 4.4 %collective-permute-start.9 = (bf16[512,1024]{1,0:T(8,128)(2,1)}, bf16[512,1024]{1,0:T(8,128)(2,1)}, u32[]{:S(2)}, u32[]{:S(2)}) collective-permute-start(bf16[512,1024]{1,0:T(8,128)(2,1)} %pad_maximum_fusion.refs_0_), channel_id=1, source_target_pairs={{0,8},{4,12},{8,16},{12,20},{16,24},{20,28},{1,9},{5,13},{9,17},{1... | collective-permute-start | bytes 3145736 | tf_op jit(solution)/shard_map/ppermute | solution.py:31
  56.2 1.7 collective-permute-start.7
  61.5 11.4 %collective-permute-done.4.refs_4_.refs_5_ = bf16[512,1024]{1,0:T(8,128)(2,1)S(1)} collective-permute-done((bf16[512,1024]{1,0:T(8,128)(2,1)S(1)}, bf16[512,1024]{1,0:T(8,128)(2,1)S(1)}, u32[]{:S(2)}, u32[]{:S(2)}) %collective-permute-start.4) | collective-permute-done | bytes 1048608 | tf_op jit(solution)/shard_map/ppermute | solution.py:36
  73.9 2.3 collective-permute-start.5
  77.1 4.1 %all-to-all-start.1 = ((f32[8,8,2048]{2,1,0:T(8,128)}), f32[8,8,2048]{2,1,0:T(8,128)S(1)}, u32[]{:S(2)}, u32[]{:S(2)}) async-start(f32[8,8,2048]{2,1,0:T(8,128)} %maximum_bitcast_fusion), calls=%async_computation.1 | async-start | bytes 1048576 | tf_op jit(solution)/shard_map/all_to_all | solution.py:338
  81.2 31.7 %all-to-all-done.1 = f32[8,8,2048]{2,1,0:T(8,128)S(1)} async-done(((f32[8,8,2048]{2,1,0:T(8,128)}), f32[8,8,2048]{2,1,0:T(8,128)S(1)}, u32[]{:S(2)}, u32[]{:S(2)}) %all-to-all-start.1) | async-done | bytes 524320 | tf_op jit(solution)/shard_map/all_to_all | solution.py:338
  113.0 1.7 broadcast_select_fusion.2.refs_3_
  117.1 1.3 collective-permute-start.10
  119.2 1.6 collective-permute-start.13
  120.8 44.9 %all_to_all.45 = bf16[8,8,2048]{2,1,0:T(8,128)(2,1)} all-to-all(bf16[8,8,2048]{2,1,0:T(8,128)(2,1)S(1)} %broadcast_in_dim.16), channel_id=1, replica_groups=mesh['dp'=8,'tensor'=4] {'dp'}, dimensions={0} | all-to-all | bytes 524288 | tf_op jit(solution)/shard_map/all_to_all | solution.py:347
  169.6 2.9 collective-permute-start.19
  172.6 3.7 %collective-permute-done.16.by_y = bf16[256,1024]{1,0:T(8,128)(2,1)} collective-permute-done((bf16[256,1024]{1,0:T(8,128)(2,1)}, bf16[256,1024]{1,0:T(8,128)(2,1)}, u32[]{:S(2)}, u32[]{:S(2)}) %collective-permute-start.16) | collective-permute-done | bytes 524320 | tf_op jit(solution)/shard_map/ppermute | solution.py:298
  176.9 7.3 %shard_map.103.part = f32[256,1024]{1,0:T(8,128)} custom-call(s32[4]{0:T(128)} %pad_add_fusion.place, bf16[256,4096]{1,0:T(8,128)(2,1)} %bitcast.36, bf16[512,1024]{1,0:T(8,128)(2,1)} %refs_0_.1, bf16[512,1024]{1,0:T(8,128)(2,1)} %collective-permute-done.2.refs_1_, bf16[512,1024]{1,0:T(8,128)(2,1)} %collective-permute-done.3.refs_2_, ...), custom_call_target="tpu_custom_call" | custom-call | flops 2147483648 | bytes 11534336 | tf_op jit(solution)/shard_map/pallas_call | solution.py:226
  184.2 5.9 %shard_map.104 = (f32[256,512]{1,0:T(8,128)}, f32[256,512]{1,0:T(8,128)}) custom-call(s32[4]{0:T(128)} %pad_add_fusion.place, bf16[256,4096]{1,0:T(8,128)(2,1)} %bitcast.34, bf16[256,1024]{1,0:T(8,128)(2,1)} %collective-permute-done.1.mine, bf16[256,1024]{1,0:T(8,128)(2,1)} %collective-permute-done.15.by_core, ...), custom_call_target="tpu_custom_call" | custom-call | flops 1073741824 | bytes 8388608 | tf_op jit(solution)/shard_map/pallas_call | solution.py:226
  190.1 5.7 %shard_map.105 = (bf16[256,512]{1,0:T(8,128)(2,1)}, bf16[256,512]{1,0:T(8,128)(2,1)}) custom-call(s32[4]{0:T(128)} %pad_add_fusion.place, bf16[256,4096]{1,0:T(8,128)(2,1)} %bitcast.35, bf16[256,1024]{1,0:T(8,128)(2,1)} %collective-permute-done.1.mine, bf16[256,1024]{1,0:T(8,128)(2,1)} %collective-permute-done.15.by_core, ...), custom_call_target="tpu_custom_call" | custom-call | flops 1073741824 | bytes 7864320 | tf_op jit(solution)/shard_map/pallas_call | solution.py:226
  197.7 5.4 %shard_map.106 = (bf16[256,1024]{1,0:T(8,128)(2,1)}, bf16[256,1024]{1,0:T(8,128)(2,1)}) custom-call(s32[4]{0:T(128)} %pad_add_fusion.place, bf16[256,4096]{1,0:T(8,128)(2,1)} %bitcast.37, bf16[64,2048]{1,0:T(8,128)(2,1)} %bitcast.38, f32[256,1024]{1,0:T(8,128)} %shard_map.103.part, bf16[512,1024]{1,0:T(8,128)(2,1)} %collective-permute-done.12.refs_0_.refs_4_, ...), custom_call_target="tpu_custom_call" | custom-call | flops 1073741824 | bytes 6553600 | tf_op jit(solution)/shard_map/pallas_call | solution.py:226
  203.1 1.6 collective-permute-done.20.come
  205.4 3.6 %shard_map.107 = (bf16[256,1024]{1,0:T(8,128)(2,1)}, f32[64,2048]{1,0:T(8,128)}) custom-call(s32[4]{0:T(128)} %pad_add_fusion.place, bf16[256,1024]{1,0:T(8,128)(2,1)} %get-tuple-element.100.query, bf16[64,2048]{1,0:T(8,128)(2,1)} %bitcast.39, bf16[256,512]{1,0:T(8,128)(2,1)} %get-tuple-element.101.keep, bf16[256,512]{1,0:T(8,128)(2,1)} %copy-done.10), custom_call_target="tpu_custom_call" | custom-call | flops 167772160 | bytes 2359296 | tf_op jit(solution)/shard_map/pallas_call | solution.py:226
  209.0 3.5 %all-to-all-start.3 = ((f32[8,8,2048]{2,1,0:T(8,128)}), f32[8,8,2048]{2,1,0:T(8,128)S(1)}, u32[]{:S(2)}, u32[]{:S(2)}) async-start(f32[8,8,2048]{2,1,0:T(8,128)} %bitcast.45), calls=%async_computation.3 | async-start | bytes 1048576 | tf_op jit(solution)/shard_map/all_to_all | solution.py:421
  212.5 1.9 collective-permute-start.23
  214.5 2.0 collective-permute-start.22
  216.4 1.9 collective-permute-start.21
  218.3 1.9 slice.23
  220.1 8.8 %shard_map.108 = bf16[4,2,256,512]{3,2,1,0:T(8,128)(2,1)} custom-call(s32[4]{0:T(128)} %pad_add_fusion.place, bf16[256,1024]{1,0:T(8,128)(2,1)} %get-tuple-element.104.query_grad, bf16[512,1024]{1,0:T(8,128)(2,1)} %refs_0_.1, bf16[512,1024]{1,0:T(8,128)(2,1)} %collective-permute-done.2.refs_1_, bf16[512,1024]{1,0:T(8,128)(2,1)} %collective-permute-done.3.refs_2_, ...), custom_call_target="tpu_custom_call" | custom-call | flops 2147483648 | bytes 13107200 | tf_op jit(solution)/shard_map/pallas_call | solution.py:226
  229.0 10.6 %all-to-all-done.3 = f32[8,8,2048]{2,1,0:T(8,128)S(1)} async-done(((f32[8,8,2048]{2,1,0:T(8,128)}), f32[8,8,2048]{2,1,0:T(8,128)S(1)}, u32[]{:S(2)}, u32[]{:S(2)}) %all-to-all-start.3) | async-done | bytes 524320 | tf_op jit(solution)/shard_map/all_to_all | solution.py:421
  239.7 6.2 %collective-permute-done.22.refs_3_ = bf16[256,1024]{1,0:T(8,128)(2,1)S(1)} collective-permute-done((bf16[256,1024]{1,0:T(8,128)(2,1)S(1)}, bf16[256,1024]{1,0:T(8,128)(2,1)S(1)}, u32[]{:S(2)}, u32[]{:S(2)}) %collective-permute-start.22) | collective-permute-done | bytes 524320 | tf_op jit(solution)/shard_map/ppermute | solution.py:31
  246.6 15.4 %all_to_all.46 = bf16[8,8,2048]{2,1,0:T(8,128)(2,1)S(1)} all-to-all(bf16[8,8,2048]{2,1,0:T(8,128)(2,1)S(1)} %broadcast_in_dim.17), channel_id=1, replica_groups=mesh['dp'=8,'tensor'=4] {'dp'}, dimensions={0} | all-to-all | bytes 524288 | tf_op jit(solution)/shard_map/all_to_all | solution.py:347
  262.1 3.6 %all-to-all-start.5 = ((bf16[4,2,256,512]{3,2,1,0:T(8,128)(2,1)}), bf16[4,2,256,512]{3,2,1,0:T(8,128)(2,1)S(1)}, u32[]{:S(2)}, u32[]{:S(2)}) async-start(bf16[4,2,256,512]{3,2,1,0:T(8,128)(2,1)} %shard_map.108), calls=%async_computation.5 | async-start | bytes 4194304 | tf_op jit(solution)/shard_map/all_to_all | solution.py:436
  267.3 1.6 collective-permute-start.26
  268.9 31.7 %collective-permute-done.24 = bf16[8,64,512]{2,1,0:T(8,128)(2,1)S(1)} collective-permute-done((bf16[8,64,512]{2,1,0:T(8,128)(2,1)}, bf16[8,64,512]{2,1,0:T(8,128)(2,1)S(1)}, u32[]{:S(2)}, u32[]{:S(2)}) %collective-permute-start.24) | collective-permute-done | bytes 524320 | tf_op jit(solution)/shard_map/ppermute | solution.py:298
  300.6 2.1 pad_maximum_fusion.1.refs_0_
  304.4 1.5 collective-permute-start.29
  306.4 2.3 fusion
  308.7 4.9 %all-to-all-start.6 = ((bf16[4,16,512]{2,1,0:T(8,128)(2,1)}), bf16[4,16,512]{2,1,0:T(8,128)(2,1)S(1)}, u32[]{:S(2)}, u32[]{:S(2)}) async-start(bf16[4,16,512]{2,1,0:T(8,128)(2,1)} %bitcast.17), calls=%async_computation.6 | async-start | bytes 131072 | tf_op jit(solution)/shard_map/all_to_all | solution.py:248
  313.6 2.6 shard_map.109
  316.3 2.8 collective-permute-done.29.refs_8_
  319.1 4.1 %collective-permute-start.30 = (bf16[8,512]{1,0:T(8,128)(2,1)S(1)}, bf16[8,512]{1,0:T(8,128)(2,1)S(1)}, u32[]{:S(2)}, u32[]{:S(2)}) collective-permute-start(bf16[8,512]{1,0:T(8,128)(2,1)S(1)} %get-tuple-element.123), channel_id=1, source_target_pairs={{0,0},{1,8},{2,16},{3,24},{4,4},{5,12},{6,20},{7,28},{8,1},{9,9},{... | collective-permute-start | bytes 24584 | tf_op jit(solution)/shard_map/ppermute | solution.py:264
  323.2 2.6 collective-permute-start.31
  325.8 6.2 %shard_map.110 = bf16[1024,512]{1,0:T(8,128)(2,1)} custom-call(s32[4]{0:T(128)} %pad_add_fusion.place, bf16[2,8,64,512]{3,2,1,0:T(8,128)(2,1)} %pad_maximum_fusion.1.refs_0_, bf16[2,8,64,512]{3,2,1,0:T(8,128)(2,1)} %collective-permute-done.28.refs_1_, bf16[256,1024]{1,0:T(8,128)(2,1)} %get-tuple-element.105.refs_2_, bf16[256,1024]{1,0:T(8,128)(2,1)} %copy-done.13, ...), custom_call_target="tpu_custom_call" | custom-call | flops 2147483648 | bytes 7340032 | tf_op jit(solution)/shard_map/pallas_call | solution.py:226
  (98 shorter events, 26.8 us)
Async XLA Ops:
  0.6 58.6 %copy-start = (bf16[512,1024]{1,0:T(8,128)(2,1)S(1)}, bf16[512,1024]{1,0:T(8,128)(2,1)}, u32[]{:S(2)}) copy-start(bf16[512,1024]{1,0:T(8,128)(2,1)} %param.14) | copy-start | bytes 3145732
  0.6 48.6 %collective-permute-start.2 = (bf16[512,1024]{1,0:T(8,128)(2,1)}, bf16[512,1024]{1,0:T(8,128)(2,1)}, u32[]{:S(2)}, u32[]{:S(2)}) collective-permute-start(bf16[512,1024]{1,0:T(8,128)(2,1)} %refs_0_.1), channel_id=1, source_target_pairs={{8,0},{12,4},{16,8},{20,12},{24,16},{28,20},{9,1},{13,5},{17,9},{2... | collective-permute-start | bytes 3145736 | tf_op jit(solution)/shard_map/ppermute | solution.py:31
  2.1 47.1 %collective-permute-start.3 = (bf16[512,1024]{1,0:T(8,128)(2,1)}, bf16[512,1024]{1,0:T(8,128)(2,1)}, u32[]{:S(2)}, u32[]{:S(2)}) collective-permute-start(bf16[512,1024]{1,0:T(8,128)(2,1)} %refs_0_.1), channel_id=1, source_target_pairs={{0,8},{4,12},{8,16},{12,20},{16,24},{20,28},{1,9},{5,13},{9,17},{1... | collective-permute-start | bytes 3145736 | tf_op jit(solution)/shard_map/ppermute | solution.py:31
  11.0 10.6 %copy-start.1 = (bf16[2,128,4096]{2,1,0:T(8,128)(2,1)}, bf16[2,128,4096]{2,1,0:T(8,128)(2,1)S(1)}, u32[]{:S(2)}) copy-start(bf16[2,128,4096]{2,1,0:T(8,128)(2,1)S(1)} %broadcast_select_fusion) | copy-start | bytes 6291460
  12.5 36.7 %all-to-all-start = ((bf16[1,72,8,512]{3,1,0,2:T(8,128)(2,1)}), bf16[1,72,8,512]{3,1,0,2:T(8,128)(2,1)}, u32[]{:S(2)}, u32[]{:S(2)}) async-start(bf16[1,72,8,512]{3,1,0,2:T(8,128)(2,1)} %copy.13), calls=%async_computation | async-start | bytes 1179648 | tf_op jit(solution)/shard_map/all_to_all | solution.py:314
  19.6 19.5 %collective-permute-start = (bf16[512,512]{1,0:T(8,128)(2,1)}, bf16[512,512]{1,0:T(8,128)(2,1)}, u32[]{:S(2)}, u32[]{:S(2)}) collective-permute-start(bf16[512,512]{1,0:T(8,128)(2,1)} %get-tuple-element.122), channel_id=1, source_target_pairs={{0,4},{4,0},{8,12},{12,8},{16,20},{20,16},{24,28},{28,24},{1,5},{5... | collective-permute-start | bytes 1572872 | tf_op jit(solution)/shard_map/ppermute | solution.py:36
  21.6 27.6 %copy-start.4 = (bf16[512,1024]{1,0:T(8,128)(2,1)S(1)}, bf16[512,1024]{1,0:T(8,128)(2,1)}, u32[]{:S(2)}) copy-start(bf16[512,1024]{1,0:T(8,128)(2,1)} %refs_0_.1) | copy-start | bytes 3145732
  21.7 38.7 %copy-start.8 = (bf16[512,1024]{1,0:T(8,128)(2,1)S(1)}, bf16[512,1024]{1,0:T(8,128)(2,1)}, u32[]{:S(2)}) copy-start(bf16[512,1024]{1,0:T(8,128)(2,1)} %param.13) | copy-start | bytes 3145732
  21.7 27.5 %collective-permute-start.1 = (bf16[256,1024]{1,0:T(8,128)(2,1)S(1)}, bf16[256,1024]{1,0:T(8,128)(2,1)}, u32[]{:S(2)}, u32[]{:S(2)}) collective-permute-start(bf16[256,1024]{1,0:T(8,128)(2,1)S(1)} %constant_dynamic-slice_fusion), channel_id=1, source_target_pairs={{0,4},{4,0},{8,12},{12,8},{16,20},{20,16},{24,28},{28,24},{1,5},{5... | collective-permute-start | bytes 1572872 | tf_op jit(solution)/shard_map/ppermute | solution.py:36
  49.2 23.7 %collective-permute-start.4 = (bf16[512,1024]{1,0:T(8,128)(2,1)S(1)}, bf16[512,1024]{1,0:T(8,128)(2,1)S(1)}, u32[]{:S(2)}, u32[]{:S(2)}) collective-permute-start(bf16[512,1024]{1,0:T(8,128)(2,1)S(1)} %copy-done.4), channel_id=1, source_target_pairs={{0,4},{4,0},{8,12},{12,8},{16,20},{20,16},{24,28},{28,24},{1,5},{5... | collective-permute-start | bytes 3145736 | tf_op jit(solution)/shard_map/ppermute | solution.py:36
  50.5 62.4 %collective-permute-start.9 = (bf16[512,1024]{1,0:T(8,128)(2,1)}, bf16[512,1024]{1,0:T(8,128)(2,1)}, u32[]{:S(2)}, u32[]{:S(2)}) collective-permute-start(bf16[512,1024]{1,0:T(8,128)(2,1)} %pad_maximum_fusion.refs_0_), channel_id=1, source_target_pairs={{0,8},{4,12},{8,16},{12,20},{16,24},{20,28},{1,9},{5,13},{9,17},{1... | collective-permute-start | bytes 3145736 | tf_op jit(solution)/shard_map/ppermute | solution.py:31
  54.9 58.0 %collective-permute-start.8 = (bf16[512,1024]{1,0:T(8,128)(2,1)}, bf16[512,1024]{1,0:T(8,128)(2,1)}, u32[]{:S(2)}, u32[]{:S(2)}) collective-permute-start(bf16[512,1024]{1,0:T(8,128)(2,1)} %pad_maximum_fusion.refs_0_), channel_id=1, source_target_pairs={{8,0},{12,4},{16,8},{20,12},{24,16},{28,20},{9,1},{13,5},{17,9},{2... | collective-permute-start | bytes 3145736 | tf_op jit(solution)/shard_map/ppermute | solution.py:31
  56.2 56.7 %collective-permute-start.7 = (bf16[512,1024]{1,0:T(8,128)(2,1)}, bf16[512,1024]{1,0:T(8,128)(2,1)}, u32[]{:S(2)}, u32[]{:S(2)}) collective-permute-start(bf16[512,1024]{1,0:T(8,128)(2,1)} %collective-permute-done.3.refs_2_), channel_id=1, source_target_pairs={{8,16},{12,20},{16,24},{20,28},{9,17},{13,21},{17,25},{21,29},{10,... | collective-permute-start | bytes 3145736 | tf_op jit(solution)/shard_map/ppermute | solution.py:31
  57.9 55.0 %collective-permute-start.6 = (bf16[512,1024]{1,0:T(8,128)(2,1)}, bf16[512,1024]{1,0:T(8,128)(2,1)}, u32[]{:S(2)}, u32[]{:S(2)}) collective-permute-start(bf16[512,1024]{1,0:T(8,128)(2,1)} %collective-permute-done.2.refs_1_), channel_id=1, source_target_pairs={{8,0},{12,4},{16,8},{20,12},{9,1},{13,5},{17,9},{21,13},{10,2},{14... | collective-permute-start | bytes 3145736 | tf_op jit(solution)/shard_map/ppermute | solution.py:31
  73.0 1.0 copy-start.5
  73.9 39.0 %collective-permute-start.5 = (bf16[512,1024]{1,0:T(8,128)(2,1)}, bf16[512,1024]{1,0:T(8,128)(2,1)S(1)}, u32[]{:S(2)}, u32[]{:S(2)}) collective-permute-start(bf16[512,1024]{1,0:T(8,128)(2,1)} %collective-permute-done.2.refs_1_), channel_id=1, source_target_pairs={{0,4},{4,0},{8,12},{12,8},{16,20},{20,16},{1,5},{5,1},{9,13},{13,9... | collective-permute-start | bytes 3145736 | tf_op jit(solution)/shard_map/ppermute | solution.py:36
  77.1 35.8 %all-to-all-start.1 = ((f32[8,8,2048]{2,1,0:T(8,128)}), f32[8,8,2048]{2,1,0:T(8,128)S(1)}, u32[]{:S(2)}, u32[]{:S(2)}) async-start(f32[8,8,2048]{2,1,0:T(8,128)} %maximum_bitcast_fusion), calls=%async_computation.1 | async-start | bytes 1048576 | tf_op jit(solution)/shard_map/all_to_all | solution.py:338
  113.0 55.4 %copy-start.6 = (bf16[512,1024]{1,0:T(8,128)(2,1)}, bf16[512,1024]{1,0:T(8,128)(2,1)S(1)}, u32[]{:S(2)}) copy-start(bf16[512,1024]{1,0:T(8,128)(2,1)S(1)} %collective-permute-done.5.refs_5_.refs_6_) | copy-start | bytes 3145732
  114.7 62.2 %copy-start.2 = (bf16[512,1024]{1,0:T(8,128)(2,1)}, bf16[512,1024]{1,0:T(8,128)(2,1)S(1)}, u32[]{:S(2)}) copy-start(bf16[512,1024]{1,0:T(8,128)(2,1)S(1)} %broadcast_select_fusion.2.refs_3_) | copy-start | bytes 3145732
  114.7 51.0 %collective-permute-start.14 = (bf16[512,1024]{1,0:T(8,128)(2,1)S(1)}, bf16[512,1024]{1,0:T(8,128)(2,1)S(1)}, u32[]{:S(2)}, u32[]{:S(2)}) collective-permute-start(bf16[512,1024]{1,0:T(8,128)(2,1)S(1)} %broadcast_select_fusion.2.refs_3_), channel_id=1, source_target_pairs={{0,4},{4,0},{8,12},{12,8},{16,20},{20,16},{24,28},{28,24},{1,5},{5... | collective-permute-start | bytes 3145736 | tf_op jit(solution)/shard_map/ppermute | solution.py:36
  115.9 49.9 %collective-permute-start.12 = (bf16[512,1024]{1,0:T(8,128)(2,1)S(1)}, bf16[512,1024]{1,0:T(8,128)(2,1)}, u32[]{:S(2)}, u32[]{:S(2)}) collective-permute-start(bf16[512,1024]{1,0:T(8,128)(2,1)S(1)} %broadcast_select_fusion.2.refs_3_), channel_id=1, source_target_pairs={{8,0},{12,4},{16,24},{20,28},{9,1},{13,5},{17,25},{21,29},{10,2},{... | collective-permute-start | bytes 3145736 | tf_op jit(solution)/shard_map/ppermute | solution.py:31
  117.1 49.6 %collective-permute-start.10 = (bf16[512,1024]{1,0:T(8,128)(2,1)}, bf16[512,1024]{1,0:T(8,128)(2,1)S(1)}, u32[]{:S(2)}, u32[]{:S(2)}) collective-permute-start(bf16[512,1024]{1,0:T(8,128)(2,1)} %collective-permute-done.8.refs_1_), channel_id=1, source_target_pairs={{8,0},{12,4},{16,8},{20,12},{9,1},{13,5},{17,9},{21,13},{10,2},{14... | collective-permute-start | bytes 3145736 | tf_op jit(solution)/shard_map/ppermute | solution.py:31
  118.4 48.3 %collective-permute-start.11 = (bf16[512,1024]{1,0:T(8,128)(2,1)}, bf16[512,1024]{1,0:T(8,128)(2,1)S(1)}, u32[]{:S(2)}, u32[]{:S(2)}) collective-permute-start(bf16[512,1024]{1,0:T(8,128)(2,1)} %collective-permute-done.9.refs_2_), channel_id=1, source_target_pairs={{8,16},{12,20},{16,24},{20,28},{9,17},{13,21},{17,25},{21,29},{10,... | collective-permute-start | bytes 3145736 | tf_op jit(solution)/shard_map/ppermute | solution.py:31
  119.2 47.5 %collective-permute-start.13 = (bf16[512,1024]{1,0:T(8,128)(2,1)}, bf16[512,1024]{1,0:T(8,128)(2,1)}, u32[]{:S(2)}, u32[]{:S(2)}) collective-permute-start(bf16[512,1024]{1,0:T(8,128)(2,1)} %collective-permute-done.3.refs_2_), channel_id=1, source_target_pairs={{8,12},{12,8},{16,20},{20,16},{24,28},{28,24},{9,13},{13,9},{17,21... | collective-permute-start | bytes 3145736 | tf_op jit(solution)/shard_map/ppermute | solution.py:36
  166.7 9.6 %collective-permute-start.16 = (bf16[256,1024]{1,0:T(8,128)(2,1)}, bf16[256,1024]{1,0:T(8,128)(2,1)}, u32[]{:S(2)}, u32[]{:S(2)}) collective-permute-start(bf16[256,1024]{1,0:T(8,128)(2,1)} %collective-permute-done.1.mine), channel_id=1, source_target_pairs={{0,2},{1,3},{2,0},{3,1},{4,6},{5,7},{6,4},{7,5},{8,10},{9,11},{10,... | collective-permute-start | bytes 1572872 | tf_op jit(solution)/shard_map/ppermute | solution.py:298
  168.4 21.8 %collective-permute-start.18 = (bf16[512,1024]{1,0:T(8,128)(2,1)}, bf16[512,1024]{1,0:T(8,128)(2,1)}, u32[]{:S(2)}, u32[]{:S(2)}) collective-permute-start(bf16[512,1024]{1,0:T(8,128)(2,1)} %broadcast_select_fusion.1.refs_2_), channel_id=1, source_target_pairs={{8,0},{12,4},{16,24},{20,28},{9,1},{13,5},{17,25},{21,29},{10,2},{... | collective-permute-start | bytes 3145736 | tf_op jit(solution)/shard_map/ppermute | solution.py:31
  169.6 27.1 %collective-permute-start.19 = (bf16[512,1024]{1,0:T(8,128)(2,1)}, bf16[512,1024]{1,0:T(8,128)(2,1)S(1)}, u32[]{:S(2)}, u32[]{:S(2)}) collective-permute-start(bf16[512,1024]{1,0:T(8,128)(2,1)} %collective-permute-done.12.refs_0_.refs_4_), channel_id=1, source_target_pairs={{0,4},{4,0},{24,28},{28,24},{1,5},{5,1},{25,29},{29,25},{2,6},{6,2... | collective-permute-start | bytes 3145736 | tf_op jit(solution)/shard_map/ppermute | solution.py:36
  172.5 11.7 %collective-permute-start.15 = (bf16[256,1024]{1,0:T(8,128)(2,1)}, bf16[256,1024]{1,0:T(8,128)(2,1)}, u32[]{:S(2)}, u32[]{:S(2)}) collective-permute-start(bf16[256,1024]{1,0:T(8,128)(2,1)} %collective-permute-done.1.mine), channel_id=1, source_target_pairs={{0,1},{1,0},{2,3},{3,2},{4,5},{5,4},{6,7},{7,6},{8,9},{9,8},{10,11... | collective-permute-start | bytes 1572872 | tf_op jit(solution)/shard_map/ppermute | solution.py:298
  176.3 8.0 %collective-permute-start.17 = (bf16[256,1024]{1,0:T(8,128)(2,1)}, bf16[256,1024]{1,0:T(8,128)(2,1)}, u32[]{:S(2)}, u32[]{:S(2)}) collective-permute-start(bf16[256,1024]{1,0:T(8,128)(2,1)} %collective-permute-done.16.by_y), channel_id=1, source_target_pairs={{0,1},{1,0},{2,3},{3,2},{4,5},{5,4},{6,7},{7,6},{8,9},{9,8},{10,11... | collective-permute-start | bytes 1572872 | tf_op jit(solution)/shard_map/ppermute | solution.py:298
  195.8 8.9 %collective-permute-start.20 = (bf16[256,512]{1,0:T(8,128)(2,1)}, bf16[256,512]{1,0:T(8,128)(2,1)S(1)}, u32[]{:S(2)}, u32[]{:S(2)}) collective-permute-start(bf16[256,512]{1,0:T(8,128)(2,1)} %get-tuple-element.102), channel_id=1, source_target_pairs={{0,4},{4,0},{8,12},{12,8},{16,20},{20,16},{24,28},{28,24},{1,5},{5... | collective-permute-start | bytes 786440 | tf_op jit(solution)/shard_map/ppermute | solution.py:36
  196.7 1.0 copy-start.9
  203.1 9.4 %copy-start.11 = (bf16[256,1024]{1,0:T(8,128)(2,1)S(1)}, bf16[256,1024]{1,0:T(8,128)(2,1)}, u32[]{:S(2)}) copy-start(bf16[256,1024]{1,0:T(8,128)(2,1)} %get-tuple-element.105.refs_2_) | copy-start | bytes 1572868
  209.0 30.6 %all-to-all-start.3 = ((f32[8,8,2048]{2,1,0:T(8,128)}), f32[8,8,2048]{2,1,0:T(8,128)S(1)}, u32[]{:S(2)}, u32[]{:S(2)}) async-start(f32[8,8,2048]{2,1,0:T(8,128)} %bitcast.45), calls=%async_computation.3 | async-start | bytes 1048576 | tf_op jit(solution)/shard_map/all_to_all | solution.py:421
  212.5 27.1 %collective-permute-start.23 = (bf16[256,1024]{1,0:T(8,128)(2,1)S(1)}, bf16[256,1024]{1,0:T(8,128)(2,1)S(1)}, u32[]{:S(2)}, u32[]{:S(2)}) collective-permute-start(bf16[256,1024]{1,0:T(8,128)(2,1)S(1)} %copy-done.11), channel_id=1, source_target_pairs={{24,0},{28,4},{0,8},{4,12},{8,16},{12,20},{16,24},{20,28},{25,1},{... | collective-permute-start | bytes 1572872 | tf_op jit(solution)/shard_map/ppermute | solution.py:31
  214.5 31.4 %collective-permute-start.22 = (bf16[256,1024]{1,0:T(8,128)(2,1)S(1)}, bf16[256,1024]{1,0:T(8,128)(2,1)S(1)}, u32[]{:S(2)}, u32[]{:S(2)}) collective-permute-start(bf16[256,1024]{1,0:T(8,128)(2,1)S(1)} %copy-done.11), channel_id=1, source_target_pairs={{8,0},{12,4},{16,8},{20,12},{24,16},{28,20},{0,24},{4,28},{9,1},{1... | collective-permute-start | bytes 1572872 | tf_op jit(solution)/shard_map/ppermute | solution.py:31
  216.4 29.4 %collective-permute-start.21 = (bf16[256,1024]{1,0:T(8,128)(2,1)S(1)}, bf16[256,1024]{1,0:T(8,128)(2,1)}, u32[]{:S(2)}, u32[]{:S(2)}) collective-permute-start(bf16[256,1024]{1,0:T(8,128)(2,1)S(1)} %copy-done.11), channel_id=1, source_target_pairs={{0,4},{4,0},{8,12},{12,8},{16,20},{20,16},{24,28},{28,24},{1,5},{5... | collective-permute-start | bytes 1572872 | tf_op jit(solution)/shard_map/ppermute | solution.py:36
  239.7 22.4 %copy-start.12 = (bf16[256,1024]{1,0:T(8,128)(2,1)}, bf16[256,1024]{1,0:T(8,128)(2,1)S(1)}, u32[]{:S(2)}) copy-start(bf16[256,1024]{1,0:T(8,128)(2,1)S(1)} %collective-permute-done.23.refs_5_) | copy-start | bytes 1572868
  262.1 42.3 %all-to-all-start.5 = ((bf16[4,2,256,512]{3,2,1,0:T(8,128)(2,1)}), bf16[4,2,256,512]{3,2,1,0:T(8,128)(2,1)S(1)}, u32[]{:S(2)}, u32[]{:S(2)}) async-start(bf16[4,2,256,512]{3,2,1,0:T(8,128)(2,1)} %shard_map.108), calls=%async_computation.5 | async-start | bytes 4194304 | tf_op jit(solution)/shard_map/all_to_all | solution.py:436
  265.7 35.0 %collective-permute-start.24 = (bf16[8,64,512]{2,1,0:T(8,128)(2,1)}, bf16[8,64,512]{2,1,0:T(8,128)(2,1)S(1)}, u32[]{:S(2)}, u32[]{:S(2)}) collective-permute-start(bf16[8,64,512]{2,1,0:T(8,128)(2,1)} %slice.23), channel_id=1, source_target_pairs={{0,2},{1,3},{2,0},{3,1},{4,6},{5,7},{6,4},{7,5},{8,10},{9,11},{10,... | collective-permute-start | bytes 1572872 | tf_op jit(solution)/shard_map/ppermute | solution.py:298
  265.8 37.0 %collective-permute-start.27 = (bf16[256,1024]{1,0:T(8,128)(2,1)}, bf16[256,1024]{1,0:T(8,128)(2,1)S(1)}, u32[]{:S(2)}, u32[]{:S(2)}) collective-permute-start(bf16[256,1024]{1,0:T(8,128)(2,1)} %get-tuple-element.105.refs_2_), channel_id=1, source_target_pairs={{16,0},{20,4},{24,8},{28,12},{0,16},{4,20},{8,24},{12,28},{17,1},{... | collective-permute-start | bytes 1572872 | tf_op jit(solution)/shard_map/ppermute | solution.py:31
  266.9 35.9 %collective-permute-start.25 = (bf16[256,1024]{1,0:T(8,128)(2,1)}, bf16[256,1024]{1,0:T(8,128)(2,1)S(1)}, u32[]{:S(2)}, u32[]{:S(2)}) collective-permute-start(bf16[256,1024]{1,0:T(8,128)(2,1)} %copy-done.13), channel_id=1, source_target_pairs={{0,4},{4,0},{8,12},{12,8},{16,20},{20,16},{24,28},{28,24},{1,5},{5... | collective-permute-start | bytes 1572872 | tf_op jit(solution)/shard_map/ppermute | solution.py:36
  267.3 37.0 %collective-permute-start.26 = (bf16[256,1024]{1,0:T(8,128)(2,1)}, bf16[256,1024]{1,0:T(8,128)(2,1)}, u32[]{:S(2)}, u32[]{:S(2)}) collective-permute-start(bf16[256,1024]{1,0:T(8,128)(2,1)} %copy-done.12), channel_id=1, source_target_pairs={{0,4},{4,0},{8,12},{12,8},{16,20},{20,16},{24,28},{28,24},{1,5},{5... | collective-permute-start | bytes 1572872 | tf_op jit(solution)/shard_map/ppermute | solution.py:36
  304.4 9.2 %copy-start.3 = (bf16[4,2,256,512]{3,2,1,0:T(8,128)(2,1)}, bf16[4,2,256,512]{3,2,1,0:T(8,128)(2,1)S(1)}, u32[]{:S(2)}) copy-start(bf16[4,2,256,512]{3,2,1,0:T(8,128)(2,1)S(1)} %all-to-all-done.5.parts) | copy-start | bytes 6291460
  304.4 14.7 %collective-permute-start.28 = (bf16[2,8,64,512]{3,2,1,0:T(8,128)(2,1)}, bf16[2,8,64,512]{3,2,1,0:T(8,128)(2,1)}, u32[]{:S(2)}, u32[]{:S(2)}) collective-permute-start(bf16[2,8,64,512]{3,2,1,0:T(8,128)(2,1)} %pad_maximum_fusion.1.refs_0_), channel_id=1, source_target_pairs={{0,1},{1,0},{2,3},{3,2},{4,5},{5,4},{6,7},{7,6},{8,9},{9,8},{10,11... | collective-permute-start | bytes 3145736 | tf_op jit(solution)/shard_map/ppermute | solution.py:298
  304.4 14.7 %collective-permute-start.29 = (bf16[256,1024]{1,0:T(8,128)(2,1)}, bf16[256,1024]{1,0:T(8,128)(2,1)}, u32[]{:S(2)}, u32[]{:S(2)}) collective-permute-start(bf16[256,1024]{1,0:T(8,128)(2,1)} %copy-done.14), channel_id=1, source_target_pairs={{0,4},{4,0},{8,12},{12,8},{16,20},{20,16},{24,28},{28,24},{1,5},{5... | collective-permute-start | bytes 1572872 | tf_op jit(solution)/shard_map/ppermute | solution.py:36
  308.7 7.6 %all-to-all-start.6 = ((bf16[4,16,512]{2,1,0:T(8,128)(2,1)}), bf16[4,16,512]{2,1,0:T(8,128)(2,1)S(1)}, u32[]{:S(2)}, u32[]{:S(2)}) async-start(bf16[4,16,512]{2,1,0:T(8,128)(2,1)} %bitcast.17), calls=%async_computation.6 | async-start | bytes 131072 | tf_op jit(solution)/shard_map/all_to_all | solution.py:248
  319.1 12.8 %collective-permute-start.30 = (bf16[8,512]{1,0:T(8,128)(2,1)S(1)}, bf16[8,512]{1,0:T(8,128)(2,1)S(1)}, u32[]{:S(2)}, u32[]{:S(2)}) collective-permute-start(bf16[8,512]{1,0:T(8,128)(2,1)S(1)} %get-tuple-element.123), channel_id=1, source_target_pairs={{0,0},{1,8},{2,16},{3,24},{4,4},{5,12},{6,20},{7,28},{8,1},{9,9},{... | collective-permute-start | bytes 24584 | tf_op jit(solution)/shard_map/ppermute | solution.py:264
  323.2 8.7 %collective-permute-start.31 = (bf16[8,512]{1,0:T(8,128)(2,1)S(1)}, bf16[8,512]{1,0:T(8,128)(2,1)S(1)}, u32[]{:S(2)}, u32[]{:S(2)}) collective-permute-start(bf16[8,512]{1,0:T(8,128)(2,1)S(1)} %get-tuple-element.124), channel_id=1, source_target_pairs={{0,4},{1,12},{2,20},{3,28},{4,0},{5,8},{6,16},{7,24},{8,5},{9,13},... | collective-permute-start | bytes 24584 | tf_op jit(solution)/shard_map/ppermute | solution.py:264
  (5 other events, 4.0 us)

commit v11 on v9

--- a/solution.py
+++ b/solution.py
@@ -12,7 +12,7 @@
 BF16 = jnp.bfloat16
 BACK = (((1,), (1,)), ((), ()))
 FIRST = (((0,), (0,)), ((), ()))
-VMEM_LIMIT = 60 * 1024 * 1024
+VMEM_LIMIT = 48 * 1024 * 1024
 
 
 def matmul(a, b, dims=None):
@@ -196,18 +196,12 @@
     each_block(line, place, relayed, range(n), write)
 
 
-def weight_grad_kernel(line, place, *refs):
-    live, refs = refs[:2], refs[2:]
-    n = (len(refs) - 2) // 2
-    attended, (out, total) = (refs[:n], refs[n : 2 * n]), refs[2 * n :]
+def weight_grad_kernel(place, own_pair, core_pair, attended, out, total):
     total[...] = jnp.zeros_like(total)
-
-    def add(i, e, index):
-        block = jnp.concatenate([part[i, index] for part in live for i in range(2)], axis=0)
-        term = matmul(attended[e][i][...], block, FIRST)
+    for d in range(attended.shape[0]):
+        parts = [pair[i, d] for pair in (own_pair, core_pair) for i in range(2)]
+        term = matmul(attended[d], jnp.concatenate(parts, axis=0), FIRST)
         total[...] += term.astype(BF16).astype(F32)
-
-    each_block(line, place, False, range(n), add)
     out[...] = total[...].astype(BF16)
 
 
@@ -345,14 +339,8 @@
     wq_others += [line.swap(block, at) for block, at in zip(wq_moved[1:], planes[1:])]
     wq_others += [line.swap(block) for block in wq_last[:1]]
     kv_all = everywhere(kv_own).reshape(images, 2 * local_cols)
-    quarter_rows = rows // 4
-    live_rows = lax.dynamic_slice_in_dim(live_flat, quarter * quarter_rows, quarter_rows, 0)
-    live_mine = lax.all_to_all(
-        live_rows.reshape(quarter_rows, n_dp, own_width), "dp", split_axis=1, concat_axis=0
-    )
-    live_mine = live_mine.reshape(n_dp, quarter_rows, own_width)
-    kv_all, live_here, live_mine, wo_pair, live_flat, *staged = gate(
-        (kv_all, live_here, live_mine, wo_pair, live_flat, *wo_two, *wq_last, *wq_others)
+    kv_all, live_here, wo_pair, live_flat, *staged = gate(
+        (kv_all, live_here, wo_pair, live_flat, *wo_two, *wq_last, *wq_others)
     )
     wo_two, staged = staged[: len(wo_two)], staged[len(wo_two) :]
     wq_last, wq_others = staged[: len(wq_last)], staged[len(wq_last) :]
@@ -394,8 +382,8 @@
         [pltpu.VMEM((rows, half_cols), F32)] * 2,
         rows * width * local_cols,
     )
-    text_flat, live_mine, grad_keep, grad_send = gate(
-        (text_flat, live_mine, grad_keep, grad_send)
+    text_flat, live_flat, grad_keep, grad_send = gate(
+        (text_flat, live_flat, grad_keep, grad_send)
     )
     grad_come = line.swap(grad_send)
     queries, attended = call(
@@ -408,10 +396,7 @@
     )
     wq_blocks = [*arrivals, *wq_others]
 
-    att_next = [line.shift(attended, m) for m in (1, line.n_z - 1)]
-    att_swapped = line.swap(attended)
-    live_y = tensor_swap(live_mine, 2)
-
+    attended_all = lax.all_gather(attended, "dp", axis=0)
     query_grad, kv_part = call(
         functools.partial(backward_kernel, image_own),
         place,
@@ -431,35 +416,33 @@
         (),
         2 * rows * width * local_cols,
     )
-    kv_grad, term, live_mine, live_y = gate((kv_grad.astype(BF16), term, live_mine, live_y))
+    kv_grad, term = gate((kv_grad.astype(BF16), term))
     kv_grad_all = everywhere(kv_grad).reshape(images, 2 * local_cols)
-    live_pair = jnp.stack([live_mine, live_y])
 
     text_parts = lax.all_to_all(term, "tensor", split_axis=0, concat_axis=0).reshape(term.shape)
-    attended, att_swapped, *att_next = gate((attended, att_swapped, *att_next))
-    att_far = [line.shift(attended, m) for m in range(2, line.n_z - 1)]
-    att_other_next = [line.swap(block) for block in att_next]
+    kv_grad_all, text_parts, live_flat = gate((kv_grad_all, text_parts, live_flat))
+    quarter_rows = rows // 4
+    live_rows = lax.dynamic_slice_in_dim(live_flat, quarter * quarter_rows, quarter_rows, 0)
+    live_mine = lax.all_to_all(
+        live_rows.reshape(quarter_rows, n_dp, own_width), "dp", split_axis=1, concat_axis=0
+    )
+    live_mine = live_mine.reshape(n_dp, quarter_rows, own_width)
+    live_pair = jnp.stack([live_mine, tensor_swap(live_mine, 2)])
     live_core = tensor_swap(live_pair, 1)
 
     image_term = matmul(kv_grad_all[:, :local_cols], key_weight, BACK)
     image_term = image_term + matmul(kv_grad_all[:, local_cols:], value_weight, BACK)
-    image_grad, text_parts, live_core, *staged = to_owner(
-        line, image_term.astype(BF16), text_parts, live_core, *att_other_next, *att_far
-    )
-    att_other_next, att_far = staged[:2], staged[2:]
-    att_other_far = [line.swap(block) for block in att_far]
+    image_grad, live_core = to_owner(line, image_term.astype(BF16), live_core)
     image_grad = image_grad.reshape(samples, image_own, width // n_tensor)
     text_grad = call(
         sum_kernel, place, (text_parts,), [shape((rows, width // n_tensor), BF16)]
     )
     text_grad = text_grad.reshape(samples, tok_rows, width // n_tensor)
 
-    att_blocks = [attended, att_next[0], *att_far, att_next[1]]
-    att_others = [att_swapped, att_other_next[0], *att_other_far, att_other_next[1]]
     weight_grad = call(
-        functools.partial(weight_grad_kernel, line),
-        place,
-        (live_pair, live_core, *att_blocks, *att_others),
+        weight_grad_kernel,
+        place,
+        (live_pair, live_core, attended_all),
         [shape((local_cols, own_width), BF16)],
         [pltpu.VMEM((local_cols, own_width), F32)],
         2 * n_dp * rows * local_cols * own_width,

time: 329 us -> 352 us (1.070)
  blocking collectives: 34.1 us -> 83.4 us
  waiting for transfers between devices: 140 us -> 116 us
  starting transfers between devices: 82.4 us -> 65.4 us
  between operations: 1 us -> 14.5 us
  local copies, waits for them, and re-layouts: 6.72 us -> 16.9 us
  Pallas kernels: 45.6 us -> 36.6 us
    all_to_all x1 -> x2, blocking collectives: 12.7 us -> 65.2 us  [everywhere(): return lax.all_to_all(copies, 'dp', split_axis=0, concat_axis=0)]
    all_to_all x1, waiting for transfers between devices: 31.1 us -> 2.27 us  [to_owner(): lax.all_to_all(terms.reshape(n_tensor, images // n_tensor, cols), 'tensor...]
    ppermute x12 -> x8, waiting for transfers between devices: 48.6 us -> 19.8 us  [swap(): return lax.ppermute(block, 'dp', pairs)]
    all_to_all x1, waiting for transfers between devices: 0.01 us -> 23.7 us  [shards(): lax.all_to_all(term, 'tensor', split_axis=0, concat_axis=0)]
    ppermute x5, waiting for transfers between devices: 2.93 us -> 15.4 us  [tensor_swap(): lax.ppermute(block, 'tensor', [(t, t ^ bit) for t in range(n_tensor)])]
    ppermute x13 -> x10, waiting for transfers between devices: 14.9 us -> 3.01 us  [move(): return lax.ppermute(block, 'dp', pairs)]
    pallas_call x8, Pallas kernels: 45.6 us -> 36.6 us  [call(): pl.pallas_call(kernel, out_shape=outs[0] if single else outs, in_specs=[p...]
    unnamed x25 -> x41, local copies, waits for them, and re-layouts: 1.87 us -> 10.8 us
  transfers between devices with their start and end apart: 37 -> 31, of which waited for: 14 -> 12; matrix products, arithmetic and copies ran while one was open for 5% -> 6% of each run, Pallas kernels for 11% -> 7%
where the time goes in v11:
time: 352 us; the launch traced here: 349 us
  waiting for transfers between devices  116 us (33%)
  blocking collectives  83.4 us (24%)
  starting transfers between devices  65.4 us (19%)
  Pallas kernels  36.6 us (10%)
  local copies, waits for them, and re-layouts  16.9 us (5%)
  between operations  14.5 us (4%)
  other arithmetic  12.7 us (4%)
    all_to_all x2, blocking collectives, everywhere(): return lax.all_to_all(copies, 'dp', split_axis=0, concat_axis=0)  65.2 us
    pallas_call x8, Pallas kernels, call(): pl.pallas_call(kernel, out_shape=outs[0] if single else outs, in_specs=[p...  36.6 us
    all_to_all x1, waiting for transfers between devices, shards(): lax.all_to_all(part_kv, 'dp', split_axis=0, concat_axis=0)  27.8 us
    all_to_all x1, waiting for transfers between devices, shards(): lax.all_to_all(term, 'tensor', split_axis=0, concat_axis=0)  23.7 us
    ppermute x10, starting transfers between devices, move(): return lax.ppermute(block, 'dp', pairs)  21.3 us
    ppermute x8, waiting for transfers between devices, swap(): return lax.ppermute(block, 'dp', pairs)  19.8 us
    all_to_all x1, blocking collectives, shards(): lax.all_to_all(live_rows.reshape(quarter_rows, n_dp, own_width), 'dp', sp...  18.3 us
    ppermute x5, waiting for transfers between devices, tensor_swap(): lax.ppermute(block, 'tensor', [(t, t ^ bit) for t in range(n_tensor)])  15.4 us
  transfers between devices with their start and end apart: 31, of which 12 were waited for; matrix products, arithmetic and copies ran while one was open for 6% of the time, Pallas kernels for 7%

profile of v11, /device:TPU:4, one launch (start us, length us, event | category | flops | bytes accessed | tf_op | source)
XLA Modules:
  0.0 349.0 jit_solution(14432426783013497771)
XLA Ops:
  7.2 1.4 collective-permute-start.2
  8.6 5.5 %collective-permute-start.3 = (bf16[512,1024]{1,0:T(8,128)(2,1)}, bf16[512,1024]{1,0:T(8,128)(2,1)}, u32[]{:S(2)}, u32[]{:S(2)}) collective-permute-start(bf16[512,1024]{1,0:T(8,128)(2,1)} %refs_0_.1), channel_id=1, source_target_pairs={{0,8},{4,12},{8,16},{12,20},{16,24},{20,28},{1,9},{5,13},{9,17},{1... | collective-permute-start | bytes 3145736 | tf_op jit(solution)/shard_map/ppermute | solution.py:31
  14.1 2.2 constant_dynamic-slice_fusion.3
  16.4 1.5 collective-permute-start
  17.9 3.2 broadcast_select_fusion
  21.1 2.0 constant_dynamic-slice_fusion.1
  24.3 3.9 %all-to-all-start = ((bf16[8,8,512]{2,0,1:T(8,128)(2,1)}), bf16[8,8,512]{2,0,1:T(8,128)(2,1)S(1)}, u32[]{:S(2)}, u32[]{:S(2)}) async-start(bf16[8,8,512]{2,0,1:T(8,128)(2,1)} %copy.14), calls=%async_computation | async-start | bytes 131072 | tf_op jit(solution)/shard_map/all_to_all | solution.py:305
  28.2 3.3 collective-permute-done
  31.5 2.3 pad_maximum_fusion.refs_0_
  33.8 7.8 %all-to-all-done = bf16[8,8,512]{2,0,1:T(8,128)(2,1)S(1)} async-done(((bf16[8,8,512]{2,0,1:T(8,128)(2,1)}), bf16[8,8,512]{2,0,1:T(8,128)(2,1)S(1)}, u32[]{:S(2)}, u32[]{:S(2)}) %all-to-all-start) | async-done | bytes 65568 | tf_op jit(solution)/shard_map/all_to_all | solution.py:305
  41.7 1.6 collective-permute-start.4
  43.2 1.3 collective-permute-start.8
  44.5 5.6 %collective-permute-start.9 = (bf16[512,1024]{1,0:T(8,128)(2,1)}, bf16[512,1024]{1,0:T(8,128)(2,1)}, u32[]{:S(2)}, u32[]{:S(2)}) collective-permute-start(bf16[512,1024]{1,0:T(8,128)(2,1)} %pad_maximum_fusion.refs_0_), channel_id=1, source_target_pairs={{0,8},{4,12},{8,16},{12,20},{16,24},{20,28},{1,9},{5,13},{9,17},{1... | collective-permute-start | bytes 3145736 | tf_op jit(solution)/shard_map/ppermute | solution.py:31
  51.4 1.6 collective-permute-start.7
  53.3 1.5 fusion.5
  54.8 10.4 %collective-permute-done.4.refs_4_.refs_5_ = bf16[512,1024]{1,0:T(8,128)(2,1)S(1)} collective-permute-done((bf16[512,1024]{1,0:T(8,128)(2,1)S(1)}, bf16[512,1024]{1,0:T(8,128)(2,1)S(1)}, u32[]{:S(2)}, u32[]{:S(2)}) %collective-permute-start.4) | collective-permute-done | bytes 1048608 | tf_op jit(solution)/shard_map/ppermute | solution.py:36
  66.2 3.4 collective-permute-start.5
  70.4 4.1 %all-to-all-start.1 = ((f32[8,8,2048]{2,1,0:T(8,128)}), f32[8,8,2048]{2,1,0:T(8,128)}, u32[]{:S(2)}, u32[]{:S(2)}) async-start(f32[8,8,2048]{2,1,0:T(8,128)} %maximum_bitcast_fusion), calls=%async_computation.1 | async-start | bytes 1048576 | tf_op jit(solution)/shard_map/all_to_all | solution.py:326
  74.6 27.8 %all-to-all-done.1 = f32[8,8,2048]{2,1,0:T(8,128)} async-done(((f32[8,8,2048]{2,1,0:T(8,128)}), f32[8,8,2048]{2,1,0:T(8,128)}, u32[]{:S(2)}, u32[]{:S(2)}) %all-to-all-start.1) | async-done | bytes 524320 | tf_op jit(solution)/shard_map/all_to_all | solution.py:326
  103.6 1.3 broadcast_select_fusion.2.refs_3_
  104.9 1.3 collective-permute-start.12
  109.1 1.7 collective-permute-start.13
  110.8 44.7 %all_to_all.64 = bf16[8,8,2048]{2,1,0:T(8,128)(2,1)S(1)} all-to-all(bf16[8,8,2048]{2,1,0:T(8,128)(2,1)S(1)} %broadcast_in_dim.16), channel_id=1, replica_groups=mesh['dp'=8,'tensor'=4] {'dp'}, dimensions={0} | all-to-all | bytes 524288 | tf_op jit(solution)/shard_map/all_to_all | solution.py:335
  159.4 3.0 collective-permute-start.19
  162.6 4.2 %collective-permute-done.16.by_y = bf16[256,1024]{1,0:T(8,128)(2,1)} collective-permute-done((bf16[256,1024]{1,0:T(8,128)(2,1)}, bf16[256,1024]{1,0:T(8,128)(2,1)}, u32[]{:S(2)}, u32[]{:S(2)}) %collective-permute-start.16) | collective-permute-done | bytes 524320 | tf_op jit(solution)/shard_map/ppermute | solution.py:292
  168.0 5.5 %shard_map.103.part = f32[256,1024]{1,0:T(8,128)S(1)} custom-call(s32[4]{0:T(128)S(1)} %pad_add_fusion.place, bf16[256,4096]{1,0:T(8,128)(2,1)} %bitcast.41, bf16[512,1024]{1,0:T(8,128)(2,1)S(1)} %copy-done.1, bf16[512,1024]{1,0:T(8,128)(2,1)S(1)} %copy-done.3, bf16[512,1024]{1,0:T(8,128)(2,1)} %collective-permute-done.3.refs_2_, ...), custom_call_target="tpu_custom_call" | custom-call | flops 2147483648 | bytes 11534336 | tf_op jit(solution)/shard_map/pallas_call | solution.py:220
  173.6 4.6 %shard_map.104 = (f32[256,512]{1,0:T(8,128)S(1)}, f32[256,512]{1,0:T(8,128)S(1)}) custom-call(s32[4]{0:T(128)S(1)} %pad_add_fusion.place, bf16[256,4096]{1,0:T(8,128)(2,1)} %bitcast.38, bf16[256,1024]{1,0:T(8,128)(2,1)} %collective-permute-done.1.mine, bf16[256,1024]{1,0:T(8,128)(2,1)} %collective-permute-done.15.by_core, ...), custom_call_target="tpu_custom_call" | custom-call | flops 1073741824 | bytes 8388608 | tf_op jit(solution)/shard_map/pallas_call | solution.py:220
  178.2 3.0 collective-permute-done.18.refs_3_
  181.2 4.6 %shard_map.105 = (bf16[256,512]{1,0:T(8,128)(2,1)S(1)}, bf16[256,512]{1,0:T(8,128)(2,1)S(1)}) custom-call(s32[4]{0:T(128)S(1)} %pad_add_fusion.place, bf16[256,4096]{1,0:T(8,128)(2,1)} %bitcast.39, bf16[256,1024]{1,0:T(8,128)(2,1)} %collective-permute-done.1.mine, bf16[256,1024]{1,0:T(8,128)(2,1)} %collective-permute-done.15.by_core, ...), custom_call_target="tpu_custom_call" | custom-call | flops 1073741824 | bytes 7864320 | tf_op jit(solution)/shard_map/pallas_call | solution.py:220
  185.8 4.4 %shard_map.106 = (bf16[256,1024]{1,0:T(8,128)(2,1)S(1)}, bf16[256,1024]{1,0:T(8,128)(2,1)S(1)}) custom-call(s32[4]{0:T(128)S(1)} %pad_add_fusion.place, bf16[256,4096]{1,0:T(8,128)(2,1)} %bitcast.42, bf16[64,2048]{1,0:T(8,128)(2,1)S(1)} %bitcast.34, f32[256,1024]{1,0:T(8,128)S(1)} %shard_map.103.part, ...), custom_call_target="tpu_custom_call" | custom-call | flops 1073741824 | bytes 6553600 | tf_op jit(solution)/shard_map/pallas_call | solution.py:220
  192.4 6.1 %collective-permute-done.20.come = bf16[256,512]{1,0:T(8,128)(2,1)S(1)} collective-permute-done((bf16[256,512]{1,0:T(8,128)(2,1)}, bf16[256,512]{1,0:T(8,128)(2,1)S(1)}, u32[]{:S(2)}, u32[]{:S(2)}) %collective-permute-start.20) | collective-permute-done | bytes 262176 | tf_op jit(solution)/shard_map/ppermute | solution.py:36
  200.5 1.9 shard_map.107
  203.9 6.0 %all-to-all-start.3 = ((f32[8,8,2048]{2,1,0:T(8,128)}), f32[8,8,2048]{2,1,0:T(8,128)}, u32[]{:S(2)}, u32[]{:S(2)}) async-start(f32[8,8,2048]{2,1,0:T(8,128)} %bitcast.36), calls=%async_computation.3 | async-start | bytes 1048576 | tf_op jit(solution)/shard_map/all_to_all | solution.py:409
  212.2 7.9 %shard_map.108 = bf16[4,2,256,512]{3,2,1,0:T(8,128)(2,1)} custom-call(s32[4]{0:T(128)S(1)} %pad_add_fusion.place, bf16[256,1024]{1,0:T(8,128)(2,1)S(1)} %copy-done.9, bf16[512,1024]{1,0:T(8,128)(2,1)S(1)} %copy-done.1, bf16[512,1024]{1,0:T(8,128)(2,1)S(1)} %copy-done.4, bf16[512,1024]{1,0:T(8,128)(2,1)} %collective-permute-done.3.refs_2_, ...), custom_call_target="tpu_custom_call" | custom-call | flops 2147483648 | bytes 13107200 | tf_op jit(solution)/shard_map/pallas_call | solution.py:220
  220.1 13.7 %all-to-all-done.3 = f32[8,8,2048]{2,1,0:T(8,128)} async-done(((f32[8,8,2048]{2,1,0:T(8,128)}), f32[8,8,2048]{2,1,0:T(8,128)}, u32[]{:S(2)}, u32[]{:S(2)}) %all-to-all-start.3) | async-done | bytes 524320 | tf_op jit(solution)/shard_map/all_to_all | solution.py:409
  234.9 20.5 %all_to_all.65 = bf16[8,8,2048]{2,1,0:T(8,128)(2,1)S(1)} all-to-all(bf16[8,8,2048]{2,1,0:T(8,128)(2,1)S(1)} %broadcast_in_dim.17), channel_id=1, replica_groups=mesh['dp'=8,'tensor'=4] {'dp'}, dimensions={0} | all-to-all | bytes 524288 | tf_op jit(solution)/shard_map/all_to_all | solution.py:335
  255.3 3.6 %all-to-all-start.5 = ((bf16[4,2,256,512]{3,2,1,0:T(8,128)(2,1)}), bf16[4,2,256,512]{3,2,1,0:T(8,128)(2,1)S(1)}, u32[]{:S(2)}, u32[]{:S(2)}) async-start(bf16[4,2,256,512]{3,2,1,0:T(8,128)(2,1)} %shard_map.108), calls=%async_computation.5 | async-start | bytes 4194304 | tf_op jit(solution)/shard_map/all_to_all | solution.py:422
  259.0 23.7 %all-to-all-done.5.parts = bf16[4,2,256,512]{3,2,1,0:T(8,128)(2,1)S(1)} async-done(((bf16[4,2,256,512]{3,2,1,0:T(8,128)(2,1)}), bf16[4,2,256,512]{3,2,1,0:T(8,128)(2,1)S(1)}, u32[]{:S(2)}, u32[]{:S(2)}) %all-to-all-start.5) | async-done | bytes 2097184 | tf_op jit(solution)/shard_map/all_to_all | solution.py:422
  284.1 18.3 %all_to_all.66 = bf16[1,64,8,512]{3,1,0,2:T(8,128)(2,1)S(1)} all-to-all(bf16[1,64,8,512]{3,1,0,2:T(8,128)(2,1)S(1)} %copy.15), channel_id=1, replica_groups=mesh['dp'=8,'tensor'=4] {'dp'}, dimensions={2} | all-to-all | bytes 1048576 | tf_op jit(solution)/shard_map/all_to_all | solution.py:426
  302.4 1.4 collective-permute-start.21
  303.7 11.2 %collective-permute-done.21 = bf16[8,64,512]{2,1,0:T(8,128)(2,1)S(1)} collective-permute-done((bf16[8,64,512]{2,1,0:T(8,128)(2,1)S(1)}, bf16[8,64,512]{2,1,0:T(8,128)(2,1)S(1)}, u32[]{:S(2)}, u32[]{:S(2)}) %collective-permute-start.21) | collective-permute-done | bytes 524320 | tf_op jit(solution)/shard_map/ppermute | solution.py:292
  317.5 4.6 %all-to-all-start.6 = ((bf16[4,16,512]{2,1,0:T(8,128)(2,1)}), bf16[4,16,512]{2,1,0:T(8,128)(2,1)S(1)}, u32[]{:S(2)}, u32[]{:S(2)}) async-start(bf16[4,16,512]{2,1,0:T(8,128)(2,1)} %bitcast.13), calls=%async_computation.6 | async-start | bytes 131072 | tf_op jit(solution)/shard_map/all_to_all | solution.py:242
  322.1 2.3 all-to-all-done.6
  324.4 4.5 %collective-permute-start.23 = (bf16[8,512]{1,0:T(8,128)(2,1)S(1)}, bf16[8,512]{1,0:T(8,128)(2,1)S(1)}, u32[]{:S(2)}, u32[]{:S(2)}) collective-permute-start(bf16[8,512]{1,0:T(8,128)(2,1)S(1)} %get-tuple-element.113), channel_id=1, source_target_pairs={{0,0},{1,8},{2,16},{3,24},{4,4},{5,12},{6,20},{7,28},{8,1},{9,9},{... | collective-permute-start | bytes 24584 | tf_op jit(solution)/shard_map/ppermute | solution.py:258
  328.9 2.2 collective-permute-start.24
  331.1 1.6 shard_map.109
  332.7 2.6 collective-permute-done.24
  335.9 6.2 %shard_map.110 = bf16[1024,512]{1,0:T(8,128)(2,1)} custom-call(s32[4]{0:T(128)S(1)} %pad_add_fusion.place, bf16[2,8,64,512]{3,2,1,0:T(8,128)(2,1)} %pad_maximum_fusion.1.own_pair, bf16[2,8,64,512]{3,2,1,0:T(8,128)(2,1)} %collective-permute-done.22.core_pair, bf16[8,256,1024]{2,1,0:T(8,128)(2,1)} %bitcast.53), custom_call_target="tpu_custom_call" | custom-call | flops 2147483648 | bytes 7340032 | tf_op jit(solution)/shard_map/pallas_call | solution.py:220
  (95 shorter events, 27.7 us)
Async XLA Ops:
  7.2 45.8 %copy-start = (bf16[512,1024]{1,0:T(8,128)(2,1)S(1)}, bf16[512,1024]{1,0:T(8,128)(2,1)}, u32[]{:S(2)}) copy-start(bf16[512,1024]{1,0:T(8,128)(2,1)} %param.13) | copy-start | bytes 3145732
  7.2 10.7 %copy-start.19 = (s32[2]{0:T(128)S(1)}, s32[2]{0:T(128)}, u32[]{:S(2)}) copy-start(s32[2]{0:T(128)} %param.11) | copy-start | bytes 28
  7.2 34.5 %collective-permute-start.2 = (bf16[512,1024]{1,0:T(8,128)(2,1)}, bf16[512,1024]{1,0:T(8,128)(2,1)S(1)}, u32[]{:S(2)}, u32[]{:S(2)}) collective-permute-start(bf16[512,1024]{1,0:T(8,128)(2,1)} %refs_0_.1), channel_id=1, source_target_pairs={{8,0},{12,4},{16,8},{20,12},{24,16},{28,20},{9,1},{13,5},{17,9},{2... | collective-permute-start | bytes 3145736 | tf_op jit(solution)/shard_map/ppermute | solution.py:31
  8.6 33.0 %collective-permute-start.3 = (bf16[512,1024]{1,0:T(8,128)(2,1)}, bf16[512,1024]{1,0:T(8,128)(2,1)}, u32[]{:S(2)}, u32[]{:S(2)}) collective-permute-start(bf16[512,1024]{1,0:T(8,128)(2,1)} %refs_0_.1), channel_id=1, source_target_pairs={{0,8},{4,12},{8,16},{12,20},{16,24},{20,28},{1,9},{5,13},{9,17},{1... | collective-permute-start | bytes 3145736 | tf_op jit(solution)/shard_map/ppermute | solution.py:31
  16.4 15.2 %collective-permute-start = (bf16[512,512]{1,0:T(8,128)(2,1)}, bf16[512,512]{1,0:T(8,128)(2,1)}, u32[]{:S(2)}, u32[]{:S(2)}) collective-permute-start(bf16[512,512]{1,0:T(8,128)(2,1)} %get-tuple-element.112), channel_id=1, source_target_pairs={{0,4},{4,0},{8,12},{12,8},{16,20},{20,16},{24,28},{28,24},{1,5},{5... | collective-permute-start | bytes 1572872 | tf_op jit(solution)/shard_map/ppermute | solution.py:36
  17.9 5.7 %copy-start.18 = (bf16[2,4,4096]{2,1,0:T(4,128)(2,1)S(1)}, bf16[2,4,4096]{2,1,0:T(4,128)(2,1)}, u32[]{:S(2)}) copy-start(bf16[2,4,4096]{2,1,0:T(4,128)(2,1)} %param.9) | copy-start | bytes 196612
  21.1 20.5 %copy-start.1 = (bf16[512,1024]{1,0:T(8,128)(2,1)S(1)}, bf16[512,1024]{1,0:T(8,128)(2,1)}, u32[]{:S(2)}) copy-start(bf16[512,1024]{1,0:T(8,128)(2,1)} %refs_0_.1) | copy-start | bytes 3145732
  23.1 18.5 %collective-permute-start.1 = (bf16[256,1024]{1,0:T(8,128)(2,1)}, bf16[256,1024]{1,0:T(8,128)(2,1)}, u32[]{:S(2)}, u32[]{:S(2)}) collective-permute-start(bf16[256,1024]{1,0:T(8,128)(2,1)} %constant_dynamic-slice_fusion.1), channel_id=1, source_target_pairs={{0,4},{4,0},{8,12},{12,8},{16,20},{20,16},{24,28},{28,24},{1,5},{5... | collective-permute-start | bytes 1572872 | tf_op jit(solution)/shard_map/ppermute | solution.py:36
  24.3 17.3 %all-to-all-start = ((bf16[8,8,512]{2,0,1:T(8,128)(2,1)}), bf16[8,8,512]{2,0,1:T(8,128)(2,1)S(1)}, u32[]{:S(2)}, u32[]{:S(2)}) async-start(bf16[8,8,512]{2,0,1:T(8,128)(2,1)} %copy.14), calls=%async_computation | async-start | bytes 131072 | tf_op jit(solution)/shard_map/all_to_all | solution.py:305
  41.6 28.8 %copy-start.2 = (bf16[512,1024]{1,0:T(8,128)(2,1)}, bf16[512,1024]{1,0:T(8,128)(2,1)S(1)}, u32[]{:S(2)}) copy-start(bf16[512,1024]{1,0:T(8,128)(2,1)S(1)} %collective-permute-done.2.refs_1_) | copy-start | bytes 3145732
  41.7 23.6 %collective-permute-start.4 = (bf16[512,1024]{1,0:T(8,128)(2,1)S(1)}, bf16[512,1024]{1,0:T(8,128)(2,1)S(1)}, u32[]{:S(2)}, u32[]{:S(2)}) collective-permute-start(bf16[512,1024]{1,0:T(8,128)(2,1)S(1)} %copy-done.1), channel_id=1, source_target_pairs={{0,4},{4,0},{8,12},{12,8},{16,20},{20,16},{24,28},{28,24},{1,5},{5... | collective-permute-start | bytes 3145736 | tf_op jit(solution)/shard_map/ppermute | solution.py:36
  43.2 60.3 %collective-permute-start.8 = (bf16[512,1024]{1,0:T(8,128)(2,1)}, bf16[512,1024]{1,0:T(8,128)(2,1)}, u32[]{:S(2)}, u32[]{:S(2)}) collective-permute-start(bf16[512,1024]{1,0:T(8,128)(2,1)} %pad_maximum_fusion.refs_0_), channel_id=1, source_target_pairs={{8,0},{12,4},{16,8},{20,12},{24,16},{28,20},{9,1},{13,5},{17,9},{2... | collective-permute-start | bytes 3145736 | tf_op jit(solution)/shard_map/ppermute | solution.py:31
  44.5 59.0 %collective-permute-start.9 = (bf16[512,1024]{1,0:T(8,128)(2,1)}, bf16[512,1024]{1,0:T(8,128)(2,1)}, u32[]{:S(2)}, u32[]{:S(2)}) collective-permute-start(bf16[512,1024]{1,0:T(8,128)(2,1)} %pad_maximum_fusion.refs_0_), channel_id=1, source_target_pairs={{0,8},{4,12},{8,16},{12,20},{16,24},{20,28},{1,9},{5,13},{9,17},{1... | collective-permute-start | bytes 3145736 | tf_op jit(solution)/shard_map/ppermute | solution.py:31
  50.1 53.4 %collective-permute-start.6 = (bf16[512,1024]{1,0:T(8,128)(2,1)S(1)}, bf16[512,1024]{1,0:T(8,128)(2,1)}, u32[]{:S(2)}, u32[]{:S(2)}) collective-permute-start(bf16[512,1024]{1,0:T(8,128)(2,1)S(1)} %collective-permute-done.2.refs_1_), channel_id=1, source_target_pairs={{8,0},{12,4},{16,8},{20,12},{9,1},{13,5},{17,9},{21,13},{10,2},{14... | collective-permute-start | bytes 3145736 | tf_op jit(solution)/shard_map/ppermute | solution.py:31
  51.4 52.2 %collective-permute-start.7 = (bf16[512,1024]{1,0:T(8,128)(2,1)}, bf16[512,1024]{1,0:T(8,128)(2,1)}, u32[]{:S(2)}, u32[]{:S(2)}) collective-permute-start(bf16[512,1024]{1,0:T(8,128)(2,1)} %collective-permute-done.3.refs_2_), channel_id=1, source_target_pairs={{8,16},{12,20},{16,24},{20,28},{9,17},{13,21},{17,25},{21,29},{10,... | collective-permute-start | bytes 3145736 | tf_op jit(solution)/shard_map/ppermute | solution.py:31
  65.2 1.0 copy-start.15
  66.2 37.4 %collective-permute-start.5 = (bf16[512,1024]{1,0:T(8,128)(2,1)S(1)}, bf16[512,1024]{1,0:T(8,128)(2,1)}, u32[]{:S(2)}, u32[]{:S(2)}) collective-permute-start(bf16[512,1024]{1,0:T(8,128)(2,1)S(1)} %collective-permute-done.2.refs_1_), channel_id=1, source_target_pairs={{0,4},{4,0},{8,12},{12,8},{16,20},{20,16},{1,5},{5,1},{9,13},{13,9... | collective-permute-start | bytes 3145736 | tf_op jit(solution)/shard_map/ppermute | solution.py:36
  70.4 32.0 %all-to-all-start.1 = ((f32[8,8,2048]{2,1,0:T(8,128)}), f32[8,8,2048]{2,1,0:T(8,128)}, u32[]{:S(2)}, u32[]{:S(2)}) async-start(f32[8,8,2048]{2,1,0:T(8,128)} %maximum_bitcast_fusion), calls=%async_computation.1 | async-start | bytes 1048576 | tf_op jit(solution)/shard_map/all_to_all | solution.py:326
  74.6 261.4 %all-gather.3.cloned.1.call-start = ((), (), s32[]{:S(2)}) async-start(), calls=%async_computation.8 | async-start | bytes 4718592 | tf_op jit(solution)/shard_map/all_gather | solution.py:399
  104.9 50.6 %collective-permute-start.12 = (bf16[512,1024]{1,0:T(8,128)(2,1)S(1)}, bf16[512,1024]{1,0:T(8,128)(2,1)}, u32[]{:S(2)}, u32[]{:S(2)}) collective-permute-start(bf16[512,1024]{1,0:T(8,128)(2,1)S(1)} %broadcast_select_fusion.2.refs_3_), channel_id=1, source_target_pairs={{8,0},{12,4},{16,24},{20,28},{9,1},{13,5},{17,25},{21,29},{10,2},{... | collective-permute-start | bytes 3145736 | tf_op jit(solution)/shard_map/ppermute | solution.py:31
  106.2 49.3 %collective-permute-start.14 = (bf16[512,1024]{1,0:T(8,128)(2,1)S(1)}, bf16[512,1024]{1,0:T(8,128)(2,1)S(1)}, u32[]{:S(2)}, u32[]{:S(2)}) collective-permute-start(bf16[512,1024]{1,0:T(8,128)(2,1)S(1)} %broadcast_select_fusion.2.refs_3_), channel_id=1, source_target_pairs={{0,4},{4,0},{8,12},{12,8},{16,20},{20,16},{24,28},{28,24},{1,5},{5... | collective-permute-start | bytes 3145736 | tf_op jit(solution)/shard_map/ppermute | solution.py:36
  107.0 49.4 %collective-permute-start.10 = (bf16[512,1024]{1,0:T(8,128)(2,1)}, bf16[512,1024]{1,0:T(8,128)(2,1)S(1)}, u32[]{:S(2)}, u32[]{:S(2)}) collective-permute-start(bf16[512,1024]{1,0:T(8,128)(2,1)} %collective-permute-done.8.refs_1_), channel_id=1, source_target_pairs={{8,0},{12,4},{16,8},{20,12},{9,1},{13,5},{17,9},{21,13},{10,2},{14... | collective-permute-start | bytes 3145736 | tf_op jit(solution)/shard_map/ppermute | solution.py:31
  108.3 48.2 %collective-permute-start.11 = (bf16[512,1024]{1,0:T(8,128)(2,1)}, bf16[512,1024]{1,0:T(8,128)(2,1)S(1)}, u32[]{:S(2)}, u32[]{:S(2)}) collective-permute-start(bf16[512,1024]{1,0:T(8,128)(2,1)} %collective-permute-done.9.refs_2_), channel_id=1, source_target_pairs={{8,16},{12,20},{16,24},{20,28},{9,17},{13,21},{17,25},{21,29},{10,... | collective-permute-start | bytes 3145736 | tf_op jit(solution)/shard_map/ppermute | solution.py:31
  109.1 47.4 %collective-permute-start.13 = (bf16[512,1024]{1,0:T(8,128)(2,1)}, bf16[512,1024]{1,0:T(8,128)(2,1)}, u32[]{:S(2)}, u32[]{:S(2)}) collective-permute-start(bf16[512,1024]{1,0:T(8,128)(2,1)} %collective-permute-done.3.refs_2_), channel_id=1, source_target_pairs={{8,12},{12,8},{16,20},{20,16},{24,28},{28,24},{9,13},{13,9},{17,21... | collective-permute-start | bytes 3145736 | tf_op jit(solution)/shard_map/ppermute | solution.py:36
  155.5 1.0 copy-start.16
  156.5 10.2 %collective-permute-start.16 = (bf16[256,1024]{1,0:T(8,128)(2,1)}, bf16[256,1024]{1,0:T(8,128)(2,1)}, u32[]{:S(2)}, u32[]{:S(2)}) collective-permute-start(bf16[256,1024]{1,0:T(8,128)(2,1)} %collective-permute-done.1.mine), channel_id=1, source_target_pairs={{0,2},{1,3},{2,0},{3,1},{4,6},{5,7},{6,4},{7,5},{8,10},{9,11},{10,... | collective-permute-start | bytes 1572872 | tf_op jit(solution)/shard_map/ppermute | solution.py:292
  158.2 23.0 %collective-permute-start.18 = (bf16[512,1024]{1,0:T(8,128)(2,1)}, bf16[512,1024]{1,0:T(8,128)(2,1)}, u32[]{:S(2)}, u32[]{:S(2)}) collective-permute-start(bf16[512,1024]{1,0:T(8,128)(2,1)} %broadcast_select_fusion.1.refs_2_), channel_id=1, source_target_pairs={{8,0},{12,4},{16,24},{20,28},{9,1},{13,5},{17,25},{21,29},{10,2},{... | collective-permute-start | bytes 3145736 | tf_op jit(solution)/shard_map/ppermute | solution.py:31
  159.4 26.4 %collective-permute-start.19 = (bf16[512,1024]{1,0:T(8,128)(2,1)}, bf16[512,1024]{1,0:T(8,128)(2,1)}, u32[]{:S(2)}, u32[]{:S(2)}) collective-permute-start(bf16[512,1024]{1,0:T(8,128)(2,1)} %collective-permute-done.12.refs_0_.refs_4_), channel_id=1, source_target_pairs={{0,4},{4,0},{24,28},{28,24},{1,5},{5,1},{25,29},{29,25},{2,6},{6,2... | collective-permute-start | bytes 3145736 | tf_op jit(solution)/shard_map/ppermute | solution.py:36
  162.5 11.1 %collective-permute-start.15 = (bf16[256,1024]{1,0:T(8,128)(2,1)}, bf16[256,1024]{1,0:T(8,128)(2,1)}, u32[]{:S(2)}, u32[]{:S(2)}) collective-permute-start(bf16[256,1024]{1,0:T(8,128)(2,1)} %collective-permute-done.1.mine), channel_id=1, source_target_pairs={{0,1},{1,0},{2,3},{3,2},{4,5},{5,4},{6,7},{7,6},{8,9},{9,8},{10,11... | collective-permute-start | bytes 1572872 | tf_op jit(solution)/shard_map/ppermute | solution.py:292
  166.7 6.8 %collective-permute-start.17 = (bf16[256,1024]{1,0:T(8,128)(2,1)}, bf16[256,1024]{1,0:T(8,128)(2,1)}, u32[]{:S(2)}, u32[]{:S(2)}) collective-permute-start(bf16[256,1024]{1,0:T(8,128)(2,1)} %collective-permute-done.16.by_y), channel_id=1, source_target_pairs={{0,1},{1,0},{2,3},{3,2},{4,5},{5,4},{6,7},{7,6},{8,9},{9,8},{10,11... | collective-permute-start | bytes 1572872 | tf_op jit(solution)/shard_map/ppermute | solution.py:292
  166.8 1.2 copy-start.3
  168.0 5.5 %copy-start.5 = (bf16[512,1024]{1,0:T(8,128)(2,1)S(1)}, bf16[512,1024]{1,0:T(8,128)(2,1)}, u32[]{:S(2)}) copy-start(bf16[512,1024]{1,0:T(8,128)(2,1)} %pad_maximum_fusion.refs_0_) | copy-start | bytes 3145732
  185.8 4.4 %copy-start.12 = (bf16[256,512]{1,0:T(8,128)(2,1)}, bf16[256,512]{1,0:T(8,128)(2,1)S(1)}, u32[]{:S(2)}) copy-start(bf16[256,512]{1,0:T(8,128)(2,1)S(1)} %get-tuple-element.98.keep) | copy-start | bytes 786436
  185.8 4.4 %copy-start.14 = (bf16[256,512]{1,0:T(8,128)(2,1)}, bf16[256,512]{1,0:T(8,128)(2,1)S(1)}, u32[]{:S(2)}) copy-start(bf16[256,512]{1,0:T(8,128)(2,1)S(1)} %get-tuple-element.99) | copy-start | bytes 786436
  190.2 0.8 copy-start.6
  191.8 6.6 %collective-permute-start.20 = (bf16[256,512]{1,0:T(8,128)(2,1)}, bf16[256,512]{1,0:T(8,128)(2,1)S(1)}, u32[]{:S(2)}, u32[]{:S(2)}) collective-permute-start(bf16[256,512]{1,0:T(8,128)(2,1)} %copy-done.14), channel_id=1, source_target_pairs={{0,4},{4,0},{8,12},{12,8},{16,20},{20,16},{24,28},{28,24},{1,5},{5... | collective-permute-start | bytes 786440 | tf_op jit(solution)/shard_map/ppermute | solution.py:36
  198.5 1.0 copy-start.7
  199.5 0.9 copy-start.13
  203.9 29.8 %all-to-all-start.3 = ((f32[8,8,2048]{2,1,0:T(8,128)}), f32[8,8,2048]{2,1,0:T(8,128)}, u32[]{:S(2)}, u32[]{:S(2)}) async-start(f32[8,8,2048]{2,1,0:T(8,128)} %bitcast.36), calls=%async_computation.3 | async-start | bytes 1048576 | tf_op jit(solution)/shard_map/all_to_all | solution.py:409
  210.0 1.2 copy-start.4
  211.2 1.0 copy-start.9
  255.3 27.3 %all-to-all-start.5 = ((bf16[4,2,256,512]{3,2,1,0:T(8,128)(2,1)}), bf16[4,2,256,512]{3,2,1,0:T(8,128)(2,1)S(1)}, u32[]{:S(2)}, u32[]{:S(2)}) async-start(bf16[4,2,256,512]{3,2,1,0:T(8,128)(2,1)} %shard_map.108), calls=%async_computation.5 | async-start | bytes 4194304 | tf_op jit(solution)/shard_map/all_to_all | solution.py:422
  284.1 32.3 %copy-start.17 = (bf16[512,1024]{1,0:T(8,128)(2,1)S(1)}, bf16[512,1024]{1,0:T(8,128)(2,1)}, u32[]{:S(2)}) copy-start(bf16[512,1024]{1,0:T(8,128)(2,1)} %param.14) | copy-start | bytes 3145732
  302.4 12.5 %collective-permute-start.21 = (bf16[8,64,512]{2,1,0:T(8,128)(2,1)S(1)}, bf16[8,64,512]{2,1,0:T(8,128)(2,1)S(1)}, u32[]{:S(2)}, u32[]{:S(2)}) collective-permute-start(bf16[8,64,512]{2,1,0:T(8,128)(2,1)S(1)} %bitcast.45), channel_id=1, source_target_pairs={{0,2},{1,3},{2,0},{3,1},{4,6},{5,7},{6,4},{7,5},{8,10},{9,11},{10,... | collective-permute-start | bytes 1572872 | tf_op jit(solution)/shard_map/ppermute | solution.py:292
  316.0 8.4 %collective-permute-start.22 = (bf16[2,8,64,512]{3,2,1,0:T(8,128)(2,1)}, bf16[2,8,64,512]{3,2,1,0:T(8,128)(2,1)}, u32[]{:S(2)}, u32[]{:S(2)}) collective-permute-start(bf16[2,8,64,512]{3,2,1,0:T(8,128)(2,1)} %pad_maximum_fusion.1.own_pair), channel_id=1, source_target_pairs={{0,1},{1,0},{2,3},{3,2},{4,5},{5,4},{6,7},{7,6},{8,9},{9,8},{10,11... | collective-permute-start | bytes 3145736 | tf_op jit(solution)/shard_map/ppermute | solution.py:292
  317.5 6.9 %all-to-all-start.6 = ((bf16[4,16,512]{2,1,0:T(8,128)(2,1)}), bf16[4,16,512]{2,1,0:T(8,128)(2,1)S(1)}, u32[]{:S(2)}, u32[]{:S(2)}) async-start(bf16[4,16,512]{2,1,0:T(8,128)(2,1)} %bitcast.13), calls=%async_computation.6 | async-start | bytes 131072 | tf_op jit(solution)/shard_map/all_to_all | solution.py:242
  324.4 8.3 %collective-permute-start.23 = (bf16[8,512]{1,0:T(8,128)(2,1)S(1)}, bf16[8,512]{1,0:T(8,128)(2,1)S(1)}, u32[]{:S(2)}, u32[]{:S(2)}) collective-permute-start(bf16[8,512]{1,0:T(8,128)(2,1)S(1)} %get-tuple-element.113), channel_id=1, source_target_pairs={{0,0},{1,8},{2,16},{3,24},{4,4},{5,12},{6,20},{7,28},{8,1},{9,9},{... | collective-permute-start | bytes 24584 | tf_op jit(solution)/shard_map/ppermute | solution.py:258
  328.9 6.4 %collective-permute-start.24 = (bf16[8,512]{1,0:T(8,128)(2,1)S(1)}, bf16[8,512]{1,0:T(8,128)(2,1)S(1)}, u32[]{:S(2)}, u32[]{:S(2)}) collective-permute-start(bf16[8,512]{1,0:T(8,128)(2,1)S(1)} %get-tuple-element.114), channel_id=1, source_target_pairs={{0,4},{1,12},{2,20},{3,28},{4,0},{5,8},{6,16},{7,24},{8,5},{9,13},... | collective-permute-start | bytes 24584 | tf_op jit(solution)/shard_map/ppermute | solution.py:258
  (3 other events, 2.4 us)
Sparse Core Ops, SparseCore 0:
  191.9 88.5 all-gather.2

commit v12 on v8

--- a/solution.py
+++ b/solution.py
@@ -12,7 +12,7 @@
 BF16 = jnp.bfloat16
 BACK = (((1,), (1,)), ((), ()))
 FIRST = (((0,), (0,)), ((), ()))
-VMEM_LIMIT = 48 * 1024 * 1024
+VMEM_LIMIT = 60 * 1024 * 1024
 
 
 def matmul(a, b, dims=None):
@@ -317,14 +317,8 @@
     quarter_cols = width // 4
     live_part = lax.dynamic_slice_in_dim(live_flat, quarter * quarter_cols, quarter_cols, 1)
     live_here = line.swap(live_part)
-    quarter_rows = rows // 4
-    live_rows = lax.dynamic_slice_in_dim(live_flat, quarter * quarter_rows, quarter_rows, 0)
-    live_mine = lax.all_to_all(
-        live_rows.reshape(quarter_rows, n_dp, own_width), "dp", split_axis=1, concat_axis=0
-    )
-    live_mine = live_mine.reshape(n_dp, quarter_rows, own_width)
-    image_cols, wo_pair, live_here, live_mine, query_weight, *wq_moved = gate(
-        (image_cols, wo_pair, live_here, live_mine, query_weight, *wq_moved)
+    image_cols, wo_pair, live_here, query_weight, *wq_moved = gate(
+        (image_cols, wo_pair, live_here, query_weight, *wq_moved)
     )
 
     n_moved = len(wq_moved)
@@ -352,19 +346,23 @@
     wo_two = line.second(wo_moved)
     wq_others += [line.swap(block, at) for block, at in zip(wq_moved[1:], planes[1:])]
     wq_others += [line.swap(block) for block in wq_last[:1]]
-    kv_own, *wq_edge = gate((kv_own, *wq_last[1:]))
     kv_all = everywhere(kv_own).reshape(images, 2 * local_cols)
-    edge_other = [line.swap(block, (0, 3)) for block in wq_edge]
     kv_all, live_here, wo_pair, live_flat, *staged = gate(
-        (kv_all, live_here, wo_pair, live_flat, *wo_two, *wq_edge, *wq_others)
+        (kv_all, live_here, wo_pair, live_flat, *wo_two, *wq_last, *wq_others)
     )
     wo_two, staged = staged[: len(wo_two)], staged[len(wo_two) :]
-    wq_last[1:], wq_others = staged[: len(wq_edge)], staged[len(wq_edge) :]
+    wq_last, wq_others = staged[: len(wq_last)], staged[len(wq_last) :]
 
     wo_last = line.third(wo_two)
+    quarter_rows = rows // 4
+    live_rows = lax.dynamic_slice_in_dim(live_flat, quarter * quarter_rows, quarter_rows, 0)
+    live_mine = lax.all_to_all(
+        live_rows.reshape(quarter_rows, n_dp, own_width), "dp", split_axis=1, concat_axis=0
+    )
+    live_mine = live_mine.reshape(n_dp, quarter_rows, own_width)
     by_y = tensor_swap(live_here, 2)
     live_pieces = [live_here, tensor_swap(live_here, 1), by_y, tensor_swap(by_y, 1)]
-    wq_others += edge_other
+    wq_others += [line.swap(block, (0, 3)) for block in wq_last[1:]]
     arrivals = [query_weight, *wq_moved, *wq_last]
     early = range(4 if relayed else len(arrivals))
     late = range(len(early), len(arrivals))
@@ -435,7 +433,7 @@
         (),
         2 * rows * width * local_cols,
     )
-    kv_grad, term, live_mine, live_y = gate((kv_grad.astype(BF16), term, live_mine, live_y))
+    kv_grad, term, live_y = gate((kv_grad.astype(BF16), term, live_y))
     kv_grad_all = everywhere(kv_grad).reshape(images, 2 * local_cols)
     live_pair = jnp.stack([live_mine, live_y])
 
@@ -443,25 +441,23 @@
     attended, att_swapped, *att_next = gate((attended, att_swapped, *att_next))
     att_far = [line.shift(attended, m) for m in range(2, line.n_z - 1)]
     att_other_next = [line.swap(block) for block in att_next]
-    kv_grad_all, live_pair, *staged = gate((kv_grad_all, live_pair, *text_parts, *att_far))
+    kv_grad_all, term, live_pair, *staged = gate(
+        (kv_grad_all, term, live_pair, *att_other_next, *text_parts, *att_far)
+    )
+    att_other_next, staged = staged[:2], staged[2:]
     text_parts, att_far = staged[: n_tensor - 2], staged[n_tensor - 2 :]
 
+    att_other_far = [line.swap(block) for block in att_far]
     live_core = tensor_swap(live_pair, 1)
     text_parts.append(tensor_swap(term[1], 1))
     image_term = matmul(kv_grad_all[:, :local_cols], key_weight, BACK)
     image_term = image_term + matmul(kv_grad_all[:, local_cols:], value_weight, BACK)
-    image_grad, live_core, *staged = to_owner(
-        line, image_term.astype(BF16), live_core, *text_parts, *att_other_next, *att_far
-    )
-    text_parts, staged = staged[: n_tensor - 1], staged[n_tensor - 1 :]
-    att_other_next, att_far = staged[:2], staged[2:]
-    att_other_far = [line.swap(block) for block in att_far]
+    image_grad, live_core, text_parts[-1], *att_other_far = to_owner(
+        line, image_term.astype(BF16), live_core, text_parts[-1], *att_other_far
+    )
     image_grad = image_grad.reshape(samples, image_own, width // n_tensor)
     text_grad = call(
-        sum_kernel,
-        place,
-        (term, *text_parts),
-        [shape((rows, width // n_tensor), BF16)],
+        sum_kernel, place, (term, *text_parts), [shape((rows, width // n_tensor), BF16)]
     )
     text_grad = text_grad.reshape(samples, tok_rows, width // n_tensor)
 

time: 342 us -> 310 us (0.906)
  waiting for transfers between devices: 172 us -> 129 us
  starting transfers between devices: 84.7 us -> 101 us
  Pallas kernels: 37.5 us -> 45.9 us
  local copies, waits for them, and re-layouts: 19.1 us -> 13.4 us
  blocking collectives: 5.4 us -> 0 us
    ppermute x13, waiting for transfers between devices: 68.1 us -> 22.9 us  [move(): return lax.ppermute(block, 'dp', pairs)]
    all_to_all x2, waiting for transfers between devices: 3.96 us -> 32.8 us  [everywhere(): return lax.all_to_all(copies, 'dp', split_axis=0, concat_axis=0)]
    ppermute x12, waiting for transfers between devices: 55.4 us -> 34.2 us  [swap(): return lax.ppermute(block, 'dp', pairs)]
    pallas_call x8, Pallas kernels: 37.5 us -> 45.9 us  [call(): pl.pallas_call(kernel, out_shape=outs[0] if single else outs, in_specs=[p...]
    unnamed x31 -> x27, local copies, waits for them, and re-layouts: 9.34 us -> 2.68 us
    all_to_all x2, starting transfers between devices: 11.5 us -> 17.4 us  [everywhere(): return lax.all_to_all(copies, 'dp', split_axis=0, concat_axis=0)]
    all_to_all x1 -> x0, blocking collectives: 5.4 us -> none  [to_owner(): lax.all_to_all(terms.reshape(n_tensor, images // n_tensor, cols), 'tensor...]
    all_to_all x1, waiting for transfers between devices: 12.5 us -> 7.81 us  [shards(): lax.all_to_all(image_flat, 'dp', split_axis=1, concat_axis=0, tiled=True)]
  transfers between devices with their start and end apart: 41 -> 42, of which waited for: 20 -> 16; matrix products, arithmetic and copies ran while one was open for 8% -> 8% of each run, Pallas kernels for 9% -> 14%
where the time goes in v12:
time: 310 us; the launch traced here: 308 us
  waiting for transfers between devices  129 us (42%)
  starting transfers between devices  101 us (33%)
  Pallas kernels  45.9 us (15%)
  other arithmetic  14.3 us (5%)
  local copies, waits for them, and re-layouts  13.4 us (4%)
  matrix products  3.34 us (1%)
    pallas_call x8, Pallas kernels, call(): pl.pallas_call(kernel, out_shape=outs[0] if single else outs, in_specs=[p...  45.9 us
    ppermute x12, waiting for transfers between devices, swap(): return lax.ppermute(block, 'dp', pairs)  34.2 us
    all_to_all x2, waiting for transfers between devices, everywhere(): return lax.all_to_all(copies, 'dp', split_axis=0, concat_axis=0)  32.8 us
    all_to_all x1, waiting for transfers between devices, shards(): lax.all_to_all(part_kv, 'dp', split_axis=0, concat_axis=0)  29.3 us
    ppermute x13, starting transfers between devices, move(): return lax.ppermute(block, 'dp', pairs)  27.7 us
    ppermute x13, waiting for transfers between devices, move(): return lax.ppermute(block, 'dp', pairs)  22.9 us
    ppermute x12, starting transfers between devices, swap(): return lax.ppermute(block, 'dp', pairs)  19.4 us
    all_to_all x2, starting transfers between devices, everywhere(): return lax.all_to_all(copies, 'dp', split_axis=0, concat_axis=0)  17.4 us
  transfers between devices with their start and end apart: 42, of which 16 were waited for; matrix products, arithmetic and copies ran while one was open for 8% of the time, Pallas kernels for 14%

profile of v12, /device:TPU:4, one launch (start us, length us, event | category | flops | bytes accessed | tf_op | source)
XLA Modules:
  0.0 308.3 jit_solution(6250946627427550971)
XLA Ops:
  2.1 5.5 %collective-permute-start.3 = (bf16[512,1024]{1,0:T(8,128)(2,1)}, bf16[512,1024]{1,0:T(8,128)(2,1)}, u32[]{:S(2)}, u32[]{:S(2)}) collective-permute-start(bf16[512,1024]{1,0:T(8,128)(2,1)} %refs_0_.1), channel_id=1, source_target_pairs={{0,8},{4,12},{8,16},{12,20},{16,24},{20,28},{1,9},{5,13},{9,17},{1... | collective-permute-start | bytes 3145736 | tf_op jit(solution)/shard_map/ppermute | solution.py:31
  7.6 2.3 constant_dynamic-slice_fusion.3
  11.5 1.8 broadcast_select_fusion
  15.5 4.8 %all-to-all-start = ((bf16[8,8,512]{2,0,1:T(8,128)(2,1)}), bf16[8,8,512]{2,0,1:T(8,128)(2,1)S(1)}, u32[]{:S(2)}, u32[]{:S(2)}) async-start(bf16[8,8,512]{2,0,1:T(8,128)(2,1)} %copy.14), calls=%async_computation | async-start | bytes 131072 | tf_op jit(solution)/shard_map/all_to_all | solution.py:313
  20.3 4.8 %collective-permute-done = bf16[512,512]{1,0:T(8,128)(2,1)} collective-permute-done((bf16[512,512]{1,0:T(8,128)(2,1)}, bf16[512,512]{1,0:T(8,128)(2,1)}, u32[]{:S(2)}, u32[]{:S(2)}) %collective-permute-start) | collective-permute-done | bytes 524320 | tf_op jit(solution)/shard_map/ppermute | solution.py:36
  25.1 2.3 pad_maximum_fusion.refs_0_
  27.3 7.8 %all-to-all-done = bf16[8,8,512]{2,0,1:T(8,128)(2,1)S(1)} async-done(((bf16[8,8,512]{2,0,1:T(8,128)(2,1)}), bf16[8,8,512]{2,0,1:T(8,128)(2,1)S(1)}, u32[]{:S(2)}, u32[]{:S(2)}) %all-to-all-start) | async-done | bytes 65568 | tf_op jit(solution)/shard_map/all_to_all | solution.py:313
  38.0 5.6 %collective-permute-start.9 = (bf16[512,1024]{1,0:T(8,128)(2,1)}, bf16[512,1024]{1,0:T(8,128)(2,1)}, u32[]{:S(2)}, u32[]{:S(2)}) collective-permute-start(bf16[512,1024]{1,0:T(8,128)(2,1)} %pad_maximum_fusion.refs_0_), channel_id=1, source_target_pairs={{0,8},{4,12},{8,16},{12,20},{16,24},{20,28},{1,9},{5,13},{9,17},{1... | collective-permute-start | bytes 3145736 | tf_op jit(solution)/shard_map/ppermute | solution.py:31
  44.9 1.7 collective-permute-start.7
  48.5 10.6 %collective-permute-done.4.refs_4_.refs_5_ = bf16[512,1024]{1,0:T(8,128)(2,1)} collective-permute-done((bf16[512,1024]{1,0:T(8,128)(2,1)}, bf16[512,1024]{1,0:T(8,128)(2,1)}, u32[]{:S(2)}, u32[]{:S(2)}) %collective-permute-start.4) | collective-permute-done | bytes 1048608 | tf_op jit(solution)/shard_map/ppermute | solution.py:36
  59.0 3.4 %collective-permute-start.5 = (bf16[512,1024]{1,0:T(8,128)(2,1)}, bf16[512,1024]{1,0:T(8,128)(2,1)}, u32[]{:S(2)}, u32[]{:S(2)}) collective-permute-start(bf16[512,1024]{1,0:T(8,128)(2,1)} %collective-permute-done.2.refs_1_), channel_id=1, source_target_pairs={{0,4},{4,0},{8,12},{12,8},{16,20},{20,16},{1,5},{5,1},{9,13},{13,9... | collective-permute-start | bytes 3145736 | tf_op jit(solution)/shard_map/ppermute | solution.py:36
  63.3 4.1 %all-to-all-start.1 = ((f32[8,8,2048]{2,1,0:T(8,128)}), f32[8,8,2048]{2,1,0:T(8,128)}, u32[]{:S(2)}, u32[]{:S(2)}) async-start(f32[8,8,2048]{2,1,0:T(8,128)} %maximum_bitcast_fusion), calls=%async_computation.1 | async-start | bytes 1048576 | tf_op jit(solution)/shard_map/all_to_all | solution.py:334
  67.4 29.3 %all-to-all-done.1 = f32[8,8,2048]{2,1,0:T(8,128)} async-done(((f32[8,8,2048]{2,1,0:T(8,128)}), f32[8,8,2048]{2,1,0:T(8,128)}, u32[]{:S(2)}, u32[]{:S(2)}) %all-to-all-start.1) | async-done | bytes 524320 | tf_op jit(solution)/shard_map/all_to_all | solution.py:334
  97.9 2.3 broadcast_select_fusion.2.refs_3_
  103.6 1.7 collective-permute-start.11
  105.3 1.6 collective-permute-start.13
  107.6 12.5 %all-to-all-start.2 = ((bf16[8,8,2048]{2,1,0:T(8,128)(2,1)}), bf16[8,8,2048]{2,1,0:T(8,128)(2,1)S(1)}, u32[]{:S(2)}, u32[]{:S(2)}) async-start(bf16[8,8,2048]{2,1,0:T(8,128)(2,1)} %broadcast_in_dim.16), calls=%async_computation.2 | async-start | bytes 524288 | tf_op jit(solution)/shard_map/all_to_all | solution.py:343
  120.1 31.4 %all-to-all-done.2 = bf16[8,8,2048]{2,1,0:T(8,128)(2,1)S(1)} async-done(((bf16[8,8,2048]{2,1,0:T(8,128)(2,1)}), bf16[8,8,2048]{2,1,0:T(8,128)(2,1)S(1)}, u32[]{:S(2)}, u32[]{:S(2)}) %all-to-all-start.2) | async-done | bytes 262176 | tf_op jit(solution)/shard_map/all_to_all | solution.py:343
  151.6 2.4 broadcast_select_fusion.1.refs_2_
  157.0 8.0 %all-to-all-start.3 = ((bf16[1,64,8,512]{3,1,0,2:T(8,128)(2,1)}), bf16[1,64,8,512]{3,1,0,2:T(8,128)(2,1)S(1)}, u32[]{:S(2)}, u32[]{:S(2)}) async-start(bf16[1,64,8,512]{3,1,0,2:T(8,128)(2,1)} %copy.15), calls=%async_computation.3 | async-start | bytes 1048576 | tf_op jit(solution)/shard_map/all_to_all | solution.py:359
  165.0 3.9 %collective-permute-start.19 = (bf16[512,1024]{1,0:T(8,128)(2,1)}, bf16[512,1024]{1,0:T(8,128)(2,1)S(1)}, u32[]{:S(2)}, u32[]{:S(2)}) collective-permute-start(bf16[512,1024]{1,0:T(8,128)(2,1)} %collective-permute-done.12.refs_0_.refs_4_), channel_id=1, source_target_pairs={{0,4},{4,0},{24,28},{28,24},{1,5},{5,1},{25,29},{29,25},{2,6},{6,2... | collective-permute-start | bytes 3145736 | tf_op jit(solution)/shard_map/ppermute | solution.py:36
  170.1 7.3 %shard_map.103.part = f32[256,1024]{1,0:T(8,128)} custom-call(s32[4]{0:T(128)} %pad_add_fusion.place, bf16[256,4096]{1,0:T(8,128)(2,1)} %bitcast.42, bf16[512,1024]{1,0:T(8,128)(2,1)} %refs_0_.1, bf16[512,1024]{1,0:T(8,128)(2,1)} %collective-permute-done.2.refs_1_, bf16[512,1024]{1,0:T(8,128)(2,1)} %collective-permute-done.3.refs_2_, ...), custom_call_target="tpu_custom_call" | custom-call | flops 2147483648 | bytes 11534336 | tf_op jit(solution)/shard_map/pallas_call | solution.py:228
  178.2 5.8 %shard_map.104 = (f32[256,512]{1,0:T(8,128)}, f32[256,512]{1,0:T(8,128)}) custom-call(s32[4]{0:T(128)} %pad_add_fusion.place, bf16[256,4096]{1,0:T(8,128)(2,1)} %bitcast.40, bf16[256,1024]{1,0:T(8,128)(2,1)} %collective-permute-done.1.mine, bf16[256,1024]{1,0:T(8,128)(2,1)} %copy-done.5, bf16[256,1024]{1,0:T(8,128)(2,1)} %collective-permute-done.16.by_y, ...), custom_call_target="tpu_custom_call" | custom-call | flops 1073741824 | bytes 8388608 | tf_op jit(solution)/shard_map/pallas_call | solution.py:228
  184.9 5.7 %shard_map.105 = (bf16[256,512]{1,0:T(8,128)(2,1)}, bf16[256,512]{1,0:T(8,128)(2,1)}) custom-call(s32[4]{0:T(128)} %pad_add_fusion.place, bf16[256,4096]{1,0:T(8,128)(2,1)} %bitcast.41, bf16[256,1024]{1,0:T(8,128)(2,1)} %collective-permute-done.1.mine, bf16[256,1024]{1,0:T(8,128)(2,1)} %copy-done.5, bf16[256,1024]{1,0:T(8,128)(2,1)} %collective-permute-done.16.by_y, ...), custom_call_target="tpu_custom_call" | custom-call | flops 1073741824 | bytes 7864320 | tf_op jit(solution)/shard_map/pallas_call | solution.py:228
  192.8 5.4 %shard_map.106 = (bf16[256,1024]{1,0:T(8,128)(2,1)}, bf16[256,1024]{1,0:T(8,128)(2,1)}) custom-call(s32[4]{0:T(128)} %pad_add_fusion.place, bf16[256,4096]{1,0:T(8,128)(2,1)} %bitcast.43, bf16[64,2048]{1,0:T(8,128)(2,1)} %bitcast.44, f32[256,1024]{1,0:T(8,128)} %shard_map.103.part, bf16[512,1024]{1,0:T(8,128)(2,1)} %collective-permute-done.12.refs_0_.refs_4_, ...), custom_call_target="tpu_custom_call" | custom-call | flops 1073741824 | bytes 6553600 | tf_op jit(solution)/shard_map/pallas_call | solution.py:228
  199.0 3.6 %shard_map.107 = (bf16[256,1024]{1,0:T(8,128)(2,1)}, f32[64,2048]{1,0:T(8,128)}) custom-call(s32[4]{0:T(128)} %pad_add_fusion.place, bf16[256,1024]{1,0:T(8,128)(2,1)} %get-tuple-element.105.query, bf16[64,2048]{1,0:T(8,128)(2,1)} %bitcast.45, bf16[256,512]{1,0:T(8,128)(2,1)} %get-tuple-element.106.keep, bf16[256,512]{1,0:T(8,128)(2,1)} %copy-done.9), custom_call_target="tpu_custom_call" | custom-call | flops 167772160 | bytes 2359296 | tf_op jit(solution)/shard_map/pallas_call | solution.py:228
  202.6 5.0 %all-to-all-start.4 = ((f32[8,8,2048]{2,1,0:T(8,128)}), f32[8,8,2048]{2,1,0:T(8,128)S(1)}, u32[]{:S(2)}, u32[]{:S(2)}) async-start(f32[8,8,2048]{2,1,0:T(8,128)} %bitcast.55), calls=%async_computation.4 | async-start | bytes 1048576 | tf_op jit(solution)/shard_map/all_to_all | solution.py:426
  207.5 2.0 collective-permute-start.22
  209.6 3.3 %collective-permute-start.23 = (bf16[256,1024]{1,0:T(8,128)(2,1)}, bf16[256,1024]{1,0:T(8,128)(2,1)}, u32[]{:S(2)}, u32[]{:S(2)}) collective-permute-start(bf16[256,1024]{1,0:T(8,128)(2,1)} %get-tuple-element.117.refs_2_), channel_id=1, source_target_pairs={{8,0},{12,4},{16,8},{20,12},{24,16},{28,20},{0,24},{4,28},{9,1},{1... | collective-permute-start | bytes 1572872 | tf_op jit(solution)/shard_map/ppermute | solution.py:31
  214.2 8.9 %shard_map.108.term = bf16[4,2,256,512]{3,2,1,0:T(8,128)(2,1)} custom-call(s32[4]{0:T(128)} %pad_add_fusion.place, bf16[256,1024]{1,0:T(8,128)(2,1)} %get-tuple-element.109.query_grad, bf16[512,1024]{1,0:T(8,128)(2,1)} %refs_0_.1, bf16[512,1024]{1,0:T(8,128)(2,1)} %collective-permute-done.2.refs_1_, bf16[512,1024]{1,0:T(8,128)(2,1)} %collective-permute-done.3.refs_2_, ...), custom_call_target="tpu_custom_call" | custom-call | flops 2147483648 | bytes 13107200 | tf_op jit(solution)/shard_map/pallas_call | solution.py:228
  223.1 3.1 %collective-permute-done.22.refs_6_ = bf16[256,1024]{1,0:T(8,128)(2,1)S(1)} collective-permute-done((bf16[256,1024]{1,0:T(8,128)(2,1)}, bf16[256,1024]{1,0:T(8,128)(2,1)S(1)}, u32[]{:S(2)}, u32[]{:S(2)}) %collective-permute-start.22) | collective-permute-done | bytes 524320 | tf_op jit(solution)/shard_map/ppermute | solution.py:36
  226.3 3.2 %collective-permute-done.23.refs_3_ = bf16[256,1024]{1,0:T(8,128)(2,1)} collective-permute-done((bf16[256,1024]{1,0:T(8,128)(2,1)}, bf16[256,1024]{1,0:T(8,128)(2,1)}, u32[]{:S(2)}, u32[]{:S(2)}) %collective-permute-start.23) | collective-permute-done | bytes 524320 | tf_op jit(solution)/shard_map/ppermute | solution.py:31
  229.4 12.9 %collective-permute-done.24.refs_5_ = bf16[256,1024]{1,0:T(8,128)(2,1)} collective-permute-done((bf16[256,1024]{1,0:T(8,128)(2,1)}, bf16[256,1024]{1,0:T(8,128)(2,1)}, u32[]{:S(2)}, u32[]{:S(2)}) %collective-permute-start.24) | collective-permute-done | bytes 524320 | tf_op jit(solution)/shard_map/ppermute | solution.py:31
  244.4 2.0 collective-permute-start.29
  246.5 2.4 slice_bitcast_fusion.1
  250.6 4.8 %all-to-all-start.5 = ((bf16[8,8,2048]{2,1,0:T(8,128)(2,1)}), bf16[8,8,2048]{2,1,0:T(8,128)(2,1)S(1)}, u32[]{:S(2)}, u32[]{:S(2)}) async-start(bf16[8,8,2048]{2,1,0:T(8,128)(2,1)} %broadcast_in_dim.17), calls=%async_computation.5 | async-start | bytes 524288 | tf_op jit(solution)/shard_map/all_to_all | solution.py:343
  255.4 2.2 pad_maximum_fusion.1.refs_0_
  257.7 9.9 %collective-permute-done.26.refs_9_ = bf16[256,1024]{1,0:T(8,128)(2,1)} collective-permute-done((bf16[256,1024]{1,0:T(8,128)(2,1)}, bf16[256,1024]{1,0:T(8,128)(2,1)}, u32[]{:S(2)}, u32[]{:S(2)}) %collective-permute-start.26) | collective-permute-done | bytes 524320 | tf_op jit(solution)/shard_map/ppermute | solution.py:36
  267.6 5.9 %collective-permute-done.29.refs_4_ = bf16[256,1024]{1,0:T(8,128)(2,1)} collective-permute-done((bf16[256,1024]{1,0:T(8,128)(2,1)}, bf16[256,1024]{1,0:T(8,128)(2,1)}, u32[]{:S(2)}, u32[]{:S(2)}) %collective-permute-start.29) | collective-permute-done | bytes 524320 | tf_op jit(solution)/shard_map/ppermute | solution.py:31
  274.9 2.0 slice_bitcast_fusion
  277.3 1.6 collective-permute-start.32
  280.5 3.9 %all-to-all-start.6 = ((bf16[4,16,512]{2,1,0:T(8,128)(2,1)}), bf16[4,16,512]{2,1,0:T(8,128)(2,1)S(1)}, u32[]{:S(2)}, u32[]{:S(2)}) async-start(bf16[4,16,512]{2,1,0:T(8,128)(2,1)} %bitcast.19), calls=%async_computation.6 | async-start | bytes 131072 | tf_op jit(solution)/shard_map/all_to_all | solution.py:250
  284.4 2.3 all-to-all-done.6
  286.7 4.9 %collective-permute-done.32.refs_8_ = bf16[256,1024]{1,0:T(8,128)(2,1)} collective-permute-done((bf16[256,1024]{1,0:T(8,128)(2,1)}, bf16[256,1024]{1,0:T(8,128)(2,1)}, u32[]{:S(2)}, u32[]{:S(2)}) %collective-permute-start.32) | collective-permute-done | bytes 524320 | tf_op jit(solution)/shard_map/ppermute | solution.py:36
  291.6 3.2 %collective-permute-start.33 = (bf16[8,512]{1,0:T(8,128)(2,1)S(1)}, bf16[8,512]{1,0:T(8,128)(2,1)S(1)}, u32[]{:S(2)}, u32[]{:S(2)}) collective-permute-start(bf16[8,512]{1,0:T(8,128)(2,1)S(1)} %get-tuple-element.135), channel_id=1, source_target_pairs={{0,0},{1,8},{2,16},{3,24},{4,4},{5,12},{6,20},{7,28},{8,1},{9,9},{... | collective-permute-start | bytes 24584 | tf_op jit(solution)/shard_map/ppermute | solution.py:266
  294.8 3.6 %collective-permute-start.34 = (bf16[8,512]{1,0:T(8,128)(2,1)S(1)}, bf16[8,512]{1,0:T(8,128)(2,1)S(1)}, u32[]{:S(2)}, u32[]{:S(2)}) collective-permute-start(bf16[8,512]{1,0:T(8,128)(2,1)S(1)} %get-tuple-element.136), channel_id=1, source_target_pairs={{0,4},{1,12},{2,20},{3,28},{4,0},{5,8},{6,16},{7,24},{8,5},{9,13},... | collective-permute-start | bytes 24584 | tf_op jit(solution)/shard_map/ppermute | solution.py:266
  298.5 6.1 %shard_map.110 = bf16[1024,512]{1,0:T(8,128)(2,1)} custom-call(s32[4]{0:T(128)} %pad_add_fusion.place, bf16[2,8,64,512]{3,2,1,0:T(8,128)(2,1)} %pad_maximum_fusion.1.refs_0_, bf16[2,8,64,512]{3,2,1,0:T(8,128)(2,1)} %collective-permute-done.30.refs_1_, bf16[256,1024]{1,0:T(8,128)(2,1)} %get-tuple-element.117.refs_2_, ...), custom_call_target="tpu_custom_call" | custom-call | flops 2147483648 | bytes 7340032 | tf_op jit(solution)/shard_map/pallas_call | solution.py:228
  304.6 3.0 shard_map.109
  (101 shorter events, 35.3 us)
Async XLA Ops:
  0.6 47.5 %copy-start = (bf16[512,1024]{1,0:T(8,128)(2,1)S(1)}, bf16[512,1024]{1,0:T(8,128)(2,1)}, u32[]{:S(2)}) copy-start(bf16[512,1024]{1,0:T(8,128)(2,1)} %param.14) | copy-start | bytes 3145732
  0.7 34.5 %collective-permute-start.2 = (bf16[512,1024]{1,0:T(8,128)(2,1)}, bf16[512,1024]{1,0:T(8,128)(2,1)}, u32[]{:S(2)}, u32[]{:S(2)}) collective-permute-start(bf16[512,1024]{1,0:T(8,128)(2,1)} %refs_0_.1), channel_id=1, source_target_pairs={{8,0},{12,4},{16,8},{20,12},{24,16},{28,20},{9,1},{13,5},{17,9},{2... | collective-permute-start | bytes 3145736 | tf_op jit(solution)/shard_map/ppermute | solution.py:31
  2.1 33.1 %collective-permute-start.3 = (bf16[512,1024]{1,0:T(8,128)(2,1)}, bf16[512,1024]{1,0:T(8,128)(2,1)}, u32[]{:S(2)}, u32[]{:S(2)}) collective-permute-start(bf16[512,1024]{1,0:T(8,128)(2,1)} %refs_0_.1), channel_id=1, source_target_pairs={{0,8},{4,12},{8,16},{12,20},{16,24},{20,28},{1,9},{5,13},{9,17},{1... | collective-permute-start | bytes 3145736 | tf_op jit(solution)/shard_map/ppermute | solution.py:31
  9.9 15.2 %collective-permute-start = (bf16[512,512]{1,0:T(8,128)(2,1)}, bf16[512,512]{1,0:T(8,128)(2,1)}, u32[]{:S(2)}, u32[]{:S(2)}) collective-permute-start(bf16[512,512]{1,0:T(8,128)(2,1)} %get-tuple-element.134), channel_id=1, source_target_pairs={{0,4},{4,0},{8,12},{12,8},{16,20},{20,16},{24,28},{28,24},{1,5},{5... | collective-permute-start | bytes 1572872 | tf_op jit(solution)/shard_map/ppermute | solution.py:36
  13.3 142.5 %copy-start.1 = (bf16[2,128,4096]{2,1,0:T(8,128)(2,1)}, bf16[2,128,4096]{2,1,0:T(8,128)(2,1)S(1)}, u32[]{:S(2)}) copy-start(bf16[2,128,4096]{2,1,0:T(8,128)(2,1)S(1)} %broadcast_select_fusion) | copy-start | bytes 6291460
  14.3 20.9 %collective-permute-start.1 = (bf16[256,1024]{1,0:T(8,128)(2,1)}, bf16[256,1024]{1,0:T(8,128)(2,1)}, u32[]{:S(2)}, u32[]{:S(2)}) collective-permute-start(bf16[256,1024]{1,0:T(8,128)(2,1)} %constant_dynamic-slice_fusion.1), channel_id=1, source_target_pairs={{0,4},{4,0},{8,12},{12,8},{16,20},{20,16},{24,28},{28,24},{1,5},{5... | collective-permute-start | bytes 1572872 | tf_op jit(solution)/shard_map/ppermute | solution.py:36
  15.5 19.7 %all-to-all-start = ((bf16[8,8,512]{2,0,1:T(8,128)(2,1)}), bf16[8,8,512]{2,0,1:T(8,128)(2,1)S(1)}, u32[]{:S(2)}, u32[]{:S(2)}) async-start(bf16[8,8,512]{2,0,1:T(8,128)(2,1)} %copy.14), calls=%async_computation | async-start | bytes 131072 | tf_op jit(solution)/shard_map/all_to_all | solution.py:313
  35.2 23.9 %collective-permute-start.4 = (bf16[512,1024]{1,0:T(8,128)(2,1)}, bf16[512,1024]{1,0:T(8,128)(2,1)}, u32[]{:S(2)}, u32[]{:S(2)}) collective-permute-start(bf16[512,1024]{1,0:T(8,128)(2,1)} %refs_0_.1), channel_id=1, source_target_pairs={{0,4},{4,0},{8,12},{12,8},{16,20},{20,16},{24,28},{28,24},{1,5},{5... | collective-permute-start | bytes 3145736 | tf_op jit(solution)/shard_map/ppermute | solution.py:36
  36.7 61.1 %collective-permute-start.8 = (bf16[512,1024]{1,0:T(8,128)(2,1)}, bf16[512,1024]{1,0:T(8,128)(2,1)}, u32[]{:S(2)}, u32[]{:S(2)}) collective-permute-start(bf16[512,1024]{1,0:T(8,128)(2,1)} %pad_maximum_fusion.refs_0_), channel_id=1, source_target_pairs={{8,0},{12,4},{16,8},{20,12},{24,16},{28,20},{9,1},{13,5},{17,9},{2... | collective-permute-start | bytes 3145736 | tf_op jit(solution)/shard_map/ppermute | solution.py:31
  38.0 59.8 %collective-permute-start.9 = (bf16[512,1024]{1,0:T(8,128)(2,1)}, bf16[512,1024]{1,0:T(8,128)(2,1)}, u32[]{:S(2)}, u32[]{:S(2)}) collective-permute-start(bf16[512,1024]{1,0:T(8,128)(2,1)} %pad_maximum_fusion.refs_0_), channel_id=1, source_target_pairs={{0,8},{4,12},{8,16},{12,20},{16,24},{20,28},{1,9},{5,13},{9,17},{1... | collective-permute-start | bytes 3145736 | tf_op jit(solution)/shard_map/ppermute | solution.py:31
  43.6 54.2 %collective-permute-start.6 = (bf16[512,1024]{1,0:T(8,128)(2,1)}, bf16[512,1024]{1,0:T(8,128)(2,1)}, u32[]{:S(2)}, u32[]{:S(2)}) collective-permute-start(bf16[512,1024]{1,0:T(8,128)(2,1)} %collective-permute-done.2.refs_1_), channel_id=1, source_target_pairs={{8,0},{12,4},{16,8},{20,12},{9,1},{13,5},{17,9},{21,13},{10,2},{14... | collective-permute-start | bytes 3145736 | tf_op jit(solution)/shard_map/ppermute | solution.py:31
  44.9 52.9 %collective-permute-start.7 = (bf16[512,1024]{1,0:T(8,128)(2,1)}, bf16[512,1024]{1,0:T(8,128)(2,1)}, u32[]{:S(2)}, u32[]{:S(2)}) collective-permute-start(bf16[512,1024]{1,0:T(8,128)(2,1)} %collective-permute-done.3.refs_2_), channel_id=1, source_target_pairs={{8,16},{12,20},{16,24},{20,28},{9,17},{13,21},{17,25},{21,29},{10,... | collective-permute-start | bytes 3145736 | tf_op jit(solution)/shard_map/ppermute | solution.py:31
  59.0 38.8 %collective-permute-start.5 = (bf16[512,1024]{1,0:T(8,128)(2,1)}, bf16[512,1024]{1,0:T(8,128)(2,1)}, u32[]{:S(2)}, u32[]{:S(2)}) collective-permute-start(bf16[512,1024]{1,0:T(8,128)(2,1)} %collective-permute-done.2.refs_1_), channel_id=1, source_target_pairs={{0,4},{4,0},{8,12},{12,8},{16,20},{20,16},{1,5},{5,1},{9,13},{13,9... | collective-permute-start | bytes 3145736 | tf_op jit(solution)/shard_map/ppermute | solution.py:36
  63.3 33.4 %all-to-all-start.1 = ((f32[8,8,2048]{2,1,0:T(8,128)}), f32[8,8,2048]{2,1,0:T(8,128)}, u32[]{:S(2)}, u32[]{:S(2)}) async-start(f32[8,8,2048]{2,1,0:T(8,128)} %maximum_bitcast_fusion), calls=%async_computation.1 | async-start | bytes 1048576 | tf_op jit(solution)/shard_map/all_to_all | solution.py:334
  100.2 51.4 %collective-permute-start.12 = (bf16[512,1024]{1,0:T(8,128)(2,1)}, bf16[512,1024]{1,0:T(8,128)(2,1)}, u32[]{:S(2)}, u32[]{:S(2)}) collective-permute-start(bf16[512,1024]{1,0:T(8,128)(2,1)} %broadcast_select_fusion.2.refs_3_), channel_id=1, source_target_pairs={{8,0},{12,4},{16,24},{20,28},{9,1},{13,5},{17,25},{21,29},{10,2},{... | collective-permute-start | bytes 3145736 | tf_op jit(solution)/shard_map/ppermute | solution.py:31
  101.5 50.1 %collective-permute-start.14 = (bf16[512,1024]{1,0:T(8,128)(2,1)}, bf16[512,1024]{1,0:T(8,128)(2,1)}, u32[]{:S(2)}, u32[]{:S(2)}) collective-permute-start(bf16[512,1024]{1,0:T(8,128)(2,1)} %broadcast_select_fusion.2.refs_3_), channel_id=1, source_target_pairs={{0,4},{4,0},{8,12},{12,8},{16,20},{20,16},{24,28},{28,24},{1,5},{5... | collective-permute-start | bytes 3145736 | tf_op jit(solution)/shard_map/ppermute | solution.py:36
  102.3 49.3 %collective-permute-start.10 = (bf16[512,1024]{1,0:T(8,128)(2,1)}, bf16[512,1024]{1,0:T(8,128)(2,1)}, u32[]{:S(2)}, u32[]{:S(2)}) collective-permute-start(bf16[512,1024]{1,0:T(8,128)(2,1)} %collective-permute-done.8.refs_1_), channel_id=1, source_target_pairs={{8,0},{12,4},{16,8},{20,12},{9,1},{13,5},{17,9},{21,13},{10,2},{14... | collective-permute-start | bytes 3145736 | tf_op jit(solution)/shard_map/ppermute | solution.py:31
  103.6 48.0 %collective-permute-start.11 = (bf16[512,1024]{1,0:T(8,128)(2,1)}, bf16[512,1024]{1,0:T(8,128)(2,1)}, u32[]{:S(2)}, u32[]{:S(2)}) collective-permute-start(bf16[512,1024]{1,0:T(8,128)(2,1)} %collective-permute-done.9.refs_2_), channel_id=1, source_target_pairs={{8,16},{12,20},{16,24},{20,28},{9,17},{13,21},{17,25},{21,29},{10,... | collective-permute-start | bytes 3145736 | tf_op jit(solution)/shard_map/ppermute | solution.py:31
  105.3 46.3 %collective-permute-start.13 = (bf16[512,1024]{1,0:T(8,128)(2,1)}, bf16[512,1024]{1,0:T(8,128)(2,1)}, u32[]{:S(2)}, u32[]{:S(2)}) collective-permute-start(bf16[512,1024]{1,0:T(8,128)(2,1)} %collective-permute-done.3.refs_2_), channel_id=1, source_target_pairs={{8,12},{12,8},{16,20},{20,16},{24,28},{28,24},{9,13},{13,9},{17,21... | collective-permute-start | bytes 3145736 | tf_op jit(solution)/shard_map/ppermute | solution.py:36
  107.6 43.9 %all-to-all-start.2 = ((bf16[8,8,2048]{2,1,0:T(8,128)(2,1)}), bf16[8,8,2048]{2,1,0:T(8,128)(2,1)S(1)}, u32[]{:S(2)}, u32[]{:S(2)}) async-start(bf16[8,8,2048]{2,1,0:T(8,128)(2,1)} %broadcast_in_dim.16), calls=%async_computation.2 | async-start | bytes 524288 | tf_op jit(solution)/shard_map/all_to_all | solution.py:343
  154.0 31.0 %collective-permute-start.18 = (bf16[512,1024]{1,0:T(8,128)(2,1)}, bf16[512,1024]{1,0:T(8,128)(2,1)}, u32[]{:S(2)}, u32[]{:S(2)}) collective-permute-start(bf16[512,1024]{1,0:T(8,128)(2,1)} %broadcast_select_fusion.1.refs_2_), channel_id=1, source_target_pairs={{8,0},{12,4},{16,24},{20,28},{9,1},{13,5},{17,25},{21,29},{10,2},{... | collective-permute-start | bytes 3145736 | tf_op jit(solution)/shard_map/ppermute | solution.py:31
  155.2 13.7 %collective-permute-start.16 = (bf16[256,1024]{1,0:T(8,128)(2,1)}, bf16[256,1024]{1,0:T(8,128)(2,1)}, u32[]{:S(2)}, u32[]{:S(2)}) collective-permute-start(bf16[256,1024]{1,0:T(8,128)(2,1)} %collective-permute-done.1.mine), channel_id=1, source_target_pairs={{0,2},{1,3},{2,0},{3,1},{4,6},{5,7},{6,4},{7,5},{8,10},{9,11},{10,... | collective-permute-start | bytes 1572872 | tf_op jit(solution)/shard_map/ppermute | solution.py:300
  157.0 33.6 %all-to-all-start.3 = ((bf16[1,64,8,512]{3,1,0,2:T(8,128)(2,1)}), bf16[1,64,8,512]{3,1,0,2:T(8,128)(2,1)S(1)}, u32[]{:S(2)}, u32[]{:S(2)}) async-start(bf16[1,64,8,512]{3,1,0,2:T(8,128)(2,1)} %copy.15), calls=%async_computation.3 | async-start | bytes 1048576 | tf_op jit(solution)/shard_map/all_to_all | solution.py:359
  165.0 26.8 %collective-permute-start.19 = (bf16[512,1024]{1,0:T(8,128)(2,1)}, bf16[512,1024]{1,0:T(8,128)(2,1)S(1)}, u32[]{:S(2)}, u32[]{:S(2)}) collective-permute-start(bf16[512,1024]{1,0:T(8,128)(2,1)} %collective-permute-done.12.refs_0_.refs_4_), channel_id=1, source_target_pairs={{0,4},{4,0},{24,28},{28,24},{1,5},{5,1},{25,29},{29,25},{2,6},{6,2... | collective-permute-start | bytes 3145736 | tf_op jit(solution)/shard_map/ppermute | solution.py:36
  168.9 8.5 %collective-permute-start.15 = (bf16[256,1024]{1,0:T(8,128)(2,1)}, bf16[256,1024]{1,0:T(8,128)(2,1)S(1)}, u32[]{:S(2)}, u32[]{:S(2)}) collective-permute-start(bf16[256,1024]{1,0:T(8,128)(2,1)} %collective-permute-done.1.mine), channel_id=1, source_target_pairs={{0,1},{1,0},{2,3},{3,2},{4,5},{5,4},{6,7},{7,6},{8,9},{9,8},{10,11... | collective-permute-start | bytes 1572872 | tf_op jit(solution)/shard_map/ppermute | solution.py:300
  169.0 8.4 %collective-permute-start.17 = (bf16[256,1024]{1,0:T(8,128)(2,1)}, bf16[256,1024]{1,0:T(8,128)(2,1)}, u32[]{:S(2)}, u32[]{:S(2)}) collective-permute-start(bf16[256,1024]{1,0:T(8,128)(2,1)} %collective-permute-done.16.by_y), channel_id=1, source_target_pairs={{0,1},{1,0},{2,3},{3,2},{4,5},{5,4},{6,7},{7,6},{8,9},{9,8},{10,11... | collective-permute-start | bytes 1572872 | tf_op jit(solution)/shard_map/ppermute | solution.py:300
  190.6 7.6 %collective-permute-start.20 = (bf16[256,512]{1,0:T(8,128)(2,1)}, bf16[256,512]{1,0:T(8,128)(2,1)S(1)}, u32[]{:S(2)}, u32[]{:S(2)}) collective-permute-start(bf16[256,512]{1,0:T(8,128)(2,1)} %get-tuple-element.107), channel_id=1, source_target_pairs={{0,4},{4,0},{8,12},{12,8},{16,20},{20,16},{24,28},{28,24},{1,5},{5... | collective-permute-start | bytes 786440 | tf_op jit(solution)/shard_map/ppermute | solution.py:36
  202.6 43.9 %all-to-all-start.4 = ((f32[8,8,2048]{2,1,0:T(8,128)}), f32[8,8,2048]{2,1,0:T(8,128)S(1)}, u32[]{:S(2)}, u32[]{:S(2)}) async-start(f32[8,8,2048]{2,1,0:T(8,128)} %bitcast.55), calls=%async_computation.4 | async-start | bytes 1048576 | tf_op jit(solution)/shard_map/all_to_all | solution.py:426
  207.5 18.7 %collective-permute-start.22 = (bf16[256,1024]{1,0:T(8,128)(2,1)}, bf16[256,1024]{1,0:T(8,128)(2,1)S(1)}, u32[]{:S(2)}, u32[]{:S(2)}) collective-permute-start(bf16[256,1024]{1,0:T(8,128)(2,1)} %get-tuple-element.117.refs_2_), channel_id=1, source_target_pairs={{0,4},{4,0},{8,12},{12,8},{16,20},{20,16},{24,28},{28,24},{1,5},{5... | collective-permute-start | bytes 1572872 | tf_op jit(solution)/shard_map/ppermute | solution.py:36
  209.6 19.9 %collective-permute-start.23 = (bf16[256,1024]{1,0:T(8,128)(2,1)}, bf16[256,1024]{1,0:T(8,128)(2,1)}, u32[]{:S(2)}, u32[]{:S(2)}) collective-permute-start(bf16[256,1024]{1,0:T(8,128)(2,1)} %get-tuple-element.117.refs_2_), channel_id=1, source_target_pairs={{8,0},{12,4},{16,8},{20,12},{24,16},{28,20},{0,24},{4,28},{9,1},{1... | collective-permute-start | bytes 1572872 | tf_op jit(solution)/shard_map/ppermute | solution.py:31
  212.8 29.5 %collective-permute-start.24 = (bf16[256,1024]{1,0:T(8,128)(2,1)}, bf16[256,1024]{1,0:T(8,128)(2,1)}, u32[]{:S(2)}, u32[]{:S(2)}) collective-permute-start(bf16[256,1024]{1,0:T(8,128)(2,1)} %get-tuple-element.117.refs_2_), channel_id=1, source_target_pairs={{24,0},{28,4},{0,8},{4,12},{8,16},{12,20},{16,24},{20,28},{25,1},{... | collective-permute-start | bytes 1572872 | tf_op jit(solution)/shard_map/ppermute | solution.py:31
  212.8 33.6 %collective-permute-start.21 = (bf16[8,64,512]{2,1,0:T(8,128)(2,1)S(1)}, bf16[8,64,512]{2,1,0:T(8,128)(2,1)S(1)}, u32[]{:S(2)}, u32[]{:S(2)}) collective-permute-start(bf16[8,64,512]{2,1,0:T(8,128)(2,1)S(1)} %bitcast.48), channel_id=1, source_target_pairs={{0,2},{1,3},{2,0},{3,1},{4,6},{5,7},{6,4},{7,5},{8,10},{9,11},{10,... | collective-permute-start | bytes 1572872 | tf_op jit(solution)/shard_map/ppermute | solution.py:300
  226.2 18.1 %copy-start.11 = (bf16[256,1024]{1,0:T(8,128)(2,1)}, bf16[256,1024]{1,0:T(8,128)(2,1)S(1)}, u32[]{:S(2)}) copy-start(bf16[256,1024]{1,0:T(8,128)(2,1)S(1)} %collective-permute-done.22.refs_6_) | copy-start | bytes 1572868
  242.3 15.3 %collective-permute-start.25 = (bf16[256,1024]{1,0:T(8,128)(2,1)}, bf16[256,1024]{1,0:T(8,128)(2,1)}, u32[]{:S(2)}, u32[]{:S(2)}) collective-permute-start(bf16[256,1024]{1,0:T(8,128)(2,1)} %collective-permute-done.23.refs_3_), channel_id=1, source_target_pairs={{0,4},{4,0},{8,12},{12,8},{16,20},{20,16},{24,28},{28,24},{1,5},{5... | collective-permute-start | bytes 1572872 | tf_op jit(solution)/shard_map/ppermute | solution.py:36
  243.8 23.8 %collective-permute-start.26 = (bf16[256,1024]{1,0:T(8,128)(2,1)}, bf16[256,1024]{1,0:T(8,128)(2,1)}, u32[]{:S(2)}, u32[]{:S(2)}) collective-permute-start(bf16[256,1024]{1,0:T(8,128)(2,1)} %collective-permute-done.24.refs_5_), channel_id=1, source_target_pairs={{0,4},{4,0},{8,12},{12,8},{16,20},{20,16},{24,28},{28,24},{1,5},{5... | collective-permute-start | bytes 1572872 | tf_op jit(solution)/shard_map/ppermute | solution.py:36
  244.4 29.0 %collective-permute-start.29 = (bf16[256,1024]{1,0:T(8,128)(2,1)}, bf16[256,1024]{1,0:T(8,128)(2,1)}, u32[]{:S(2)}, u32[]{:S(2)}) collective-permute-start(bf16[256,1024]{1,0:T(8,128)(2,1)} %get-tuple-element.117.refs_2_), channel_id=1, source_target_pairs={{16,0},{20,4},{24,8},{28,12},{0,16},{4,20},{8,24},{12,28},{17,1},{... | collective-permute-start | bytes 1572872 | tf_op jit(solution)/shard_map/ppermute | solution.py:31
  248.9 26.0 %collective-permute-start.27 = (bf16[2,256,512]{2,1,0:T(8,128)(2,1)}, bf16[2,256,512]{2,1,0:T(8,128)(2,1)S(1)}, u32[]{:S(2)}, u32[]{:S(2)}) collective-permute-start(bf16[2,256,512]{2,1,0:T(8,128)(2,1)} %get-tuple-element.132), channel_id=1, source_target_pairs={{0,2},{1,3},{2,0},{3,1},{4,6},{5,7},{6,4},{7,5},{8,10},{9,11},{10,... | collective-permute-start | bytes 1572872 | tf_op jit(solution)/shard_map/ppermute | solution.py:300
  249.9 25.0 %collective-permute-start.28 = (bf16[2,256,512]{2,1,0:T(8,128)(2,1)}, bf16[2,256,512]{2,1,0:T(8,128)(2,1)}, u32[]{:S(2)}, u32[]{:S(2)}) collective-permute-start(bf16[2,256,512]{2,1,0:T(8,128)(2,1)} %get-tuple-element.131), channel_id=1, source_target_pairs={{0,3},{1,2},{2,1},{3,0},{4,7},{5,6},{6,5},{7,4},{8,11},{9,10},{10,... | collective-permute-start | bytes 1572872 | tf_op jit(solution)/shard_map/ppermute | solution.py:300
  250.6 24.2 %all-to-all-start.5 = ((bf16[8,8,2048]{2,1,0:T(8,128)(2,1)}), bf16[8,8,2048]{2,1,0:T(8,128)(2,1)S(1)}, u32[]{:S(2)}, u32[]{:S(2)}) async-start(bf16[8,8,2048]{2,1,0:T(8,128)(2,1)} %broadcast_in_dim.17), calls=%async_computation.5 | async-start | bytes 524288 | tf_op jit(solution)/shard_map/all_to_all | solution.py:343
  255.4 23.9 %copy-start.2 = (bf16[512,1024]{1,0:T(8,128)(2,1)S(1)}, bf16[512,1024]{1,0:T(8,128)(2,1)}, u32[]{:S(2)}) copy-start(bf16[512,1024]{1,0:T(8,128)(2,1)} %param.13) | copy-start | bytes 3145732
  274.9 29.7 %copy-start.6 = (bf16[2,256,512]{2,1,0:T(8,128)(2,1)}, bf16[2,256,512]{2,1,0:T(8,128)(2,1)S(1)}, u32[]{:S(2)}) copy-start(bf16[2,256,512]{2,1,0:T(8,128)(2,1)S(1)} %collective-permute-done.27.refs_0_) | copy-start | bytes 1572868
  274.9 16.7 %collective-permute-start.30 = (bf16[2,8,64,512]{3,2,1,0:T(8,128)(2,1)}, bf16[2,8,64,512]{3,2,1,0:T(8,128)(2,1)}, u32[]{:S(2)}, u32[]{:S(2)}) collective-permute-start(bf16[2,8,64,512]{3,2,1,0:T(8,128)(2,1)} %pad_maximum_fusion.1.refs_0_), channel_id=1, source_target_pairs={{0,1},{1,0},{2,3},{3,2},{4,5},{5,4},{6,7},{7,6},{8,9},{9,8},{10,11... | collective-permute-start | bytes 3145736 | tf_op jit(solution)/shard_map/ppermute | solution.py:300
  276.9 9.7 %collective-permute-start.31 = (bf16[2,256,512]{2,1,0:T(8,128)(2,1)}, bf16[2,256,512]{2,1,0:T(8,128)(2,1)S(1)}, u32[]{:S(2)}, u32[]{:S(2)}) collective-permute-start(bf16[2,256,512]{2,1,0:T(8,128)(2,1)} %slice_bitcast_fusion), channel_id=1, source_target_pairs={{0,1},{1,0},{2,3},{3,2},{4,5},{5,4},{6,7},{7,6},{8,9},{9,8},{10,11... | collective-permute-start | bytes 1572872 | tf_op jit(solution)/shard_map/ppermute | solution.py:300
  277.3 14.3 %collective-permute-start.32 = (bf16[256,1024]{1,0:T(8,128)(2,1)}, bf16[256,1024]{1,0:T(8,128)(2,1)}, u32[]{:S(2)}, u32[]{:S(2)}) collective-permute-start(bf16[256,1024]{1,0:T(8,128)(2,1)} %collective-permute-done.29.refs_4_), channel_id=1, source_target_pairs={{0,4},{4,0},{8,12},{12,8},{16,20},{20,16},{24,28},{28,24},{1,5},{5... | collective-permute-start | bytes 1572872 | tf_op jit(solution)/shard_map/ppermute | solution.py:36
  280.5 6.2 %all-to-all-start.6 = ((bf16[4,16,512]{2,1,0:T(8,128)(2,1)}), bf16[4,16,512]{2,1,0:T(8,128)(2,1)S(1)}, u32[]{:S(2)}, u32[]{:S(2)}) async-start(bf16[4,16,512]{2,1,0:T(8,128)(2,1)} %bitcast.19), calls=%async_computation.6 | async-start | bytes 131072 | tf_op jit(solution)/shard_map/all_to_all | solution.py:250
  286.7 17.9 %copy-start.7 = (bf16[2,256,512]{2,1,0:T(8,128)(2,1)}, bf16[2,256,512]{2,1,0:T(8,128)(2,1)S(1)}, u32[]{:S(2)}) copy-start(bf16[2,256,512]{2,1,0:T(8,128)(2,1)S(1)} %collective-permute-done.31.refs_2_) | copy-start | bytes 1572868
  291.6 16.1 %collective-permute-start.33 = (bf16[8,512]{1,0:T(8,128)(2,1)S(1)}, bf16[8,512]{1,0:T(8,128)(2,1)S(1)}, u32[]{:S(2)}, u32[]{:S(2)}) collective-permute-start(bf16[8,512]{1,0:T(8,128)(2,1)S(1)} %get-tuple-element.135), channel_id=1, source_target_pairs={{0,0},{1,8},{2,16},{3,24},{4,4},{5,12},{6,20},{7,28},{8,1},{9,9},{... | collective-permute-start | bytes 24584 | tf_op jit(solution)/shard_map/ppermute | solution.py:266
  294.8 12.8 %collective-permute-start.34 = (bf16[8,512]{1,0:T(8,128)(2,1)S(1)}, bf16[8,512]{1,0:T(8,128)(2,1)S(1)}, u32[]{:S(2)}, u32[]{:S(2)}) collective-permute-start(bf16[8,512]{1,0:T(8,128)(2,1)S(1)} %get-tuple-element.136), channel_id=1, source_target_pairs={{0,4},{1,12},{2,20},{3,28},{4,0},{5,8},{6,16},{7,24},{8,5},{9,13},... | collective-permute-start | bytes 24584 | tf_op jit(solution)/shard_map/ppermute | solution.py:266
  (7 other events, 29.8 us)

commit v13 on v12

--- a/solution.py
+++ b/solution.py
@@ -374,6 +374,7 @@
         (),
         2 * rows * width * local_cols,
     )
+
     half = shape((rows, half_cols), F32)
     wo_early = [wo_pair, *wo_moved]
     grad_parts = call(
@@ -411,6 +412,7 @@
     wq_blocks = [*arrivals, *wq_others]
 
     att_next = [line.shift(attended, m) for m in (1, line.n_z - 1)]
+    attended, grad_come = gate((attended, grad_come))
     att_swapped = line.swap(attended)
     live_y = tensor_swap(live_mine, 2)
 
@@ -422,8 +424,6 @@
         (),
         10 * images * rows * local_cols,
     )
-    kv_part = kv_part.reshape(n_dp, image_rows, 2 * local_cols)
-    kv_grad = jnp.sum(lax.all_to_all(kv_part, "dp", split_axis=0, concat_axis=0), axis=0)
     chunk = n_dp // n_tensor
     term = call(
         functools.partial(term_kernel, line, relayed),
@@ -433,14 +433,17 @@
         (),
         2 * rows * width * local_cols,
     )
-    kv_grad, term, live_y = gate((kv_grad.astype(BF16), term, live_y))
-    kv_grad_all = everywhere(kv_grad).reshape(images, 2 * local_cols)
-    live_pair = jnp.stack([live_mine, live_y])
-
+    kv_part, term, live_y, attended, att_swapped, *att_next = gate(
+        (kv_part, term, live_y, attended, att_swapped, *att_next)
+    )
+
+    kv_part = kv_part.reshape(n_dp, image_rows, 2 * local_cols)
+    kv_grad = jnp.sum(lax.all_to_all(kv_part, "dp", split_axis=0, concat_axis=0), axis=0)
+    kv_grad_all = everywhere(kv_grad.astype(BF16)).reshape(images, 2 * local_cols)
     text_parts = [tensor_swap(term[k], k) for k in range(2, n_tensor)]
-    attended, att_swapped, *att_next = gate((attended, att_swapped, *att_next))
     att_far = [line.shift(attended, m) for m in range(2, line.n_z - 1)]
     att_other_next = [line.swap(block) for block in att_next]
+    live_pair = jnp.stack([live_mine, live_y])
     kv_grad_all, term, live_pair, *staged = gate(
         (kv_grad_all, term, live_pair, *att_other_next, *text_parts, *att_far)
     )
@@ -452,13 +455,13 @@
     text_parts.append(tensor_swap(term[1], 1))
     image_term = matmul(kv_grad_all[:, :local_cols], key_weight, BACK)
     image_term = image_term + matmul(kv_grad_all[:, local_cols:], value_weight, BACK)
-    image_grad, live_core, text_parts[-1], *att_other_far = to_owner(
-        line, image_term.astype(BF16), live_core, text_parts[-1], *att_other_far
-    )
-    image_grad = image_grad.reshape(samples, image_own, width // n_tensor)
     text_grad = call(
         sum_kernel, place, (term, *text_parts), [shape((rows, width // n_tensor), BF16)]
     )
+    image_grad, live_core, text_grad, *att_other_far = to_owner(
+        line, image_term.astype(BF16), live_core, text_grad, *att_other_far
+    )
+    image_grad = image_grad.reshape(samples, image_own, width // n_tensor)
     text_grad = text_grad.reshape(samples, tok_rows, width // n_tensor)
 
     att_blocks = [attended, att_next[0], *att_far, att_next[1]]

time: 310 us -> 301 us (0.971)
  waiting for transfers between devices: 129 us -> 123 us
    all_to_all x1, waiting for transfers between devices: 0.01 us -> 17.9 us  [shards(): lax.all_to_all(kv_part, 'dp', split_axis=0, concat_axis=0)]
    ppermute x12, waiting for transfers between devices: 34.2 us -> 17.7 us  [swap(): return lax.ppermute(block, 'dp', pairs)]
    ppermute x13, waiting for transfers between devices: 22.9 us -> 15.4 us  [move(): return lax.ppermute(block, 'dp', pairs)]
  transfers between devices with their start and end apart: 42 -> 42, of which waited for: 16 -> 13; matrix products, arithmetic and copies ran while one was open for 8% -> 8% of each run, Pallas kernels for 14% -> 15%
where the time goes in v13:
time: 301 us; the launch traced here: 299 us
  waiting for transfers between devices  123 us (41%)
  starting transfers between devices  98.5 us (33%)
  Pallas kernels  45.7 us (15%)
  other arithmetic  14.3 us (5%)
  local copies, waits for them, and re-layouts  13.2 us (4%)
  matrix products  3.32 us (1%)
    pallas_call x8, Pallas kernels, call(): pl.pallas_call(kernel, out_shape=outs[0] if single else outs, in_specs=[p...  45.7 us
    all_to_all x2, waiting for transfers between devices, everywhere(): return lax.all_to_all(copies, 'dp', split_axis=0, concat_axis=0)  32.8 us
    all_to_all x1, waiting for transfers between devices, shards(): lax.all_to_all(part_kv, 'dp', split_axis=0, concat_axis=0)  29.3 us
    ppermute x13, starting transfers between devices, move(): return lax.ppermute(block, 'dp', pairs)  28 us
    ppermute x12, starting transfers between devices, swap(): return lax.ppermute(block, 'dp', pairs)  18.8 us
    all_to_all x1, waiting for transfers between devices, shards(): lax.all_to_all(kv_part, 'dp', split_axis=0, concat_axis=0)  17.9 us
    ppermute x12, waiting for transfers between devices, swap(): return lax.ppermute(block, 'dp', pairs)  17.7 us
    all_to_all x2, starting transfers between devices, everywhere(): return lax.all_to_all(copies, 'dp', split_axis=0, concat_axis=0)  15.8 us
  transfers between devices with their start and end apart: 42, of which 13 were waited for; matrix products, arithmetic and copies ran while one was open for 8% of the time, Pallas kernels for 15%

profile of v13, /device:TPU:4, one launch (start us, length us, event | category | flops | bytes accessed | tf_op | source)
XLA Modules:
  0.0 299.3 jit_solution(5238669831366123844)
XLA Ops:
  2.1 5.5 %collective-permute-start.3 = (bf16[512,1024]{1,0:T(8,128)(2,1)}, bf16[512,1024]{1,0:T(8,128)(2,1)}, u32[]{:S(2)}, u32[]{:S(2)}) collective-permute-start(bf16[512,1024]{1,0:T(8,128)(2,1)} %refs_0_.1), channel_id=1, source_target_pairs={{0,8},{4,12},{8,16},{12,20},{16,24},{20,28},{1,9},{5,13},{9,17},{1... | collective-permute-start | bytes 3145736 | tf_op jit(solution)/shard_map/ppermute | solution.py:31
  7.6 2.3 constant_dynamic-slice_fusion.3
  11.5 1.8 broadcast_select_fusion
  15.5 4.8 %all-to-all-start = ((bf16[8,8,512]{2,0,1:T(8,128)(2,1)}), bf16[8,8,512]{2,0,1:T(8,128)(2,1)S(1)}, u32[]{:S(2)}, u32[]{:S(2)}) async-start(bf16[8,8,512]{2,0,1:T(8,128)(2,1)} %copy.14), calls=%async_computation | async-start | bytes 131072 | tf_op jit(solution)/shard_map/all_to_all | solution.py:313
  20.3 4.7 %collective-permute-done = bf16[512,512]{1,0:T(8,128)(2,1)} collective-permute-done((bf16[512,512]{1,0:T(8,128)(2,1)}, bf16[512,512]{1,0:T(8,128)(2,1)}, u32[]{:S(2)}, u32[]{:S(2)}) %collective-permute-start) | collective-permute-done | bytes 524320 | tf_op jit(solution)/shard_map/ppermute | solution.py:36
  25.1 2.3 pad_maximum_fusion.refs_0_
  27.3 7.8 %all-to-all-done = bf16[8,8,512]{2,0,1:T(8,128)(2,1)S(1)} async-done(((bf16[8,8,512]{2,0,1:T(8,128)(2,1)}), bf16[8,8,512]{2,0,1:T(8,128)(2,1)S(1)}, u32[]{:S(2)}, u32[]{:S(2)}) %all-to-all-start) | async-done | bytes 65568 | tf_op jit(solution)/shard_map/all_to_all | solution.py:313
  35.2 1.6 collective-permute-start.4
  38.0 5.5 %collective-permute-start.9 = (bf16[512,1024]{1,0:T(8,128)(2,1)}, bf16[512,1024]{1,0:T(8,128)(2,1)}, u32[]{:S(2)}, u32[]{:S(2)}) collective-permute-start(bf16[512,1024]{1,0:T(8,128)(2,1)} %pad_maximum_fusion.refs_0_), channel_id=1, source_target_pairs={{0,8},{4,12},{8,16},{12,20},{16,24},{20,28},{1,9},{5,13},{9,17},{1... | collective-permute-start | bytes 3145736 | tf_op jit(solution)/shard_map/ppermute | solution.py:31
  44.8 1.7 collective-permute-start.7
  46.5 1.5 fusion.4
  48.3 10.7 %collective-permute-done.4.refs_4_.refs_5_ = bf16[512,1024]{1,0:T(8,128)(2,1)} collective-permute-done((bf16[512,1024]{1,0:T(8,128)(2,1)}, bf16[512,1024]{1,0:T(8,128)(2,1)}, u32[]{:S(2)}, u32[]{:S(2)}) %collective-permute-start.4) | collective-permute-done | bytes 1048608 | tf_op jit(solution)/shard_map/ppermute | solution.py:36
  59.0 3.4 %collective-permute-start.5 = (bf16[512,1024]{1,0:T(8,128)(2,1)}, bf16[512,1024]{1,0:T(8,128)(2,1)}, u32[]{:S(2)}, u32[]{:S(2)}) collective-permute-start(bf16[512,1024]{1,0:T(8,128)(2,1)} %collective-permute-done.2.refs_1_), channel_id=1, source_target_pairs={{0,4},{4,0},{8,12},{12,8},{16,20},{20,16},{1,5},{5,1},{9,13},{13,9... | collective-permute-start | bytes 3145736 | tf_op jit(solution)/shard_map/ppermute | solution.py:36
  63.3 4.2 %all-to-all-start.1 = ((f32[8,8,2048]{2,1,0:T(8,128)}), f32[8,8,2048]{2,1,0:T(8,128)}, u32[]{:S(2)}, u32[]{:S(2)}) async-start(f32[8,8,2048]{2,1,0:T(8,128)} %maximum_bitcast_fusion), calls=%async_computation.1 | async-start | bytes 1048576 | tf_op jit(solution)/shard_map/all_to_all | solution.py:334
  67.4 29.3 %all-to-all-done.1 = f32[8,8,2048]{2,1,0:T(8,128)} async-done(((f32[8,8,2048]{2,1,0:T(8,128)}), f32[8,8,2048]{2,1,0:T(8,128)}, u32[]{:S(2)}, u32[]{:S(2)}) %all-to-all-start.1) | async-done | bytes 524320 | tf_op jit(solution)/shard_map/all_to_all | solution.py:334
  97.9 2.3 broadcast_select_fusion.2.refs_3_
  103.6 1.7 collective-permute-start.11
  105.3 1.6 collective-permute-start.13
  107.6 12.4 %all-to-all-start.2 = ((bf16[8,8,2048]{2,1,0:T(8,128)(2,1)}), bf16[8,8,2048]{2,1,0:T(8,128)(2,1)S(1)}, u32[]{:S(2)}, u32[]{:S(2)}) async-start(bf16[8,8,2048]{2,1,0:T(8,128)(2,1)} %broadcast_in_dim.16), calls=%async_computation.2 | async-start | bytes 524288 | tf_op jit(solution)/shard_map/all_to_all | solution.py:343
  120.0 31.5 %all-to-all-done.2 = bf16[8,8,2048]{2,1,0:T(8,128)(2,1)S(1)} async-done(((bf16[8,8,2048]{2,1,0:T(8,128)(2,1)}), bf16[8,8,2048]{2,1,0:T(8,128)(2,1)S(1)}, u32[]{:S(2)}, u32[]{:S(2)}) %all-to-all-start.2) | async-done | bytes 262176 | tf_op jit(solution)/shard_map/all_to_all | solution.py:343
  151.6 2.4 broadcast_select_fusion.1.refs_2_
  157.0 8.1 %all-to-all-start.3 = ((bf16[1,64,8,512]{3,1,0,2:T(8,128)(2,1)}), bf16[1,64,8,512]{3,1,0,2:T(8,128)(2,1)S(1)}, u32[]{:S(2)}, u32[]{:S(2)}) async-start(bf16[1,64,8,512]{3,1,0,2:T(8,128)(2,1)} %copy.15), calls=%async_computation.3 | async-start | bytes 1048576 | tf_op jit(solution)/shard_map/all_to_all | solution.py:359
  165.1 3.9 %collective-permute-start.19 = (bf16[512,1024]{1,0:T(8,128)(2,1)}, bf16[512,1024]{1,0:T(8,128)(2,1)S(1)}, u32[]{:S(2)}, u32[]{:S(2)}) collective-permute-start(bf16[512,1024]{1,0:T(8,128)(2,1)} %collective-permute-done.12.refs_0_.refs_4_), channel_id=1, source_target_pairs={{0,4},{4,0},{24,28},{28,24},{1,5},{5,1},{25,29},{29,25},{2,6},{6,2... | collective-permute-start | bytes 3145736 | tf_op jit(solution)/shard_map/ppermute | solution.py:36
  170.3 7.3 %shard_map.103.part = f32[256,1024]{1,0:T(8,128)} custom-call(s32[4]{0:T(128)} %pad_add_fusion.place, bf16[256,4096]{1,0:T(8,128)(2,1)} %bitcast.42, bf16[512,1024]{1,0:T(8,128)(2,1)} %refs_0_.1, bf16[512,1024]{1,0:T(8,128)(2,1)} %collective-permute-done.2.refs_1_, bf16[512,1024]{1,0:T(8,128)(2,1)} %collective-permute-done.3.refs_2_, ...), custom_call_target="tpu_custom_call" | custom-call | flops 2147483648 | bytes 11534336 | tf_op jit(solution)/shard_map/pallas_call | solution.py:228
  178.4 5.8 %shard_map.104 = (f32[256,512]{1,0:T(8,128)}, f32[256,512]{1,0:T(8,128)}) custom-call(s32[4]{0:T(128)} %pad_add_fusion.place, bf16[256,4096]{1,0:T(8,128)(2,1)} %bitcast.40, bf16[256,1024]{1,0:T(8,128)(2,1)} %collective-permute-done.1.mine, bf16[256,1024]{1,0:T(8,128)(2,1)} %copy-done.5, bf16[256,1024]{1,0:T(8,128)(2,1)} %collective-permute-done.16.by_y, ...), custom_call_target="tpu_custom_call" | custom-call | flops 1073741824 | bytes 8388608 | tf_op jit(solution)/shard_map/pallas_call | solution.py:228
  185.0 5.7 %shard_map.105 = (bf16[256,512]{1,0:T(8,128)(2,1)}, bf16[256,512]{1,0:T(8,128)(2,1)}) custom-call(s32[4]{0:T(128)} %pad_add_fusion.place, bf16[256,4096]{1,0:T(8,128)(2,1)} %bitcast.41, bf16[256,1024]{1,0:T(8,128)(2,1)} %collective-permute-done.1.mine, bf16[256,1024]{1,0:T(8,128)(2,1)} %copy-done.5, bf16[256,1024]{1,0:T(8,128)(2,1)} %collective-permute-done.16.by_y, ...), custom_call_target="tpu_custom_call" | custom-call | flops 1073741824 | bytes 7864320 | tf_op jit(solution)/shard_map/pallas_call | solution.py:228
  193.1 5.3 %shard_map.106 = (bf16[256,1024]{1,0:T(8,128)(2,1)}, bf16[256,1024]{1,0:T(8,128)(2,1)}) custom-call(s32[4]{0:T(128)} %pad_add_fusion.place, bf16[256,4096]{1,0:T(8,128)(2,1)} %bitcast.43, bf16[64,2048]{1,0:T(8,128)(2,1)} %bitcast.44, f32[256,1024]{1,0:T(8,128)} %shard_map.103.part, bf16[512,1024]{1,0:T(8,128)(2,1)} %collective-permute-done.12.refs_0_.refs_4_, ...), custom_call_target="tpu_custom_call" | custom-call | flops 1073741824 | bytes 6553600 | tf_op jit(solution)/shard_map/pallas_call | solution.py:228
  198.4 2.8 collective-permute-start.23
  201.3 1.5 collective-permute-start.21
  202.8 1.6 collective-permute-start.22
  204.4 3.6 %shard_map.107 = (bf16[256,1024]{1,0:T(8,128)(2,1)}, f32[64,2048]{1,0:T(8,128)}) custom-call(s32[4]{0:T(128)} %pad_add_fusion.place, bf16[256,1024]{1,0:T(8,128)(2,1)} %get-tuple-element.107.query, bf16[64,2048]{1,0:T(8,128)(2,1)} %bitcast.45, bf16[256,512]{1,0:T(8,128)(2,1)} %get-tuple-element.108.keep, bf16[256,512]{1,0:T(8,128)(2,1)} %copy-done.9), custom_call_target="tpu_custom_call" | custom-call | flops 167772160 | bytes 2359296 | tf_op jit(solution)/shard_map/pallas_call | solution.py:228
  207.9 8.8 %shard_map.108.term = bf16[4,2,256,512]{3,2,1,0:T(8,128)(2,1)} custom-call(s32[4]{0:T(128)} %pad_add_fusion.place, bf16[256,1024]{1,0:T(8,128)(2,1)} %get-tuple-element.113.query_grad, bf16[512,1024]{1,0:T(8,128)(2,1)} %refs_0_.1, bf16[512,1024]{1,0:T(8,128)(2,1)} %collective-permute-done.2.refs_1_, bf16[512,1024]{1,0:T(8,128)(2,1)} %collective-permute-done.3.refs_2_, ...), custom_call_target="tpu_custom_call" | custom-call | flops 2147483648 | bytes 13107200 | tf_op jit(solution)/shard_map/pallas_call | solution.py:228
  216.7 7.1 %collective-permute-done.24.refs_5_ = bf16[256,1024]{1,0:T(8,128)(2,1)} collective-permute-done((bf16[256,1024]{1,0:T(8,128)(2,1)}, bf16[256,1024]{1,0:T(8,128)(2,1)}, u32[]{:S(2)}, u32[]{:S(2)}) %collective-permute-start.24) | collective-permute-done | bytes 524320 | tf_op jit(solution)/shard_map/ppermute | solution.py:31
  223.9 4.0 %all-to-all-start.4 = ((f32[8,8,2048]{2,1,0:T(8,128)}), f32[8,8,2048]{2,1,0:T(8,128)S(1)}, u32[]{:S(2)}, u32[]{:S(2)}) async-start(f32[8,8,2048]{2,1,0:T(8,128)} %bitcast.13), calls=%async_computation.4 | async-start | bytes 1048576 | tf_op jit(solution)/shard_map/all_to_all | solution.py:441
  227.9 2.2 slice_bitcast_fusion.1
  231.2 2.0 collective-permute-start.25
  233.3 2.9 collective-permute-start.29
  236.2 17.9 %all-to-all-done.4 = f32[8,8,2048]{2,1,0:T(8,128)S(1)} async-done(((f32[8,8,2048]{2,1,0:T(8,128)}), f32[8,8,2048]{2,1,0:T(8,128)S(1)}, u32[]{:S(2)}, u32[]{:S(2)}) %all-to-all-start.4) | async-done | bytes 524320 | tf_op jit(solution)/shard_map/all_to_all | solution.py:441
  254.8 3.4 %all-to-all-start.5 = ((bf16[8,8,2048]{2,1,0:T(8,128)(2,1)}), bf16[8,8,2048]{2,1,0:T(8,128)(2,1)S(1)}, u32[]{:S(2)}, u32[]{:S(2)}) async-start(bf16[8,8,2048]{2,1,0:T(8,128)(2,1)} %broadcast_in_dim.17), calls=%async_computation.5 | async-start | bytes 524288 | tf_op jit(solution)/shard_map/all_to_all | solution.py:343
  258.2 2.2 pad_maximum_fusion.1.refs_0_
  260.5 7.5 %collective-permute-done.29.refs_4_ = bf16[256,1024]{1,0:T(8,128)(2,1)} collective-permute-done((bf16[256,1024]{1,0:T(8,128)(2,1)}, bf16[256,1024]{1,0:T(8,128)(2,1)}, u32[]{:S(2)}, u32[]{:S(2)}) %collective-permute-start.29) | collective-permute-done | bytes 524320 | tf_op jit(solution)/shard_map/ppermute | solution.py:31
  269.2 1.9 slice_bitcast_fusion
  274.6 3.8 %all-to-all-start.6 = ((bf16[4,16,512]{2,1,0:T(8,128)(2,1)}), bf16[4,16,512]{2,1,0:T(8,128)(2,1)S(1)}, u32[]{:S(2)}, u32[]{:S(2)}) async-start(bf16[4,16,512]{2,1,0:T(8,128)(2,1)} %bitcast.19), calls=%async_computation.6 | async-start | bytes 131072 | tf_op jit(solution)/shard_map/all_to_all | solution.py:250
  278.4 2.3 all-to-all-done.6
  281.5 3.0 %shard_map.109 = bf16[256,1024]{1,0:T(8,128)(2,1)} custom-call(s32[4]{0:T(128)} %pad_add_fusion.place, bf16[4,2,256,512]{3,2,1,0:T(8,128)(2,1)} %shard_map.108.term, bf16[2,256,512]{2,1,0:T(8,128)(2,1)} %copy-done.6, bf16[2,256,512]{2,1,0:T(8,128)(2,1)} %collective-permute-done.28.refs_1_, bf16[2,256,512]{2,1,0:T(8,128)(2,1)} %copy-done.7), custom_call_target="tpu_custom_call" | custom-call | bytes 4194304 | tf_op jit(solution)/shard_map/pallas_call | solution.py:228
  285.8 3.1 %collective-permute-start.33 = (bf16[8,512]{1,0:T(8,128)(2,1)S(1)}, bf16[8,512]{1,0:T(8,128)(2,1)S(1)}, u32[]{:S(2)}, u32[]{:S(2)}) collective-permute-start(bf16[8,512]{1,0:T(8,128)(2,1)S(1)} %get-tuple-element.139), channel_id=1, source_target_pairs={{0,0},{1,8},{2,16},{3,24},{4,4},{5,12},{6,20},{7,28},{8,1},{9,9},{... | collective-permute-start | bytes 24584 | tf_op jit(solution)/shard_map/ppermute | solution.py:266
  288.9 3.6 %collective-permute-start.34 = (bf16[8,512]{1,0:T(8,128)(2,1)S(1)}, bf16[8,512]{1,0:T(8,128)(2,1)S(1)}, u32[]{:S(2)}, u32[]{:S(2)}) collective-permute-start(bf16[8,512]{1,0:T(8,128)(2,1)S(1)} %get-tuple-element.140), channel_id=1, source_target_pairs={{0,4},{1,12},{2,20},{3,28},{4,0},{5,8},{6,16},{7,24},{8,5},{9,13},... | collective-permute-start | bytes 24584 | tf_op jit(solution)/shard_map/ppermute | solution.py:266
  292.5 6.2 %shard_map.110 = bf16[1024,512]{1,0:T(8,128)(2,1)} custom-call(s32[4]{0:T(128)} %pad_add_fusion.place, bf16[2,8,64,512]{3,2,1,0:T(8,128)(2,1)} %pad_maximum_fusion.1.refs_0_, bf16[2,8,64,512]{3,2,1,0:T(8,128)(2,1)} %collective-permute-done.30.refs_1_, bf16[256,1024]{1,0:T(8,128)(2,1)} %get-tuple-element.121.refs_2_, ...), custom_call_target="tpu_custom_call" | custom-call | flops 2147483648 | bytes 7340032 | tf_op jit(solution)/shard_map/pallas_call | solution.py:228
  (99 shorter events, 31.7 us)
Async XLA Ops:
  0.6 47.4 %copy-start = (bf16[512,1024]{1,0:T(8,128)(2,1)S(1)}, bf16[512,1024]{1,0:T(8,128)(2,1)}, u32[]{:S(2)}) copy-start(bf16[512,1024]{1,0:T(8,128)(2,1)} %param.14) | copy-start | bytes 3145732
  0.6 10.7 %copy-start.11 = (s32[2]{0:T(128)S(1)}, s32[2]{0:T(128)}, u32[]{:S(2)}) copy-start(s32[2]{0:T(128)} %param.11) | copy-start | bytes 28
  0.7 34.5 %collective-permute-start.2 = (bf16[512,1024]{1,0:T(8,128)(2,1)}, bf16[512,1024]{1,0:T(8,128)(2,1)}, u32[]{:S(2)}, u32[]{:S(2)}) collective-permute-start(bf16[512,1024]{1,0:T(8,128)(2,1)} %refs_0_.1), channel_id=1, source_target_pairs={{8,0},{12,4},{16,8},{20,12},{24,16},{28,20},{9,1},{13,5},{17,9},{2... | collective-permute-start | bytes 3145736 | tf_op jit(solution)/shard_map/ppermute | solution.py:31
  2.1 33.1 %collective-permute-start.3 = (bf16[512,1024]{1,0:T(8,128)(2,1)}, bf16[512,1024]{1,0:T(8,128)(2,1)}, u32[]{:S(2)}, u32[]{:S(2)}) collective-permute-start(bf16[512,1024]{1,0:T(8,128)(2,1)} %refs_0_.1), channel_id=1, source_target_pairs={{0,8},{4,12},{8,16},{12,20},{16,24},{20,28},{1,9},{5,13},{9,17},{1... | collective-permute-start | bytes 3145736 | tf_op jit(solution)/shard_map/ppermute | solution.py:31
  9.9 15.2 %collective-permute-start = (bf16[512,512]{1,0:T(8,128)(2,1)}, bf16[512,512]{1,0:T(8,128)(2,1)}, u32[]{:S(2)}, u32[]{:S(2)}) collective-permute-start(bf16[512,512]{1,0:T(8,128)(2,1)} %get-tuple-element.138), channel_id=1, source_target_pairs={{0,4},{4,0},{8,12},{12,8},{16,20},{20,16},{24,28},{28,24},{1,5},{5... | collective-permute-start | bytes 1572872 | tf_op jit(solution)/shard_map/ppermute | solution.py:36
  13.3 142.6 %copy-start.1 = (bf16[2,128,4096]{2,1,0:T(8,128)(2,1)}, bf16[2,128,4096]{2,1,0:T(8,128)(2,1)S(1)}, u32[]{:S(2)}) copy-start(bf16[2,128,4096]{2,1,0:T(8,128)(2,1)S(1)} %broadcast_select_fusion) | copy-start | bytes 6291460
  14.3 20.9 %collective-permute-start.1 = (bf16[256,1024]{1,0:T(8,128)(2,1)}, bf16[256,1024]{1,0:T(8,128)(2,1)}, u32[]{:S(2)}, u32[]{:S(2)}) collective-permute-start(bf16[256,1024]{1,0:T(8,128)(2,1)} %constant_dynamic-slice_fusion.1), channel_id=1, source_target_pairs={{0,4},{4,0},{8,12},{12,8},{16,20},{20,16},{24,28},{28,24},{1,5},{5... | collective-permute-start | bytes 1572872 | tf_op jit(solution)/shard_map/ppermute | solution.py:36
  15.5 19.7 %all-to-all-start = ((bf16[8,8,512]{2,0,1:T(8,128)(2,1)}), bf16[8,8,512]{2,0,1:T(8,128)(2,1)S(1)}, u32[]{:S(2)}, u32[]{:S(2)}) async-start(bf16[8,8,512]{2,0,1:T(8,128)(2,1)} %copy.14), calls=%async_computation | async-start | bytes 131072 | tf_op jit(solution)/shard_map/all_to_all | solution.py:313
  35.2 23.9 %collective-permute-start.4 = (bf16[512,1024]{1,0:T(8,128)(2,1)}, bf16[512,1024]{1,0:T(8,128)(2,1)}, u32[]{:S(2)}, u32[]{:S(2)}) collective-permute-start(bf16[512,1024]{1,0:T(8,128)(2,1)} %refs_0_.1), channel_id=1, source_target_pairs={{0,4},{4,0},{8,12},{12,8},{16,20},{20,16},{24,28},{28,24},{1,5},{5... | collective-permute-start | bytes 3145736 | tf_op jit(solution)/shard_map/ppermute | solution.py:36
  36.7 61.1 %collective-permute-start.8 = (bf16[512,1024]{1,0:T(8,128)(2,1)}, bf16[512,1024]{1,0:T(8,128)(2,1)}, u32[]{:S(2)}, u32[]{:S(2)}) collective-permute-start(bf16[512,1024]{1,0:T(8,128)(2,1)} %pad_maximum_fusion.refs_0_), channel_id=1, source_target_pairs={{8,0},{12,4},{16,8},{20,12},{24,16},{28,20},{9,1},{13,5},{17,9},{2... | collective-permute-start | bytes 3145736 | tf_op jit(solution)/shard_map/ppermute | solution.py:31
  38.0 59.9 %collective-permute-start.9 = (bf16[512,1024]{1,0:T(8,128)(2,1)}, bf16[512,1024]{1,0:T(8,128)(2,1)}, u32[]{:S(2)}, u32[]{:S(2)}) collective-permute-start(bf16[512,1024]{1,0:T(8,128)(2,1)} %pad_maximum_fusion.refs_0_), channel_id=1, source_target_pairs={{0,8},{4,12},{8,16},{12,20},{16,24},{20,28},{1,9},{5,13},{9,17},{1... | collective-permute-start | bytes 3145736 | tf_op jit(solution)/shard_map/ppermute | solution.py:31
  43.5 54.3 %collective-permute-start.6 = (bf16[512,1024]{1,0:T(8,128)(2,1)}, bf16[512,1024]{1,0:T(8,128)(2,1)}, u32[]{:S(2)}, u32[]{:S(2)}) collective-permute-start(bf16[512,1024]{1,0:T(8,128)(2,1)} %collective-permute-done.2.refs_1_), channel_id=1, source_target_pairs={{8,0},{12,4},{16,8},{20,12},{9,1},{13,5},{17,9},{21,13},{10,2},{14... | collective-permute-start | bytes 3145736 | tf_op jit(solution)/shard_map/ppermute | solution.py:31
  44.8 53.0 %collective-permute-start.7 = (bf16[512,1024]{1,0:T(8,128)(2,1)}, bf16[512,1024]{1,0:T(8,128)(2,1)}, u32[]{:S(2)}, u32[]{:S(2)}) collective-permute-start(bf16[512,1024]{1,0:T(8,128)(2,1)} %collective-permute-done.3.refs_2_), channel_id=1, source_target_pairs={{8,16},{12,20},{16,24},{20,28},{9,17},{13,21},{17,25},{21,29},{10,... | collective-permute-start | bytes 3145736 | tf_op jit(solution)/shard_map/ppermute | solution.py:31
  59.0 38.8 %collective-permute-start.5 = (bf16[512,1024]{1,0:T(8,128)(2,1)}, bf16[512,1024]{1,0:T(8,128)(2,1)}, u32[]{:S(2)}, u32[]{:S(2)}) collective-permute-start(bf16[512,1024]{1,0:T(8,128)(2,1)} %collective-permute-done.2.refs_1_), channel_id=1, source_target_pairs={{0,4},{4,0},{8,12},{12,8},{16,20},{20,16},{1,5},{5,1},{9,13},{13,9... | collective-permute-start | bytes 3145736 | tf_op jit(solution)/shard_map/ppermute | solution.py:36
  63.3 33.5 %all-to-all-start.1 = ((f32[8,8,2048]{2,1,0:T(8,128)}), f32[8,8,2048]{2,1,0:T(8,128)}, u32[]{:S(2)}, u32[]{:S(2)}) async-start(f32[8,8,2048]{2,1,0:T(8,128)} %maximum_bitcast_fusion), calls=%async_computation.1 | async-start | bytes 1048576 | tf_op jit(solution)/shard_map/all_to_all | solution.py:334
  100.2 51.4 %collective-permute-start.12 = (bf16[512,1024]{1,0:T(8,128)(2,1)}, bf16[512,1024]{1,0:T(8,128)(2,1)}, u32[]{:S(2)}, u32[]{:S(2)}) collective-permute-start(bf16[512,1024]{1,0:T(8,128)(2,1)} %broadcast_select_fusion.2.refs_3_), channel_id=1, source_target_pairs={{8,0},{12,4},{16,24},{20,28},{9,1},{13,5},{17,25},{21,29},{10,2},{... | collective-permute-start | bytes 3145736 | tf_op jit(solution)/shard_map/ppermute | solution.py:31
  101.5 50.1 %collective-permute-start.14 = (bf16[512,1024]{1,0:T(8,128)(2,1)}, bf16[512,1024]{1,0:T(8,128)(2,1)}, u32[]{:S(2)}, u32[]{:S(2)}) collective-permute-start(bf16[512,1024]{1,0:T(8,128)(2,1)} %broadcast_select_fusion.2.refs_3_), channel_id=1, source_target_pairs={{0,4},{4,0},{8,12},{12,8},{16,20},{20,16},{24,28},{28,24},{1,5},{5... | collective-permute-start | bytes 3145736 | tf_op jit(solution)/shard_map/ppermute | solution.py:36
  102.3 49.3 %collective-permute-start.10 = (bf16[512,1024]{1,0:T(8,128)(2,1)}, bf16[512,1024]{1,0:T(8,128)(2,1)}, u32[]{:S(2)}, u32[]{:S(2)}) collective-permute-start(bf16[512,1024]{1,0:T(8,128)(2,1)} %collective-permute-done.8.refs_1_), channel_id=1, source_target_pairs={{8,0},{12,4},{16,8},{20,12},{9,1},{13,5},{17,9},{21,13},{10,2},{14... | collective-permute-start | bytes 3145736 | tf_op jit(solution)/shard_map/ppermute | solution.py:31
  103.6 48.0 %collective-permute-start.11 = (bf16[512,1024]{1,0:T(8,128)(2,1)}, bf16[512,1024]{1,0:T(8,128)(2,1)}, u32[]{:S(2)}, u32[]{:S(2)}) collective-permute-start(bf16[512,1024]{1,0:T(8,128)(2,1)} %collective-permute-done.9.refs_2_), channel_id=1, source_target_pairs={{8,16},{12,20},{16,24},{20,28},{9,17},{13,21},{17,25},{21,29},{10,... | collective-permute-start | bytes 3145736 | tf_op jit(solution)/shard_map/ppermute | solution.py:31
  105.3 46.3 %collective-permute-start.13 = (bf16[512,1024]{1,0:T(8,128)(2,1)}, bf16[512,1024]{1,0:T(8,128)(2,1)}, u32[]{:S(2)}, u32[]{:S(2)}) collective-permute-start(bf16[512,1024]{1,0:T(8,128)(2,1)} %collective-permute-done.3.refs_2_), channel_id=1, source_target_pairs={{8,12},{12,8},{16,20},{20,16},{24,28},{28,24},{9,13},{13,9},{17,21... | collective-permute-start | bytes 3145736 | tf_op jit(solution)/shard_map/ppermute | solution.py:36
  107.6 43.9 %all-to-all-start.2 = ((bf16[8,8,2048]{2,1,0:T(8,128)(2,1)}), bf16[8,8,2048]{2,1,0:T(8,128)(2,1)S(1)}, u32[]{:S(2)}, u32[]{:S(2)}) async-start(bf16[8,8,2048]{2,1,0:T(8,128)(2,1)} %broadcast_in_dim.16), calls=%async_computation.2 | async-start | bytes 524288 | tf_op jit(solution)/shard_map/all_to_all | solution.py:343
  154.0 31.0 %collective-permute-start.18 = (bf16[512,1024]{1,0:T(8,128)(2,1)}, bf16[512,1024]{1,0:T(8,128)(2,1)}, u32[]{:S(2)}, u32[]{:S(2)}) collective-permute-start(bf16[512,1024]{1,0:T(8,128)(2,1)} %broadcast_select_fusion.1.refs_2_), channel_id=1, source_target_pairs={{8,0},{12,4},{16,24},{20,28},{9,1},{13,5},{17,25},{21,29},{10,2},{... | collective-permute-start | bytes 3145736 | tf_op jit(solution)/shard_map/ppermute | solution.py:31
  155.3 13.8 %collective-permute-start.16 = (bf16[256,1024]{1,0:T(8,128)(2,1)}, bf16[256,1024]{1,0:T(8,128)(2,1)}, u32[]{:S(2)}, u32[]{:S(2)}) collective-permute-start(bf16[256,1024]{1,0:T(8,128)(2,1)} %collective-permute-done.1.mine), channel_id=1, source_target_pairs={{0,2},{1,3},{2,0},{3,1},{4,6},{5,7},{6,4},{7,5},{8,10},{9,11},{10,... | collective-permute-start | bytes 1572872 | tf_op jit(solution)/shard_map/ppermute | solution.py:300
  157.0 33.6 %all-to-all-start.3 = ((bf16[1,64,8,512]{3,1,0,2:T(8,128)(2,1)}), bf16[1,64,8,512]{3,1,0,2:T(8,128)(2,1)S(1)}, u32[]{:S(2)}, u32[]{:S(2)}) async-start(bf16[1,64,8,512]{3,1,0,2:T(8,128)(2,1)} %copy.15), calls=%async_computation.3 | async-start | bytes 1048576 | tf_op jit(solution)/shard_map/all_to_all | solution.py:359
  165.1 27.0 %collective-permute-start.19 = (bf16[512,1024]{1,0:T(8,128)(2,1)}, bf16[512,1024]{1,0:T(8,128)(2,1)S(1)}, u32[]{:S(2)}, u32[]{:S(2)}) collective-permute-start(bf16[512,1024]{1,0:T(8,128)(2,1)} %collective-permute-done.12.refs_0_.refs_4_), channel_id=1, source_target_pairs={{0,4},{4,0},{24,28},{28,24},{1,5},{5,1},{25,29},{29,25},{2,6},{6,2... | collective-permute-start | bytes 3145736 | tf_op jit(solution)/shard_map/ppermute | solution.py:36
  169.0 8.5 %collective-permute-start.15 = (bf16[256,1024]{1,0:T(8,128)(2,1)}, bf16[256,1024]{1,0:T(8,128)(2,1)S(1)}, u32[]{:S(2)}, u32[]{:S(2)}) collective-permute-start(bf16[256,1024]{1,0:T(8,128)(2,1)} %collective-permute-done.1.mine), channel_id=1, source_target_pairs={{0,1},{1,0},{2,3},{3,2},{4,5},{5,4},{6,7},{7,6},{8,9},{9,8},{10,11... | collective-permute-start | bytes 1572872 | tf_op jit(solution)/shard_map/ppermute | solution.py:300
  169.1 8.5 %collective-permute-start.17 = (bf16[256,1024]{1,0:T(8,128)(2,1)}, bf16[256,1024]{1,0:T(8,128)(2,1)}, u32[]{:S(2)}, u32[]{:S(2)}) collective-permute-start(bf16[256,1024]{1,0:T(8,128)(2,1)} %collective-permute-done.16.by_y), channel_id=1, source_target_pairs={{0,1},{1,0},{2,3},{3,2},{4,5},{5,4},{6,7},{7,6},{8,9},{9,8},{10,11... | collective-permute-start | bytes 1572872 | tf_op jit(solution)/shard_map/ppermute | solution.py:300
  190.6 12.2 %collective-permute-start.20 = (bf16[256,512]{1,0:T(8,128)(2,1)}, bf16[256,512]{1,0:T(8,128)(2,1)S(1)}, u32[]{:S(2)}, u32[]{:S(2)}) collective-permute-start(bf16[256,512]{1,0:T(8,128)(2,1)} %get-tuple-element.110), channel_id=1, source_target_pairs={{0,4},{4,0},{8,12},{12,8},{16,20},{20,16},{24,28},{28,24},{1,5},{5... | collective-permute-start | bytes 786440 | tf_op jit(solution)/shard_map/ppermute | solution.py:36
  198.4 18.3 %collective-permute-start.23 = (bf16[256,1024]{1,0:T(8,128)(2,1)}, bf16[256,1024]{1,0:T(8,128)(2,1)}, u32[]{:S(2)}, u32[]{:S(2)}) collective-permute-start(bf16[256,1024]{1,0:T(8,128)(2,1)} %get-tuple-element.121.refs_2_), channel_id=1, source_target_pairs={{8,0},{12,4},{16,8},{20,12},{24,16},{28,20},{0,24},{4,28},{9,1},{1... | collective-permute-start | bytes 1572872 | tf_op jit(solution)/shard_map/ppermute | solution.py:31
  201.3 22.6 %collective-permute-start.24 = (bf16[256,1024]{1,0:T(8,128)(2,1)}, bf16[256,1024]{1,0:T(8,128)(2,1)}, u32[]{:S(2)}, u32[]{:S(2)}) collective-permute-start(bf16[256,1024]{1,0:T(8,128)(2,1)} %get-tuple-element.121.refs_2_), channel_id=1, source_target_pairs={{24,0},{28,4},{0,8},{4,12},{8,16},{12,20},{16,24},{20,28},{25,1},{... | collective-permute-start | bytes 1572872 | tf_op jit(solution)/shard_map/ppermute | solution.py:31
  201.3 22.6 %collective-permute-start.21 = (bf16[8,64,512]{2,1,0:T(8,128)(2,1)S(1)}, bf16[8,64,512]{2,1,0:T(8,128)(2,1)S(1)}, u32[]{:S(2)}, u32[]{:S(2)}) collective-permute-start(bf16[8,64,512]{2,1,0:T(8,128)(2,1)S(1)} %bitcast.48), channel_id=1, source_target_pairs={{0,2},{1,3},{2,0},{3,1},{4,6},{5,7},{6,4},{7,5},{8,10},{9,11},{10,... | collective-permute-start | bytes 1572872 | tf_op jit(solution)/shard_map/ppermute | solution.py:300
  202.8 21.1 %collective-permute-start.22 = (bf16[256,1024]{1,0:T(8,128)(2,1)}, bf16[256,1024]{1,0:T(8,128)(2,1)}, u32[]{:S(2)}, u32[]{:S(2)}) collective-permute-start(bf16[256,1024]{1,0:T(8,128)(2,1)} %get-tuple-element.121.refs_2_), channel_id=1, source_target_pairs={{0,4},{4,0},{8,12},{12,8},{16,20},{20,16},{24,28},{28,24},{1,5},{5... | collective-permute-start | bytes 1572872 | tf_op jit(solution)/shard_map/ppermute | solution.py:36
  223.8 31.0 %copy-start.8 = (bf16[8,64,512]{2,1,0:T(8,128)(2,1)}, bf16[8,64,512]{2,1,0:T(8,128)(2,1)S(1)}, u32[]{:S(2)}) copy-start(bf16[8,64,512]{2,1,0:T(8,128)(2,1)S(1)} %collective-permute-done.21) | copy-start | bytes 1572868
  223.9 30.2 %all-to-all-start.4 = ((f32[8,8,2048]{2,1,0:T(8,128)}), f32[8,8,2048]{2,1,0:T(8,128)S(1)}, u32[]{:S(2)}, u32[]{:S(2)}) async-start(f32[8,8,2048]{2,1,0:T(8,128)} %bitcast.13), calls=%async_computation.4 | async-start | bytes 1048576 | tf_op jit(solution)/shard_map/all_to_all | solution.py:441
  230.1 30.3 %collective-permute-start.27 = (bf16[2,256,512]{2,1,0:T(8,128)(2,1)}, bf16[2,256,512]{2,1,0:T(8,128)(2,1)S(1)}, u32[]{:S(2)}, u32[]{:S(2)}) collective-permute-start(bf16[2,256,512]{2,1,0:T(8,128)(2,1)} %get-tuple-element.136), channel_id=1, source_target_pairs={{0,2},{1,3},{2,0},{3,1},{4,6},{5,7},{6,4},{7,5},{8,10},{9,11},{10,... | collective-permute-start | bytes 1572872 | tf_op jit(solution)/shard_map/ppermute | solution.py:300
  231.2 29.2 %collective-permute-start.28 = (bf16[2,256,512]{2,1,0:T(8,128)(2,1)}, bf16[2,256,512]{2,1,0:T(8,128)(2,1)}, u32[]{:S(2)}, u32[]{:S(2)}) collective-permute-start(bf16[2,256,512]{2,1,0:T(8,128)(2,1)} %get-tuple-element.135), channel_id=1, source_target_pairs={{0,3},{1,2},{2,1},{3,0},{4,7},{5,6},{6,5},{7,4},{8,11},{9,10},{10,... | collective-permute-start | bytes 1572872 | tf_op jit(solution)/shard_map/ppermute | solution.py:300
  231.2 29.2 %collective-permute-start.25 = (bf16[256,1024]{1,0:T(8,128)(2,1)}, bf16[256,1024]{1,0:T(8,128)(2,1)}, u32[]{:S(2)}, u32[]{:S(2)}) collective-permute-start(bf16[256,1024]{1,0:T(8,128)(2,1)} %collective-permute-done.23.refs_3_), channel_id=1, source_target_pairs={{0,4},{4,0},{8,12},{12,8},{16,20},{20,16},{24,28},{28,24},{1,5},{5... | collective-permute-start | bytes 1572872 | tf_op jit(solution)/shard_map/ppermute | solution.py:36
  233.2 27.2 %collective-permute-start.26 = (bf16[256,1024]{1,0:T(8,128)(2,1)}, bf16[256,1024]{1,0:T(8,128)(2,1)}, u32[]{:S(2)}, u32[]{:S(2)}) collective-permute-start(bf16[256,1024]{1,0:T(8,128)(2,1)} %collective-permute-done.24.refs_5_), channel_id=1, source_target_pairs={{0,4},{4,0},{8,12},{12,8},{16,20},{20,16},{24,28},{28,24},{1,5},{5... | collective-permute-start | bytes 1572872 | tf_op jit(solution)/shard_map/ppermute | solution.py:36
  233.3 34.7 %collective-permute-start.29 = (bf16[256,1024]{1,0:T(8,128)(2,1)}, bf16[256,1024]{1,0:T(8,128)(2,1)}, u32[]{:S(2)}, u32[]{:S(2)}) collective-permute-start(bf16[256,1024]{1,0:T(8,128)(2,1)} %get-tuple-element.121.refs_2_), channel_id=1, source_target_pairs={{16,0},{20,4},{24,8},{28,12},{0,16},{4,20},{8,24},{12,28},{17,1},{... | collective-permute-start | bytes 1572872 | tf_op jit(solution)/shard_map/ppermute | solution.py:31
  254.8 14.4 %all-to-all-start.5 = ((bf16[8,8,2048]{2,1,0:T(8,128)(2,1)}), bf16[8,8,2048]{2,1,0:T(8,128)(2,1)S(1)}, u32[]{:S(2)}, u32[]{:S(2)}) async-start(bf16[8,8,2048]{2,1,0:T(8,128)(2,1)} %broadcast_in_dim.17), calls=%async_computation.5 | async-start | bytes 524288 | tf_op jit(solution)/shard_map/all_to_all | solution.py:343
  258.2 15.3 %copy-start.2 = (bf16[512,1024]{1,0:T(8,128)(2,1)S(1)}, bf16[512,1024]{1,0:T(8,128)(2,1)}, u32[]{:S(2)}) copy-start(bf16[512,1024]{1,0:T(8,128)(2,1)} %param.13) | copy-start | bytes 3145732
  260.5 20.3 %copy-start.6 = (bf16[2,256,512]{2,1,0:T(8,128)(2,1)}, bf16[2,256,512]{2,1,0:T(8,128)(2,1)S(1)}, u32[]{:S(2)}) copy-start(bf16[2,256,512]{2,1,0:T(8,128)(2,1)S(1)} %collective-permute-done.27.refs_0_) | copy-start | bytes 1572868
  269.2 16.5 %collective-permute-start.30 = (bf16[2,8,64,512]{3,2,1,0:T(8,128)(2,1)}, bf16[2,8,64,512]{3,2,1,0:T(8,128)(2,1)}, u32[]{:S(2)}, u32[]{:S(2)}) collective-permute-start(bf16[2,8,64,512]{3,2,1,0:T(8,128)(2,1)} %pad_maximum_fusion.1.refs_0_), channel_id=1, source_target_pairs={{0,1},{1,0},{2,3},{3,2},{4,5},{5,4},{6,7},{7,6},{8,9},{9,8},{10,11... | collective-permute-start | bytes 3145736 | tf_op jit(solution)/shard_map/ppermute | solution.py:300
  271.1 9.6 %collective-permute-start.31 = (bf16[2,256,512]{2,1,0:T(8,128)(2,1)}, bf16[2,256,512]{2,1,0:T(8,128)(2,1)S(1)}, u32[]{:S(2)}, u32[]{:S(2)}) collective-permute-start(bf16[2,256,512]{2,1,0:T(8,128)(2,1)} %slice_bitcast_fusion), channel_id=1, source_target_pairs={{0,1},{1,0},{2,3},{3,2},{4,5},{5,4},{6,7},{7,6},{8,9},{9,8},{10,11... | collective-permute-start | bytes 1572872 | tf_op jit(solution)/shard_map/ppermute | solution.py:300
  271.6 14.1 %collective-permute-start.32 = (bf16[256,1024]{1,0:T(8,128)(2,1)}, bf16[256,1024]{1,0:T(8,128)(2,1)}, u32[]{:S(2)}, u32[]{:S(2)}) collective-permute-start(bf16[256,1024]{1,0:T(8,128)(2,1)} %collective-permute-done.29.refs_4_), channel_id=1, source_target_pairs={{0,4},{4,0},{8,12},{12,8},{16,20},{20,16},{24,28},{28,24},{1,5},{5... | collective-permute-start | bytes 1572872 | tf_op jit(solution)/shard_map/ppermute | solution.py:36
  274.6 6.1 %all-to-all-start.6 = ((bf16[4,16,512]{2,1,0:T(8,128)(2,1)}), bf16[4,16,512]{2,1,0:T(8,128)(2,1)S(1)}, u32[]{:S(2)}, u32[]{:S(2)}) async-start(bf16[4,16,512]{2,1,0:T(8,128)(2,1)} %bitcast.19), calls=%async_computation.6 | async-start | bytes 131072 | tf_op jit(solution)/shard_map/all_to_all | solution.py:250
  285.8 12.9 %collective-permute-start.33 = (bf16[8,512]{1,0:T(8,128)(2,1)S(1)}, bf16[8,512]{1,0:T(8,128)(2,1)S(1)}, u32[]{:S(2)}, u32[]{:S(2)}) collective-permute-start(bf16[8,512]{1,0:T(8,128)(2,1)S(1)} %get-tuple-element.139), channel_id=1, source_target_pairs={{0,0},{1,8},{2,16},{3,24},{4,4},{5,12},{6,20},{7,28},{8,1},{9,9},{... | collective-permute-start | bytes 24584 | tf_op jit(solution)/shard_map/ppermute | solution.py:266
  288.9 9.8 %collective-permute-start.34 = (bf16[8,512]{1,0:T(8,128)(2,1)S(1)}, bf16[8,512]{1,0:T(8,128)(2,1)S(1)}, u32[]{:S(2)}, u32[]{:S(2)}) collective-permute-start(bf16[8,512]{1,0:T(8,128)(2,1)S(1)} %get-tuple-element.140), channel_id=1, source_target_pairs={{0,4},{1,12},{2,20},{3,28},{4,0},{5,8},{6,16},{7,24},{8,5},{9,13},... | collective-permute-start | bytes 24584 | tf_op jit(solution)/shard_map/ppermute | solution.py:266
  (6 other events, 11.9 us)

commit v14 on v13

--- a/solution.py
+++ b/solution.py
@@ -347,103 +347,100 @@
     wq_others += [line.swap(block, at) for block, at in zip(wq_moved[1:], planes[1:])]
     wq_others += [line.swap(block) for block in wq_last[:1]]
     kv_all = everywhere(kv_own).reshape(images, 2 * local_cols)
-    kv_all, live_here, wo_pair, live_flat, *staged = gate(
-        (kv_all, live_here, wo_pair, live_flat, *wo_two, *wq_last, *wq_others)
+    early = range(2 if relayed else 1 + n_moved)
+    query_part = call(
+        functools.partial(query_kernel, line, relayed, early),
+        place,
+        (text_flat, query_weight, *wq_moved[: len(early) - 1], *wq_others[: len(early)]),
+        [shape((rows, local_cols), F32)],
+        (),
+        rows * width * local_cols,
+    )
+    kv_all, query_part, live_here, wo_pair, live_flat, *staged = gate(
+        (kv_all, query_part, live_here, wo_pair, live_flat, *wo_two, *wq_last, *wq_others)
     )
     wo_two, staged = staged[: len(wo_two)], staged[len(wo_two) :]
     wq_last, wq_others = staged[: len(wq_last)], staged[len(wq_last) :]
 
     wo_last = line.third(wo_two)
+    by_y = tensor_swap(live_here, 2)
+    live_pieces = [live_here, tensor_swap(live_here, 1), by_y, tensor_swap(by_y, 1)]
+    wq_others += [line.swap(block, (0, 3)) for block in wq_last[1:]]
+    half = shape((rows, half_cols), F32)
+    wo_early = [wo_pair, *wo_moved]
+    grad_parts = call(
+        functools.partial(grad_kernel, line, range(len(wo_early)), 0),
+        place,
+        (live_flat, *live_pieces, *wo_early),
+        [half] * 2,
+        (),
+        rows * width * local_cols,
+    )
+
+    arrivals = [query_weight, *wq_moved, *wq_last]
+    late = range(len(early), len(arrivals))
+
+    wo_late = range(len(wo_early), len(wo_early) + len(wo_last))
+    grad_keep, grad_send = call(
+        functools.partial(grad_kernel, line, wo_late, 2),
+        place,
+        (live_flat, *live_pieces, *grad_parts, *wo_last),
+        [shape((rows, half_cols), BF16)] * 2,
+        [pltpu.VMEM((rows, half_cols), F32)] * 2,
+        rows * width * local_cols,
+    )
+    text_flat, grad_keep, grad_send = gate((text_flat, grad_keep, grad_send))
+    grad_come = line.swap(grad_send)
+    queries, attended = call(
+        functools.partial(forward_kernel, line, relayed, late, image_own),
+        place,
+        (text_flat, kv_all, query_part, *arrivals[len(early) :], *wq_others[len(early) :]),
+        [shape((rows, local_cols), BF16)] * 2,
+        [pltpu.VMEM((rows, local_cols), F32)],
+        rows * width * local_cols,
+    )
+    wq_blocks = [*arrivals, *wq_others]
+
+    att_next = [line.shift(attended, m) for m in (1, line.n_z - 1)]
+    attended, grad_come = gate((attended, grad_come))
+    att_swapped = line.swap(attended)
+
+    query_grad, kv_part = call(
+        functools.partial(backward_kernel, image_own),
+        place,
+        (queries, kv_all, grad_keep, grad_come),
+        [shape((rows, local_cols), BF16), shape((images, 2 * local_cols), F32)],
+        (),
+        10 * images * rows * local_cols,
+    )
+    chunk = n_dp // n_tensor
+    term = call(
+        functools.partial(term_kernel, line, relayed),
+        place,
+        (query_grad, *wq_blocks),
+        [shape((n_tensor, chunk, rows, own_width), BF16)],
+        (),
+        2 * rows * width * local_cols,
+    )
+    term, live_flat = gate((term, live_flat))
     quarter_rows = rows // 4
     live_rows = lax.dynamic_slice_in_dim(live_flat, quarter * quarter_rows, quarter_rows, 0)
     live_mine = lax.all_to_all(
         live_rows.reshape(quarter_rows, n_dp, own_width), "dp", split_axis=1, concat_axis=0
     )
     live_mine = live_mine.reshape(n_dp, quarter_rows, own_width)
-    by_y = tensor_swap(live_here, 2)
-    live_pieces = [live_here, tensor_swap(live_here, 1), by_y, tensor_swap(by_y, 1)]
-    wq_others += [line.swap(block, (0, 3)) for block in wq_last[1:]]
-    arrivals = [query_weight, *wq_moved, *wq_last]
-    early = range(4 if relayed else len(arrivals))
-    late = range(len(early), len(arrivals))
-    query_part = call(
-        functools.partial(query_kernel, line, relayed, early),
-        place,
-        (text_flat, *arrivals[: len(early)], *wq_others[: len(early)]),
-        [shape((rows, local_cols), F32)],
-        (),
-        2 * rows * width * local_cols,
-    )
-
-    half = shape((rows, half_cols), F32)
-    wo_early = [wo_pair, *wo_moved]
-    grad_parts = call(
-        functools.partial(grad_kernel, line, range(len(wo_early)), 0),
-        place,
-        (live_flat, *live_pieces, *wo_early),
-        [half] * 2,
-        (),
-        rows * width * local_cols,
-    )
-
-    query_part, *grad_parts = gate((query_part, *grad_parts))
-
-    wo_late = range(len(wo_early), len(wo_early) + len(wo_last))
-    grad_keep, grad_send = call(
-        functools.partial(grad_kernel, line, wo_late, 2),
-        place,
-        (live_flat, *live_pieces, *grad_parts, *wo_last),
-        [shape((rows, half_cols), BF16)] * 2,
-        [pltpu.VMEM((rows, half_cols), F32)] * 2,
-        rows * width * local_cols,
-    )
-    text_flat, live_mine, grad_keep, grad_send = gate(
-        (text_flat, live_mine, grad_keep, grad_send)
-    )
-    grad_come = line.swap(grad_send)
-    queries, attended = call(
-        functools.partial(forward_kernel, line, relayed, late, image_own),
-        place,
-        (text_flat, kv_all, query_part, *arrivals[len(early) :], *wq_others[len(early) :]),
-        [shape((rows, local_cols), BF16)] * 2,
-        [pltpu.VMEM((rows, local_cols), F32)],
-        rows * width * local_cols,
-    )
-    wq_blocks = [*arrivals, *wq_others]
-
-    att_next = [line.shift(attended, m) for m in (1, line.n_z - 1)]
-    attended, grad_come = gate((attended, grad_come))
-    att_swapped = line.swap(attended)
-    live_y = tensor_swap(live_mine, 2)
-
-    query_grad, kv_part = call(
-        functools.partial(backward_kernel, image_own),
-        place,
-        (queries, kv_all, grad_keep, grad_come),
-        [shape((rows, local_cols), BF16), shape((images, 2 * local_cols), F32)],
-        (),
-        10 * images * rows * local_cols,
-    )
-    chunk = n_dp // n_tensor
-    term = call(
-        functools.partial(term_kernel, line, relayed),
-        place,
-        (query_grad, *wq_blocks),
-        [shape((n_tensor, chunk, rows, own_width), BF16)],
-        (),
-        2 * rows * width * local_cols,
-    )
-    kv_part, term, live_y, attended, att_swapped, *att_next = gate(
-        (kv_part, term, live_y, attended, att_swapped, *att_next)
+    kv_part, term, attended, att_swapped, *att_next = gate(
+        (kv_part, term, attended, att_swapped, *att_next)
     )
 
     kv_part = kv_part.reshape(n_dp, image_rows, 2 * local_cols)
     kv_grad = jnp.sum(lax.all_to_all(kv_part, "dp", split_axis=0, concat_axis=0), axis=0)
-    kv_grad_all = everywhere(kv_grad.astype(BF16)).reshape(images, 2 * local_cols)
+    kv_grad, live_mine = gate((kv_grad.astype(BF16), live_mine))
+    kv_grad_all = everywhere(kv_grad).reshape(images, 2 * local_cols)
     text_parts = [tensor_swap(term[k], k) for k in range(2, n_tensor)]
     att_far = [line.shift(attended, m) for m in range(2, line.n_z - 1)]
     att_other_next = [line.swap(block) for block in att_next]
-    live_pair = jnp.stack([live_mine, live_y])
+    live_pair = jnp.stack([live_mine, tensor_swap(live_mine, 2)])
     kv_grad_all, term, live_pair, *staged = gate(
         (kv_grad_all, term, live_pair, *att_other_next, *text_parts, *att_far)
     )

time: 301 us -> 319 us (1.060)
  waiting for transfers between devices: 123 us -> 149 us
  starting transfers between devices: 98.5 us -> 92.3 us
    ppermute x8, waiting for transfers between devices: 0.02 us -> 23.7 us  [tensor_swap(): lax.ppermute(block, 'tensor', [(t, t ^ bit) for t in range(n_tensor)])]
    all_to_all x1, waiting for transfers between devices: 0.01 us -> 12.2 us  [shards(): lax.all_to_all(live_rows.reshape(quarter_rows, n_dp, own_width), 'dp', sp...]
    all_to_all x1, waiting for transfers between devices: 17.9 us -> 10.6 us  [shards(): lax.all_to_all(kv_part, 'dp', split_axis=0, concat_axis=0)]
    all_to_all x2, waiting for transfers between devices: 32.8 us -> 27.4 us  [everywhere(): return lax.all_to_all(copies, 'dp', split_axis=0, concat_axis=0)]
    all_to_all x1, starting transfers between devices: 8.06 us -> 4.15 us  [shards(): lax.all_to_all(live_rows.reshape(quarter_rows, n_dp, own_width), 'dp', sp...]
    ppermute x13, waiting for transfers between devices: 15.4 us -> 19.3 us  [move(): return lax.ppermute(block, 'dp', pairs)]
  transfers between devices with their start and end apart: 42 -> 42, of which waited for: 13 -> 18; matrix products, arithmetic and copies ran while one was open for 8% -> 8% of each run, Pallas kernels for 15% -> 14%
where the time goes in v14:
time: 319 us; the launch traced here: 317 us
  waiting for transfers between devices  149 us (47%)
  starting transfers between devices  92.3 us (29%)
  Pallas kernels  45.7 us (14%)
  other arithmetic  13.3 us (4%)
  local copies, waits for them, and re-layouts  12.3 us (4%)
  matrix products  3.34 us (1%)
    pallas_call x8, Pallas kernels, call(): pl.pallas_call(kernel, out_shape=outs[0] if single else outs, in_specs=[p...  45.7 us
    all_to_all x1, waiting for transfers between devices, shards(): lax.all_to_all(part_kv, 'dp', split_axis=0, concat_axis=0)  29.5 us
    ppermute x13, starting transfers between devices, move(): return lax.ppermute(block, 'dp', pairs)  27.6 us
    all_to_all x2, waiting for transfers between devices, everywhere(): return lax.all_to_all(copies, 'dp', split_axis=0, concat_axis=0)  27.4 us
    ppermute x8, waiting for transfers between devices, tensor_swap(): lax.ppermute(block, 'tensor', [(t, t ^ bit) for t in range(n_tensor)])  23.7 us
    ppermute x13, waiting for transfers between devices, move(): return lax.ppermute(block, 'dp', pairs)  19.3 us
    ppermute x12, starting transfers between devices, swap(): return lax.ppermute(block, 'dp', pairs)  17.7 us
    ppermute x12, waiting for transfers between devices, swap(): return lax.ppermute(block, 'dp', pairs)  16.2 us
  transfers between devices with their start and end apart: 42, of which 18 were waited for; matrix products, arithmetic and copies ran while one was open for 8% of the time, Pallas kernels for 14%

profile of v14, /device:TPU:4, one launch (start us, length us, event | category | flops | bytes accessed | tf_op | source)
XLA Modules:
  0.0 316.9 jit_solution(234609563517954810)
XLA Ops:
  2.1 5.6 %collective-permute-start.3 = (bf16[512,1024]{1,0:T(8,128)(2,1)}, bf16[512,1024]{1,0:T(8,128)(2,1)}, u32[]{:S(2)}, u32[]{:S(2)}) collective-permute-start(bf16[512,1024]{1,0:T(8,128)(2,1)} %refs_0_.1), channel_id=1, source_target_pairs={{0,8},{4,12},{8,16},{12,20},{16,24},{20,28},{1,9},{5,13},{9,17},{1... | collective-permute-start | bytes 3145736 | tf_op jit(solution)/shard_map/ppermute | solution.py:31
  7.6 2.3 constant_dynamic-slice_fusion.3
  11.5 1.8 broadcast_select_fusion
  15.5 4.8 %all-to-all-start = ((bf16[8,8,512]{2,0,1:T(8,128)(2,1)}), bf16[8,8,512]{2,0,1:T(8,128)(2,1)S(1)}, u32[]{:S(2)}, u32[]{:S(2)}) async-start(bf16[8,8,512]{2,0,1:T(8,128)(2,1)} %copy.14), calls=%async_computation | async-start | bytes 131072 | tf_op jit(solution)/shard_map/all_to_all | solution.py:313
  20.3 4.8 %collective-permute-done = bf16[512,512]{1,0:T(8,128)(2,1)} collective-permute-done((bf16[512,512]{1,0:T(8,128)(2,1)}, bf16[512,512]{1,0:T(8,128)(2,1)}, u32[]{:S(2)}, u32[]{:S(2)}) %collective-permute-start) | collective-permute-done | bytes 524320 | tf_op jit(solution)/shard_map/ppermute | solution.py:36
  25.1 2.3 pad_maximum_fusion.refs_0_
  27.4 7.8 %all-to-all-done = bf16[8,8,512]{2,0,1:T(8,128)(2,1)S(1)} async-done(((bf16[8,8,512]{2,0,1:T(8,128)(2,1)}), bf16[8,8,512]{2,0,1:T(8,128)(2,1)S(1)}, u32[]{:S(2)}, u32[]{:S(2)}) %all-to-all-start) | async-done | bytes 65568 | tf_op jit(solution)/shard_map/all_to_all | solution.py:313
  35.2 1.6 collective-permute-start.4
  38.0 5.6 %collective-permute-start.9 = (bf16[512,1024]{1,0:T(8,128)(2,1)}, bf16[512,1024]{1,0:T(8,128)(2,1)}, u32[]{:S(2)}, u32[]{:S(2)}) collective-permute-start(bf16[512,1024]{1,0:T(8,128)(2,1)} %pad_maximum_fusion.refs_0_), channel_id=1, source_target_pairs={{0,8},{4,12},{8,16},{12,20},{16,24},{20,28},{1,9},{5,13},{9,17},{1... | collective-permute-start | bytes 3145736 | tf_op jit(solution)/shard_map/ppermute | solution.py:31
  44.9 1.6 collective-permute-start.7
  48.4 10.6 %collective-permute-done.4.refs_2_.refs_5_ = bf16[512,1024]{1,0:T(8,128)(2,1)} collective-permute-done((bf16[512,1024]{1,0:T(8,128)(2,1)}, bf16[512,1024]{1,0:T(8,128)(2,1)}, u32[]{:S(2)}, u32[]{:S(2)}) %collective-permute-start.4) | collective-permute-done | bytes 1048608 | tf_op jit(solution)/shard_map/ppermute | solution.py:36
  59.1 3.4 %collective-permute-start.5 = (bf16[512,1024]{1,0:T(8,128)(2,1)}, bf16[512,1024]{1,0:T(8,128)(2,1)S(1)}, u32[]{:S(2)}, u32[]{:S(2)}) collective-permute-start(bf16[512,1024]{1,0:T(8,128)(2,1)} %collective-permute-done.2.refs_1_), channel_id=1, source_target_pairs={{0,4},{4,0},{8,12},{12,8},{16,20},{20,16},{1,5},{5,1},{9,13},{13,9... | collective-permute-start | bytes 3145736 | tf_op jit(solution)/shard_map/ppermute | solution.py:36
  63.3 3.9 %all-to-all-start.1 = ((f32[8,8,2048]{2,1,0:T(8,128)}), f32[8,8,2048]{2,1,0:T(8,128)S(1)}, u32[]{:S(2)}, u32[]{:S(2)}) async-start(f32[8,8,2048]{2,1,0:T(8,128)} %maximum_bitcast_fusion), calls=%async_computation.1 | async-start | bytes 1048576 | tf_op jit(solution)/shard_map/all_to_all | solution.py:334
  67.2 29.5 %all-to-all-done.1 = f32[8,8,2048]{2,1,0:T(8,128)S(1)} async-done(((f32[8,8,2048]{2,1,0:T(8,128)}), f32[8,8,2048]{2,1,0:T(8,128)S(1)}, u32[]{:S(2)}, u32[]{:S(2)}) %all-to-all-start.1) | async-done | bytes 524320 | tf_op jit(solution)/shard_map/all_to_all | solution.py:334
  102.5 1.7 collective-permute-start.11
  104.1 1.6 collective-permute-start.13
  106.5 11.6 %all-to-all-start.2 = ((bf16[8,8,2048]{2,1,0:T(8,128)(2,1)}), bf16[8,8,2048]{2,1,0:T(8,128)(2,1)S(1)}, u32[]{:S(2)}, u32[]{:S(2)}) async-start(bf16[8,8,2048]{2,1,0:T(8,128)(2,1)} %broadcast_in_dim.16), calls=%async_computation.2 | async-start | bytes 524288 | tf_op jit(solution)/shard_map/all_to_all | solution.py:343
  118.7 5.4 %shard_map.103.part = f32[256,1024]{1,0:T(8,128)} custom-call(s32[4]{0:T(128)} %pad_add_fusion.place, bf16[256,4096]{1,0:T(8,128)(2,1)} %bitcast.42, bf16[512,1024]{1,0:T(8,128)(2,1)} %refs_0_.1, bf16[512,1024]{1,0:T(8,128)(2,1)} %collective-permute-done.2.refs_1_, bf16[512,1024]{1,0:T(8,128)(2,1)} %collective-permute-done.4.refs_2_.refs_5_, ...), custom_call_target="tpu_custom_call" | custom-call | flops 1073741824 | bytes 7340032 | tf_op jit(solution)/shard_map/pallas_call | solution.py:228
  124.1 26.1 %all-to-all-done.2 = bf16[8,8,2048]{2,1,0:T(8,128)(2,1)S(1)} async-done(((bf16[8,8,2048]{2,1,0:T(8,128)(2,1)}), bf16[8,8,2048]{2,1,0:T(8,128)(2,1)S(1)}, u32[]{:S(2)}, u32[]{:S(2)}) %all-to-all-start.2) | async-done | bytes 262176 | tf_op jit(solution)/shard_map/all_to_all | solution.py:343
  150.8 2.3 broadcast_select_fusion.1.refs_2_
  154.4 3.0 collective-permute-start.19
  157.6 3.5 %collective-permute-done.16.by_y = bf16[256,1024]{1,0:T(8,128)(2,1)S(1)} collective-permute-done((bf16[256,1024]{1,0:T(8,128)(2,1)}, bf16[256,1024]{1,0:T(8,128)(2,1)S(1)}, u32[]{:S(2)}, u32[]{:S(2)}) %collective-permute-start.16) | collective-permute-done | bytes 524320 | tf_op jit(solution)/shard_map/ppermute | solution.py:300
  161.1 2.0 collective-permute-done.17.by_both
  163.1 5.8 %shard_map.104 = (f32[256,512]{1,0:T(8,128)}, f32[256,512]{1,0:T(8,128)}) custom-call(s32[4]{0:T(128)} %pad_add_fusion.place, bf16[256,4096]{1,0:T(8,128)(2,1)} %bitcast.39, bf16[256,1024]{1,0:T(8,128)(2,1)} %collective-permute-done.1.mine, bf16[256,1024]{1,0:T(8,128)(2,1)} %collective-permute-done.15.by_core, bf16[256,1024]{1,0:T(8,128)(2,1)} %copy-done.9, ...), custom_call_target="tpu_custom_call" | custom-call | flops 1073741824 | bytes 8388608 | tf_op jit(solution)/shard_map/pallas_call | solution.py:228
  168.9 8.0 %collective-permute-done.18.refs_3_ = bf16[512,1024]{1,0:T(8,128)(2,1)} collective-permute-done((bf16[512,1024]{1,0:T(8,128)(2,1)}, bf16[512,1024]{1,0:T(8,128)(2,1)}, u32[]{:S(2)}, u32[]{:S(2)}) %collective-permute-start.18) | collective-permute-done | bytes 1048608 | tf_op jit(solution)/shard_map/ppermute | solution.py:31
  177.0 5.7 %shard_map.105 = (bf16[256,512]{1,0:T(8,128)(2,1)}, bf16[256,512]{1,0:T(8,128)(2,1)}) custom-call(s32[4]{0:T(128)} %pad_add_fusion.place, bf16[256,4096]{1,0:T(8,128)(2,1)} %bitcast.40, bf16[256,1024]{1,0:T(8,128)(2,1)} %collective-permute-done.1.mine, bf16[256,1024]{1,0:T(8,128)(2,1)} %collective-permute-done.15.by_core, bf16[256,1024]{1,0:T(8,128)(2,1)} %copy-done.9, ...), custom_call_target="tpu_custom_call" | custom-call | flops 1073741824 | bytes 7864320 | tf_op jit(solution)/shard_map/pallas_call | solution.py:228
  184.1 7.2 %shard_map.106 = (bf16[256,1024]{1,0:T(8,128)(2,1)}, bf16[256,1024]{1,0:T(8,128)(2,1)}) custom-call(s32[4]{0:T(128)} %pad_add_fusion.place, bf16[256,4096]{1,0:T(8,128)(2,1)} %bitcast.43, bf16[64,2048]{1,0:T(8,128)(2,1)} %bitcast.44, f32[256,1024]{1,0:T(8,128)} %shard_map.103.part, bf16[512,1024]{1,0:T(8,128)(2,1)} %collective-permute-done.3.refs_0_.refs_2_, ...), custom_call_target="tpu_custom_call" | custom-call | flops 1073741824 | bytes 10747904 | tf_op jit(solution)/shard_map/pallas_call | solution.py:228
  191.2 4.4 %collective-permute-start.22 = (bf16[256,1024]{1,0:T(8,128)(2,1)}, bf16[256,1024]{1,0:T(8,128)(2,1)}, u32[]{:S(2)}, u32[]{:S(2)}) collective-permute-start(bf16[256,1024]{1,0:T(8,128)(2,1)} %get-tuple-element.121.refs_2_), channel_id=1, source_target_pairs={{8,0},{12,4},{16,8},{20,12},{24,16},{28,20},{0,24},{4,28},{9,1},{1... | collective-permute-start | bytes 1572872 | tf_op jit(solution)/shard_map/ppermute | solution.py:31
  195.7 1.7 collective-permute-start.21
  197.4 3.6 %shard_map.107 = (bf16[256,1024]{1,0:T(8,128)(2,1)}, f32[64,2048]{1,0:T(8,128)}) custom-call(s32[4]{0:T(128)} %pad_add_fusion.place, bf16[256,1024]{1,0:T(8,128)(2,1)} %get-tuple-element.103.query, bf16[64,2048]{1,0:T(8,128)(2,1)} %bitcast.45, bf16[256,512]{1,0:T(8,128)(2,1)} %get-tuple-element.104.keep, bf16[256,512]{1,0:T(8,128)(2,1)} %copy-done.11), custom_call_target="tpu_custom_call" | custom-call | flops 167772160 | bytes 2359296 | tf_op jit(solution)/shard_map/pallas_call | solution.py:228
  201.0 8.9 %shard_map.108.term = bf16[4,2,256,512]{3,2,1,0:T(8,128)(2,1)} custom-call(s32[4]{0:T(128)} %pad_add_fusion.place, bf16[256,1024]{1,0:T(8,128)(2,1)} %get-tuple-element.109.query_grad, bf16[512,1024]{1,0:T(8,128)(2,1)} %refs_0_.1, bf16[512,1024]{1,0:T(8,128)(2,1)} %collective-permute-done.2.refs_1_, ...), custom_call_target="tpu_custom_call" | custom-call | flops 2147483648 | bytes 13107200 | tf_op jit(solution)/shard_map/pallas_call | solution.py:228
  209.9 4.2 %collective-permute-done.23.refs_5_ = bf16[256,1024]{1,0:T(8,128)(2,1)} collective-permute-done((bf16[256,1024]{1,0:T(8,128)(2,1)}, bf16[256,1024]{1,0:T(8,128)(2,1)}, u32[]{:S(2)}, u32[]{:S(2)}) %collective-permute-start.23) | collective-permute-done | bytes 524320 | tf_op jit(solution)/shard_map/ppermute | solution.py:31
  214.1 4.2 %all-to-all-start.3 = ((f32[8,8,2048]{2,1,0:T(8,128)}), f32[8,8,2048]{2,1,0:T(8,128)}, u32[]{:S(2)}, u32[]{:S(2)}) async-start(f32[8,8,2048]{2,1,0:T(8,128)} %bitcast.10), calls=%async_computation.3 | async-start | bytes 1048576 | tf_op jit(solution)/shard_map/all_to_all | solution.py:437
  220.5 10.6 %all-to-all-done.3 = f32[8,8,2048]{2,1,0:T(8,128)} async-done(((f32[8,8,2048]{2,1,0:T(8,128)}), f32[8,8,2048]{2,1,0:T(8,128)}, u32[]{:S(2)}, u32[]{:S(2)}) %all-to-all-start.3) | async-done | bytes 524320 | tf_op jit(solution)/shard_map/all_to_all | solution.py:437
  231.2 4.1 %all-to-all-start.4 = ((bf16[1,64,8,512]{3,1,0,2:T(8,128)(2,1)}), bf16[1,64,8,512]{3,1,0,2:T(8,128)(2,1)}, u32[]{:S(2)}, u32[]{:S(2)}) async-start(bf16[1,64,8,512]{3,1,0,2:T(8,128)(2,1)} %copy.15), calls=%async_computation.4 | async-start | bytes 1048576 | tf_op jit(solution)/shard_map/all_to_all | solution.py:428
  236.4 12.2 %all-to-all-done.4 = bf16[1,64,8,512]{3,1,0,2:T(8,128)(2,1)} async-done(((bf16[1,64,8,512]{3,1,0,2:T(8,128)(2,1)}), bf16[1,64,8,512]{3,1,0,2:T(8,128)(2,1)}, u32[]{:S(2)}, u32[]{:S(2)}) %all-to-all-start.4) | async-done | bytes 524320 | tf_op jit(solution)/shard_map/all_to_all | solution.py:428
  253.7 10.1 %collective-permute-done.24 = bf16[8,64,512]{2,1,0:T(8,128)(2,1)} collective-permute-done((bf16[8,64,512]{2,1,0:T(8,128)(2,1)}, bf16[8,64,512]{2,1,0:T(8,128)(2,1)}, u32[]{:S(2)}, u32[]{:S(2)}) %collective-permute-start.24) | collective-permute-done | bytes 524320 | tf_op jit(solution)/shard_map/ppermute | solution.py:300
  265.3 4.3 %all-to-all-start.5 = ((bf16[8,8,2048]{2,1,0:T(8,128)(2,1)}), bf16[8,8,2048]{2,1,0:T(8,128)(2,1)S(1)}, u32[]{:S(2)}, u32[]{:S(2)}) async-start(bf16[8,8,2048]{2,1,0:T(8,128)(2,1)} %broadcast_in_dim.17), calls=%async_computation.5 | async-start | bytes 524288 | tf_op jit(solution)/shard_map/all_to_all | solution.py:343
  269.6 2.3 pad_maximum_fusion.1.refs_0_
  271.9 3.1 collective-permute-done.27.refs_0_
  275.0 5.0 %collective-permute-done.28.refs_1_ = bf16[2,256,512]{2,1,0:T(8,128)(2,1)} collective-permute-done((bf16[2,256,512]{2,1,0:T(8,128)(2,1)}, bf16[2,256,512]{2,1,0:T(8,128)(2,1)}, u32[]{:S(2)}, u32[]{:S(2)}) %collective-permute-start.28) | collective-permute-done | bytes 524320 | tf_op jit(solution)/shard_map/ppermute | solution.py:300
  280.0 7.1 %collective-permute-done.29.refs_4_ = bf16[256,1024]{1,0:T(8,128)(2,1)} collective-permute-done((bf16[256,1024]{1,0:T(8,128)(2,1)}, bf16[256,1024]{1,0:T(8,128)(2,1)}, u32[]{:S(2)}, u32[]{:S(2)}) %collective-permute-start.29) | collective-permute-done | bytes 524320 | tf_op jit(solution)/shard_map/ppermute | solution.py:31
  292.3 4.5 %all-to-all-start.6 = ((bf16[4,16,512]{2,1,0:T(8,128)(2,1)}), bf16[4,16,512]{2,1,0:T(8,128)(2,1)S(1)}, u32[]{:S(2)}, u32[]{:S(2)}) async-start(bf16[4,16,512]{2,1,0:T(8,128)(2,1)} %bitcast.19), calls=%async_computation.6 | async-start | bytes 131072 | tf_op jit(solution)/shard_map/all_to_all | solution.py:250
  296.8 2.3 all-to-all-done.6
  299.9 3.0 shard_map.109
  303.7 4.0 %collective-permute-start.33 = (bf16[8,512]{1,0:T(8,128)(2,1)S(1)}, bf16[8,512]{1,0:T(8,128)(2,1)S(1)}, u32[]{:S(2)}, u32[]{:S(2)}) collective-permute-start(bf16[8,512]{1,0:T(8,128)(2,1)S(1)} %get-tuple-element.139), channel_id=1, source_target_pairs={{0,0},{1,8},{2,16},{3,24},{4,4},{5,12},{6,20},{7,28},{8,1},{9,9},{... | collective-permute-start | bytes 24584 | tf_op jit(solution)/shard_map/ppermute | solution.py:266
  307.7 2.4 collective-permute-start.34
  310.1 6.2 %shard_map.110 = bf16[1024,512]{1,0:T(8,128)(2,1)} custom-call(s32[4]{0:T(128)} %pad_add_fusion.place, bf16[2,8,64,512]{3,2,1,0:T(8,128)(2,1)} %pad_maximum_fusion.1.refs_0_, bf16[2,8,64,512]{3,2,1,0:T(8,128)(2,1)} %collective-permute-done.30.refs_1_, bf16[256,1024]{1,0:T(8,128)(2,1)} %get-tuple-element.121.refs_2_, ...), custom_call_target="tpu_custom_call" | custom-call | flops 2147483648 | bytes 7340032 | tf_op jit(solution)/shard_map/pallas_call | solution.py:228
  (105 shorter events, 38.2 us)
Async XLA Ops:
  0.6 47.5 %copy-start = (bf16[512,1024]{1,0:T(8,128)(2,1)S(1)}, bf16[512,1024]{1,0:T(8,128)(2,1)}, u32[]{:S(2)}) copy-start(bf16[512,1024]{1,0:T(8,128)(2,1)} %param.14) | copy-start | bytes 3145732
  0.7 34.5 %collective-permute-start.2 = (bf16[512,1024]{1,0:T(8,128)(2,1)}, bf16[512,1024]{1,0:T(8,128)(2,1)}, u32[]{:S(2)}, u32[]{:S(2)}) collective-permute-start(bf16[512,1024]{1,0:T(8,128)(2,1)} %refs_0_.1), channel_id=1, source_target_pairs={{8,0},{12,4},{16,8},{20,12},{24,16},{28,20},{9,1},{13,5},{17,9},{2... | collective-permute-start | bytes 3145736 | tf_op jit(solution)/shard_map/ppermute | solution.py:31
  2.1 33.1 %collective-permute-start.3 = (bf16[512,1024]{1,0:T(8,128)(2,1)}, bf16[512,1024]{1,0:T(8,128)(2,1)}, u32[]{:S(2)}, u32[]{:S(2)}) collective-permute-start(bf16[512,1024]{1,0:T(8,128)(2,1)} %refs_0_.1), channel_id=1, source_target_pairs={{0,8},{4,12},{8,16},{12,20},{16,24},{20,28},{1,9},{5,13},{9,17},{1... | collective-permute-start | bytes 3145736 | tf_op jit(solution)/shard_map/ppermute | solution.py:31
  9.9 15.2 %collective-permute-start = (bf16[512,512]{1,0:T(8,128)(2,1)}, bf16[512,512]{1,0:T(8,128)(2,1)}, u32[]{:S(2)}, u32[]{:S(2)}) collective-permute-start(bf16[512,512]{1,0:T(8,128)(2,1)} %get-tuple-element.138), channel_id=1, source_target_pairs={{0,4},{4,0},{8,12},{12,8},{16,20},{20,16},{24,28},{28,24},{1,5},{5... | collective-permute-start | bytes 1572872 | tf_op jit(solution)/shard_map/ppermute | solution.py:36
  13.3 34.8 %copy-start.1 = (bf16[2,128,4096]{2,1,0:T(8,128)(2,1)}, bf16[2,128,4096]{2,1,0:T(8,128)(2,1)S(1)}, u32[]{:S(2)}) copy-start(bf16[2,128,4096]{2,1,0:T(8,128)(2,1)S(1)} %broadcast_select_fusion) | copy-start | bytes 6291460
  14.3 20.9 %collective-permute-start.1 = (bf16[256,1024]{1,0:T(8,128)(2,1)}, bf16[256,1024]{1,0:T(8,128)(2,1)}, u32[]{:S(2)}, u32[]{:S(2)}) collective-permute-start(bf16[256,1024]{1,0:T(8,128)(2,1)} %constant_dynamic-slice_fusion.1), channel_id=1, source_target_pairs={{0,4},{4,0},{8,12},{12,8},{16,20},{20,16},{24,28},{28,24},{1,5},{5... | collective-permute-start | bytes 1572872 | tf_op jit(solution)/shard_map/ppermute | solution.py:36
  15.5 19.7 %all-to-all-start = ((bf16[8,8,512]{2,0,1:T(8,128)(2,1)}), bf16[8,8,512]{2,0,1:T(8,128)(2,1)S(1)}, u32[]{:S(2)}, u32[]{:S(2)}) async-start(bf16[8,8,512]{2,0,1:T(8,128)(2,1)} %copy.14), calls=%async_computation | async-start | bytes 131072 | tf_op jit(solution)/shard_map/all_to_all | solution.py:313
  35.2 23.9 %collective-permute-start.4 = (bf16[512,1024]{1,0:T(8,128)(2,1)}, bf16[512,1024]{1,0:T(8,128)(2,1)}, u32[]{:S(2)}, u32[]{:S(2)}) collective-permute-start(bf16[512,1024]{1,0:T(8,128)(2,1)} %refs_0_.1), channel_id=1, source_target_pairs={{0,4},{4,0},{8,12},{12,8},{16,20},{20,16},{24,28},{28,24},{1,5},{5... | collective-permute-start | bytes 3145736 | tf_op jit(solution)/shard_map/ppermute | solution.py:36
  36.7 60.0 %collective-permute-start.8 = (bf16[512,1024]{1,0:T(8,128)(2,1)}, bf16[512,1024]{1,0:T(8,128)(2,1)}, u32[]{:S(2)}, u32[]{:S(2)}) collective-permute-start(bf16[512,1024]{1,0:T(8,128)(2,1)} %pad_maximum_fusion.refs_0_), channel_id=1, source_target_pairs={{8,0},{12,4},{16,8},{20,12},{24,16},{28,20},{9,1},{13,5},{17,9},{2... | collective-permute-start | bytes 3145736 | tf_op jit(solution)/shard_map/ppermute | solution.py:31
  38.0 58.7 %collective-permute-start.9 = (bf16[512,1024]{1,0:T(8,128)(2,1)}, bf16[512,1024]{1,0:T(8,128)(2,1)}, u32[]{:S(2)}, u32[]{:S(2)}) collective-permute-start(bf16[512,1024]{1,0:T(8,128)(2,1)} %pad_maximum_fusion.refs_0_), channel_id=1, source_target_pairs={{0,8},{4,12},{8,16},{12,20},{16,24},{20,28},{1,9},{5,13},{9,17},{1... | collective-permute-start | bytes 3145736 | tf_op jit(solution)/shard_map/ppermute | solution.py:31
  43.6 53.0 %collective-permute-start.6 = (bf16[512,1024]{1,0:T(8,128)(2,1)}, bf16[512,1024]{1,0:T(8,128)(2,1)}, u32[]{:S(2)}, u32[]{:S(2)}) collective-permute-start(bf16[512,1024]{1,0:T(8,128)(2,1)} %collective-permute-done.2.refs_1_), channel_id=1, source_target_pairs={{8,0},{12,4},{16,8},{20,12},{9,1},{13,5},{17,9},{21,13},{10,2},{14... | collective-permute-start | bytes 3145736 | tf_op jit(solution)/shard_map/ppermute | solution.py:31
  44.9 51.8 %collective-permute-start.7 = (bf16[512,1024]{1,0:T(8,128)(2,1)}, bf16[512,1024]{1,0:T(8,128)(2,1)}, u32[]{:S(2)}, u32[]{:S(2)}) collective-permute-start(bf16[512,1024]{1,0:T(8,128)(2,1)} %collective-permute-done.3.refs_0_.refs_2_), channel_id=1, source_target_pairs={{8,16},{12,20},{16,24},{20,28},{9,17},{13,21},{17,25},{21,29},{10,... | collective-permute-start | bytes 3145736 | tf_op jit(solution)/shard_map/ppermute | solution.py:31
  59.1 37.7 %collective-permute-start.5 = (bf16[512,1024]{1,0:T(8,128)(2,1)}, bf16[512,1024]{1,0:T(8,128)(2,1)S(1)}, u32[]{:S(2)}, u32[]{:S(2)}) collective-permute-start(bf16[512,1024]{1,0:T(8,128)(2,1)} %collective-permute-done.2.refs_1_), channel_id=1, source_target_pairs={{0,4},{4,0},{8,12},{12,8},{16,20},{20,16},{1,5},{5,1},{9,13},{13,9... | collective-permute-start | bytes 3145736 | tf_op jit(solution)/shard_map/ppermute | solution.py:36
  63.3 33.4 %all-to-all-start.1 = ((f32[8,8,2048]{2,1,0:T(8,128)}), f32[8,8,2048]{2,1,0:T(8,128)S(1)}, u32[]{:S(2)}, u32[]{:S(2)}) async-start(f32[8,8,2048]{2,1,0:T(8,128)} %maximum_bitcast_fusion), calls=%async_computation.1 | async-start | bytes 1048576 | tf_op jit(solution)/shard_map/all_to_all | solution.py:334
  99.0 25.0 %copy-start.3 = (bf16[512,1024]{1,0:T(8,128)(2,1)}, bf16[512,1024]{1,0:T(8,128)(2,1)S(1)}, u32[]{:S(2)}) copy-start(bf16[512,1024]{1,0:T(8,128)(2,1)S(1)} %broadcast_select_fusion.2.refs_1_.refs_3_) | copy-start | bytes 3145732
  99.1 51.2 %collective-permute-start.12 = (bf16[512,1024]{1,0:T(8,128)(2,1)S(1)}, bf16[512,1024]{1,0:T(8,128)(2,1)S(1)}, u32[]{:S(2)}, u32[]{:S(2)}) collective-permute-start(bf16[512,1024]{1,0:T(8,128)(2,1)S(1)} %broadcast_select_fusion.2.refs_1_.refs_3_), channel_id=1, source_target_pairs={{8,0},{12,4},{16,24},{20,28},{9,1},{13,5},{17,25},{21,29},{10,2},{... | collective-permute-start | bytes 3145736 | tf_op jit(solution)/shard_map/ppermute | solution.py:31
  100.4 49.9 %collective-permute-start.14 = (bf16[512,1024]{1,0:T(8,128)(2,1)S(1)}, bf16[512,1024]{1,0:T(8,128)(2,1)}, u32[]{:S(2)}, u32[]{:S(2)}) collective-permute-start(bf16[512,1024]{1,0:T(8,128)(2,1)S(1)} %broadcast_select_fusion.2.refs_1_.refs_3_), channel_id=1, source_target_pairs={{0,4},{4,0},{8,12},{12,8},{16,20},{20,16},{24,28},{28,24},{1,5},{5... | collective-permute-start | bytes 3145736 | tf_op jit(solution)/shard_map/ppermute | solution.py:36
  101.2 49.0 %collective-permute-start.10 = (bf16[512,1024]{1,0:T(8,128)(2,1)}, bf16[512,1024]{1,0:T(8,128)(2,1)}, u32[]{:S(2)}, u32[]{:S(2)}) collective-permute-start(bf16[512,1024]{1,0:T(8,128)(2,1)} %collective-permute-done.8.refs_1_), channel_id=1, source_target_pairs={{8,0},{12,4},{16,8},{20,12},{9,1},{13,5},{17,9},{21,13},{10,2},{14... | collective-permute-start | bytes 3145736 | tf_op jit(solution)/shard_map/ppermute | solution.py:31
  102.5 47.8 %collective-permute-start.11 = (bf16[512,1024]{1,0:T(8,128)(2,1)}, bf16[512,1024]{1,0:T(8,128)(2,1)}, u32[]{:S(2)}, u32[]{:S(2)}) collective-permute-start(bf16[512,1024]{1,0:T(8,128)(2,1)} %collective-permute-done.9.refs_2_), channel_id=1, source_target_pairs={{8,16},{12,20},{16,24},{20,28},{9,17},{13,21},{17,25},{21,29},{10,... | collective-permute-start | bytes 3145736 | tf_op jit(solution)/shard_map/ppermute | solution.py:31
  104.1 46.1 %collective-permute-start.13 = (bf16[512,1024]{1,0:T(8,128)(2,1)}, bf16[512,1024]{1,0:T(8,128)(2,1)}, u32[]{:S(2)}, u32[]{:S(2)}) collective-permute-start(bf16[512,1024]{1,0:T(8,128)(2,1)} %collective-permute-done.3.refs_0_.refs_2_), channel_id=1, source_target_pairs={{8,12},{12,8},{16,20},{20,16},{24,28},{28,24},{9,13},{13,9},{17,21... | collective-permute-start | bytes 3145736 | tf_op jit(solution)/shard_map/ppermute | solution.py:36
  106.5 43.7 %all-to-all-start.2 = ((bf16[8,8,2048]{2,1,0:T(8,128)(2,1)}), bf16[8,8,2048]{2,1,0:T(8,128)(2,1)S(1)}, u32[]{:S(2)}, u32[]{:S(2)}) async-start(bf16[8,8,2048]{2,1,0:T(8,128)(2,1)} %broadcast_in_dim.16), calls=%async_computation.2 | async-start | bytes 524288 | tf_op jit(solution)/shard_map/all_to_all | solution.py:343
  150.2 18.7 %copy-start.8 = (bf16[8,8,2048]{2,1,0:T(8,128)(2,1)}, bf16[8,8,2048]{2,1,0:T(8,128)(2,1)S(1)}, u32[]{:S(2)}) copy-start(bf16[8,8,2048]{2,1,0:T(8,128)(2,1)S(1)} %all-to-all-done.2) | copy-start | bytes 786436
  150.2 18.7 %copy-start.4 = (bf16[512,1024]{1,0:T(8,128)(2,1)}, bf16[512,1024]{1,0:T(8,128)(2,1)S(1)}, u32[]{:S(2)}) copy-start(bf16[512,1024]{1,0:T(8,128)(2,1)S(1)} %collective-permute-done.12.refs_2_.refs_4_) | copy-start | bytes 3145732
  150.3 10.8 %collective-permute-start.16 = (bf16[256,1024]{1,0:T(8,128)(2,1)}, bf16[256,1024]{1,0:T(8,128)(2,1)S(1)}, u32[]{:S(2)}, u32[]{:S(2)}) collective-permute-start(bf16[256,1024]{1,0:T(8,128)(2,1)} %collective-permute-done.1.mine), channel_id=1, source_target_pairs={{0,2},{1,3},{2,0},{3,1},{4,6},{5,7},{6,4},{7,5},{8,10},{9,11},{10,... | collective-permute-start | bytes 1572872 | tf_op jit(solution)/shard_map/ppermute | solution.py:300
  153.2 23.8 %collective-permute-start.18 = (bf16[512,1024]{1,0:T(8,128)(2,1)}, bf16[512,1024]{1,0:T(8,128)(2,1)}, u32[]{:S(2)}, u32[]{:S(2)}) collective-permute-start(bf16[512,1024]{1,0:T(8,128)(2,1)} %broadcast_select_fusion.1.refs_2_), channel_id=1, source_target_pairs={{8,0},{12,4},{16,24},{20,28},{9,1},{13,5},{17,25},{21,29},{10,2},{... | collective-permute-start | bytes 3145736 | tf_op jit(solution)/shard_map/ppermute | solution.py:31
  154.4 28.5 %collective-permute-start.19 = (bf16[512,1024]{1,0:T(8,128)(2,1)S(1)}, bf16[512,1024]{1,0:T(8,128)(2,1)S(1)}, u32[]{:S(2)}, u32[]{:S(2)}) collective-permute-start(bf16[512,1024]{1,0:T(8,128)(2,1)S(1)} %collective-permute-done.12.refs_2_.refs_4_), channel_id=1, source_target_pairs={{0,4},{4,0},{24,28},{28,24},{1,5},{5,1},{25,29},{29,25},{2,6},{6,2... | collective-permute-start | bytes 3145736 | tf_op jit(solution)/shard_map/ppermute | solution.py:36
  157.5 3.6 %collective-permute-start.15 = (bf16[256,1024]{1,0:T(8,128)(2,1)}, bf16[256,1024]{1,0:T(8,128)(2,1)}, u32[]{:S(2)}, u32[]{:S(2)}) collective-permute-start(bf16[256,1024]{1,0:T(8,128)(2,1)} %collective-permute-done.1.mine), channel_id=1, source_target_pairs={{0,1},{1,0},{2,3},{3,2},{4,5},{5,4},{6,7},{7,6},{8,9},{9,8},{10,11... | collective-permute-start | bytes 1572872 | tf_op jit(solution)/shard_map/ppermute | solution.py:300
  161.1 2.0 collective-permute-start.17
  182.6 13.0 %collective-permute-start.20 = (bf16[256,512]{1,0:T(8,128)(2,1)}, bf16[256,512]{1,0:T(8,128)(2,1)S(1)}, u32[]{:S(2)}, u32[]{:S(2)}) collective-permute-start(bf16[256,512]{1,0:T(8,128)(2,1)} %get-tuple-element.106), channel_id=1, source_target_pairs={{0,4},{4,0},{8,12},{12,8},{16,20},{20,16},{24,28},{28,24},{1,5},{5... | collective-permute-start | bytes 786440 | tf_op jit(solution)/shard_map/ppermute | solution.py:36
  191.2 18.6 %collective-permute-start.22 = (bf16[256,1024]{1,0:T(8,128)(2,1)}, bf16[256,1024]{1,0:T(8,128)(2,1)}, u32[]{:S(2)}, u32[]{:S(2)}) collective-permute-start(bf16[256,1024]{1,0:T(8,128)(2,1)} %get-tuple-element.121.refs_2_), channel_id=1, source_target_pairs={{8,0},{12,4},{16,8},{20,12},{24,16},{28,20},{0,24},{4,28},{9,1},{1... | collective-permute-start | bytes 1572872 | tf_op jit(solution)/shard_map/ppermute | solution.py:31
  195.7 18.4 %collective-permute-start.23 = (bf16[256,1024]{1,0:T(8,128)(2,1)}, bf16[256,1024]{1,0:T(8,128)(2,1)}, u32[]{:S(2)}, u32[]{:S(2)}) collective-permute-start(bf16[256,1024]{1,0:T(8,128)(2,1)} %get-tuple-element.121.refs_2_), channel_id=1, source_target_pairs={{24,0},{28,4},{0,8},{4,12},{8,16},{12,20},{16,24},{20,28},{25,1},{... | collective-permute-start | bytes 1572872 | tf_op jit(solution)/shard_map/ppermute | solution.py:31
  195.7 18.4 %collective-permute-start.21 = (bf16[256,1024]{1,0:T(8,128)(2,1)}, bf16[256,1024]{1,0:T(8,128)(2,1)}, u32[]{:S(2)}, u32[]{:S(2)}) collective-permute-start(bf16[256,1024]{1,0:T(8,128)(2,1)} %get-tuple-element.121.refs_2_), channel_id=1, source_target_pairs={{0,4},{4,0},{8,12},{12,8},{16,20},{20,16},{24,28},{28,24},{1,5},{5... | collective-permute-start | bytes 1572872 | tf_op jit(solution)/shard_map/ppermute | solution.py:36
  214.1 17.1 %all-to-all-start.3 = ((f32[8,8,2048]{2,1,0:T(8,128)}), f32[8,8,2048]{2,1,0:T(8,128)}, u32[]{:S(2)}, u32[]{:S(2)}) async-start(f32[8,8,2048]{2,1,0:T(8,128)} %bitcast.10), calls=%async_computation.3 | async-start | bytes 1048576 | tf_op jit(solution)/shard_map/all_to_all | solution.py:437
  219.4 30.5 %copy-start.2 = (bf16[4,2,256,512]{3,2,1,0:T(8,128)(2,1)S(1)}, bf16[4,2,256,512]{3,2,1,0:T(8,128)(2,1)}, u32[]{:S(2)}) copy-start(bf16[4,2,256,512]{3,2,1,0:T(8,128)(2,1)} %shard_map.108.term) | copy-start | bytes 6291460
  231.2 17.4 %all-to-all-start.4 = ((bf16[1,64,8,512]{3,1,0,2:T(8,128)(2,1)}), bf16[1,64,8,512]{3,1,0,2:T(8,128)(2,1)}, u32[]{:S(2)}, u32[]{:S(2)}) async-start(bf16[1,64,8,512]{3,1,0,2:T(8,128)(2,1)} %copy.15), calls=%async_computation.4 | async-start | bytes 1048576 | tf_op jit(solution)/shard_map/all_to_all | solution.py:428
  248.6 15.2 %collective-permute-start.24 = (bf16[8,64,512]{2,1,0:T(8,128)(2,1)}, bf16[8,64,512]{2,1,0:T(8,128)(2,1)}, u32[]{:S(2)}, u32[]{:S(2)}) collective-permute-start(bf16[8,64,512]{2,1,0:T(8,128)(2,1)} %bitcast.13), channel_id=1, source_target_pairs={{0,2},{1,3},{2,0},{3,1},{4,6},{5,7},{6,4},{7,5},{8,10},{9,11},{10,... | collective-permute-start | bytes 1572872 | tf_op jit(solution)/shard_map/ppermute | solution.py:300
  250.9 24.1 %collective-permute-start.27 = (bf16[2,256,512]{2,1,0:T(8,128)(2,1)}, bf16[2,256,512]{2,1,0:T(8,128)(2,1)}, u32[]{:S(2)}, u32[]{:S(2)}) collective-permute-start(bf16[2,256,512]{2,1,0:T(8,128)(2,1)} %get-tuple-element.136), channel_id=1, source_target_pairs={{0,2},{1,3},{2,0},{3,1},{4,6},{5,7},{6,4},{7,5},{8,10},{9,11},{10,... | collective-permute-start | bytes 1572872 | tf_op jit(solution)/shard_map/ppermute | solution.py:300
  251.6 28.3 %collective-permute-start.28 = (bf16[2,256,512]{2,1,0:T(8,128)(2,1)}, bf16[2,256,512]{2,1,0:T(8,128)(2,1)}, u32[]{:S(2)}, u32[]{:S(2)}) collective-permute-start(bf16[2,256,512]{2,1,0:T(8,128)(2,1)} %get-tuple-element.135), channel_id=1, source_target_pairs={{0,3},{1,2},{2,1},{3,0},{4,7},{5,6},{6,5},{7,4},{8,11},{9,10},{10,... | collective-permute-start | bytes 1572872 | tf_op jit(solution)/shard_map/ppermute | solution.py:300
  251.6 28.3 %collective-permute-start.25 = (bf16[256,1024]{1,0:T(8,128)(2,1)}, bf16[256,1024]{1,0:T(8,128)(2,1)}, u32[]{:S(2)}, u32[]{:S(2)}) collective-permute-start(bf16[256,1024]{1,0:T(8,128)(2,1)} %collective-permute-done.22.refs_3_), channel_id=1, source_target_pairs={{0,4},{4,0},{8,12},{12,8},{16,20},{20,16},{24,28},{28,24},{1,5},{5... | collective-permute-start | bytes 1572872 | tf_op jit(solution)/shard_map/ppermute | solution.py:36
  253.1 26.9 %collective-permute-start.26 = (bf16[256,1024]{1,0:T(8,128)(2,1)}, bf16[256,1024]{1,0:T(8,128)(2,1)}, u32[]{:S(2)}, u32[]{:S(2)}) collective-permute-start(bf16[256,1024]{1,0:T(8,128)(2,1)} %collective-permute-done.23.refs_5_), channel_id=1, source_target_pairs={{0,4},{4,0},{8,12},{12,8},{16,20},{20,16},{24,28},{28,24},{1,5},{5... | collective-permute-start | bytes 1572872 | tf_op jit(solution)/shard_map/ppermute | solution.py:36
  263.7 23.3 %collective-permute-start.29 = (bf16[256,1024]{1,0:T(8,128)(2,1)}, bf16[256,1024]{1,0:T(8,128)(2,1)}, u32[]{:S(2)}, u32[]{:S(2)}) collective-permute-start(bf16[256,1024]{1,0:T(8,128)(2,1)} %get-tuple-element.121.refs_2_), channel_id=1, source_target_pairs={{16,0},{20,4},{24,8},{28,12},{0,16},{4,20},{8,24},{12,28},{17,1},{... | collective-permute-start | bytes 1572872 | tf_op jit(solution)/shard_map/ppermute | solution.py:31
  265.3 23.1 %all-to-all-start.5 = ((bf16[8,8,2048]{2,1,0:T(8,128)(2,1)}), bf16[8,8,2048]{2,1,0:T(8,128)(2,1)S(1)}, u32[]{:S(2)}, u32[]{:S(2)}) async-start(bf16[8,8,2048]{2,1,0:T(8,128)(2,1)} %broadcast_in_dim.17), calls=%async_computation.5 | async-start | bytes 524288 | tf_op jit(solution)/shard_map/all_to_all | solution.py:343
  288.3 15.4 %collective-permute-start.30 = (bf16[2,8,64,512]{3,2,1,0:T(8,128)(2,1)}, bf16[2,8,64,512]{3,2,1,0:T(8,128)(2,1)}, u32[]{:S(2)}, u32[]{:S(2)}) collective-permute-start(bf16[2,8,64,512]{3,2,1,0:T(8,128)(2,1)} %pad_maximum_fusion.1.refs_0_), channel_id=1, source_target_pairs={{0,1},{1,0},{2,3},{3,2},{4,5},{5,4},{6,7},{7,6},{8,9},{9,8},{10,11... | collective-permute-start | bytes 3145736 | tf_op jit(solution)/shard_map/ppermute | solution.py:300
  289.2 10.0 %collective-permute-start.31 = (bf16[2,256,512]{2,1,0:T(8,128)(2,1)}, bf16[2,256,512]{2,1,0:T(8,128)(2,1)S(1)}, u32[]{:S(2)}, u32[]{:S(2)}) collective-permute-start(bf16[2,256,512]{2,1,0:T(8,128)(2,1)} %slice_bitcast_fusion), channel_id=1, source_target_pairs={{0,1},{1,0},{2,3},{3,2},{4,5},{5,4},{6,7},{7,6},{8,9},{9,8},{10,11... | collective-permute-start | bytes 1572872 | tf_op jit(solution)/shard_map/ppermute | solution.py:300
  289.7 14.0 %collective-permute-start.32 = (bf16[256,1024]{1,0:T(8,128)(2,1)}, bf16[256,1024]{1,0:T(8,128)(2,1)S(1)}, u32[]{:S(2)}, u32[]{:S(2)}) collective-permute-start(bf16[256,1024]{1,0:T(8,128)(2,1)} %collective-permute-done.29.refs_4_), channel_id=1, source_target_pairs={{0,4},{4,0},{8,12},{12,8},{16,20},{20,16},{24,28},{28,24},{1,5},{5... | collective-permute-start | bytes 1572872 | tf_op jit(solution)/shard_map/ppermute | solution.py:36
  292.3 6.8 %all-to-all-start.6 = ((bf16[4,16,512]{2,1,0:T(8,128)(2,1)}), bf16[4,16,512]{2,1,0:T(8,128)(2,1)S(1)}, u32[]{:S(2)}, u32[]{:S(2)}) async-start(bf16[4,16,512]{2,1,0:T(8,128)(2,1)} %bitcast.19), calls=%async_computation.6 | async-start | bytes 131072 | tf_op jit(solution)/shard_map/all_to_all | solution.py:250
  303.7 12.5 %collective-permute-start.33 = (bf16[8,512]{1,0:T(8,128)(2,1)S(1)}, bf16[8,512]{1,0:T(8,128)(2,1)S(1)}, u32[]{:S(2)}, u32[]{:S(2)}) collective-permute-start(bf16[8,512]{1,0:T(8,128)(2,1)S(1)} %get-tuple-element.139), channel_id=1, source_target_pairs={{0,0},{1,8},{2,16},{3,24},{4,4},{5,12},{6,20},{7,28},{8,1},{9,9},{... | collective-permute-start | bytes 24584 | tf_op jit(solution)/shard_map/ppermute | solution.py:266
  307.7 8.6 %collective-permute-start.34 = (bf16[8,512]{1,0:T(8,128)(2,1)S(1)}, bf16[8,512]{1,0:T(8,128)(2,1)S(1)}, u32[]{:S(2)}, u32[]{:S(2)}) collective-permute-start(bf16[8,512]{1,0:T(8,128)(2,1)S(1)} %get-tuple-element.140), channel_id=1, source_target_pairs={{0,4},{1,12},{2,20},{3,28},{4,0},{5,8},{6,16},{7,24},{8,5},{9,13},... | collective-permute-start | bytes 24584 | tf_op jit(solution)/shard_map/ppermute | solution.py:266
  (9 other events, 30.0 us)

commit v15 on v14

--- a/solution.py
+++ b/solution.py
@@ -191,34 +191,34 @@
 
     def write(i, e, index):
         term = matmul(query_grad[...], weights[e][i][...], BACK)
-        member = lax.bitwise_xor(lax.div(index, chunk), place[3])
-        out[member, lax.rem(index, chunk)] = term.astype(BF16)
+        out[lax.div(index, chunk), lax.rem(index, chunk)] = term.astype(BF16)
 
     each_block(line, place, relayed, range(n), write)
 
 
-def weight_grad_kernel(line, place, *refs):
-    live, refs = refs[:2], refs[2:]
-    n = (len(refs) - 2) // 2
-    attended, (out, total) = (refs[:n], refs[n : 2 * n]), refs[2 * n :]
-    total[...] = jnp.zeros_like(total)
-
-    def add(i, e, index):
-        block = jnp.concatenate([part[i, index] for part in live for i in range(2)], axis=0)
-        term = matmul(attended[e][i][...], block, FIRST)
+def weight_grad_kernel(line, which, parts, place, own_pair, core_pair, *refs):
+    before, refs = refs[:parts], refs[parts:]
+    n = len(which)
+    attended, outs = (refs[:n], refs[n : 2 * n]), refs[2 * n :]
+    total = outs[-1]
+    total[...] = before[0][...] if parts else jnp.zeros_like(total)
+
+    def add(j, e, index):
+        block = [pair[i, index] for pair in (own_pair, core_pair) for i in range(2)]
+        term = matmul(attended[e][j][...], jnp.concatenate(block, axis=0), FIRST)
         total[...] += term.astype(BF16).astype(F32)
 
-    each_block(line, place, False, range(n), add)
-    out[...] = total[...].astype(BF16)
-
-
-def sum_kernel(place, term, *refs):
-    parts, out = refs[:-1], refs[-1]
-    width = term.shape[3]
-    for c in range(term.shape[1]):
-        total = term[0, c].astype(F32)
-        for part in parts:
-            total = total + part[c].astype(F32)
+    each_block(line, place, False, which, add)
+    if parts:
+        outs[0][...] = total[...].astype(BF16)
+
+
+def sum_kernel(place, parts, out):
+    width = parts.shape[3]
+    for c in range(parts.shape[1]):
+        total = parts[0, c].astype(F32)
+        for k in range(1, parts.shape[0]):
+            total = total + parts[k, c].astype(F32)
         out[:, c * width : (c + 1) * width] = total.astype(BF16)
 
 
@@ -287,7 +287,7 @@
     n_tensor = lax.axis_size("tensor")
     dp_at, tensor_at = lax.axis_index("dp"), lax.axis_index("tensor")
     x, quarter = dp_at % 2, tensor_at % 4
-    place = jnp.stack([dp_at // 2, x, quarter, tensor_at]).astype(jnp.int32)
+    place = jnp.stack([dp_at // 2, x, quarter]).astype(jnp.int32)
     rows = samples * tok_rows
     image_rows = samples * image_own
     images = n_dp * image_rows
@@ -364,6 +364,13 @@
 
     wo_last = line.third(wo_two)
     by_y = tensor_swap(live_here, 2)
+    live_late, by_y = gate((live_flat, by_y))
+    quarter_rows = rows // 4
+    live_rows = lax.dynamic_slice_in_dim(live_late, quarter * quarter_rows, quarter_rows, 0)
+    live_mine = lax.all_to_all(
+        live_rows.reshape(quarter_rows, n_dp, own_width), "dp", split_axis=1, concat_axis=0
+    )
+    live_mine = live_mine.reshape(n_dp, quarter_rows, own_width)
     live_pieces = [live_here, tensor_swap(live_here, 1), by_y, tensor_swap(by_y, 1)]
     wq_others += [line.swap(block, (0, 3)) for block in wq_last[1:]]
     half = shape((rows, half_cols), F32)
@@ -389,7 +396,9 @@
         [pltpu.VMEM((rows, half_cols), F32)] * 2,
         rows * width * local_cols,
     )
-    text_flat, grad_keep, grad_send = gate((text_flat, grad_keep, grad_send))
+    text_flat, live_mine, grad_keep, grad_send = gate(
+        (text_flat, live_mine, grad_keep, grad_send)
+    )
     grad_come = line.swap(grad_send)
     queries, attended = call(
         functools.partial(forward_kernel, line, relayed, late, image_own),
@@ -422,54 +431,49 @@
         (),
         2 * rows * width * local_cols,
     )
-    term, live_flat = gate((term, live_flat))
-    quarter_rows = rows // 4
-    live_rows = lax.dynamic_slice_in_dim(live_flat, quarter * quarter_rows, quarter_rows, 0)
-    live_mine = lax.all_to_all(
-        live_rows.reshape(quarter_rows, n_dp, own_width), "dp", split_axis=1, concat_axis=0
-    )
-    live_mine = live_mine.reshape(n_dp, quarter_rows, own_width)
-    kv_part, term, attended, att_swapped, *att_next = gate(
-        (kv_part, term, attended, att_swapped, *att_next)
+    live_pair = jnp.stack([live_mine, tensor_swap(live_mine, 2)])
+    kv_part, term, live_pair, attended, att_swapped, *att_next = gate(
+        (kv_part, term, live_pair, attended, att_swapped, *att_next)
     )
 
     kv_part = kv_part.reshape(n_dp, image_rows, 2 * local_cols)
     kv_grad = jnp.sum(lax.all_to_all(kv_part, "dp", split_axis=0, concat_axis=0), axis=0)
-    kv_grad, live_mine = gate((kv_grad.astype(BF16), live_mine))
-    kv_grad_all = everywhere(kv_grad).reshape(images, 2 * local_cols)
-    text_parts = [tensor_swap(term[k], k) for k in range(2, n_tensor)]
+    kv_grad_all = everywhere(kv_grad.astype(BF16)).reshape(images, 2 * local_cols)
+    text_parts = lax.all_to_all(term, "tensor", split_axis=0, concat_axis=0).reshape(term.shape)
+    live_core = tensor_swap(live_pair, 1)
     att_far = [line.shift(attended, m) for m in range(2, line.n_z - 1)]
     att_other_next = [line.swap(block) for block in att_next]
-    live_pair = jnp.stack([live_mine, tensor_swap(live_mine, 2)])
-    kv_grad_all, term, live_pair, *staged = gate(
-        (kv_grad_all, term, live_pair, *att_other_next, *text_parts, *att_far)
-    )
-    att_other_next, staged = staged[:2], staged[2:]
-    text_parts, att_far = staged[: n_tensor - 2], staged[n_tensor - 2 :]
+    text_parts, *att_far = gate((text_parts, *att_far))
+    text_grad = call(
+        sum_kernel, place, (text_parts,), [shape((rows, width // n_tensor), BF16)]
+    )
+    next_at, far_at = (0, 1, line.n_z - 1), range(2, line.n_z - 1)
+    weight_part = call(
+        functools.partial(weight_grad_kernel, line, next_at, 0),
+        place,
+        (live_pair, live_core, attended, *att_next, att_swapped, *att_other_next),
+        [shape((local_cols, own_width), F32)],
+        (),
+        6 * 2 * rows * local_cols * own_width,
+    )
+    kv_grad_all, text_grad = gate((kv_grad_all, text_grad))
 
     att_other_far = [line.swap(block) for block in att_far]
-    live_core = tensor_swap(live_pair, 1)
-    text_parts.append(tensor_swap(term[1], 1))
     image_term = matmul(kv_grad_all[:, :local_cols], key_weight, BACK)
     image_term = image_term + matmul(kv_grad_all[:, local_cols:], value_weight, BACK)
-    text_grad = call(
-        sum_kernel, place, (term, *text_parts), [shape((rows, width // n_tensor), BF16)]
-    )
-    image_grad, live_core, text_grad, *att_other_far = to_owner(
-        line, image_term.astype(BF16), live_core, text_grad, *att_other_far
+    image_grad, weight_part, *att_other_far = to_owner(
+        line, image_term.astype(BF16), weight_part, *att_other_far
     )
     image_grad = image_grad.reshape(samples, image_own, width // n_tensor)
     text_grad = text_grad.reshape(samples, tok_rows, width // n_tensor)
 
-    att_blocks = [attended, att_next[0], *att_far, att_next[1]]
-    att_others = [att_swapped, att_other_next[0], *att_other_far, att_other_next[1]]
     weight_grad = call(
-        functools.partial(weight_grad_kernel, line),
-        place,
-        (live_pair, live_core, *att_blocks, *att_others),
+        functools.partial(weight_grad_kernel, line, far_at, 1),
+        place,
+        (live_pair, live_core, weight_part, *att_far, *att_other_far),
         [shape((local_cols, own_width), BF16)],
         [pltpu.VMEM((local_cols, own_width), F32)],
-        2 * n_dp * rows * local_cols * own_width,
+        2 * 2 * rows * local_cols * own_width,
     )
     return text_grad, image_grad, weight_grad
 

time: 319 us -> 330 us (1.034)
  blocking collectives: 0 us -> 15.8 us
  waiting for transfers between devices: 149 us -> 144 us
  local copies, waits for them, and re-layouts: 12.3 us -> 8.33 us
  Pallas kernels: 45.7 us -> 49.1 us
    ppermute x12, waiting for transfers between devices: 16.2 us -> 37.8 us  [swap(): return lax.ppermute(block, 'dp', pairs)]
    all_to_all x0 -> x1, blocking collectives: none -> 15.8 us  [shards(): lax.all_to_all(kv_part, 'dp', split_axis=0, concat_axis=0)]
    ppermute x8 -> x5, waiting for transfers between devices: 23.7 us -> 9.1 us  [tensor_swap(): lax.ppermute(block, 'tensor', [(t, t ^ bit) for t in range(n_tensor)])]
    ppermute x13, waiting for transfers between devices: 19.3 us -> 6.07 us  [move(): return lax.ppermute(block, 'dp', pairs)]
    all_to_all x1, waiting for transfers between devices: 10.6 us -> 22.8 us  [shards(): lax.all_to_all(term, 'tensor', split_axis=0, concat_axis=0)]
    all_to_all x1, waiting for transfers between devices: 12.2 us -> 0.01 us  [shards(): lax.all_to_all(live_rows.reshape(quarter_rows, n_dp, own_width), 'dp', sp...]
    pallas_call x8 -> x9, Pallas kernels: 45.7 us -> 49.1 us  [call(): pl.pallas_call(kernel, out_shape=outs[0] if single else outs, in_specs=[p...]
  transfers between devices with their start and end apart: 42 -> 39, of which waited for: 18 -> 17; matrix products, arithmetic and copies ran while one was open for 8% -> 6% of each run, Pallas kernels for 14% -> 15%
where the time goes in v15:
time: 330 us; the launch traced here: 328 us
  waiting for transfers between devices  144 us (44%)
  starting transfers between devices  94.1 us (29%)
  Pallas kernels  49.1 us (15%)
  blocking collectives  15.8 us (5%)
  other arithmetic  12.2 us (4%)
  local copies, waits for them, and re-layouts  8.33 us (3%)
  matrix products  3.34 us (1%)
    pallas_call x9, Pallas kernels, call(): pl.pallas_call(kernel, out_shape=outs[0] if single else outs, in_specs=[p...  49.1 us
    ppermute x12, waiting for transfers between devices, swap(): return lax.ppermute(block, 'dp', pairs)  37.8 us
    all_to_all x2, waiting for transfers between devices, everywhere(): return lax.all_to_all(copies, 'dp', split_axis=0, concat_axis=0)  29.8 us
    all_to_all x1, waiting for transfers between devices, shards(): lax.all_to_all(part_kv, 'dp', split_axis=0, concat_axis=0)  29.3 us
    ppermute x13, starting transfers between devices, move(): return lax.ppermute(block, 'dp', pairs)  27.1 us
    all_to_all x1, waiting for transfers between devices, shards(): lax.all_to_all(term, 'tensor', split_axis=0, concat_axis=0)  22.8 us
    ppermute x12, starting transfers between devices, swap(): return lax.ppermute(block, 'dp', pairs)  18.5 us
    all_to_all x2, starting transfers between devices, everywhere(): return lax.all_to_all(copies, 'dp', split_axis=0, concat_axis=0)  16 us
  transfers between devices with their start and end apart: 39, of which 17 were waited for; matrix products, arithmetic and copies ran while one was open for 6% of the time, Pallas kernels for 15%

profile of v15, /device:TPU:4, one launch (start us, length us, event | category | flops | bytes accessed | tf_op | source)
XLA Modules:
  0.0 327.6 jit_solution(2843991999566549280)
XLA Ops:
  2.1 5.5 %collective-permute-start.3 = (bf16[512,1024]{1,0:T(8,128)(2,1)}, bf16[512,1024]{1,0:T(8,128)(2,1)}, u32[]{:S(2)}, u32[]{:S(2)}) collective-permute-start(bf16[512,1024]{1,0:T(8,128)(2,1)} %refs_0_.1), channel_id=1, source_target_pairs={{0,8},{4,12},{8,16},{12,20},{16,24},{20,28},{1,9},{5,13},{9,17},{1... | collective-permute-start | bytes 3145736 | tf_op jit(solution)/shard_map/ppermute | solution.py:31
  7.6 2.2 constant_dynamic-slice_fusion.3
  11.4 1.8 broadcast_select_fusion
  15.4 4.9 %all-to-all-start = ((bf16[8,8,512]{2,0,1:T(8,128)(2,1)}), bf16[8,8,512]{2,0,1:T(8,128)(2,1)S(1)}, u32[]{:S(2)}, u32[]{:S(2)}) async-start(bf16[8,8,512]{2,0,1:T(8,128)(2,1)} %copy.14), calls=%async_computation | async-start | bytes 131072 | tf_op jit(solution)/shard_map/all_to_all | solution.py:313
  20.3 4.7 %collective-permute-done = bf16[512,512]{1,0:T(8,128)(2,1)} collective-permute-done((bf16[512,512]{1,0:T(8,128)(2,1)}, bf16[512,512]{1,0:T(8,128)(2,1)}, u32[]{:S(2)}, u32[]{:S(2)}) %collective-permute-start) | collective-permute-done | bytes 524320 | tf_op jit(solution)/shard_map/ppermute | solution.py:36
  25.0 2.3 pad_maximum_fusion.refs_0_
  27.4 7.8 %all-to-all-done = bf16[8,8,512]{2,0,1:T(8,128)(2,1)S(1)} async-done(((bf16[8,8,512]{2,0,1:T(8,128)(2,1)}), bf16[8,8,512]{2,0,1:T(8,128)(2,1)S(1)}, u32[]{:S(2)}, u32[]{:S(2)}) %all-to-all-start) | async-done | bytes 65568 | tf_op jit(solution)/shard_map/all_to_all | solution.py:313
  35.1 1.6 collective-permute-start.4
  38.0 5.5 %collective-permute-start.9 = (bf16[512,1024]{1,0:T(8,128)(2,1)}, bf16[512,1024]{1,0:T(8,128)(2,1)}, u32[]{:S(2)}, u32[]{:S(2)}) collective-permute-start(bf16[512,1024]{1,0:T(8,128)(2,1)} %pad_maximum_fusion.refs_0_), channel_id=1, source_target_pairs={{0,8},{4,12},{8,16},{12,20},{16,24},{20,28},{1,9},{5,13},{9,17},{1... | collective-permute-start | bytes 3145736 | tf_op jit(solution)/shard_map/ppermute | solution.py:31
  44.8 1.7 collective-permute-start.7
  48.3 10.7 %collective-permute-done.4.refs_2_.refs_5_ = bf16[512,1024]{1,0:T(8,128)(2,1)} collective-permute-done((bf16[512,1024]{1,0:T(8,128)(2,1)}, bf16[512,1024]{1,0:T(8,128)(2,1)}, u32[]{:S(2)}, u32[]{:S(2)}) %collective-permute-start.4) | collective-permute-done | bytes 1048608 | tf_op jit(solution)/shard_map/ppermute | solution.py:36
  59.0 3.4 %collective-permute-start.5 = (bf16[512,1024]{1,0:T(8,128)(2,1)}, bf16[512,1024]{1,0:T(8,128)(2,1)}, u32[]{:S(2)}, u32[]{:S(2)}) collective-permute-start(bf16[512,1024]{1,0:T(8,128)(2,1)} %collective-permute-done.2.refs_1_), channel_id=1, source_target_pairs={{0,4},{4,0},{8,12},{12,8},{16,20},{20,16},{1,5},{5,1},{9,13},{13,9... | collective-permute-start | bytes 3145736 | tf_op jit(solution)/shard_map/ppermute | solution.py:36
  63.3 4.2 %all-to-all-start.1 = ((f32[8,8,2048]{2,1,0:T(8,128)}), f32[8,8,2048]{2,1,0:T(8,128)}, u32[]{:S(2)}, u32[]{:S(2)}) async-start(f32[8,8,2048]{2,1,0:T(8,128)} %maximum_bitcast_fusion), calls=%async_computation.1 | async-start | bytes 1048576 | tf_op jit(solution)/shard_map/all_to_all | solution.py:334
  67.4 29.3 %all-to-all-done.1 = f32[8,8,2048]{2,1,0:T(8,128)} async-done(((f32[8,8,2048]{2,1,0:T(8,128)}), f32[8,8,2048]{2,1,0:T(8,128)}, u32[]{:S(2)}, u32[]{:S(2)}) %all-to-all-start.1) | async-done | bytes 524320 | tf_op jit(solution)/shard_map/all_to_all | solution.py:334
  97.9 2.3 broadcast_select_fusion.2.refs_1_.refs_3_
  103.6 1.6 collective-permute-start.11
  105.3 1.7 collective-permute-start.13
  107.7 12.4 %all-to-all-start.2 = ((bf16[8,8,2048]{2,1,0:T(8,128)(2,1)}), bf16[8,8,2048]{2,1,0:T(8,128)(2,1)S(1)}, u32[]{:S(2)}, u32[]{:S(2)}) async-start(bf16[8,8,2048]{2,1,0:T(8,128)(2,1)} %broadcast_in_dim.16), calls=%async_computation.2 | async-start | bytes 524288 | tf_op jit(solution)/shard_map/all_to_all | solution.py:343
  120.7 5.4 %shard_map.103.part = f32[256,1024]{1,0:T(8,128)} custom-call(s32[3]{0:T(128)} %pad_add_fusion.place, bf16[256,4096]{1,0:T(8,128)(2,1)} %bitcast.35, bf16[512,1024]{1,0:T(8,128)(2,1)} %refs_0_.1, bf16[512,1024]{1,0:T(8,128)(2,1)} %collective-permute-done.2.refs_1_, bf16[512,1024]{1,0:T(8,128)(2,1)} %collective-permute-done.4.refs_2_.refs_5_, ...), custom_call_target="tpu_custom_call" | custom-call | flops 1073741824 | bytes 7340032 | tf_op jit(solution)/shard_map/pallas_call | solution.py:228
  126.1 25.5 %all-to-all-done.2 = bf16[8,8,2048]{2,1,0:T(8,128)(2,1)S(1)} async-done(((bf16[8,8,2048]{2,1,0:T(8,128)(2,1)}), bf16[8,8,2048]{2,1,0:T(8,128)(2,1)S(1)}, u32[]{:S(2)}, u32[]{:S(2)}) %all-to-all-start.2) | async-done | bytes 262176 | tf_op jit(solution)/shard_map/all_to_all | solution.py:343
  152.2 2.3 broadcast_select_fusion.1.refs_2_
  155.8 6.7 %collective-permute-done.15.by_y = bf16[256,1024]{1,0:T(8,128)(2,1)} collective-permute-done((bf16[256,1024]{1,0:T(8,128)(2,1)}, bf16[256,1024]{1,0:T(8,128)(2,1)}, u32[]{:S(2)}, u32[]{:S(2)}) %collective-permute-start.15) | collective-permute-done | bytes 524320 | tf_op jit(solution)/shard_map/ppermute | solution.py:300
  163.7 4.8 %all-to-all-start.3 = ((bf16[1,64,8,512]{3,1,0,2:T(8,128)(2,1)}), bf16[1,64,8,512]{3,1,0,2:T(8,128)(2,1)S(1)}, u32[]{:S(2)}, u32[]{:S(2)}) async-start(bf16[1,64,8,512]{3,1,0,2:T(8,128)(2,1)} %copy.15), calls=%async_computation.3 | async-start | bytes 1048576 | tf_op jit(solution)/shard_map/all_to_all | solution.py:370
  168.5 3.9 %collective-permute-start.19 = (bf16[512,1024]{1,0:T(8,128)(2,1)}, bf16[512,1024]{1,0:T(8,128)(2,1)S(1)}, u32[]{:S(2)}, u32[]{:S(2)}) collective-permute-start(bf16[512,1024]{1,0:T(8,128)(2,1)} %collective-permute-done.12.refs_2_.refs_4_), channel_id=1, source_target_pairs={{0,4},{4,0},{24,28},{28,24},{1,5},{5,1},{25,29},{29,25},{2,6},{6,2... | collective-permute-start | bytes 3145736 | tf_op jit(solution)/shard_map/ppermute | solution.py:36
  173.0 1.6 collective-permute-done.16.by_core
  176.2 5.8 %shard_map.104 = (f32[256,512]{1,0:T(8,128)}, f32[256,512]{1,0:T(8,128)}) custom-call(s32[3]{0:T(128)} %pad_add_fusion.place, bf16[256,4096]{1,0:T(8,128)(2,1)} %bitcast.33, bf16[256,1024]{1,0:T(8,128)(2,1)} %collective-permute-done.1.mine, bf16[256,1024]{1,0:T(8,128)(2,1)} %copy-done.6, bf16[256,1024]{1,0:T(8,128)(2,1)} %collective-permute-done.15.by_y, ...), custom_call_target="tpu_custom_call" | custom-call | flops 1073741824 | bytes 8388608 | tf_op jit(solution)/shard_map/pallas_call | solution.py:228
  182.0 3.2 collective-permute-done.18.refs_3_
  185.2 5.7 %shard_map.105 = (bf16[256,512]{1,0:T(8,128)(2,1)}, bf16[256,512]{1,0:T(8,128)(2,1)}) custom-call(s32[3]{0:T(128)} %pad_add_fusion.place, bf16[256,4096]{1,0:T(8,128)(2,1)} %bitcast.34, bf16[256,1024]{1,0:T(8,128)(2,1)} %collective-permute-done.1.mine, bf16[256,1024]{1,0:T(8,128)(2,1)} %copy-done.6, bf16[256,1024]{1,0:T(8,128)(2,1)} %collective-permute-done.15.by_y, ...), custom_call_target="tpu_custom_call" | custom-call | flops 1073741824 | bytes 7864320 | tf_op jit(solution)/shard_map/pallas_call | solution.py:228
  191.3 1.5 collective-permute-start.21
  192.8 5.6 %collective-permute-done.19.refs_5_.refs_9_ = bf16[512,1024]{1,0:T(8,128)(2,1)S(1)} collective-permute-done((bf16[512,1024]{1,0:T(8,128)(2,1)}, bf16[512,1024]{1,0:T(8,128)(2,1)S(1)}, u32[]{:S(2)}, u32[]{:S(2)}) %collective-permute-start.19) | collective-permute-done | bytes 1048608 | tf_op jit(solution)/shard_map/ppermute | solution.py:36
  199.4 7.2 %shard_map.106 = (bf16[256,1024]{1,0:T(8,128)(2,1)}, bf16[256,1024]{1,0:T(8,128)(2,1)}) custom-call(s32[3]{0:T(128)} %pad_add_fusion.place, bf16[256,4096]{1,0:T(8,128)(2,1)} %bitcast.36, bf16[64,2048]{1,0:T(8,128)(2,1)} %bitcast.37, f32[256,1024]{1,0:T(8,128)} %shard_map.103.part, bf16[512,1024]{1,0:T(8,128)(2,1)} %collective-permute-done.3.refs_0_.refs_2_, ...), custom_call_target="tpu_custom_call" | custom-call | flops 1073741824 | bytes 10747904 | tf_op jit(solution)/shard_map/pallas_call | solution.py:228
  206.5 3.8 %collective-permute-start.23 = (bf16[256,1024]{1,0:T(8,128)(2,1)}, bf16[256,1024]{1,0:T(8,128)(2,1)S(1)}, u32[]{:S(2)}, u32[]{:S(2)}) collective-permute-start(bf16[256,1024]{1,0:T(8,128)(2,1)} %get-tuple-element.113.refs_0_), channel_id=1, source_target_pairs={{8,0},{12,4},{16,8},{20,12},{24,16},{28,20},{0,24},{4,28},{9,1},{1... | collective-permute-start | bytes 1572872 | tf_op jit(solution)/shard_map/ppermute | solution.py:31
  211.7 3.6 %shard_map.107 = (bf16[256,1024]{1,0:T(8,128)(2,1)}, f32[64,2048]{1,0:T(8,128)}) custom-call(s32[3]{0:T(128)} %pad_add_fusion.place, bf16[256,1024]{1,0:T(8,128)(2,1)} %get-tuple-element.100.query, bf16[64,2048]{1,0:T(8,128)(2,1)} %bitcast.38, bf16[256,512]{1,0:T(8,128)(2,1)} %get-tuple-element.101.keep, bf16[256,512]{1,0:T(8,128)(2,1)} %copy-done.10), custom_call_target="tpu_custom_call" | custom-call | flops 167772160 | bytes 2359296 | tf_op jit(solution)/shard_map/pallas_call | solution.py:228
  215.2 8.9 %shard_map.108 = bf16[4,2,256,512]{3,2,1,0:T(8,128)(2,1)} custom-call(s32[3]{0:T(128)} %pad_add_fusion.place, bf16[256,1024]{1,0:T(8,128)(2,1)} %get-tuple-element.106.query_grad, bf16[512,1024]{1,0:T(8,128)(2,1)} %refs_0_.1, bf16[512,1024]{1,0:T(8,128)(2,1)} %collective-permute-done.2.refs_1_, bf16[512,1024]{1,0:T(8,128)(2,1)} %collective-permute-done.3.refs_0_.refs_2_, ...), custom_call_target="tpu_custom_call" | custom-call | flops 2147483648 | bytes 13107200 | tf_op jit(solution)/shard_map/pallas_call | solution.py:228
  224.3 2.9 collective-permute-done.24.refs_2_
  227.2 15.8 %all_to_all.64 = f32[8,8,2048]{2,1,0:T(8,128)S(1)} all-to-all(f32[8,8,2048]{2,1,0:T(8,128)S(1)} %bitcast.47), channel_id=1, replica_groups=mesh['dp'=8,'tensor'=4] {'dp'}, dimensions={0} | all-to-all | bytes 1048576 | tf_op jit(solution)/shard_map/all_to_all | solution.py:440
  243.0 4.9 %all-to-all-start.6 = ((bf16[4,2,256,512]{3,2,1,0:T(8,128)(2,1)}), bf16[4,2,256,512]{3,2,1,0:T(8,128)(2,1)}, u32[]{:S(2)}, u32[]{:S(2)}) async-start(bf16[4,2,256,512]{3,2,1,0:T(8,128)(2,1)} %shard_map.108), calls=%async_computation.6 | async-start | bytes 4194304 | tf_op jit(solution)/shard_map/all_to_all | solution.py:442
  249.2 22.8 %all-to-all-done.6.parts = bf16[4,2,256,512]{3,2,1,0:T(8,128)(2,1)} async-done(((bf16[4,2,256,512]{3,2,1,0:T(8,128)(2,1)}), bf16[4,2,256,512]{3,2,1,0:T(8,128)(2,1)}, u32[]{:S(2)}, u32[]{:S(2)}) %all-to-all-start.6) | async-done | bytes 2097184 | tf_op jit(solution)/shard_map/all_to_all | solution.py:442
  272.8 3.6 %all-to-all-start.5 = ((bf16[8,8,2048]{2,1,0:T(8,128)(2,1)}), bf16[8,8,2048]{2,1,0:T(8,128)(2,1)S(1)}, u32[]{:S(2)}, u32[]{:S(2)}) async-start(bf16[8,8,2048]{2,1,0:T(8,128)(2,1)} %broadcast_in_dim.17), calls=%async_computation.5 | async-start | bytes 524288 | tf_op jit(solution)/shard_map/all_to_all | solution.py:343
  276.4 2.0 collective-permute-start.27
  278.5 2.6 shard_map.109
  281.2 4.3 %all-to-all-done.5 = bf16[8,8,2048]{2,1,0:T(8,128)(2,1)S(1)} async-done(((bf16[8,8,2048]{2,1,0:T(8,128)(2,1)}), bf16[8,8,2048]{2,1,0:T(8,128)(2,1)S(1)}, u32[]{:S(2)}, u32[]{:S(2)}) %all-to-all-start.5) | async-done | bytes 262176 | tf_op jit(solution)/shard_map/all_to_all | solution.py:343
  288.3 4.7 %all-to-all-start.7 = ((bf16[4,16,512]{2,1,0:T(8,128)(2,1)}), bf16[4,16,512]{2,1,0:T(8,128)(2,1)S(1)}, u32[]{:S(2)}, u32[]{:S(2)}) async-start(bf16[4,16,512]{2,1,0:T(8,128)(2,1)} %bitcast.17), calls=%async_computation.7 | async-start | bytes 131072 | tf_op jit(solution)/shard_map/all_to_all | solution.py:250
  294.3 11.2 %collective-permute-done.28.refs_5_ = bf16[256,1024]{1,0:T(8,128)(2,1)} collective-permute-done((bf16[256,1024]{1,0:T(8,128)(2,1)}, bf16[256,1024]{1,0:T(8,128)(2,1)}, u32[]{:S(2)}, u32[]{:S(2)}) %collective-permute-start.28) | collective-permute-done | bytes 524320 | tf_op jit(solution)/shard_map/ppermute | solution.py:36
  305.6 5.7 %shard_map.110.refs_0_ = f32[1024,512]{1,0:T(8,128)} custom-call(s32[3]{0:T(128)} %pad_add_fusion.place, bf16[2,8,64,512]{3,2,1,0:T(8,128)(2,1)} %copy-done.2, bf16[2,8,64,512]{3,2,1,0:T(8,128)(2,1)} %collective-permute-done.26.core_pair, bf16[256,1024]{1,0:T(8,128)(2,1)} %get-tuple-element.113.refs_0_, bf16[256,1024]{1,0:T(8,128)(2,1)} %copy-done.9, ...), custom_call_target="tpu_custom_call" | custom-call | flops 1610612736 | bytes 7340032 | tf_op jit(solution)/shard_map/pallas_call | solution.py:228
  311.3 4.2 %collective-permute-done.29.refs_2_ = bf16[256,1024]{1,0:T(8,128)(2,1)} collective-permute-done((bf16[256,1024]{1,0:T(8,128)(2,1)}, bf16[256,1024]{1,0:T(8,128)(2,1)}, u32[]{:S(2)}, u32[]{:S(2)}) %collective-permute-start.29) | collective-permute-done | bytes 524320 | tf_op jit(solution)/shard_map/ppermute | solution.py:36
  315.4 5.1 %collective-permute-start.30 = (bf16[8,512]{1,0:T(8,128)(2,1)S(1)}, bf16[8,512]{1,0:T(8,128)(2,1)S(1)}, u32[]{:S(2)}, u32[]{:S(2)}) collective-permute-start(bf16[8,512]{1,0:T(8,128)(2,1)S(1)} %get-tuple-element.127), channel_id=1, source_target_pairs={{0,0},{1,8},{2,16},{3,24},{4,4},{5,12},{6,20},{7,28},{8,1},{9,9},{... | collective-permute-start | bytes 24584 | tf_op jit(solution)/shard_map/ppermute | solution.py:266
  321.7 4.2 %shard_map.111 = bf16[1024,512]{1,0:T(8,128)(2,1)} custom-call(s32[3]{0:T(128)} %pad_add_fusion.place, bf16[2,8,64,512]{3,2,1,0:T(8,128)(2,1)} %copy-done.2, bf16[2,8,64,512]{3,2,1,0:T(8,128)(2,1)} %collective-permute-done.26.core_pair, f32[1024,512]{1,0:T(8,128)} %shard_map.110.refs_0_, bf16[256,1024]{1,0:T(8,128)(2,1)} %collective-permute-done.25.refs_1_, ...), custom_call_target="tpu_custom_call" | custom-call | flops 536870912 | bytes 6291456 | tf_op jit(solution)/shard_map/pallas_call | solution.py:228
  (95 shorter events, 33.4 us)
Async XLA Ops:
  0.6 45.9 %copy-start = (bf16[512,1024]{1,0:T(8,128)(2,1)S(1)}, bf16[512,1024]{1,0:T(8,128)(2,1)}, u32[]{:S(2)}) copy-start(bf16[512,1024]{1,0:T(8,128)(2,1)} %param.13) | copy-start | bytes 3145732
  0.6 10.7 %copy-start.12 = (s32[2]{0:T(128)S(1)}, s32[2]{0:T(128)}, u32[]{:S(2)}) copy-start(s32[2]{0:T(128)} %param.11) | copy-start | bytes 28
  0.7 34.5 %collective-permute-start.2 = (bf16[512,1024]{1,0:T(8,128)(2,1)}, bf16[512,1024]{1,0:T(8,128)(2,1)}, u32[]{:S(2)}, u32[]{:S(2)}) collective-permute-start(bf16[512,1024]{1,0:T(8,128)(2,1)} %refs_0_.1), channel_id=1, source_target_pairs={{8,0},{12,4},{16,8},{20,12},{24,16},{28,20},{9,1},{13,5},{17,9},{2... | collective-permute-start | bytes 3145736 | tf_op jit(solution)/shard_map/ppermute | solution.py:31
  2.1 33.1 %collective-permute-start.3 = (bf16[512,1024]{1,0:T(8,128)(2,1)}, bf16[512,1024]{1,0:T(8,128)(2,1)}, u32[]{:S(2)}, u32[]{:S(2)}) collective-permute-start(bf16[512,1024]{1,0:T(8,128)(2,1)} %refs_0_.1), channel_id=1, source_target_pairs={{0,8},{4,12},{8,16},{12,20},{16,24},{20,28},{1,9},{5,13},{9,17},{1... | collective-permute-start | bytes 3145736 | tf_op jit(solution)/shard_map/ppermute | solution.py:31
  9.9 15.2 %collective-permute-start = (bf16[512,512]{1,0:T(8,128)(2,1)}, bf16[512,512]{1,0:T(8,128)(2,1)}, u32[]{:S(2)}, u32[]{:S(2)}) collective-permute-start(bf16[512,512]{1,0:T(8,128)(2,1)} %get-tuple-element.126), channel_id=1, source_target_pairs={{0,4},{4,0},{8,12},{12,8},{16,20},{20,16},{24,28},{28,24},{1,5},{5... | collective-permute-start | bytes 1572872 | tf_op jit(solution)/shard_map/ppermute | solution.py:36
  11.4 3.3 %copy-start.11 = (bf16[2,4,4096]{2,1,0:T(4,128)(2,1)S(1)}, bf16[2,4,4096]{2,1,0:T(4,128)(2,1)}, u32[]{:S(2)}) copy-start(bf16[2,4,4096]{2,1,0:T(4,128)(2,1)} %param.9) | copy-start | bytes 196612
  13.3 149.3 %copy-start.1 = (bf16[2,128,4096]{2,1,0:T(8,128)(2,1)}, bf16[2,128,4096]{2,1,0:T(8,128)(2,1)S(1)}, u32[]{:S(2)}) copy-start(bf16[2,128,4096]{2,1,0:T(8,128)(2,1)S(1)} %broadcast_select_fusion) | copy-start | bytes 6291460
  14.2 20.9 %collective-permute-start.1 = (bf16[256,1024]{1,0:T(8,128)(2,1)}, bf16[256,1024]{1,0:T(8,128)(2,1)}, u32[]{:S(2)}, u32[]{:S(2)}) collective-permute-start(bf16[256,1024]{1,0:T(8,128)(2,1)} %constant_dynamic-slice_fusion.1), channel_id=1, source_target_pairs={{0,4},{4,0},{8,12},{12,8},{16,20},{20,16},{24,28},{28,24},{1,5},{5... | collective-permute-start | bytes 1572872 | tf_op jit(solution)/shard_map/ppermute | solution.py:36
  15.4 19.7 %all-to-all-start = ((bf16[8,8,512]{2,0,1:T(8,128)(2,1)}), bf16[8,8,512]{2,0,1:T(8,128)(2,1)S(1)}, u32[]{:S(2)}, u32[]{:S(2)}) async-start(bf16[8,8,512]{2,0,1:T(8,128)(2,1)} %copy.14), calls=%async_computation | async-start | bytes 131072 | tf_op jit(solution)/shard_map/all_to_all | solution.py:313
  35.1 23.9 %collective-permute-start.4 = (bf16[512,1024]{1,0:T(8,128)(2,1)}, bf16[512,1024]{1,0:T(8,128)(2,1)}, u32[]{:S(2)}, u32[]{:S(2)}) collective-permute-start(bf16[512,1024]{1,0:T(8,128)(2,1)} %refs_0_.1), channel_id=1, source_target_pairs={{0,4},{4,0},{8,12},{12,8},{16,20},{20,16},{24,28},{28,24},{1,5},{5... | collective-permute-start | bytes 3145736 | tf_op jit(solution)/shard_map/ppermute | solution.py:36
  36.7 61.2 %collective-permute-start.8 = (bf16[512,1024]{1,0:T(8,128)(2,1)}, bf16[512,1024]{1,0:T(8,128)(2,1)}, u32[]{:S(2)}, u32[]{:S(2)}) collective-permute-start(bf16[512,1024]{1,0:T(8,128)(2,1)} %pad_maximum_fusion.refs_0_), channel_id=1, source_target_pairs={{8,0},{12,4},{16,8},{20,12},{24,16},{28,20},{9,1},{13,5},{17,9},{2... | collective-permute-start | bytes 3145736 | tf_op jit(solution)/shard_map/ppermute | solution.py:31
  38.0 59.9 %collective-permute-start.9 = (bf16[512,1024]{1,0:T(8,128)(2,1)}, bf16[512,1024]{1,0:T(8,128)(2,1)}, u32[]{:S(2)}, u32[]{:S(2)}) collective-permute-start(bf16[512,1024]{1,0:T(8,128)(2,1)} %pad_maximum_fusion.refs_0_), channel_id=1, source_target_pairs={{0,8},{4,12},{8,16},{12,20},{16,24},{20,28},{1,9},{5,13},{9,17},{1... | collective-permute-start | bytes 3145736 | tf_op jit(solution)/shard_map/ppermute | solution.py:31
  43.5 54.3 %collective-permute-start.6 = (bf16[512,1024]{1,0:T(8,128)(2,1)}, bf16[512,1024]{1,0:T(8,128)(2,1)}, u32[]{:S(2)}, u32[]{:S(2)}) collective-permute-start(bf16[512,1024]{1,0:T(8,128)(2,1)} %collective-permute-done.2.refs_1_), channel_id=1, source_target_pairs={{8,0},{12,4},{16,8},{20,12},{9,1},{13,5},{17,9},{21,13},{10,2},{14... | collective-permute-start | bytes 3145736 | tf_op jit(solution)/shard_map/ppermute | solution.py:31
  44.8 53.0 %collective-permute-start.7 = (bf16[512,1024]{1,0:T(8,128)(2,1)}, bf16[512,1024]{1,0:T(8,128)(2,1)}, u32[]{:S(2)}, u32[]{:S(2)}) collective-permute-start(bf16[512,1024]{1,0:T(8,128)(2,1)} %collective-permute-done.3.refs_0_.refs_2_), channel_id=1, source_target_pairs={{8,16},{12,20},{16,24},{20,28},{9,17},{13,21},{17,25},{21,29},{10,... | collective-permute-start | bytes 3145736 | tf_op jit(solution)/shard_map/ppermute | solution.py:31
  59.0 38.9 %collective-permute-start.5 = (bf16[512,1024]{1,0:T(8,128)(2,1)}, bf16[512,1024]{1,0:T(8,128)(2,1)}, u32[]{:S(2)}, u32[]{:S(2)}) collective-permute-start(bf16[512,1024]{1,0:T(8,128)(2,1)} %collective-permute-done.2.refs_1_), channel_id=1, source_target_pairs={{0,4},{4,0},{8,12},{12,8},{16,20},{20,16},{1,5},{5,1},{9,13},{13,9... | collective-permute-start | bytes 3145736 | tf_op jit(solution)/shard_map/ppermute | solution.py:36
  63.3 33.5 %all-to-all-start.1 = ((f32[8,8,2048]{2,1,0:T(8,128)}), f32[8,8,2048]{2,1,0:T(8,128)}, u32[]{:S(2)}, u32[]{:S(2)}) async-start(f32[8,8,2048]{2,1,0:T(8,128)} %maximum_bitcast_fusion), calls=%async_computation.1 | async-start | bytes 1048576 | tf_op jit(solution)/shard_map/all_to_all | solution.py:334
  100.2 51.4 %collective-permute-start.12 = (bf16[512,1024]{1,0:T(8,128)(2,1)}, bf16[512,1024]{1,0:T(8,128)(2,1)}, u32[]{:S(2)}, u32[]{:S(2)}) collective-permute-start(bf16[512,1024]{1,0:T(8,128)(2,1)} %broadcast_select_fusion.2.refs_1_.refs_3_), channel_id=1, source_target_pairs={{8,0},{12,4},{16,24},{20,28},{9,1},{13,5},{17,25},{21,29},{10,2},{... | collective-permute-start | bytes 3145736 | tf_op jit(solution)/shard_map/ppermute | solution.py:31
  101.5 50.1 %collective-permute-start.14 = (bf16[512,1024]{1,0:T(8,128)(2,1)}, bf16[512,1024]{1,0:T(8,128)(2,1)}, u32[]{:S(2)}, u32[]{:S(2)}) collective-permute-start(bf16[512,1024]{1,0:T(8,128)(2,1)} %broadcast_select_fusion.2.refs_1_.refs_3_), channel_id=1, source_target_pairs={{0,4},{4,0},{8,12},{12,8},{16,20},{20,16},{24,28},{28,24},{1,5},{5... | collective-permute-start | bytes 3145736 | tf_op jit(solution)/shard_map/ppermute | solution.py:36
  102.3 49.3 %collective-permute-start.10 = (bf16[512,1024]{1,0:T(8,128)(2,1)}, bf16[512,1024]{1,0:T(8,128)(2,1)}, u32[]{:S(2)}, u32[]{:S(2)}) collective-permute-start(bf16[512,1024]{1,0:T(8,128)(2,1)} %collective-permute-done.8.refs_1_), channel_id=1, source_target_pairs={{8,0},{12,4},{16,8},{20,12},{9,1},{13,5},{17,9},{21,13},{10,2},{14... | collective-permute-start | bytes 3145736 | tf_op jit(solution)/shard_map/ppermute | solution.py:31
  103.6 48.0 %collective-permute-start.11 = (bf16[512,1024]{1,0:T(8,128)(2,1)}, bf16[512,1024]{1,0:T(8,128)(2,1)}, u32[]{:S(2)}, u32[]{:S(2)}) collective-permute-start(bf16[512,1024]{1,0:T(8,128)(2,1)} %collective-permute-done.9.refs_2_), channel_id=1, source_target_pairs={{8,16},{12,20},{16,24},{20,28},{9,17},{13,21},{17,25},{21,29},{10,... | collective-permute-start | bytes 3145736 | tf_op jit(solution)/shard_map/ppermute | solution.py:31
  105.3 46.3 %collective-permute-start.13 = (bf16[512,1024]{1,0:T(8,128)(2,1)}, bf16[512,1024]{1,0:T(8,128)(2,1)}, u32[]{:S(2)}, u32[]{:S(2)}) collective-permute-start(bf16[512,1024]{1,0:T(8,128)(2,1)} %collective-permute-done.3.refs_0_.refs_2_), channel_id=1, source_target_pairs={{8,12},{12,8},{16,20},{20,16},{24,28},{28,24},{9,13},{13,9},{17,21... | collective-permute-start | bytes 3145736 | tf_op jit(solution)/shard_map/ppermute | solution.py:36
  107.7 43.9 %all-to-all-start.2 = ((bf16[8,8,2048]{2,1,0:T(8,128)(2,1)}), bf16[8,8,2048]{2,1,0:T(8,128)(2,1)S(1)}, u32[]{:S(2)}, u32[]{:S(2)}) async-start(bf16[8,8,2048]{2,1,0:T(8,128)(2,1)} %broadcast_in_dim.16), calls=%async_computation.2 | async-start | bytes 524288 | tf_op jit(solution)/shard_map/all_to_all | solution.py:343
  151.6 11.0 %copy-start.5 = (bf16[8,8,2048]{2,1,0:T(8,128)(2,1)}, bf16[8,8,2048]{2,1,0:T(8,128)(2,1)S(1)}, u32[]{:S(2)}) copy-start(bf16[8,8,2048]{2,1,0:T(8,128)(2,1)S(1)} %all-to-all-done.2) | copy-start | bytes 786436
  151.6 10.9 %collective-permute-start.15 = (bf16[256,1024]{1,0:T(8,128)(2,1)}, bf16[256,1024]{1,0:T(8,128)(2,1)}, u32[]{:S(2)}, u32[]{:S(2)}) collective-permute-start(bf16[256,1024]{1,0:T(8,128)(2,1)} %collective-permute-done.1.mine), channel_id=1, source_target_pairs={{0,2},{1,3},{2,0},{3,1},{4,6},{5,7},{6,4},{7,5},{8,10},{9,11},{10,... | collective-permute-start | bytes 1572872 | tf_op jit(solution)/shard_map/ppermute | solution.py:300
  154.5 30.7 %collective-permute-start.18 = (bf16[512,1024]{1,0:T(8,128)(2,1)}, bf16[512,1024]{1,0:T(8,128)(2,1)}, u32[]{:S(2)}, u32[]{:S(2)}) collective-permute-start(bf16[512,1024]{1,0:T(8,128)(2,1)} %broadcast_select_fusion.1.refs_2_), channel_id=1, source_target_pairs={{8,0},{12,4},{16,24},{20,28},{9,1},{13,5},{17,25},{21,29},{10,2},{... | collective-permute-start | bytes 3145736 | tf_op jit(solution)/shard_map/ppermute | solution.py:31
  163.7 27.2 %all-to-all-start.3 = ((bf16[1,64,8,512]{3,1,0,2:T(8,128)(2,1)}), bf16[1,64,8,512]{3,1,0,2:T(8,128)(2,1)S(1)}, u32[]{:S(2)}, u32[]{:S(2)}) async-start(bf16[1,64,8,512]{3,1,0,2:T(8,128)(2,1)} %copy.15), calls=%async_computation.3 | async-start | bytes 1048576 | tf_op jit(solution)/shard_map/all_to_all | solution.py:370
  168.5 29.9 %collective-permute-start.19 = (bf16[512,1024]{1,0:T(8,128)(2,1)}, bf16[512,1024]{1,0:T(8,128)(2,1)S(1)}, u32[]{:S(2)}, u32[]{:S(2)}) collective-permute-start(bf16[512,1024]{1,0:T(8,128)(2,1)} %collective-permute-done.12.refs_2_.refs_4_), channel_id=1, source_target_pairs={{0,4},{4,0},{24,28},{28,24},{1,5},{5,1},{25,29},{29,25},{2,6},{6,2... | collective-permute-start | bytes 3145736 | tf_op jit(solution)/shard_map/ppermute | solution.py:36
  172.4 2.2 collective-permute-start.16
  172.5 2.9 collective-permute-start.17
  190.9 19.4 %collective-permute-start.20 = (bf16[256,512]{1,0:T(8,128)(2,1)}, bf16[256,512]{1,0:T(8,128)(2,1)S(1)}, u32[]{:S(2)}, u32[]{:S(2)}) collective-permute-start(bf16[256,512]{1,0:T(8,128)(2,1)} %get-tuple-element.103), channel_id=1, source_target_pairs={{0,4},{4,0},{8,12},{12,8},{16,20},{20,16},{24,28},{28,24},{1,5},{5... | collective-permute-start | bytes 786440 | tf_op jit(solution)/shard_map/ppermute | solution.py:36
  191.3 32.9 %collective-permute-start.21 = (bf16[8,64,512]{2,1,0:T(8,128)(2,1)S(1)}, bf16[8,64,512]{2,1,0:T(8,128)(2,1)S(1)}, u32[]{:S(2)}, u32[]{:S(2)}) collective-permute-start(bf16[8,64,512]{2,1,0:T(8,128)(2,1)S(1)} %bitcast.41), channel_id=1, source_target_pairs={{0,2},{1,3},{2,0},{3,1},{4,6},{5,7},{6,4},{7,5},{8,10},{9,11},{10,... | collective-permute-start | bytes 1572872 | tf_op jit(solution)/shard_map/ppermute | solution.py:300
  206.5 17.8 %collective-permute-start.23 = (bf16[256,1024]{1,0:T(8,128)(2,1)}, bf16[256,1024]{1,0:T(8,128)(2,1)S(1)}, u32[]{:S(2)}, u32[]{:S(2)}) collective-permute-start(bf16[256,1024]{1,0:T(8,128)(2,1)} %get-tuple-element.113.refs_0_), channel_id=1, source_target_pairs={{8,0},{12,4},{16,8},{20,12},{24,16},{28,20},{0,24},{4,28},{9,1},{1... | collective-permute-start | bytes 1572872 | tf_op jit(solution)/shard_map/ppermute | solution.py:31
  210.3 16.9 %collective-permute-start.24 = (bf16[256,1024]{1,0:T(8,128)(2,1)}, bf16[256,1024]{1,0:T(8,128)(2,1)}, u32[]{:S(2)}, u32[]{:S(2)}) collective-permute-start(bf16[256,1024]{1,0:T(8,128)(2,1)} %get-tuple-element.113.refs_0_), channel_id=1, source_target_pairs={{24,0},{28,4},{0,8},{4,12},{8,16},{12,20},{16,24},{20,28},{25,1},{... | collective-permute-start | bytes 1572872 | tf_op jit(solution)/shard_map/ppermute | solution.py:31
  210.3 16.9 %collective-permute-start.22 = (bf16[256,1024]{1,0:T(8,128)(2,1)}, bf16[256,1024]{1,0:T(8,128)(2,1)}, u32[]{:S(2)}, u32[]{:S(2)}) collective-permute-start(bf16[256,1024]{1,0:T(8,128)(2,1)} %get-tuple-element.113.refs_0_), channel_id=1, source_target_pairs={{0,4},{4,0},{8,12},{12,8},{16,20},{20,16},{24,28},{28,24},{1,5},{5... | collective-permute-start | bytes 1572872 | tf_op jit(solution)/shard_map/ppermute | solution.py:36
  224.2 3.0 copy-start.8
  224.3 23.6 %copy-start.2 = (bf16[2,8,64,512]{3,2,1,0:T(8,128)(2,1)}, bf16[2,8,64,512]{3,2,1,0:T(8,128)(2,1)S(1)}, u32[]{:S(2)}) copy-start(bf16[2,8,64,512]{3,2,1,0:T(8,128)(2,1)S(1)} %pad_maximum_fusion.1.own_pair) | copy-start | bytes 3145732
  224.3 18.7 %copy-start.9 = (bf16[256,1024]{1,0:T(8,128)(2,1)}, bf16[256,1024]{1,0:T(8,128)(2,1)S(1)}, u32[]{:S(2)}) copy-start(bf16[256,1024]{1,0:T(8,128)(2,1)S(1)} %collective-permute-done.23.refs_1_) | copy-start | bytes 1572868
  243.0 29.1 %all-to-all-start.6 = ((bf16[4,2,256,512]{3,2,1,0:T(8,128)(2,1)}), bf16[4,2,256,512]{3,2,1,0:T(8,128)(2,1)}, u32[]{:S(2)}, u32[]{:S(2)}) async-start(bf16[4,2,256,512]{3,2,1,0:T(8,128)(2,1)} %shard_map.108), calls=%async_computation.6 | async-start | bytes 4194304 | tf_op jit(solution)/shard_map/all_to_all | solution.py:442
  247.9 57.7 %collective-permute-start.26 = (bf16[2,8,64,512]{3,2,1,0:T(8,128)(2,1)S(1)}, bf16[2,8,64,512]{3,2,1,0:T(8,128)(2,1)}, u32[]{:S(2)}, u32[]{:S(2)}) collective-permute-start(bf16[2,8,64,512]{3,2,1,0:T(8,128)(2,1)S(1)} %pad_maximum_fusion.1.own_pair), channel_id=1, source_target_pairs={{0,1},{1,0},{2,3},{3,2},{4,5},{5,4},{6,7},{7,6},{8,9},{9,8},{10,11... | collective-permute-start | bytes 3145736 | tf_op jit(solution)/shard_map/ppermute | solution.py:300
  248.1 30.4 %collective-permute-start.25 = (bf16[256,1024]{1,0:T(8,128)(2,1)}, bf16[256,1024]{1,0:T(8,128)(2,1)}, u32[]{:S(2)}, u32[]{:S(2)}) collective-permute-start(bf16[256,1024]{1,0:T(8,128)(2,1)} %get-tuple-element.113.refs_0_), channel_id=1, source_target_pairs={{16,0},{20,4},{24,8},{28,12},{0,16},{4,20},{8,24},{12,28},{17,1},{... | collective-permute-start | bytes 1572872 | tf_op jit(solution)/shard_map/ppermute | solution.py:31
  272.8 12.7 %all-to-all-start.5 = ((bf16[8,8,2048]{2,1,0:T(8,128)(2,1)}), bf16[8,8,2048]{2,1,0:T(8,128)(2,1)S(1)}, u32[]{:S(2)}, u32[]{:S(2)}) async-start(bf16[8,8,2048]{2,1,0:T(8,128)(2,1)} %broadcast_in_dim.17), calls=%async_computation.5 | async-start | bytes 524288 | tf_op jit(solution)/shard_map/all_to_all | solution.py:343
  276.4 10.8 %copy-start.4 = (bf16[512,1024]{1,0:T(8,128)(2,1)S(1)}, bf16[512,1024]{1,0:T(8,128)(2,1)}, u32[]{:S(2)}) copy-start(bf16[512,1024]{1,0:T(8,128)(2,1)} %param.14) | copy-start | bytes 3145732
  276.4 17.9 %collective-permute-start.27 = (bf16[256,1024]{1,0:T(8,128)(2,1)}, bf16[256,1024]{1,0:T(8,128)(2,1)}, u32[]{:S(2)}, u32[]{:S(2)}) collective-permute-start(bf16[256,1024]{1,0:T(8,128)(2,1)} %copy-done.9), channel_id=1, source_target_pairs={{0,4},{4,0},{8,12},{12,8},{16,20},{20,16},{24,28},{28,24},{1,5},{5... | collective-permute-start | bytes 1572872 | tf_op jit(solution)/shard_map/ppermute | solution.py:36
  278.4 27.2 %collective-permute-start.28 = (bf16[256,1024]{1,0:T(8,128)(2,1)}, bf16[256,1024]{1,0:T(8,128)(2,1)}, u32[]{:S(2)}, u32[]{:S(2)}) collective-permute-start(bf16[256,1024]{1,0:T(8,128)(2,1)} %collective-permute-done.24.refs_2_), channel_id=1, source_target_pairs={{0,4},{4,0},{8,12},{12,8},{16,20},{20,16},{24,28},{28,24},{1,5},{5... | collective-permute-start | bytes 1572872 | tf_op jit(solution)/shard_map/ppermute | solution.py:36
  285.5 29.9 %collective-permute-start.29 = (bf16[256,1024]{1,0:T(8,128)(2,1)}, bf16[256,1024]{1,0:T(8,128)(2,1)}, u32[]{:S(2)}, u32[]{:S(2)}) collective-permute-start(bf16[256,1024]{1,0:T(8,128)(2,1)} %collective-permute-done.25.refs_1_), channel_id=1, source_target_pairs={{0,4},{4,0},{8,12},{12,8},{16,20},{20,16},{24,28},{28,24},{1,5},{5... | collective-permute-start | bytes 1572872 | tf_op jit(solution)/shard_map/ppermute | solution.py:36
  288.3 22.9 %all-to-all-start.7 = ((bf16[4,16,512]{2,1,0:T(8,128)(2,1)}), bf16[4,16,512]{2,1,0:T(8,128)(2,1)S(1)}, u32[]{:S(2)}, u32[]{:S(2)}) async-start(bf16[4,16,512]{2,1,0:T(8,128)(2,1)} %bitcast.17), calls=%async_computation.7 | async-start | bytes 131072 | tf_op jit(solution)/shard_map/all_to_all | solution.py:250
  315.4 10.5 %collective-permute-start.30 = (bf16[8,512]{1,0:T(8,128)(2,1)S(1)}, bf16[8,512]{1,0:T(8,128)(2,1)S(1)}, u32[]{:S(2)}, u32[]{:S(2)}) collective-permute-start(bf16[8,512]{1,0:T(8,128)(2,1)S(1)} %get-tuple-element.127), channel_id=1, source_target_pairs={{0,0},{1,8},{2,16},{3,24},{4,4},{5,12},{6,20},{7,28},{8,1},{9,9},{... | collective-permute-start | bytes 24584 | tf_op jit(solution)/shard_map/ppermute | solution.py:266
  320.6 6.4 %collective-permute-start.31 = (bf16[8,512]{1,0:T(8,128)(2,1)S(1)}, bf16[8,512]{1,0:T(8,128)(2,1)S(1)}, u32[]{:S(2)}, u32[]{:S(2)}) collective-permute-start(bf16[8,512]{1,0:T(8,128)(2,1)S(1)} %get-tuple-element.128), channel_id=1, source_target_pairs={{0,4},{1,12},{2,20},{3,28},{4,0},{5,8},{6,16},{7,24},{8,5},{9,13},... | collective-permute-start | bytes 24584 | tf_op jit(solution)/shard_map/ppermute | solution.py:266
  (4 other events, 4.0 us)

commit v16 on v13

--- a/solution.py
+++ b/solution.py
@@ -12,7 +12,7 @@
 BF16 = jnp.bfloat16
 BACK = (((1,), (1,)), ((), ()))
 FIRST = (((0,), (0,)), ((), ()))
-VMEM_LIMIT = 60 * 1024 * 1024
+VMEM_LIMIT = 24 * 1024 * 1024
 
 
 def matmul(a, b, dims=None):

time: 301 us -> 300 us (level)
  Pallas kernels: 45.7 us -> 34.6 us
  local copies, waits for them, and re-layouts: 13.2 us -> 19.9 us
    pallas_call x8, Pallas kernels: 45.7 us -> 34.6 us  [call(): pl.pallas_call(kernel, out_shape=outs[0] if single else outs, in_specs=[p...]
    unnamed x25 -> x45, local copies, waits for them, and re-layouts: 2.84 us -> 11.8 us
  transfers between devices with their start and end apart: 42 -> 42, of which waited for: 13 -> 13; matrix products, arithmetic and copies ran while one was open for 8% -> 7% of each run, Pallas kernels for 15% -> 12%
where the time goes in v16:
time: 300 us; the launch traced here: 299 us
  waiting for transfers between devices  126 us (42%)
  starting transfers between devices  98.7 us (33%)
  Pallas kernels  34.6 us (12%)
  local copies, waits for them, and re-layouts  19.9 us (7%)
  other arithmetic  14.8 us (5%)
  matrix products  3.32 us (1%)
    pallas_call x8, Pallas kernels, call(): pl.pallas_call(kernel, out_shape=outs[0] if single else outs, in_specs=[p...  34.6 us
    all_to_all x2, waiting for transfers between devices, everywhere(): return lax.all_to_all(copies, 'dp', split_axis=0, concat_axis=0)  32.7 us
    all_to_all x1, waiting for transfers between devices, shards(): lax.all_to_all(part_kv, 'dp', split_axis=0, concat_axis=0)  28.5 us
    ppermute x13, starting transfers between devices, move(): return lax.ppermute(block, 'dp', pairs)  27.1 us
    ppermute x12, waiting for transfers between devices, swap(): return lax.ppermute(block, 'dp', pairs)  20.1 us
    ppermute x12, starting transfers between devices, swap(): return lax.ppermute(block, 'dp', pairs)  19.7 us
    all_to_all x1, waiting for transfers between devices, shards(): lax.all_to_all(kv_part, 'dp', split_axis=0, concat_axis=0)  19.5 us
    all_to_all x2, starting transfers between devices, everywhere(): return lax.all_to_all(copies, 'dp', split_axis=0, concat_axis=0)  15.9 us
  transfers between devices with their start and end apart: 42, of which 13 were waited for; matrix products, arithmetic and copies ran while one was open for 7% of the time, Pallas kernels for 12%

profile of v16, /device:TPU:4, one launch (start us, length us, event | category | flops | bytes accessed | tf_op | source)
XLA Modules:
  0.0 298.7 jit_solution(10958923531118609101)
XLA Ops:
  2.1 5.5 %collective-permute-start.3 = (bf16[512,1024]{1,0:T(8,128)(2,1)}, bf16[512,1024]{1,0:T(8,128)(2,1)}, u32[]{:S(2)}, u32[]{:S(2)}) collective-permute-start(bf16[512,1024]{1,0:T(8,128)(2,1)} %refs_0_.1), channel_id=1, source_target_pairs={{0,8},{4,12},{8,16},{12,20},{16,24},{20,28},{1,9},{5,13},{9,17},{1... | collective-permute-start | bytes 3145736 | tf_op jit(solution)/shard_map/ppermute | solution.py:31
  7.6 2.2 constant_dynamic-slice_fusion.3
  11.4 1.8 broadcast_select_fusion
  15.4 4.8 %all-to-all-start = ((bf16[8,8,512]{2,0,1:T(8,128)(2,1)}), bf16[8,8,512]{2,0,1:T(8,128)(2,1)S(1)}, u32[]{:S(2)}, u32[]{:S(2)}) async-start(bf16[8,8,512]{2,0,1:T(8,128)(2,1)} %copy.14), calls=%async_computation | async-start | bytes 131072 | tf_op jit(solution)/shard_map/all_to_all | solution.py:313
  20.2 4.8 %collective-permute-done = bf16[512,512]{1,0:T(8,128)(2,1)} collective-permute-done((bf16[512,512]{1,0:T(8,128)(2,1)}, bf16[512,512]{1,0:T(8,128)(2,1)}, u32[]{:S(2)}, u32[]{:S(2)}) %collective-permute-start) | collective-permute-done | bytes 524320 | tf_op jit(solution)/shard_map/ppermute | solution.py:36
  25.1 2.3 pad_maximum_fusion.refs_0_
  27.3 7.8 %all-to-all-done = bf16[8,8,512]{2,0,1:T(8,128)(2,1)S(1)} async-done(((bf16[8,8,512]{2,0,1:T(8,128)(2,1)}), bf16[8,8,512]{2,0,1:T(8,128)(2,1)S(1)}, u32[]{:S(2)}, u32[]{:S(2)}) %all-to-all-start) | async-done | bytes 65568 | tf_op jit(solution)/shard_map/all_to_all | solution.py:313
  38.0 5.5 %collective-permute-start.9 = (bf16[512,1024]{1,0:T(8,128)(2,1)}, bf16[512,1024]{1,0:T(8,128)(2,1)}, u32[]{:S(2)}, u32[]{:S(2)}) collective-permute-start(bf16[512,1024]{1,0:T(8,128)(2,1)} %pad_maximum_fusion.refs_0_), channel_id=1, source_target_pairs={{0,8},{4,12},{8,16},{12,20},{16,24},{20,28},{1,9},{5,13},{9,17},{1... | collective-permute-start | bytes 3145736 | tf_op jit(solution)/shard_map/ppermute | solution.py:31
  44.8 1.7 collective-permute-start.7
  48.3 10.6 %collective-permute-done.4.refs_4_.refs_5_ = bf16[512,1024]{1,0:T(8,128)(2,1)S(1)} collective-permute-done((bf16[512,1024]{1,0:T(8,128)(2,1)}, bf16[512,1024]{1,0:T(8,128)(2,1)S(1)}, u32[]{:S(2)}, u32[]{:S(2)}) %collective-permute-start.4) | collective-permute-done | bytes 1048608 | tf_op jit(solution)/shard_map/ppermute | solution.py:36
  59.9 3.4 %collective-permute-start.5 = (bf16[512,1024]{1,0:T(8,128)(2,1)}, bf16[512,1024]{1,0:T(8,128)(2,1)}, u32[]{:S(2)}, u32[]{:S(2)}) collective-permute-start(bf16[512,1024]{1,0:T(8,128)(2,1)} %collective-permute-done.2.refs_1_), channel_id=1, source_target_pairs={{0,4},{4,0},{8,12},{12,8},{16,20},{20,16},{1,5},{5,1},{9,13},{13,9... | collective-permute-start | bytes 3145736 | tf_op jit(solution)/shard_map/ppermute | solution.py:36
  64.1 4.1 %all-to-all-start.1 = ((f32[8,8,2048]{2,1,0:T(8,128)}), f32[8,8,2048]{2,1,0:T(8,128)}, u32[]{:S(2)}, u32[]{:S(2)}) async-start(f32[8,8,2048]{2,1,0:T(8,128)} %maximum_bitcast_fusion), calls=%async_computation.1 | async-start | bytes 1048576 | tf_op jit(solution)/shard_map/all_to_all | solution.py:334
  68.3 28.5 %all-to-all-done.1 = f32[8,8,2048]{2,1,0:T(8,128)} async-done(((f32[8,8,2048]{2,1,0:T(8,128)}), f32[8,8,2048]{2,1,0:T(8,128)}, u32[]{:S(2)}, u32[]{:S(2)}) %all-to-all-start.1) | async-done | bytes 524320 | tf_op jit(solution)/shard_map/all_to_all | solution.py:334
  97.9 2.3 broadcast_select_fusion.2.refs_3_
  103.6 1.7 collective-permute-start.11
  105.2 1.7 collective-permute-start.13
  107.6 12.5 %all-to-all-start.2 = ((bf16[8,8,2048]{2,1,0:T(8,128)(2,1)}), bf16[8,8,2048]{2,1,0:T(8,128)(2,1)S(1)}, u32[]{:S(2)}, u32[]{:S(2)}) async-start(bf16[8,8,2048]{2,1,0:T(8,128)(2,1)} %broadcast_in_dim.16), calls=%async_computation.2 | async-start | bytes 524288 | tf_op jit(solution)/shard_map/all_to_all | solution.py:343
  120.1 31.4 %all-to-all-done.2 = bf16[8,8,2048]{2,1,0:T(8,128)(2,1)S(1)} async-done(((bf16[8,8,2048]{2,1,0:T(8,128)(2,1)}), bf16[8,8,2048]{2,1,0:T(8,128)(2,1)S(1)}, u32[]{:S(2)}, u32[]{:S(2)}) %all-to-all-start.2) | async-done | bytes 262176 | tf_op jit(solution)/shard_map/all_to_all | solution.py:343
  151.6 2.4 broadcast_select_fusion.1.refs_2_
  157.0 8.0 %all-to-all-start.3 = ((bf16[1,64,8,512]{3,1,0,2:T(8,128)(2,1)}), bf16[1,64,8,512]{3,1,0,2:T(8,128)(2,1)}, u32[]{:S(2)}, u32[]{:S(2)}) async-start(bf16[1,64,8,512]{3,1,0,2:T(8,128)(2,1)} %copy.15), calls=%async_computation.3 | async-start | bytes 1048576 | tf_op jit(solution)/shard_map/all_to_all | solution.py:359
  165.0 3.9 %collective-permute-start.19 = (bf16[512,1024]{1,0:T(8,128)(2,1)}, bf16[512,1024]{1,0:T(8,128)(2,1)}, u32[]{:S(2)}, u32[]{:S(2)}) collective-permute-start(bf16[512,1024]{1,0:T(8,128)(2,1)} %collective-permute-done.12.refs_0_.refs_4_), channel_id=1, source_target_pairs={{0,4},{4,0},{24,28},{28,24},{1,5},{5,1},{25,29},{29,25},{2,6},{6,2... | collective-permute-start | bytes 3145736 | tf_op jit(solution)/shard_map/ppermute | solution.py:36
  169.5 1.6 copy-done.1
  173.6 5.2 %shard_map.103.part = f32[256,1024]{1,0:T(8,128)S(1)} custom-call(s32[4]{0:T(128)S(1)} %pad_add_fusion.place, bf16[256,4096]{1,0:T(8,128)(2,1)S(1)} %bitcast.42, bf16[512,1024]{1,0:T(8,128)(2,1)S(1)} %copy-done.3, bf16[512,1024]{1,0:T(8,128)(2,1)} %collective-permute-done.2.refs_1_, bf16[512,1024]{1,0:T(8,128)(2,1)} %collective-permute-done.3.refs_2_, ...), custom_call_target="tpu_custom_call" | custom-call | flops 2147483648 | bytes 11534336 | tf_op jit(solution)/shard_map/pallas_call | solution.py:228
  178.8 4.3 %shard_map.104 = (f32[256,512]{1,0:T(8,128)S(1)}, f32[256,512]{1,0:T(8,128)S(1)}) custom-call(s32[4]{0:T(128)S(1)} %pad_add_fusion.place, bf16[256,4096]{1,0:T(8,128)(2,1)S(1)} %bitcast.40, bf16[256,1024]{1,0:T(8,128)(2,1)} %collective-permute-done.1.mine, bf16[256,1024]{1,0:T(8,128)(2,1)} %collective-permute-done.15.by_core, ...), custom_call_target="tpu_custom_call" | custom-call | flops 1073741824 | bytes 8388608 | tf_op jit(solution)/shard_map/pallas_call | solution.py:228
  183.1 1.8 collective-permute-done.18.refs_3_
  184.9 4.0 %shard_map.105 = (bf16[256,512]{1,0:T(8,128)(2,1)S(1)}, bf16[256,512]{1,0:T(8,128)(2,1)S(1)}) custom-call(s32[4]{0:T(128)S(1)} %pad_add_fusion.place, bf16[256,4096]{1,0:T(8,128)(2,1)S(1)} %bitcast.41, bf16[256,1024]{1,0:T(8,128)(2,1)} %collective-permute-done.1.mine, bf16[256,1024]{1,0:T(8,128)(2,1)} %collective-permute-done.15.by_core, ...), custom_call_target="tpu_custom_call" | custom-call | flops 1073741824 | bytes 7864320 | tf_op jit(solution)/shard_map/pallas_call | solution.py:228
  190.7 2.3 collective-permute-done.19.refs_1_.refs_9_
  193.0 1.6 copy-done.2
  195.8 4.3 %shard_map.106 = (bf16[256,1024]{1,0:T(8,128)(2,1)S(1)}, bf16[256,1024]{1,0:T(8,128)(2,1)}) custom-call(s32[4]{0:T(128)S(1)} %pad_add_fusion.place, bf16[256,4096]{1,0:T(8,128)(2,1)S(1)} %bitcast.43, bf16[64,2048]{1,0:T(8,128)(2,1)S(1)} %bitcast.44, f32[256,1024]{1,0:T(8,128)S(1)} %copy-done.9, bf16[512,1024]{1,0:T(8,128)(2,1)} %collective-permute-done.12.refs_0_.refs_4_, ...), custom_call_target="tpu_custom_call" | custom-call | flops 1073741824 | bytes 6553600 | tf_op jit(solution)/shard_map/pallas_call | solution.py:228
  200.1 1.8 collective-permute-start.23
  203.7 2.5 collective-permute-start.22
  206.2 1.9 shard_map.107
  208.8 6.7 %shard_map.108.term = bf16[4,2,256,512]{3,2,1,0:T(8,128)(2,1)S(1)} custom-call(s32[4]{0:T(128)S(1)} %pad_add_fusion.place, bf16[256,1024]{1,0:T(8,128)(2,1)S(1)} %get-tuple-element.113.query_grad, bf16[512,1024]{1,0:T(8,128)(2,1)S(1)} %copy-done.4, bf16[512,1024]{1,0:T(8,128)(2,1)} %collective-permute-done.2.refs_1_, ...), custom_call_target="tpu_custom_call" | custom-call | flops 2147483648 | bytes 13107200 | tf_op jit(solution)/shard_map/pallas_call | solution.py:228
  215.6 7.7 %collective-permute-done.24.refs_5_ = bf16[256,1024]{1,0:T(8,128)(2,1)} collective-permute-done((bf16[256,1024]{1,0:T(8,128)(2,1)}, bf16[256,1024]{1,0:T(8,128)(2,1)}, u32[]{:S(2)}, u32[]{:S(2)}) %collective-permute-start.24) | collective-permute-done | bytes 524320 | tf_op jit(solution)/shard_map/ppermute | solution.py:31
  224.9 4.1 %all-to-all-start.4 = ((f32[8,8,2048]{2,1,0:T(8,128)}), f32[8,8,2048]{2,1,0:T(8,128)}, u32[]{:S(2)}, u32[]{:S(2)}) async-start(f32[8,8,2048]{2,1,0:T(8,128)} %bitcast.46), calls=%async_computation.4 | async-start | bytes 1048576 | tf_op jit(solution)/shard_map/all_to_all | solution.py:441
  231.3 1.9 collective-permute-start.25
  233.3 2.8 collective-permute-start.29
  236.1 19.5 %all-to-all-done.4 = f32[8,8,2048]{2,1,0:T(8,128)} async-done(((f32[8,8,2048]{2,1,0:T(8,128)}), f32[8,8,2048]{2,1,0:T(8,128)}, u32[]{:S(2)}, u32[]{:S(2)}) %all-to-all-start.4) | async-done | bytes 524320 | tf_op jit(solution)/shard_map/all_to_all | solution.py:441
  257.4 3.4 %all-to-all-start.5 = ((bf16[8,8,2048]{2,1,0:T(8,128)(2,1)}), bf16[8,8,2048]{2,1,0:T(8,128)(2,1)S(1)}, u32[]{:S(2)}, u32[]{:S(2)}) async-start(bf16[8,8,2048]{2,1,0:T(8,128)(2,1)} %broadcast_in_dim.17), calls=%async_computation.5 | async-start | bytes 524288 | tf_op jit(solution)/shard_map/all_to_all | solution.py:343
  260.8 2.3 pad_maximum_fusion.1.refs_0_
  263.1 5.8 %collective-permute-done.29.refs_4_ = bf16[256,1024]{1,0:T(8,128)(2,1)} collective-permute-done((bf16[256,1024]{1,0:T(8,128)(2,1)}, bf16[256,1024]{1,0:T(8,128)(2,1)}, u32[]{:S(2)}, u32[]{:S(2)}) %collective-permute-start.29) | collective-permute-done | bytes 524320 | tf_op jit(solution)/shard_map/ppermute | solution.py:31
  274.4 4.0 %all-to-all-start.6 = ((bf16[4,16,512]{2,1,0:T(8,128)(2,1)}), bf16[4,16,512]{2,1,0:T(8,128)(2,1)S(1)}, u32[]{:S(2)}, u32[]{:S(2)}) async-start(bf16[4,16,512]{2,1,0:T(8,128)(2,1)} %bitcast.19), calls=%async_computation.6 | async-start | bytes 131072 | tf_op jit(solution)/shard_map/all_to_all | solution.py:250
  278.4 2.3 all-to-all-done.6
  280.8 2.5 shard_map.109
  283.3 2.3 collective-permute-done.32.refs_8_
  285.6 3.2 %collective-permute-start.33 = (bf16[8,512]{1,0:T(8,128)(2,1)S(1)}, bf16[8,512]{1,0:T(8,128)(2,1)S(1)}, u32[]{:S(2)}, u32[]{:S(2)}) collective-permute-start(bf16[8,512]{1,0:T(8,128)(2,1)S(1)} %get-tuple-element.139), channel_id=1, source_target_pairs={{0,0},{1,8},{2,16},{3,24},{4,4},{5,12},{6,20},{7,28},{8,1},{9,9},{... | collective-permute-start | bytes 24584 | tf_op jit(solution)/shard_map/ppermute | solution.py:266
  288.8 3.5 %collective-permute-start.34 = (bf16[8,512]{1,0:T(8,128)(2,1)S(1)}, bf16[8,512]{1,0:T(8,128)(2,1)S(1)}, u32[]{:S(2)}, u32[]{:S(2)}) collective-permute-start(bf16[8,512]{1,0:T(8,128)(2,1)S(1)} %get-tuple-element.140), channel_id=1, source_target_pairs={{0,4},{1,12},{2,20},{3,28},{4,0},{5,8},{6,16},{7,24},{8,5},{9,13},... | collective-permute-start | bytes 24584 | tf_op jit(solution)/shard_map/ppermute | solution.py:266
  292.3 5.7 %shard_map.110 = bf16[1024,512]{1,0:T(8,128)(2,1)} custom-call(s32[4]{0:T(128)S(1)} %pad_add_fusion.place, bf16[2,8,64,512]{3,2,1,0:T(8,128)(2,1)S(1)} %copy-done.11, bf16[2,8,64,512]{3,2,1,0:T(8,128)(2,1)} %collective-permute-done.30.refs_1_, bf16[256,1024]{1,0:T(8,128)(2,1)} %get-tuple-element.121.refs_2_, ...), custom_call_target="tpu_custom_call" | custom-call | flops 2147483648 | bytes 7340032 | tf_op jit(solution)/shard_map/pallas_call | solution.py:228
  (119 shorter events, 41.6 us)
Async XLA Ops:
  0.6 47.4 %copy-start = (bf16[512,1024]{1,0:T(8,128)(2,1)S(1)}, bf16[512,1024]{1,0:T(8,128)(2,1)}, u32[]{:S(2)}) copy-start(bf16[512,1024]{1,0:T(8,128)(2,1)} %param.14) | copy-start | bytes 3145732
  0.6 10.7 %copy-start.21 = (s32[2]{0:T(128)S(1)}, s32[2]{0:T(128)}, u32[]{:S(2)}) copy-start(s32[2]{0:T(128)} %param.11) | copy-start | bytes 28
  0.7 34.5 %collective-permute-start.2 = (bf16[512,1024]{1,0:T(8,128)(2,1)}, bf16[512,1024]{1,0:T(8,128)(2,1)}, u32[]{:S(2)}, u32[]{:S(2)}) collective-permute-start(bf16[512,1024]{1,0:T(8,128)(2,1)} %refs_0_.1), channel_id=1, source_target_pairs={{8,0},{12,4},{16,8},{20,12},{24,16},{28,20},{9,1},{13,5},{17,9},{2... | collective-permute-start | bytes 3145736 | tf_op jit(solution)/shard_map/ppermute | solution.py:31
  2.1 33.1 %collective-permute-start.3 = (bf16[512,1024]{1,0:T(8,128)(2,1)}, bf16[512,1024]{1,0:T(8,128)(2,1)}, u32[]{:S(2)}, u32[]{:S(2)}) collective-permute-start(bf16[512,1024]{1,0:T(8,128)(2,1)} %refs_0_.1), channel_id=1, source_target_pairs={{0,8},{4,12},{8,16},{12,20},{16,24},{20,28},{1,9},{5,13},{9,17},{1... | collective-permute-start | bytes 3145736 | tf_op jit(solution)/shard_map/ppermute | solution.py:31
  9.9 15.2 %collective-permute-start = (bf16[512,512]{1,0:T(8,128)(2,1)}, bf16[512,512]{1,0:T(8,128)(2,1)}, u32[]{:S(2)}, u32[]{:S(2)}) collective-permute-start(bf16[512,512]{1,0:T(8,128)(2,1)} %get-tuple-element.138), channel_id=1, source_target_pairs={{0,4},{4,0},{8,12},{12,8},{16,20},{20,16},{24,28},{28,24},{1,5},{5... | collective-permute-start | bytes 1572872 | tf_op jit(solution)/shard_map/ppermute | solution.py:36
  14.1 21.0 %collective-permute-start.1 = (bf16[256,1024]{1,0:T(8,128)(2,1)}, bf16[256,1024]{1,0:T(8,128)(2,1)}, u32[]{:S(2)}, u32[]{:S(2)}) collective-permute-start(bf16[256,1024]{1,0:T(8,128)(2,1)} %constant_dynamic-slice_fusion.1), channel_id=1, source_target_pairs={{0,4},{4,0},{8,12},{12,8},{16,20},{20,16},{24,28},{28,24},{1,5},{5... | collective-permute-start | bytes 1572872 | tf_op jit(solution)/shard_map/ppermute | solution.py:36
  15.4 19.8 %all-to-all-start = ((bf16[8,8,512]{2,0,1:T(8,128)(2,1)}), bf16[8,8,512]{2,0,1:T(8,128)(2,1)S(1)}, u32[]{:S(2)}, u32[]{:S(2)}) async-start(bf16[8,8,512]{2,0,1:T(8,128)(2,1)} %copy.14), calls=%async_computation | async-start | bytes 131072 | tf_op jit(solution)/shard_map/all_to_all | solution.py:313
  35.2 23.8 %collective-permute-start.4 = (bf16[512,1024]{1,0:T(8,128)(2,1)}, bf16[512,1024]{1,0:T(8,128)(2,1)S(1)}, u32[]{:S(2)}, u32[]{:S(2)}) collective-permute-start(bf16[512,1024]{1,0:T(8,128)(2,1)} %refs_0_.1), channel_id=1, source_target_pairs={{0,4},{4,0},{8,12},{12,8},{16,20},{20,16},{24,28},{28,24},{1,5},{5... | collective-permute-start | bytes 3145736 | tf_op jit(solution)/shard_map/ppermute | solution.py:36
  36.7 61.1 %collective-permute-start.8 = (bf16[512,1024]{1,0:T(8,128)(2,1)}, bf16[512,1024]{1,0:T(8,128)(2,1)}, u32[]{:S(2)}, u32[]{:S(2)}) collective-permute-start(bf16[512,1024]{1,0:T(8,128)(2,1)} %pad_maximum_fusion.refs_0_), channel_id=1, source_target_pairs={{8,0},{12,4},{16,8},{20,12},{24,16},{28,20},{9,1},{13,5},{17,9},{2... | collective-permute-start | bytes 3145736 | tf_op jit(solution)/shard_map/ppermute | solution.py:31
  38.0 59.9 %collective-permute-start.9 = (bf16[512,1024]{1,0:T(8,128)(2,1)}, bf16[512,1024]{1,0:T(8,128)(2,1)}, u32[]{:S(2)}, u32[]{:S(2)}) collective-permute-start(bf16[512,1024]{1,0:T(8,128)(2,1)} %pad_maximum_fusion.refs_0_), channel_id=1, source_target_pairs={{0,8},{4,12},{8,16},{12,20},{16,24},{20,28},{1,9},{5,13},{9,17},{1... | collective-permute-start | bytes 3145736 | tf_op jit(solution)/shard_map/ppermute | solution.py:31
  43.5 54.3 %collective-permute-start.6 = (bf16[512,1024]{1,0:T(8,128)(2,1)}, bf16[512,1024]{1,0:T(8,128)(2,1)}, u32[]{:S(2)}, u32[]{:S(2)}) collective-permute-start(bf16[512,1024]{1,0:T(8,128)(2,1)} %collective-permute-done.2.refs_1_), channel_id=1, source_target_pairs={{8,0},{12,4},{16,8},{20,12},{9,1},{13,5},{17,9},{21,13},{10,2},{14... | collective-permute-start | bytes 3145736 | tf_op jit(solution)/shard_map/ppermute | solution.py:31
  44.8 53.0 %collective-permute-start.7 = (bf16[512,1024]{1,0:T(8,128)(2,1)}, bf16[512,1024]{1,0:T(8,128)(2,1)}, u32[]{:S(2)}, u32[]{:S(2)}) collective-permute-start(bf16[512,1024]{1,0:T(8,128)(2,1)} %collective-permute-done.3.refs_2_), channel_id=1, source_target_pairs={{8,16},{12,20},{16,24},{20,28},{9,17},{13,21},{17,25},{21,29},{10,... | collective-permute-start | bytes 3145736 | tf_op jit(solution)/shard_map/ppermute | solution.py:31
  59.9 38.0 %collective-permute-start.5 = (bf16[512,1024]{1,0:T(8,128)(2,1)}, bf16[512,1024]{1,0:T(8,128)(2,1)}, u32[]{:S(2)}, u32[]{:S(2)}) collective-permute-start(bf16[512,1024]{1,0:T(8,128)(2,1)} %collective-permute-done.2.refs_1_), channel_id=1, source_target_pairs={{0,4},{4,0},{8,12},{12,8},{16,20},{20,16},{1,5},{5,1},{9,13},{13,9... | collective-permute-start | bytes 3145736 | tf_op jit(solution)/shard_map/ppermute | solution.py:36
  64.1 32.6 %all-to-all-start.1 = ((f32[8,8,2048]{2,1,0:T(8,128)}), f32[8,8,2048]{2,1,0:T(8,128)}, u32[]{:S(2)}, u32[]{:S(2)}) async-start(f32[8,8,2048]{2,1,0:T(8,128)} %maximum_bitcast_fusion), calls=%async_computation.1 | async-start | bytes 1048576 | tf_op jit(solution)/shard_map/all_to_all | solution.py:334
  100.2 51.4 %collective-permute-start.12 = (bf16[512,1024]{1,0:T(8,128)(2,1)}, bf16[512,1024]{1,0:T(8,128)(2,1)}, u32[]{:S(2)}, u32[]{:S(2)}) collective-permute-start(bf16[512,1024]{1,0:T(8,128)(2,1)} %broadcast_select_fusion.2.refs_3_), channel_id=1, source_target_pairs={{8,0},{12,4},{16,24},{20,28},{9,1},{13,5},{17,25},{21,29},{10,2},{... | collective-permute-start | bytes 3145736 | tf_op jit(solution)/shard_map/ppermute | solution.py:31
  101.5 50.1 %collective-permute-start.14 = (bf16[512,1024]{1,0:T(8,128)(2,1)}, bf16[512,1024]{1,0:T(8,128)(2,1)}, u32[]{:S(2)}, u32[]{:S(2)}) collective-permute-start(bf16[512,1024]{1,0:T(8,128)(2,1)} %broadcast_select_fusion.2.refs_3_), channel_id=1, source_target_pairs={{0,4},{4,0},{8,12},{12,8},{16,20},{20,16},{24,28},{28,24},{1,5},{5... | collective-permute-start | bytes 3145736 | tf_op jit(solution)/shard_map/ppermute | solution.py:36
  102.3 49.3 %collective-permute-start.10 = (bf16[512,1024]{1,0:T(8,128)(2,1)}, bf16[512,1024]{1,0:T(8,128)(2,1)}, u32[]{:S(2)}, u32[]{:S(2)}) collective-permute-start(bf16[512,1024]{1,0:T(8,128)(2,1)} %collective-permute-done.8.refs_1_), channel_id=1, source_target_pairs={{8,0},{12,4},{16,8},{20,12},{9,1},{13,5},{17,9},{21,13},{10,2},{14... | collective-permute-start | bytes 3145736 | tf_op jit(solution)/shard_map/ppermute | solution.py:31
  103.6 48.0 %collective-permute-start.11 = (bf16[512,1024]{1,0:T(8,128)(2,1)}, bf16[512,1024]{1,0:T(8,128)(2,1)}, u32[]{:S(2)}, u32[]{:S(2)}) collective-permute-start(bf16[512,1024]{1,0:T(8,128)(2,1)} %collective-permute-done.9.refs_2_), channel_id=1, source_target_pairs={{8,16},{12,20},{16,24},{20,28},{9,17},{13,21},{17,25},{21,29},{10,... | collective-permute-start | bytes 3145736 | tf_op jit(solution)/shard_map/ppermute | solution.py:31
  105.2 46.3 %collective-permute-start.13 = (bf16[512,1024]{1,0:T(8,128)(2,1)}, bf16[512,1024]{1,0:T(8,128)(2,1)}, u32[]{:S(2)}, u32[]{:S(2)}) collective-permute-start(bf16[512,1024]{1,0:T(8,128)(2,1)} %collective-permute-done.3.refs_2_), channel_id=1, source_target_pairs={{8,12},{12,8},{16,20},{20,16},{24,28},{28,24},{9,13},{13,9},{17,21... | collective-permute-start | bytes 3145736 | tf_op jit(solution)/shard_map/ppermute | solution.py:36
  107.6 43.9 %all-to-all-start.2 = ((bf16[8,8,2048]{2,1,0:T(8,128)(2,1)}), bf16[8,8,2048]{2,1,0:T(8,128)(2,1)S(1)}, u32[]{:S(2)}, u32[]{:S(2)}) async-start(bf16[8,8,2048]{2,1,0:T(8,128)(2,1)} %broadcast_in_dim.16), calls=%async_computation.2 | async-start | bytes 524288 | tf_op jit(solution)/shard_map/all_to_all | solution.py:343
  154.0 31.0 %collective-permute-start.18 = (bf16[512,1024]{1,0:T(8,128)(2,1)}, bf16[512,1024]{1,0:T(8,128)(2,1)}, u32[]{:S(2)}, u32[]{:S(2)}) collective-permute-start(bf16[512,1024]{1,0:T(8,128)(2,1)} %broadcast_select_fusion.1.refs_2_), channel_id=1, source_target_pairs={{8,0},{12,4},{16,24},{20,28},{9,1},{13,5},{17,25},{21,29},{10,2},{... | collective-permute-start | bytes 3145736 | tf_op jit(solution)/shard_map/ppermute | solution.py:31
  155.2 13.7 %collective-permute-start.16 = (bf16[256,1024]{1,0:T(8,128)(2,1)}, bf16[256,1024]{1,0:T(8,128)(2,1)}, u32[]{:S(2)}, u32[]{:S(2)}) collective-permute-start(bf16[256,1024]{1,0:T(8,128)(2,1)} %collective-permute-done.1.mine), channel_id=1, source_target_pairs={{0,2},{1,3},{2,0},{3,1},{4,6},{5,7},{6,4},{7,5},{8,10},{9,11},{10,... | collective-permute-start | bytes 1572872 | tf_op jit(solution)/shard_map/ppermute | solution.py:300
  157.0 33.3 %all-to-all-start.3 = ((bf16[1,64,8,512]{3,1,0,2:T(8,128)(2,1)}), bf16[1,64,8,512]{3,1,0,2:T(8,128)(2,1)}, u32[]{:S(2)}, u32[]{:S(2)}) async-start(bf16[1,64,8,512]{3,1,0,2:T(8,128)(2,1)} %copy.15), calls=%async_computation.3 | async-start | bytes 1048576 | tf_op jit(solution)/shard_map/all_to_all | solution.py:359
  165.0 28.0 %collective-permute-start.19 = (bf16[512,1024]{1,0:T(8,128)(2,1)}, bf16[512,1024]{1,0:T(8,128)(2,1)}, u32[]{:S(2)}, u32[]{:S(2)}) collective-permute-start(bf16[512,1024]{1,0:T(8,128)(2,1)} %collective-permute-done.12.refs_0_.refs_4_), channel_id=1, source_target_pairs={{0,4},{4,0},{24,28},{28,24},{1,5},{5,1},{25,29},{29,25},{2,6},{6,2... | collective-permute-start | bytes 3145736 | tf_op jit(solution)/shard_map/ppermute | solution.py:36
  168.9 9.9 %collective-permute-start.15 = (bf16[256,1024]{1,0:T(8,128)(2,1)}, bf16[256,1024]{1,0:T(8,128)(2,1)}, u32[]{:S(2)}, u32[]{:S(2)}) collective-permute-start(bf16[256,1024]{1,0:T(8,128)(2,1)} %collective-permute-done.1.mine), channel_id=1, source_target_pairs={{0,1},{1,0},{2,3},{3,2},{4,5},{5,4},{6,7},{7,6},{8,9},{9,8},{10,11... | collective-permute-start | bytes 1572872 | tf_op jit(solution)/shard_map/ppermute | solution.py:300
  169.0 9.9 %collective-permute-start.17 = (bf16[256,1024]{1,0:T(8,128)(2,1)}, bf16[256,1024]{1,0:T(8,128)(2,1)}, u32[]{:S(2)}, u32[]{:S(2)}) collective-permute-start(bf16[256,1024]{1,0:T(8,128)(2,1)} %collective-permute-done.16.by_y), channel_id=1, source_target_pairs={{0,1},{1,0},{2,3},{3,2},{4,5},{5,4},{6,7},{7,6},{8,9},{9,8},{10,11... | collective-permute-start | bytes 1572872 | tf_op jit(solution)/shard_map/ppermute | solution.py:300
  190.3 13.4 %collective-permute-start.20 = (bf16[256,512]{1,0:T(8,128)(2,1)}, bf16[256,512]{1,0:T(8,128)(2,1)S(1)}, u32[]{:S(2)}, u32[]{:S(2)}) collective-permute-start(bf16[256,512]{1,0:T(8,128)(2,1)} %copy-done.17), channel_id=1, source_target_pairs={{0,4},{4,0},{8,12},{12,8},{16,20},{20,16},{24,28},{28,24},{1,5},{5... | collective-permute-start | bytes 786440 | tf_op jit(solution)/shard_map/ppermute | solution.py:36
  195.8 13.0 %copy-start.4 = (bf16[512,1024]{1,0:T(8,128)(2,1)S(1)}, bf16[512,1024]{1,0:T(8,128)(2,1)}, u32[]{:S(2)}) copy-start(bf16[512,1024]{1,0:T(8,128)(2,1)} %refs_0_.1) | copy-start | bytes 3145732
  195.8 13.0 %copy-start.7 = (bf16[512,1024]{1,0:T(8,128)(2,1)S(1)}, bf16[512,1024]{1,0:T(8,128)(2,1)}, u32[]{:S(2)}) copy-start(bf16[512,1024]{1,0:T(8,128)(2,1)} %copy-done.5) | copy-start | bytes 3145732
  200.1 15.5 %collective-permute-start.23 = (bf16[256,1024]{1,0:T(8,128)(2,1)}, bf16[256,1024]{1,0:T(8,128)(2,1)}, u32[]{:S(2)}, u32[]{:S(2)}) collective-permute-start(bf16[256,1024]{1,0:T(8,128)(2,1)} %get-tuple-element.121.refs_2_), channel_id=1, source_target_pairs={{8,0},{12,4},{16,8},{20,12},{24,16},{28,20},{0,24},{4,28},{9,1},{1... | collective-permute-start | bytes 1572872 | tf_op jit(solution)/shard_map/ppermute | solution.py:31
  202.0 21.4 %collective-permute-start.24 = (bf16[256,1024]{1,0:T(8,128)(2,1)}, bf16[256,1024]{1,0:T(8,128)(2,1)}, u32[]{:S(2)}, u32[]{:S(2)}) collective-permute-start(bf16[256,1024]{1,0:T(8,128)(2,1)} %get-tuple-element.121.refs_2_), channel_id=1, source_target_pairs={{24,0},{28,4},{0,8},{4,12},{8,16},{12,20},{16,24},{20,28},{25,1},{... | collective-permute-start | bytes 1572872 | tf_op jit(solution)/shard_map/ppermute | solution.py:31
  202.2 21.2 %collective-permute-start.21 = (bf16[8,64,512]{2,1,0:T(8,128)(2,1)}, bf16[8,64,512]{2,1,0:T(8,128)(2,1)S(1)}, u32[]{:S(2)}, u32[]{:S(2)}) collective-permute-start(bf16[8,64,512]{2,1,0:T(8,128)(2,1)} %bitcast.12), channel_id=1, source_target_pairs={{0,2},{1,3},{2,0},{3,1},{4,6},{5,7},{6,4},{7,5},{8,10},{9,11},{10,... | collective-permute-start | bytes 1572872 | tf_op jit(solution)/shard_map/ppermute | solution.py:300
  203.7 19.6 %collective-permute-start.22 = (bf16[256,1024]{1,0:T(8,128)(2,1)}, bf16[256,1024]{1,0:T(8,128)(2,1)S(1)}, u32[]{:S(2)}, u32[]{:S(2)}) collective-permute-start(bf16[256,1024]{1,0:T(8,128)(2,1)} %get-tuple-element.121.refs_2_), channel_id=1, source_target_pairs={{0,4},{4,0},{8,12},{12,8},{16,20},{20,16},{24,28},{28,24},{1,5},{5... | collective-permute-start | bytes 1572872 | tf_op jit(solution)/shard_map/ppermute | solution.py:36
  224.9 30.6 %all-to-all-start.4 = ((f32[8,8,2048]{2,1,0:T(8,128)}), f32[8,8,2048]{2,1,0:T(8,128)}, u32[]{:S(2)}, u32[]{:S(2)}) async-start(f32[8,8,2048]{2,1,0:T(8,128)} %bitcast.46), calls=%async_computation.4 | async-start | bytes 1048576 | tf_op jit(solution)/shard_map/all_to_all | solution.py:441
  230.1 32.9 %collective-permute-start.27 = (bf16[2,256,512]{2,1,0:T(8,128)(2,1)}, bf16[2,256,512]{2,1,0:T(8,128)(2,1)}, u32[]{:S(2)}, u32[]{:S(2)}) collective-permute-start(bf16[2,256,512]{2,1,0:T(8,128)(2,1)} %get-tuple-element.136), channel_id=1, source_target_pairs={{0,2},{1,3},{2,0},{3,1},{4,6},{5,7},{6,4},{7,5},{8,10},{9,11},{10,... | collective-permute-start | bytes 1572872 | tf_op jit(solution)/shard_map/ppermute | solution.py:300
  231.3 31.8 %collective-permute-start.28 = (bf16[2,256,512]{2,1,0:T(8,128)(2,1)}, bf16[2,256,512]{2,1,0:T(8,128)(2,1)}, u32[]{:S(2)}, u32[]{:S(2)}) collective-permute-start(bf16[2,256,512]{2,1,0:T(8,128)(2,1)} %get-tuple-element.135), channel_id=1, source_target_pairs={{0,3},{1,2},{2,1},{3,0},{4,7},{5,6},{6,5},{7,4},{8,11},{9,10},{10,... | collective-permute-start | bytes 1572872 | tf_op jit(solution)/shard_map/ppermute | solution.py:300
  231.3 31.8 %collective-permute-start.25 = (bf16[256,1024]{1,0:T(8,128)(2,1)}, bf16[256,1024]{1,0:T(8,128)(2,1)}, u32[]{:S(2)}, u32[]{:S(2)}) collective-permute-start(bf16[256,1024]{1,0:T(8,128)(2,1)} %collective-permute-done.23.refs_3_), channel_id=1, source_target_pairs={{0,4},{4,0},{8,12},{12,8},{16,20},{20,16},{24,28},{28,24},{1,5},{5... | collective-permute-start | bytes 1572872 | tf_op jit(solution)/shard_map/ppermute | solution.py:36
  233.2 29.9 %collective-permute-start.26 = (bf16[256,1024]{1,0:T(8,128)(2,1)}, bf16[256,1024]{1,0:T(8,128)(2,1)}, u32[]{:S(2)}, u32[]{:S(2)}) collective-permute-start(bf16[256,1024]{1,0:T(8,128)(2,1)} %collective-permute-done.24.refs_5_), channel_id=1, source_target_pairs={{0,4},{4,0},{8,12},{12,8},{16,20},{20,16},{24,28},{28,24},{1,5},{5... | collective-permute-start | bytes 1572872 | tf_op jit(solution)/shard_map/ppermute | solution.py:36
  233.3 35.5 %collective-permute-start.29 = (bf16[256,1024]{1,0:T(8,128)(2,1)}, bf16[256,1024]{1,0:T(8,128)(2,1)}, u32[]{:S(2)}, u32[]{:S(2)}) collective-permute-start(bf16[256,1024]{1,0:T(8,128)(2,1)} %get-tuple-element.121.refs_2_), channel_id=1, source_target_pairs={{16,0},{20,4},{24,8},{28,12},{0,16},{4,20},{8,24},{12,28},{17,1},{... | collective-permute-start | bytes 1572872 | tf_op jit(solution)/shard_map/ppermute | solution.py:31
  257.4 12.8 %all-to-all-start.5 = ((bf16[8,8,2048]{2,1,0:T(8,128)(2,1)}), bf16[8,8,2048]{2,1,0:T(8,128)(2,1)S(1)}, u32[]{:S(2)}, u32[]{:S(2)}) async-start(bf16[8,8,2048]{2,1,0:T(8,128)(2,1)} %broadcast_in_dim.17), calls=%async_computation.5 | async-start | bytes 524288 | tf_op jit(solution)/shard_map/all_to_all | solution.py:343
  270.1 15.5 %collective-permute-start.30 = (bf16[2,8,64,512]{3,2,1,0:T(8,128)(2,1)}, bf16[2,8,64,512]{3,2,1,0:T(8,128)(2,1)}, u32[]{:S(2)}, u32[]{:S(2)}) collective-permute-start(bf16[2,8,64,512]{3,2,1,0:T(8,128)(2,1)} %pad_maximum_fusion.1.refs_0_), channel_id=1, source_target_pairs={{0,1},{1,0},{2,3},{3,2},{4,5},{5,4},{6,7},{7,6},{8,9},{9,8},{10,11... | collective-permute-start | bytes 3145736 | tf_op jit(solution)/shard_map/ppermute | solution.py:300
  271.0 9.8 %collective-permute-start.31 = (bf16[2,256,512]{2,1,0:T(8,128)(2,1)}, bf16[2,256,512]{2,1,0:T(8,128)(2,1)}, u32[]{:S(2)}, u32[]{:S(2)}) collective-permute-start(bf16[2,256,512]{2,1,0:T(8,128)(2,1)} %slice_bitcast_fusion), channel_id=1, source_target_pairs={{0,1},{1,0},{2,3},{3,2},{4,5},{5,4},{6,7},{7,6},{8,9},{9,8},{10,11... | collective-permute-start | bytes 1572872 | tf_op jit(solution)/shard_map/ppermute | solution.py:300
  271.5 14.1 %collective-permute-start.32 = (bf16[256,1024]{1,0:T(8,128)(2,1)}, bf16[256,1024]{1,0:T(8,128)(2,1)}, u32[]{:S(2)}, u32[]{:S(2)}) collective-permute-start(bf16[256,1024]{1,0:T(8,128)(2,1)} %collective-permute-done.29.refs_4_), channel_id=1, source_target_pairs={{0,4},{4,0},{8,12},{12,8},{16,20},{20,16},{24,28},{28,24},{1,5},{5... | collective-permute-start | bytes 1572872 | tf_op jit(solution)/shard_map/ppermute | solution.py:36
  274.4 6.3 %all-to-all-start.6 = ((bf16[4,16,512]{2,1,0:T(8,128)(2,1)}), bf16[4,16,512]{2,1,0:T(8,128)(2,1)S(1)}, u32[]{:S(2)}, u32[]{:S(2)}) async-start(bf16[4,16,512]{2,1,0:T(8,128)(2,1)} %bitcast.19), calls=%async_computation.6 | async-start | bytes 131072 | tf_op jit(solution)/shard_map/all_to_all | solution.py:250
  280.7 11.6 %copy-start.11 = (bf16[2,8,64,512]{3,2,1,0:T(8,128)(2,1)S(1)}, bf16[2,8,64,512]{3,2,1,0:T(8,128)(2,1)}, u32[]{:S(2)}) copy-start(bf16[2,8,64,512]{3,2,1,0:T(8,128)(2,1)} %pad_maximum_fusion.1.refs_0_) | copy-start | bytes 3145732
  280.7 11.6 %copy-start.16 = (bf16[256,1024]{1,0:T(8,128)(2,1)S(1)}, bf16[256,1024]{1,0:T(8,128)(2,1)}, u32[]{:S(2)}) copy-start(bf16[256,1024]{1,0:T(8,128)(2,1)} %copy-done.15) | copy-start | bytes 1572868
  285.6 12.4 %collective-permute-start.33 = (bf16[8,512]{1,0:T(8,128)(2,1)S(1)}, bf16[8,512]{1,0:T(8,128)(2,1)S(1)}, u32[]{:S(2)}, u32[]{:S(2)}) collective-permute-start(bf16[8,512]{1,0:T(8,128)(2,1)S(1)} %get-tuple-element.139), channel_id=1, source_target_pairs={{0,0},{1,8},{2,16},{3,24},{4,4},{5,12},{6,20},{7,28},{8,1},{9,9},{... | collective-permute-start | bytes 24584 | tf_op jit(solution)/shard_map/ppermute | solution.py:266
  288.8 9.2 %collective-permute-start.34 = (bf16[8,512]{1,0:T(8,128)(2,1)S(1)}, bf16[8,512]{1,0:T(8,128)(2,1)S(1)}, u32[]{:S(2)}, u32[]{:S(2)}) collective-permute-start(bf16[8,512]{1,0:T(8,128)(2,1)S(1)} %get-tuple-element.140), channel_id=1, source_target_pairs={{0,4},{1,12},{2,20},{3,28},{4,0},{5,8},{6,16},{7,24},{8,5},{9,13},... | collective-permute-start | bytes 24584 | tf_op jit(solution)/shard_map/ppermute | solution.py:266
  (16 other events, 38.0 us)

commit v17 on v16

--- a/solution.py
+++ b/solution.py
@@ -444,36 +444,33 @@
     att_far = [line.shift(attended, m) for m in range(2, line.n_z - 1)]
     att_other_next = [line.swap(block) for block in att_next]
     live_pair = jnp.stack([live_mine, live_y])
-    kv_grad_all, term, live_pair, *staged = gate(
-        (kv_grad_all, term, live_pair, *att_other_next, *text_parts, *att_far)
-    )
-    att_other_next, staged = staged[:2], staged[2:]
-    text_parts, att_far = staged[: n_tensor - 2], staged[n_tensor - 2 :]
-
     att_other_far = [line.swap(block) for block in att_far]
     live_core = tensor_swap(live_pair, 1)
+
+    att_blocks = [attended, att_next[0], *att_far, att_next[1]]
+    att_others = [att_swapped, att_other_next[0], *att_other_far, att_other_next[1]]
+    weight_grad = call(
+        functools.partial(weight_grad_kernel, line),
+        place,
+        (live_pair, live_core, *att_blocks, *att_others),
+        [shape((local_cols, own_width), BF16)],
+        [pltpu.VMEM((local_cols, own_width), F32)],
+        2 * n_dp * rows * local_cols * own_width,
+    )
+    kv_grad_all, term, weight_grad, *text_parts = gate(
+        (kv_grad_all, term, weight_grad, *text_parts)
+    )
+
     text_parts.append(tensor_swap(term[1], 1))
     image_term = matmul(kv_grad_all[:, :local_cols], key_weight, BACK)
     image_term = image_term + matmul(kv_grad_all[:, local_cols:], value_weight, BACK)
     text_grad = call(
         sum_kernel, place, (term, *text_parts), [shape((rows, width // n_tensor), BF16)]
     )
-    image_grad, live_core, text_grad, *att_other_far = to_owner(
-        line, image_term.astype(BF16), live_core, text_grad, *att_other_far
-    )
+    image_grad, text_grad = to_owner(line, image_term.astype(BF16), text_grad)
     image_grad = image_grad.reshape(samples, image_own, width // n_tensor)
     text_grad = text_grad.reshape(samples, tok_rows, width // n_tensor)
 
-    att_blocks = [attended, att_next[0], *att_far, att_next[1]]
-    att_others = [att_swapped, att_other_next[0], *att_other_far, att_other_next[1]]
-    weight_grad = call(
-        functools.partial(weight_grad_kernel, line),
-        place,
-        (live_pair, live_core, *att_blocks, *att_others),
-        [shape((local_cols, own_width), BF16)],
-        [pltpu.VMEM((local_cols, own_width), F32)],
-        2 * n_dp * rows * local_cols * own_width,
-    )
     return text_grad, image_grad, weight_grad
 
 

time: 300 us -> 312 us (1.040)
  waiting for transfers between devices: 126 us -> 132 us
    all_to_all x1, waiting for transfers between devices: 19.5 us -> 0.89 us  [shards(): lax.all_to_all(kv_part, 'dp', split_axis=0, concat_axis=0)]
    ppermute x13, waiting for transfers between devices: 15.3 us -> 28.8 us  [move(): return lax.ppermute(block, 'dp', pairs)]
    ppermute x12, waiting for transfers between devices: 20.1 us -> 27.9 us  [swap(): return lax.ppermute(block, 'dp', pairs)]
    ppermute x2, waiting for transfers between devices: 0.01 us -> 4.75 us  [to_owner(): come.append(lax.ppermute(block, ('dp', 'tensor'), pairs))]
    unnamed x45 -> x47, local copies, waits for them, and re-layouts: 11.8 us -> 14.9 us
  transfers between devices with their start and end apart: 42 -> 42, of which waited for: 13 -> 14; matrix products, arithmetic and copies ran while one was open for 7% -> 7% of each run, Pallas kernels for 12% -> 10%
where the time goes in v17:
time: 312 us; the launch traced here: 309 us
  waiting for transfers between devices  132 us (42%)
  starting transfers between devices  99.5 us (32%)
  Pallas kernels  34.7 us (11%)
  local copies, waits for them, and re-layouts  22.9 us (7%)
  other arithmetic  14.9 us (5%)
  matrix products  3.34 us (1%)
    pallas_call x8, Pallas kernels, call(): pl.pallas_call(kernel, out_shape=outs[0] if single else outs, in_specs=[p...  34.7 us
    all_to_all x2, waiting for transfers between devices, everywhere(): return lax.all_to_all(copies, 'dp', split_axis=0, concat_axis=0)  31.4 us
    ppermute x13, waiting for transfers between devices, move(): return lax.ppermute(block, 'dp', pairs)  28.8 us
    all_to_all x1, waiting for transfers between devices, shards(): lax.all_to_all(part_kv, 'dp', split_axis=0, concat_axis=0)  28.4 us
    ppermute x12, waiting for transfers between devices, swap(): return lax.ppermute(block, 'dp', pairs)  27.9 us
    ppermute x13, starting transfers between devices, move(): return lax.ppermute(block, 'dp', pairs)  24.9 us
    ppermute x12, starting transfers between devices, swap(): return lax.ppermute(block, 'dp', pairs)  19.7 us
    all_to_all x2, starting transfers between devices, everywhere(): return lax.all_to_all(copies, 'dp', split_axis=0, concat_axis=0)  17.3 us
  transfers between devices with their start and end apart: 42, of which 14 were waited for; matrix products, arithmetic and copies ran while one was open for 7% of the time, Pallas kernels for 10%

profile of v17, /device:TPU:4, one launch (start us, length us, event | category | flops | bytes accessed | tf_op | source)
XLA Modules:
  0.0 308.7 jit_solution(14562217071740958372)
XLA Ops:
  2.1 5.6 %collective-permute-start.3 = (bf16[512,1024]{1,0:T(8,128)(2,1)}, bf16[512,1024]{1,0:T(8,128)(2,1)}, u32[]{:S(2)}, u32[]{:S(2)}) collective-permute-start(bf16[512,1024]{1,0:T(8,128)(2,1)} %refs_0_.1), channel_id=1, source_target_pairs={{0,8},{4,12},{8,16},{12,20},{16,24},{20,28},{1,9},{5,13},{9,17},{1... | collective-permute-start | bytes 3145736 | tf_op jit(solution)/shard_map/ppermute | solution.py:31
  7.7 2.2 constant_dynamic-slice_fusion.3
  11.5 1.8 broadcast_select_fusion
  15.4 4.8 %all-to-all-start = ((bf16[8,8,512]{2,0,1:T(8,128)(2,1)}), bf16[8,8,512]{2,0,1:T(8,128)(2,1)S(1)}, u32[]{:S(2)}, u32[]{:S(2)}) async-start(bf16[8,8,512]{2,0,1:T(8,128)(2,1)} %copy.14), calls=%async_computation | async-start | bytes 131072 | tf_op jit(solution)/shard_map/all_to_all | solution.py:313
  20.2 4.8 %collective-permute-done = bf16[512,512]{1,0:T(8,128)(2,1)} collective-permute-done((bf16[512,512]{1,0:T(8,128)(2,1)}, bf16[512,512]{1,0:T(8,128)(2,1)}, u32[]{:S(2)}, u32[]{:S(2)}) %collective-permute-start) | collective-permute-done | bytes 524320 | tf_op jit(solution)/shard_map/ppermute | solution.py:36
  25.1 2.3 pad_maximum_fusion.refs_0_
  27.3 7.8 %all-to-all-done = bf16[8,8,512]{2,0,1:T(8,128)(2,1)S(1)} async-done(((bf16[8,8,512]{2,0,1:T(8,128)(2,1)}), bf16[8,8,512]{2,0,1:T(8,128)(2,1)S(1)}, u32[]{:S(2)}, u32[]{:S(2)}) %all-to-all-start) | async-done | bytes 65568 | tf_op jit(solution)/shard_map/all_to_all | solution.py:313
  35.2 1.6 collective-permute-start.4
  38.0 5.6 %collective-permute-start.9 = (bf16[512,1024]{1,0:T(8,128)(2,1)}, bf16[512,1024]{1,0:T(8,128)(2,1)}, u32[]{:S(2)}, u32[]{:S(2)}) collective-permute-start(bf16[512,1024]{1,0:T(8,128)(2,1)} %pad_maximum_fusion.refs_0_), channel_id=1, source_target_pairs={{0,8},{4,12},{8,16},{12,20},{16,24},{20,28},{1,9},{5,13},{9,17},{1... | collective-permute-start | bytes 3145736 | tf_op jit(solution)/shard_map/ppermute | solution.py:31
  44.9 1.7 collective-permute-start.7
  48.4 10.6 %collective-permute-done.4.refs_4_.refs_5_ = bf16[512,1024]{1,0:T(8,128)(2,1)S(1)} collective-permute-done((bf16[512,1024]{1,0:T(8,128)(2,1)}, bf16[512,1024]{1,0:T(8,128)(2,1)S(1)}, u32[]{:S(2)}, u32[]{:S(2)}) %collective-permute-start.4) | collective-permute-done | bytes 1048608 | tf_op jit(solution)/shard_map/ppermute | solution.py:36
  59.9 3.4 %collective-permute-start.5 = (bf16[512,1024]{1,0:T(8,128)(2,1)}, bf16[512,1024]{1,0:T(8,128)(2,1)}, u32[]{:S(2)}, u32[]{:S(2)}) collective-permute-start(bf16[512,1024]{1,0:T(8,128)(2,1)} %collective-permute-done.2.refs_1_), channel_id=1, source_target_pairs={{0,4},{4,0},{8,12},{12,8},{16,20},{20,16},{1,5},{5,1},{9,13},{13,9... | collective-permute-start | bytes 3145736 | tf_op jit(solution)/shard_map/ppermute | solution.py:36
  64.1 4.2 %all-to-all-start.1 = ((f32[8,8,2048]{2,1,0:T(8,128)}), f32[8,8,2048]{2,1,0:T(8,128)}, u32[]{:S(2)}, u32[]{:S(2)}) async-start(f32[8,8,2048]{2,1,0:T(8,128)} %maximum_bitcast_fusion), calls=%async_computation.1 | async-start | bytes 1048576 | tf_op jit(solution)/shard_map/all_to_all | solution.py:334
  68.3 28.4 %all-to-all-done.1 = f32[8,8,2048]{2,1,0:T(8,128)} async-done(((f32[8,8,2048]{2,1,0:T(8,128)}), f32[8,8,2048]{2,1,0:T(8,128)}, u32[]{:S(2)}, u32[]{:S(2)}) %all-to-all-start.1) | async-done | bytes 524320 | tf_op jit(solution)/shard_map/all_to_all | solution.py:334
  97.9 2.3 broadcast_select_fusion.2.refs_3_
  103.6 1.7 collective-permute-start.11
  105.3 1.7 collective-permute-start.13
  107.6 12.5 %all-to-all-start.2 = ((bf16[8,8,2048]{2,1,0:T(8,128)(2,1)}), bf16[8,8,2048]{2,1,0:T(8,128)(2,1)S(1)}, u32[]{:S(2)}, u32[]{:S(2)}) async-start(bf16[8,8,2048]{2,1,0:T(8,128)(2,1)} %broadcast_in_dim.16), calls=%async_computation.2 | async-start | bytes 524288 | tf_op jit(solution)/shard_map/all_to_all | solution.py:343
  120.1 31.4 %all-to-all-done.2 = bf16[8,8,2048]{2,1,0:T(8,128)(2,1)S(1)} async-done(((bf16[8,8,2048]{2,1,0:T(8,128)(2,1)}), bf16[8,8,2048]{2,1,0:T(8,128)(2,1)S(1)}, u32[]{:S(2)}, u32[]{:S(2)}) %all-to-all-start.2) | async-done | bytes 262176 | tf_op jit(solution)/shard_map/all_to_all | solution.py:343
  151.6 2.4 broadcast_select_fusion.1.refs_2_
  157.0 8.0 %all-to-all-start.3 = ((bf16[1,64,8,512]{3,1,0,2:T(8,128)(2,1)}), bf16[1,64,8,512]{3,1,0,2:T(8,128)(2,1)}, u32[]{:S(2)}, u32[]{:S(2)}) async-start(bf16[1,64,8,512]{3,1,0,2:T(8,128)(2,1)} %copy.15), calls=%async_computation.3 | async-start | bytes 1048576 | tf_op jit(solution)/shard_map/all_to_all | solution.py:359
  165.0 3.9 %collective-permute-start.19 = (bf16[512,1024]{1,0:T(8,128)(2,1)}, bf16[512,1024]{1,0:T(8,128)(2,1)}, u32[]{:S(2)}, u32[]{:S(2)}) collective-permute-start(bf16[512,1024]{1,0:T(8,128)(2,1)} %collective-permute-done.12.refs_0_.refs_4_), channel_id=1, source_target_pairs={{0,4},{4,0},{24,28},{28,24},{1,5},{5,1},{25,29},{29,25},{2,6},{6,2... | collective-permute-start | bytes 3145736 | tf_op jit(solution)/shard_map/ppermute | solution.py:36
  169.6 1.6 copy-done.1
  173.6 5.2 %shard_map.103.part = f32[256,1024]{1,0:T(8,128)S(1)} custom-call(s32[4]{0:T(128)S(1)} %pad_add_fusion.place, bf16[256,4096]{1,0:T(8,128)(2,1)S(1)} %bitcast.42, bf16[512,1024]{1,0:T(8,128)(2,1)S(1)} %copy-done.3, bf16[512,1024]{1,0:T(8,128)(2,1)} %collective-permute-done.2.refs_1_, bf16[512,1024]{1,0:T(8,128)(2,1)} %collective-permute-done.3.refs_2_, ...), custom_call_target="tpu_custom_call" | custom-call | flops 2147483648 | bytes 11534336 | tf_op jit(solution)/shard_map/pallas_call | solution.py:228
  178.9 4.3 %shard_map.104 = (f32[256,512]{1,0:T(8,128)S(1)}, f32[256,512]{1,0:T(8,128)S(1)}) custom-call(s32[4]{0:T(128)S(1)} %pad_add_fusion.place, bf16[256,4096]{1,0:T(8,128)(2,1)S(1)} %bitcast.40, bf16[256,1024]{1,0:T(8,128)(2,1)} %collective-permute-done.1.mine, bf16[256,1024]{1,0:T(8,128)(2,1)} %collective-permute-done.15.by_core, ...), custom_call_target="tpu_custom_call" | custom-call | flops 1073741824 | bytes 8388608 | tf_op jit(solution)/shard_map/pallas_call | solution.py:228
  183.1 1.8 collective-permute-done.18.refs_3_
  185.0 4.0 %shard_map.105 = (bf16[256,512]{1,0:T(8,128)(2,1)S(1)}, bf16[256,512]{1,0:T(8,128)(2,1)S(1)}) custom-call(s32[4]{0:T(128)S(1)} %pad_add_fusion.place, bf16[256,4096]{1,0:T(8,128)(2,1)S(1)} %bitcast.41, bf16[256,1024]{1,0:T(8,128)(2,1)} %collective-permute-done.1.mine, bf16[256,1024]{1,0:T(8,128)(2,1)} %collective-permute-done.15.by_core, ...), custom_call_target="tpu_custom_call" | custom-call | flops 1073741824 | bytes 7864320 | tf_op jit(solution)/shard_map/pallas_call | solution.py:228
  190.7 2.3 collective-permute-done.19.refs_1_.refs_9_
  193.0 1.6 copy-done.2
  195.8 4.3 %shard_map.106 = (bf16[256,1024]{1,0:T(8,128)(2,1)S(1)}, bf16[256,1024]{1,0:T(8,128)(2,1)}) custom-call(s32[4]{0:T(128)S(1)} %pad_add_fusion.place, bf16[256,4096]{1,0:T(8,128)(2,1)S(1)} %bitcast.43, bf16[64,2048]{1,0:T(8,128)(2,1)S(1)} %bitcast.44, f32[256,1024]{1,0:T(8,128)S(1)} %copy-done.9, bf16[512,1024]{1,0:T(8,128)(2,1)} %collective-permute-done.12.refs_0_.refs_4_, ...), custom_call_target="tpu_custom_call" | custom-call | flops 1073741824 | bytes 6553600 | tf_op jit(solution)/shard_map/pallas_call | solution.py:228
  200.1 1.8 collective-permute-start.23
  203.7 2.5 collective-permute-start.22
  206.2 1.9 shard_map.107
  208.9 6.7 %shard_map.108.term = bf16[4,2,256,512]{3,2,1,0:T(8,128)(2,1)S(1)} custom-call(s32[4]{0:T(128)S(1)} %pad_add_fusion.place, bf16[256,1024]{1,0:T(8,128)(2,1)S(1)} %get-tuple-element.108.query_grad, bf16[512,1024]{1,0:T(8,128)(2,1)S(1)} %copy-done.4, bf16[512,1024]{1,0:T(8,128)(2,1)} %collective-permute-done.2.refs_1_, ...), custom_call_target="tpu_custom_call" | custom-call | flops 2147483648 | bytes 13107200 | tf_op jit(solution)/shard_map/pallas_call | solution.py:228
  215.6 7.7 %collective-permute-done.24.refs_5_ = bf16[256,1024]{1,0:T(8,128)(2,1)} collective-permute-done((bf16[256,1024]{1,0:T(8,128)(2,1)}, bf16[256,1024]{1,0:T(8,128)(2,1)}, u32[]{:S(2)}, u32[]{:S(2)}) %collective-permute-start.24) | collective-permute-done | bytes 524320 | tf_op jit(solution)/shard_map/ppermute | solution.py:31
  225.5 5.4 %all-to-all-start.4 = ((f32[8,8,2048]{2,1,0:T(8,128)}), f32[8,8,2048]{2,1,0:T(8,128)}, u32[]{:S(2)}, u32[]{:S(2)}) async-start(f32[8,8,2048]{2,1,0:T(8,128)} %bitcast.46), calls=%async_computation.4 | async-start | bytes 1048576 | tf_op jit(solution)/shard_map/all_to_all | solution.py:441
  230.9 2.3 pad_maximum_fusion.1.refs_0_
  233.2 2.0 collective-permute-start.27
  235.3 19.3 %collective-permute-done.26.refs_4_ = bf16[256,1024]{1,0:T(8,128)(2,1)} collective-permute-done((bf16[256,1024]{1,0:T(8,128)(2,1)}, bf16[256,1024]{1,0:T(8,128)(2,1)}, u32[]{:S(2)}, u32[]{:S(2)}) %collective-permute-start.26) | collective-permute-done | bytes 524320 | tf_op jit(solution)/shard_map/ppermute | solution.py:31
  261.3 4.8 %all-to-all-start.5 = ((bf16[8,8,2048]{2,1,0:T(8,128)(2,1)}), bf16[8,8,2048]{2,1,0:T(8,128)(2,1)S(1)}, u32[]{:S(2)}, u32[]{:S(2)}) async-start(bf16[8,8,2048]{2,1,0:T(8,128)(2,1)} %broadcast_in_dim.17), calls=%async_computation.5 | async-start | bytes 524288 | tf_op jit(solution)/shard_map/all_to_all | solution.py:343
  266.2 10.2 %collective-permute-done.28.refs_8_ = bf16[256,1024]{1,0:T(8,128)(2,1)} collective-permute-done((bf16[256,1024]{1,0:T(8,128)(2,1)}, bf16[256,1024]{1,0:T(8,128)(2,1)}, u32[]{:S(2)}, u32[]{:S(2)}) %collective-permute-start.28) | collective-permute-done | bytes 524320 | tf_op jit(solution)/shard_map/ppermute | solution.py:36
  278.5 5.8 %shard_map.109 = bf16[1024,512]{1,0:T(8,128)(2,1)} custom-call(s32[4]{0:T(128)S(1)} %pad_add_fusion.place, bf16[2,8,64,512]{3,2,1,0:T(8,128)(2,1)} %pad_maximum_fusion.1.refs_0_, bf16[2,8,64,512]{3,2,1,0:T(8,128)(2,1)} %collective-permute-done.25.refs_1_, bf16[256,1024]{1,0:T(8,128)(2,1)} %get-tuple-element.114.refs_2_, ...), custom_call_target="tpu_custom_call" | custom-call | flops 2147483648 | bytes 7340032 | tf_op jit(solution)/shard_map/pallas_call | solution.py:228
  286.8 4.8 %all-to-all-start.6 = ((bf16[4,16,512]{2,1,0:T(8,128)(2,1)}), bf16[4,16,512]{2,1,0:T(8,128)(2,1)S(1)}, u32[]{:S(2)}, u32[]{:S(2)}) async-start(bf16[4,16,512]{2,1,0:T(8,128)(2,1)} %bitcast.19), calls=%async_computation.6 | async-start | bytes 131072 | tf_op jit(solution)/shard_map/all_to_all | solution.py:250
  291.6 2.3 all-to-all-done.6
  293.9 2.4 shard_map.110
  296.3 5.3 %collective-permute-start.33 = (bf16[8,512]{1,0:T(8,128)(2,1)S(1)}, bf16[8,512]{1,0:T(8,128)(2,1)S(1)}, u32[]{:S(2)}, u32[]{:S(2)}) collective-permute-start(bf16[8,512]{1,0:T(8,128)(2,1)S(1)} %get-tuple-element.129), channel_id=1, source_target_pairs={{0,0},{1,8},{2,16},{3,24},{4,4},{5,12},{6,20},{7,28},{8,1},{9,9},{... | collective-permute-start | bytes 24584 | tf_op jit(solution)/shard_map/ppermute | solution.py:266
  301.7 1.6 collective-permute-start.34
  303.7 4.4 %collective-permute-done.34 = bf16[8,512]{1,0:T(8,128)(2,1)S(1)} collective-permute-done((bf16[8,512]{1,0:T(8,128)(2,1)S(1)}, bf16[8,512]{1,0:T(8,128)(2,1)S(1)}, u32[]{:S(2)}, u32[]{:S(2)}) %collective-permute-start.34) | collective-permute-done | bytes 8224 | tf_op jit(solution)/shard_map/ppermute | solution.py:266
  (121 shorter events, 42.6 us)
Async XLA Ops:
  0.6 47.4 %copy-start = (bf16[512,1024]{1,0:T(8,128)(2,1)S(1)}, bf16[512,1024]{1,0:T(8,128)(2,1)}, u32[]{:S(2)}) copy-start(bf16[512,1024]{1,0:T(8,128)(2,1)} %param.14) | copy-start | bytes 3145732
  0.6 10.7 %copy-start.22 = (s32[2]{0:T(128)S(1)}, s32[2]{0:T(128)}, u32[]{:S(2)}) copy-start(s32[2]{0:T(128)} %param.11) | copy-start | bytes 28
  0.7 34.5 %collective-permute-start.2 = (bf16[512,1024]{1,0:T(8,128)(2,1)}, bf16[512,1024]{1,0:T(8,128)(2,1)}, u32[]{:S(2)}, u32[]{:S(2)}) collective-permute-start(bf16[512,1024]{1,0:T(8,128)(2,1)} %refs_0_.1), channel_id=1, source_target_pairs={{8,0},{12,4},{16,8},{20,12},{24,16},{28,20},{9,1},{13,5},{17,9},{2... | collective-permute-start | bytes 3145736 | tf_op jit(solution)/shard_map/ppermute | solution.py:31
  2.1 33.1 %collective-permute-start.3 = (bf16[512,1024]{1,0:T(8,128)(2,1)}, bf16[512,1024]{1,0:T(8,128)(2,1)}, u32[]{:S(2)}, u32[]{:S(2)}) collective-permute-start(bf16[512,1024]{1,0:T(8,128)(2,1)} %refs_0_.1), channel_id=1, source_target_pairs={{0,8},{4,12},{8,16},{12,20},{16,24},{20,28},{1,9},{5,13},{9,17},{1... | collective-permute-start | bytes 3145736 | tf_op jit(solution)/shard_map/ppermute | solution.py:31
  9.9 15.2 %collective-permute-start = (bf16[512,512]{1,0:T(8,128)(2,1)}, bf16[512,512]{1,0:T(8,128)(2,1)}, u32[]{:S(2)}, u32[]{:S(2)}) collective-permute-start(bf16[512,512]{1,0:T(8,128)(2,1)} %get-tuple-element.128), channel_id=1, source_target_pairs={{0,4},{4,0},{8,12},{12,8},{16,20},{20,16},{24,28},{28,24},{1,5},{5... | collective-permute-start | bytes 1572872 | tf_op jit(solution)/shard_map/ppermute | solution.py:36
  14.2 21.0 %collective-permute-start.1 = (bf16[256,1024]{1,0:T(8,128)(2,1)}, bf16[256,1024]{1,0:T(8,128)(2,1)}, u32[]{:S(2)}, u32[]{:S(2)}) collective-permute-start(bf16[256,1024]{1,0:T(8,128)(2,1)} %constant_dynamic-slice_fusion.1), channel_id=1, source_target_pairs={{0,4},{4,0},{8,12},{12,8},{16,20},{20,16},{24,28},{28,24},{1,5},{5... | collective-permute-start | bytes 1572872 | tf_op jit(solution)/shard_map/ppermute | solution.py:36
  15.4 19.8 %all-to-all-start = ((bf16[8,8,512]{2,0,1:T(8,128)(2,1)}), bf16[8,8,512]{2,0,1:T(8,128)(2,1)S(1)}, u32[]{:S(2)}, u32[]{:S(2)}) async-start(bf16[8,8,512]{2,0,1:T(8,128)(2,1)} %copy.14), calls=%async_computation | async-start | bytes 131072 | tf_op jit(solution)/shard_map/all_to_all | solution.py:313
  35.2 23.8 %collective-permute-start.4 = (bf16[512,1024]{1,0:T(8,128)(2,1)}, bf16[512,1024]{1,0:T(8,128)(2,1)S(1)}, u32[]{:S(2)}, u32[]{:S(2)}) collective-permute-start(bf16[512,1024]{1,0:T(8,128)(2,1)} %refs_0_.1), channel_id=1, source_target_pairs={{0,4},{4,0},{8,12},{12,8},{16,20},{20,16},{24,28},{28,24},{1,5},{5... | collective-permute-start | bytes 3145736 | tf_op jit(solution)/shard_map/ppermute | solution.py:36
  36.7 61.1 %collective-permute-start.8 = (bf16[512,1024]{1,0:T(8,128)(2,1)}, bf16[512,1024]{1,0:T(8,128)(2,1)}, u32[]{:S(2)}, u32[]{:S(2)}) collective-permute-start(bf16[512,1024]{1,0:T(8,128)(2,1)} %pad_maximum_fusion.refs_0_), channel_id=1, source_target_pairs={{8,0},{12,4},{16,8},{20,12},{24,16},{28,20},{9,1},{13,5},{17,9},{2... | collective-permute-start | bytes 3145736 | tf_op jit(solution)/shard_map/ppermute | solution.py:31
  38.0 59.9 %collective-permute-start.9 = (bf16[512,1024]{1,0:T(8,128)(2,1)}, bf16[512,1024]{1,0:T(8,128)(2,1)}, u32[]{:S(2)}, u32[]{:S(2)}) collective-permute-start(bf16[512,1024]{1,0:T(8,128)(2,1)} %pad_maximum_fusion.refs_0_), channel_id=1, source_target_pairs={{0,8},{4,12},{8,16},{12,20},{16,24},{20,28},{1,9},{5,13},{9,17},{1... | collective-permute-start | bytes 3145736 | tf_op jit(solution)/shard_map/ppermute | solution.py:31
  43.6 54.3 %collective-permute-start.6 = (bf16[512,1024]{1,0:T(8,128)(2,1)}, bf16[512,1024]{1,0:T(8,128)(2,1)}, u32[]{:S(2)}, u32[]{:S(2)}) collective-permute-start(bf16[512,1024]{1,0:T(8,128)(2,1)} %collective-permute-done.2.refs_1_), channel_id=1, source_target_pairs={{8,0},{12,4},{16,8},{20,12},{9,1},{13,5},{17,9},{21,13},{10,2},{14... | collective-permute-start | bytes 3145736 | tf_op jit(solution)/shard_map/ppermute | solution.py:31
  44.9 53.0 %collective-permute-start.7 = (bf16[512,1024]{1,0:T(8,128)(2,1)}, bf16[512,1024]{1,0:T(8,128)(2,1)}, u32[]{:S(2)}, u32[]{:S(2)}) collective-permute-start(bf16[512,1024]{1,0:T(8,128)(2,1)} %collective-permute-done.3.refs_2_), channel_id=1, source_target_pairs={{8,16},{12,20},{16,24},{20,28},{9,17},{13,21},{17,25},{21,29},{10,... | collective-permute-start | bytes 3145736 | tf_op jit(solution)/shard_map/ppermute | solution.py:31
  59.9 38.0 %collective-permute-start.5 = (bf16[512,1024]{1,0:T(8,128)(2,1)}, bf16[512,1024]{1,0:T(8,128)(2,1)}, u32[]{:S(2)}, u32[]{:S(2)}) collective-permute-start(bf16[512,1024]{1,0:T(8,128)(2,1)} %collective-permute-done.2.refs_1_), channel_id=1, source_target_pairs={{0,4},{4,0},{8,12},{12,8},{16,20},{20,16},{1,5},{5,1},{9,13},{13,9... | collective-permute-start | bytes 3145736 | tf_op jit(solution)/shard_map/ppermute | solution.py:36
  64.1 32.6 %all-to-all-start.1 = ((f32[8,8,2048]{2,1,0:T(8,128)}), f32[8,8,2048]{2,1,0:T(8,128)}, u32[]{:S(2)}, u32[]{:S(2)}) async-start(f32[8,8,2048]{2,1,0:T(8,128)} %maximum_bitcast_fusion), calls=%async_computation.1 | async-start | bytes 1048576 | tf_op jit(solution)/shard_map/all_to_all | solution.py:334
  100.2 51.4 %collective-permute-start.12 = (bf16[512,1024]{1,0:T(8,128)(2,1)}, bf16[512,1024]{1,0:T(8,128)(2,1)}, u32[]{:S(2)}, u32[]{:S(2)}) collective-permute-start(bf16[512,1024]{1,0:T(8,128)(2,1)} %broadcast_select_fusion.2.refs_3_), channel_id=1, source_target_pairs={{8,0},{12,4},{16,24},{20,28},{9,1},{13,5},{17,25},{21,29},{10,2},{... | collective-permute-start | bytes 3145736 | tf_op jit(solution)/shard_map/ppermute | solution.py:31
  101.5 50.1 %collective-permute-start.14 = (bf16[512,1024]{1,0:T(8,128)(2,1)}, bf16[512,1024]{1,0:T(8,128)(2,1)}, u32[]{:S(2)}, u32[]{:S(2)}) collective-permute-start(bf16[512,1024]{1,0:T(8,128)(2,1)} %broadcast_select_fusion.2.refs_3_), channel_id=1, source_target_pairs={{0,4},{4,0},{8,12},{12,8},{16,20},{20,16},{24,28},{28,24},{1,5},{5... | collective-permute-start | bytes 3145736 | tf_op jit(solution)/shard_map/ppermute | solution.py:36
  102.3 49.3 %collective-permute-start.10 = (bf16[512,1024]{1,0:T(8,128)(2,1)}, bf16[512,1024]{1,0:T(8,128)(2,1)}, u32[]{:S(2)}, u32[]{:S(2)}) collective-permute-start(bf16[512,1024]{1,0:T(8,128)(2,1)} %collective-permute-done.8.refs_1_), channel_id=1, source_target_pairs={{8,0},{12,4},{16,8},{20,12},{9,1},{13,5},{17,9},{21,13},{10,2},{14... | collective-permute-start | bytes 3145736 | tf_op jit(solution)/shard_map/ppermute | solution.py:31
  103.6 48.0 %collective-permute-start.11 = (bf16[512,1024]{1,0:T(8,128)(2,1)}, bf16[512,1024]{1,0:T(8,128)(2,1)}, u32[]{:S(2)}, u32[]{:S(2)}) collective-permute-start(bf16[512,1024]{1,0:T(8,128)(2,1)} %collective-permute-done.9.refs_2_), channel_id=1, source_target_pairs={{8,16},{12,20},{16,24},{20,28},{9,17},{13,21},{17,25},{21,29},{10,... | collective-permute-start | bytes 3145736 | tf_op jit(solution)/shard_map/ppermute | solution.py:31
  105.3 46.3 %collective-permute-start.13 = (bf16[512,1024]{1,0:T(8,128)(2,1)}, bf16[512,1024]{1,0:T(8,128)(2,1)}, u32[]{:S(2)}, u32[]{:S(2)}) collective-permute-start(bf16[512,1024]{1,0:T(8,128)(2,1)} %collective-permute-done.3.refs_2_), channel_id=1, source_target_pairs={{8,12},{12,8},{16,20},{20,16},{24,28},{28,24},{9,13},{13,9},{17,21... | collective-permute-start | bytes 3145736 | tf_op jit(solution)/shard_map/ppermute | solution.py:36
  107.6 43.9 %all-to-all-start.2 = ((bf16[8,8,2048]{2,1,0:T(8,128)(2,1)}), bf16[8,8,2048]{2,1,0:T(8,128)(2,1)S(1)}, u32[]{:S(2)}, u32[]{:S(2)}) async-start(bf16[8,8,2048]{2,1,0:T(8,128)(2,1)} %broadcast_in_dim.16), calls=%async_computation.2 | async-start | bytes 524288 | tf_op jit(solution)/shard_map/all_to_all | solution.py:343
  154.0 31.0 %collective-permute-start.18 = (bf16[512,1024]{1,0:T(8,128)(2,1)}, bf16[512,1024]{1,0:T(8,128)(2,1)}, u32[]{:S(2)}, u32[]{:S(2)}) collective-permute-start(bf16[512,1024]{1,0:T(8,128)(2,1)} %broadcast_select_fusion.1.refs_2_), channel_id=1, source_target_pairs={{8,0},{12,4},{16,24},{20,28},{9,1},{13,5},{17,25},{21,29},{10,2},{... | collective-permute-start | bytes 3145736 | tf_op jit(solution)/shard_map/ppermute | solution.py:31
  155.3 13.7 %collective-permute-start.16 = (bf16[256,1024]{1,0:T(8,128)(2,1)}, bf16[256,1024]{1,0:T(8,128)(2,1)}, u32[]{:S(2)}, u32[]{:S(2)}) collective-permute-start(bf16[256,1024]{1,0:T(8,128)(2,1)} %collective-permute-done.1.mine), channel_id=1, source_target_pairs={{0,2},{1,3},{2,0},{3,1},{4,6},{5,7},{6,4},{7,5},{8,10},{9,11},{10,... | collective-permute-start | bytes 1572872 | tf_op jit(solution)/shard_map/ppermute | solution.py:300
  157.0 33.4 %all-to-all-start.3 = ((bf16[1,64,8,512]{3,1,0,2:T(8,128)(2,1)}), bf16[1,64,8,512]{3,1,0,2:T(8,128)(2,1)}, u32[]{:S(2)}, u32[]{:S(2)}) async-start(bf16[1,64,8,512]{3,1,0,2:T(8,128)(2,1)} %copy.15), calls=%async_computation.3 | async-start | bytes 1048576 | tf_op jit(solution)/shard_map/all_to_all | solution.py:359
  165.0 28.0 %collective-permute-start.19 = (bf16[512,1024]{1,0:T(8,128)(2,1)}, bf16[512,1024]{1,0:T(8,128)(2,1)}, u32[]{:S(2)}, u32[]{:S(2)}) collective-permute-start(bf16[512,1024]{1,0:T(8,128)(2,1)} %collective-permute-done.12.refs_0_.refs_4_), channel_id=1, source_target_pairs={{0,4},{4,0},{24,28},{28,24},{1,5},{5,1},{25,29},{29,25},{2,6},{6,2... | collective-permute-start | bytes 3145736 | tf_op jit(solution)/shard_map/ppermute | solution.py:36
  168.9 9.9 %collective-permute-start.15 = (bf16[256,1024]{1,0:T(8,128)(2,1)}, bf16[256,1024]{1,0:T(8,128)(2,1)}, u32[]{:S(2)}, u32[]{:S(2)}) collective-permute-start(bf16[256,1024]{1,0:T(8,128)(2,1)} %collective-permute-done.1.mine), channel_id=1, source_target_pairs={{0,1},{1,0},{2,3},{3,2},{4,5},{5,4},{6,7},{7,6},{8,9},{9,8},{10,11... | collective-permute-start | bytes 1572872 | tf_op jit(solution)/shard_map/ppermute | solution.py:300
  169.0 9.9 %collective-permute-start.17 = (bf16[256,1024]{1,0:T(8,128)(2,1)}, bf16[256,1024]{1,0:T(8,128)(2,1)}, u32[]{:S(2)}, u32[]{:S(2)}) collective-permute-start(bf16[256,1024]{1,0:T(8,128)(2,1)} %collective-permute-done.16.by_y), channel_id=1, source_target_pairs={{0,1},{1,0},{2,3},{3,2},{4,5},{5,4},{6,7},{7,6},{8,9},{9,8},{10,11... | collective-permute-start | bytes 1572872 | tf_op jit(solution)/shard_map/ppermute | solution.py:300
  173.6 5.3 %copy-start.10 = (bf16[512,1024]{1,0:T(8,128)(2,1)S(1)}, bf16[512,1024]{1,0:T(8,128)(2,1)}, u32[]{:S(2)}) copy-start(bf16[512,1024]{1,0:T(8,128)(2,1)} %pad_maximum_fusion.refs_0_) | copy-start | bytes 3145732
  190.4 13.3 %collective-permute-start.20 = (bf16[256,512]{1,0:T(8,128)(2,1)}, bf16[256,512]{1,0:T(8,128)(2,1)S(1)}, u32[]{:S(2)}, u32[]{:S(2)}) collective-permute-start(bf16[256,512]{1,0:T(8,128)(2,1)} %copy-done.18), channel_id=1, source_target_pairs={{0,4},{4,0},{8,12},{12,8},{16,20},{20,16},{24,28},{28,24},{1,5},{5... | collective-permute-start | bytes 786440 | tf_op jit(solution)/shard_map/ppermute | solution.py:36
  195.8 10.4 %copy-start.13 = (bf16[256,512]{1,0:T(8,128)(2,1)S(1)}, bf16[256,512]{1,0:T(8,128)(2,1)}, u32[]{:S(2)}) copy-start(bf16[256,512]{1,0:T(8,128)(2,1)} %copy-done.12) | copy-start | bytes 786436
  195.8 13.1 %copy-start.4 = (bf16[512,1024]{1,0:T(8,128)(2,1)S(1)}, bf16[512,1024]{1,0:T(8,128)(2,1)}, u32[]{:S(2)}) copy-start(bf16[512,1024]{1,0:T(8,128)(2,1)} %refs_0_.1) | copy-start | bytes 3145732
  195.8 13.1 %copy-start.7 = (bf16[512,1024]{1,0:T(8,128)(2,1)S(1)}, bf16[512,1024]{1,0:T(8,128)(2,1)}, u32[]{:S(2)}) copy-start(bf16[512,1024]{1,0:T(8,128)(2,1)} %copy-done.5) | copy-start | bytes 3145732
  200.1 15.5 %collective-permute-start.23 = (bf16[256,1024]{1,0:T(8,128)(2,1)}, bf16[256,1024]{1,0:T(8,128)(2,1)}, u32[]{:S(2)}, u32[]{:S(2)}) collective-permute-start(bf16[256,1024]{1,0:T(8,128)(2,1)} %get-tuple-element.114.refs_2_), channel_id=1, source_target_pairs={{8,0},{12,4},{16,8},{20,12},{24,16},{28,20},{0,24},{4,28},{9,1},{1... | collective-permute-start | bytes 1572872 | tf_op jit(solution)/shard_map/ppermute | solution.py:31
  202.0 21.4 %collective-permute-start.24 = (bf16[256,1024]{1,0:T(8,128)(2,1)}, bf16[256,1024]{1,0:T(8,128)(2,1)}, u32[]{:S(2)}, u32[]{:S(2)}) collective-permute-start(bf16[256,1024]{1,0:T(8,128)(2,1)} %get-tuple-element.114.refs_2_), channel_id=1, source_target_pairs={{24,0},{28,4},{0,8},{4,12},{8,16},{12,20},{16,24},{20,28},{25,1},{... | collective-permute-start | bytes 1572872 | tf_op jit(solution)/shard_map/ppermute | solution.py:31
  202.2 21.2 %collective-permute-start.21 = (bf16[8,64,512]{2,1,0:T(8,128)(2,1)}, bf16[8,64,512]{2,1,0:T(8,128)(2,1)S(1)}, u32[]{:S(2)}, u32[]{:S(2)}) collective-permute-start(bf16[8,64,512]{2,1,0:T(8,128)(2,1)} %bitcast.12), channel_id=1, source_target_pairs={{0,2},{1,3},{2,0},{3,1},{4,6},{5,7},{6,4},{7,5},{8,10},{9,11},{10,... | collective-permute-start | bytes 1572872 | tf_op jit(solution)/shard_map/ppermute | solution.py:300
  203.7 19.7 %collective-permute-start.22 = (bf16[256,1024]{1,0:T(8,128)(2,1)}, bf16[256,1024]{1,0:T(8,128)(2,1)S(1)}, u32[]{:S(2)}, u32[]{:S(2)}) collective-permute-start(bf16[256,1024]{1,0:T(8,128)(2,1)} %get-tuple-element.114.refs_2_), channel_id=1, source_target_pairs={{0,4},{4,0},{8,12},{12,8},{16,20},{20,16},{24,28},{28,24},{1,5},{5... | collective-permute-start | bytes 1572872 | tf_op jit(solution)/shard_map/ppermute | solution.py:36
  224.9 29.6 %collective-permute-start.26 = (bf16[256,1024]{1,0:T(8,128)(2,1)}, bf16[256,1024]{1,0:T(8,128)(2,1)}, u32[]{:S(2)}, u32[]{:S(2)}) collective-permute-start(bf16[256,1024]{1,0:T(8,128)(2,1)} %get-tuple-element.114.refs_2_), channel_id=1, source_target_pairs={{16,0},{20,4},{24,8},{28,12},{0,16},{4,20},{8,24},{12,28},{17,1},{... | collective-permute-start | bytes 1572872 | tf_op jit(solution)/shard_map/ppermute | solution.py:31
  225.5 34.0 %all-to-all-start.4 = ((f32[8,8,2048]{2,1,0:T(8,128)}), f32[8,8,2048]{2,1,0:T(8,128)}, u32[]{:S(2)}, u32[]{:S(2)}) async-start(f32[8,8,2048]{2,1,0:T(8,128)} %bitcast.46), calls=%async_computation.4 | async-start | bytes 1048576 | tf_op jit(solution)/shard_map/all_to_all | solution.py:441
  233.2 32.9 %collective-permute-start.25 = (bf16[2,8,64,512]{3,2,1,0:T(8,128)(2,1)}, bf16[2,8,64,512]{3,2,1,0:T(8,128)(2,1)}, u32[]{:S(2)}, u32[]{:S(2)}) collective-permute-start(bf16[2,8,64,512]{3,2,1,0:T(8,128)(2,1)} %pad_maximum_fusion.1.refs_0_), channel_id=1, source_target_pairs={{0,1},{1,0},{2,3},{3,2},{4,5},{5,4},{6,7},{7,6},{8,9},{9,8},{10,11... | collective-permute-start | bytes 3145736 | tf_op jit(solution)/shard_map/ppermute | solution.py:300
  233.2 24.6 %collective-permute-start.27 = (bf16[256,1024]{1,0:T(8,128)(2,1)}, bf16[256,1024]{1,0:T(8,128)(2,1)S(1)}, u32[]{:S(2)}, u32[]{:S(2)}) collective-permute-start(bf16[256,1024]{1,0:T(8,128)(2,1)} %collective-permute-done.23.refs_3_), channel_id=1, source_target_pairs={{0,4},{4,0},{8,12},{12,8},{16,20},{20,16},{24,28},{28,24},{1,5},{5... | collective-permute-start | bytes 1572872 | tf_op jit(solution)/shard_map/ppermute | solution.py:36
  235.3 30.9 %collective-permute-start.29 = (bf16[256,1024]{1,0:T(8,128)(2,1)}, bf16[256,1024]{1,0:T(8,128)(2,1)}, u32[]{:S(2)}, u32[]{:S(2)}) collective-permute-start(bf16[256,1024]{1,0:T(8,128)(2,1)} %collective-permute-done.24.refs_5_), channel_id=1, source_target_pairs={{0,4},{4,0},{8,12},{12,8},{16,20},{20,16},{24,28},{28,24},{1,5},{5... | collective-permute-start | bytes 1572872 | tf_op jit(solution)/shard_map/ppermute | solution.py:36
  254.6 21.8 %collective-permute-start.28 = (bf16[256,1024]{1,0:T(8,128)(2,1)}, bf16[256,1024]{1,0:T(8,128)(2,1)}, u32[]{:S(2)}, u32[]{:S(2)}) collective-permute-start(bf16[256,1024]{1,0:T(8,128)(2,1)} %collective-permute-done.26.refs_4_), channel_id=1, source_target_pairs={{0,4},{4,0},{8,12},{12,8},{16,20},{20,16},{24,28},{28,24},{1,5},{5... | collective-permute-start | bytes 1572872 | tf_op jit(solution)/shard_map/ppermute | solution.py:36
  257.1 27.2 %collective-permute-start.30 = (bf16[2,256,512]{2,1,0:T(8,128)(2,1)}, bf16[2,256,512]{2,1,0:T(8,128)(2,1)}, u32[]{:S(2)}, u32[]{:S(2)}) collective-permute-start(bf16[2,256,512]{2,1,0:T(8,128)(2,1)} %get-tuple-element.126), channel_id=1, source_target_pairs={{0,2},{1,3},{2,0},{3,1},{4,6},{5,7},{6,4},{7,5},{8,10},{9,11},{10,... | collective-permute-start | bytes 1572872 | tf_op jit(solution)/shard_map/ppermute | solution.py:300
  258.7 25.7 %collective-permute-start.31 = (bf16[2,256,512]{2,1,0:T(8,128)(2,1)}, bf16[2,256,512]{2,1,0:T(8,128)(2,1)}, u32[]{:S(2)}, u32[]{:S(2)}) collective-permute-start(bf16[2,256,512]{2,1,0:T(8,128)(2,1)} %get-tuple-element.125), channel_id=1, source_target_pairs={{0,3},{1,2},{2,1},{3,0},{4,7},{5,6},{6,5},{7,4},{8,11},{9,10},{10,... | collective-permute-start | bytes 1572872 | tf_op jit(solution)/shard_map/ppermute | solution.py:300
  261.3 23.0 %all-to-all-start.5 = ((bf16[8,8,2048]{2,1,0:T(8,128)(2,1)}), bf16[8,8,2048]{2,1,0:T(8,128)(2,1)S(1)}, u32[]{:S(2)}, u32[]{:S(2)}) async-start(bf16[8,8,2048]{2,1,0:T(8,128)(2,1)} %broadcast_in_dim.17), calls=%async_computation.5 | async-start | bytes 524288 | tf_op jit(solution)/shard_map/all_to_all | solution.py:343
  285.2 8.7 %collective-permute-start.32 = (bf16[2,256,512]{2,1,0:T(8,128)(2,1)}, bf16[2,256,512]{2,1,0:T(8,128)(2,1)}, u32[]{:S(2)}, u32[]{:S(2)}) collective-permute-start(bf16[2,256,512]{2,1,0:T(8,128)(2,1)} %slice_bitcast_fusion), channel_id=1, source_target_pairs={{0,1},{1,0},{2,3},{3,2},{4,5},{5,4},{6,7},{7,6},{8,9},{9,8},{10,11... | collective-permute-start | bytes 1572872 | tf_op jit(solution)/shard_map/ppermute | solution.py:300
  286.8 7.1 %all-to-all-start.6 = ((bf16[4,16,512]{2,1,0:T(8,128)(2,1)}), bf16[4,16,512]{2,1,0:T(8,128)(2,1)S(1)}, u32[]{:S(2)}, u32[]{:S(2)}) async-start(bf16[4,16,512]{2,1,0:T(8,128)(2,1)} %bitcast.19), calls=%async_computation.6 | async-start | bytes 131072 | tf_op jit(solution)/shard_map/all_to_all | solution.py:250
  296.3 7.3 %collective-permute-start.33 = (bf16[8,512]{1,0:T(8,128)(2,1)S(1)}, bf16[8,512]{1,0:T(8,128)(2,1)S(1)}, u32[]{:S(2)}, u32[]{:S(2)}) collective-permute-start(bf16[8,512]{1,0:T(8,128)(2,1)S(1)} %get-tuple-element.129), channel_id=1, source_target_pairs={{0,0},{1,8},{2,16},{3,24},{4,4},{5,12},{6,20},{7,28},{8,1},{9,9},{... | collective-permute-start | bytes 24584 | tf_op jit(solution)/shard_map/ppermute | solution.py:266
  301.7 6.4 %collective-permute-start.34 = (bf16[8,512]{1,0:T(8,128)(2,1)S(1)}, bf16[8,512]{1,0:T(8,128)(2,1)S(1)}, u32[]{:S(2)}, u32[]{:S(2)}) collective-permute-start(bf16[8,512]{1,0:T(8,128)(2,1)S(1)} %get-tuple-element.130), channel_id=1, source_target_pairs={{0,4},{1,12},{2,20},{3,28},{4,0},{5,8},{6,16},{7,24},{8,5},{9,13},... | collective-permute-start | bytes 24584 | tf_op jit(solution)/shard_map/ppermute | solution.py:266
  (17 other events, 23.5 us)

commit v18 on v14

--- a/solution.py
+++ b/solution.py
@@ -12,7 +12,7 @@
 BF16 = jnp.bfloat16
 BACK = (((1,), (1,)), ((), ()))
 FIRST = (((0,), (0,)), ((), ()))
-VMEM_LIMIT = 60 * 1024 * 1024
+VMEM_LIMIT = 24 * 1024 * 1024
 
 
 def matmul(a, b, dims=None):
@@ -363,6 +363,12 @@
     wq_last, wq_others = staged[: len(wq_last)], staged[len(wq_last) :]
 
     wo_last = line.third(wo_two)
+    quarter_rows = rows // 4
+    live_rows = lax.dynamic_slice_in_dim(live_flat, quarter * quarter_rows, quarter_rows, 0)
+    live_mine = lax.all_to_all(
+        live_rows.reshape(quarter_rows, n_dp, own_width), "dp", split_axis=1, concat_axis=0
+    )
+    live_mine = live_mine.reshape(n_dp, quarter_rows, own_width)
     by_y = tensor_swap(live_here, 2)
     live_pieces = [live_here, tensor_swap(live_here, 1), by_y, tensor_swap(by_y, 1)]
     wq_others += [line.swap(block, (0, 3)) for block in wq_last[1:]]
@@ -422,25 +428,17 @@
         (),
         2 * rows * width * local_cols,
     )
-    term, live_flat = gate((term, live_flat))
-    quarter_rows = rows // 4
-    live_rows = lax.dynamic_slice_in_dim(live_flat, quarter * quarter_rows, quarter_rows, 0)
-    live_mine = lax.all_to_all(
-        live_rows.reshape(quarter_rows, n_dp, own_width), "dp", split_axis=1, concat_axis=0
-    )
-    live_mine = live_mine.reshape(n_dp, quarter_rows, own_width)
-    kv_part, term, attended, att_swapped, *att_next = gate(
-        (kv_part, term, attended, att_swapped, *att_next)
+    kv_part, term, live_y, attended, att_swapped, *att_next = gate(
+        (kv_part, term, tensor_swap(live_mine, 2), attended, att_swapped, *att_next)
     )
 
     kv_part = kv_part.reshape(n_dp, image_rows, 2 * local_cols)
     kv_grad = jnp.sum(lax.all_to_all(kv_part, "dp", split_axis=0, concat_axis=0), axis=0)
-    kv_grad, live_mine = gate((kv_grad.astype(BF16), live_mine))
-    kv_grad_all = everywhere(kv_grad).reshape(images, 2 * local_cols)
+    kv_grad_all = everywhere(kv_grad.astype(BF16)).reshape(images, 2 * local_cols)
     text_parts = [tensor_swap(term[k], k) for k in range(2, n_tensor)]
     att_far = [line.shift(attended, m) for m in range(2, line.n_z - 1)]
     att_other_next = [line.swap(block) for block in att_next]
-    live_pair = jnp.stack([live_mine, tensor_swap(live_mine, 2)])
+    live_pair = jnp.stack([live_mine, live_y])
     kv_grad_all, term, live_pair, *staged = gate(
         (kv_grad_all, term, live_pair, *att_other_next, *text_parts, *att_far)
     )

time: 319 us -> 298 us (0.934)
  waiting for transfers between devices: 149 us -> 125 us
  Pallas kernels: 45.7 us -> 34.3 us
  local copies, waits for them, and re-layouts: 12.3 us -> 20.7 us
  starting transfers between devices: 92.3 us -> 97.2 us
    ppermute x8, waiting for transfers between devices: 23.7 us -> 2.37 us  [tensor_swap(): lax.ppermute(block, 'tensor', [(t, t ^ bit) for t in range(n_tensor)])]
    all_to_all x1, waiting for transfers between devices: 12.2 us -> 0.01 us  [shards(): lax.all_to_all(live_rows.reshape(quarter_rows, n_dp, own_width), 'dp', sp...]
    pallas_call x8, Pallas kernels: 45.7 us -> 34.3 us  [call(): pl.pallas_call(kernel, out_shape=outs[0] if single else outs, in_specs=[p...]
    unnamed x31 -> x43, local copies, waits for them, and re-layouts: 3.04 us -> 12.6 us
    all_to_all x1, waiting for transfers between devices: 10.6 us -> 18.8 us  [shards(): lax.all_to_all(kv_part, 'dp', split_axis=0, concat_axis=0)]
    ppermute x13, waiting for transfers between devices: 19.3 us -> 22.5 us  [move(): return lax.ppermute(block, 'dp', pairs)]
  transfers between devices with their start and end apart: 42 -> 42, of which waited for: 18 -> 14; matrix products, arithmetic and copies ran while one was open for 8% -> 8% of each run, Pallas kernels for 14% -> 12%
where the time goes in v18:
time: 298 us; the launch traced here: 296 us
  waiting for transfers between devices  125 us (42%)
  starting transfers between devices  97.2 us (33%)
  Pallas kernels  34.3 us (12%)
  local copies, waits for them, and re-layouts  20.7 us (7%)
  other arithmetic  14.8 us (5%)
  matrix products  3.34 us (1%)
    pallas_call x8, Pallas kernels, call(): pl.pallas_call(kernel, out_shape=outs[0] if single else outs, in_specs=[p...  34.3 us
    ppermute x13, starting transfers between devices, move(): return lax.ppermute(block, 'dp', pairs)  29.4 us
    all_to_all x1, waiting for transfers between devices, shards(): lax.all_to_all(part_kv, 'dp', split_axis=0, concat_axis=0)  28.4 us
    all_to_all x2, waiting for transfers between devices, everywhere(): return lax.all_to_all(copies, 'dp', split_axis=0, concat_axis=0)  24.5 us
    ppermute x13, waiting for transfers between devices, move(): return lax.ppermute(block, 'dp', pairs)  22.5 us
    all_to_all x1, waiting for transfers between devices, shards(): lax.all_to_all(kv_part, 'dp', split_axis=0, concat_axis=0)  18.8 us
    ppermute x12, waiting for transfers between devices, swap(): return lax.ppermute(block, 'dp', pairs)  18 us
    ppermute x12, starting transfers between devices, swap(): return lax.ppermute(block, 'dp', pairs)  18 us
  transfers between devices with their start and end apart: 42, of which 14 were waited for; matrix products, arithmetic and copies ran while one was open for 8% of the time, Pallas kernels for 12%

profile of v18, /device:TPU:4, one launch (start us, length us, event | category | flops | bytes accessed | tf_op | source)
XLA Modules:
  0.0 296.1 jit_solution(17895639792824702072)
XLA Ops:
  2.1 5.6 %collective-permute-start.3 = (bf16[512,1024]{1,0:T(8,128)(2,1)}, bf16[512,1024]{1,0:T(8,128)(2,1)}, u32[]{:S(2)}, u32[]{:S(2)}) collective-permute-start(bf16[512,1024]{1,0:T(8,128)(2,1)} %refs_0_.1), channel_id=1, source_target_pairs={{0,8},{4,12},{8,16},{12,20},{16,24},{20,28},{1,9},{5,13},{9,17},{1... | collective-permute-start | bytes 3145736 | tf_op jit(solution)/shard_map/ppermute | solution.py:31
  7.6 2.2 constant_dynamic-slice_fusion.3
  11.4 1.8 broadcast_select_fusion
  15.4 4.8 %all-to-all-start = ((bf16[8,8,512]{2,0,1:T(8,128)(2,1)}), bf16[8,8,512]{2,0,1:T(8,128)(2,1)S(1)}, u32[]{:S(2)}, u32[]{:S(2)}) async-start(bf16[8,8,512]{2,0,1:T(8,128)(2,1)} %copy.14), calls=%async_computation | async-start | bytes 131072 | tf_op jit(solution)/shard_map/all_to_all | solution.py:313
  20.2 4.9 %collective-permute-done = bf16[512,512]{1,0:T(8,128)(2,1)} collective-permute-done((bf16[512,512]{1,0:T(8,128)(2,1)}, bf16[512,512]{1,0:T(8,128)(2,1)}, u32[]{:S(2)}, u32[]{:S(2)}) %collective-permute-start) | collective-permute-done | bytes 524320 | tf_op jit(solution)/shard_map/ppermute | solution.py:36
  25.1 2.4 pad_maximum_fusion.refs_0_
  27.4 7.7 %all-to-all-done = bf16[8,8,512]{2,0,1:T(8,128)(2,1)S(1)} async-done(((bf16[8,8,512]{2,0,1:T(8,128)(2,1)}), bf16[8,8,512]{2,0,1:T(8,128)(2,1)S(1)}, u32[]{:S(2)}, u32[]{:S(2)}) %all-to-all-start) | async-done | bytes 65568 | tf_op jit(solution)/shard_map/all_to_all | solution.py:313
  38.0 5.5 %collective-permute-start.9 = (bf16[512,1024]{1,0:T(8,128)(2,1)}, bf16[512,1024]{1,0:T(8,128)(2,1)}, u32[]{:S(2)}, u32[]{:S(2)}) collective-permute-start(bf16[512,1024]{1,0:T(8,128)(2,1)} %pad_maximum_fusion.refs_0_), channel_id=1, source_target_pairs={{0,8},{4,12},{8,16},{12,20},{16,24},{20,28},{1,9},{5,13},{9,17},{1... | collective-permute-start | bytes 3145736 | tf_op jit(solution)/shard_map/ppermute | solution.py:31
  44.8 1.7 collective-permute-start.7
  48.3 10.6 %collective-permute-done.4.refs_2_.refs_5_ = bf16[512,1024]{1,0:T(8,128)(2,1)S(1)} collective-permute-done((bf16[512,1024]{1,0:T(8,128)(2,1)}, bf16[512,1024]{1,0:T(8,128)(2,1)S(1)}, u32[]{:S(2)}, u32[]{:S(2)}) %collective-permute-start.4) | collective-permute-done | bytes 1048608 | tf_op jit(solution)/shard_map/ppermute | solution.py:36
  59.9 3.4 %collective-permute-start.5 = (bf16[512,1024]{1,0:T(8,128)(2,1)}, bf16[512,1024]{1,0:T(8,128)(2,1)}, u32[]{:S(2)}, u32[]{:S(2)}) collective-permute-start(bf16[512,1024]{1,0:T(8,128)(2,1)} %collective-permute-done.2.refs_1_), channel_id=1, source_target_pairs={{0,4},{4,0},{8,12},{12,8},{16,20},{20,16},{1,5},{5,1},{9,13},{13,9... | collective-permute-start | bytes 3145736 | tf_op jit(solution)/shard_map/ppermute | solution.py:36
  64.1 4.1 %all-to-all-start.1 = ((f32[8,8,2048]{2,1,0:T(8,128)}), f32[8,8,2048]{2,1,0:T(8,128)}, u32[]{:S(2)}, u32[]{:S(2)}) async-start(f32[8,8,2048]{2,1,0:T(8,128)} %maximum_bitcast_fusion), calls=%async_computation.1 | async-start | bytes 1048576 | tf_op jit(solution)/shard_map/all_to_all | solution.py:334
  68.3 28.4 %all-to-all-done.1 = f32[8,8,2048]{2,1,0:T(8,128)} async-done(((f32[8,8,2048]{2,1,0:T(8,128)}), f32[8,8,2048]{2,1,0:T(8,128)}, u32[]{:S(2)}, u32[]{:S(2)}) %all-to-all-start.1) | async-done | bytes 524320 | tf_op jit(solution)/shard_map/all_to_all | solution.py:334
  97.9 2.3 broadcast_select_fusion.2.refs_1_.refs_3_
  103.6 1.7 collective-permute-start.11
  105.2 1.7 collective-permute-start.13
  107.6 12.5 %all-to-all-start.2 = ((bf16[8,8,2048]{2,1,0:T(8,128)(2,1)}), bf16[8,8,2048]{2,1,0:T(8,128)(2,1)S(1)}, u32[]{:S(2)}, u32[]{:S(2)}) async-start(bf16[8,8,2048]{2,1,0:T(8,128)(2,1)} %broadcast_in_dim.16), calls=%async_computation.2 | async-start | bytes 524288 | tf_op jit(solution)/shard_map/all_to_all | solution.py:343
  120.2 1.6 copy-done.1
  124.2 3.1 %shard_map.103.part = f32[256,1024]{1,0:T(8,128)S(1)} custom-call(s32[4]{0:T(128)S(1)} %pad_add_fusion.place, bf16[256,4096]{1,0:T(8,128)(2,1)S(1)} %bitcast.43, bf16[512,1024]{1,0:T(8,128)(2,1)S(1)} %copy-done.3, bf16[512,1024]{1,0:T(8,128)(2,1)} %collective-permute-done.2.refs_1_, bf16[512,1024]{1,0:T(8,128)(2,1)S(1)} %copy-done.6, ...), custom_call_target="tpu_custom_call" | custom-call | flops 1073741824 | bytes 7340032 | tf_op jit(solution)/shard_map/pallas_call | solution.py:228
  128.4 23.2 %all-to-all-done.2 = bf16[8,8,2048]{2,1,0:T(8,128)(2,1)S(1)} async-done(((bf16[8,8,2048]{2,1,0:T(8,128)(2,1)}), bf16[8,8,2048]{2,1,0:T(8,128)(2,1)S(1)}, u32[]{:S(2)}, u32[]{:S(2)}) %all-to-all-start.2) | async-done | bytes 262176 | tf_op jit(solution)/shard_map/all_to_all | solution.py:343
  152.1 2.3 broadcast_select_fusion.1.refs_2_
  155.7 3.0 %collective-permute-start.19 = (bf16[512,1024]{1,0:T(8,128)(2,1)}, bf16[512,1024]{1,0:T(8,128)(2,1)}, u32[]{:S(2)}, u32[]{:S(2)}) collective-permute-start(bf16[512,1024]{1,0:T(8,128)(2,1)} %collective-permute-done.12.refs_2_.refs_4_), channel_id=1, source_target_pairs={{0,4},{4,0},{24,28},{28,24},{1,5},{5,1},{25,29},{29,25},{2,6},{6,2... | collective-permute-start | bytes 3145736 | tf_op jit(solution)/shard_map/ppermute | solution.py:36
  160.0 6.6 %all-to-all-start.3 = ((bf16[1,64,8,512]{3,1,0,2:T(8,128)(2,1)}), bf16[1,64,8,512]{3,1,0,2:T(8,128)(2,1)}, u32[]{:S(2)}, u32[]{:S(2)}) async-start(bf16[1,64,8,512]{3,1,0,2:T(8,128)(2,1)} %copy.15), calls=%async_computation.3 | async-start | bytes 1048576 | tf_op jit(solution)/shard_map/all_to_all | solution.py:368
  167.0 1.6 collective-permute-done.15.by_core
  170.6 3.6 %shard_map.104 = (f32[256,512]{1,0:T(8,128)S(1)}, f32[256,512]{1,0:T(8,128)S(1)}) custom-call(s32[4]{0:T(128)S(1)} %pad_add_fusion.place, bf16[256,4096]{1,0:T(8,128)(2,1)S(1)} %bitcast.41, bf16[256,1024]{1,0:T(8,128)(2,1)} %collective-permute-done.1.mine, bf16[256,1024]{1,0:T(8,128)(2,1)S(1)} %collective-permute-done.15.by_core, ...), custom_call_target="tpu_custom_call" | custom-call | flops 1073741824 | bytes 8388608 | tf_op jit(solution)/shard_map/pallas_call | solution.py:228
  174.3 10.9 %collective-permute-done.18.refs_3_ = bf16[512,1024]{1,0:T(8,128)(2,1)} collective-permute-done((bf16[512,1024]{1,0:T(8,128)(2,1)}, bf16[512,1024]{1,0:T(8,128)(2,1)}, u32[]{:S(2)}, u32[]{:S(2)}) %collective-permute-start.18) | collective-permute-done | bytes 1048608 | tf_op jit(solution)/shard_map/ppermute | solution.py:31
  185.2 4.3 %shard_map.105 = (bf16[256,512]{1,0:T(8,128)(2,1)S(1)}, bf16[256,512]{1,0:T(8,128)(2,1)}) custom-call(s32[4]{0:T(128)S(1)} %pad_add_fusion.place, bf16[256,4096]{1,0:T(8,128)(2,1)S(1)} %bitcast.42, bf16[256,1024]{1,0:T(8,128)(2,1)} %collective-permute-done.1.mine, bf16[256,1024]{1,0:T(8,128)(2,1)S(1)} %collective-permute-done.15.by_core, ...), custom_call_target="tpu_custom_call" | custom-call | flops 1073741824 | bytes 7864320 | tf_op jit(solution)/shard_map/pallas_call | solution.py:228
  192.1 1.6 copy-done.2
  194.9 6.4 %shard_map.106 = (bf16[256,1024]{1,0:T(8,128)(2,1)S(1)}, bf16[256,1024]{1,0:T(8,128)(2,1)}) custom-call(s32[4]{0:T(128)S(1)} %pad_add_fusion.place, bf16[256,4096]{1,0:T(8,128)(2,1)S(1)} %bitcast.44, bf16[64,2048]{1,0:T(8,128)(2,1)S(1)} %bitcast.45, f32[256,1024]{1,0:T(8,128)S(1)} %copy-done.9, bf16[512,1024]{1,0:T(8,128)(2,1)} %collective-permute-done.3.refs_0_.refs_2_, ...), custom_call_target="tpu_custom_call" | custom-call | flops 1073741824 | bytes 10747904 | tf_op jit(solution)/shard_map/pallas_call | solution.py:228
  201.3 4.3 %collective-permute-start.23 = (bf16[256,1024]{1,0:T(8,128)(2,1)}, bf16[256,1024]{1,0:T(8,128)(2,1)}, u32[]{:S(2)}, u32[]{:S(2)}) collective-permute-start(bf16[256,1024]{1,0:T(8,128)(2,1)} %get-tuple-element.115.refs_2_), channel_id=1, source_target_pairs={{8,0},{12,4},{16,8},{20,12},{24,16},{28,20},{0,24},{4,28},{9,1},{1... | collective-permute-start | bytes 1572872 | tf_op jit(solution)/shard_map/ppermute | solution.py:31
  205.6 1.7 collective-permute-start.22
  207.3 1.9 shard_map.107
  210.0 6.7 %shard_map.108.term = bf16[4,2,256,512]{3,2,1,0:T(8,128)(2,1)S(1)} custom-call(s32[4]{0:T(128)S(1)} %pad_add_fusion.place, bf16[256,1024]{1,0:T(8,128)(2,1)S(1)} %get-tuple-element.106.query_grad, bf16[512,1024]{1,0:T(8,128)(2,1)S(1)} %copy-done.4, bf16[512,1024]{1,0:T(8,128)(2,1)} %collective-permute-done.2.refs_1_, ...), custom_call_target="tpu_custom_call" | custom-call | flops 2147483648 | bytes 13107200 | tf_op jit(solution)/shard_map/pallas_call | solution.py:228
  216.8 5.4 %collective-permute-done.24.refs_5_ = bf16[256,1024]{1,0:T(8,128)(2,1)} collective-permute-done((bf16[256,1024]{1,0:T(8,128)(2,1)}, bf16[256,1024]{1,0:T(8,128)(2,1)}, u32[]{:S(2)}, u32[]{:S(2)}) %collective-permute-start.24) | collective-permute-done | bytes 524320 | tf_op jit(solution)/shard_map/ppermute | solution.py:31
  222.9 4.2 %all-to-all-start.4 = ((f32[8,8,2048]{2,1,0:T(8,128)}), f32[8,8,2048]{2,1,0:T(8,128)}, u32[]{:S(2)}, u32[]{:S(2)}) async-start(f32[8,8,2048]{2,1,0:T(8,128)} %bitcast.47), calls=%async_computation.4 | async-start | bytes 1048576 | tf_op jit(solution)/shard_map/all_to_all | solution.py:436
  228.7 2.0 collective-permute-start.25
  230.8 2.9 collective-permute-start.29
  233.7 18.8 %all-to-all-done.4 = f32[8,8,2048]{2,1,0:T(8,128)} async-done(((f32[8,8,2048]{2,1,0:T(8,128)}), f32[8,8,2048]{2,1,0:T(8,128)}, u32[]{:S(2)}, u32[]{:S(2)}) %all-to-all-start.4) | async-done | bytes 524320 | tf_op jit(solution)/shard_map/all_to_all | solution.py:436
  254.2 3.5 %all-to-all-start.5 = ((bf16[8,8,2048]{2,1,0:T(8,128)(2,1)}), bf16[8,8,2048]{2,1,0:T(8,128)(2,1)S(1)}, u32[]{:S(2)}, u32[]{:S(2)}) async-start(bf16[8,8,2048]{2,1,0:T(8,128)(2,1)} %broadcast_in_dim.17), calls=%async_computation.5 | async-start | bytes 524288 | tf_op jit(solution)/shard_map/all_to_all | solution.py:343
  257.7 2.3 pad_maximum_fusion.1.refs_0_
  260.0 6.2 %collective-permute-done.29.refs_4_ = bf16[256,1024]{1,0:T(8,128)(2,1)} collective-permute-done((bf16[256,1024]{1,0:T(8,128)(2,1)}, bf16[256,1024]{1,0:T(8,128)(2,1)}, u32[]{:S(2)}, u32[]{:S(2)}) %collective-permute-start.29) | collective-permute-done | bytes 524320 | tf_op jit(solution)/shard_map/ppermute | solution.py:31
  271.8 3.8 %all-to-all-start.6 = ((bf16[4,16,512]{2,1,0:T(8,128)(2,1)}), bf16[4,16,512]{2,1,0:T(8,128)(2,1)S(1)}, u32[]{:S(2)}, u32[]{:S(2)}) async-start(bf16[4,16,512]{2,1,0:T(8,128)(2,1)} %bitcast.20), calls=%async_computation.6 | async-start | bytes 131072 | tf_op jit(solution)/shard_map/all_to_all | solution.py:250
  275.6 2.3 all-to-all-done.6
  277.9 2.5 shard_map.109
  280.5 2.5 collective-permute-done.32.refs_8_
  283.0 3.0 %collective-permute-start.33 = (bf16[8,512]{1,0:T(8,128)(2,1)S(1)}, bf16[8,512]{1,0:T(8,128)(2,1)S(1)}, u32[]{:S(2)}, u32[]{:S(2)}) collective-permute-start(bf16[8,512]{1,0:T(8,128)(2,1)S(1)} %get-tuple-element.133), channel_id=1, source_target_pairs={{0,0},{1,8},{2,16},{3,24},{4,4},{5,12},{6,20},{7,28},{8,1},{9,9},{... | collective-permute-start | bytes 24584 | tf_op jit(solution)/shard_map/ppermute | solution.py:266
  286.0 3.7 %collective-permute-start.34 = (bf16[8,512]{1,0:T(8,128)(2,1)S(1)}, bf16[8,512]{1,0:T(8,128)(2,1)S(1)}, u32[]{:S(2)}, u32[]{:S(2)}) collective-permute-start(bf16[8,512]{1,0:T(8,128)(2,1)S(1)} %get-tuple-element.134), channel_id=1, source_target_pairs={{0,4},{1,12},{2,20},{3,28},{4,0},{5,8},{6,16},{7,24},{8,5},{9,13},... | collective-permute-start | bytes 24584 | tf_op jit(solution)/shard_map/ppermute | solution.py:266
  289.7 5.7 %shard_map.110 = bf16[1024,512]{1,0:T(8,128)(2,1)} custom-call(s32[4]{0:T(128)S(1)} %pad_add_fusion.place, bf16[2,8,64,512]{3,2,1,0:T(8,128)(2,1)S(1)} %copy-done.11, bf16[2,8,64,512]{3,2,1,0:T(8,128)(2,1)} %collective-permute-done.30.refs_1_, bf16[256,1024]{1,0:T(8,128)(2,1)} %get-tuple-element.115.refs_2_, ...), custom_call_target="tpu_custom_call" | custom-call | flops 2147483648 | bytes 7340032 | tf_op jit(solution)/shard_map/pallas_call | solution.py:228
  (117 shorter events, 42.2 us)
Async XLA Ops:
  0.6 47.4 %copy-start = (bf16[512,1024]{1,0:T(8,128)(2,1)S(1)}, bf16[512,1024]{1,0:T(8,128)(2,1)}, u32[]{:S(2)}) copy-start(bf16[512,1024]{1,0:T(8,128)(2,1)} %param.14) | copy-start | bytes 3145732
  0.7 34.5 %collective-permute-start.2 = (bf16[512,1024]{1,0:T(8,128)(2,1)}, bf16[512,1024]{1,0:T(8,128)(2,1)}, u32[]{:S(2)}, u32[]{:S(2)}) collective-permute-start(bf16[512,1024]{1,0:T(8,128)(2,1)} %refs_0_.1), channel_id=1, source_target_pairs={{8,0},{12,4},{16,8},{20,12},{24,16},{28,20},{9,1},{13,5},{17,9},{2... | collective-permute-start | bytes 3145736 | tf_op jit(solution)/shard_map/ppermute | solution.py:31
  2.1 33.1 %collective-permute-start.3 = (bf16[512,1024]{1,0:T(8,128)(2,1)}, bf16[512,1024]{1,0:T(8,128)(2,1)}, u32[]{:S(2)}, u32[]{:S(2)}) collective-permute-start(bf16[512,1024]{1,0:T(8,128)(2,1)} %refs_0_.1), channel_id=1, source_target_pairs={{0,8},{4,12},{8,16},{12,20},{16,24},{20,28},{1,9},{5,13},{9,17},{1... | collective-permute-start | bytes 3145736 | tf_op jit(solution)/shard_map/ppermute | solution.py:31
  9.9 15.2 %collective-permute-start = (bf16[512,512]{1,0:T(8,128)(2,1)}, bf16[512,512]{1,0:T(8,128)(2,1)}, u32[]{:S(2)}, u32[]{:S(2)}) collective-permute-start(bf16[512,512]{1,0:T(8,128)(2,1)} %get-tuple-element.132), channel_id=1, source_target_pairs={{0,4},{4,0},{8,12},{12,8},{16,20},{20,16},{24,28},{28,24},{1,5},{5... | collective-permute-start | bytes 1572872 | tf_op jit(solution)/shard_map/ppermute | solution.py:36
  14.1 21.0 %collective-permute-start.1 = (bf16[256,1024]{1,0:T(8,128)(2,1)}, bf16[256,1024]{1,0:T(8,128)(2,1)}, u32[]{:S(2)}, u32[]{:S(2)}) collective-permute-start(bf16[256,1024]{1,0:T(8,128)(2,1)} %constant_dynamic-slice_fusion.1), channel_id=1, source_target_pairs={{0,4},{4,0},{8,12},{12,8},{16,20},{20,16},{24,28},{28,24},{1,5},{5... | collective-permute-start | bytes 1572872 | tf_op jit(solution)/shard_map/ppermute | solution.py:36
  15.4 19.8 %all-to-all-start = ((bf16[8,8,512]{2,0,1:T(8,128)(2,1)}), bf16[8,8,512]{2,0,1:T(8,128)(2,1)S(1)}, u32[]{:S(2)}, u32[]{:S(2)}) async-start(bf16[8,8,512]{2,0,1:T(8,128)(2,1)} %copy.14), calls=%async_computation | async-start | bytes 131072 | tf_op jit(solution)/shard_map/all_to_all | solution.py:313
  35.2 23.8 %collective-permute-start.4 = (bf16[512,1024]{1,0:T(8,128)(2,1)}, bf16[512,1024]{1,0:T(8,128)(2,1)S(1)}, u32[]{:S(2)}, u32[]{:S(2)}) collective-permute-start(bf16[512,1024]{1,0:T(8,128)(2,1)} %refs_0_.1), channel_id=1, source_target_pairs={{0,4},{4,0},{8,12},{12,8},{16,20},{20,16},{24,28},{28,24},{1,5},{5... | collective-permute-start | bytes 3145736 | tf_op jit(solution)/shard_map/ppermute | solution.py:36
  36.7 61.1 %collective-permute-start.8 = (bf16[512,1024]{1,0:T(8,128)(2,1)}, bf16[512,1024]{1,0:T(8,128)(2,1)}, u32[]{:S(2)}, u32[]{:S(2)}) collective-permute-start(bf16[512,1024]{1,0:T(8,128)(2,1)} %pad_maximum_fusion.refs_0_), channel_id=1, source_target_pairs={{8,0},{12,4},{16,8},{20,12},{24,16},{28,20},{9,1},{13,5},{17,9},{2... | collective-permute-start | bytes 3145736 | tf_op jit(solution)/shard_map/ppermute | solution.py:31
  38.0 59.8 %collective-permute-start.9 = (bf16[512,1024]{1,0:T(8,128)(2,1)}, bf16[512,1024]{1,0:T(8,128)(2,1)}, u32[]{:S(2)}, u32[]{:S(2)}) collective-permute-start(bf16[512,1024]{1,0:T(8,128)(2,1)} %pad_maximum_fusion.refs_0_), channel_id=1, source_target_pairs={{0,8},{4,12},{8,16},{12,20},{16,24},{20,28},{1,9},{5,13},{9,17},{1... | collective-permute-start | bytes 3145736 | tf_op jit(solution)/shard_map/ppermute | solution.py:31
  43.5 54.3 %collective-permute-start.6 = (bf16[512,1024]{1,0:T(8,128)(2,1)}, bf16[512,1024]{1,0:T(8,128)(2,1)}, u32[]{:S(2)}, u32[]{:S(2)}) collective-permute-start(bf16[512,1024]{1,0:T(8,128)(2,1)} %collective-permute-done.2.refs_1_), channel_id=1, source_target_pairs={{8,0},{12,4},{16,8},{20,12},{9,1},{13,5},{17,9},{21,13},{10,2},{14... | collective-permute-start | bytes 3145736 | tf_op jit(solution)/shard_map/ppermute | solution.py:31
  44.8 53.0 %collective-permute-start.7 = (bf16[512,1024]{1,0:T(8,128)(2,1)}, bf16[512,1024]{1,0:T(8,128)(2,1)}, u32[]{:S(2)}, u32[]{:S(2)}) collective-permute-start(bf16[512,1024]{1,0:T(8,128)(2,1)} %collective-permute-done.3.refs_0_.refs_2_), channel_id=1, source_target_pairs={{8,16},{12,20},{16,24},{20,28},{9,17},{13,21},{17,25},{21,29},{10,... | collective-permute-start | bytes 3145736 | tf_op jit(solution)/shard_map/ppermute | solution.py:31
  59.9 37.9 %collective-permute-start.5 = (bf16[512,1024]{1,0:T(8,128)(2,1)}, bf16[512,1024]{1,0:T(8,128)(2,1)}, u32[]{:S(2)}, u32[]{:S(2)}) collective-permute-start(bf16[512,1024]{1,0:T(8,128)(2,1)} %collective-permute-done.2.refs_1_), channel_id=1, source_target_pairs={{0,4},{4,0},{8,12},{12,8},{16,20},{20,16},{1,5},{5,1},{9,13},{13,9... | collective-permute-start | bytes 3145736 | tf_op jit(solution)/shard_map/ppermute | solution.py:36
  64.1 32.6 %all-to-all-start.1 = ((f32[8,8,2048]{2,1,0:T(8,128)}), f32[8,8,2048]{2,1,0:T(8,128)}, u32[]{:S(2)}, u32[]{:S(2)}) async-start(f32[8,8,2048]{2,1,0:T(8,128)} %maximum_bitcast_fusion), calls=%async_computation.1 | async-start | bytes 1048576 | tf_op jit(solution)/shard_map/all_to_all | solution.py:334
  100.2 51.4 %collective-permute-start.12 = (bf16[512,1024]{1,0:T(8,128)(2,1)}, bf16[512,1024]{1,0:T(8,128)(2,1)}, u32[]{:S(2)}, u32[]{:S(2)}) collective-permute-start(bf16[512,1024]{1,0:T(8,128)(2,1)} %broadcast_select_fusion.2.refs_1_.refs_3_), channel_id=1, source_target_pairs={{8,0},{12,4},{16,24},{20,28},{9,1},{13,5},{17,25},{21,29},{10,2},{... | collective-permute-start | bytes 3145736 | tf_op jit(solution)/shard_map/ppermute | solution.py:31
  101.5 50.1 %collective-permute-start.14 = (bf16[512,1024]{1,0:T(8,128)(2,1)}, bf16[512,1024]{1,0:T(8,128)(2,1)}, u32[]{:S(2)}, u32[]{:S(2)}) collective-permute-start(bf16[512,1024]{1,0:T(8,128)(2,1)} %broadcast_select_fusion.2.refs_1_.refs_3_), channel_id=1, source_target_pairs={{0,4},{4,0},{8,12},{12,8},{16,20},{20,16},{24,28},{28,24},{1,5},{5... | collective-permute-start | bytes 3145736 | tf_op jit(solution)/shard_map/ppermute | solution.py:36
  102.3 49.3 %collective-permute-start.10 = (bf16[512,1024]{1,0:T(8,128)(2,1)}, bf16[512,1024]{1,0:T(8,128)(2,1)}, u32[]{:S(2)}, u32[]{:S(2)}) collective-permute-start(bf16[512,1024]{1,0:T(8,128)(2,1)} %collective-permute-done.8.refs_1_), channel_id=1, source_target_pairs={{8,0},{12,4},{16,8},{20,12},{9,1},{13,5},{17,9},{21,13},{10,2},{14... | collective-permute-start | bytes 3145736 | tf_op jit(solution)/shard_map/ppermute | solution.py:31
  103.6 48.0 %collective-permute-start.11 = (bf16[512,1024]{1,0:T(8,128)(2,1)}, bf16[512,1024]{1,0:T(8,128)(2,1)}, u32[]{:S(2)}, u32[]{:S(2)}) collective-permute-start(bf16[512,1024]{1,0:T(8,128)(2,1)} %collective-permute-done.9.refs_2_), channel_id=1, source_target_pairs={{8,16},{12,20},{16,24},{20,28},{9,17},{13,21},{17,25},{21,29},{10,... | collective-permute-start | bytes 3145736 | tf_op jit(solution)/shard_map/ppermute | solution.py:31
  105.2 46.3 %collective-permute-start.13 = (bf16[512,1024]{1,0:T(8,128)(2,1)}, bf16[512,1024]{1,0:T(8,128)(2,1)}, u32[]{:S(2)}, u32[]{:S(2)}) collective-permute-start(bf16[512,1024]{1,0:T(8,128)(2,1)} %collective-permute-done.3.refs_0_.refs_2_), channel_id=1, source_target_pairs={{8,12},{12,8},{16,20},{20,16},{24,28},{28,24},{9,13},{13,9},{17,21... | collective-permute-start | bytes 3145736 | tf_op jit(solution)/shard_map/ppermute | solution.py:36
  107.6 43.9 %all-to-all-start.2 = ((bf16[8,8,2048]{2,1,0:T(8,128)(2,1)}), bf16[8,8,2048]{2,1,0:T(8,128)(2,1)S(1)}, u32[]{:S(2)}, u32[]{:S(2)}) async-start(bf16[8,8,2048]{2,1,0:T(8,128)(2,1)} %broadcast_in_dim.16), calls=%async_computation.2 | async-start | bytes 524288 | tf_op jit(solution)/shard_map/all_to_all | solution.py:343
  151.6 15.0 %collective-permute-start.16 = (bf16[256,1024]{1,0:T(8,128)(2,1)}, bf16[256,1024]{1,0:T(8,128)(2,1)}, u32[]{:S(2)}, u32[]{:S(2)}) collective-permute-start(bf16[256,1024]{1,0:T(8,128)(2,1)} %collective-permute-done.1.mine), channel_id=1, source_target_pairs={{0,2},{1,3},{2,0},{3,1},{4,6},{5,7},{6,4},{7,5},{8,10},{9,11},{10,... | collective-permute-start | bytes 1572872 | tf_op jit(solution)/shard_map/ppermute | solution.py:300
  154.5 30.7 %collective-permute-start.18 = (bf16[512,1024]{1,0:T(8,128)(2,1)}, bf16[512,1024]{1,0:T(8,128)(2,1)}, u32[]{:S(2)}, u32[]{:S(2)}) collective-permute-start(bf16[512,1024]{1,0:T(8,128)(2,1)} %broadcast_select_fusion.1.refs_2_), channel_id=1, source_target_pairs={{8,0},{12,4},{16,24},{20,28},{9,1},{13,5},{17,25},{21,29},{10,2},{... | collective-permute-start | bytes 3145736 | tf_op jit(solution)/shard_map/ppermute | solution.py:31
  155.7 36.3 %collective-permute-start.19 = (bf16[512,1024]{1,0:T(8,128)(2,1)}, bf16[512,1024]{1,0:T(8,128)(2,1)}, u32[]{:S(2)}, u32[]{:S(2)}) collective-permute-start(bf16[512,1024]{1,0:T(8,128)(2,1)} %collective-permute-done.12.refs_2_.refs_4_), channel_id=1, source_target_pairs={{0,4},{4,0},{24,28},{28,24},{1,5},{5,1},{25,29},{29,25},{2,6},{6,2... | collective-permute-start | bytes 3145736 | tf_op jit(solution)/shard_map/ppermute | solution.py:36
  160.0 30.6 %all-to-all-start.3 = ((bf16[1,64,8,512]{3,1,0,2:T(8,128)(2,1)}), bf16[1,64,8,512]{3,1,0,2:T(8,128)(2,1)}, u32[]{:S(2)}, u32[]{:S(2)}) async-start(bf16[1,64,8,512]{3,1,0,2:T(8,128)(2,1)} %copy.15), calls=%async_computation.3 | async-start | bytes 1048576 | tf_op jit(solution)/shard_map/all_to_all | solution.py:368
  166.5 2.1 collective-permute-start.15
  166.6 2.9 collective-permute-start.17
  190.2 15.4 %collective-permute-start.20 = (bf16[256,512]{1,0:T(8,128)(2,1)}, bf16[256,512]{1,0:T(8,128)(2,1)S(1)}, u32[]{:S(2)}, u32[]{:S(2)}) collective-permute-start(bf16[256,512]{1,0:T(8,128)(2,1)} %get-tuple-element.103), channel_id=1, source_target_pairs={{0,4},{4,0},{8,12},{12,8},{16,20},{20,16},{24,28},{28,24},{1,5},{5... | collective-permute-start | bytes 786440 | tf_op jit(solution)/shard_map/ppermute | solution.py:36
  190.6 26.2 %collective-permute-start.21 = (bf16[8,64,512]{2,1,0:T(8,128)(2,1)}, bf16[8,64,512]{2,1,0:T(8,128)(2,1)S(1)}, u32[]{:S(2)}, u32[]{:S(2)}) collective-permute-start(bf16[8,64,512]{2,1,0:T(8,128)(2,1)} %bitcast.12), channel_id=1, source_target_pairs={{0,2},{1,3},{2,0},{3,1},{4,6},{5,7},{6,4},{7,5},{8,10},{9,11},{10,... | collective-permute-start | bytes 1572872 | tf_op jit(solution)/shard_map/ppermute | solution.py:300
  194.9 12.4 %copy-start.14 = (bf16[256,512]{1,0:T(8,128)(2,1)S(1)}, bf16[256,512]{1,0:T(8,128)(2,1)}, u32[]{:S(2)}) copy-start(bf16[256,512]{1,0:T(8,128)(2,1)} %copy-done.13) | copy-start | bytes 786436
  194.9 15.1 %copy-start.4 = (bf16[512,1024]{1,0:T(8,128)(2,1)S(1)}, bf16[512,1024]{1,0:T(8,128)(2,1)}, u32[]{:S(2)}) copy-start(bf16[512,1024]{1,0:T(8,128)(2,1)} %refs_0_.1) | copy-start | bytes 3145732
  194.9 15.1 %copy-start.7 = (bf16[512,1024]{1,0:T(8,128)(2,1)S(1)}, bf16[512,1024]{1,0:T(8,128)(2,1)}, u32[]{:S(2)}) copy-start(bf16[512,1024]{1,0:T(8,128)(2,1)} %copy-done.5) | copy-start | bytes 3145732
  201.3 15.5 %collective-permute-start.23 = (bf16[256,1024]{1,0:T(8,128)(2,1)}, bf16[256,1024]{1,0:T(8,128)(2,1)}, u32[]{:S(2)}, u32[]{:S(2)}) collective-permute-start(bf16[256,1024]{1,0:T(8,128)(2,1)} %get-tuple-element.115.refs_2_), channel_id=1, source_target_pairs={{8,0},{12,4},{16,8},{20,12},{24,16},{28,20},{0,24},{4,28},{9,1},{1... | collective-permute-start | bytes 1572872 | tf_op jit(solution)/shard_map/ppermute | solution.py:31
  205.6 16.6 %collective-permute-start.24 = (bf16[256,1024]{1,0:T(8,128)(2,1)}, bf16[256,1024]{1,0:T(8,128)(2,1)}, u32[]{:S(2)}, u32[]{:S(2)}) collective-permute-start(bf16[256,1024]{1,0:T(8,128)(2,1)} %get-tuple-element.115.refs_2_), channel_id=1, source_target_pairs={{24,0},{28,4},{0,8},{4,12},{8,16},{12,20},{16,24},{20,28},{25,1},{... | collective-permute-start | bytes 1572872 | tf_op jit(solution)/shard_map/ppermute | solution.py:31
  205.6 16.5 %collective-permute-start.22 = (bf16[256,1024]{1,0:T(8,128)(2,1)}, bf16[256,1024]{1,0:T(8,128)(2,1)S(1)}, u32[]{:S(2)}, u32[]{:S(2)}) collective-permute-start(bf16[256,1024]{1,0:T(8,128)(2,1)} %get-tuple-element.115.refs_2_), channel_id=1, source_target_pairs={{0,4},{4,0},{8,12},{12,8},{16,20},{20,16},{24,28},{28,24},{1,5},{5... | collective-permute-start | bytes 1572872 | tf_op jit(solution)/shard_map/ppermute | solution.py:36
  222.9 29.5 %all-to-all-start.4 = ((f32[8,8,2048]{2,1,0:T(8,128)}), f32[8,8,2048]{2,1,0:T(8,128)}, u32[]{:S(2)}, u32[]{:S(2)}) async-start(f32[8,8,2048]{2,1,0:T(8,128)} %bitcast.47), calls=%async_computation.4 | async-start | bytes 1048576 | tf_op jit(solution)/shard_map/all_to_all | solution.py:436
  228.2 31.8 %collective-permute-start.27 = (bf16[2,256,512]{2,1,0:T(8,128)(2,1)}, bf16[2,256,512]{2,1,0:T(8,128)(2,1)}, u32[]{:S(2)}, u32[]{:S(2)}) collective-permute-start(bf16[2,256,512]{2,1,0:T(8,128)(2,1)} %get-tuple-element.130), channel_id=1, source_target_pairs={{0,2},{1,3},{2,0},{3,1},{4,6},{5,7},{6,4},{7,5},{8,10},{9,11},{10,... | collective-permute-start | bytes 1572872 | tf_op jit(solution)/shard_map/ppermute | solution.py:300
  228.7 31.3 %collective-permute-start.28 = (bf16[2,256,512]{2,1,0:T(8,128)(2,1)}, bf16[2,256,512]{2,1,0:T(8,128)(2,1)}, u32[]{:S(2)}, u32[]{:S(2)}) collective-permute-start(bf16[2,256,512]{2,1,0:T(8,128)(2,1)} %get-tuple-element.129), channel_id=1, source_target_pairs={{0,3},{1,2},{2,1},{3,0},{4,7},{5,6},{6,5},{7,4},{8,11},{9,10},{10,... | collective-permute-start | bytes 1572872 | tf_op jit(solution)/shard_map/ppermute | solution.py:300
  228.7 31.3 %collective-permute-start.25 = (bf16[256,1024]{1,0:T(8,128)(2,1)}, bf16[256,1024]{1,0:T(8,128)(2,1)}, u32[]{:S(2)}, u32[]{:S(2)}) collective-permute-start(bf16[256,1024]{1,0:T(8,128)(2,1)} %collective-permute-done.23.refs_3_), channel_id=1, source_target_pairs={{0,4},{4,0},{8,12},{12,8},{16,20},{20,16},{24,28},{28,24},{1,5},{5... | collective-permute-start | bytes 1572872 | tf_op jit(solution)/shard_map/ppermute | solution.py:36
  230.7 29.3 %collective-permute-start.26 = (bf16[256,1024]{1,0:T(8,128)(2,1)}, bf16[256,1024]{1,0:T(8,128)(2,1)}, u32[]{:S(2)}, u32[]{:S(2)}) collective-permute-start(bf16[256,1024]{1,0:T(8,128)(2,1)} %collective-permute-done.24.refs_5_), channel_id=1, source_target_pairs={{0,4},{4,0},{8,12},{12,8},{16,20},{20,16},{24,28},{28,24},{1,5},{5... | collective-permute-start | bytes 1572872 | tf_op jit(solution)/shard_map/ppermute | solution.py:36
  230.8 35.4 %collective-permute-start.29 = (bf16[256,1024]{1,0:T(8,128)(2,1)}, bf16[256,1024]{1,0:T(8,128)(2,1)}, u32[]{:S(2)}, u32[]{:S(2)}) collective-permute-start(bf16[256,1024]{1,0:T(8,128)(2,1)} %get-tuple-element.115.refs_2_), channel_id=1, source_target_pairs={{16,0},{20,4},{24,8},{28,12},{0,16},{4,20},{8,24},{12,28},{17,1},{... | collective-permute-start | bytes 1572872 | tf_op jit(solution)/shard_map/ppermute | solution.py:31
  254.2 13.3 %all-to-all-start.5 = ((bf16[8,8,2048]{2,1,0:T(8,128)(2,1)}), bf16[8,8,2048]{2,1,0:T(8,128)(2,1)S(1)}, u32[]{:S(2)}, u32[]{:S(2)}) async-start(bf16[8,8,2048]{2,1,0:T(8,128)(2,1)} %broadcast_in_dim.17), calls=%async_computation.5 | async-start | bytes 524288 | tf_op jit(solution)/shard_map/all_to_all | solution.py:343
  267.5 15.5 %collective-permute-start.30 = (bf16[2,8,64,512]{3,2,1,0:T(8,128)(2,1)}, bf16[2,8,64,512]{3,2,1,0:T(8,128)(2,1)}, u32[]{:S(2)}, u32[]{:S(2)}) collective-permute-start(bf16[2,8,64,512]{3,2,1,0:T(8,128)(2,1)} %pad_maximum_fusion.1.refs_0_), channel_id=1, source_target_pairs={{0,1},{1,0},{2,3},{3,2},{4,5},{5,4},{6,7},{7,6},{8,9},{9,8},{10,11... | collective-permute-start | bytes 3145736 | tf_op jit(solution)/shard_map/ppermute | solution.py:300
  268.4 9.6 %collective-permute-start.31 = (bf16[2,256,512]{2,1,0:T(8,128)(2,1)}, bf16[2,256,512]{2,1,0:T(8,128)(2,1)}, u32[]{:S(2)}, u32[]{:S(2)}) collective-permute-start(bf16[2,256,512]{2,1,0:T(8,128)(2,1)} %slice_bitcast_fusion), channel_id=1, source_target_pairs={{0,1},{1,0},{2,3},{3,2},{4,5},{5,4},{6,7},{7,6},{8,9},{9,8},{10,11... | collective-permute-start | bytes 1572872 | tf_op jit(solution)/shard_map/ppermute | solution.py:300
  268.9 14.1 %collective-permute-start.32 = (bf16[256,1024]{1,0:T(8,128)(2,1)}, bf16[256,1024]{1,0:T(8,128)(2,1)}, u32[]{:S(2)}, u32[]{:S(2)}) collective-permute-start(bf16[256,1024]{1,0:T(8,128)(2,1)} %collective-permute-done.29.refs_4_), channel_id=1, source_target_pairs={{0,4},{4,0},{8,12},{12,8},{16,20},{20,16},{24,28},{28,24},{1,5},{5... | collective-permute-start | bytes 1572872 | tf_op jit(solution)/shard_map/ppermute | solution.py:36
  271.8 6.0 %all-to-all-start.6 = ((bf16[4,16,512]{2,1,0:T(8,128)(2,1)}), bf16[4,16,512]{2,1,0:T(8,128)(2,1)S(1)}, u32[]{:S(2)}, u32[]{:S(2)}) async-start(bf16[4,16,512]{2,1,0:T(8,128)(2,1)} %bitcast.20), calls=%async_computation.6 | async-start | bytes 131072 | tf_op jit(solution)/shard_map/all_to_all | solution.py:250
  277.9 11.8 %copy-start.11 = (bf16[2,8,64,512]{3,2,1,0:T(8,128)(2,1)S(1)}, bf16[2,8,64,512]{3,2,1,0:T(8,128)(2,1)}, u32[]{:S(2)}) copy-start(bf16[2,8,64,512]{3,2,1,0:T(8,128)(2,1)} %pad_maximum_fusion.1.refs_0_) | copy-start | bytes 3145732
  277.9 11.8 %copy-start.16 = (bf16[256,1024]{1,0:T(8,128)(2,1)S(1)}, bf16[256,1024]{1,0:T(8,128)(2,1)}, u32[]{:S(2)}) copy-start(bf16[256,1024]{1,0:T(8,128)(2,1)} %copy-done.15) | copy-start | bytes 1572868
  283.0 12.4 %collective-permute-start.33 = (bf16[8,512]{1,0:T(8,128)(2,1)S(1)}, bf16[8,512]{1,0:T(8,128)(2,1)S(1)}, u32[]{:S(2)}, u32[]{:S(2)}) collective-permute-start(bf16[8,512]{1,0:T(8,128)(2,1)S(1)} %get-tuple-element.133), channel_id=1, source_target_pairs={{0,0},{1,8},{2,16},{3,24},{4,4},{5,12},{6,20},{7,28},{8,1},{9,9},{... | collective-permute-start | bytes 24584 | tf_op jit(solution)/shard_map/ppermute | solution.py:266
  286.0 9.4 %collective-permute-start.34 = (bf16[8,512]{1,0:T(8,128)(2,1)S(1)}, bf16[8,512]{1,0:T(8,128)(2,1)S(1)}, u32[]{:S(2)}, u32[]{:S(2)}) collective-permute-start(bf16[8,512]{1,0:T(8,128)(2,1)S(1)} %get-tuple-element.134), channel_id=1, source_target_pairs={{0,4},{1,12},{2,20},{3,28},{4,0},{5,8},{6,16},{7,24},{8,5},{9,13},... | collective-permute-start | bytes 24584 | tf_op jit(solution)/shard_map/ppermute | solution.py:266
  (15 other events, 35.0 us)

commit v19 on v18

--- a/solution.py
+++ b/solution.py
@@ -434,28 +434,24 @@
 
     kv_part = kv_part.reshape(n_dp, image_rows, 2 * local_cols)
     kv_grad = jnp.sum(lax.all_to_all(kv_part, "dp", split_axis=0, concat_axis=0), axis=0)
-    kv_grad_all = everywhere(kv_grad.astype(BF16)).reshape(images, 2 * local_cols)
-    text_parts = [tensor_swap(term[k], k) for k in range(2, n_tensor)]
+    text_parts = [tensor_swap(term[k], k) for k in range(n_tensor - 1, 0, -1)]
+    live_pair = jnp.stack([live_mine, live_y])
+    live_core = tensor_swap(live_pair, 1)
+    kv_grad, live_core, text_parts[-1], attended, *att_next = gate(
+        (kv_grad.astype(BF16), live_core, text_parts[-1], attended, *att_next)
+    )
+    kv_grad_all = everywhere(kv_grad).reshape(images, 2 * local_cols)
     att_far = [line.shift(attended, m) for m in range(2, line.n_z - 1)]
     att_other_next = [line.swap(block) for block in att_next]
-    live_pair = jnp.stack([live_mine, live_y])
-    kv_grad_all, term, live_pair, *staged = gate(
-        (kv_grad_all, term, live_pair, *att_other_next, *text_parts, *att_far)
-    )
-    att_other_next, staged = staged[:2], staged[2:]
-    text_parts, att_far = staged[: n_tensor - 2], staged[n_tensor - 2 :]
-
     att_other_far = [line.swap(block) for block in att_far]
-    live_core = tensor_swap(live_pair, 1)
-    text_parts.append(tensor_swap(term[1], 1))
+    text_grad = call(
+        sum_kernel, place, (term, *text_parts), [shape((rows, width // n_tensor), BF16)]
+    )
+    kv_grad_all, text_grad, *att_other_next = gate((kv_grad_all, text_grad, *att_other_next))
+
     image_term = matmul(kv_grad_all[:, :local_cols], key_weight, BACK)
     image_term = image_term + matmul(kv_grad_all[:, local_cols:], value_weight, BACK)
-    text_grad = call(
-        sum_kernel, place, (term, *text_parts), [shape((rows, width // n_tensor), BF16)]
-    )
-    image_grad, live_core, text_grad, *att_other_far = to_owner(
-        line, image_term.astype(BF16), live_core, text_grad, *att_other_far
-    )
+    image_grad, *att_other_far = to_owner(line, image_term.astype(BF16), *att_other_far)
     image_grad = image_grad.reshape(samples, image_own, width // n_tensor)
     text_grad = text_grad.reshape(samples, tok_rows, width // n_tensor)
 

time: 298 us -> 306 us (1.027)
  waiting for transfers between devices: 125 us -> 133 us
    all_to_all x2, waiting for transfers between devices: 24.5 us -> 41.9 us  [everywhere(): return lax.all_to_all(copies, 'dp', split_axis=0, concat_axis=0)]
    all_to_all x1, waiting for transfers between devices: 18.8 us -> 11.9 us  [shards(): lax.all_to_all(kv_part, 'dp', split_axis=0, concat_axis=0)]
    ppermute x13, waiting for transfers between devices: 22.5 us -> 16 us  [move(): return lax.ppermute(block, 'dp', pairs)]
    unnamed x43 -> x49, local copies, waits for them, and re-layouts: 12.6 us -> 12.8 us
  transfers between devices with their start and end apart: 42 -> 42, of which waited for: 14 -> 14; matrix products, arithmetic and copies ran while one was open for 8% -> 7% of each run, Pallas kernels for 12% -> 11%
where the time goes in v19:
time: 306 us; the launch traced here: 304 us
  waiting for transfers between devices  133 us (43%)
  starting transfers between devices  97.9 us (32%)
  Pallas kernels  33.2 us (11%)
  local copies, waits for them, and re-layouts  20.2 us (7%)
  other arithmetic  14.8 us (5%)
  matrix products  4.58 us (1%)
    all_to_all x2, waiting for transfers between devices, everywhere(): return lax.all_to_all(copies, 'dp', split_axis=0, concat_axis=0)  41.9 us
    pallas_call x8, Pallas kernels, call(): pl.pallas_call(kernel, out_shape=outs[0] if single else outs, in_specs=[p...  33.2 us
    all_to_all x1, waiting for transfers between devices, shards(): lax.all_to_all(part_kv, 'dp', split_axis=0, concat_axis=0)  28.5 us
    ppermute x13, starting transfers between devices, move(): return lax.ppermute(block, 'dp', pairs)  26.7 us
    ppermute x12, waiting for transfers between devices, swap(): return lax.ppermute(block, 'dp', pairs)  19.2 us
    ppermute x12, starting transfers between devices, swap(): return lax.ppermute(block, 'dp', pairs)  18.3 us
    all_to_all x2, starting transfers between devices, everywhere(): return lax.all_to_all(copies, 'dp', split_axis=0, concat_axis=0)  17.5 us
    ppermute x13, waiting for transfers between devices, move(): return lax.ppermute(block, 'dp', pairs)  16 us
  transfers between devices with their start and end apart: 42, of which 14 were waited for; matrix products, arithmetic and copies ran while one was open for 7% of the time, Pallas kernels for 11%

profile of v19, /device:TPU:4, one launch (start us, length us, event | category | flops | bytes accessed | tf_op | source)
XLA Modules:
  0.0 304.4 jit_solution(15307963720983864684)
XLA Ops:
  2.1 5.5 %collective-permute-start.3 = (bf16[512,1024]{1,0:T(8,128)(2,1)}, bf16[512,1024]{1,0:T(8,128)(2,1)}, u32[]{:S(2)}, u32[]{:S(2)}) collective-permute-start(bf16[512,1024]{1,0:T(8,128)(2,1)} %refs_0_.1), channel_id=1, source_target_pairs={{0,8},{4,12},{8,16},{12,20},{16,24},{20,28},{1,9},{5,13},{9,17},{1... | collective-permute-start | bytes 3145736 | tf_op jit(solution)/shard_map/ppermute | solution.py:31
  7.6 2.2 constant_dynamic-slice_fusion.3
  11.4 1.8 broadcast_select_fusion
  15.3 4.9 %all-to-all-start = ((bf16[8,8,512]{2,0,1:T(8,128)(2,1)}), bf16[8,8,512]{2,0,1:T(8,128)(2,1)S(1)}, u32[]{:S(2)}, u32[]{:S(2)}) async-start(bf16[8,8,512]{2,0,1:T(8,128)(2,1)} %copy.14), calls=%async_computation | async-start | bytes 131072 | tf_op jit(solution)/shard_map/all_to_all | solution.py:313
  20.2 4.8 %collective-permute-done = bf16[512,512]{1,0:T(8,128)(2,1)} collective-permute-done((bf16[512,512]{1,0:T(8,128)(2,1)}, bf16[512,512]{1,0:T(8,128)(2,1)}, u32[]{:S(2)}, u32[]{:S(2)}) %collective-permute-start) | collective-permute-done | bytes 524320 | tf_op jit(solution)/shard_map/ppermute | solution.py:36
  25.0 2.4 pad_maximum_fusion.refs_0_
  27.4 7.7 %all-to-all-done = bf16[8,8,512]{2,0,1:T(8,128)(2,1)S(1)} async-done(((bf16[8,8,512]{2,0,1:T(8,128)(2,1)}), bf16[8,8,512]{2,0,1:T(8,128)(2,1)S(1)}, u32[]{:S(2)}, u32[]{:S(2)}) %all-to-all-start) | async-done | bytes 65568 | tf_op jit(solution)/shard_map/all_to_all | solution.py:313
  38.0 5.5 %collective-permute-start.9 = (bf16[512,1024]{1,0:T(8,128)(2,1)}, bf16[512,1024]{1,0:T(8,128)(2,1)}, u32[]{:S(2)}, u32[]{:S(2)}) collective-permute-start(bf16[512,1024]{1,0:T(8,128)(2,1)} %pad_maximum_fusion.refs_0_), channel_id=1, source_target_pairs={{0,8},{4,12},{8,16},{12,20},{16,24},{20,28},{1,9},{5,13},{9,17},{1... | collective-permute-start | bytes 3145736 | tf_op jit(solution)/shard_map/ppermute | solution.py:31
  44.8 1.7 collective-permute-start.7
  48.3 10.6 %collective-permute-done.4.refs_2_.refs_5_ = bf16[512,1024]{1,0:T(8,128)(2,1)S(1)} collective-permute-done((bf16[512,1024]{1,0:T(8,128)(2,1)}, bf16[512,1024]{1,0:T(8,128)(2,1)S(1)}, u32[]{:S(2)}, u32[]{:S(2)}) %collective-permute-start.4) | collective-permute-done | bytes 1048608 | tf_op jit(solution)/shard_map/ppermute | solution.py:36
  59.9 3.4 %collective-permute-start.5 = (bf16[512,1024]{1,0:T(8,128)(2,1)}, bf16[512,1024]{1,0:T(8,128)(2,1)}, u32[]{:S(2)}, u32[]{:S(2)}) collective-permute-start(bf16[512,1024]{1,0:T(8,128)(2,1)} %collective-permute-done.2.refs_1_), channel_id=1, source_target_pairs={{0,4},{4,0},{8,12},{12,8},{16,20},{20,16},{1,5},{5,1},{9,13},{13,9... | collective-permute-start | bytes 3145736 | tf_op jit(solution)/shard_map/ppermute | solution.py:36
  64.1 4.1 %all-to-all-start.1 = ((f32[8,8,2048]{2,1,0:T(8,128)}), f32[8,8,2048]{2,1,0:T(8,128)}, u32[]{:S(2)}, u32[]{:S(2)}) async-start(f32[8,8,2048]{2,1,0:T(8,128)} %maximum_bitcast_fusion), calls=%async_computation.1 | async-start | bytes 1048576 | tf_op jit(solution)/shard_map/all_to_all | solution.py:334
  68.3 28.5 %all-to-all-done.1 = f32[8,8,2048]{2,1,0:T(8,128)} async-done(((f32[8,8,2048]{2,1,0:T(8,128)}), f32[8,8,2048]{2,1,0:T(8,128)}, u32[]{:S(2)}, u32[]{:S(2)}) %all-to-all-start.1) | async-done | bytes 524320 | tf_op jit(solution)/shard_map/all_to_all | solution.py:334
  97.9 2.3 broadcast_select_fusion.2.refs_1_.refs_3_
  103.6 1.7 collective-permute-start.11
  105.3 1.7 collective-permute-start.13
  107.6 12.5 %all-to-all-start.2 = ((bf16[8,8,2048]{2,1,0:T(8,128)(2,1)}), bf16[8,8,2048]{2,1,0:T(8,128)(2,1)S(1)}, u32[]{:S(2)}, u32[]{:S(2)}) async-start(bf16[8,8,2048]{2,1,0:T(8,128)(2,1)} %broadcast_in_dim.16), calls=%async_computation.2 | async-start | bytes 524288 | tf_op jit(solution)/shard_map/all_to_all | solution.py:343
  120.2 1.6 copy-done.1
  124.2 3.1 %shard_map.103.part = f32[256,1024]{1,0:T(8,128)S(1)} custom-call(s32[4]{0:T(128)S(1)} %pad_add_fusion.place, bf16[256,4096]{1,0:T(8,128)(2,1)S(1)} %bitcast.43, bf16[512,1024]{1,0:T(8,128)(2,1)S(1)} %copy-done.3, bf16[512,1024]{1,0:T(8,128)(2,1)} %collective-permute-done.2.refs_1_, bf16[512,1024]{1,0:T(8,128)(2,1)S(1)} %copy-done.6, ...), custom_call_target="tpu_custom_call" | custom-call | flops 1073741824 | bytes 7340032 | tf_op jit(solution)/shard_map/pallas_call | solution.py:228
  128.4 23.1 %all-to-all-done.2 = bf16[8,8,2048]{2,1,0:T(8,128)(2,1)S(1)} async-done(((bf16[8,8,2048]{2,1,0:T(8,128)(2,1)}), bf16[8,8,2048]{2,1,0:T(8,128)(2,1)S(1)}, u32[]{:S(2)}, u32[]{:S(2)}) %all-to-all-start.2) | async-done | bytes 262176 | tf_op jit(solution)/shard_map/all_to_all | solution.py:343
  152.1 2.3 broadcast_select_fusion.1.refs_2_
  155.8 3.0 collective-permute-start.19
  160.0 6.6 %all-to-all-start.3 = ((bf16[1,64,8,512]{3,1,0,2:T(8,128)(2,1)}), bf16[1,64,8,512]{3,1,0,2:T(8,128)(2,1)}, u32[]{:S(2)}, u32[]{:S(2)}) async-start(bf16[1,64,8,512]{3,1,0,2:T(8,128)(2,1)} %copy.15), calls=%async_computation.3 | async-start | bytes 1048576 | tf_op jit(solution)/shard_map/all_to_all | solution.py:368
  167.1 1.6 collective-permute-done.15.by_core
  170.7 3.6 %shard_map.104 = (f32[256,512]{1,0:T(8,128)S(1)}, f32[256,512]{1,0:T(8,128)S(1)}) custom-call(s32[4]{0:T(128)S(1)} %pad_add_fusion.place, bf16[256,4096]{1,0:T(8,128)(2,1)S(1)} %bitcast.41, bf16[256,1024]{1,0:T(8,128)(2,1)} %collective-permute-done.1.mine, bf16[256,1024]{1,0:T(8,128)(2,1)S(1)} %collective-permute-done.15.by_core, ...), custom_call_target="tpu_custom_call" | custom-call | flops 1073741824 | bytes 8388608 | tf_op jit(solution)/shard_map/pallas_call | solution.py:228
  174.3 10.9 %collective-permute-done.18.refs_3_ = bf16[512,1024]{1,0:T(8,128)(2,1)} collective-permute-done((bf16[512,1024]{1,0:T(8,128)(2,1)}, bf16[512,1024]{1,0:T(8,128)(2,1)}, u32[]{:S(2)}, u32[]{:S(2)}) %collective-permute-start.18) | collective-permute-done | bytes 1048608 | tf_op jit(solution)/shard_map/ppermute | solution.py:31
  185.2 4.4 %shard_map.105 = (bf16[256,512]{1,0:T(8,128)(2,1)S(1)}, bf16[256,512]{1,0:T(8,128)(2,1)}) custom-call(s32[4]{0:T(128)S(1)} %pad_add_fusion.place, bf16[256,4096]{1,0:T(8,128)(2,1)S(1)} %bitcast.42, bf16[256,1024]{1,0:T(8,128)(2,1)} %collective-permute-done.1.mine, bf16[256,1024]{1,0:T(8,128)(2,1)S(1)} %collective-permute-done.15.by_core, ...), custom_call_target="tpu_custom_call" | custom-call | flops 1073741824 | bytes 7864320 | tf_op jit(solution)/shard_map/pallas_call | solution.py:228
  195.0 5.5 %shard_map.106 = (bf16[256,1024]{1,0:T(8,128)(2,1)S(1)}, bf16[256,1024]{1,0:T(8,128)(2,1)S(1)}) custom-call(s32[4]{0:T(128)S(1)} %pad_add_fusion.place, bf16[256,4096]{1,0:T(8,128)(2,1)S(1)} %bitcast.44, bf16[64,2048]{1,0:T(8,128)(2,1)S(1)} %bitcast.45, f32[256,1024]{1,0:T(8,128)S(1)} %copy-done.9, bf16[512,1024]{1,0:T(8,128)(2,1)} %collective-permute-done.3.refs_0_.refs_2_, ...), custom_call_target="tpu_custom_call" | custom-call | flops 1073741824 | bytes 10747904 | tf_op jit(solution)/shard_map/pallas_call | solution.py:228
  200.5 4.4 %collective-permute-start.23 = (bf16[256,1024]{1,0:T(8,128)(2,1)S(1)}, bf16[256,1024]{1,0:T(8,128)(2,1)S(1)}, u32[]{:S(2)}, u32[]{:S(2)}) collective-permute-start(bf16[256,1024]{1,0:T(8,128)(2,1)S(1)} %get-tuple-element.122.refs_2_), channel_id=1, source_target_pairs={{8,0},{12,4},{16,8},{20,12},{24,16},{28,20},{0,24},{4,28},{9,1},{1... | collective-permute-start | bytes 1572872 | tf_op jit(solution)/shard_map/ppermute | solution.py:31
  204.9 1.7 collective-permute-start.22
  206.6 1.9 shard_map.107
  209.3 6.7 %shard_map.108.term = bf16[4,2,256,512]{3,2,1,0:T(8,128)(2,1)S(1)} custom-call(s32[4]{0:T(128)S(1)} %pad_add_fusion.place, bf16[256,1024]{1,0:T(8,128)(2,1)S(1)} %get-tuple-element.106.query_grad, bf16[512,1024]{1,0:T(8,128)(2,1)S(1)} %copy-done.4, bf16[512,1024]{1,0:T(8,128)(2,1)} %collective-permute-done.2.refs_1_, ...), custom_call_target="tpu_custom_call" | custom-call | flops 2147483648 | bytes 13107200 | tf_op jit(solution)/shard_map/pallas_call | solution.py:228
  216.1 5.1 %collective-permute-done.24.refs_5_ = bf16[256,1024]{1,0:T(8,128)(2,1)S(1)} collective-permute-done((bf16[256,1024]{1,0:T(8,128)(2,1)S(1)}, bf16[256,1024]{1,0:T(8,128)(2,1)S(1)}, u32[]{:S(2)}, u32[]{:S(2)}) %collective-permute-start.24) | collective-permute-done | bytes 524320 | tf_op jit(solution)/shard_map/ppermute | solution.py:31
  222.2 2.2 pad_maximum_fusion.1.refs_0_
  224.3 4.4 %all-to-all-start.4 = ((f32[8,8,2048]{2,1,0:T(8,128)}), f32[8,8,2048]{2,1,0:T(8,128)}, u32[]{:S(2)}, u32[]{:S(2)}) async-start(f32[8,8,2048]{2,1,0:T(8,128)} %bitcast.47), calls=%async_computation.4 | async-start | bytes 1048576 | tf_op jit(solution)/shard_map/all_to_all | solution.py:436
  232.1 11.9 %all-to-all-done.4 = f32[8,8,2048]{2,1,0:T(8,128)} async-done(((f32[8,8,2048]{2,1,0:T(8,128)}), f32[8,8,2048]{2,1,0:T(8,128)}, u32[]{:S(2)}, u32[]{:S(2)}) %all-to-all-start.4) | async-done | bytes 524320 | tf_op jit(solution)/shard_map/all_to_all | solution.py:436
  248.0 5.0 %all-to-all-start.5 = ((bf16[8,8,2048]{2,1,0:T(8,128)(2,1)}), bf16[8,8,2048]{2,1,0:T(8,128)(2,1)S(1)}, u32[]{:S(2)}, u32[]{:S(2)}) async-start(bf16[8,8,2048]{2,1,0:T(8,128)(2,1)} %broadcast_in_dim.17), calls=%async_computation.5 | async-start | bytes 524288 | tf_op jit(solution)/shard_map/all_to_all | solution.py:343
  253.0 2.9 collective-permute-done.28.refs_1_
  256.0 2.4 shard_map.109
  258.4 18.7 %all-to-all-done.5 = bf16[8,8,2048]{2,1,0:T(8,128)(2,1)S(1)} async-done(((bf16[8,8,2048]{2,1,0:T(8,128)(2,1)}), bf16[8,8,2048]{2,1,0:T(8,128)(2,1)S(1)}, u32[]{:S(2)}, u32[]{:S(2)}) %all-to-all-start.5) | async-done | bytes 262176 | tf_op jit(solution)/shard_map/all_to_all | solution.py:343
  277.1 1.7 collective-permute-start.32
  279.3 2.3 fusion
  281.6 3.8 %all-to-all-start.6 = ((bf16[4,16,512]{2,1,0:T(8,128)(2,1)}), bf16[4,16,512]{2,1,0:T(8,128)(2,1)S(1)}, u32[]{:S(2)}, u32[]{:S(2)}) async-start(bf16[4,16,512]{2,1,0:T(8,128)(2,1)} %bitcast.22), calls=%async_computation.6 | async-start | bytes 131072 | tf_op jit(solution)/shard_map/all_to_all | solution.py:250
  285.4 2.3 all-to-all-done.6
  287.7 3.7 %collective-permute-done.32.refs_8_ = bf16[256,1024]{1,0:T(8,128)(2,1)} collective-permute-done((bf16[256,1024]{1,0:T(8,128)(2,1)}, bf16[256,1024]{1,0:T(8,128)(2,1)}, u32[]{:S(2)}, u32[]{:S(2)}) %collective-permute-start.32) | collective-permute-done | bytes 524320 | tf_op jit(solution)/shard_map/ppermute | solution.py:36
  291.4 3.0 %collective-permute-start.33 = (bf16[8,512]{1,0:T(8,128)(2,1)S(1)}, bf16[8,512]{1,0:T(8,128)(2,1)S(1)}, u32[]{:S(2)}, u32[]{:S(2)}) collective-permute-start(bf16[8,512]{1,0:T(8,128)(2,1)S(1)} %get-tuple-element.134), channel_id=1, source_target_pairs={{0,0},{1,8},{2,16},{3,24},{4,4},{5,12},{6,20},{7,28},{8,1},{9,9},{... | collective-permute-start | bytes 24584 | tf_op jit(solution)/shard_map/ppermute | solution.py:266
  294.4 3.8 %collective-permute-start.34 = (bf16[8,512]{1,0:T(8,128)(2,1)S(1)}, bf16[8,512]{1,0:T(8,128)(2,1)S(1)}, u32[]{:S(2)}, u32[]{:S(2)}) collective-permute-start(bf16[8,512]{1,0:T(8,128)(2,1)S(1)} %get-tuple-element.135), channel_id=1, source_target_pairs={{0,4},{1,12},{2,20},{3,28},{4,0},{5,8},{6,16},{7,24},{8,5},{9,13},... | collective-permute-start | bytes 24584 | tf_op jit(solution)/shard_map/ppermute | solution.py:266
  298.3 5.5 %shard_map.110 = bf16[1024,512]{1,0:T(8,128)(2,1)} custom-call(s32[4]{0:T(128)S(1)} %pad_add_fusion.place, bf16[2,8,64,512]{3,2,1,0:T(8,128)(2,1)} %pad_maximum_fusion.1.refs_0_, bf16[2,8,64,512]{3,2,1,0:T(8,128)(2,1)} %collective-permute-done.25.refs_1_, bf16[256,1024]{1,0:T(8,128)(2,1)S(1)} %copy-done.15, bf16[256,1024]{1,0:T(8,128)(2,1)S(1)} %copy-done.17, ...), custom_call_target="tpu_custom_call" | custom-call | flops 2147483648 | bytes 7340032 | tf_op jit(solution)/shard_map/pallas_call | solution.py:228
  (122 shorter events, 42.7 us)
Async XLA Ops:
  0.6 47.4 %copy-start = (bf16[512,1024]{1,0:T(8,128)(2,1)S(1)}, bf16[512,1024]{1,0:T(8,128)(2,1)}, u32[]{:S(2)}) copy-start(bf16[512,1024]{1,0:T(8,128)(2,1)} %param.14) | copy-start | bytes 3145732
  0.7 34.5 %collective-permute-start.2 = (bf16[512,1024]{1,0:T(8,128)(2,1)}, bf16[512,1024]{1,0:T(8,128)(2,1)}, u32[]{:S(2)}, u32[]{:S(2)}) collective-permute-start(bf16[512,1024]{1,0:T(8,128)(2,1)} %refs_0_.1), channel_id=1, source_target_pairs={{8,0},{12,4},{16,8},{20,12},{24,16},{28,20},{9,1},{13,5},{17,9},{2... | collective-permute-start | bytes 3145736 | tf_op jit(solution)/shard_map/ppermute | solution.py:31
  2.1 33.0 %collective-permute-start.3 = (bf16[512,1024]{1,0:T(8,128)(2,1)}, bf16[512,1024]{1,0:T(8,128)(2,1)}, u32[]{:S(2)}, u32[]{:S(2)}) collective-permute-start(bf16[512,1024]{1,0:T(8,128)(2,1)} %refs_0_.1), channel_id=1, source_target_pairs={{0,8},{4,12},{8,16},{12,20},{16,24},{20,28},{1,9},{5,13},{9,17},{1... | collective-permute-start | bytes 3145736 | tf_op jit(solution)/shard_map/ppermute | solution.py:31
  9.9 15.2 %collective-permute-start = (bf16[512,512]{1,0:T(8,128)(2,1)}, bf16[512,512]{1,0:T(8,128)(2,1)}, u32[]{:S(2)}, u32[]{:S(2)}) collective-permute-start(bf16[512,512]{1,0:T(8,128)(2,1)} %get-tuple-element.133), channel_id=1, source_target_pairs={{0,4},{4,0},{8,12},{12,8},{16,20},{20,16},{24,28},{28,24},{1,5},{5... | collective-permute-start | bytes 1572872 | tf_op jit(solution)/shard_map/ppermute | solution.py:36
  14.1 21.0 %collective-permute-start.1 = (bf16[256,1024]{1,0:T(8,128)(2,1)}, bf16[256,1024]{1,0:T(8,128)(2,1)}, u32[]{:S(2)}, u32[]{:S(2)}) collective-permute-start(bf16[256,1024]{1,0:T(8,128)(2,1)} %constant_dynamic-slice_fusion.1), channel_id=1, source_target_pairs={{0,4},{4,0},{8,12},{12,8},{16,20},{20,16},{24,28},{28,24},{1,5},{5... | collective-permute-start | bytes 1572872 | tf_op jit(solution)/shard_map/ppermute | solution.py:36
  15.3 19.8 %all-to-all-start = ((bf16[8,8,512]{2,0,1:T(8,128)(2,1)}), bf16[8,8,512]{2,0,1:T(8,128)(2,1)S(1)}, u32[]{:S(2)}, u32[]{:S(2)}) async-start(bf16[8,8,512]{2,0,1:T(8,128)(2,1)} %copy.14), calls=%async_computation | async-start | bytes 131072 | tf_op jit(solution)/shard_map/all_to_all | solution.py:313
  35.1 23.8 %collective-permute-start.4 = (bf16[512,1024]{1,0:T(8,128)(2,1)}, bf16[512,1024]{1,0:T(8,128)(2,1)S(1)}, u32[]{:S(2)}, u32[]{:S(2)}) collective-permute-start(bf16[512,1024]{1,0:T(8,128)(2,1)} %refs_0_.1), channel_id=1, source_target_pairs={{0,4},{4,0},{8,12},{12,8},{16,20},{20,16},{24,28},{28,24},{1,5},{5... | collective-permute-start | bytes 3145736 | tf_op jit(solution)/shard_map/ppermute | solution.py:36
  36.7 61.1 %collective-permute-start.8 = (bf16[512,1024]{1,0:T(8,128)(2,1)}, bf16[512,1024]{1,0:T(8,128)(2,1)}, u32[]{:S(2)}, u32[]{:S(2)}) collective-permute-start(bf16[512,1024]{1,0:T(8,128)(2,1)} %pad_maximum_fusion.refs_0_), channel_id=1, source_target_pairs={{8,0},{12,4},{16,8},{20,12},{24,16},{28,20},{9,1},{13,5},{17,9},{2... | collective-permute-start | bytes 3145736 | tf_op jit(solution)/shard_map/ppermute | solution.py:31
  38.0 59.9 %collective-permute-start.9 = (bf16[512,1024]{1,0:T(8,128)(2,1)}, bf16[512,1024]{1,0:T(8,128)(2,1)}, u32[]{:S(2)}, u32[]{:S(2)}) collective-permute-start(bf16[512,1024]{1,0:T(8,128)(2,1)} %pad_maximum_fusion.refs_0_), channel_id=1, source_target_pairs={{0,8},{4,12},{8,16},{12,20},{16,24},{20,28},{1,9},{5,13},{9,17},{1... | collective-permute-start | bytes 3145736 | tf_op jit(solution)/shard_map/ppermute | solution.py:31
  43.5 54.3 %collective-permute-start.6 = (bf16[512,1024]{1,0:T(8,128)(2,1)}, bf16[512,1024]{1,0:T(8,128)(2,1)}, u32[]{:S(2)}, u32[]{:S(2)}) collective-permute-start(bf16[512,1024]{1,0:T(8,128)(2,1)} %collective-permute-done.2.refs_1_), channel_id=1, source_target_pairs={{8,0},{12,4},{16,8},{20,12},{9,1},{13,5},{17,9},{21,13},{10,2},{14... | collective-permute-start | bytes 3145736 | tf_op jit(solution)/shard_map/ppermute | solution.py:31
  44.8 53.0 %collective-permute-start.7 = (bf16[512,1024]{1,0:T(8,128)(2,1)}, bf16[512,1024]{1,0:T(8,128)(2,1)}, u32[]{:S(2)}, u32[]{:S(2)}) collective-permute-start(bf16[512,1024]{1,0:T(8,128)(2,1)} %collective-permute-done.3.refs_0_.refs_2_), channel_id=1, source_target_pairs={{8,16},{12,20},{16,24},{20,28},{9,17},{13,21},{17,25},{21,29},{10,... | collective-permute-start | bytes 3145736 | tf_op jit(solution)/shard_map/ppermute | solution.py:31
  59.9 38.0 %collective-permute-start.5 = (bf16[512,1024]{1,0:T(8,128)(2,1)}, bf16[512,1024]{1,0:T(8,128)(2,1)}, u32[]{:S(2)}, u32[]{:S(2)}) collective-permute-start(bf16[512,1024]{1,0:T(8,128)(2,1)} %collective-permute-done.2.refs_1_), channel_id=1, source_target_pairs={{0,4},{4,0},{8,12},{12,8},{16,20},{20,16},{1,5},{5,1},{9,13},{13,9... | collective-permute-start | bytes 3145736 | tf_op jit(solution)/shard_map/ppermute | solution.py:36
  64.1 32.6 %all-to-all-start.1 = ((f32[8,8,2048]{2,1,0:T(8,128)}), f32[8,8,2048]{2,1,0:T(8,128)}, u32[]{:S(2)}, u32[]{:S(2)}) async-start(f32[8,8,2048]{2,1,0:T(8,128)} %maximum_bitcast_fusion), calls=%async_computation.1 | async-start | bytes 1048576 | tf_op jit(solution)/shard_map/all_to_all | solution.py:334
  100.2 51.4 %collective-permute-start.12 = (bf16[512,1024]{1,0:T(8,128)(2,1)}, bf16[512,1024]{1,0:T(8,128)(2,1)}, u32[]{:S(2)}, u32[]{:S(2)}) collective-permute-start(bf16[512,1024]{1,0:T(8,128)(2,1)} %broadcast_select_fusion.2.refs_1_.refs_3_), channel_id=1, source_target_pairs={{8,0},{12,4},{16,24},{20,28},{9,1},{13,5},{17,25},{21,29},{10,2},{... | collective-permute-start | bytes 3145736 | tf_op jit(solution)/shard_map/ppermute | solution.py:31
  101.5 50.1 %collective-permute-start.14 = (bf16[512,1024]{1,0:T(8,128)(2,1)}, bf16[512,1024]{1,0:T(8,128)(2,1)}, u32[]{:S(2)}, u32[]{:S(2)}) collective-permute-start(bf16[512,1024]{1,0:T(8,128)(2,1)} %broadcast_select_fusion.2.refs_1_.refs_3_), channel_id=1, source_target_pairs={{0,4},{4,0},{8,12},{12,8},{16,20},{20,16},{24,28},{28,24},{1,5},{5... | collective-permute-start | bytes 3145736 | tf_op jit(solution)/shard_map/ppermute | solution.py:36
  102.3 49.3 %collective-permute-start.10 = (bf16[512,1024]{1,0:T(8,128)(2,1)}, bf16[512,1024]{1,0:T(8,128)(2,1)}, u32[]{:S(2)}, u32[]{:S(2)}) collective-permute-start(bf16[512,1024]{1,0:T(8,128)(2,1)} %collective-permute-done.8.refs_1_), channel_id=1, source_target_pairs={{8,0},{12,4},{16,8},{20,12},{9,1},{13,5},{17,9},{21,13},{10,2},{14... | collective-permute-start | bytes 3145736 | tf_op jit(solution)/shard_map/ppermute | solution.py:31
  103.6 48.0 %collective-permute-start.11 = (bf16[512,1024]{1,0:T(8,128)(2,1)}, bf16[512,1024]{1,0:T(8,128)(2,1)}, u32[]{:S(2)}, u32[]{:S(2)}) collective-permute-start(bf16[512,1024]{1,0:T(8,128)(2,1)} %collective-permute-done.9.refs_2_), channel_id=1, source_target_pairs={{8,16},{12,20},{16,24},{20,28},{9,17},{13,21},{17,25},{21,29},{10,... | collective-permute-start | bytes 3145736 | tf_op jit(solution)/shard_map/ppermute | solution.py:31
  105.3 46.3 %collective-permute-start.13 = (bf16[512,1024]{1,0:T(8,128)(2,1)}, bf16[512,1024]{1,0:T(8,128)(2,1)}, u32[]{:S(2)}, u32[]{:S(2)}) collective-permute-start(bf16[512,1024]{1,0:T(8,128)(2,1)} %collective-permute-done.3.refs_0_.refs_2_), channel_id=1, source_target_pairs={{8,12},{12,8},{16,20},{20,16},{24,28},{28,24},{9,13},{13,9},{17,21... | collective-permute-start | bytes 3145736 | tf_op jit(solution)/shard_map/ppermute | solution.py:36
  107.6 43.9 %all-to-all-start.2 = ((bf16[8,8,2048]{2,1,0:T(8,128)(2,1)}), bf16[8,8,2048]{2,1,0:T(8,128)(2,1)S(1)}, u32[]{:S(2)}, u32[]{:S(2)}) async-start(bf16[8,8,2048]{2,1,0:T(8,128)(2,1)} %broadcast_in_dim.16), calls=%async_computation.2 | async-start | bytes 524288 | tf_op jit(solution)/shard_map/all_to_all | solution.py:343
  151.6 15.0 %collective-permute-start.16 = (bf16[256,1024]{1,0:T(8,128)(2,1)}, bf16[256,1024]{1,0:T(8,128)(2,1)}, u32[]{:S(2)}, u32[]{:S(2)}) collective-permute-start(bf16[256,1024]{1,0:T(8,128)(2,1)} %collective-permute-done.1.mine), channel_id=1, source_target_pairs={{0,2},{1,3},{2,0},{3,1},{4,6},{5,7},{6,4},{7,5},{8,10},{9,11},{10,... | collective-permute-start | bytes 1572872 | tf_op jit(solution)/shard_map/ppermute | solution.py:300
  154.5 30.7 %collective-permute-start.18 = (bf16[512,1024]{1,0:T(8,128)(2,1)}, bf16[512,1024]{1,0:T(8,128)(2,1)}, u32[]{:S(2)}, u32[]{:S(2)}) collective-permute-start(bf16[512,1024]{1,0:T(8,128)(2,1)} %broadcast_select_fusion.1.refs_2_), channel_id=1, source_target_pairs={{8,0},{12,4},{16,24},{20,28},{9,1},{13,5},{17,25},{21,29},{10,2},{... | collective-permute-start | bytes 3145736 | tf_op jit(solution)/shard_map/ppermute | solution.py:31
  155.8 36.4 %collective-permute-start.19 = (bf16[512,1024]{1,0:T(8,128)(2,1)}, bf16[512,1024]{1,0:T(8,128)(2,1)}, u32[]{:S(2)}, u32[]{:S(2)}) collective-permute-start(bf16[512,1024]{1,0:T(8,128)(2,1)} %collective-permute-done.12.refs_2_.refs_4_), channel_id=1, source_target_pairs={{0,4},{4,0},{24,28},{28,24},{1,5},{5,1},{25,29},{29,25},{2,6},{6,2... | collective-permute-start | bytes 3145736 | tf_op jit(solution)/shard_map/ppermute | solution.py:36
  160.0 30.6 %all-to-all-start.3 = ((bf16[1,64,8,512]{3,1,0,2:T(8,128)(2,1)}), bf16[1,64,8,512]{3,1,0,2:T(8,128)(2,1)}, u32[]{:S(2)}, u32[]{:S(2)}) async-start(bf16[1,64,8,512]{3,1,0,2:T(8,128)(2,1)} %copy.15), calls=%async_computation.3 | async-start | bytes 1048576 | tf_op jit(solution)/shard_map/all_to_all | solution.py:368
  166.6 2.1 collective-permute-start.15
  166.6 2.9 collective-permute-start.17
  190.3 14.6 %collective-permute-start.20 = (bf16[256,512]{1,0:T(8,128)(2,1)}, bf16[256,512]{1,0:T(8,128)(2,1)S(1)}, u32[]{:S(2)}, u32[]{:S(2)}) collective-permute-start(bf16[256,512]{1,0:T(8,128)(2,1)} %get-tuple-element.103), channel_id=1, source_target_pairs={{0,4},{4,0},{8,12},{12,8},{16,20},{20,16},{24,28},{28,24},{1,5},{5... | collective-permute-start | bytes 786440 | tf_op jit(solution)/shard_map/ppermute | solution.py:36
  190.6 25.4 %collective-permute-start.21 = (bf16[8,64,512]{2,1,0:T(8,128)(2,1)}, bf16[8,64,512]{2,1,0:T(8,128)(2,1)S(1)}, u32[]{:S(2)}, u32[]{:S(2)}) collective-permute-start(bf16[8,64,512]{2,1,0:T(8,128)(2,1)} %bitcast.12), channel_id=1, source_target_pairs={{0,2},{1,3},{2,0},{3,1},{4,6},{5,7},{6,4},{7,5},{8,10},{9,11},{10,... | collective-permute-start | bytes 1572872 | tf_op jit(solution)/shard_map/ppermute | solution.py:300
  200.5 15.6 %copy-start.14 = (bf16[256,1024]{1,0:T(8,128)(2,1)}, bf16[256,1024]{1,0:T(8,128)(2,1)S(1)}, u32[]{:S(2)}) copy-start(bf16[256,1024]{1,0:T(8,128)(2,1)S(1)} %get-tuple-element.122.refs_2_) | copy-start | bytes 1572868
  200.5 15.6 %collective-permute-start.23 = (bf16[256,1024]{1,0:T(8,128)(2,1)S(1)}, bf16[256,1024]{1,0:T(8,128)(2,1)S(1)}, u32[]{:S(2)}, u32[]{:S(2)}) collective-permute-start(bf16[256,1024]{1,0:T(8,128)(2,1)S(1)} %get-tuple-element.122.refs_2_), channel_id=1, source_target_pairs={{8,0},{12,4},{16,8},{20,12},{24,16},{28,20},{0,24},{4,28},{9,1},{1... | collective-permute-start | bytes 1572872 | tf_op jit(solution)/shard_map/ppermute | solution.py:31
  204.9 16.3 %collective-permute-start.24 = (bf16[256,1024]{1,0:T(8,128)(2,1)S(1)}, bf16[256,1024]{1,0:T(8,128)(2,1)S(1)}, u32[]{:S(2)}, u32[]{:S(2)}) collective-permute-start(bf16[256,1024]{1,0:T(8,128)(2,1)S(1)} %get-tuple-element.122.refs_2_), channel_id=1, source_target_pairs={{24,0},{28,4},{0,8},{4,12},{8,16},{12,20},{16,24},{20,28},{25,1},{... | collective-permute-start | bytes 1572872 | tf_op jit(solution)/shard_map/ppermute | solution.py:31
  204.9 16.3 %collective-permute-start.22 = (bf16[256,1024]{1,0:T(8,128)(2,1)S(1)}, bf16[256,1024]{1,0:T(8,128)(2,1)S(1)}, u32[]{:S(2)}, u32[]{:S(2)}) collective-permute-start(bf16[256,1024]{1,0:T(8,128)(2,1)S(1)} %get-tuple-element.122.refs_2_), channel_id=1, source_target_pairs={{0,4},{4,0},{8,12},{12,8},{16,20},{20,16},{24,28},{28,24},{1,5},{5... | collective-permute-start | bytes 1572872 | tf_op jit(solution)/shard_map/ppermute | solution.py:36
  224.3 20.8 %collective-permute-start.25 = (bf16[2,8,64,512]{3,2,1,0:T(8,128)(2,1)}, bf16[2,8,64,512]{3,2,1,0:T(8,128)(2,1)}, u32[]{:S(2)}, u32[]{:S(2)}) collective-permute-start(bf16[2,8,64,512]{3,2,1,0:T(8,128)(2,1)} %pad_maximum_fusion.1.refs_0_), channel_id=1, source_target_pairs={{0,1},{1,0},{2,3},{3,2},{4,5},{5,4},{6,7},{7,6},{8,9},{9,8},{10,11... | collective-permute-start | bytes 3145736 | tf_op jit(solution)/shard_map/ppermute | solution.py:300
  224.3 19.7 %all-to-all-start.4 = ((f32[8,8,2048]{2,1,0:T(8,128)}), f32[8,8,2048]{2,1,0:T(8,128)}, u32[]{:S(2)}, u32[]{:S(2)}) async-start(f32[8,8,2048]{2,1,0:T(8,128)} %bitcast.47), calls=%async_computation.4 | async-start | bytes 1048576 | tf_op jit(solution)/shard_map/all_to_all | solution.py:436
  229.9 15.2 %collective-permute-start.26 = (bf16[2,256,512]{2,1,0:T(8,128)(2,1)}, bf16[2,256,512]{2,1,0:T(8,128)(2,1)}, u32[]{:S(2)}, u32[]{:S(2)}) collective-permute-start(bf16[2,256,512]{2,1,0:T(8,128)(2,1)} %get-tuple-element.131), channel_id=1, source_target_pairs={{0,1},{1,0},{2,3},{3,2},{4,5},{5,4},{6,7},{7,6},{8,9},{9,8},{10,11... | collective-permute-start | bytes 1572872 | tf_op jit(solution)/shard_map/ppermute | solution.py:300
  230.2 22.8 %collective-permute-start.27 = (bf16[2,256,512]{2,1,0:T(8,128)(2,1)}, bf16[2,256,512]{2,1,0:T(8,128)(2,1)}, u32[]{:S(2)}, u32[]{:S(2)}) collective-permute-start(bf16[2,256,512]{2,1,0:T(8,128)(2,1)} %get-tuple-element.130), channel_id=1, source_target_pairs={{0,3},{1,2},{2,1},{3,0},{4,7},{5,6},{6,5},{7,4},{8,11},{9,10},{10,... | collective-permute-start | bytes 1572872 | tf_op jit(solution)/shard_map/ppermute | solution.py:300
  230.5 25.4 %collective-permute-start.28 = (bf16[2,256,512]{2,1,0:T(8,128)(2,1)}, bf16[2,256,512]{2,1,0:T(8,128)(2,1)}, u32[]{:S(2)}, u32[]{:S(2)}) collective-permute-start(bf16[2,256,512]{2,1,0:T(8,128)(2,1)} %get-tuple-element.129), channel_id=1, source_target_pairs={{0,2},{1,3},{2,0},{3,1},{4,6},{5,7},{6,4},{7,5},{8,10},{9,11},{10,... | collective-permute-start | bytes 1572872 | tf_op jit(solution)/shard_map/ppermute | solution.py:300
  245.1 32.0 %collective-permute-start.29 = (bf16[256,1024]{1,0:T(8,128)(2,1)}, bf16[256,1024]{1,0:T(8,128)(2,1)}, u32[]{:S(2)}, u32[]{:S(2)}) collective-permute-start(bf16[256,1024]{1,0:T(8,128)(2,1)} %copy-done.16), channel_id=1, source_target_pairs={{0,4},{4,0},{8,12},{12,8},{16,20},{20,16},{24,28},{28,24},{1,5},{5... | collective-permute-start | bytes 1572872 | tf_op jit(solution)/shard_map/ppermute | solution.py:36
  246.6 30.5 %collective-permute-start.30 = (bf16[256,1024]{1,0:T(8,128)(2,1)}, bf16[256,1024]{1,0:T(8,128)(2,1)}, u32[]{:S(2)}, u32[]{:S(2)}) collective-permute-start(bf16[256,1024]{1,0:T(8,128)(2,1)} %copy-done.18), channel_id=1, source_target_pairs={{0,4},{4,0},{8,12},{12,8},{16,20},{20,16},{24,28},{28,24},{1,5},{5... | collective-permute-start | bytes 1572872 | tf_op jit(solution)/shard_map/ppermute | solution.py:36
  247.2 29.9 %collective-permute-start.31 = (bf16[256,1024]{1,0:T(8,128)(2,1)}, bf16[256,1024]{1,0:T(8,128)(2,1)}, u32[]{:S(2)}, u32[]{:S(2)}) collective-permute-start(bf16[256,1024]{1,0:T(8,128)(2,1)} %copy-done.14), channel_id=1, source_target_pairs={{16,0},{20,4},{24,8},{28,12},{0,16},{4,20},{8,24},{12,28},{17,1},{... | collective-permute-start | bytes 1572872 | tf_op jit(solution)/shard_map/ppermute | solution.py:31
  248.0 29.1 %all-to-all-start.5 = ((bf16[8,8,2048]{2,1,0:T(8,128)(2,1)}), bf16[8,8,2048]{2,1,0:T(8,128)(2,1)S(1)}, u32[]{:S(2)}, u32[]{:S(2)}) async-start(bf16[8,8,2048]{2,1,0:T(8,128)(2,1)} %broadcast_in_dim.17), calls=%async_computation.5 | async-start | bytes 524288 | tf_op jit(solution)/shard_map/all_to_all | solution.py:343
  258.4 39.9 %copy-start.15 = (bf16[256,1024]{1,0:T(8,128)(2,1)S(1)}, bf16[256,1024]{1,0:T(8,128)(2,1)}, u32[]{:S(2)}) copy-start(bf16[256,1024]{1,0:T(8,128)(2,1)} %copy-done.14) | copy-start | bytes 1572868
  258.4 39.9 %copy-start.17 = (bf16[256,1024]{1,0:T(8,128)(2,1)S(1)}, bf16[256,1024]{1,0:T(8,128)(2,1)}, u32[]{:S(2)}) copy-start(bf16[256,1024]{1,0:T(8,128)(2,1)} %copy-done.16) | copy-start | bytes 1572868
  258.4 39.9 %copy-start.19 = (bf16[256,1024]{1,0:T(8,128)(2,1)S(1)}, bf16[256,1024]{1,0:T(8,128)(2,1)}, u32[]{:S(2)}) copy-start(bf16[256,1024]{1,0:T(8,128)(2,1)} %copy-done.18) | copy-start | bytes 1572868
  258.4 39.9 %copy-start.21 = (bf16[256,1024]{1,0:T(8,128)(2,1)S(1)}, bf16[256,1024]{1,0:T(8,128)(2,1)}, u32[]{:S(2)}) copy-start(bf16[256,1024]{1,0:T(8,128)(2,1)} %copy-done.20) | copy-start | bytes 1572868
  277.1 14.2 %collective-permute-start.32 = (bf16[256,1024]{1,0:T(8,128)(2,1)}, bf16[256,1024]{1,0:T(8,128)(2,1)}, u32[]{:S(2)}, u32[]{:S(2)}) collective-permute-start(bf16[256,1024]{1,0:T(8,128)(2,1)} %collective-permute-done.31.refs_4_), channel_id=1, source_target_pairs={{0,4},{4,0},{8,12},{12,8},{16,20},{20,16},{24,28},{28,24},{1,5},{5... | collective-permute-start | bytes 1572872 | tf_op jit(solution)/shard_map/ppermute | solution.py:36
  281.6 6.0 %all-to-all-start.6 = ((bf16[4,16,512]{2,1,0:T(8,128)(2,1)}), bf16[4,16,512]{2,1,0:T(8,128)(2,1)S(1)}, u32[]{:S(2)}, u32[]{:S(2)}) async-start(bf16[4,16,512]{2,1,0:T(8,128)(2,1)} %bitcast.22), calls=%async_computation.6 | async-start | bytes 131072 | tf_op jit(solution)/shard_map/all_to_all | solution.py:250
  291.4 12.4 %collective-permute-start.33 = (bf16[8,512]{1,0:T(8,128)(2,1)S(1)}, bf16[8,512]{1,0:T(8,128)(2,1)S(1)}, u32[]{:S(2)}, u32[]{:S(2)}) collective-permute-start(bf16[8,512]{1,0:T(8,128)(2,1)S(1)} %get-tuple-element.134), channel_id=1, source_target_pairs={{0,0},{1,8},{2,16},{3,24},{4,4},{5,12},{6,20},{7,28},{8,1},{9,9},{... | collective-permute-start | bytes 24584 | tf_op jit(solution)/shard_map/ppermute | solution.py:266
  294.4 9.4 %collective-permute-start.34 = (bf16[8,512]{1,0:T(8,128)(2,1)S(1)}, bf16[8,512]{1,0:T(8,128)(2,1)S(1)}, u32[]{:S(2)}, u32[]{:S(2)}) collective-permute-start(bf16[8,512]{1,0:T(8,128)(2,1)S(1)} %get-tuple-element.135), channel_id=1, source_target_pairs={{0,4},{1,12},{2,20},{3,28},{4,0},{5,8},{6,16},{7,24},{8,5},{9,13},... | collective-permute-start | bytes 24584 | tf_op jit(solution)/shard_map/ppermute | solution.py:266
  (18 other events, 72.8 us)
